TPU v7x, 32 devices: a whole 2x2x4 slice. The times are simulated.
32 devices in a mesh: rows: 8 (over z, y), cols: 4 (over x, core).
Axes of the slice: x: 2, y: 2, z: 4, core: 2. Of those that a mesh axis runs over, the one named last changes fastest.
Arguments:
- activations: bfloat16 [128, 64, 384], P('rows', 'cols'), may hold values from -6 to 6
- grad_out: bfloat16 [128, 64, 384], P('rows', 'cols'), may hold values from -6 to 6
- kernels: float32 [2, 7, 7, 384], replicated, may hold values from -0.875 to 0.875
- norm_gains: float32 [2, 384], replicated, may hold values from 0.5 to 1.5
- norm_shifts: float32 [2, 384], replicated, may hold values from -3 to 3
- w_in: bfloat16 [2, 384, 1536], replicated, may hold values from -0.3125 to 0.3125
- b_in: float32 [2, 1536], replicated, may hold values from -3 to 3
- w_out: bfloat16 [2, 384, 1536], replicated, may hold values from -0.15625 to 0.15625
Outputs:
- grad_in: bfloat16 [128, 64, 384], P('rows', 'cols')
- grad_kernels: float32 [2, 7, 7, 384], replicated
- grad_gains: float32 [2, 384], replicated
- grad_shifts: float32 [2, 384], replicated
- grad_b_in: float32 [2, 1536], replicated
- grad_w_in: float32 [2, 384, 1536], P(None, None, ('rows', 'cols'))
- grad_w_out: float32 [2, 384, 1536], P(None, None, ('rows', 'cols'))
All inputs are finite; a program needn't handle non-finite values.
Results may differ from a plain program's by a relative error of at most 0.017.
Values may be sent and summed in bfloat16 or wider, within the bound.
No kernel may reach another device: no remote copies, remote signals or barrier semaphores. Data moves between devices by JAX's collectives and lax.ppermute only.
A program may use at most 128 MiB of HBM per device.

v0:
```python
import math

import jax
import jax.numpy as jnp
from jax import lax
from jax.sharding import PartitionSpec as P

EPSILON = 1e-06
ROOT_HALF = 0.7071067811865476
INV_ROOT_TAU = 0.3989422804014327


def with_halo(block, sides, width):
    for axis, dim in sides:
        count = lax.axis_size(axis)
        forward = [(i, i + 1) for i in range(count - 1)]
        backward = [(target, source) for source, target in forward]
        low = lax.ppermute(
            lax.slice_in_dim(block, block.shape[dim] - width, None, axis=dim), axis, forward
        )
        high = lax.ppermute(lax.slice_in_dim(block, 0, width, axis=dim), axis, backward)
        block = jnp.concatenate([low, block, high], axis=dim)
    return block


def gelu_parts(pre_act):
    normal_cdf = 0.5 * (1.0 + lax.erf(pre_act * ROOT_HALF))
    density = jnp.exp(-0.5 * pre_act * pre_act) * INV_ROOT_TAU
    return (pre_act * normal_cdf, normal_cdf + pre_act * density)


def conv_from(padded, kernel, out_rows, out_cols):
    running = jnp.zeros((out_rows, out_cols, padded.shape[2]), jnp.float32)
    for row_off in range(7):
        for col_off in range(7):
            running = (
                running
                + kernel[row_off, col_off]
                * padded[row_off : row_off + out_rows, col_off : col_off + out_cols]
            )
    return running


def conv_back(padded_grad, kernel, out_rows, out_cols):
    running = jnp.zeros((out_rows, out_cols, padded_grad.shape[2]), jnp.float32)
    for row_off in range(7):
        for col_off in range(7):
            running = (
                running
                + kernel[row_off, col_off]
                * padded_grad[
                    6 - row_off : 6 - row_off + out_rows, 6 - col_off : 6 - col_off + out_cols
                ]
            )
    return running


def kernel_grad(grad_z, padded_in):
    out_rows, out_cols = (grad_z.shape[0], grad_z.shape[1])
    kernel_taps = []
    for row_off in range(7):
        for col_off in range(7):
            kernel_taps.append(
                jnp.sum(
                    grad_z * padded_in[row_off : row_off + out_rows, col_off : col_off + out_cols],
                    axis=(0, 1),
                )
            )
    return jnp.stack(kernel_taps).reshape(7, 7, grad_z.shape[2])


def norm_fwd(source, gain, shift):
    center = source - jnp.mean(source, axis=-1, keepdims=True)
    inv_std = lax.rsqrt(jnp.mean(center * center, axis=-1, keepdims=True) + EPSILON)
    norm_hat = center * inv_std
    return (norm_hat, inv_std, (norm_hat * gain + shift).astype(jnp.bfloat16))


def norm_back(grad_n, norm_hat, inv_std, gain):
    scaled = grad_n * gain
    return inv_std * (
        scaled
        - jnp.mean(scaled, axis=-1, keepdims=True)
        - norm_hat * jnp.mean(scaled * norm_hat, axis=-1, keepdims=True)
    )


def mlp_hidden(normed_flat, weight_in, bias_in):
    pre_act = jnp.dot(normed_flat, weight_in, preferred_element_type=jnp.float32) + bias_in
    activation, gelu_slope = gelu_parts(pre_act)
    return (activation.astype(jnp.bfloat16), gelu_slope)


def mlp_forward(normed_flat, weight_in, bias_in, weight_out):
    act_b, gelu_slope = mlp_hidden(normed_flat, weight_in, bias_in)
    mixed = lax.dot_general(
        act_b, weight_out, (((1,), (1,)), ((), ())), preferred_element_type=jnp.float32
    )
    return (act_b, gelu_slope, mixed)


def input_rim(source):
    return with_halo(source, (("rows", 0), ("cols", 1)), 3)


def layer_back(
    grad_b,
    normed_flat,
    act_b,
    gelu_slope,
    norm_hat,
    inv_std,
    kernel,
    gain,
    weight_in,
    weight_out,
    padded_in,
):
    tile_rows, tile_cols, channels = grad_b.shape
    grad_flat = grad_b.reshape(-1, channels)
    grad_wo = lax.dot_general(
        grad_flat, act_b, (((0,), (0,)), ((), ())), preferred_element_type=jnp.float32
    )
    grad_pre = jnp.dot(grad_flat, weight_out, preferred_element_type=jnp.float32) * gelu_slope
    grad_preb = grad_pre.astype(jnp.bfloat16)
    grad_wi = lax.dot_general(
        normed_flat, grad_preb, (((0,), (0,)), ((), ())), preferred_element_type=jnp.float32
    )
    grad_bias = jnp.sum(grad_pre, axis=0)
    grad_n = lax.dot_general(
        grad_preb, weight_in, (((1,), (1,)), ((), ())), preferred_element_type=jnp.float32
    ).reshape(grad_b.shape)
    grad_gain = jnp.sum(grad_n * norm_hat, axis=(0, 1))
    grad_shift = jnp.sum(grad_n, axis=(0, 1))
    grad_z = norm_back(grad_n, norm_hat, inv_std, gain).astype(jnp.bfloat16)
    padded_grad = with_halo(grad_z, (("rows", 0), ("cols", 1)), 3)
    kernel_taps = kernel_grad(grad_z.astype(jnp.float32), padded_in)
    spread = conv_back(padded_grad.astype(jnp.float32), kernel, tile_rows, tile_cols)
    return (spread, kernel_taps, grad_gain, grad_shift, grad_bias, grad_wi, grad_wo)


def shards(activations, grad_out, kernels, norm_gains, norm_shifts, w_in, b_in, w_out):
    tile_rows, tile_cols, channels = activations.shape
    grad_scale = 1.0 / math.sqrt(
        tile_rows * tile_cols * lax.axis_size("rows") * lax.axis_size("cols")
    )
    padded_in = input_rim(activations).astype(jnp.float32)
    conv_one = conv_from(padded_in, kernels[0], tile_rows, tile_cols)
    hat_one, inv_one, normed_grid = norm_fwd(conv_one, norm_gains[0], norm_shifts[0])
    normed_one = normed_grid.reshape(-1, channels)
    act_one, slope_one, mixed_one = mlp_forward(normed_one, w_in[0], b_in[0], w_out[0])
    middle = (activations.astype(jnp.float32) + mixed_one.reshape(activations.shape)).astype(
        jnp.bfloat16
    )
    padded_mid = input_rim(middle)
    padded_mid_wide = padded_mid.astype(jnp.float32)
    conv_two = conv_from(padded_mid_wide, kernels[1], tile_rows, tile_cols)
    hat_two, inv_two, normed_grid_two = norm_fwd(conv_two, norm_gains[1], norm_shifts[1])
    normed_two = normed_grid_two.reshape(-1, channels)
    act_two, slope_two = mlp_hidden(normed_two, w_in[1], b_in[1])
    back_two = layer_back(
        grad_out,
        normed_two,
        act_two,
        slope_two,
        hat_two,
        inv_two,
        kernels[1],
        norm_gains[1],
        w_in[1],
        w_out[1],
        padded_mid_wide,
    )
    grad_mid = (grad_out.astype(jnp.float32) + back_two[0]).astype(jnp.bfloat16)
    back_one = layer_back(
        grad_mid,
        normed_one,
        act_one,
        slope_one,
        hat_one,
        inv_one,
        kernels[0],
        norm_gains[0],
        w_in[0],
        w_out[0],
        padded_in,
    )
    grad_in = (grad_mid.astype(jnp.float32) + back_one[0]).astype(jnp.bfloat16)
    grad_kernels, grad_gains, grad_shifts, grad_b_in = lax.psum(
        (
            jnp.stack([back_one[1], back_two[1]]) * grad_scale,
            jnp.stack([back_one[2], back_two[2]]) * grad_scale,
            jnp.stack([back_one[3], back_two[3]]) * grad_scale,
            jnp.stack([back_one[4], back_two[4]]) * grad_scale,
        ),
        ("rows", "cols"),
    )
    stacked_in = jnp.stack([back_one[5], back_two[5]]) * grad_scale
    stacked_out = jnp.stack([back_one[6], back_two[6]]) * grad_scale
    grad_w_in, grad_w_out = (
        lax.psum_scatter(stacked_in, ("rows", "cols"), scatter_dimension=2, tiled=True),
        lax.psum_scatter(stacked_out, ("rows", "cols"), scatter_dimension=2, tiled=True),
    )
    return (grad_in, grad_kernels, grad_gains, grad_shifts, grad_b_in, grad_w_in, grad_w_out)


def solution(mesh):
    return jax.shard_map(
        shards,
        mesh=mesh,
        in_specs=(P("rows", "cols", None), P("rows", "cols", None), P(), P(), P(), P(), P(), P()),
        out_specs=(
            P("rows", "cols", None),
            P(),
            P(),
            P(),
            P(),
            P(None, None, ("rows", "cols")),
            P(None, None, ("rows", "cols")),
        ),
        check_vma=False,
    )
```

profile of v0, /device:TPU:0, one launch (start us, length us, event | category | flops | bytes accessed | tf_op | source)
XLA Modules:
  0.0 352.2 jit_solution(7030744163227129644)
XLA Ops:
  9.3 5.5 %collective-permute-start = (bf16[3,16,384]{2,1,0:T(8,128)(2,1)S(1)}, bf16[3,16,384]{2,1,0:T(8,128)(2,1)S(1)}, u32[]{:S(2)}, u32[]{:S(2)}) collective-permute-start(bf16[3,16,384]{2,1,0:T(8,128)(2,1)S(1)} %get-tuple-element.269), channel_id=1, source_target_pairs={{0,4},{4,8},{8,12},{12,16},{16,20},{20,24},{24,28},{1,5},{5,9},{9,... | collective-permute-start | bytes 110600 | tf_op jit(solution)/shard_map/ppermute | solution.py:18
  23.2 3.3 collective-permute-done.3
  26.6 3.7 %fusion.226 = (f32[16,16]{1,0:T(8,128)S(1)}, f32[16,16,384]{2,1,0:T(8,128)S(1)}) fusion(f32[22,22,384]{2,1,0:T(8,128)S(1)} %maximum_convert_fusion, f32[384]{0:T(512)S(1)} %get-tuple-element.184, f32[384]{0:T(512)S(1)} %get-tuple-element.185, f32[384]{0:T(512)S(1)} %get-tuple-element.186, f32[384]{0:T(512)S(1)} %get-tuple-element.187, ...), kind=kLoop, calls=%fused_computation.589 | loop fusion | flops 9633536 | bytes 19737088 | tf_op jit(solution)/shard_map/reduce_sum | solution.py:73
  31.8 1.8 multiply_convert_fusion.1
  34.8 4.3 %collective-permute-start.4 = (bf16[3,16,384]{2,1,0:T(8,128)(2,1)S(1)}, bf16[3,16,384]{2,1,0:T(8,128)(2,1)S(1)}, u32[]{:S(2)}, u32[]{:S(2)}) collective-permute-start(bf16[3,16,384]{2,1,0:T(8,128)(2,1)S(1)} %get-tuple-element.266), channel_id=1, source_target_pairs={{0,4},{4,8},{8,12},{12,16},{16,20},{20,24},{24,28},{1,5},{5,9},{9,... | collective-permute-start | bytes 110600 | tf_op jit(solution)/shard_map/ppermute | solution.py:18
  40.7 4.2 %collective-permute-done.5 = bf16[3,16,384]{2,1,0:T(8,128)(2,1)S(1)} collective-permute-done((bf16[3,16,384]{2,1,0:T(8,128)(2,1)S(1)}, bf16[3,16,384]{2,1,0:T(8,128)(2,1)S(1)}, u32[]{:S(2)}, u32[]{:S(2)}) %collective-permute-start.5) | collective-permute-done | bytes 36896 | tf_op jit(solution)/shard_map/ppermute | solution.py:21
  45.0 3.4 collective-permute-start.6
  50.0 2.5 collective-permute-done.7
  52.6 3.6 %fusion.225 = (f32[16,16]{1,0:T(8,128)S(1)}, f32[16,16,384]{2,1,0:T(8,128)S(1)}) fusion(f32[22,22,384]{2,1,0:T(8,128)S(1)} %maximum_convert_fusion.1, f32[384]{0:T(512)} %get-tuple-element.135, f32[384]{0:T(512)} %get-tuple-element.136, f32[384]{0:T(512)} %get-tuple-element.137, f32[384]{0:T(512)} %get-tuple-element.138, f32[384]{0:T(512)} %get-tuple-element.139, ...), kind=kLoop, calls=%fused_computation.588 | loop fusion | flops 9633536 | bytes 19737088 | tf_op jit(solution)/shard_map/reduce_sum | solution.py:73
  57.8 1.5 fusion.228
  62.8 3.8 %collective-permute-start.8 = (bf16[3,16,384]{2,1,0:T(8,128)(2,1)S(1)}, bf16[3,16,384]{2,1,0:T(8,128)(2,1)S(1)}, u32[]{:S(2)}, u32[]{:S(2)}) collective-permute-start(bf16[3,16,384]{2,1,0:T(8,128)(2,1)S(1)} %get-tuple-element.264), channel_id=1, source_target_pairs={{0,4},{4,8},{8,12},{12,16},{16,20},{20,24},{24,28},{1,5},{5,9},{9,... | collective-permute-start | bytes 110600 | tf_op jit(solution)/shard_map/ppermute | solution.py:18
  66.6 1.5 collective-permute-start.9
  68.1 2.0 convolution_bitcast_fusion
  70.1 2.4 collective-permute-done.9
  73.2 4.0 %collective-permute-start.10 = (bf16[22,3,384]{2,1,0:T(4,128)(2,1)}, bf16[22,3,384]{2,1,0:T(4,128)(2,1)}, u32[]{:S(2)}, u32[]{:S(2)}) collective-permute-start(bf16[22,3,384]{2,1,0:T(4,128)(2,1)} %get-tuple-element.256), channel_id=1, source_target_pairs={{0,1},{1,2},{2,3},{4,5},{5,6},{6,7},{8,9},{9,10},{10,11},{12,13},{... | collective-permute-start | bytes 152072 | tf_op jit(solution)/shard_map/ppermute | solution.py:18
  95.3 4.3 %stack.447 = f32[49,384]{1,0:T(8,128)S(1)} concatenate(f32[1,384]{1,0:T(1,128)S(1)} %stack.398, f32[1,384]{1,0:T(1,128)S(1)} %stack.399, f32[1,384]{1,0:T(1,128)} %stack.400, f32[1,384]{1,0:T(1,128)} %stack.401, f32[1,384]{1,0:T(1,128)} %stack.402, f32[1,384]{1,0:T(1,128)} %stack.403, f32[1,384]{1,0:T(1,128)} %stack.404, f32[1,384]{1,0:T(1,128)} %stack.405, f32[1,384]{1,0:T(1,128)} %stack.406, ...), dimensions={0} | concatenate | bytes 150528 | tf_op jit(solution)/shard_map/stack | solution.py:69
  100.7 3.9 %fusion.177 = bf16[16,16,384]{2,1,0:T(8,128)(2,1)S(1)} fusion(f32[22,22,384]{2,1,0:T(8,128)S(1)} %maximum_convert_fusion.2, bf16[16,16,384]{2,1,0:T(8,128)(2,1)} %param.9, f32[384]{0:T(512)} %get-tuple-element.135, f32[384]{0:T(512)} %get-tuple-element.136, f32[384]{0:T(512)} %get-tuple-element.137, f32[384]{0:T(512)} %get-tuple-element.138, ...), kind=kLoop, calls=%fused_computation.344 | loop fusion | flops 9830400 | bytes 19736064 | tf_op jit(solution)/shard_map/convert_element_type | solution.py:174
  106.5 2.0 multiply_reduce_fusion.1
  108.5 1.5 fusion.74
  111.7 1.9 convolution_bitcast_fusion.1
  113.6 1.9 convolution_bitcast_fusion.3
  116.2 5.1 %maximum_multiply_fusion.1 = f32[2,384,1536]{2,1,0:T(8,128)} fusion(f32[1,384,1536]{2,1,0:T(8,128)} %convolution_bitcast_fusion, f32[1,384,1536]{2,1,0:T(8,128)} %convolution_bitcast_fusion.1), kind=kLoop, calls=%fused_computation.99 | loop fusion | flops 2359296 | bytes 9437184 | tf_op jit(solution)/shard_map/mul | solution.py:199
  121.3 8.2 %copy.28 = f32[2,384,1536]{1,0,2:T(2,128)} copy(f32[2,384,1536]{2,1,0:T(8,128)} %maximum_multiply_fusion.1) | data formatting | bytes 9437184 | tf_op jit(solution)/shard_map/mul | solution.py:199
  129.4 4.6 %maximum_multiply_fusion = f32[2,384,1536]{2,1,0:T(8,128)} fusion(f32[1,384,1536]{2,1,0:T(8,128)S(1)} %convolution_bitcast_fusion.2, f32[1,384,1536]{2,1,0:T(8,128)} %convolution_bitcast_fusion.3), kind=kLoop, calls=%fused_computation.98 | loop fusion | flops 2359296 | bytes 9437184 | tf_op jit(solution)/shard_map/mul | solution.py:198
  134.0 8.2 %copy.26 = f32[2,384,1536]{1,0,2:T(2,128)} copy(f32[2,384,1536]{2,1,0:T(8,128)} %maximum_multiply_fusion) | data formatting | bytes 9437184 | tf_op jit(solution)/shard_map/mul | solution.py:198
  145.6 4.0 %collective-permute-start.12 = (bf16[3,16,384]{2,1,0:T(8,128)(2,1)S(1)}, bf16[3,16,384]{2,1,0:T(8,128)(2,1)S(1)}, u32[]{:S(2)}, u32[]{:S(2)}) collective-permute-start(bf16[3,16,384]{2,1,0:T(8,128)(2,1)S(1)} %get-tuple-element.262), channel_id=1, source_target_pairs={{0,4},{4,8},{8,12},{12,16},{16,20},{20,24},{24,28},{1,5},{5,9},{9,... | collective-permute-start | bytes 110600 | tf_op jit(solution)/shard_map/ppermute | solution.py:18
  151.8 4.8 %collective-permute-done.13 = bf16[3,16,384]{2,1,0:T(8,128)(2,1)S(1)} collective-permute-done((bf16[3,16,384]{2,1,0:T(8,128)(2,1)S(1)}, bf16[3,16,384]{2,1,0:T(8,128)(2,1)S(1)}, u32[]{:S(2)}, u32[]{:S(2)}) %collective-permute-start.13) | collective-permute-done | bytes 36896 | tf_op jit(solution)/shard_map/ppermute | solution.py:21
  156.7 2.3 collective-permute-start.14
  160.3 46.4 %all-reduce.2 = (f32[2,384]{1,0:T(2,128)}, f32[2,384]{1,0:T(2,128)}, f32[2,1536]{1,0:T(2,128)}) all-reduce(f32[2,384]{1,0:T(2,128)S(1)} %maximum_multiply_fusion.4, f32[2,384]{1,0:T(2,128)S(1)} %maximum_multiply_fusion.5, f32[2,1536]{1,0:T(2,128)S(1)} %maximum_multiply_fusion.3), channel_id=1, replica_groups=mesh['rows'=8,'cols'=4] {'rows','cols'}, use_global_device_ids=true, to_apply=%region_109.0 | all-reduce | flops 4608 | bytes 36864 | tf_op jit(solution)/shard_map/psum | solution.py:189
  207.2 4.1 %fusion.127 = bf16[16,16,384]{2,1,0:T(8,128)(2,1)} fusion(f32[22,22,384]{2,1,0:T(8,128)S(1)} %maximum_convert_fusion.3, bf16[16,16,384]{2,1,0:T(8,128)(2,1)S(1)} %copy-done.3, f32[384]{0:T(512)S(1)} %copy-done.77, f32[384]{0:T(512)S(1)} %copy-done.79, f32[384]{0:T(512)S(1)} %copy-done.81, f32[384]{0:T(512)S(1)} %copy-done.83, f32[384]{0:T(512)S(1)} %copy-done.85, ...), kind=kLoop, calls=%fused_computation.245 | loop fusion | flops 9830400 | bytes 19736064 | tf_op jit(solution)/shard_map/convert_element_type | solution.py:188
  211.3 129.1 %all-reduce.6.cloned.1.call-done = (f32[2,7,7,384]{3,2,1,0:T(8,128)}, f32[2,384,1536]{1,0,2:T(2,128)}, f32[2,384,1536]{1,0,2:T(2,128)}) async-done(((f32[2,7,7,384]{3,2,1,0:T(8,128)}, f32[2,384,1536]{1,0,2:T(2,128)}, f32[2,384,1536]{1,0,2:T(2,128)}), (f32[2,7,7,384]{3,2,1,0:T(8,128)}, f32[2,384,1536]{1,0,2:T(2,128)}, f32[2,384,1536]{1,0,2:T(2,128)})) %all-reduce.6.cloned.1.call-update) | async-done | bytes 9587728 | tf_op jit(solution)/shard_map/psum | solution.py:189
  340.4 1.7 copy.29
  (435 shorter events, 54.1 us)
Async XLA Ops:
  7.2 333.2 %all-reduce.6.cloned.1.call-start = ((), (), s32[]{:S(2)}) async-start(), calls=%async_computation | async-start | bytes 19218432 | tf_op jit(solution)/shard_map/psum | solution.py:189
  8.0 11.7 %collective-permute-start.1 = (bf16[3,16,384]{2,1,0:T(8,128)(2,1)S(1)}, bf16[3,16,384]{2,1,0:T(8,128)(2,1)S(1)}, u32[]{:S(2)}, u32[]{:S(2)}) collective-permute-start(bf16[3,16,384]{2,1,0:T(8,128)(2,1)S(1)} %get-tuple-element.268), channel_id=1, source_target_pairs={{4,0},{8,4},{12,8},{16,12},{20,16},{24,20},{28,24},{5,1},{9,5},{13... | collective-permute-start | bytes 110600 | tf_op jit(solution)/shard_map/ppermute | solution.py:21
  9.3 9.4 %collective-permute-start = (bf16[3,16,384]{2,1,0:T(8,128)(2,1)S(1)}, bf16[3,16,384]{2,1,0:T(8,128)(2,1)S(1)}, u32[]{:S(2)}, u32[]{:S(2)}) collective-permute-start(bf16[3,16,384]{2,1,0:T(8,128)(2,1)S(1)} %get-tuple-element.269), channel_id=1, source_target_pairs={{0,4},{4,8},{8,12},{12,16},{16,20},{20,24},{24,28},{1,5},{5,9},{9,... | collective-permute-start | bytes 110600 | tf_op jit(solution)/shard_map/ppermute | solution.py:18
  19.8 3.4 collective-permute-start.2
  21.2 5.2 %collective-permute-start.3 = (bf16[22,3,384]{2,1,0:T(4,128)(2,1)S(1)}, bf16[22,3,384]{2,1,0:T(4,128)(2,1)S(1)}, u32[]{:S(2)}, u32[]{:S(2)}) collective-permute-start(bf16[22,3,384]{2,1,0:T(4,128)(2,1)S(1)} %get-tuple-element.261), channel_id=1, source_target_pairs={{1,0},{2,1},{3,2},{5,4},{6,5},{7,6},{9,8},{10,9},{11,10},{13,12},{... | collective-permute-start | bytes 152072 | tf_op jit(solution)/shard_map/ppermute | solution.py:21
  34.8 6.0 %collective-permute-start.4 = (bf16[3,16,384]{2,1,0:T(8,128)(2,1)S(1)}, bf16[3,16,384]{2,1,0:T(8,128)(2,1)S(1)}, u32[]{:S(2)}, u32[]{:S(2)}) collective-permute-start(bf16[3,16,384]{2,1,0:T(8,128)(2,1)S(1)} %get-tuple-element.266), channel_id=1, source_target_pairs={{0,4},{4,8},{8,12},{12,16},{16,20},{20,24},{24,28},{1,5},{5,9},{9,... | collective-permute-start | bytes 110600 | tf_op jit(solution)/shard_map/ppermute | solution.py:18
  39.1 5.9 %collective-permute-start.5 = (bf16[3,16,384]{2,1,0:T(8,128)(2,1)S(1)}, bf16[3,16,384]{2,1,0:T(8,128)(2,1)S(1)}, u32[]{:S(2)}, u32[]{:S(2)}) collective-permute-start(bf16[3,16,384]{2,1,0:T(8,128)(2,1)S(1)} %get-tuple-element.267), channel_id=1, source_target_pairs={{4,0},{8,4},{12,8},{16,12},{20,16},{24,20},{28,24},{5,1},{9,5},{13... | collective-permute-start | bytes 110600 | tf_op jit(solution)/shard_map/ppermute | solution.py:21
  45.0 4.9 %collective-permute-start.6 = (bf16[22,3,384]{2,1,0:T(4,128)(2,1)S(1)}, bf16[22,3,384]{2,1,0:T(4,128)(2,1)S(1)}, u32[]{:S(2)}, u32[]{:S(2)}) collective-permute-start(bf16[22,3,384]{2,1,0:T(4,128)(2,1)S(1)} %get-tuple-element.258), channel_id=1, source_target_pairs={{0,1},{1,2},{2,3},{4,5},{5,6},{6,7},{8,9},{9,10},{10,11},{12,13},{... | collective-permute-start | bytes 152072 | tf_op jit(solution)/shard_map/ppermute | solution.py:18
  48.5 4.0 %collective-permute-start.7 = (bf16[22,3,384]{2,1,0:T(4,128)(2,1)S(1)}, bf16[22,3,384]{2,1,0:T(4,128)(2,1)S(1)}, u32[]{:S(2)}, u32[]{:S(2)}) collective-permute-start(bf16[22,3,384]{2,1,0:T(4,128)(2,1)S(1)} %get-tuple-element.259), channel_id=1, source_target_pairs={{1,0},{2,1},{3,2},{5,4},{6,5},{7,6},{9,8},{10,9},{11,10},{13,12},{... | collective-permute-start | bytes 152072 | tf_op jit(solution)/shard_map/ppermute | solution.py:21
  62.8 7.3 %collective-permute-start.8 = (bf16[3,16,384]{2,1,0:T(8,128)(2,1)S(1)}, bf16[3,16,384]{2,1,0:T(8,128)(2,1)S(1)}, u32[]{:S(2)}, u32[]{:S(2)}) collective-permute-start(bf16[3,16,384]{2,1,0:T(8,128)(2,1)S(1)} %get-tuple-element.264), channel_id=1, source_target_pairs={{0,4},{4,8},{8,12},{12,16},{16,20},{20,24},{24,28},{1,5},{5,9},{9,... | collective-permute-start | bytes 110600 | tf_op jit(solution)/shard_map/ppermute | solution.py:18
  66.6 5.9 %collective-permute-start.9 = (bf16[3,16,384]{2,1,0:T(8,128)(2,1)S(1)}, bf16[3,16,384]{2,1,0:T(8,128)(2,1)S(1)}, u32[]{:S(2)}, u32[]{:S(2)}) collective-permute-start(bf16[3,16,384]{2,1,0:T(8,128)(2,1)S(1)} %get-tuple-element.265), channel_id=1, source_target_pairs={{4,0},{8,4},{12,8},{16,12},{20,16},{24,20},{28,24},{5,1},{9,5},{13... | collective-permute-start | bytes 110600 | tf_op jit(solution)/shard_map/ppermute | solution.py:21
  73.2 26.4 %collective-permute-start.10 = (bf16[22,3,384]{2,1,0:T(4,128)(2,1)}, bf16[22,3,384]{2,1,0:T(4,128)(2,1)}, u32[]{:S(2)}, u32[]{:S(2)}) collective-permute-start(bf16[22,3,384]{2,1,0:T(4,128)(2,1)} %get-tuple-element.256), channel_id=1, source_target_pairs={{0,1},{1,2},{2,3},{4,5},{5,6},{6,7},{8,9},{9,10},{10,11},{12,13},{... | collective-permute-start | bytes 152072 | tf_op jit(solution)/shard_map/ppermute | solution.py:18
  77.2 22.4 %collective-permute-start.11 = (bf16[22,3,384]{2,1,0:T(4,128)(2,1)}, bf16[22,3,384]{2,1,0:T(4,128)(2,1)}, u32[]{:S(2)}, u32[]{:S(2)}) collective-permute-start(bf16[22,3,384]{2,1,0:T(4,128)(2,1)} %get-tuple-element.257), channel_id=1, source_target_pairs={{1,0},{2,1},{3,2},{5,4},{6,5},{7,6},{9,8},{10,9},{11,10},{13,12},{... | collective-permute-start | bytes 152072 | tf_op jit(solution)/shard_map/ppermute | solution.py:21
  142.9 63.9 %copy-start.3 = (bf16[16,16,384]{2,1,0:T(8,128)(2,1)S(1)}, bf16[16,16,384]{2,1,0:T(8,128)(2,1)}, u32[]{:S(2)}) copy-start(bf16[16,16,384]{2,1,0:T(8,128)(2,1)} %copy-done.2) | copy-start | bytes 589828
  142.9 63.9 %copy-start.15 = (f32[384]{0:T(512)S(1)}, f32[384]{0:T(512)}, u32[]{:S(2)}) copy-start(f32[384]{0:T(512)} %copy-done.14) | copy-start | bytes 4612
  142.9 63.9 %copy-start.17 = (f32[384]{0:T(512)S(1)}, f32[384]{0:T(512)}, u32[]{:S(2)}) copy-start(f32[384]{0:T(512)} %copy-done.16) | copy-start | bytes 4612
  142.9 63.9 %copy-start.19 = (f32[384]{0:T(512)S(1)}, f32[384]{0:T(512)}, u32[]{:S(2)}) copy-start(f32[384]{0:T(512)} %copy-done.18) | copy-start | bytes 4612
  143.0 63.9 %copy-start.21 = (f32[384]{0:T(512)S(1)}, f32[384]{0:T(512)}, u32[]{:S(2)}) copy-start(f32[384]{0:T(512)} %copy-done.20) | copy-start | bytes 4612
  143.0 63.9 %copy-start.23 = (f32[384]{0:T(512)S(1)}, f32[384]{0:T(512)}, u32[]{:S(2)}) copy-start(f32[384]{0:T(512)} %copy-done.22) | copy-start | bytes 4612
  143.0 63.9 %copy-start.25 = (f32[384]{0:T(512)S(1)}, f32[384]{0:T(512)}, u32[]{:S(2)}) copy-start(f32[384]{0:T(512)} %copy-done.24) | copy-start | bytes 4612
  143.0 63.9 %copy-start.27 = (f32[384]{0:T(512)S(1)}, f32[384]{0:T(512)}, u32[]{:S(2)}) copy-start(f32[384]{0:T(512)} %copy-done.26) | copy-start | bytes 4612
  143.0 63.9 %copy-start.29 = (f32[384]{0:T(512)S(1)}, f32[384]{0:T(512)}, u32[]{:S(2)}) copy-start(f32[384]{0:T(512)} %copy-done.28) | copy-start | bytes 4612
  143.0 63.9 %copy-start.31 = (f32[384]{0:T(512)S(1)}, f32[384]{0:T(512)}, u32[]{:S(2)}) copy-start(f32[384]{0:T(512)} %copy-done.30) | copy-start | bytes 4612
  143.0 63.9 %copy-start.33 = (f32[384]{0:T(512)S(1)}, f32[384]{0:T(512)}, u32[]{:S(2)}) copy-start(f32[384]{0:T(512)} %copy-done.32) | copy-start | bytes 4612
  143.0 63.9 %copy-start.35 = (f32[384]{0:T(512)S(1)}, f32[384]{0:T(512)}, u32[]{:S(2)}) copy-start(f32[384]{0:T(512)} %copy-done.34) | copy-start | bytes 4612
  143.0 63.9 %copy-start.37 = (f32[384]{0:T(512)S(1)}, f32[384]{0:T(512)}, u32[]{:S(2)}) copy-start(f32[384]{0:T(512)} %copy-done.36) | copy-start | bytes 4612
  143.0 63.9 %copy-start.39 = (f32[384]{0:T(512)S(1)}, f32[384]{0:T(512)}, u32[]{:S(2)}) copy-start(f32[384]{0:T(512)} %copy-done.38) | copy-start | bytes 4612
  143.1 63.9 %copy-start.41 = (f32[384]{0:T(512)S(1)}, f32[384]{0:T(512)}, u32[]{:S(2)}) copy-start(f32[384]{0:T(512)} %copy-done.40) | copy-start | bytes 4612
  145.6 6.2 %collective-permute-start.12 = (bf16[3,16,384]{2,1,0:T(8,128)(2,1)S(1)}, bf16[3,16,384]{2,1,0:T(8,128)(2,1)S(1)}, u32[]{:S(2)}, u32[]{:S(2)}) collective-permute-start(bf16[3,16,384]{2,1,0:T(8,128)(2,1)S(1)} %get-tuple-element.262), channel_id=1, source_target_pairs={{0,4},{4,8},{8,12},{12,16},{16,20},{20,24},{24,28},{1,5},{5,9},{9,... | collective-permute-start | bytes 110600 | tf_op jit(solution)/shard_map/ppermute | solution.py:18
  149.6 7.0 %collective-permute-start.13 = (bf16[3,16,384]{2,1,0:T(8,128)(2,1)S(1)}, bf16[3,16,384]{2,1,0:T(8,128)(2,1)S(1)}, u32[]{:S(2)}, u32[]{:S(2)}) collective-permute-start(bf16[3,16,384]{2,1,0:T(8,128)(2,1)S(1)} %get-tuple-element.263), channel_id=1, source_target_pairs={{4,0},{8,4},{12,8},{16,12},{20,16},{24,20},{28,24},{5,1},{9,5},{13... | collective-permute-start | bytes 110600 | tf_op jit(solution)/shard_map/ppermute | solution.py:21
  156.7 50.0 %collective-permute-start.14 = (bf16[22,3,384]{2,1,0:T(4,128)(2,1)S(1)}, bf16[22,3,384]{2,1,0:T(4,128)(2,1)S(1)}, u32[]{:S(2)}, u32[]{:S(2)}) collective-permute-start(bf16[22,3,384]{2,1,0:T(4,128)(2,1)S(1)} %get-tuple-element.254), channel_id=1, source_target_pairs={{0,1},{1,2},{2,3},{4,5},{5,6},{6,7},{8,9},{9,10},{10,11},{12,13},{... | collective-permute-start | bytes 152072 | tf_op jit(solution)/shard_map/ppermute | solution.py:18
  158.9 47.7 %collective-permute-start.15 = (bf16[22,3,384]{2,1,0:T(4,128)(2,1)S(1)}, bf16[22,3,384]{2,1,0:T(4,128)(2,1)S(1)}, u32[]{:S(2)}, u32[]{:S(2)}) collective-permute-start(bf16[22,3,384]{2,1,0:T(4,128)(2,1)S(1)} %get-tuple-element.255), channel_id=1, source_target_pairs={{1,0},{2,1},{3,2},{5,4},{6,5},{7,6},{9,8},{10,9},{11,10},{13,12},{... | collective-permute-start | bytes 152072 | tf_op jit(solution)/shard_map/ppermute | solution.py:21
  (111 other events, 2528.0 us)
Sparse Core Ops, SparseCore 0:
  143.0 197.3 all-reduce.5
where the time goes:
time: 354 us; the launch traced here: 352 us
  waiting for transfers between devices  146 us (41%)
  local copies, waits for them, and re-layouts  53.7 us (15%)
  blocking collectives  46.4 us (13%)
  starting transfers between devices  39.4 us (11%)
  other arithmetic  34.7 us (10%)
  between operations  16.8 us (5%)
  matrix products  14.8 us (4%)
    psum x1, waiting for transfers between devices, shards(): lax.psum((jnp.stack([back_one[1], back_two[1]]) * grad_scale, jnp.stack([...  129 us
    psum x1, blocking collectives, shards(): lax.psum((jnp.stack([back_one[1], back_two[1]]) * grad_scale, jnp.stack([...  46.4 us
    ppermute x8, starting transfers between devices, with_halo(): lax.ppermute(lax.slice_in_dim(block, block.shape[dim] - width, None, axis...  28.8 us
    another operation x100, local copies, waits for them, and re-layouts, kernel_grad(): return jnp.stack(kernel_taps).reshape(7, 7, grad_z.shape[2])  20.7 us
    ppermute x8, waiting for transfers between devices, with_halo(): lax.ppermute(lax.slice_in_dim(block, 0, width, axis=dim), axis, backward)  17.2 us
    ppermute x8, starting transfers between devices, with_halo(): lax.ppermute(lax.slice_in_dim(block, 0, width, axis=dim), axis, backward)  10.5 us
    unnamed x259, local copies, waits for them, and re-layouts  8.74 us
    mul x1, local copies, waits for them, and re-layouts, shards(): stacked_in = jnp.stack([back_one[5], back_two[5]]) * grad_scale  8.17 us
  transfers between devices with their start and end apart: 17, of which 7 were waited for; matrix products, arithmetic and copies ran while one was open for 10% of the time, Pallas kernels for 0%

commit v1 on v0

--- a/solution.py
+++ b/solution.py
@@ -119,12 +119,12 @@
     tile_rows, tile_cols, channels = grad_b.shape
     grad_flat = grad_b.reshape(-1, channels)
     grad_wo = lax.dot_general(
-        grad_flat, act_b, (((0,), (0,)), ((), ())), preferred_element_type=jnp.float32
+        act_b, grad_flat, (((0,), (0,)), ((), ())), preferred_element_type=jnp.float32
     )
     grad_pre = jnp.dot(grad_flat, weight_out, preferred_element_type=jnp.float32) * gelu_slope
     grad_preb = grad_pre.astype(jnp.bfloat16)
     grad_wi = lax.dot_general(
-        normed_flat, grad_preb, (((0,), (0,)), ((), ())), preferred_element_type=jnp.float32
+        grad_preb, normed_flat, (((0,), (0,)), ((), ())), preferred_element_type=jnp.float32
     )
     grad_bias = jnp.sum(grad_pre, axis=0)
     grad_n = lax.dot_general(
@@ -186,21 +186,37 @@
         padded_in,
     )
     grad_in = (grad_mid.astype(jnp.float32) + back_one[0]).astype(jnp.bfloat16)
-    grad_kernels, grad_gains, grad_shifts, grad_b_in = lax.psum(
-        (
-            jnp.stack([back_one[1], back_two[1]]) * grad_scale,
-            jnp.stack([back_one[2], back_two[2]]) * grad_scale,
-            jnp.stack([back_one[3], back_two[3]]) * grad_scale,
-            jnp.stack([back_one[4], back_two[4]]) * grad_scale,
-        ),
-        ("rows", "cols"),
-    )
-    stacked_in = jnp.stack([back_one[5], back_two[5]]) * grad_scale
-    stacked_out = jnp.stack([back_one[6], back_two[6]]) * grad_scale
-    grad_w_in, grad_w_out = (
-        lax.psum_scatter(stacked_in, ("rows", "cols"), scatter_dimension=2, tiled=True),
-        lax.psum_scatter(stacked_out, ("rows", "cols"), scatter_dimension=2, tiled=True),
-    )
+    small = jnp.concatenate(
+        [
+            part.reshape(-1)
+            for back in (back_one, back_two)
+            for part in (back[1], back[2], back[3], back[4])
+        ]
+    ).reshape(-1, channels)
+    small = lax.psum(small, ("rows", "cols")) * grad_scale
+    hidden = w_in.shape[2]
+    small = small.reshape(2, -1)
+    taps = 49 * channels
+    grad_kernels = small[:, :taps].reshape(2, 7, 7, channels)
+    grad_gains = small[:, taps : taps + channels]
+    grad_shifts = small[:, taps + channels : taps + 2 * channels]
+    grad_b_in = small[:, taps + 2 * channels :]
+    slices = []
+    for back in (back_one, back_two):
+        count = lax.axis_size("rows") * lax.axis_size("cols")
+        both = jnp.concatenate(
+            [
+                back[5].astype(jnp.bfloat16).reshape(count, -1, channels),
+                back[6].astype(jnp.bfloat16).reshape(count, -1, channels),
+            ],
+            axis=1,
+        )
+        mine = lax.psum_scatter(
+            both, ("rows", "cols"), scatter_dimension=0, tiled=True
+        ).reshape(2, hidden // count, channels)
+        slices.append(jnp.swapaxes(mine.astype(jnp.float32) * grad_scale, 1, 2))
+    grad_w_in = jnp.stack([slices[0][0], slices[1][0]])
+    grad_w_out = jnp.stack([slices[0][1], slices[1][1]])
     return (grad_in, grad_kernels, grad_gains, grad_shifts, grad_b_in, grad_w_in, grad_w_out)
 
 

time: 354 us -> 451 us (1.27)
  waiting for transfers between devices: 146 us -> 315 us
  blocking collectives: 46.4 us -> 0 us
  local copies, waits for them, and re-layouts: 53.7 us -> 27.9 us
  starting transfers between devices: 39.4 us -> 48.1 us
    reduce_scatter x0 -> x2, waiting for transfers between devices: none -> 203 us  [shards(): lax.psum_scatter(both, ('rows', 'cols'), scatter_dimension=0, tiled=True)]
    psum x1 -> x0, blocking collectives: 46.4 us -> none  [shards(): lax.psum((jnp.stack([back_one[1], back_two[1]]) * grad_scale, jnp.stack([...]
    psum x1, waiting for transfers between devices: 129 us -> 107 us  [shards(): small = lax.psum(small, ('rows', 'cols')) * grad_scale]
    ppermute x8, waiting for transfers between devices: 17.2 us -> 0.25 us  [with_halo(): lax.ppermute(lax.slice_in_dim(block, 0, width, axis=dim), axis, backward)]
    mul x2 -> x0, local copies, waits for them, and re-layouts: 16.3 us -> none  [the longest x1 8.17 us: shards(): stacked_in = jnp.stack([back_one[5], back_two[5]]) * grad_scale]
    ppermute x8, starting transfers between devices: 28.8 us -> 37.7 us  [with_halo(): lax.ppermute(lax.slice_in_dim(block, block.shape[dim] - width, None, axis...]
    mul x6 -> x3, other arithmetic: 10.4 us -> 2.73 us  [the longest x2 1.79 us: shards(): slices.append(jnp.swapaxes(mine.astype(jnp.float32) * grad_scale, 1, 2))]
    another operation x100, local copies, waits for them, and re-layouts: 20.7 us -> 15 us  [kernel_grad(): return jnp.stack(kernel_taps).reshape(7, 7, grad_z.shape[2])]
  transfers between devices with their start and end apart: 17 -> 19, of which waited for: 7 -> 9; matrix products, arithmetic and copies ran while one was open for 10% -> 7% of each run, Pallas kernels for 0% -> 0%
where the time goes in v1:
time: 451 us; the launch traced here: 450 us
  waiting for transfers between devices  315 us (70%)
  starting transfers between devices  48.1 us (11%)
  other arithmetic  30.4 us (7%)
  local copies, waits for them, and re-layouts  27.9 us (6%)
  between operations  16.7 us (4%)
  matrix products  11.9 us (3%)
    reduce_scatter x2, waiting for transfers between devices, shards(): lax.psum_scatter(both, ('rows', 'cols'), scatter_dimension=0, tiled=True)  203 us
    psum x1, waiting for transfers between devices, shards(): small = lax.psum(small, ('rows', 'cols')) * grad_scale  107 us
    ppermute x8, starting transfers between devices, with_halo(): lax.ppermute(lax.slice_in_dim(block, block.shape[dim] - width, None, axis...  37.7 us
    another operation x100, local copies, waits for them, and re-layouts, kernel_grad(): return jnp.stack(kernel_taps).reshape(7, 7, grad_z.shape[2])  15 us
    ppermute x8, starting transfers between devices, with_halo(): lax.ppermute(lax.slice_in_dim(block, 0, width, axis=dim), axis, backward)  10.3 us
  transfers between devices with their start and end apart: 19, of which 9 were waited for; matrix products, arithmetic and copies ran while one was open for 7% of the time, Pallas kernels for 0%

profile of v1, /device:TPU:0, one launch (start us, length us, event | category | flops | bytes accessed | tf_op | source)
XLA Modules:
  0.0 450.1 jit_solution(9568536492789975020)
XLA Ops:
  8.0 4.9 %collective-permute-start = (bf16[3,16,384]{2,1,0:T(8,128)(2,1)S(1)}, bf16[3,16,384]{2,1,0:T(8,128)(2,1)S(1)}, u32[]{:S(2)}, u32[]{:S(2)}) collective-permute-start(bf16[3,16,384]{2,1,0:T(8,128)(2,1)S(1)} %get-tuple-element.242), channel_id=1, source_target_pairs={{0,4},{4,8},{8,12},{12,16},{16,20},{20,24},{24,28},{1,5},{5,9},{9,... | collective-permute-start | bytes 110600 | tf_op jit(solution)/shard_map/ppermute | solution.py:18
  12.9 1.3 collective-permute-start.1
  18.8 1.3 collective-permute-start.3
  20.1 3.0 collective-permute-start.2
  24.2 3.1 fusion.226
  28.7 1.8 multiply_convert_fusion.1
  31.5 1.3 collective-permute-start.5
  32.8 5.0 %collective-permute-start.4 = (bf16[3,16,384]{2,1,0:T(8,128)(2,1)S(1)}, bf16[3,16,384]{2,1,0:T(8,128)(2,1)S(1)}, u32[]{:S(2)}, u32[]{:S(2)}) collective-permute-start(bf16[3,16,384]{2,1,0:T(8,128)(2,1)S(1)} %get-tuple-element.239), channel_id=1, source_target_pairs={{0,4},{4,8},{8,12},{12,16},{16,20},{20,24},{24,28},{1,5},{5,9},{9,... | collective-permute-start | bytes 110600 | tf_op jit(solution)/shard_map/ppermute | solution.py:18
  38.0 1.3 collective-permute-done.4
  39.4 1.3 collective-permute-start.7
  40.7 3.2 collective-permute-start.6
  45.0 3.7 fusion.225
  51.2 1.5 fusion.227
  55.7 1.7 convolution_convert_fusion
  58.6 5.4 %collective-permute-start.8 = (bf16[3,16,384]{2,1,0:T(8,128)(2,1)S(1)}, bf16[3,16,384]{2,1,0:T(8,128)(2,1)S(1)}, u32[]{:S(2)}, u32[]{:S(2)}) collective-permute-start(bf16[3,16,384]{2,1,0:T(8,128)(2,1)S(1)} %get-tuple-element.237), channel_id=1, source_target_pairs={{0,4},{4,8},{8,12},{12,16},{16,20},{20,24},{24,28},{1,5},{5,9},{9,... | collective-permute-start | bytes 110600 | tf_op jit(solution)/shard_map/ppermute | solution.py:18
  66.2 1.3 collective-permute-start.11
  67.5 6.1 %collective-permute-start.10 = (bf16[22,3,384]{2,1,0:T(4,128)(2,1)}, bf16[22,3,384]{2,1,0:T(4,128)(2,1)}, u32[]{:S(2)}, u32[]{:S(2)}) collective-permute-start(bf16[22,3,384]{2,1,0:T(4,128)(2,1)} %get-tuple-element.229), channel_id=1, source_target_pairs={{0,1},{1,2},{2,3},{4,5},{5,6},{6,7},{8,9},{9,10},{10,11},{12,13},{... | collective-permute-start | bytes 152072 | tf_op jit(solution)/shard_map/ppermute | solution.py:18
  86.1 2.9 stack.405
  90.1 3.8 fusion.177
  95.6 1.9 multiply_reduce_fusion.1
  97.6 1.6 fusion.74
  103.0 1.7 pad_maximum_fusion.1
  107.0 1.6 pad_maximum_fusion
  109.1 1.3 collective-permute-start.13
  110.4 5.8 %collective-permute-start.12 = (bf16[3,16,384]{2,1,0:T(8,128)(2,1)S(1)}, bf16[3,16,384]{2,1,0:T(8,128)(2,1)S(1)}, u32[]{:S(2)}, u32[]{:S(2)}) collective-permute-start(bf16[3,16,384]{2,1,0:T(8,128)(2,1)S(1)} %get-tuple-element.235), channel_id=1, source_target_pairs={{0,4},{4,8},{8,12},{12,16},{16,20},{20,24},{24,28},{1,5},{5,9},{9,... | collective-permute-start | bytes 110600 | tf_op jit(solution)/shard_map/ppermute | solution.py:18
  116.2 1.6 collective-permute-done.12
  117.8 1.3 collective-permute-start.15
  119.1 4.3 collective-permute-start.14
  123.4 107.3 %all-reduce.2.cloned.1.call-done = f32[110,384]{1,0:T(8,128)} async-done(((f32[110,384]{1,0:T(8,128)}), f32[110,384]{1,0:T(8,128)}) %all-reduce.2.cloned.1.call-update) | async-done | bytes 168976 | tf_op jit(solution)/shard_map/psum | solution.py:196
  234.1 3.5 fusion.127
  237.6 99.4 %reduce-scatter.5.cloned.1.call-done = bf16[1,96,384]{2,1,0:T(8,128)(2,1)} async-done(((bf16[32,96,384]{2,1,0:T(8,128)(2,1)}), bf16[1,96,384]{2,1,0:T(8,128)(2,1)}) %reduce-scatter.5.cloned.1.call-update) | async-done | bytes 73744 | tf_op jit(solution)/shard_map/reduce_scatter | solution.py:214
  338.0 103.3 %reduce-scatter.3.cloned.1.call-done = bf16[1,96,384]{2,1,0:T(8,128)(2,1)} async-done(((bf16[32,96,384]{2,1,0:T(8,128)(2,1)}), bf16[1,96,384]{2,1,0:T(8,128)(2,1)}) %reduce-scatter.3.cloned.1.call-update) | async-done | bytes 73744 | tf_op jit(solution)/shard_map/reduce_scatter | solution.py:214
  (448 shorter events, 44.9 us)
Async XLA Ops:
  7.2 223.5 %all-reduce.2.cloned.1.call-start = ((), (), s32[]{:S(2)}) async-start(), calls=%async_computation.2 | async-start | bytes 344064 | tf_op jit(solution)/shard_map/psum | solution.py:196
  8.0 9.5 %collective-permute-start = (bf16[3,16,384]{2,1,0:T(8,128)(2,1)S(1)}, bf16[3,16,384]{2,1,0:T(8,128)(2,1)S(1)}, u32[]{:S(2)}, u32[]{:S(2)}) collective-permute-start(bf16[3,16,384]{2,1,0:T(8,128)(2,1)S(1)} %get-tuple-element.242), channel_id=1, source_target_pairs={{0,4},{4,8},{8,12},{12,16},{16,20},{20,24},{24,28},{1,5},{5,9},{9,... | collective-permute-start | bytes 110600 | tf_op jit(solution)/shard_map/ppermute | solution.py:18
  12.9 5.9 %collective-permute-start.1 = (bf16[3,16,384]{2,1,0:T(8,128)(2,1)S(1)}, bf16[3,16,384]{2,1,0:T(8,128)(2,1)S(1)}, u32[]{:S(2)}, u32[]{:S(2)}) collective-permute-start(bf16[3,16,384]{2,1,0:T(8,128)(2,1)S(1)} %get-tuple-element.241), channel_id=1, source_target_pairs={{4,0},{8,4},{12,8},{16,12},{20,16},{24,20},{28,24},{5,1},{9,5},{13... | collective-permute-start | bytes 110600 | tf_op jit(solution)/shard_map/ppermute | solution.py:21
  18.8 5.0 %collective-permute-start.3 = (bf16[22,3,384]{2,1,0:T(4,128)(2,1)S(1)}, bf16[22,3,384]{2,1,0:T(4,128)(2,1)S(1)}, u32[]{:S(2)}, u32[]{:S(2)}) collective-permute-start(bf16[22,3,384]{2,1,0:T(4,128)(2,1)S(1)} %get-tuple-element.234), channel_id=1, source_target_pairs={{1,0},{2,1},{3,2},{5,4},{6,5},{7,6},{9,8},{10,9},{11,10},{13,12},{... | collective-permute-start | bytes 152072 | tf_op jit(solution)/shard_map/ppermute | solution.py:21
  20.1 3.9 collective-permute-start.2
  31.5 6.6 %collective-permute-start.5 = (bf16[3,16,384]{2,1,0:T(8,128)(2,1)S(1)}, bf16[3,16,384]{2,1,0:T(8,128)(2,1)S(1)}, u32[]{:S(2)}, u32[]{:S(2)}) collective-permute-start(bf16[3,16,384]{2,1,0:T(8,128)(2,1)S(1)} %get-tuple-element.240), channel_id=1, source_target_pairs={{4,0},{8,4},{12,8},{16,12},{20,16},{24,20},{28,24},{5,1},{9,5},{13... | collective-permute-start | bytes 110600 | tf_op jit(solution)/shard_map/ppermute | solution.py:21
  32.8 6.6 %collective-permute-start.4 = (bf16[3,16,384]{2,1,0:T(8,128)(2,1)S(1)}, bf16[3,16,384]{2,1,0:T(8,128)(2,1)S(1)}, u32[]{:S(2)}, u32[]{:S(2)}) collective-permute-start(bf16[3,16,384]{2,1,0:T(8,128)(2,1)S(1)} %get-tuple-element.239), channel_id=1, source_target_pairs={{0,4},{4,8},{8,12},{12,16},{16,20},{20,24},{24,28},{1,5},{5,9},{9,... | collective-permute-start | bytes 110600 | tf_op jit(solution)/shard_map/ppermute | solution.py:18
  39.4 4.7 %collective-permute-start.7 = (bf16[22,3,384]{2,1,0:T(4,128)(2,1)S(1)}, bf16[22,3,384]{2,1,0:T(4,128)(2,1)S(1)}, u32[]{:S(2)}, u32[]{:S(2)}) collective-permute-start(bf16[22,3,384]{2,1,0:T(4,128)(2,1)S(1)} %get-tuple-element.232), channel_id=1, source_target_pairs={{1,0},{2,1},{3,2},{5,4},{6,5},{7,6},{9,8},{10,9},{11,10},{13,12},{... | collective-permute-start | bytes 152072 | tf_op jit(solution)/shard_map/ppermute | solution.py:21
  40.7 4.1 collective-permute-start.6
  57.3 7.3 %collective-permute-start.9 = (bf16[3,16,384]{2,1,0:T(8,128)(2,1)S(1)}, bf16[3,16,384]{2,1,0:T(8,128)(2,1)S(1)}, u32[]{:S(2)}, u32[]{:S(2)}) collective-permute-start(bf16[3,16,384]{2,1,0:T(8,128)(2,1)S(1)} %get-tuple-element.238), channel_id=1, source_target_pairs={{4,0},{8,4},{12,8},{16,12},{20,16},{24,20},{28,24},{5,1},{9,5},{13... | collective-permute-start | bytes 110600 | tf_op jit(solution)/shard_map/ppermute | solution.py:21
  58.6 6.9 %collective-permute-start.8 = (bf16[3,16,384]{2,1,0:T(8,128)(2,1)S(1)}, bf16[3,16,384]{2,1,0:T(8,128)(2,1)S(1)}, u32[]{:S(2)}, u32[]{:S(2)}) collective-permute-start(bf16[3,16,384]{2,1,0:T(8,128)(2,1)S(1)} %get-tuple-element.237), channel_id=1, source_target_pairs={{0,4},{4,8},{8,12},{12,16},{16,20},{20,24},{24,28},{1,5},{5,9},{9,... | collective-permute-start | bytes 110600 | tf_op jit(solution)/shard_map/ppermute | solution.py:18
  66.2 22.9 %collective-permute-start.11 = (bf16[22,3,384]{2,1,0:T(4,128)(2,1)}, bf16[22,3,384]{2,1,0:T(4,128)(2,1)S(1)}, u32[]{:S(2)}, u32[]{:S(2)}) collective-permute-start(bf16[22,3,384]{2,1,0:T(4,128)(2,1)} %get-tuple-element.230), channel_id=1, source_target_pairs={{1,0},{2,1},{3,2},{5,4},{6,5},{7,6},{9,8},{10,9},{11,10},{13,12},{... | collective-permute-start | bytes 152072 | tf_op jit(solution)/shard_map/ppermute | solution.py:21
  67.5 21.6 %collective-permute-start.10 = (bf16[22,3,384]{2,1,0:T(4,128)(2,1)}, bf16[22,3,384]{2,1,0:T(4,128)(2,1)}, u32[]{:S(2)}, u32[]{:S(2)}) collective-permute-start(bf16[22,3,384]{2,1,0:T(4,128)(2,1)} %get-tuple-element.229), channel_id=1, source_target_pairs={{0,1},{1,2},{2,3},{4,5},{5,6},{6,7},{8,9},{9,10},{10,11},{12,13},{... | collective-permute-start | bytes 152072 | tf_op jit(solution)/shard_map/ppermute | solution.py:18
  102.9 234.1 %reduce-scatter.5.cloned.1.call-start = ((), (), s32[]{:S(2)}) async-start(), calls=%async_computation.4 | async-start | bytes 2433024 | tf_op jit(solution)/shard_map/reduce_scatter | solution.py:214
  104.7 336.6 %reduce-scatter.3.cloned.1.call-start = ((), (), s32[]{:S(2)}) async-start(), calls=%async_computation.3 | async-start | bytes 2433024 | tf_op jit(solution)/shard_map/reduce_scatter | solution.py:214
  108.7 125.1 %copy-start.11 = (f32[384]{0:T(512)S(1)}, f32[384]{0:T(512)}, u32[]{:S(2)}) copy-start(f32[384]{0:T(512)} %copy-done.10) | copy-start | bytes 4612
  108.7 125.1 %copy-start.13 = (f32[384]{0:T(512)S(1)}, f32[384]{0:T(512)}, u32[]{:S(2)}) copy-start(f32[384]{0:T(512)} %copy-done.12) | copy-start | bytes 4612
  108.7 125.1 %copy-start.15 = (f32[384]{0:T(512)S(1)}, f32[384]{0:T(512)}, u32[]{:S(2)}) copy-start(f32[384]{0:T(512)} %copy-done.14) | copy-start | bytes 4612
  108.7 125.1 %copy-start.17 = (f32[384]{0:T(512)S(1)}, f32[384]{0:T(512)}, u32[]{:S(2)}) copy-start(f32[384]{0:T(512)} %copy-done.16) | copy-start | bytes 4612
  108.7 125.1 %copy-start.19 = (f32[384]{0:T(512)S(1)}, f32[384]{0:T(512)}, u32[]{:S(2)}) copy-start(f32[384]{0:T(512)} %copy-done.18) | copy-start | bytes 4612
  108.7 125.1 %copy-start.21 = (f32[384]{0:T(512)S(1)}, f32[384]{0:T(512)}, u32[]{:S(2)}) copy-start(f32[384]{0:T(512)} %copy-done.20) | copy-start | bytes 4612
  108.7 125.1 %copy-start.23 = (f32[384]{0:T(512)S(1)}, f32[384]{0:T(512)}, u32[]{:S(2)}) copy-start(f32[384]{0:T(512)} %copy-done.22) | copy-start | bytes 4612
  108.7 125.1 %copy-start.25 = (f32[384]{0:T(512)S(1)}, f32[384]{0:T(512)}, u32[]{:S(2)}) copy-start(f32[384]{0:T(512)} %copy-done.24) | copy-start | bytes 4612
  108.8 125.1 %copy-start.27 = (f32[384]{0:T(512)S(1)}, f32[384]{0:T(512)}, u32[]{:S(2)}) copy-start(f32[384]{0:T(512)} %copy-done.26) | copy-start | bytes 4612
  108.8 125.1 %copy-start.29 = (f32[384]{0:T(512)S(1)}, f32[384]{0:T(512)}, u32[]{:S(2)}) copy-start(f32[384]{0:T(512)} %copy-done.28) | copy-start | bytes 4612
  108.8 125.1 %copy-start.31 = (f32[384]{0:T(512)S(1)}, f32[384]{0:T(512)}, u32[]{:S(2)}) copy-start(f32[384]{0:T(512)} %copy-done.30) | copy-start | bytes 4612
  108.8 125.1 %copy-start.33 = (f32[384]{0:T(512)S(1)}, f32[384]{0:T(512)}, u32[]{:S(2)}) copy-start(f32[384]{0:T(512)} %copy-done.32) | copy-start | bytes 4612
  108.8 125.1 %copy-start.35 = (f32[384]{0:T(512)S(1)}, f32[384]{0:T(512)}, u32[]{:S(2)}) copy-start(f32[384]{0:T(512)} %copy-done.34) | copy-start | bytes 4612
  109.1 7.1 %collective-permute-start.13 = (bf16[3,16,384]{2,1,0:T(8,128)(2,1)S(1)}, bf16[3,16,384]{2,1,0:T(8,128)(2,1)S(1)}, u32[]{:S(2)}, u32[]{:S(2)}) collective-permute-start(bf16[3,16,384]{2,1,0:T(8,128)(2,1)S(1)} %get-tuple-element.236), channel_id=1, source_target_pairs={{4,0},{8,4},{12,8},{16,12},{20,16},{24,20},{28,24},{5,1},{9,5},{13... | collective-permute-start | bytes 110600 | tf_op jit(solution)/shard_map/ppermute | solution.py:21
  110.4 7.4 %collective-permute-start.12 = (bf16[3,16,384]{2,1,0:T(8,128)(2,1)S(1)}, bf16[3,16,384]{2,1,0:T(8,128)(2,1)S(1)}, u32[]{:S(2)}, u32[]{:S(2)}) collective-permute-start(bf16[3,16,384]{2,1,0:T(8,128)(2,1)S(1)} %get-tuple-element.235), channel_id=1, source_target_pairs={{0,4},{4,8},{8,12},{12,16},{16,20},{20,24},{24,28},{1,5},{5,9},{9,... | collective-permute-start | bytes 110600 | tf_op jit(solution)/shard_map/ppermute | solution.py:18
  117.8 115.8 %collective-permute-start.15 = (bf16[22,3,384]{2,1,0:T(4,128)(2,1)S(1)}, bf16[22,3,384]{2,1,0:T(4,128)(2,1)S(1)}, u32[]{:S(2)}, u32[]{:S(2)}) collective-permute-start(bf16[22,3,384]{2,1,0:T(4,128)(2,1)S(1)} %get-tuple-element.228), channel_id=1, source_target_pairs={{1,0},{2,1},{3,2},{5,4},{6,5},{7,6},{9,8},{10,9},{11,10},{13,12},{... | collective-permute-start | bytes 152072 | tf_op jit(solution)/shard_map/ppermute | solution.py:21
  119.1 114.5 %collective-permute-start.14 = (bf16[22,3,384]{2,1,0:T(4,128)(2,1)S(1)}, bf16[22,3,384]{2,1,0:T(4,128)(2,1)S(1)}, u32[]{:S(2)}, u32[]{:S(2)}) collective-permute-start(bf16[22,3,384]{2,1,0:T(4,128)(2,1)S(1)} %get-tuple-element.227), channel_id=1, source_target_pairs={{0,1},{1,2},{2,3},{4,5},{5,6},{6,7},{8,9},{9,10},{10,11},{12,13},{... | collective-permute-start | bytes 152072 | tf_op jit(solution)/shard_map/ppermute | solution.py:18
  (115 other events, 4071.0 us)
Sparse Core Ops, SparseCore 0:
  103.0 127.5 all-reduce.1
  236.0 101.0 reduce-scatter.4
  343.2 98.0 reduce-scatter.2

commit v2 on v0

v2 whole, which is shorter than its diff:
```python
import functools
import math

import jax
import jax.numpy as jnp
from jax import lax
from jax.experimental import pallas as pl
from jax.experimental.pallas import tpu as pltpu
from jax.sharding import PartitionSpec as P

EPSILON = 1e-06
INV_ROOT_TAU = 0.3989422804014327
HALF_LOG2E = 0.7213475204444817
ERFC_SLOPE = 0.4 * 0.7071067811865476
ERFC_TERMS = (
    0.22479419400284972,
    0.2383621945582281,
    0.12991301634379934,
    0.4353236101490443,
    -0.41611664430523265,
    0.7235898182708315,
    -0.41436965913692125,
    0.07850346878444278,
)
LANES = 128
HALO = 3
WIDE = 9
F32 = jnp.float32
BF16 = jnp.bfloat16


def normal_parts(x):
    bell = jnp.exp2(x * x * (-HALF_LOG2E))
    t = 1.0 / (1.0 + ERFC_SLOPE * jnp.abs(x))
    series = 0.5 * ERFC_TERMS[7]
    for term in ERFC_TERMS[6::-1]:
        series = series * t + 0.5 * term
    tail = series * t * bell
    return jnp.where(x >= 0, 1.0 - tail, tail), bell


def gelu_only(x):
    cdf, _ = normal_parts(x)
    return x * cdf


def gelu_parts(x):
    cdf, bell = normal_parts(x)
    return x * cdf, cdf + x * bell * INV_ROOT_TAU


def strip_rows(rows, cols):
    most = max(1, 288 // cols)
    return max(d for d in range(1, rows + 1) if rows % d == 0 and d <= most)


def conv_pass(source, row0, col0, taps, target, rows, cols):
    strip = strip_rows(rows, cols)
    groups = source.shape[0]

    def one_strip(step, carry):
        g = step // (rows // strip)
        top = (step % (rows // strip)) * strip
        sums = [jnp.zeros((cols, LANES), F32) for _ in range(strip)]
        for b in range(7):
            weights = [taps[g, pl.ds(7 * a + b, 1), :] for a in range(7)]
            for r in range(strip + 6):
                line = source[g, row0 + top + r, pl.ds(col0 + b, cols), :]
                for a in range(7):
                    if 0 <= r - a < strip:
                        sums[r - a] = sums[r - a] + weights[a] * line
        for i in range(strip):
            target[g, top + i] = sums[i]
        return carry

    lax.fori_loop(0, groups * (rows // strip), one_strip, 0)


def tap_pass(source, row0, col0, grad, grow0, gcol0, target, rows, cols):
    for g in range(source.shape[0]):
        lanes = slice(g * LANES, (g + 1) * LANES)
        for b in range(7):
            def one_row(i, sums):
                line = grad[g, grow0 + i, pl.ds(gcol0, cols), :]
                out = []
                for a in range(7):
                    part = line * source[g, row0 + i + a, pl.ds(col0 + b, cols), :]
                    out.append(sums[a] + part.reshape(cols // 8, 8, LANES).sum(0))
                return tuple(out)

            sums = lax.fori_loop(
                0, rows, one_row, tuple(jnp.zeros((8, LANES), F32) for _ in range(7)), unroll=4
            )
            for a in range(7):
                target[pl.ds(7 * a + b, 1), lanes] = jnp.sum(sums[a], axis=0, keepdims=True)


def joined(ref, rows, cols=slice(None)):
    parts = [ref[g, rows, cols, :] for g in range(ref.shape[0])]
    return jnp.concatenate([p.reshape(-1, LANES) for p in parts], axis=1)


def split_to(ref, rows, value, shape):
    for g in range(ref.shape[0]):
        ref[g, rows] = value[:, g * LANES : (g + 1) * LANES].reshape(*shape, LANES)


def norm_parts(z):
    center = z - jnp.mean(z, axis=-1, keepdims=True)
    inv = lax.rsqrt(jnp.mean(center * center, axis=-1, keepdims=True) + EPSILON)
    return center * inv, inv


def norm_back(dn, hat, inv, gain):
    scaled = dn * gain
    return inv * (
        scaled
        - jnp.mean(scaled, axis=-1, keepdims=True)
        - hat * jnp.mean(scaled * hat, axis=-1, keepdims=True)
    )


def dot_nn(a, b):
    return jnp.dot(a, b, preferred_element_type=F32)


def dot_nt(a, b):
    return lax.dot_general(a, b, (((1,), (1,)), ((), ())), preferred_element_type=F32)


def dot_tn(a, b):
    return lax.dot_general(a, b, (((0,), (0,)), ((), ())), preferred_element_type=F32)


def pixel_blocks(pixels):
    best = max(d for d in range(16, 257, 16) if pixels % d == 0)
    return [slice(start, start + best) for start in range(0, pixels, best)]


def hidden_chunks(hidden):
    size = 256 if hidden % 256 == 0 else hidden
    return [slice(start, start + size) for start in range(0, hidden, size)]


def mlp_grads(normed, normed_in, grad, grad_in, inside, w_in, b_in, w_out, act, gpre, dwi, dwo, db):
    pixels = grad.shape[0]
    hidden = w_in.shape[2]
    for cut in hidden_chunks(hidden):
        bias = b_in[:, cut]
        bias_sum = None
        for block in pixel_blocks(pixels):
            pre = dot_nn(normed[block, :], w_in[0, :, cut]) + bias
            value, slope = gelu_parts(pre)
            act[block, cut] = value.astype(BF16)
            gradient = dot_nn(grad[block, :], w_out[0, :, cut]) * slope
            gpre[block, cut] = gradient.astype(BF16)
            if inside is not None:
                gradient = gradient * inside[block, :1]
            part = jnp.sum(gradient, axis=0, keepdims=True)
            bias_sum = part if bias_sum is None else bias_sum + part
        db[:, cut] = bias_sum
        dwo[cut, :] = dot_tn(act[:, cut], grad_in[...]).astype(BF16)
        dwi[cut, :] = dot_tn(gpre[:, cut], normed_in[...]).astype(BF16)


def fetch_layers(triples, arrived):
    copies = [
        pltpu.make_async_copy(source.at[pl.ds(layer, 1)], target, arrived.at[i])
        for i, (source, layer, target) in enumerate(triples)
    ]
    for copy in copies:
        copy.start()
    return copies


def first_kernel(
    place, xpad, gpad, gcenter, taps, gains, shifts, w_in, w_out, b_in, dz_out, z_out, dwi, dwo, db, dgain, dshift, dk,
    xs, zs, mids, zs1, act0, hat1, inv1, normed1, normed1_in, inside, act1, gpre1,
    w_in0, w_out0, w_in1, w_out1, arrived,
):
    waits = fetch_layers(((w_in, 0, w_in0), (w_out, 0, w_out0), (w_in, 1, w_in1), (w_out, 1, w_out1)), arrived)
    groups = xs.shape[0]
    mid_rows, mid_cols = zs.shape[1:3]
    dz_rows, dz_cols = zs1.shape[1:3]
    rows, cols = z_out.shape[1:3]
    side = (mid_rows - rows) // 2
    for g in range(groups):
        xs[g] = xpad[:, :, g * LANES : (g + 1) * LANES].astype(F32)
    conv_pass(xs, 0, 5, taps.at[0], zs, mid_rows, mid_cols)
    z_out[...] = zs[:, side : side + rows, 8 : 8 + cols, :]

    strip = max(d for d in range(1, mid_rows + 1) if mid_rows % d == 0 and d * mid_cols <= 256)
    count = strip * mid_cols
    hidden = w_in0.shape[2]
    waits[0].wait()
    waits[1].wait()

    def one_strip(step, carry):
        top = step * strip
        hat, _ = norm_parts(joined(zs, pl.ds(top, strip)))
        normed = (hat * gains[0:1] + shifts[0:1]).astype(BF16)
        for cut in hidden_chunks(hidden):
            pre = dot_nn(normed, w_in0[0, :, cut]) + b_in[0, :, cut]
            act0[:, cut] = gelu_only(pre).astype(BF16)
        mixed = dot_nt(act0[...], w_out0[0])
        row = lax.broadcasted_iota(jnp.int32, (strip, mid_cols, 1), 0) + (top - side) + place[0]
        col = lax.broadcasted_iota(jnp.int32, (strip, mid_cols, 1), 1) - 8 + place[1]
        real = (row >= 0) & (row < place[2]) & (col >= 0) & (col < place[3])
        real = jnp.where(real, 1.0, 0.0).reshape(count, 1)
        base = joined(xs, pl.ds(top + HALO, strip), slice(8, 8 + mid_cols))
        mid = (base + mixed).astype(BF16).astype(F32) * real
        split_to(mids, pl.ds(top, strip), mid, (strip, mid_cols))
        return carry

    lax.fori_loop(0, mid_rows // strip, one_strip, 0)

    conv_pass(mids, 0, 2, taps.at[1], zs1, dz_rows, dz_cols)
    strip1 = max(
        d for d in range(1, dz_rows + 1) if dz_rows % d == 0 and d * dz_cols <= 64 or d == 1
    )

    def one_norm(step, carry):
        top = step * strip1
        pixels = pl.ds(pl.multiple_of(top * dz_cols, 8), strip1 * dz_cols)
        hat, inv = norm_parts(joined(zs1, pl.ds(top, strip1)))
        row = lax.broadcasted_iota(jnp.int32, (strip1, dz_cols, 1), 0) + top
        col = lax.broadcasted_iota(jnp.int32, (strip1, dz_cols, 1), 1)
        own = (row >= HALO) & (row < HALO + rows) & (col >= HALO) & (col < HALO + cols)
        own = jnp.where(own, 1.0, 0.0).reshape(strip1 * dz_cols, 1)
        normed = hat * gains[1:2] + shifts[1:2]
        hat1[pixels, :] = hat
        normed1[pixels, :] = normed
        inv1[pixels, :] = jnp.broadcast_to(inv, (strip1 * dz_cols, LANES))
        inside[pixels, :] = jnp.broadcast_to(own, (strip1 * dz_cols, LANES))
        return carry

    lax.fori_loop(0, dz_rows // strip1, one_norm, 0)
    normed1_in[...] = (normed1[...] * inside[:, :1]).astype(BF16)
    normed_b = normed1[...].astype(BF16)
    waits[2].wait()
    waits[3].wait()
    mlp_grads(
        normed_b, normed1_in, gpad, gcenter, inside, w_in1, b_in.at[1], w_out1, act1, gpre1,
        dwi, dwo, db,
    )
    gain_sum = jnp.zeros((1, groups * LANES), F32)
    shift_sum = jnp.zeros((1, groups * LANES), F32)
    pixels = dz_rows * dz_cols
    step = max(d for d in range(16, 257, 16) if pixels % d == 0)
    for start in range(0, pixels, step):
        block = slice(start, start + step)
        dn = dot_nt(gpre1[block, :], w_in1[0])
        hat = hat1[block, :]
        kept = dn * inside[block, :1]
        gain_sum += jnp.sum(kept * hat, axis=0, keepdims=True)
        shift_sum += jnp.sum(kept, axis=0, keepdims=True)
        dz = norm_back(dn, hat, inv1[block, :1], gains[1:2])
        hat1[block, :] = dz.astype(BF16).astype(F32)
    dgain[...] = gain_sum
    dshift[...] = shift_sum
    for g in range(groups):
        dz_out[g] = hat1[:, g * LANES : (g + 1) * LANES].reshape(dz_rows, dz_cols, LANES)
    tap_pass(mids, side - HALO, 5, dz_out, HALO, HALO, dk, rows, cols)


def second_kernel(
    dz1, grad, z0, xpad, taps_back, gains, shifts, w_in, w_out, b_in,
    mid_out, dz_out, dwi, dwo, db, dgain, dshift, dk,
    xs, spread, dzs, normed, gmid, act, gpre, w_in0, w_out0, arrived,
):
    waits = fetch_layers(((w_in, 0, w_in0), (w_out, 0, w_out0)), arrived)
    groups, rows, cols = z0.shape[:3]
    pixels = rows * cols
    conv_pass(dz1, 0, 0, taps_back.at[1], spread, rows, cols)
    gm = (grad[...].astype(F32) + joined(spread, slice(None))).astype(BF16)
    gmid[...] = gm
    mid_out[...] = gm
    hat, inv = norm_parts(joined(z0, slice(None)))
    normed[...] = (hat * gains[0:1] + shifts[0:1]).astype(BF16)
    waits[0].wait()
    waits[1].wait()
    mlp_grads(
        normed, normed, gmid, gmid, None, w_in0, b_in.at[0], w_out0, act, gpre, dwi, dwo, db
    )
    dn = dot_nt(gpre[...], w_in0[0])
    dgain[...] = jnp.sum(dn * hat, axis=0, keepdims=True)
    dshift[...] = jnp.sum(dn, axis=0, keepdims=True)
    dz = norm_back(dn, hat, inv, gains[0:1]).astype(BF16)
    dz_out[...] = dz
    split_to(dzs, slice(None), dz.astype(F32), (rows, cols))
    skip = xpad.shape[0] // 2 - rows // 2 - HALO
    for g in range(groups):
        xs[g] = xpad[skip : skip + rows + 2 * HALO, :, g * LANES : (g + 1) * LANES].astype(F32)
    tap_pass(xs, 0, 13, dzs, 0, 0, dk, rows, cols)


def third_kernel(dzpad, gmid, taps_back, out, dzs, spread):
    for g in range(dzs.shape[0]):
        dzs[g] = dzpad[:, :, g * LANES : (g + 1) * LANES].astype(F32)
    rows, cols = spread.shape[1:3]
    conv_pass(dzs, 0, 5, taps_back.at[0], spread, rows, cols)
    out[...] = (gmid[...].astype(F32) + joined(spread, slice(None))).astype(BF16)


def shape(*dims, dtype=F32):
    return jax.ShapeDtypeStruct(dims, dtype)


def run(kernel, outs, scratch, args, specs=None, fetched=0, name=None):
    vmem = pl.BlockSpec(memory_space=pltpu.VMEM)
    semaphores = [pltpu.SemaphoreType.DMA((fetched,))] if fetched else []
    return pl.pallas_call(
        kernel,
        out_shape=outs,
        in_specs=[
            vmem if s is None else pl.BlockSpec(memory_space=s) for s in (specs or [None] * len(args))
        ],
        out_specs=tuple(vmem for _ in outs),
        scratch_shapes=[pltpu.VMEM(s.shape, s.dtype) for s in scratch] + semaphores,
        compiler_params=pltpu.CompilerParams(vmem_limit_bytes=50 * 1024 * 1024),
        name=name,
    )(*args)


def swap_edges(low_edge, high_edge, axis):
    count = lax.axis_size(axis)
    odd = lax.axis_index(axis) % 2 == 1
    first = lax.ppermute(
        jnp.where(odd, low_edge, high_edge), axis, [(i, i ^ 1) for i in range(count) if i ^ 1 < count]
    )
    pairs = [(i, i + 1) for i in range(1, count - 1, 2)]
    second = lax.ppermute(
        jnp.where(odd, high_edge, low_edge), axis, pairs + [(j, i) for i, j in pairs]
    )
    return jnp.where(odd, first, second), jnp.where(odd, second, first)


def padded_tile(tile, width):
    low, high = swap_edges(tile[:, :width], tile[:, -width:], "cols")
    wide = jnp.concatenate([low, tile, high], axis=1)
    low, high = swap_edges(wide[:width], wide[-width:], "rows")
    return jnp.concatenate([low, wide, high], axis=0)


def padded_pair(acts, grads):
    low, high = swap_edges(
        jnp.concatenate([acts[:, :WIDE], grads[:, :HALO]], axis=1),
        jnp.concatenate([acts[:, -WIDE:], grads[:, -HALO:]], axis=1),
        "cols",
    )
    acts = jnp.concatenate([low[:, :WIDE], acts, high[:, :WIDE]], axis=1)
    grads = jnp.concatenate([low[:, WIDE:], grads, high[:, WIDE:]], axis=1)
    room = ((0, 0), (0, acts.shape[1] - grads.shape[1]), (0, 0))
    low, high = swap_edges(
        jnp.concatenate([acts[:WIDE], jnp.pad(grads[:HALO], room)], axis=0),
        jnp.concatenate([acts[-WIDE:], jnp.pad(grads[-HALO:], room)], axis=0),
        "rows",
    )
    used = grads.shape[1]
    acts = jnp.concatenate([low[:WIDE], acts, high[:WIDE]], axis=0)
    grads = jnp.concatenate([low[WIDE:, :used], grads, high[WIDE:, :used]], axis=0)
    return acts, grads


def flip_bit(value, bit):
    both = ("rows", "cols")
    total = lax.axis_size("rows") * lax.axis_size("cols")
    return lax.ppermute(value, both, [(i, i ^ (1 << bit)) for i in range(total)])


def halves(chunks, dim, mine):
    other = lax.dynamic_index_in_dim(chunks, 1 - mine, dim, keepdims=False)
    own = lax.dynamic_index_in_dim(chunks, mine, dim, keepdims=False)
    return other, own


def summed(own, got):
    return (own.astype(F32) + got.astype(F32)).astype(BF16)


def shards(activations, grad_out, kernels, norm_gains, norm_shifts, w_in, b_in, w_out):
    rows, cols, channels = activations.shape
    layers, _, hidden = w_in.shape
    groups = channels // LANES
    n_rows, n_cols = lax.axis_size("rows"), lax.axis_size("cols")
    total = n_rows * n_cols
    bits = total.bit_length() - 1
    me = lax.axis_index("rows") * n_cols + lax.axis_index("cols")
    grad_scale = 1.0 / math.sqrt(rows * cols * total)

    taps = kernels.reshape(layers, 49, groups, LANES).transpose(0, 2, 1, 3)
    taps_back = taps[:, :, ::-1]
    biases = b_in[:, None, :]

    acts, grads = padded_pair(activations, grad_out)
    gap = 16 - WIDE
    xpad = jnp.pad(acts, ((0, 0), (gap, gap), (0, 0)))
    dz_rows, dz_cols = rows + 2 * HALO, cols + 8
    spare = dz_cols - cols - 2 * HALO
    gpad = jnp.pad(grads, ((0, 0), (0, spare), (0, 0))).reshape(-1, channels)
    gcenter = jnp.pad(
        grad_out, ((HALO, HALO), (HALO, HALO + spare), (0, 0))
    ).reshape(-1, channels)
    place = jnp.stack(
        [
            lax.axis_index("rows") * rows,
            lax.axis_index("cols") * cols,
            jnp.int32(rows * n_rows),
            jnp.int32(cols * n_cols),
        ]
    ).astype(jnp.int32)

    mid_rows, mid_cols = rows + 4 * HALO, cols + 16
    count = dz_rows * dz_cols
    strip = max(d for d in range(1, mid_rows + 1) if mid_rows % d == 0 and d * mid_cols <= 256)
    weights = [shape(1, channels, hidden, dtype=BF16)] * 2
    small_outs = (
        shape(hidden, channels, dtype=BF16), shape(hidden, channels, dtype=BF16),
        shape(1, hidden), shape(1, channels), shape(1, channels), shape(49, channels),
    )
    dz1, z0, *back1 = run(
        first_kernel,
        (shape(groups, dz_rows, dz_cols, LANES), shape(groups, rows, cols, LANES)) + small_outs,
        [
            shape(groups, *xpad.shape[:2], LANES),
            shape(groups, mid_rows, mid_cols, LANES),
            shape(groups, mid_rows, mid_cols, LANES),
            shape(groups, dz_rows, dz_cols, LANES),
            shape(strip * mid_cols, hidden, dtype=BF16),
            shape(count, channels),
            shape(count, LANES),
            shape(count, channels),
            shape(count, channels, dtype=BF16),
            shape(count, LANES),
            shape(count, hidden, dtype=BF16),
            shape(count, hidden, dtype=BF16),
        ]
        + weights * 2,
        (place, xpad, gpad, gcenter, taps, norm_gains, norm_shifts, w_in, w_out, biases),
        [pltpu.SMEM] + [None] * 6 + [pl.ANY] * 2 + [None],
        fetched=4,
        name="first",
    )
    pixels = rows * cols
    grad_mid, dz0, *back0 = run(
        second_kernel,
        (shape(pixels, channels, dtype=BF16), shape(pixels, channels, dtype=BF16)) + small_outs,
        [
            shape(groups, rows + 2 * HALO, xpad.shape[1], LANES),
            shape(groups, rows, cols, LANES),
            shape(groups, rows, cols, LANES),
            shape(pixels, channels, dtype=BF16),
            shape(pixels, channels, dtype=BF16),
            shape(pixels, hidden, dtype=BF16),
            shape(pixels, hidden, dtype=BF16),
        ]
        + weights,
        (dz1, grad_out.reshape(pixels, channels), z0, xpad, taps_back, norm_gains, norm_shifts,
         w_in, w_out, biases),
        [None] * 7 + [pl.ANY] * 2 + [None],
        fetched=2,
        name="second",
    )

    mine = [(me >> k) & 1 for k in range(bits)]
    per = hidden // total
    chunks = jnp.stack(
        [grad.reshape(total, per, channels) for back in (back0, back1) for grad in back[:2]], axis=1
    )
    small = jnp.concatenate(
        [part.reshape(-1) for back in (back0, back1) for part in back[2:]]
    ).astype(BF16)
    small_len = small.shape[0]
    small = jnp.pad(small, (0, -small_len % (16 * channels))).reshape(-1, channels)
    for k in range(bits):
        size = chunks.shape[0] // 2
        send, keep = halves(chunks.reshape(size, 2, -1, channels), 1, mine[k])
        send = send.reshape(-1, channels)
        got = flip_bit(jnp.concatenate([send, small], axis=0), k)
        edge = send.shape[0]
        chunks = summed(keep, got[:edge].reshape(keep.shape))
        small = summed(small, got[edge:])
    shares = chunks.reshape(layers, 2, per, channels).astype(F32) * grad_scale
    shares = jnp.swapaxes(shares, 2, 3)
    small = (small.astype(F32) * grad_scale).reshape(-1)[:small_len].reshape(layers, -1)

    dzpad = padded_tile(dz0.reshape(rows, cols, channels), HALO)
    dzpad = jnp.pad(dzpad, ((0, 0), (5, 16 - 5 - 2 * HALO), (0, 0)))
    (grad_in,) = run(
        third_kernel,
        (shape(pixels, channels, dtype=BF16),),
        [shape(groups, *dzpad.shape[:2], LANES), shape(groups, rows, cols, LANES)],
        (dzpad, grad_mid, taps_back),
        name="third",
    )
    cuts = [0, hidden, hidden + channels, hidden + 2 * channels, hidden + 51 * channels]
    parts = [small[:, a:b] for a, b in zip(cuts[:-1], cuts[1:])]
    return (
        grad_in.reshape(rows, cols, channels),
        parts[3].reshape(layers, 7, 7, channels),
        parts[1],
        parts[2],
        parts[0],
        shares[:, 0],
        shares[:, 1],
    )


def solution(mesh):
    tile = P("rows", "cols", None)
    sliced = P(None, None, ("rows", "cols"))
    return jax.shard_map(
        shards,
        mesh=mesh,
        in_specs=(tile, tile, P(), P(), P(), P(), P(), P()),
        out_specs=(tile, P(), P(), P(), P(), sliced, sliced),
        check_vma=False,
    )
```

time: 354 us -> 164 us (0.46)
  waiting for transfers between devices: 146 us -> 72.5 us
  blocking collectives: 46.4 us -> 0 us
  Pallas kernels: 0 us -> 46 us
  local copies, waits for them, and re-layouts: 53.7 us -> 13.6 us
  other arithmetic: 34.7 us -> 11.1 us
  starting transfers between devices: 39.4 us -> 18.9 us
  between operations: 16.8 us -> 1.19 us
  matrix products: 14.8 us -> 0 us
    psum x1 -> x0, waiting for transfers between devices: 129 us -> none  [shards(): lax.psum((jnp.stack([back_one[1], back_two[1]]) * grad_scale, jnp.stack([...]
    ppermute x16 -> x13, waiting for transfers between devices: 17.4 us -> 72.5 us  [the longest x5 59.5 us: flip_bit(): return lax.ppermute(value, both, [(i, i ^ 1 << bit) for i in range(total)])]
    psum x1 -> x0, blocking collectives: 46.4 us -> none  [shards(): lax.psum((jnp.stack([back_one[1], back_two[1]]) * grad_scale, jnp.stack([...]
    pallas_call x0 -> x3, Pallas kernels: none -> 46 us  [run(): pl.pallas_call(kernel, out_shape=outs, in_specs=[vmem if s is None else p...]
    another operation x108 -> x0, local copies, waits for them, and re-layouts: 23.5 us -> none  [the longest x100 20.7 us: kernel_grad(): return jnp.stack(kernel_taps).reshape(7, 7, grad_z.shape[2])]
    ppermute x16 -> x13, starting transfers between devices: 39.3 us -> 18.9 us  [the longest x5 11.5 us: flip_bit(): return lax.ppermute(value, both, [(i, i ^ 1 << bit) for i in range(total)])]
    mul x2 -> x0, local copies, waits for them, and re-layouts: 16.3 us -> none  [the longest x1 8.17 us: shards(): stacked_in = jnp.stack([back_one[5], back_two[5]]) * grad_scale]
    dot_general x11 -> x0, matrix products: 14.8 us -> none  [the longest x2 3.89 us: layer_back(): lax.dot_general(grad_flat, act_b, (((0,), (0,)), ((), ())), preferred_ele...]
  transfers between devices with their start and end apart: 17 -> 13, of which waited for: 7 -> 7; matrix products, arithmetic and copies ran while one was open for 10% -> 1% of each run, Pallas kernels for 0% -> 2%
where the time goes in v2:
time: 164 us; the launch traced here: 163 us
  waiting for transfers between devices  72.5 us (44%)
  Pallas kernels  46 us (28%)
  starting transfers between devices  18.9 us (12%)
  local copies, waits for them, and re-layouts  13.6 us (8%)
  other arithmetic  11.1 us (7%)
    ppermute x5, waiting for transfers between devices, flip_bit(): return lax.ppermute(value, both, [(i, i ^ 1 << bit) for i in range(total)])  59.5 us
    pallas_call x3, Pallas kernels, run(): pl.pallas_call(kernel, out_shape=outs, in_specs=[vmem if s is None else p...  46 us
    ppermute x4, waiting for transfers between devices, swap_edges(): lax.ppermute(jnp.where(odd, low_edge, high_edge), axis, [(i, i ^ 1) for i...  13 us
    ppermute x5, starting transfers between devices, flip_bit(): return lax.ppermute(value, both, [(i, i ^ 1 << bit) for i in range(total)])  11.5 us
    ppermute x4, starting transfers between devices, swap_edges(): lax.ppermute(jnp.where(odd, low_edge, high_edge), axis, [(i, i ^ 1) for i...  4.75 us
    slice x4, local copies, waits for them, and re-layouts, shards(): chunks = summed(keep, got[:edge].reshape(keep.shape))  3.38 us
  transfers between devices with their start and end apart: 13, of which 7 were waited for; matrix products, arithmetic and copies ran while one was open for 1% of the time, Pallas kernels for 2%

profile of v2, /device:TPU:0, one launch (start us, length us, event | category | flops | bytes accessed | tf_op | source)
XLA Modules:
  0.0 163.4 jit_solution(18187823059012531269)
XLA Ops:
  0.6 1.0 fusion.39
  1.6 1.1 fusion.38
  5.7 3.0 %collective-permute-start.2 = (bf16[12,34,384]{2,1,0:T(8,128)(2,1)S(1)}, bf16[12,34,384]{2,1,0:T(8,128)(2,1)S(1)}, u32[]{:S(2)}, u32[]{:S(2)}) collective-permute-start(bf16[12,34,384]{2,1,0:T(8,128)(2,1)S(1)} %get-tuple-element.50), channel_id=1, source_target_pairs={{0,4},{4,0},{8,12},{12,8},{16,20},{20,16},{24,28},{28,24},{1,5},{5... | collective-permute-start | bytes 940040 | tf_op jit(solution)/shard_map/ppermute | solution.py:328
  8.7 0.7 collective-permute-start.3
  9.7 12.6 %collective-permute-done.2 = bf16[12,34,384]{2,1,0:T(8,128)(2,1)S(1)} collective-permute-done((bf16[12,34,384]{2,1,0:T(8,128)(2,1)S(1)}, bf16[12,34,384]{2,1,0:T(8,128)(2,1)S(1)}, u32[]{:S(2)}, u32[]{:S(2)}) %collective-permute-start.2) | collective-permute-done | bytes 313376 | tf_op jit(solution)/shard_map/ppermute | solution.py:328
  22.5 1.5 select_maximum_fusion.xpad
  24.3 32.0 %first.1 = (f32[3,22,24,128]{3,2,1,0:T(8,128)S(1)}, f32[3,16,16,128]{3,2,1,0:T(8,128)S(1)}, bf16[1536,384]{1,0:T(8,128)(2,1)S(1)}, bf16[1536,384]{1,0:T(8,128)(2...) custom-call(s32[4]{0:T(128)S(1)} %pad_add_fusion.place, ...), custom_call_target="tpu_custom_call" | custom-call | tf_op jit(solution)/shard_map/first/pallas_call | solution.py:312
  56.3 11.1 %second.1 = (bf16[256,384]{1,0:T(8,128)(2,1)S(1)}, bf16[256,384]{1,0:T(8,128)(2,1)S(1)}, bf16[1536,384]{1,0:T(8,128)(2,1)S(1)}, bf16[1536,384]{1,0:T(8,128)(2,1)...) custom-call(f32[3,22,24,128]{3,2,1,0:T(8,128)S(1)} %get-tuple-element.23.dz1, ...), custom_call_target="tpu_custom_call" | custom-call | tf_op jit(solution)/shard_map/second/pallas_call | solution.py:312
  70.2 2.0 %pad_maximum_fusion = bf16[32,4,48,384]{3,2,1,0:T(8,128)(2,1)S(1)} fusion(bf16[32,1,48,384]{3,2,1,0:T(8,128)(2,1)} %bitcast.93, bf16[32,1,48,384]{3,2,1,0:T(8,128)(2,1)S(1)} %bitcast.77, bf16[32,1,48,384]{3,2,1,0:T(8,128)(2,1)} %bitcast.94, bf16[32,1,48,384]{3,2,1,0:T(8,128)(2,1)S(1)} %bitcast.78), kind=kLoop, calls=%fused_computation | loop fusion | flops 7077888 | bytes 9437184 | tf_op jit(solution)/shard_map/stack | solution.py:467
  72.7 1.7 %pad_maximum_fusion.1 = bf16[3184,384]{1,0:T(8,128)(2,1)} fusion(bf16[112,384]{1,0:T(8,128)(2,1)S(1)} %reshape.160, bf16[3072,384]{1,0:T(8,128)(2,1)S(1)} %bitcast.81), kind=kLoop, calls=%fused_computation.6 | loop fusion | flops 4890624 | bytes 4890624 | tf_op jit(solution)/shard_map/concatenate | solution.py:479
  74.4 3.3 %collective-permute-start.8 = (bf16[3184,384]{1,0:T(8,128)(2,1)}, bf16[3184,384]{1,0:T(8,128)(2,1)}, u32[]{:S(2)}, u32[]{:S(2)}) collective-permute-start(bf16[3184,384]{1,0:T(8,128)(2,1)} %pad_maximum_fusion.1), channel_id=1, source_target_pairs={{0,1},{1,0},{2,3},{3,2},{4,5},{5,4},{6,7},{7,6},{8,9},{9,8},{10,11... | collective-permute-start | bytes 7335944 | tf_op jit(solution)/shard_map/ppermute | solution.py:368
  77.7 4.6 %collective-permute-done.8 = bf16[3184,384]{1,0:T(8,128)(2,1)} collective-permute-done((bf16[3184,384]{1,0:T(8,128)(2,1)}, bf16[3184,384]{1,0:T(8,128)(2,1)}, u32[]{:S(2)}, u32[]{:S(2)}) %collective-permute-start.8) | collective-permute-done | bytes 2445344 | tf_op jit(solution)/shard_map/ppermute | solution.py:368
  82.3 1.9 %slice.162 = bf16[3072,384]{1,0:T(8,128)(2,1)S(1)} slice(bf16[3184,384]{1,0:T(8,128)(2,1)} %collective-permute-done.8), slice={[0:3072], [0:384]} | slice | bytes 4718592 | tf_op jit(solution)/shard_map/slice | solution.py:481
  84.3 0.7 fusion
  85.2 0.9 add_convert_fusion.4
  86.1 1.2 pad_maximum_fusion.2
  87.3 0.9 collective-permute-start.9
  88.2 29.5 %collective-permute-done.9 = bf16[1648,384]{1,0:T(8,128)(2,1)} collective-permute-done((bf16[1648,384]{1,0:T(8,128)(2,1)}, bf16[1648,384]{1,0:T(8,128)(2,1)}, u32[]{:S(2)}, u32[]{:S(2)}) %collective-permute-start.9) | collective-permute-done | bytes 1265696 | tf_op jit(solution)/shard_map/ppermute | solution.py:368
  117.7 1.4 slice.164
  119.4 0.9 constant_dynamic-slice_fusion.1
  120.4 0.9 add_convert_fusion.3
  121.4 2.2 %collective-permute-start.10 = (bf16[880,384]{1,0:T(8,128)(2,1)S(1)}, bf16[880,384]{1,0:T(8,128)(2,1)S(1)}, u32[]{:S(2)}, u32[]{:S(2)}) collective-permute-start(bf16[880,384]{1,0:T(8,128)(2,1)S(1)} %pad_maximum_fusion.3), channel_id=1, source_target_pairs={{0,4},{1,5},{2,6},{3,7},{4,0},{5,1},{6,2},{7,3},{8,12},{9,13},{10,... | collective-permute-start | bytes 2027528 | tf_op jit(solution)/shard_map/ppermute | solution.py:368
  124.4 14.1 %collective-permute-done.10 = bf16[880,384]{1,0:T(8,128)(2,1)S(1)} collective-permute-done((bf16[880,384]{1,0:T(8,128)(2,1)S(1)}, bf16[880,384]{1,0:T(8,128)(2,1)S(1)}, u32[]{:S(2)}, u32[]{:S(2)}) %collective-permute-start.10) | collective-permute-done | bytes 675872 | tf_op jit(solution)/shard_map/ppermute | solution.py:368
  138.9 2.2 %collective-permute-start.11 = (bf16[496,384]{1,0:T(8,128)(2,1)S(1)}, bf16[496,384]{1,0:T(8,128)(2,1)S(1)}, u32[]{:S(2)}, u32[]{:S(2)}) collective-permute-start(bf16[496,384]{1,0:T(8,128)(2,1)S(1)} %pad_maximum_fusion.5), channel_id=1, source_target_pairs={{0,8},{1,9},{2,10},{3,11},{4,12},{5,13},{6,14},{7,15},{8,0},{9,1},... | collective-permute-start | bytes 1142792 | tf_op jit(solution)/shard_map/ppermute | solution.py:368
  141.2 1.2 collective-permute-start.6
  142.5 0.7 collective-permute-start.7
  143.1 6.2 %collective-permute-done.11 = bf16[496,384]{1,0:T(8,128)(2,1)S(1)} collective-permute-done((bf16[496,384]{1,0:T(8,128)(2,1)S(1)}, bf16[496,384]{1,0:T(8,128)(2,1)S(1)}, u32[]{:S(2)}, u32[]{:S(2)}) %collective-permute-start.11) | collective-permute-done | bytes 380960 | tf_op jit(solution)/shard_map/ppermute | solution.py:368
  149.6 2.8 %collective-permute-start.12 = (bf16[304,384]{1,0:T(8,128)(2,1)S(1)}, bf16[304,384]{1,0:T(8,128)(2,1)S(1)}, u32[]{:S(2)}, u32[]{:S(2)}) collective-permute-start(bf16[304,384]{1,0:T(8,128)(2,1)S(1)} %pad_maximum_fusion.8), channel_id=1, source_target_pairs={{0,16},{1,17},{2,18},{3,19},{4,20},{5,21},{6,22},{7,23},{8,24},{9,... | collective-permute-start | bytes 700424 | tf_op jit(solution)/shard_map/ppermute | solution.py:368
  152.6 2.9 %third.1 = bf16[256,384]{1,0:T(8,128)(2,1)} custom-call(bf16[22,32,384]{2,1,0:T(8,128)(2,1)S(1)} %select_maximum_fusion.2.dzpad, bf16[256,384]{1,0:T(8,128)(2,1)S(1)} %get-tuple-element.26.gmid, f32[2,3,49,128]{3,2,1,0:T(8,128)S(1)} %rev.3.taps_back), custom_call_target="tpu_custom_call" | custom-call | tf_op jit(solution)/shard_map/third/pallas_call | solution.py:312
  155.5 5.1 %collective-permute-done.12 = bf16[304,384]{1,0:T(8,128)(2,1)S(1)} collective-permute-done((bf16[304,384]{1,0:T(8,128)(2,1)S(1)}, bf16[304,384]{1,0:T(8,128)(2,1)S(1)}, u32[]{:S(2)}, u32[]{:S(2)}) %collective-permute-start.12) | collective-permute-done | bytes 233504 | tf_op jit(solution)/shard_map/ppermute | solution.py:368
  160.7 0.7 slice.172
  162.6 0.7 slice_bitcast_fusion
  (89 shorter events, 10.4 us)
Async XLA Ops:
  1.6 3.0 %copy-start.3 = (bf16[16,16,384]{2,1,0:T(8,128)(2,1)S(1)}, bf16[16,16,384]{2,1,0:T(8,128)(2,1)}, u32[]{:S(2)}) copy-start(bf16[16,16,384]{2,1,0:T(8,128)(2,1)} %param.8) | copy-start | bytes 589828
  2.9 1.6 collective-permute-start
  3.5 1.1 collective-permute-start.1
  4.6 0.9 copy-start
  5.5 3.9 %copy-start.5 = (f32[2,7,7,384]{3,0,2,1:T(2,128)S(1)}, f32[2,7,7,384]{3,0,2,1:T(2,128)}, u32[]{:S(2)}) copy-start(f32[2,7,7,384]{3,0,2,1:T(2,128)} %param.10) | copy-start | bytes 451588
  5.5 4.1 %copy-start.6 = (f32[2,1536]{1,0:T(2,128)S(1)}, f32[2,1536]{1,0:T(2,128)}, u32[]{:S(2)}) copy-start(f32[2,1536]{1,0:T(2,128)} %param.14) | copy-start | bytes 36868
  5.7 16.6 %collective-permute-start.2 = (bf16[12,34,384]{2,1,0:T(8,128)(2,1)S(1)}, bf16[12,34,384]{2,1,0:T(8,128)(2,1)S(1)}, u32[]{:S(2)}, u32[]{:S(2)}) collective-permute-start(bf16[12,34,384]{2,1,0:T(8,128)(2,1)S(1)} %get-tuple-element.50), channel_id=1, source_target_pairs={{0,4},{4,0},{8,12},{12,8},{16,20},{20,16},{24,28},{28,24},{1,5},{5... | collective-permute-start | bytes 940040 | tf_op jit(solution)/shard_map/ppermute | solution.py:328
  8.7 13.7 %collective-permute-start.3 = (bf16[12,34,384]{2,1,0:T(8,128)(2,1)S(1)}, bf16[12,34,384]{2,1,0:T(8,128)(2,1)S(1)}, u32[]{:S(2)}, u32[]{:S(2)}) collective-permute-start(bf16[12,34,384]{2,1,0:T(8,128)(2,1)S(1)} %get-tuple-element.51), channel_id=1, source_target_pairs={{4,8},{12,16},{20,24},{8,4},{16,12},{24,20},{5,9},{13,17},{21,25},... | collective-permute-start | bytes 940040 | tf_op jit(solution)/shard_map/ppermute | solution.py:332
  22.5 1.8 %copy-start.1 = (f32[2,384]{1,0:T(2,128)S(1)}, f32[2,384]{1,0:T(2,128)}, u32[]{:S(2)}) copy-start(f32[2,384]{1,0:T(2,128)} %gains.3) | copy-start | bytes 9220
  22.5 1.8 %copy-start.2 = (f32[2,384]{1,0:T(2,128)S(1)}, f32[2,384]{1,0:T(2,128)}, u32[]{:S(2)}) copy-start(f32[2,384]{1,0:T(2,128)} %shifts.3) | copy-start | bytes 9220
  74.4 8.0 %collective-permute-start.8 = (bf16[3184,384]{1,0:T(8,128)(2,1)}, bf16[3184,384]{1,0:T(8,128)(2,1)}, u32[]{:S(2)}, u32[]{:S(2)}) collective-permute-start(bf16[3184,384]{1,0:T(8,128)(2,1)} %pad_maximum_fusion.1), channel_id=1, source_target_pairs={{0,1},{1,0},{2,3},{3,2},{4,5},{5,4},{6,7},{7,6},{8,9},{9,8},{10,11... | collective-permute-start | bytes 7335944 | tf_op jit(solution)/shard_map/ppermute | solution.py:368
  87.3 30.4 %collective-permute-start.9 = (bf16[1648,384]{1,0:T(8,128)(2,1)}, bf16[1648,384]{1,0:T(8,128)(2,1)}, u32[]{:S(2)}, u32[]{:S(2)}) collective-permute-start(bf16[1648,384]{1,0:T(8,128)(2,1)} %pad_maximum_fusion.2), channel_id=1, source_target_pairs={{0,2},{1,3},{2,0},{3,1},{4,6},{5,7},{6,4},{7,5},{8,10},{9,11},{10,... | collective-permute-start | bytes 3797000 | tf_op jit(solution)/shard_map/ppermute | solution.py:368
  121.3 17.3 %copy-start.4 = (bf16[4,1,192,384]{3,2,1,0:T(8,128)(2,1)S(1)}, bf16[4,1,192,384]{3,2,1,0:T(8,128)(2,1)}, u32[]{:S(2)}) copy-start(bf16[4,1,192,384]{3,2,1,0:T(8,128)(2,1)} %get-tuple-element.46) | copy-start | bytes 1769476
  121.4 17.1 %collective-permute-start.10 = (bf16[880,384]{1,0:T(8,128)(2,1)S(1)}, bf16[880,384]{1,0:T(8,128)(2,1)S(1)}, u32[]{:S(2)}, u32[]{:S(2)}) collective-permute-start(bf16[880,384]{1,0:T(8,128)(2,1)S(1)} %pad_maximum_fusion.3), channel_id=1, source_target_pairs={{0,4},{1,5},{2,6},{3,7},{4,0},{5,1},{6,2},{7,3},{8,12},{9,13},{10,... | collective-permute-start | bytes 2027528 | tf_op jit(solution)/shard_map/ppermute | solution.py:368
  123.7 17.4 %collective-permute-start.4 = (bf16[16,3,384]{2,1,0:T(4,128)(2,1)S(1)}, bf16[16,3,384]{2,1,0:T(4,128)(2,1)S(1)}, u32[]{:S(2)}, u32[]{:S(2)}) collective-permute-start(bf16[16,3,384]{2,1,0:T(4,128)(2,1)S(1)} %get-tuple-element.62), channel_id=1, source_target_pairs={{0,1},{1,0},{2,3},{3,2},{4,5},{5,4},{6,7},{7,6},{8,9},{9,8},{10,11... | collective-permute-start | bytes 110600 | tf_op jit(solution)/shard_map/ppermute | solution.py:328
  123.8 17.3 %collective-permute-start.5 = (bf16[16,3,384]{2,1,0:T(4,128)(2,1)S(1)}, bf16[16,3,384]{2,1,0:T(4,128)(2,1)S(1)}, u32[]{:S(2)}, u32[]{:S(2)}) collective-permute-start(bf16[16,3,384]{2,1,0:T(4,128)(2,1)S(1)} %get-tuple-element.63), channel_id=1, source_target_pairs={{1,2},{2,1},{5,6},{6,5},{9,10},{10,9},{13,14},{14,13},{17,18},{18,... | collective-permute-start | bytes 110600 | tf_op jit(solution)/shard_map/ppermute | solution.py:332
  138.9 10.5 %collective-permute-start.11 = (bf16[496,384]{1,0:T(8,128)(2,1)S(1)}, bf16[496,384]{1,0:T(8,128)(2,1)S(1)}, u32[]{:S(2)}, u32[]{:S(2)}) collective-permute-start(bf16[496,384]{1,0:T(8,128)(2,1)S(1)} %pad_maximum_fusion.5), channel_id=1, source_target_pairs={{0,8},{1,9},{2,10},{3,11},{4,12},{5,13},{6,14},{7,15},{8,0},{9,1},... | collective-permute-start | bytes 1142792 | tf_op jit(solution)/shard_map/ppermute | solution.py:368
  141.2 11.2 %collective-permute-start.6 = (bf16[3,22,384]{2,1,0:T(8,128)(2,1)S(1)}, bf16[3,22,384]{2,1,0:T(8,128)(2,1)S(1)}, u32[]{:S(2)}, u32[]{:S(2)}) collective-permute-start(bf16[3,22,384]{2,1,0:T(8,128)(2,1)S(1)} %get-tuple-element.39), channel_id=1, source_target_pairs={{0,4},{4,0},{8,12},{12,8},{16,20},{20,16},{24,28},{28,24},{1,5},{5... | collective-permute-start | bytes 152072 | tf_op jit(solution)/shard_map/ppermute | solution.py:328
  142.5 9.9 %collective-permute-start.7 = (bf16[3,22,384]{2,1,0:T(8,128)(2,1)S(1)}, bf16[3,22,384]{2,1,0:T(8,128)(2,1)S(1)}, u32[]{:S(2)}, u32[]{:S(2)}) collective-permute-start(bf16[3,22,384]{2,1,0:T(8,128)(2,1)S(1)} %broadcast_select_fusion.10), channel_id=1, source_target_pairs={{4,8},{12,16},{20,24},{8,4},{16,12},{24,20},{5,9},{13,17},{21,25},... | collective-permute-start | bytes 152072 | tf_op jit(solution)/shard_map/ppermute | solution.py:332
  149.6 11.0 %collective-permute-start.12 = (bf16[304,384]{1,0:T(8,128)(2,1)S(1)}, bf16[304,384]{1,0:T(8,128)(2,1)S(1)}, u32[]{:S(2)}, u32[]{:S(2)}) collective-permute-start(bf16[304,384]{1,0:T(8,128)(2,1)S(1)} %pad_maximum_fusion.8), channel_id=1, source_target_pairs={{0,16},{1,17},{2,18},{3,19},{4,20},{5,21},{6,22},{7,23},{8,24},{9,... | collective-permute-start | bytes 700424 | tf_op jit(solution)/shard_map/ppermute | solution.py:368

commit v3 on v2

v3 whole, which is shorter than its diff:
```python
import functools
import math

import jax
import jax.numpy as jnp
from jax import lax
from jax.experimental import pallas as pl
from jax.experimental.pallas import tpu as pltpu
from jax.sharding import PartitionSpec as P

EPSILON = 1e-06
INV_ROOT_TAU = 0.3989422804014327
HALF_LOG2E = 0.7213475204444817
ERFC_SLOPE = 0.4 * 0.7071067811865476
ERFC_TERMS = (
    0.22479419400284972,
    0.2383621945582281,
    0.12991301634379934,
    0.4353236101490443,
    -0.41611664430523265,
    0.7235898182708315,
    -0.41436965913692125,
    0.07850346878444278,
)
LANES = 128
HALO = 3
WIDE = 2 * HALO
F32 = jnp.float32
BF16 = jnp.bfloat16


def normal_parts(x):
    bell = jnp.exp2(x * x * (-HALF_LOG2E))
    t = 1.0 / (1.0 + ERFC_SLOPE * jnp.abs(x))
    series = 0.5 * ERFC_TERMS[7]
    for term in ERFC_TERMS[6::-1]:
        series = series * t + 0.5 * term
    tail = series * t * bell
    return jnp.where(x >= 0, 1.0 - tail, tail), bell


def gelu_only(x):
    cdf, _ = normal_parts(x)
    return x * cdf


def gelu_parts(x):
    cdf, bell = normal_parts(x)
    return x * cdf, cdf + x * bell * INV_ROOT_TAU


def strip_rows(rows, cols):
    most = max(1, 288 // cols)
    return max(d for d in range(1, rows + 1) if rows % d == 0 and d <= most)


def conv_pass(source, row0, col0, taps, target, rows, cols):
    strip = strip_rows(rows, cols)
    groups = source.shape[0]

    def one_strip(step, carry):
        g = step // (rows // strip)
        top = (step % (rows // strip)) * strip
        sums = [jnp.zeros((cols, LANES), F32) for _ in range(strip)]
        for b in range(7):
            weights = [taps[g, pl.ds(7 * a + b, 1), :] for a in range(7)]
            for r in range(strip + 6):
                line = source[g, row0 + top + r, pl.ds(col0 + b, cols), :]
                for a in range(7):
                    if 0 <= r - a < strip:
                        sums[r - a] = sums[r - a] + weights[a] * line
        for i in range(strip):
            target[g, top + i] = sums[i]
        return carry

    lax.fori_loop(0, groups * (rows // strip), one_strip, 0)


def tap_pass(source, row0, col0, grad, grow0, gcol0, target, first, rows, cols):
    for g in range(source.shape[0]):
        lanes = slice(g * LANES, (g + 1) * LANES)
        for b in range(7):
            def one_row(i, sums):
                line = grad[g, grow0 + i, pl.ds(gcol0, cols), :]
                out = []
                for a in range(7):
                    part = line * source[g, row0 + i + a, pl.ds(col0 + b, cols), :]
                    out.append(sums[a] + part.reshape(cols // 8, 8, LANES).sum(0))
                return tuple(out)

            sums = lax.fori_loop(
                0, rows, one_row, tuple(jnp.zeros((8, LANES), F32) for _ in range(7)), unroll=4
            )
            for a in range(7):
                target[pl.ds(first + 7 * a + b, 1), lanes] = jnp.sum(sums[a], axis=0, keepdims=True)


def joined(ref, rows, cols=slice(None)):
    parts = [ref[g, rows, cols, :] for g in range(ref.shape[0])]
    return jnp.concatenate([p.reshape(-1, LANES) for p in parts], axis=1)


def split_to(ref, rows, value, shape):
    for g in range(ref.shape[0]):
        ref[g, rows] = value[:, g * LANES : (g + 1) * LANES].reshape(*shape, LANES)


def norm_parts(z):
    center = z - jnp.mean(z, axis=-1, keepdims=True)
    inv = lax.rsqrt(jnp.mean(center * center, axis=-1, keepdims=True) + EPSILON)
    return center * inv, inv


def norm_back(dn, hat, inv, gain):
    scaled = dn * gain
    return inv * (
        scaled
        - jnp.mean(scaled, axis=-1, keepdims=True)
        - hat * jnp.mean(scaled * hat, axis=-1, keepdims=True)
    )


def dot_nn(a, b):
    return jnp.dot(a, b, preferred_element_type=F32)


def dot_nt(a, b):
    return lax.dot_general(a, b, (((1,), (1,)), ((), ())), preferred_element_type=F32)


def dot_tn(a, b):
    return lax.dot_general(a, b, (((0,), (0,)), ((), ())), preferred_element_type=F32)


def pixel_blocks(pixels):
    best = max(d for d in range(16, 257, 16) if pixels % d == 0)
    return [slice(start, start + best) for start in range(0, pixels, best)]


def hidden_chunks(hidden):
    size = 256 if hidden % 256 == 0 else hidden
    return [slice(start, start + size) for start in range(0, hidden, size)]


def mlp_grads(normed, grad, w_in, b_in, w_out, act, gpre, dw, db):
    pixels = grad.shape[0]
    for cut in hidden_chunks(w_in.shape[2]):
        bias = b_in[:, cut]
        bias_sum = None
        for block in pixel_blocks(pixels):
            pre = dot_nn(normed[block, :], w_in[0, :, cut]) + bias
            value, slope = gelu_parts(pre)
            act[block, cut] = value.astype(BF16)
            gradient = dot_nn(grad[block, :], w_out[0, :, cut]) * slope
            gpre[block, cut] = gradient.astype(BF16)
            part = jnp.sum(gradient, axis=0, keepdims=True)
            bias_sum = part if bias_sum is None else bias_sum + part
        db[:, cut] = bias_sum
        dw[1, cut, :] = dot_tn(act[:, cut], grad[...]).astype(BF16)
        dw[0, cut, :] = dot_tn(gpre[:, cut], normed[...]).astype(BF16)


def fetch_layers(triples, arrived):
    copies = [
        pltpu.make_async_copy(source.at[pl.ds(layer, 1)], target, arrived.at[i])
        for i, (source, layer, target) in enumerate(triples)
    ]
    for copy in copies:
        copy.start()
    return copies


def block_back(z, grad, layer, gains, shifts, weights, b_in, outs, scratch):
    dz_out, dw, db, dgain, dshift = outs
    normed, act, gpre = scratch
    gain = gains[layer : layer + 1]
    hat, inv = norm_parts(joined(z, slice(None)))
    normed[...] = (hat * gain + shifts[layer : layer + 1]).astype(BF16)
    w_in, w_out, waits = weights
    for wait in waits:
        wait.wait()
    mlp_grads(normed, grad, w_in, b_in.at[layer], w_out, act, gpre, dw, db)
    dn = dot_nt(gpre[...], w_in[0])
    dgain[...] = jnp.sum(dn * hat, axis=0, keepdims=True)
    dshift[...] = jnp.sum(dn, axis=0, keepdims=True)
    dz_out[...] = norm_back(dn, hat, inv, gain).astype(BF16)


def forward_kernel(
    place, xpad, taps, gains, shifts, w_in, w_out, b_in, mids, z_out,
    xs, zs, act, w_in0, w_out0, arrived,
):
    waits = fetch_layers(((w_in, 0, w_in0), (w_out, 0, w_out0)), arrived)
    groups, mid_rows, mid_cols = zs.shape[:3]
    rows, cols = z_out.shape[1:3]
    for g in range(groups):
        xs[g] = xpad[:, :, g * LANES : (g + 1) * LANES].astype(F32)
    conv_pass(xs, 0, 0, taps.at[0], zs, mid_rows, mid_cols)
    z_out[...] = zs[:, HALO : HALO + rows, HALO : HALO + cols, :]
    strip = act.shape[0] // mid_cols
    for wait in waits:
        wait.wait()

    def one_strip(step, carry):
        top = step * strip
        hat, _ = norm_parts(joined(zs, pl.ds(top, strip)))
        normed = (hat * gains[0:1] + shifts[0:1]).astype(BF16)
        for cut in hidden_chunks(w_in0.shape[2]):
            pre = dot_nn(normed, w_in0[0, :, cut]) + b_in[0, :, cut]
            act[:, cut] = gelu_only(pre).astype(BF16)
        mixed = dot_nt(act[...], w_out0[0])
        row = lax.broadcasted_iota(jnp.int32, (strip, mid_cols, 1), 0) + (top - HALO) + place[0]
        col = lax.broadcasted_iota(jnp.int32, (strip, mid_cols, 1), 1) - HALO + place[1]
        real = (row >= 0) & (row < place[2]) & (col >= 0) & (col < place[3])
        real = jnp.where(real, 1.0, 0.0).reshape(strip * mid_cols, 1)
        base = joined(xs, pl.ds(top + HALO, strip), slice(HALO, HALO + mid_cols))
        mid = (base + mixed).astype(BF16).astype(F32) * real
        split_to(mids, pl.ds(top, strip), mid, (strip, mid_cols))
        return carry

    lax.fori_loop(0, mid_rows // strip, one_strip, 0)


def top_kernel(
    mids, grad, taps, gains, shifts, w_in, w_out, b_in, dz_out, dw, db, dgain, dshift,
    z, normed, act, gpre, w_in1, w_out1, arrived,
):
    waits = fetch_layers(((w_in, 1, w_in1), (w_out, 1, w_out1)), arrived)
    conv_pass(mids, 0, 0, taps.at[1], z, *z.shape[1:3])
    block_back(
        z, grad, 1, gains, shifts, (w_in1, w_out1, waits), b_in,
        (dz_out, dw, db, dgain, dshift), (normed, act, gpre),
    )


def low_kernel(
    dzpad, grad, z0, taps_back, gains, shifts, w_in, w_out, b_in,
    gmid, dz_out, dw, db, dgain, dshift,
    dzs, spread, normed, act, gpre, w_in0, w_out0, arrived,
):
    waits = fetch_layers(((w_in, 0, w_in0), (w_out, 0, w_out0)), arrived)
    spread_pass(dzpad, dzs, taps_back.at[1], spread)
    gmid[...] = (grad[...].astype(F32) + joined(spread, slice(None))).astype(BF16)
    block_back(
        z0, gmid, 0, gains, shifts, (w_in0, w_out0, waits), b_in,
        (dz_out, dw, db, dgain, dshift), (normed, act, gpre),
    )


def spread_pass(dzpad, dzs, taps_back, spread):
    for g in range(dzs.shape[0]):
        dzs[g] = dzpad[:, :, g * LANES : (g + 1) * LANES].astype(F32)
    conv_pass(dzs, 0, 0, taps_back, spread, *spread.shape[1:3])


def last_kernel(dzpad, gmid, taps_back, out, dzs, spread):
    spread_pass(dzpad, dzs, taps_back.at[0], spread)
    out[...] = (gmid[...].astype(F32) + joined(spread, slice(None))).astype(BF16)


def taps_kernel(source, row0, col0, dz, db, dgain, dshift, out, xs, dzs, sums):
    rows, cols = dzs.shape[1:3]
    channels = out.shape[1]
    split_to(dzs, slice(None), dz[...].astype(F32), (rows, cols))
    if xs is None:
        values = source
    else:
        for g in range(dzs.shape[0]):
            xs[g] = source[:, :, g * LANES : (g + 1) * LANES].astype(F32)
        values = xs
    sums[...] = jnp.zeros(sums.shape, F32)
    count = db.shape[1] // channels
    for k in range(count):
        sums[k : k + 1, :] = db[:, k * channels : (k + 1) * channels]
    sums[count : count + 1, :] = dgain[...]
    sums[count + 1 : count + 2, :] = dshift[...]
    tap_pass(values, row0, col0, dzs, 0, 0, sums, count + 2, rows, cols)
    out[...] = sums[...].astype(BF16)


def top_taps_kernel(source, dz, db, dgain, dshift, out, dzs, sums):
    taps_kernel(source, 0, 0, dz, db, dgain, dshift, out, None, dzs, sums)


def low_taps_kernel(source, dz, db, dgain, dshift, out, xs, dzs, sums):
    taps_kernel(source, HALO, HALO, dz, db, dgain, dshift, out, xs, dzs, sums)


def shape(*dims, dtype=F32):
    return jax.ShapeDtypeStruct(dims, dtype)


def run(kernel, outs, scratch, args, specs=None, fetched=0, name=None):
    vmem = pl.BlockSpec(memory_space=pltpu.VMEM)
    semaphores = [pltpu.SemaphoreType.DMA((fetched,))] if fetched else []
    return pl.pallas_call(
        kernel,
        out_shape=outs,
        in_specs=[
            vmem if s is None else pl.BlockSpec(memory_space=s) for s in (specs or [None] * len(args))
        ],
        out_specs=tuple(vmem for _ in outs),
        scratch_shapes=[pltpu.VMEM(s.shape, s.dtype) for s in scratch] + semaphores,
        compiler_params=pltpu.CompilerParams(vmem_limit_bytes=50 * 1024 * 1024),
        name=name,
    )(*args)


def swap_edges(low_edge, high_edge, axis):
    count = lax.axis_size(axis)
    odd = lax.axis_index(axis) % 2 == 1
    first = lax.ppermute(
        jnp.where(odd, low_edge, high_edge), axis, [(i, i ^ 1) for i in range(count) if i ^ 1 < count]
    )
    pairs = [(i, i + 1) for i in range(1, count - 1, 2)]
    second = lax.ppermute(
        jnp.where(odd, high_edge, low_edge), axis, pairs + [(j, i) for i, j in pairs]
    )
    return jnp.where(odd, first, second), jnp.where(odd, second, first)


def edges(tile, axis):
    count = tile.shape[axis]
    return (
        lax.slice_in_dim(tile, 0, HALO, axis=axis),
        lax.slice_in_dim(tile, count - HALO, count, axis=axis),
    )


def padded_tile(tile, width):
    low, high = swap_edges(tile[:, :width], tile[:, -width:], "cols")
    wide = jnp.concatenate([low, tile, high], axis=1)
    low, high = swap_edges(wide[:width], wide[-width:], "rows")
    return jnp.concatenate([low, wide, high], axis=0)


def flip_bit(value, bit):
    both = ("rows", "cols")
    total = lax.axis_size("rows") * lax.axis_size("cols")
    return lax.ppermute(value, both, [(i, i ^ (1 << bit)) for i in range(total)])


def halves(chunks, dim, mine):
    other = lax.dynamic_index_in_dim(chunks, 1 - mine, dim, keepdims=False)
    own = lax.dynamic_index_in_dim(chunks, mine, dim, keepdims=False)
    return other, own


def summed(own, got):
    return (own.astype(F32) + got.astype(F32)).astype(BF16)


def step(chunks, order, bit, mine):
    spot = order.index(bit)
    per = chunks.shape[-2:]
    pair = chunks.reshape((-1, 2 ** spot, 2, 2 ** (len(order) - spot - 1)) + per)
    send, keep = halves(pair, 2, mine[bit])
    return keep, flip_bit(send, bit), [b for b in order if b != bit]


def shards(activations, grad_out, kernels, norm_gains, norm_shifts, w_in, b_in, w_out):
    rows, cols, channels = activations.shape
    layers, _, hidden = w_in.shape
    groups = channels // LANES
    n_rows, n_cols = lax.axis_size("rows"), lax.axis_size("cols")
    total = n_rows * n_cols
    bits = total.bit_length() - 1
    col_bits = n_cols.bit_length() - 1
    me = lax.axis_index("rows") * n_cols + lax.axis_index("cols")
    mine = [(me >> k) & 1 for k in range(bits)]
    grad_scale = 1.0 / math.sqrt(rows * cols * total)
    pixels = rows * cols

    taps = kernels.reshape(layers, 49, groups, LANES).transpose(0, 2, 1, 3)
    taps_back = taps[:, :, ::-1]
    biases = b_in[:, None, :]
    place = jnp.stack(
        [
            lax.axis_index("rows") * rows,
            lax.axis_index("cols") * cols,
            jnp.int32(rows * n_rows),
            jnp.int32(cols * n_cols),
        ]
    ).astype(jnp.int32)
    grad_flat = grad_out.reshape(pixels, channels)

    def widened(tile, width, to):
        wide = padded_tile(tile, width)
        return jnp.pad(wide, ((0, 0), (0, to - wide.shape[1]), (0, 0)))

    mid_rows, mid_cols = rows + 2 * HALO, cols + 8
    strip = max(d for d in range(1, mid_rows + 1) if mid_rows % d == 0 and d * mid_cols <= 264)
    weights = [shape(1, channels, hidden, dtype=BF16)] * 2
    tile_scratch = [
        shape(pixels, channels, dtype=BF16),
        shape(pixels, hidden, dtype=BF16),
        shape(pixels, hidden, dtype=BF16),
    ] + weights
    tile_z = shape(groups, rows, cols, LANES)
    tile_b = shape(pixels, channels, dtype=BF16)
    back_outs = (
        tile_b, shape(2, hidden, channels, dtype=BF16),
        shape(1, hidden), shape(1, channels), shape(1, channels),
    )
    small_rows = 64

    xpad = widened(activations, WIDE, cols + 16)
    mids, z0 = run(
        forward_kernel,
        (shape(groups, mid_rows, mid_cols, LANES), tile_z),
        [
            shape(groups, *xpad.shape[:2], LANES),
            shape(groups, mid_rows, mid_cols, LANES),
            shape(strip * mid_cols, hidden, dtype=BF16),
        ]
        + weights,
        (place, xpad, taps, norm_gains, norm_shifts, w_in, w_out, biases),
        [pltpu.SMEM] + [None] * 4 + [pl.ANY] * 2 + [None],
        fetched=2,
        name="forward",
    )
    dz1, dw1, *small1 = run(
        top_kernel,
        back_outs,
        [tile_z] + tile_scratch,
        (mids, grad_flat, taps, norm_gains, norm_shifts, w_in, w_out, biases),
        [None] * 5 + [pl.ANY] * 2 + [None],
        fetched=2,
        name="top",
    )
    fence = lax.optimization_barrier
    per = hidden // total
    every = list(range(bits - 1, -1, -1))
    sides = (col_bits - 1, col_bits)

    def start(dw):
        chunks, order = dw.reshape(2, total, per, channels), every
        for bit in range(col_bits - 2):
            keep, got, order = step(chunks, order, bit, mine)
            chunks = summed(keep, got)
        if col_bits > 1:
            return step(chunks, order, col_bits - 2, mine)
        return chunks, None, order

    def settled(flight):
        keep, got, order = flight
        return (keep if got is None else summed(keep, got)), order

    def fork(flight):
        chunks, order = settled(flight)
        return [step(chunks[i], order, sides[i], mine) for i in range(2)]

    def cross(flights):
        done = [settled(f) for f in flights]
        return [step(done[i][0], done[i][1], sides[1 - i], mine) for i in range(2)]

    def merge(flights):
        done = [settled(f) for f in flights]
        return jnp.stack([d[0].reshape(-1, per, channels) for d in done]), done[0][1]

    def onward(chunks, order):
        return step(chunks, order, order[-1], mine)

    def fenced(values):
        leaves, tree = jax.tree.flatten(values)
        arrays = [i for i, leaf in enumerate(leaves) if not isinstance(leaf, int)]
        for i, value in zip(arrays, fence(tuple(leaves[i] for i in arrays))):
            leaves[i] = value
        return jax.tree.unflatten(tree, leaves)

    dz1, dw1 = fence((dz1, dw1))
    sides1 = swap_edges(*edges(dz1.reshape(rows, cols, channels), 1), "cols")
    run1 = start(dw1)
    (small1,) = run(
        top_taps_kernel,
        (shape(small_rows, channels, dtype=BF16),),
        [tile_z, shape(small_rows, channels)],
        (mids, dz1, *small1),
        name="top_taps",
    )
    sides1, dz1, small1 = fenced((sides1, dz1, small1))
    wide1 = jnp.concatenate([sides1[0], dz1.reshape(rows, cols, channels), sides1[1]], axis=1)
    ends1 = swap_edges(*edges(wide1, 0), "rows")
    ends1, wide1, run1 = fenced((ends1, wide1, run1))
    pair1 = fork(run1)
    dzpad1 = jnp.pad(
        jnp.concatenate([ends1[0], wide1, ends1[1]], axis=0),
        ((0, 0), (0, 16 - 2 * HALO), (0, 0)),
    )
    spread_scratch = [shape(groups, *dzpad1.shape[:2], LANES), tile_z]
    grad_mid, dz0, dw0, *small0 = run(
        low_kernel,
        (tile_b,) + back_outs,
        spread_scratch + tile_scratch,
        (dzpad1, grad_flat, z0, taps_back, norm_gains, norm_shifts, w_in, w_out, biases),
        [None] * 6 + [pl.ANY] * 2 + [None],
        fetched=2,
        name="low",
    )
    dz0, dw0, pair1 = fenced((dz0, dw0, pair1))
    run0 = start(dw0)
    pair1 = cross(pair1)
    sides0 = swap_edges(*edges(dz0.reshape(rows, cols, channels), 1), "cols")
    (small0,) = run(
        low_taps_kernel,
        (shape(small_rows, channels, dtype=BF16),),
        [shape(groups, *xpad.shape[:2], LANES), tile_z, shape(small_rows, channels)],
        (xpad, dz0, *small0),
        name="low_taps",
    )
    small = jnp.concatenate([small0, small1], axis=0)
    run0, pair1, sides0, small, dz0 = fenced((run0, pair1, sides0, small, dz0))
    pair0 = fork(run0)
    wide0 = jnp.concatenate([sides0[0], dz0.reshape(rows, cols, channels), sides0[1]], axis=1)
    ends0 = swap_edges(*edges(wide0, 0), "rows")
    run1 = onward(*merge(pair1))
    small_got = flip_bit(small, 0)
    ends0, wide0, run1, small, small_got = fenced((ends0, wide0, run1, small, small_got))
    run1 = onward(*settled(run1)) if len(run1[2]) else run1
    small = summed(small, small_got)
    small_got = flip_bit(small, 1)
    dzpad0 = jnp.pad(
        jnp.concatenate([ends0[0], wide0, ends0[1]], axis=0),
        ((0, 0), (0, 16 - 2 * HALO), (0, 0)),
    )
    (grad_in,) = run(
        last_kernel, (tile_b,), spread_scratch, (dzpad0, grad_mid, taps_back), name="last"
    )
    pair0, run1, small, small_got, grad_in = fenced((pair0, run1, small, small_got, grad_in))
    pair0 = cross(pair0)
    small = summed(small, small_got)
    small_got = flip_bit(small, 2)

    def finish(flight):
        chunks, order = settled(flight)
        while order:
            chunks, order = settled(onward(chunks, order))
        return jnp.swapaxes(chunks.reshape(2, per, channels).astype(F32) * grad_scale, 1, 2)

    share1 = finish(run1)
    pair0, small, small_got = fenced((pair0, small, small_got))
    run0 = onward(*merge(pair0))
    small = summed(small, small_got)
    bit = 3
    while run0[2]:
        small_got = flip_bit(small, bit)
        run0, small, small_got = fenced((run0, small, small_got))
        run0 = onward(*settled(run0))
        small = summed(small, small_got)
        bit += 1
    for left in range(bit, bits):
        small = summed(small, flip_bit(small, left))
    shares = [finish(run0), share1]
    small = small.reshape(layers, small_rows, channels).astype(F32) * grad_scale
    count = hidden // channels
    return (
        grad_in.reshape(rows, cols, channels),
        small[:, count + 2 : count + 51].reshape(layers, 7, 7, channels),
        small[:, count],
        small[:, count + 1],
        small[:, :count].reshape(layers, hidden),
        jnp.stack([share[0] for share in shares]),
        jnp.stack([share[1] for share in shares]),
    )


def solution(mesh):
    tile = P("rows", "cols", None)
    sliced = P(None, None, ("rows", "cols"))
    return jax.shard_map(
        shards,
        mesh=mesh,
        in_specs=(tile, tile, P(), P(), P(), P(), P(), P()),
        out_specs=(tile, P(), P(), P(), P(), sliced, sliced),
        check_vma=False,
    )
```

time: 164 us -> 120 us (0.73)
  waiting for transfers between devices: 72.5 us -> 23.3 us
  starting transfers between devices: 18.9 us -> 52.8 us
  Pallas kernels: 46 us -> 28.5 us
  local copies, waits for them, and re-layouts: 13.6 us -> 5.27 us
  other arithmetic: 11.1 us -> 7.98 us
    ppermute x5 -> x19, waiting for transfers between devices: 59.5 us -> 18.8 us  [flip_bit(): return lax.ppermute(value, both, [(i, i ^ 1 << bit) for i in range(total)])]
    pallas_call x3 -> x6, Pallas kernels: 46 us -> 28.5 us  [run(): pl.pallas_call(kernel, out_shape=outs, in_specs=[vmem if s is None else p...]
    ppermute x4 -> x6, starting transfers between devices: 4.75 us -> 21.9 us  [swap_edges(): lax.ppermute(jnp.where(odd, low_edge, high_edge), axis, [(i, i ^ 1) for i...]
    ppermute x5 -> x19, starting transfers between devices: 11.5 us -> 26.7 us  [flip_bit(): return lax.ppermute(value, both, [(i, i ^ 1 << bit) for i in range(total)])]
    ppermute x4 -> x6, waiting for transfers between devices: 13 us -> 4.49 us  [swap_edges(): lax.ppermute(jnp.where(odd, low_edge, high_edge), axis, [(i, i ^ 1) for i...]
    slice x17 -> x7, local copies, waits for them, and re-layouts: 7.54 us -> 1.03 us  [the longest x2 0.76 us: shards(): small[:, count + 2:count + 51].reshape(layers, 7, 7, channels)]
    concatenate x7 -> x5, other arithmetic: 4.68 us -> 1.23 us  [the longest x1 0.89 us: shards(): jnp.concatenate([ends1[0], wide1, ends1[1]], axis=0)]
    squeeze x1 -> x14, local copies, waits for them, and re-layouts: 0.73 us -> 3.34 us  [the longest x13 2.76 us: halves(): other = lax.dynamic_index_in_dim(chunks, 1 - mine, dim, keepdims=False)]
  transfers between devices with their start and end apart: 13 -> 31, of which waited for: 7 -> 14; matrix products, arithmetic and copies ran while one was open for 1% -> 4% of each run, Pallas kernels for 2% -> 11%
where the time goes in v3:
time: 120 us; the launch traced here: 119 us
  starting transfers between devices  52.8 us (44%)
  Pallas kernels  28.5 us (24%)
  waiting for transfers between devices  23.3 us (19%)
  other arithmetic  7.98 us (7%)
  local copies, waits for them, and re-layouts  5.27 us (4%)
  between operations  1.28 us (1%)
    pallas_call x6, Pallas kernels, run(): pl.pallas_call(kernel, out_shape=outs, in_specs=[vmem if s is None else p...  28.5 us
    ppermute x19, starting transfers between devices, flip_bit(): return lax.ppermute(value, both, [(i, i ^ 1 << bit) for i in range(total)])  26.7 us
    ppermute x6, starting transfers between devices, swap_edges(): lax.ppermute(jnp.where(odd, low_edge, high_edge), axis, [(i, i ^ 1) for i...  21.9 us
    ppermute x19, waiting for transfers between devices, flip_bit(): return lax.ppermute(value, both, [(i, i ^ 1 << bit) for i in range(total)])  18.8 us
    ppermute x6, waiting for transfers between devices, swap_edges(): lax.ppermute(jnp.where(odd, low_edge, high_edge), axis, [(i, i ^ 1) for i...  4.49 us
    ppermute x6, starting transfers between devices, swap_edges(): lax.ppermute(jnp.where(odd, high_edge, low_edge), axis, pairs + [(j, i) f...  4.15 us
    squeeze x13, local copies, waits for them, and re-layouts, halves(): other = lax.dynamic_index_in_dim(chunks, 1 - mine, dim, keepdims=False)  2.76 us
    convert_element_type x16, other arithmetic, summed(): return (own.astype(F32) + got.astype(F32)).astype(BF16)  2.51 us
  transfers between devices with their start and end apart: 31, of which 14 were waited for; matrix products, arithmetic and copies ran while one was open for 4% of the time, Pallas kernels for 11%

profile of v3, /device:TPU:0, one launch (start us, length us, event | category | flops | bytes accessed | tf_op | source)
XLA Modules:
  0.0 119.1 jit_solution(15141211653650417776)
XLA Ops:
  4.3 2.9 %collective-permute-start.2 = (bf16[6,28,384]{2,1,0:T(8,128)(2,1)S(1)}, bf16[6,28,384]{2,1,0:T(8,128)(2,1)S(1)}, u32[]{:S(2)}, u32[]{:S(2)}) collective-permute-start(bf16[6,28,384]{2,1,0:T(8,128)(2,1)S(1)} %get-tuple-element.155), channel_id=1, source_target_pairs={{0,4},{4,0},{8,12},{12,8},{16,20},{20,16},{24,28},{28,24},{1,5},{5... | collective-permute-start | bytes 387080 | tf_op jit(solution)/shard_map/ppermute | solution.py:312
  8.2 2.1 %collective-permute-done.2 = bf16[6,28,384]{2,1,0:T(8,128)(2,1)S(1)} collective-permute-done((bf16[6,28,384]{2,1,0:T(8,128)(2,1)S(1)}, bf16[6,28,384]{2,1,0:T(8,128)(2,1)S(1)}, u32[]{:S(2)}, u32[]{:S(2)}) %collective-permute-start.2) | collective-permute-done | bytes 129056 | tf_op jit(solution)/shard_map/ppermute | solution.py:312
  10.6 8.7 %forward.1 = (f32[3,22,24,128]{3,2,1,0:T(8,128)S(1)}, f32[3,16,16,128]{3,2,1,0:T(8,128)S(1)}) custom-call(s32[4]{0:T(128)S(1)} %pad_add_fusion.place, bf16[28,32,384]{2,1,0:T(8,128)(2,1)S(1)} %fusion.12.xpad.source, f32[2,3,49,128]{3,2,1,0:T(8,128)S(1)} %bitcast.86, f32[2,384]{1,0:T(2,128)S(1)} %copy-done.1, f32[2,384]{1,0:T(2,128)S(1)} %copy-done.2, ...), custom_call_target="tpu_custom_call" | custom-call | tf_op jit(solution)/shard_map/forward/pallas_call | solution.py:296
  19.3 6.8 %top.1 = (bf16[256,384]{1,0:T(8,128)(2,1)S(1)}, bf16[2,1536,384]{2,1,0:T(8,128)(2,1)S(1)}, f32[1,1536]{1,0:T(1,128)S(1)}, f32[1,384]{1,0:T(1,128)S(1)}, f32[1,384]{1,0:T(1,128)S(1)}) custom-call(f32[3,22,24,128]{3,2,1,0:T(8,128)S(1)} %get-tuple-element.73.mids.source, bf16[256,384]{1,0:T(8,128)(2,1)S(1)} %bitcast.95, f32[2,3,49,128]{3,2,1,0:T(8,128)S(1)} %bitcast.87, ...), custom_call_target="tpu_custom_call" | custom-call | tf_op jit(solution)/shard_map/top/pallas_call | solution.py:296
  27.4 4.6 %collective-permute-start.8 = (bf16[2,16,1,48,384]{4,3,1,2,0:T(8,128)(2,1)}, bf16[2,16,1,48,384]{4,3,1,2,0:T(8,128)(2,1)}, u32[]{:S(2)}, u32[]{:S(2)}) collective-permute-start(bf16[2,16,1,48,384]{4,3,1,2,0:T(8,128)(2,1)} %get-tuple-element.141), channel_id=1, source_target_pairs={{0,1},{1,0},{2,3},{3,2},{4,5},{5,4},{6,7},{7,6},{8,9},{9,8},{10,11... | collective-permute-start | bytes 3538952 | tf_op jit(solution)/shard_map/ppermute | solution.py:340
  32.7 3.5 %collective-permute-start.4 = (bf16[16,3,384]{2,1,0:T(4,128)(2,1)S(1)}, bf16[16,3,384]{2,1,0:T(4,128)(2,1)S(1)}, u32[]{:S(2)}, u32[]{:S(2)}) collective-permute-start(bf16[16,3,384]{2,1,0:T(4,128)(2,1)S(1)} %get-tuple-element.180), channel_id=1, source_target_pairs={{0,1},{1,0},{2,3},{3,2},{4,5},{5,4},{6,7},{7,6},{8,9},{9,8},{10,11... | collective-permute-start | bytes 110600 | tf_op jit(solution)/shard_map/ppermute | solution.py:312
  36.2 1.8 %top_taps.1 = bf16[64,384]{1,0:T(8,128)(2,1)S(1)} custom-call(f32[3,22,24,128]{3,2,1,0:T(8,128)S(1)} %get-tuple-element.73.mids.source, bf16[256,384]{1,0:T(8,128)(2,1)S(1)} %get-tuple-element.81.dz, f32[1,1536]{1,0:T(1,128)S(1)} %get-tuple-element.77.db, f32[1,384]{1,0:T(1,128)S(1)} %get-tuple-element.78.dgain, f32[1,384]{1,0:T(1,128)S(1)} %get-tuple-element.79.dshift), custom_call_target="tpu_custom_call" | custom-call | tf_op jit(solution)/shard_map/top_taps/pallas_call | solution.py:296
  39.1 8.7 %collective-permute-start.6 = (bf16[3,22,384]{2,1,0:T(8,128)(2,1)S(1)}, bf16[3,22,384]{2,1,0:T(8,128)(2,1)S(1)}, u32[]{:S(2)}, u32[]{:S(2)}) collective-permute-start(bf16[3,22,384]{2,1,0:T(8,128)(2,1)S(1)} %get-tuple-element.172), channel_id=1, source_target_pairs={{0,4},{4,0},{8,12},{12,8},{16,20},{20,16},{24,28},{28,24},{1,5},{5... | collective-permute-start | bytes 152072 | tf_op jit(solution)/shard_map/ppermute | solution.py:312
  47.8 2.1 %collective-permute-done.6 = bf16[3,22,384]{2,1,0:T(8,128)(2,1)S(1)} collective-permute-done((bf16[3,22,384]{2,1,0:T(8,128)(2,1)S(1)}, bf16[3,22,384]{2,1,0:T(8,128)(2,1)S(1)}, u32[]{:S(2)}, u32[]{:S(2)}) %collective-permute-start.6) | collective-permute-done | bytes 50720 | tf_op jit(solution)/shard_map/ppermute | solution.py:312
  50.5 1.6 %add_convert_fusion.1 = bf16[2,16,1,48,384]{4,3,1,2,0:T(8,128)(2,1)S(1)} fusion(bf16[2,16,1,48,384]{4,3,1,2,0:T(8,128)(2,1)} %collective-permute-done.8, bf16[2,16,1,48,384]{4,3,1,2,0:T(8,128)(2,1)S(1)} %get-tuple-element.90), kind=kLoop, calls=%fused_computation.1 | loop fusion | flops 2359296 | bytes 3538944 | tf_op jit(solution)/shard_map/convert_element_type | solution.py:350
  52.3 2.1 %collective-permute-start.10 = (bf16[1,4,2,48,384]{4,3,2,1,0:T(8,128)(2,1)S(1)}, bf16[1,4,2,48,384]{4,3,2,1,0:T(8,128)(2,1)S(1)}, u32[]{:S(2)}, u32[]{:S(2)}) collective-permute-start(bf16[1,4,2,48,384]{4,3,2,1,0:T(8,128)(2,1)S(1)} %get-tuple-element.151), channel_id=1, source_target_pairs={{0,4},{1,5},{2,6},{3,7},{4,0},{5,1},{6,2},{7,3},{8,12},{9,13},{10,... | collective-permute-start | bytes 884744 | tf_op jit(solution)/shard_map/ppermute | solution.py:340
  57.6 6.8 %low.1 = (bf16[256,384]{1,0:T(8,128)(2,1)S(1)}, bf16[256,384]{1,0:T(8,128)(2,1)S(1)}, bf16[2,1536,384]{2,1,0:T(8,128)(2,1)S(1)}, f32[1,1536]{1,0:T(1,128)S(1)}, ...) custom-call(bf16[22,32,384]{2,1,0:T(8,128)(2,1)S(1)} %fusion.16.dzpad, bf16[256,384]{1,0:T(8,128)(2,1)S(1)} %bitcast.96, ...), custom_call_target="tpu_custom_call" | custom-call | tf_op jit(solution)/shard_map/low/pallas_call | solution.py:296
  65.5 2.0 %collective-permute-start.14 = (bf16[16,3,384]{2,1,0:T(4,128)(2,1)S(1)}, bf16[16,3,384]{2,1,0:T(4,128)(2,1)S(1)}, u32[]{:S(2)}, u32[]{:S(2)}) collective-permute-start(bf16[16,3,384]{2,1,0:T(4,128)(2,1)S(1)} %get-tuple-element.178), channel_id=1, source_target_pairs={{0,1},{1,0},{2,3},{3,2},{4,5},{5,4},{6,7},{7,6},{8,9},{9,8},{10,11... | collective-permute-start | bytes 110600 | tf_op jit(solution)/shard_map/ppermute | solution.py:312
  67.8 1.5 %collective-permute-start.13 = (bf16[1,4,1,48,384]{4,3,2,1,0:T(8,128)(2,1)S(1)}, bf16[1,4,1,48,384]{4,3,2,1,0:T(8,128)(2,1)S(1)}, u32[]{:S(2)}, u32[]{:S(2)}) collective-permute-start(bf16[1,4,1,48,384]{4,3,2,1,0:T(8,128)(2,1)S(1)} %get-tuple-element.167), channel_id=1, source_target_pairs={{0,2},{1,3},{2,0},{3,1},{4,6},{5,7},{6,4},{7,5},{8,10},{9,11},{10,... | collective-permute-start | bytes 442376 | tf_op jit(solution)/shard_map/ppermute | solution.py:340
  69.4 1.9 %low_taps.1 = bf16[64,384]{1,0:T(8,128)(2,1)S(1)} custom-call(bf16[28,32,384]{2,1,0:T(8,128)(2,1)S(1)} %fusion.12.xpad.source, bf16[256,384]{1,0:T(8,128)(2,1)S(1)} %get-tuple-element.105.dz, f32[1,1536]{1,0:T(1,128)S(1)} %get-tuple-element.98.db, f32[1,384]{1,0:T(1,128)S(1)} %get-tuple-element.99.dgain, f32[1,384]{1,0:T(1,128)S(1)} %get-tuple-element.100.dshift), custom_call_target="tpu_custom_call" | custom-call | tf_op jit(solution)/shard_map/low_taps/pallas_call | solution.py:296
  71.4 2.0 %collective-permute-done.12 = bf16[1,4,1,48,384]{4,3,1,2,0:T(8,128)(2,1)S(1)} collective-permute-done((bf16[1,4,1,48,384]{4,3,1,2,0:T(8,128)(2,1)S(1)}, bf16[1,4,1,48,384]{4,3,1,2,0:T(8,128)(2,1)S(1)}, u32[]{:S(2)}, u32[]{:S(2)}) %collective-permute-start.12) | collective-permute-done | bytes 147488 | tf_op jit(solution)/shard_map/ppermute | solution.py:340
  75.6 4.3 %collective-permute-start.18 = (bf16[3,22,384]{2,1,0:T(8,128)(2,1)S(1)}, bf16[3,22,384]{2,1,0:T(8,128)(2,1)S(1)}, u32[]{:S(2)}, u32[]{:S(2)}) collective-permute-start(bf16[3,22,384]{2,1,0:T(8,128)(2,1)S(1)} %get-tuple-element.166), channel_id=1, source_target_pairs={{0,4},{4,0},{8,12},{12,8},{16,20},{20,16},{24,28},{28,24},{1,5},{5... | collective-permute-start | bytes 152072 | tf_op jit(solution)/shard_map/ppermute | solution.py:312
  80.1 1.6 %collective-permute-start.20 = (bf16[2,2,1,48,384]{4,3,1,0,2:T(8,128)(2,1)S(1)}, bf16[2,2,1,48,384]{4,3,1,0,2:T(8,128)(2,1)S(1)}, u32[]{:S(2)}, u32[]{:S(2)}) collective-permute-start(bf16[2,2,1,48,384]{4,3,1,0,2:T(8,128)(2,1)S(1)} %get-tuple-element.163), channel_id=1, source_target_pairs={{0,8},{1,9},{2,10},{3,11},{4,12},{5,13},{6,14},{7,15},{8,0},{9,1},... | collective-permute-start | bytes 442376 | tf_op jit(solution)/shard_map/ppermute | solution.py:340
  82.1 1.7 %collective-permute-start.16 = (bf16[1,8,1,48,384]{4,3,1,2,0:T(8,128)(2,1)S(1)}, bf16[1,8,1,48,384]{4,3,1,2,0:T(8,128)(2,1)S(1)}, u32[]{:S(2)}, u32[]{:S(2)}) collective-permute-start(bf16[1,8,1,48,384]{4,3,1,2,0:T(8,128)(2,1)S(1)} %get-tuple-element.149), channel_id=1, source_target_pairs={{0,2},{1,3},{2,0},{3,1},{4,6},{5,7},{6,4},{7,5},{8,10},{9,11},{10,... | collective-permute-start | bytes 884744 | tf_op jit(solution)/shard_map/ppermute | solution.py:340
  83.9 1.9 %collective-permute-done.20 = bf16[2,2,1,48,384]{4,3,1,0,2:T(8,128)(2,1)S(1)} collective-permute-done((bf16[2,2,1,48,384]{4,3,1,0,2:T(8,128)(2,1)S(1)}, bf16[2,2,1,48,384]{4,3,1,0,2:T(8,128)(2,1)S(1)}, u32[]{:S(2)}, u32[]{:S(2)}) %collective-permute-start.20) | collective-permute-done | bytes 147488 | tf_op jit(solution)/shard_map/ppermute | solution.py:340
  85.9 2.1 %collective-permute-start.22 = (bf16[2,1,1,48,384]{4,3,1,0,2:T(8,128)(2,1)S(1)}, bf16[2,1,1,48,384]{4,3,1,0,2:T(8,128)(2,1)S(1)}, u32[]{:S(2)}, u32[]{:S(2)}) collective-permute-start(bf16[2,1,1,48,384]{4,3,1,0,2:T(8,128)(2,1)S(1)} %get-tuple-element.189), channel_id=1, source_target_pairs={{0,16},{1,17},{2,18},{3,19},{4,20},{5,21},{6,22},{7,23},{8,24},{9,... | collective-permute-start | bytes 221192 | tf_op jit(solution)/shard_map/ppermute | solution.py:340
  88.0 1.8 %collective-permute-start.23 = (bf16[128,384]{1,0:T(8,128)(2,1)S(1)}, bf16[128,384]{1,0:T(8,128)(2,1)S(1)}, u32[]{:S(2)}, u32[]{:S(2)}) collective-permute-start(bf16[128,384]{1,0:T(8,128)(2,1)S(1)} %add_convert_fusion.16), channel_id=1, source_target_pairs={{0,2},{1,3},{2,0},{3,1},{4,6},{5,7},{6,4},{7,5},{8,10},{9,11},{10,... | collective-permute-start | bytes 294920 | tf_op jit(solution)/shard_map/ppermute | solution.py:340
  89.9 2.5 %last.1 = bf16[256,384]{1,0:T(8,128)(2,1)} custom-call(bf16[22,32,384]{2,1,0:T(8,128)(2,1)S(1)} %fusion.18.dzpad, bf16[256,384]{1,0:T(8,128)(2,1)S(1)} %get-tuple-element.119.gmid, f32[2,3,49,128]{3,2,1,0:T(8,128)S(1)} %rev.3.taps_back), custom_call_target="tpu_custom_call" | custom-call | tf_op jit(solution)/shard_map/last/pallas_call | solution.py:296
  92.8 1.5 %collective-permute-start.26 = (bf16[128,384]{1,0:T(8,128)(2,1)S(1)}, bf16[128,384]{1,0:T(8,128)(2,1)S(1)}, u32[]{:S(2)}, u32[]{:S(2)}) collective-permute-start(bf16[128,384]{1,0:T(8,128)(2,1)S(1)} %add_convert_fusion.15), channel_id=1, source_target_pairs={{0,4},{1,5},{2,6},{3,7},{4,0},{5,1},{6,2},{7,3},{8,12},{9,13},{10,... | collective-permute-start | bytes 294920 | tf_op jit(solution)/shard_map/ppermute | solution.py:340
  95.2 1.8 %collective-permute-start.25 = (bf16[1,4,1,48,384]{4,3,2,1,0:T(8,128)(2,1)S(1)}, bf16[1,4,1,48,384]{4,3,2,1,0:T(8,128)(2,1)S(1)}, u32[]{:S(2)}, u32[]{:S(2)}) collective-permute-start(bf16[1,4,1,48,384]{4,3,2,1,0:T(8,128)(2,1)S(1)} %get-tuple-element.159), channel_id=1, source_target_pairs={{0,2},{1,3},{2,0},{3,1},{4,6},{5,7},{6,4},{7,5},{8,10},{9,11},{10,... | collective-permute-start | bytes 442376 | tf_op jit(solution)/shard_map/ppermute | solution.py:340
  98.0 1.7 %collective-permute-done.24 = bf16[1,4,1,48,384]{4,3,1,2,0:T(8,128)(2,1)S(1)} collective-permute-done((bf16[1,4,1,48,384]{4,3,1,2,0:T(8,128)(2,1)S(1)}, bf16[1,4,1,48,384]{4,3,1,2,0:T(8,128)(2,1)S(1)}, u32[]{:S(2)}, u32[]{:S(2)}) %collective-permute-start.24) | collective-permute-done | bytes 147488 | tf_op jit(solution)/shard_map/ppermute | solution.py:340
  100.4 1.6 %collective-permute-start.28 = (bf16[128,384]{1,0:T(8,128)(2,1)S(1)}, bf16[128,384]{1,0:T(8,128)(2,1)S(1)}, u32[]{:S(2)}, u32[]{:S(2)}) collective-permute-start(bf16[128,384]{1,0:T(8,128)(2,1)S(1)} %add_convert_fusion.14), channel_id=1, source_target_pairs={{0,8},{1,9},{2,10},{3,11},{4,12},{5,13},{6,14},{7,15},{8,0},{9,1},... | collective-permute-start | bytes 294920 | tf_op jit(solution)/shard_map/ppermute | solution.py:340
  102.7 2.3 %collective-permute-done.28 = bf16[128,384]{1,0:T(8,128)(2,1)S(1)} collective-permute-done((bf16[128,384]{1,0:T(8,128)(2,1)S(1)}, bf16[128,384]{1,0:T(8,128)(2,1)S(1)}, u32[]{:S(2)}, u32[]{:S(2)}) %collective-permute-start.28) | collective-permute-done | bytes 98336 | tf_op jit(solution)/shard_map/ppermute | solution.py:340
  105.1 2.9 %collective-permute-done.27 = bf16[2,2,1,48,384]{4,3,0,2,1:T(8,128)(2,1)S(1)} collective-permute-done((bf16[2,2,1,48,384]{4,3,0,2,1:T(8,128)(2,1)S(1)}, bf16[2,2,1,48,384]{4,3,0,2,1:T(8,128)(2,1)S(1)}, u32[]{:S(2)}, u32[]{:S(2)}) %collective-permute-start.27) | collective-permute-done | bytes 147488 | tf_op jit(solution)/shard_map/ppermute | solution.py:340
  108.1 2.4 %collective-permute-start.30 = (bf16[2,1,1,48,384]{4,3,0,2,1:T(8,128)(2,1)S(1)}, bf16[2,1,1,48,384]{4,3,0,2,1:T(8,128)(2,1)S(1)}, u32[]{:S(2)}, u32[]{:S(2)}) collective-permute-start(bf16[2,1,1,48,384]{4,3,0,2,1:T(8,128)(2,1)S(1)} %constant_dynamic-slice_fusion), channel_id=1, source_target_pairs={{0,16},{1,17},{2,18},{3,19},{4,20},{5,21},{6,22},{7,23},{8,24},{9,... | collective-permute-start | bytes 221192 | tf_op jit(solution)/shard_map/ppermute | solution.py:340
  111.2 2.6 %collective-permute-done.30 = bf16[2,1,1,48,384]{4,3,0,2,1:T(8,128)(2,1)S(1)} collective-permute-done((bf16[2,1,1,48,384]{4,3,0,2,1:T(8,128)(2,1)S(1)}, bf16[2,1,1,48,384]{4,3,0,2,1:T(8,128)(2,1)S(1)}, u32[]{:S(2)}, u32[]{:S(2)}) %collective-permute-start.30) | collective-permute-done | bytes 73760 | tf_op jit(solution)/shard_map/ppermute | solution.py:340
  114.6 2.5 %collective-permute-done.29 = bf16[128,384]{1,0:T(8,128)(2,1)S(1)} collective-permute-done((bf16[128,384]{1,0:T(8,128)(2,1)S(1)}, bf16[128,384]{1,0:T(8,128)(2,1)S(1)}, u32[]{:S(2)}, u32[]{:S(2)}) %collective-permute-start.29) | collective-permute-done | bytes 98336 | tf_op jit(solution)/shard_map/ppermute | solution.py:340
  (116 shorter events, 23.2 us)
Async XLA Ops:
  1.7 1.5 %collective-permute-start = (bf16[16,6,384]{2,1,0:T(8,128)(2,1)S(1)}, bf16[16,6,384]{2,1,0:T(8,128)(2,1)S(1)}, u32[]{:S(2)}, u32[]{:S(2)}) collective-permute-start(bf16[16,6,384]{2,1,0:T(8,128)(2,1)S(1)} %get-tuple-element.183), channel_id=1, source_target_pairs={{0,1},{1,0},{2,3},{3,2},{4,5},{5,4},{6,7},{7,6},{8,9},{9,8},{10,11... | collective-permute-start | bytes 221192 | tf_op jit(solution)/shard_map/ppermute | solution.py:312
  2.2 0.9 collective-permute-start.1
  4.3 6.1 %collective-permute-start.2 = (bf16[6,28,384]{2,1,0:T(8,128)(2,1)S(1)}, bf16[6,28,384]{2,1,0:T(8,128)(2,1)S(1)}, u32[]{:S(2)}, u32[]{:S(2)}) collective-permute-start(bf16[6,28,384]{2,1,0:T(8,128)(2,1)S(1)} %get-tuple-element.155), channel_id=1, source_target_pairs={{0,4},{4,0},{8,12},{12,8},{16,20},{20,16},{24,28},{28,24},{1,5},{5... | collective-permute-start | bytes 387080 | tf_op jit(solution)/shard_map/ppermute | solution.py:312
  7.2 3.1 %collective-permute-start.3 = (bf16[6,28,384]{2,1,0:T(8,128)(2,1)S(1)}, bf16[6,28,384]{2,1,0:T(8,128)(2,1)S(1)}, u32[]{:S(2)}, u32[]{:S(2)}) collective-permute-start(bf16[6,28,384]{2,1,0:T(8,128)(2,1)S(1)} %get-tuple-element.156), channel_id=1, source_target_pairs={{4,8},{12,16},{20,24},{8,4},{16,12},{24,20},{5,9},{13,17},{21,25},... | collective-permute-start | bytes 387080 | tf_op jit(solution)/shard_map/ppermute | solution.py:316
  10.6 8.7 %copy-start = (bf16[16,16,384]{2,1,0:T(8,128)(2,1)S(1)}, bf16[16,16,384]{2,1,0:T(8,128)(2,1)}, u32[]{:S(2)}) copy-start(bf16[16,16,384]{2,1,0:T(8,128)(2,1)} %param.9) | copy-start | bytes 589828
  27.4 23.1 %collective-permute-start.8 = (bf16[2,16,1,48,384]{4,3,1,2,0:T(8,128)(2,1)}, bf16[2,16,1,48,384]{4,3,1,2,0:T(8,128)(2,1)}, u32[]{:S(2)}, u32[]{:S(2)}) collective-permute-start(bf16[2,16,1,48,384]{4,3,1,2,0:T(8,128)(2,1)} %get-tuple-element.141), channel_id=1, source_target_pairs={{0,1},{1,0},{2,3},{3,2},{4,5},{5,4},{6,7},{7,6},{8,9},{9,8},{10,11... | collective-permute-start | bytes 3538952 | tf_op jit(solution)/shard_map/ppermute | solution.py:340
  32.0 6.0 %collective-permute-start.5 = (bf16[16,3,384]{2,1,0:T(4,128)(2,1)S(1)}, bf16[16,3,384]{2,1,0:T(4,128)(2,1)S(1)}, u32[]{:S(2)}, u32[]{:S(2)}) collective-permute-start(bf16[16,3,384]{2,1,0:T(4,128)(2,1)S(1)} %get-tuple-element.179), channel_id=1, source_target_pairs={{1,2},{2,1},{5,6},{6,5},{9,10},{10,9},{13,14},{14,13},{17,18},{18,... | collective-permute-start | bytes 110600 | tf_op jit(solution)/shard_map/ppermute | solution.py:316
  32.7 5.3 %collective-permute-start.4 = (bf16[16,3,384]{2,1,0:T(4,128)(2,1)S(1)}, bf16[16,3,384]{2,1,0:T(4,128)(2,1)S(1)}, u32[]{:S(2)}, u32[]{:S(2)}) collective-permute-start(bf16[16,3,384]{2,1,0:T(4,128)(2,1)S(1)} %get-tuple-element.180), channel_id=1, source_target_pairs={{0,1},{1,0},{2,3},{3,2},{4,5},{5,4},{6,7},{7,6},{8,9},{9,8},{10,11... | collective-permute-start | bytes 110600 | tf_op jit(solution)/shard_map/ppermute | solution.py:312
  38.2 9.5 %collective-permute-start.7 = (bf16[3,22,384]{2,1,0:T(8,128)(2,1)S(1)}, bf16[3,22,384]{2,1,0:T(8,128)(2,1)S(1)}, u32[]{:S(2)}, u32[]{:S(2)}) collective-permute-start(bf16[3,22,384]{2,1,0:T(8,128)(2,1)S(1)} %get-tuple-element.171), channel_id=1, source_target_pairs={{4,8},{12,16},{20,24},{8,4},{16,12},{24,20},{5,9},{13,17},{21,25},... | collective-permute-start | bytes 152072 | tf_op jit(solution)/shard_map/ppermute | solution.py:316
  39.1 10.8 %collective-permute-start.6 = (bf16[3,22,384]{2,1,0:T(8,128)(2,1)S(1)}, bf16[3,22,384]{2,1,0:T(8,128)(2,1)S(1)}, u32[]{:S(2)}, u32[]{:S(2)}) collective-permute-start(bf16[3,22,384]{2,1,0:T(8,128)(2,1)S(1)} %get-tuple-element.172), channel_id=1, source_target_pairs={{0,4},{4,0},{8,12},{12,8},{16,20},{20,16},{24,28},{28,24},{1,5},{5... | collective-permute-start | bytes 152072 | tf_op jit(solution)/shard_map/ppermute | solution.py:312
  52.3 12.1 %collective-permute-start.10 = (bf16[1,4,2,48,384]{4,3,2,1,0:T(8,128)(2,1)S(1)}, bf16[1,4,2,48,384]{4,3,2,1,0:T(8,128)(2,1)S(1)}, u32[]{:S(2)}, u32[]{:S(2)}) collective-permute-start(bf16[1,4,2,48,384]{4,3,2,1,0:T(8,128)(2,1)S(1)} %get-tuple-element.151), channel_id=1, source_target_pairs={{0,4},{1,5},{2,6},{3,7},{4,0},{5,1},{6,2},{7,3},{8,12},{9,13},{10,... | collective-permute-start | bytes 884744 | tf_op jit(solution)/shard_map/ppermute | solution.py:340
  55.2 9.2 %collective-permute-start.9 = (bf16[1,8,1,48,384]{4,3,1,2,0:T(8,128)(2,1)}, bf16[1,8,1,48,384]{4,3,1,2,0:T(8,128)(2,1)S(1)}, u32[]{:S(2)}, u32[]{:S(2)}) collective-permute-start(bf16[1,8,1,48,384]{4,3,1,2,0:T(8,128)(2,1)} %get-tuple-element.153), channel_id=1, source_target_pairs={{0,2},{1,3},{2,0},{3,1},{4,6},{5,7},{6,4},{7,5},{8,10},{9,11},{10,... | collective-permute-start | bytes 884744 | tf_op jit(solution)/shard_map/ppermute | solution.py:340
  64.7 9.4 %collective-permute-start.11 = (bf16[2,16,1,48,384]{4,3,1,2,0:T(8,128)(2,1)S(1)}, bf16[2,16,1,48,384]{4,3,1,2,0:T(8,128)(2,1)S(1)}, u32[]{:S(2)}, u32[]{:S(2)}) collective-permute-start(bf16[2,16,1,48,384]{4,3,1,2,0:T(8,128)(2,1)S(1)} %get-tuple-element.139), channel_id=1, source_target_pairs={{0,1},{1,0},{2,3},{3,2},{4,5},{5,4},{6,7},{7,6},{8,9},{9,8},{10,11... | collective-permute-start | bytes 3538952 | tf_op jit(solution)/shard_map/ppermute | solution.py:340
  64.8 6.5 %collective-permute-start.15 = (bf16[16,3,384]{2,1,0:T(4,128)(2,1)S(1)}, bf16[16,3,384]{2,1,0:T(4,128)(2,1)S(1)}, u32[]{:S(2)}, u32[]{:S(2)}) collective-permute-start(bf16[16,3,384]{2,1,0:T(4,128)(2,1)S(1)} %get-tuple-element.177), channel_id=1, source_target_pairs={{1,2},{2,1},{5,6},{6,5},{9,10},{10,9},{13,14},{14,13},{17,18},{18,... | collective-permute-start | bytes 110600 | tf_op jit(solution)/shard_map/ppermute | solution.py:316
  65.5 5.8 %collective-permute-start.14 = (bf16[16,3,384]{2,1,0:T(4,128)(2,1)S(1)}, bf16[16,3,384]{2,1,0:T(4,128)(2,1)S(1)}, u32[]{:S(2)}, u32[]{:S(2)}) collective-permute-start(bf16[16,3,384]{2,1,0:T(4,128)(2,1)S(1)} %get-tuple-element.178), channel_id=1, source_target_pairs={{0,1},{1,0},{2,3},{3,2},{4,5},{5,4},{6,7},{7,6},{8,9},{9,8},{10,11... | collective-permute-start | bytes 110600 | tf_op jit(solution)/shard_map/ppermute | solution.py:312
  67.6 5.8 %collective-permute-start.12 = (bf16[1,4,1,48,384]{4,3,1,2,0:T(8,128)(2,1)S(1)}, bf16[1,4,1,48,384]{4,3,1,2,0:T(8,128)(2,1)S(1)}, u32[]{:S(2)}, u32[]{:S(2)}) collective-permute-start(bf16[1,4,1,48,384]{4,3,1,2,0:T(8,128)(2,1)S(1)} %get-tuple-element.169), channel_id=1, source_target_pairs={{0,4},{1,5},{2,6},{3,7},{4,0},{5,1},{6,2},{7,3},{8,12},{9,13},{10,... | collective-permute-start | bytes 442376 | tf_op jit(solution)/shard_map/ppermute | solution.py:340
  67.8 6.2 %collective-permute-start.13 = (bf16[1,4,1,48,384]{4,3,2,1,0:T(8,128)(2,1)S(1)}, bf16[1,4,1,48,384]{4,3,2,1,0:T(8,128)(2,1)S(1)}, u32[]{:S(2)}, u32[]{:S(2)}) collective-permute-start(bf16[1,4,1,48,384]{4,3,2,1,0:T(8,128)(2,1)S(1)} %get-tuple-element.167), channel_id=1, source_target_pairs={{0,2},{1,3},{2,0},{3,1},{4,6},{5,7},{6,4},{7,5},{8,10},{9,11},{10,... | collective-permute-start | bytes 442376 | tf_op jit(solution)/shard_map/ppermute | solution.py:340
  74.6 9.2 %collective-permute-start.21 = (bf16[128,384]{1,0:T(8,128)(2,1)S(1)}, bf16[128,384]{1,0:T(8,128)(2,1)S(1)}, u32[]{:S(2)}, u32[]{:S(2)}) collective-permute-start(bf16[128,384]{1,0:T(8,128)(2,1)S(1)} %pad_maximum_fusion.7), channel_id=1, source_target_pairs={{0,1},{1,0},{2,3},{3,2},{4,5},{5,4},{6,7},{7,6},{8,9},{9,8},{10,11... | collective-permute-start | bytes 294920 | tf_op jit(solution)/shard_map/ppermute | solution.py:340
  74.9 7.2 %collective-permute-start.19 = (bf16[3,22,384]{2,1,0:T(8,128)(2,1)S(1)}, bf16[3,22,384]{2,1,0:T(8,128)(2,1)S(1)}, u32[]{:S(2)}, u32[]{:S(2)}) collective-permute-start(bf16[3,22,384]{2,1,0:T(8,128)(2,1)S(1)} %get-tuple-element.165), channel_id=1, source_target_pairs={{4,8},{12,16},{20,24},{8,4},{16,12},{24,20},{5,9},{13,17},{21,25},... | collective-permute-start | bytes 152072 | tf_op jit(solution)/shard_map/ppermute | solution.py:316
  75.6 8.3 %collective-permute-start.18 = (bf16[3,22,384]{2,1,0:T(8,128)(2,1)S(1)}, bf16[3,22,384]{2,1,0:T(8,128)(2,1)S(1)}, u32[]{:S(2)}, u32[]{:S(2)}) collective-permute-start(bf16[3,22,384]{2,1,0:T(8,128)(2,1)S(1)} %get-tuple-element.166), channel_id=1, source_target_pairs={{0,4},{4,0},{8,12},{12,8},{16,20},{20,16},{24,28},{28,24},{1,5},{5... | collective-permute-start | bytes 152072 | tf_op jit(solution)/shard_map/ppermute | solution.py:312
  80.1 5.8 %collective-permute-start.20 = (bf16[2,2,1,48,384]{4,3,1,0,2:T(8,128)(2,1)S(1)}, bf16[2,2,1,48,384]{4,3,1,0,2:T(8,128)(2,1)S(1)}, u32[]{:S(2)}, u32[]{:S(2)}) collective-permute-start(bf16[2,2,1,48,384]{4,3,1,0,2:T(8,128)(2,1)S(1)} %get-tuple-element.163), channel_id=1, source_target_pairs={{0,8},{1,9},{2,10},{3,11},{4,12},{5,13},{6,14},{7,15},{8,0},{9,1},... | collective-permute-start | bytes 442376 | tf_op jit(solution)/shard_map/ppermute | solution.py:340
  81.7 11.0 %collective-permute-start.17 = (bf16[1,4,2,48,384]{4,3,2,1,0:T(8,128)(2,1)S(1)}, bf16[1,4,2,48,384]{4,3,2,1,0:T(8,128)(2,1)S(1)}, u32[]{:S(2)}, u32[]{:S(2)}) collective-permute-start(bf16[1,4,2,48,384]{4,3,2,1,0:T(8,128)(2,1)S(1)} %get-tuple-element.147), channel_id=1, source_target_pairs={{0,4},{1,5},{2,6},{3,7},{4,0},{5,1},{6,2},{7,3},{8,12},{9,13},{10,... | collective-permute-start | bytes 884744 | tf_op jit(solution)/shard_map/ppermute | solution.py:340
  82.1 10.6 %collective-permute-start.16 = (bf16[1,8,1,48,384]{4,3,1,2,0:T(8,128)(2,1)S(1)}, bf16[1,8,1,48,384]{4,3,1,2,0:T(8,128)(2,1)S(1)}, u32[]{:S(2)}, u32[]{:S(2)}) collective-permute-start(bf16[1,8,1,48,384]{4,3,1,2,0:T(8,128)(2,1)S(1)} %get-tuple-element.149), channel_id=1, source_target_pairs={{0,2},{1,3},{2,0},{3,1},{4,6},{5,7},{6,4},{7,5},{8,10},{9,11},{10,... | collective-permute-start | bytes 884744 | tf_op jit(solution)/shard_map/ppermute | solution.py:340
  85.9 6.5 %collective-permute-start.22 = (bf16[2,1,1,48,384]{4,3,1,0,2:T(8,128)(2,1)S(1)}, bf16[2,1,1,48,384]{4,3,1,0,2:T(8,128)(2,1)S(1)}, u32[]{:S(2)}, u32[]{:S(2)}) collective-permute-start(bf16[2,1,1,48,384]{4,3,1,0,2:T(8,128)(2,1)S(1)} %get-tuple-element.189), channel_id=1, source_target_pairs={{0,16},{1,17},{2,18},{3,19},{4,20},{5,21},{6,22},{7,23},{8,24},{9,... | collective-permute-start | bytes 221192 | tf_op jit(solution)/shard_map/ppermute | solution.py:340
  88.0 4.7 %collective-permute-start.23 = (bf16[128,384]{1,0:T(8,128)(2,1)S(1)}, bf16[128,384]{1,0:T(8,128)(2,1)S(1)}, u32[]{:S(2)}, u32[]{:S(2)}) collective-permute-start(bf16[128,384]{1,0:T(8,128)(2,1)S(1)} %add_convert_fusion.16), channel_id=1, source_target_pairs={{0,2},{1,3},{2,0},{3,1},{4,6},{5,7},{6,4},{7,5},{8,10},{9,11},{10,... | collective-permute-start | bytes 294920 | tf_op jit(solution)/shard_map/ppermute | solution.py:340
  92.8 5.2 %collective-permute-start.26 = (bf16[128,384]{1,0:T(8,128)(2,1)S(1)}, bf16[128,384]{1,0:T(8,128)(2,1)S(1)}, u32[]{:S(2)}, u32[]{:S(2)}) collective-permute-start(bf16[128,384]{1,0:T(8,128)(2,1)S(1)} %add_convert_fusion.15), channel_id=1, source_target_pairs={{0,4},{1,5},{2,6},{3,7},{4,0},{5,1},{6,2},{7,3},{8,12},{9,13},{10,... | collective-permute-start | bytes 294920 | tf_op jit(solution)/shard_map/ppermute | solution.py:340
  94.4 5.2 %collective-permute-start.24 = (bf16[1,4,1,48,384]{4,3,1,2,0:T(8,128)(2,1)S(1)}, bf16[1,4,1,48,384]{4,3,1,2,0:T(8,128)(2,1)S(1)}, u32[]{:S(2)}, u32[]{:S(2)}) collective-permute-start(bf16[1,4,1,48,384]{4,3,1,2,0:T(8,128)(2,1)S(1)} %get-tuple-element.161), channel_id=1, source_target_pairs={{0,4},{1,5},{2,6},{3,7},{4,0},{5,1},{6,2},{7,3},{8,12},{9,13},{10,... | collective-permute-start | bytes 442376 | tf_op jit(solution)/shard_map/ppermute | solution.py:340
  95.2 5.2 %collective-permute-start.25 = (bf16[1,4,1,48,384]{4,3,2,1,0:T(8,128)(2,1)S(1)}, bf16[1,4,1,48,384]{4,3,2,1,0:T(8,128)(2,1)S(1)}, u32[]{:S(2)}, u32[]{:S(2)}) collective-permute-start(bf16[1,4,1,48,384]{4,3,2,1,0:T(8,128)(2,1)S(1)} %get-tuple-element.159), channel_id=1, source_target_pairs={{0,2},{1,3},{2,0},{3,1},{4,6},{5,7},{6,4},{7,5},{8,10},{9,11},{10,... | collective-permute-start | bytes 442376 | tf_op jit(solution)/shard_map/ppermute | solution.py:340
  100.4 4.7 %collective-permute-start.28 = (bf16[128,384]{1,0:T(8,128)(2,1)S(1)}, bf16[128,384]{1,0:T(8,128)(2,1)S(1)}, u32[]{:S(2)}, u32[]{:S(2)}) collective-permute-start(bf16[128,384]{1,0:T(8,128)(2,1)S(1)} %add_convert_fusion.14), channel_id=1, source_target_pairs={{0,8},{1,9},{2,10},{3,11},{4,12},{5,13},{6,14},{7,15},{8,0},{9,1},... | collective-permute-start | bytes 294920 | tf_op jit(solution)/shard_map/ppermute | solution.py:340
  102.2 5.9 %collective-permute-start.27 = (bf16[2,2,1,48,384]{4,3,0,2,1:T(8,128)(2,1)S(1)}, bf16[2,2,1,48,384]{4,3,0,2,1:T(8,128)(2,1)S(1)}, u32[]{:S(2)}, u32[]{:S(2)}) collective-permute-start(bf16[2,2,1,48,384]{4,3,0,2,1:T(8,128)(2,1)S(1)} %copy.30), channel_id=1, source_target_pairs={{0,8},{1,9},{2,10},{3,11},{4,12},{5,13},{6,14},{7,15},{8,0},{9,1},... | collective-permute-start | bytes 442376 | tf_op jit(solution)/shard_map/ppermute | solution.py:340
  108.1 5.7 %collective-permute-start.30 = (bf16[2,1,1,48,384]{4,3,0,2,1:T(8,128)(2,1)S(1)}, bf16[2,1,1,48,384]{4,3,0,2,1:T(8,128)(2,1)S(1)}, u32[]{:S(2)}, u32[]{:S(2)}) collective-permute-start(bf16[2,1,1,48,384]{4,3,0,2,1:T(8,128)(2,1)S(1)} %constant_dynamic-slice_fusion), channel_id=1, source_target_pairs={{0,16},{1,17},{2,18},{3,19},{4,20},{5,21},{6,22},{7,23},{8,24},{9,... | collective-permute-start | bytes 221192 | tf_op jit(solution)/shard_map/ppermute | solution.py:340
  110.5 6.6 %collective-permute-start.29 = (bf16[128,384]{1,0:T(8,128)(2,1)S(1)}, bf16[128,384]{1,0:T(8,128)(2,1)S(1)}, u32[]{:S(2)}, u32[]{:S(2)}) collective-permute-start(bf16[128,384]{1,0:T(8,128)(2,1)S(1)} %add_convert_fusion.13), channel_id=1, source_target_pairs={{0,16},{1,17},{2,18},{3,19},{4,20},{5,21},{6,22},{7,23},{8,24},{9,... | collective-permute-start | bytes 294920 | tf_op jit(solution)/shard_map/ppermute | solution.py:340
  (5 other events, 27.0 us)

commit v4 on v3

--- a/solution.py
+++ b/solution.py
@@ -156,8 +156,13 @@
             part = jnp.sum(gradient, axis=0, keepdims=True)
             bias_sum = part if bias_sum is None else bias_sum + part
         db[:, cut] = bias_sum
-        dw[1, cut, :] = dot_tn(act[:, cut], grad[...]).astype(BF16)
-        dw[0, cut, :] = dot_tn(gpre[:, cut], normed[...]).astype(BF16)
+        if dw is not None:
+            weight_grads(normed, grad, act, gpre, dw, cut)
+
+
+def weight_grads(normed, grad, act, gpre, dw, cut):
+    dw[1, cut, :] = dot_tn(act[:, cut], grad[...]).astype(BF16)
+    dw[0, cut, :] = dot_tn(gpre[:, cut], normed[...]).astype(BF16)
 
 
 def fetch_layers(triples, arrived):
@@ -222,14 +227,14 @@
 
 
 def top_kernel(
-    mids, grad, taps, gains, shifts, w_in, w_out, b_in, dz_out, dw, db, dgain, dshift,
-    z, normed, act, gpre, w_in1, w_out1, arrived,
+    mids, grad, taps, gains, shifts, w_in, w_out, b_in,
+    dz_out, normed, act, gpre, db, dgain, dshift, z, w_in1, w_out1, arrived,
 ):
     waits = fetch_layers(((w_in, 1, w_in1), (w_out, 1, w_out1)), arrived)
     conv_pass(mids, 0, 0, taps.at[1], z, *z.shape[1:3])
     block_back(
         z, grad, 1, gains, shifts, (w_in1, w_out1, waits), b_in,
-        (dz_out, dw, db, dgain, dshift), (normed, act, gpre),
+        (dz_out, None, db, dgain, dshift), (normed, act, gpre),
     )
 
 
@@ -278,7 +283,9 @@
     out[...] = sums[...].astype(BF16)
 
 
-def top_taps_kernel(source, dz, db, dgain, dshift, out, dzs, sums):
+def top_taps_kernel(source, dz, normed, act, gpre, grad, db, dgain, dshift, dw, out, dzs, sums):
+    for cut in hidden_chunks(act.shape[1]):
+        weight_grads(normed, grad, act, gpre, dw, cut)
     taps_kernel(source, 0, 0, dz, db, dgain, dshift, out, None, dzs, sums)
 
 
@@ -306,32 +313,27 @@
     )(*args)
 
 
-def swap_edges(low_edge, high_edge, axis):
+def edges(tile, axis, width, odd):
+    count = tile.shape[axis]
+    low = lax.slice_in_dim(tile, 0, width, axis=axis)
+    high = lax.slice_in_dim(tile, count - width, count, axis=axis)
+    return jnp.where(odd, low, high), jnp.where(odd, high, low)
+
+
+def to_twin(edge, axis):
     count = lax.axis_size(axis)
-    odd = lax.axis_index(axis) % 2 == 1
-    first = lax.ppermute(
-        jnp.where(odd, low_edge, high_edge), axis, [(i, i ^ 1) for i in range(count) if i ^ 1 < count]
-    )
-    pairs = [(i, i + 1) for i in range(1, count - 1, 2)]
-    second = lax.ppermute(
-        jnp.where(odd, high_edge, low_edge), axis, pairs + [(j, i) for i, j in pairs]
-    )
-    return jnp.where(odd, first, second), jnp.where(odd, second, first)
-
-
-def edges(tile, axis):
-    count = tile.shape[axis]
-    return (
-        lax.slice_in_dim(tile, 0, HALO, axis=axis),
-        lax.slice_in_dim(tile, count - HALO, count, axis=axis),
-    )
-
-
-def padded_tile(tile, width):
-    low, high = swap_edges(tile[:, :width], tile[:, -width:], "cols")
-    wide = jnp.concatenate([low, tile, high], axis=1)
-    low, high = swap_edges(wide[:width], wide[-width:], "rows")
-    return jnp.concatenate([low, wide, high], axis=0)
+    return lax.ppermute(edge, axis, [(i, i ^ 1) for i in range(count) if i ^ 1 < count])
+
+
+def to_other(edge, axis):
+    pairs = [(i, i + 1) for i in range(1, lax.axis_size(axis) - 1, 2)]
+    return lax.ppermute(edge, axis, pairs + [(j, i) for i, j in pairs])
+
+
+def rimmed(tile, from_twin, from_other, axis, odd):
+    low = jnp.where(odd, from_twin, from_other)
+    high = jnp.where(odd, from_other, from_twin)
+    return jnp.concatenate([low, tile, high], axis=axis)
 
 
 def flip_bit(value, bit):
@@ -350,12 +352,21 @@
     return (own.astype(F32) + got.astype(F32)).astype(BF16)
 
 
-def step(chunks, order, bit, mine):
+def step(chunks, order, bit, mine, *riders):
     spot = order.index(bit)
     per = chunks.shape[-2:]
     pair = chunks.reshape((-1, 2 ** spot, 2, 2 ** (len(order) - spot - 1)) + per)
     send, keep = halves(pair, 2, mine[bit])
-    return keep, flip_bit(send, bit), [b for b in order if b != bit]
+    left = [b for b in order if b != bit]
+    if not riders:
+        return keep, flip_bit(send, bit), left, ()
+    parts = [part.reshape(-1, per[-1]) for part in (send,) + riders]
+    got = flip_bit(jnp.concatenate(parts, axis=0), bit)
+    came, first = [], 0
+    for part, like in zip(parts, (send,) + riders):
+        came.append(got[first : first + part.shape[0]].reshape(like.shape))
+        first += part.shape[0]
+    return keep, came[0], left, tuple(came[1:])
 
 
 def shards(activations, grad_out, kernels, norm_gains, norm_shifts, w_in, b_in, w_out):
@@ -384,27 +395,31 @@
     ).astype(jnp.int32)
     grad_flat = grad_out.reshape(pixels, channels)
 
-    def widened(tile, width, to):
-        wide = padded_tile(tile, width)
-        return jnp.pad(wide, ((0, 0), (0, to - wide.shape[1]), (0, 0)))
+    odd_col = lax.axis_index("cols") % 2 == 1
+    odd_row = lax.axis_index("rows") % 2 == 1
+
+    def rim_cols(tile, width):
+        twin, other = edges(tile, 1, width, odd_col)
+        return rimmed(tile, to_twin(twin, "cols"), to_other(other, "cols"), 1, odd_col)
+
+    def rim_rows(tile, width):
+        twin, other = edges(tile, 0, width, odd_row)
+        return rimmed(tile, to_twin(twin, "rows"), to_other(other, "rows"), 0, odd_row)
+
+    def filled(wide):
+        return jnp.pad(wide, ((0, 0), (0, cols + 16 - wide.shape[1]), (0, 0)))
 
     mid_rows, mid_cols = rows + 2 * HALO, cols + 8
     strip = max(d for d in range(1, mid_rows + 1) if mid_rows % d == 0 and d * mid_cols <= 264)
     weights = [shape(1, channels, hidden, dtype=BF16)] * 2
-    tile_scratch = [
-        shape(pixels, channels, dtype=BF16),
-        shape(pixels, hidden, dtype=BF16),
-        shape(pixels, hidden, dtype=BF16),
-    ] + weights
     tile_z = shape(groups, rows, cols, LANES)
     tile_b = shape(pixels, channels, dtype=BF16)
-    back_outs = (
-        tile_b, shape(2, hidden, channels, dtype=BF16),
-        shape(1, hidden), shape(1, channels), shape(1, channels),
-    )
+    tile_h = shape(pixels, hidden, dtype=BF16)
+    grads_b = shape(2, hidden, channels, dtype=BF16)
+    small_outs = (shape(1, hidden), shape(1, channels), shape(1, channels))
     small_rows = 64
 
-    xpad = widened(activations, WIDE, cols + 16)
+    xpad = filled(rim_rows(rim_cols(activations, WIDE), WIDE))
     mids, z0 = run(
         forward_kernel,
         (shape(groups, mid_rows, mid_cols, LANES), tile_z),
@@ -419,88 +434,90 @@
         fetched=2,
         name="forward",
     )
-    dz1, dw1, *small1 = run(
+    dz1, normed1, act1, gpre1, *small1 = run(
         top_kernel,
-        back_outs,
-        [tile_z] + tile_scratch,
+        (tile_b, tile_b, tile_h, tile_h) + small_outs,
+        [tile_z] + weights,
         (mids, grad_flat, taps, norm_gains, norm_shifts, w_in, w_out, biases),
         [None] * 5 + [pl.ANY] * 2 + [None],
         fetched=2,
         name="top",
     )
-    fence = lax.optimization_barrier
+
     per = hidden // total
-    every = list(range(bits - 1, -1, -1))
     sides = (col_bits - 1, col_bits)
 
-    def start(dw):
-        chunks, order = dw.reshape(2, total, per, channels), every
-        for bit in range(col_bits - 2):
-            keep, got, order = step(chunks, order, bit, mine)
-            chunks = summed(keep, got)
-        if col_bits > 1:
-            return step(chunks, order, col_bits - 2, mine)
-        return chunks, None, order
+    def fenced(*values):
+        leaves, tree = jax.tree.flatten(values)
+        arrays = [i for i, leaf in enumerate(leaves) if not isinstance(leaf, int)]
+        for i, value in zip(arrays, lax.optimization_barrier(tuple(leaves[i] for i in arrays))):
+            leaves[i] = value
+        return jax.tree.unflatten(tree, leaves)
 
     def settled(flight):
-        keep, got, order = flight
-        return (keep if got is None else summed(keep, got)), order
-
-    def fork(flight):
+        return summed(flight[0], flight[1]), flight[2]
+
+    def start(dw, small, *riders):
+        chunks, order = dw.reshape(2, total, per, channels), list(range(bits - 1, -1, -1))
+        came = ()
+        for bit in range(col_bits - 1):
+            if bit:
+                chunks, order = settled(flight)
+                small = [summed(s, g) for s, g in zip(small, small_got)]
+            flight = step(chunks, order, bit, mine, *small, *(() if bit else riders))
+            small_got = flight[3][: len(small)]
+            came = came or flight[3][len(small) :]
+        return flight[:3], small, small_got, came
+
+    def fork(flight, first=(), second=()):
         chunks, order = settled(flight)
-        return [step(chunks[i], order, sides[i], mine) for i in range(2)]
-
-    def cross(flights):
+        return [step(chunks[i], order, sides[i], mine, *r) for i, r in enumerate((first, second))]
+
+    def cross(flights, first=()):
         done = [settled(f) for f in flights]
-        return [step(done[i][0], done[i][1], sides[1 - i], mine) for i in range(2)]
+        return [step(*done[i], sides[1 - i], mine, *r) for i, r in enumerate((first, ()))]
 
     def merge(flights):
         done = [settled(f) for f in flights]
         return jnp.stack([d[0].reshape(-1, per, channels) for d in done]), done[0][1]
 
-    def onward(chunks, order):
-        return step(chunks, order, order[-1], mine)
-
-    def fenced(values):
-        leaves, tree = jax.tree.flatten(values)
-        arrays = [i for i, leaf in enumerate(leaves) if not isinstance(leaf, int)]
-        for i, value in zip(arrays, fence(tuple(leaves[i] for i in arrays))):
-            leaves[i] = value
-        return jax.tree.unflatten(tree, leaves)
-
-    dz1, dw1 = fence((dz1, dw1))
-    sides1 = swap_edges(*edges(dz1.reshape(rows, cols, channels), 1), "cols")
-    run1 = start(dw1)
-    (small1,) = run(
+    def onward(chunks, order, *riders):
+        return step(chunks, order, order[-1], mine, *riders)
+
+    def finish(flight):
+        chunks, order = settled(flight)
+        while order:
+            chunks, order = settled(onward(chunks, order))
+        return jnp.swapaxes(chunks.reshape(2, per, channels).astype(F32) * grad_scale, 1, 2)
+
+    tile1 = dz1.reshape(rows, cols, channels)
+    twin, other = edges(tile1, 1, HALO, odd_col)
+    twin, other = to_twin(twin, "cols"), to_other(other, "cols")
+    dw1, small1 = run(
         top_taps_kernel,
-        (shape(small_rows, channels, dtype=BF16),),
+        (grads_b, shape(small_rows, channels, dtype=BF16)),
         [tile_z, shape(small_rows, channels)],
-        (mids, dz1, *small1),
+        (mids, dz1, normed1, act1, gpre1, grad_flat, *small1),
         name="top_taps",
     )
-    sides1, dz1, small1 = fenced((sides1, dz1, small1))
-    wide1 = jnp.concatenate([sides1[0], dz1.reshape(rows, cols, channels), sides1[1]], axis=1)
-    ends1 = swap_edges(*edges(wide1, 0), "rows")
-    ends1, wide1, run1 = fenced((ends1, wide1, run1))
+    tile1, twin, other, dw1, small1 = fenced(tile1, twin, other, dw1, small1)
+    wide1 = rimmed(tile1, twin, other, 1, odd_col)
+    run1, _, _, _ = start(dw1, [])
+    twin, other = edges(wide1, 0, HALO, odd_row)
+    twin, other = to_twin(twin, "rows"), to_other(other, "rows")
+    wide1, twin, other, run1 = fenced(wide1, twin, other, run1)
     pair1 = fork(run1)
-    dzpad1 = jnp.pad(
-        jnp.concatenate([ends1[0], wide1, ends1[1]], axis=0),
-        ((0, 0), (0, 16 - 2 * HALO), (0, 0)),
-    )
+    dzpad1 = filled(rimmed(wide1, twin, other, 0, odd_row))
     spread_scratch = [shape(groups, *dzpad1.shape[:2], LANES), tile_z]
     grad_mid, dz0, dw0, *small0 = run(
         low_kernel,
-        (tile_b,) + back_outs,
-        spread_scratch + tile_scratch,
+        (tile_b, tile_b, grads_b) + small_outs,
+        spread_scratch + [tile_b, tile_h, tile_h] + weights,
         (dzpad1, grad_flat, z0, taps_back, norm_gains, norm_shifts, w_in, w_out, biases),
         [None] * 6 + [pl.ANY] * 2 + [None],
         fetched=2,
         name="low",
     )
-    dz0, dw0, pair1 = fenced((dz0, dw0, pair1))
-    run0 = start(dw0)
-    pair1 = cross(pair1)
-    sides0 = swap_edges(*edges(dz0.reshape(rows, cols, channels), 1), "cols")
     (small0,) = run(
         low_taps_kernel,
         (shape(small_rows, channels, dtype=BF16),),
@@ -508,48 +525,40 @@
         (xpad, dz0, *small0),
         name="low_taps",
     )
+    dz0, dw0, pair1, small0 = fenced(dz0, dw0, pair1, small0)
+    tile0 = dz0.reshape(rows, cols, channels)
     small = jnp.concatenate([small0, small1], axis=0)
-    run0, pair1, sides0, small, dz0 = fenced((run0, pair1, sides0, small, dz0))
-    pair0 = fork(run0)
-    wide0 = jnp.concatenate([sides0[0], dz0.reshape(rows, cols, channels), sides0[1]], axis=1)
-    ends0 = swap_edges(*edges(wide0, 0), "rows")
+    twin, other = edges(tile0, 1, HALO, odd_col)
+    run0, (small,), small_got, (twin,) = start(dw0, [small], twin)
+    other = to_other(other, "cols")
+    pair1 = cross(pair1)
+    run0, small, small_got, tile0, twin, other = fenced(run0, small, small_got, tile0, twin, other)
+    small = summed(small, small_got[0])
+    wide0 = rimmed(tile0, twin, other, 1, odd_col)
+    twin, other = edges(wide0, 0, HALO, odd_row)
+    pair0 = fork(run0, (small,), (twin,))
+    other = to_other(other, "rows")
+    pair0, pair1, small, wide0, other = fenced(pair0, pair1, small, wide0, other)
+    small = summed(small, pair0[0][3][0])
+    twin = pair0[1][3][0]
+    pair0 = cross(pair0, (small,))
     run1 = onward(*merge(pair1))
-    small_got = flip_bit(small, 0)
-    ends0, wide0, run1, small, small_got = fenced((ends0, wide0, run1, small, small_got))
-    run1 = onward(*settled(run1)) if len(run1[2]) else run1
-    small = summed(small, small_got)
-    small_got = flip_bit(small, 1)
-    dzpad0 = jnp.pad(
-        jnp.concatenate([ends0[0], wide0, ends0[1]], axis=0),
-        ((0, 0), (0, 16 - 2 * HALO), (0, 0)),
-    )
     (grad_in,) = run(
-        last_kernel, (tile_b,), spread_scratch, (dzpad0, grad_mid, taps_back), name="last"
-    )
-    pair0, run1, small, small_got, grad_in = fenced((pair0, run1, small, small_got, grad_in))
-    pair0 = cross(pair0)
-    small = summed(small, small_got)
-    small_got = flip_bit(small, 2)
-
-    def finish(flight):
-        chunks, order = settled(flight)
-        while order:
-            chunks, order = settled(onward(chunks, order))
-        return jnp.swapaxes(chunks.reshape(2, per, channels).astype(F32) * grad_scale, 1, 2)
-
+        last_kernel,
+        (tile_b,),
+        spread_scratch,
+        (filled(rimmed(wide0, twin, other, 0, odd_row)), grad_mid, taps_back),
+        name="last",
+    )
+    pair0, run1, small, grad_in = fenced(pair0, run1, small, grad_in)
+    small = summed(small, pair0[0][3][0])
+    run0 = onward(*merge(pair0), small)
     share1 = finish(run1)
-    pair0, small, small_got = fenced((pair0, small, small_got))
-    run0 = onward(*merge(pair0))
-    small = summed(small, small_got)
-    bit = 3
     while run0[2]:
-        small_got = flip_bit(small, bit)
-        run0, small, small_got = fenced((run0, small, small_got))
-        run0 = onward(*settled(run0))
-        small = summed(small, small_got)
-        bit += 1
-    for left in range(bit, bits):
-        small = summed(small, flip_bit(small, left))
+        run0, small = fenced(run0, small)
+        small = summed(small, run0[3][0])
+        run0 = onward(*settled(run0), small)
+    small = summed(small, run0[3][0])
     shares = [finish(run0), share1]
     small = small.reshape(layers, small_rows, channels).astype(F32) * grad_scale
     count = hidden // channels

time: 120 us -> 138 us (1.15)
  starting transfers between devices: 52.8 us -> 37.8 us
  waiting for transfers between devices: 23.3 us -> 36.3 us
  local copies, waits for them, and re-layouts: 5.27 us -> 18 us
  other arithmetic: 7.98 us -> 15.5 us
    ppermute x19 -> x14, starting transfers between devices: 26.7 us -> 13.5 us  [flip_bit(): return lax.ppermute(value, both, [(i, i ^ 1 << bit) for i in range(total)])]
    ppermute x19 -> x14, waiting for transfers between devices: 18.8 us -> 31.8 us  [flip_bit(): return lax.ppermute(value, both, [(i, i ^ 1 << bit) for i in range(total)])]
    slice x2 -> x15, local copies, waits for them, and re-layouts: 0.24 us -> 5.09 us  [the longest x13 4.85 us: step(): came.append(got[first:first + part.shape[0]].reshape(like.shape))]
    convert_element_type x16, other arithmetic: 2.51 us -> 6.98 us  [summed(): return (own.astype(F32) + got.astype(F32)).astype(BF16)]
    unnamed x14 -> x32, local copies, waits for them, and re-layouts: 0.64 us -> 4.05 us
    squeeze x13 -> x7, local copies, waits for them, and re-layouts: 2.76 us -> 5.64 us  [halves(): other = lax.dynamic_index_in_dim(chunks, 1 - mine, dim, keepdims=False)]
    ppermute x12 -> x10, starting transfers between devices: 26.1 us -> 24.3 us  [the longest x4 19.6 us: to_twin(): lax.ppermute(edge, axis, [(i, i ^ 1) for i in range(count) if i ^ 1 < cou...]
    concatenate x5 -> x11, other arithmetic: 1.42 us -> 2.97 us  [the longest x6 2.37 us: step(): got = flip_bit(jnp.concatenate(parts, axis=0), bit)]
  transfers between devices with their start and end apart: 31 -> 24, of which waited for: 14 -> 11; matrix products, arithmetic and copies ran while one was open for 4% -> 10% of each run, Pallas kernels for 11% -> 11%
where the time goes in v4:
time: 138 us; the launch traced here: 137 us
  starting transfers between devices  37.8 us (27%)
  waiting for transfers between devices  36.3 us (26%)
  Pallas kernels  28.5 us (21%)
  local copies, waits for them, and re-layouts  18 us (13%)
  other arithmetic  15.5 us (11%)
  between operations  1.39 us (1%)
    ppermute x14, waiting for transfers between devices, flip_bit(): return lax.ppermute(value, both, [(i, i ^ 1 << bit) for i in range(total)])  31.8 us
    pallas_call x6, Pallas kernels, run(): pl.pallas_call(kernel, out_shape=outs, in_specs=[vmem if s is None else p...  28.5 us
    ppermute x4, starting transfers between devices, to_twin(): lax.ppermute(edge, axis, [(i, i ^ 1) for i in range(count) if i ^ 1 < cou...  19.6 us
    ppermute x14, starting transfers between devices, flip_bit(): return lax.ppermute(value, both, [(i, i ^ 1 << bit) for i in range(total)])  13.5 us
    convert_element_type x16, other arithmetic, summed(): return (own.astype(F32) + got.astype(F32)).astype(BF16)  6.98 us
    squeeze x7, local copies, waits for them, and re-layouts, halves(): other = lax.dynamic_index_in_dim(chunks, 1 - mine, dim, keepdims=False)  5.64 us
    slice x13, local copies, waits for them, and re-layouts, step(): came.append(got[first:first + part.shape[0]].reshape(like.shape))  4.85 us
    ppermute x6, starting transfers between devices, to_other(): return lax.ppermute(edge, axis, pairs + [(j, i) for i, j in pairs])  4.74 us
  transfers between devices with their start and end apart: 24, of which 11 were waited for; matrix products, arithmetic and copies ran while one was open for 10% of the time, Pallas kernels for 11%

profile of v4, /device:TPU:0, one launch (start us, length us, event | category | flops | bytes accessed | tf_op | source)
XLA Modules:
  0.0 137.4 jit_solution(10117037695445803441)
XLA Ops:
  4.3 2.9 %collective-permute-start.2 = (bf16[6,28,384]{2,1,0:T(8,128)(2,1)S(1)}, bf16[6,28,384]{2,1,0:T(8,128)(2,1)S(1)}, u32[]{:S(2)}, u32[]{:S(2)}) collective-permute-start(bf16[6,28,384]{2,1,0:T(8,128)(2,1)S(1)} %get-tuple-element.157), channel_id=1, source_target_pairs={{0,4},{4,0},{8,12},{12,8},{16,20},{20,16},{24,28},{28,24},{1,5},{5... | collective-permute-start | bytes 387080 | tf_op jit(solution)/shard_map/ppermute | solution.py:325
  8.2 2.1 %collective-permute-done.2 = bf16[6,28,384]{2,1,0:T(8,128)(2,1)S(1)} collective-permute-done((bf16[6,28,384]{2,1,0:T(8,128)(2,1)S(1)}, bf16[6,28,384]{2,1,0:T(8,128)(2,1)S(1)}, u32[]{:S(2)}, u32[]{:S(2)}) %collective-permute-start.2) | collective-permute-done | bytes 129056 | tf_op jit(solution)/shard_map/ppermute | solution.py:325
  10.6 8.6 %forward.1 = (f32[3,22,24,128]{3,2,1,0:T(8,128)S(1)}, f32[3,16,16,128]{3,2,1,0:T(8,128)S(1)}) custom-call(s32[4]{0:T(128)S(1)} %pad_add_fusion.place, bf16[28,32,384]{2,1,0:T(8,128)(2,1)S(1)} %fusion.12.xpad.source, f32[2,3,49,128]{3,2,1,0:T(8,128)S(1)} %bitcast.91, f32[2,384]{1,0:T(2,128)S(1)} %copy-done.3, f32[2,384]{1,0:T(2,128)S(1)} %copy-done.4, ...), custom_call_target="tpu_custom_call" | custom-call | tf_op jit(solution)/shard_map/forward/pallas_call | solution.py:303
  19.3 4.6 %top.1 = (bf16[256,384]{1,0:T(8,128)(2,1)S(1)}, bf16[256,384]{1,0:T(8,128)(2,1)S(1)}, bf16[256,1536]{1,0:T(8,128)(2,1)S(1)}, bf16[256,1536]{1,0:T(8,128)(2,1)S(1...) custom-call(f32[3,22,24,128]{3,2,1,0:T(8,128)S(1)} %get-tuple-element.74.mids.source, ...), custom_call_target="tpu_custom_call" | custom-call | tf_op jit(solution)/shard_map/top/pallas_call | solution.py:303
  26.7 7.5 %collective-permute-start.4 = (bf16[16,3,384]{2,1,0:T(4,128)(2,1)}, bf16[16,3,384]{2,1,0:T(4,128)(2,1)}, u32[]{:S(2)}, u32[]{:S(2)}) collective-permute-start(bf16[16,3,384]{2,1,0:T(4,128)(2,1)} %get-tuple-element.182), channel_id=1, source_target_pairs={{0,1},{1,0},{2,3},{3,2},{4,5},{5,4},{6,7},{7,6},{8,9},{9,8},{10,11... | collective-permute-start | bytes 110600 | tf_op jit(solution)/shard_map/ppermute | solution.py:325
  35.3 4.2 %top_taps.1 = (bf16[2,1536,384]{2,1,0:T(8,128)(2,1)}, bf16[64,384]{1,0:T(8,128)(2,1)S(1)}) custom-call(f32[3,22,24,128]{3,2,1,0:T(8,128)S(1)} %get-tuple-element.74.mids.source, bf16[256,384]{1,0:T(8,128)(2,1)S(1)} %get-tuple-element.75.dz, bf16[256,384]{1,0:T(8,128)(2,1)S(1)} %get-tuple-element.76.normed, bf16[256,1536]{1,0:T(8,128)(2,1)S(1)} %get-tuple-element.77.act, ...), custom_call_target="tpu_custom_call" | custom-call | tf_op jit(solution)/shard_map/top_taps/pallas_call | solution.py:303
  39.5 3.3 %dynamic-slice_bitcast_fusion.1 = (bf16[2,16,1,48,384]{4,3,1,2,0:T(8,128)(2,1)}, bf16[2,16,1,48,384]{4,3,1,2,0:T(8,128)(2,1)}) fusion(bf16[2,16,2,1,48,384]{5,4,2,1,0,3:T(8,128)(2,1)} %bitcast.103, s32[]{:T(128)S(6)} %select_n.198, s32[]{:T(128)S(6)} %select_n.197), kind=kLoop, calls=%fused_computation.10 | loop fusion | bytes 4718600 | tf_op jit(solution)/shard_map/jit(dynamic_index_in_dim)/squeeze | solution.py:346
  44.7 8.6 %collective-permute-start.6 = (bf16[3,22,384]{2,1,0:T(8,128)(2,1)S(1)}, bf16[3,22,384]{2,1,0:T(8,128)(2,1)S(1)}, u32[]{:S(2)}, u32[]{:S(2)}) collective-permute-start(bf16[3,22,384]{2,1,0:T(8,128)(2,1)S(1)} %get-tuple-element.174), channel_id=1, source_target_pairs={{0,4},{4,0},{8,12},{12,8},{16,20},{20,16},{24,28},{28,24},{1,5},{5... | collective-permute-start | bytes 152072 | tf_op jit(solution)/shard_map/ppermute | solution.py:325
  53.4 2.2 %collective-permute-done.6 = bf16[3,22,384]{2,1,0:T(8,128)(2,1)S(1)} collective-permute-done((bf16[3,22,384]{2,1,0:T(8,128)(2,1)S(1)}, bf16[3,22,384]{2,1,0:T(8,128)(2,1)S(1)}, u32[]{:S(2)}, u32[]{:S(2)}) %collective-permute-start.6) | collective-permute-done | bytes 50720 | tf_op jit(solution)/shard_map/ppermute | solution.py:325
  55.6 1.9 %add_convert_fusion.1 = bf16[2,16,1,48,384]{4,3,1,2,0:T(8,128)(2,1)S(1)} fusion(bf16[2,16,1,48,384]{4,3,1,2,0:T(8,128)(2,1)} %collective-permute-done.8, bf16[2,16,1,48,384]{4,3,1,2,0:T(8,128)(2,1)} %get-tuple-element.94), kind=kLoop, calls=%fused_computation.1 | loop fusion | flops 2359296 | bytes 3538944 | tf_op jit(solution)/shard_map/convert_element_type | solution.py:352
  58.4 1.9 %collective-permute-start.10 = (bf16[1,4,2,48,384]{4,3,2,1,0:T(8,128)(2,1)S(1)}, bf16[1,4,2,48,384]{4,3,2,1,0:T(8,128)(2,1)S(1)}, u32[]{:S(2)}, u32[]{:S(2)}) collective-permute-start(bf16[1,4,2,48,384]{4,3,2,1,0:T(8,128)(2,1)S(1)} %get-tuple-element.153), channel_id=1, source_target_pairs={{0,4},{1,5},{2,6},{3,7},{4,0},{5,1},{6,2},{7,3},{8,12},{9,13},{10,... | collective-permute-start | bytes 884744 | tf_op jit(solution)/shard_map/ppermute | solution.py:342
  61.6 6.7 %low.1 = (bf16[256,384]{1,0:T(8,128)(2,1)S(1)}, bf16[256,384]{1,0:T(8,128)(2,1)S(1)}, bf16[2,1536,384]{2,1,0:T(8,128)(2,1)S(1)}, f32[1,1536]{1,0:T(1,128)S(1)}, ...) custom-call(bf16[22,32,384]{2,1,0:T(8,128)(2,1)S(1)} %fusion.16.dzpad, bf16[256,384]{1,0:T(8,128)(2,1)S(1)} %bitcast.97, ...), custom_call_target="tpu_custom_call" | custom-call | tf_op jit(solution)/shard_map/low/pallas_call | solution.py:303
  68.3 1.9 %low_taps.1 = bf16[64,384]{1,0:T(8,128)(2,1)S(1)} custom-call(bf16[28,32,384]{2,1,0:T(8,128)(2,1)S(1)} %fusion.12.xpad.source, bf16[256,384]{1,0:T(8,128)(2,1)S(1)} %get-tuple-element.102.dz, f32[1,1536]{1,0:T(1,128)S(1)} %get-tuple-element.96.db, f32[1,384]{1,0:T(1,128)S(1)} %get-tuple-element.97.dgain, f32[1,384]{1,0:T(1,128)S(1)} %get-tuple-element.98.dshift), custom_call_target="tpu_custom_call" | custom-call | tf_op jit(solution)/shard_map/low_taps/pallas_call | solution.py:303
  71.1 1.3 constant_dynamic-slice_fusion.9
  72.5 1.5 %pad_maximum_fusion = bf16[1712,384]{1,0:T(8,128)(2,1)S(1)} fusion(bf16[48,384]{1,0:T(8,128)(2,1)S(1)} %reshape.160, bf16[64,384]{1,0:T(8,128)(2,1)S(1)} %get-tuple-element.101, bf16[64,384]{1,0:T(8,128)(2,1)S(1)} %low_taps.1, bf16[1536,384]{1,0:T(8,128)(2,1)} %bitcast.102), kind=kLoop, calls=%fused_computation.8 | loop fusion | flops 5259264 | bytes 2629632 | tf_op jit(solution)/shard_map/concatenate | solution.py:364
  75.6 1.6 %collective-permute-done.11 = bf16[1712,384]{1,0:T(8,128)(2,1)} collective-permute-done((bf16[1712,384]{1,0:T(8,128)(2,1)S(1)}, bf16[1712,384]{1,0:T(8,128)(2,1)}, u32[]{:S(2)}, u32[]{:S(2)}) %collective-permute-start.11) | collective-permute-done | bytes 1314848 | tf_op jit(solution)/shard_map/ppermute | solution.py:342
  78.0 1.5 %slice.157 = bf16[128,384]{1,0:T(8,128)(2,1)} slice(bf16[1712,384]{1,0:T(8,128)(2,1)} %collective-permute-done.11), slice={[1536:1664], [0:384]} | slice | bytes 196608 | tf_op jit(solution)/shard_map/slice | solution.py:367
  79.5 2.4 %slice.156 = bf16[1536,384]{1,0:T(8,128)(2,1)} slice(bf16[1712,384]{1,0:T(8,128)(2,1)} %collective-permute-done.11), slice={[0:1536], [0:384]} | slice | bytes 2359296 | tf_op jit(solution)/shard_map/slice | solution.py:367
  82.0 1.6 %add_convert_fusion = bf16[2,16,1,48,384]{4,3,1,2,0:T(8,128)(2,1)S(1)} fusion(bf16[2,16,1,48,384]{4,3,1,2,0:T(8,128)(2,1)S(1)} %get-tuple-element.103, bf16[2,16,1,48,384]{4,3,1,0,2:T(8,128)(2,1)} %bitcast.18), kind=kLoop, calls=%fused_computation | loop fusion | flops 2359296 | bytes 3538944 | tf_op jit(solution)/shard_map/convert_element_type | solution.py:352
  86.9 3.4 %collective-permute-start.13 = (bf16[512,384]{1,0:T(8,128)(2,1)S(1)}, bf16[512,384]{1,0:T(8,128)(2,1)S(1)}, u32[]{:S(2)}, u32[]{:S(2)}) collective-permute-start(bf16[512,384]{1,0:T(8,128)(2,1)S(1)} %pad_maximum_fusion.1), channel_id=1, source_target_pairs={{0,2},{1,3},{2,0},{3,1},{4,6},{5,7},{6,4},{7,5},{8,10},{9,11},{10,... | collective-permute-start | bytes 1179656 | tf_op jit(solution)/shard_map/ppermute | solution.py:342
  92.1 4.2 %collective-permute-done.14 = bf16[450,384]{1,0:T(8,128)(2,1)S(1)} collective-permute-done((bf16[450,384]{1,0:T(8,128)(2,1)}, bf16[450,384]{1,0:T(8,128)(2,1)S(1)}, u32[]{:S(2)}, u32[]{:S(2)}) %collective-permute-start.14) | collective-permute-done | bytes 345632 | tf_op jit(solution)/shard_map/ppermute | solution.py:342
  96.4 3.7 %collective-permute-done.13 = bf16[512,384]{1,0:T(8,128)(2,1)S(1)} collective-permute-done((bf16[512,384]{1,0:T(8,128)(2,1)S(1)}, bf16[512,384]{1,0:T(8,128)(2,1)S(1)}, u32[]{:S(2)}, u32[]{:S(2)}) %collective-permute-start.13) | collective-permute-done | bytes 393248 | tf_op jit(solution)/shard_map/ppermute | solution.py:342
  100.2 3.1 %collective-permute-done.16 = bf16[1,4,1,48,384]{4,3,2,1,0:T(8,128)(2,1)S(1)} collective-permute-done((bf16[1,4,1,48,384]{4,3,2,1,0:T(8,128)(2,1)S(1)}, bf16[1,4,1,48,384]{4,3,2,1,0:T(8,128)(2,1)S(1)}, u32[]{:S(2)}, u32[]{:S(2)}) %collective-permute-start.16) | collective-permute-done | bytes 147488 | tf_op jit(solution)/shard_map/ppermute | solution.py:342
  105.1 1.6 %collective-permute-start.20 = (bf16[2,2,1,48,384]{4,3,1,0,2:T(8,128)(2,1)S(1)}, bf16[2,2,1,48,384]{4,3,1,0,2:T(8,128)(2,1)S(1)}, u32[]{:S(2)}, u32[]{:S(2)}) collective-permute-start(bf16[2,2,1,48,384]{4,3,1,0,2:T(8,128)(2,1)S(1)} %get-tuple-element.161), channel_id=1, source_target_pairs={{0,8},{1,9},{2,10},{3,11},{4,12},{5,13},{6,14},{7,15},{8,0},{9,1},... | collective-permute-start | bytes 442376 | tf_op jit(solution)/shard_map/ppermute | solution.py:342
  107.2 1.3 collective-permute-start.19
  108.6 2.4 %last.1 = bf16[256,384]{1,0:T(8,128)(2,1)} custom-call(bf16[22,32,384]{2,1,0:T(8,128)(2,1)S(1)} %fusion.18.dzpad, bf16[256,384]{1,0:T(8,128)(2,1)S(1)} %get-tuple-element.127.gmid, f32[2,3,49,128]{3,2,1,0:T(8,128)S(1)} %rev.3.taps_back), custom_call_target="tpu_custom_call" | custom-call | tf_op jit(solution)/shard_map/last/pallas_call | solution.py:303
  111.0 3.5 %collective-permute-done.18 = bf16[320,384]{1,0:T(8,128)(2,1)S(1)} collective-permute-done((bf16[320,384]{1,0:T(8,128)(2,1)S(1)}, bf16[320,384]{1,0:T(8,128)(2,1)S(1)}, u32[]{:S(2)}, u32[]{:S(2)}) %collective-permute-start.18) | collective-permute-done | bytes 245792 | tf_op jit(solution)/shard_map/ppermute | solution.py:342
  114.7 1.4 %collective-permute-start.23 = (bf16[2,1,1,48,384]{4,3,1,0,2:T(8,128)(2,1)S(1)}, bf16[2,1,1,48,384]{4,3,1,0,2:T(8,128)(2,1)S(1)}, u32[]{:S(2)}, u32[]{:S(2)}) collective-permute-start(bf16[2,1,1,48,384]{4,3,1,0,2:T(8,128)(2,1)S(1)} %constant_dynamic-slice_fusion), channel_id=1, source_target_pairs={{0,16},{1,17},{2,18},{3,19},{4,20},{5,21},{6,22},{7,23},{8,24},{9,... | collective-permute-start | bytes 221192 | tf_op jit(solution)/shard_map/ppermute | solution.py:342
  116.3 1.8 %collective-permute-start.21 = (bf16[320,384]{1,0:T(8,128)(2,1)S(1)}, bf16[320,384]{1,0:T(8,128)(2,1)S(1)}, u32[]{:S(2)}, u32[]{:S(2)}) collective-permute-start(bf16[320,384]{1,0:T(8,128)(2,1)S(1)} %pad_maximum_fusion.6), channel_id=1, source_target_pairs={{0,8},{1,9},{2,10},{3,11},{4,12},{5,13},{6,14},{7,15},{8,0},{9,1},... | collective-permute-start | bytes 737288 | tf_op jit(solution)/shard_map/ppermute | solution.py:342
  118.1 2.6 %collective-permute-done.23 = bf16[2,1,1,48,384]{4,3,1,0,2:T(8,128)(2,1)S(1)} collective-permute-done((bf16[2,1,1,48,384]{4,3,1,0,2:T(8,128)(2,1)S(1)}, bf16[2,1,1,48,384]{4,3,1,0,2:T(8,128)(2,1)S(1)}, u32[]{:S(2)}, u32[]{:S(2)}) %collective-permute-start.23) | collective-permute-done | bytes 73760 | tf_op jit(solution)/shard_map/ppermute | solution.py:342
  120.8 4.0 %collective-permute-done.21 = bf16[320,384]{1,0:T(8,128)(2,1)S(1)} collective-permute-done((bf16[320,384]{1,0:T(8,128)(2,1)S(1)}, bf16[320,384]{1,0:T(8,128)(2,1)S(1)}, u32[]{:S(2)}, u32[]{:S(2)}) %collective-permute-start.21) | collective-permute-done | bytes 245792 | tf_op jit(solution)/shard_map/ppermute | solution.py:342
  125.6 9.0 %collective-permute-done.22 = bf16[224,384]{1,0:T(8,128)(2,1)S(1)} collective-permute-done((bf16[224,384]{1,0:T(8,128)(2,1)S(1)}, bf16[224,384]{1,0:T(8,128)(2,1)S(1)}, u32[]{:S(2)}, u32[]{:S(2)}) %collective-permute-start.22) | collective-permute-done | bytes 172064 | tf_op jit(solution)/shard_map/ppermute | solution.py:342
  (142 shorter events, 27.5 us)
Async XLA Ops:
  0.6 7.2 %copy-start.14 = (f32[2,1536]{1,0:T(2,128)S(1)}, f32[2,1536]{1,0:T(2,128)}, u32[]{:S(2)}) copy-start(f32[2,1536]{1,0:T(2,128)} %param.14) | copy-start | bytes 36868
  0.6 7.3 %copy-start.12 = (f32[2,7,7,384]{3,0,2,1:T(2,128)S(1)}, f32[2,7,7,384]{3,0,2,1:T(2,128)}, u32[]{:S(2)}) copy-start(f32[2,7,7,384]{3,0,2,1:T(2,128)} %param.10) | copy-start | bytes 451588
  1.7 8.7 %copy-start.5 = (bf16[16,16,384]{2,1,0:T(8,128)(2,1)S(1)}, bf16[16,16,384]{2,1,0:T(8,128)(2,1)}, u32[]{:S(2)}) copy-start(bf16[16,16,384]{2,1,0:T(8,128)(2,1)} %param.8) | copy-start | bytes 589828
  1.7 1.5 %collective-permute-start = (bf16[16,6,384]{2,1,0:T(8,128)(2,1)S(1)}, bf16[16,6,384]{2,1,0:T(8,128)(2,1)S(1)}, u32[]{:S(2)}, u32[]{:S(2)}) collective-permute-start(bf16[16,6,384]{2,1,0:T(8,128)(2,1)S(1)} %get-tuple-element.185), channel_id=1, source_target_pairs={{0,1},{1,0},{2,3},{3,2},{4,5},{5,4},{6,7},{7,6},{8,9},{9,8},{10,11... | collective-permute-start | bytes 221192 | tf_op jit(solution)/shard_map/ppermute | solution.py:325
  2.2 0.9 collective-permute-start.1
  4.3 6.1 %collective-permute-start.2 = (bf16[6,28,384]{2,1,0:T(8,128)(2,1)S(1)}, bf16[6,28,384]{2,1,0:T(8,128)(2,1)S(1)}, u32[]{:S(2)}, u32[]{:S(2)}) collective-permute-start(bf16[6,28,384]{2,1,0:T(8,128)(2,1)S(1)} %get-tuple-element.157), channel_id=1, source_target_pairs={{0,4},{4,0},{8,12},{12,8},{16,20},{20,16},{24,28},{28,24},{1,5},{5... | collective-permute-start | bytes 387080 | tf_op jit(solution)/shard_map/ppermute | solution.py:325
  7.2 3.1 %collective-permute-start.3 = (bf16[6,28,384]{2,1,0:T(8,128)(2,1)S(1)}, bf16[6,28,384]{2,1,0:T(8,128)(2,1)S(1)}, u32[]{:S(2)}, u32[]{:S(2)}) collective-permute-start(bf16[6,28,384]{2,1,0:T(8,128)(2,1)S(1)} %get-tuple-element.158), channel_id=1, source_target_pairs={{4,8},{12,16},{20,24},{8,4},{16,12},{24,20},{5,9},{13,17},{21,25},... | collective-permute-start | bytes 387080 | tf_op jit(solution)/shard_map/ppermute | solution.py:330
  7.9 2.7 %copy-start.3 = (f32[2,384]{1,0:T(2,128)S(1)}, f32[2,384]{1,0:T(2,128)}, u32[]{:S(2)}) copy-start(f32[2,384]{1,0:T(2,128)} %gains.5) | copy-start | bytes 9220
  10.6 8.7 %copy-start = (bf16[16,16,384]{2,1,0:T(8,128)(2,1)S(1)}, bf16[16,16,384]{2,1,0:T(8,128)(2,1)}, u32[]{:S(2)}) copy-start(bf16[16,16,384]{2,1,0:T(8,128)(2,1)} %param.9) | copy-start | bytes 589828
  25.5 14.0 %collective-permute-start.5 = (bf16[16,3,384]{2,1,0:T(4,128)(2,1)}, bf16[16,3,384]{2,1,0:T(4,128)(2,1)}, u32[]{:S(2)}, u32[]{:S(2)}) collective-permute-start(bf16[16,3,384]{2,1,0:T(4,128)(2,1)} %get-tuple-element.181), channel_id=1, source_target_pairs={{1,2},{2,1},{5,6},{6,5},{9,10},{10,9},{13,14},{14,13},{17,18},{18,... | collective-permute-start | bytes 110600 | tf_op jit(solution)/shard_map/ppermute | solution.py:330
  26.7 12.8 %collective-permute-start.4 = (bf16[16,3,384]{2,1,0:T(4,128)(2,1)}, bf16[16,3,384]{2,1,0:T(4,128)(2,1)}, u32[]{:S(2)}, u32[]{:S(2)}) collective-permute-start(bf16[16,3,384]{2,1,0:T(4,128)(2,1)} %get-tuple-element.182), channel_id=1, source_target_pairs={{0,1},{1,0},{2,3},{3,2},{4,5},{5,4},{6,7},{7,6},{8,9},{9,8},{10,11... | collective-permute-start | bytes 110600 | tf_op jit(solution)/shard_map/ppermute | solution.py:325
  42.8 12.8 %collective-permute-start.8 = (bf16[2,16,1,48,384]{4,3,1,2,0:T(8,128)(2,1)}, bf16[2,16,1,48,384]{4,3,1,2,0:T(8,128)(2,1)}, u32[]{:S(2)}, u32[]{:S(2)}) collective-permute-start(bf16[2,16,1,48,384]{4,3,1,2,0:T(8,128)(2,1)} %get-tuple-element.143), channel_id=1, source_target_pairs={{0,1},{1,0},{2,3},{3,2},{4,5},{5,4},{6,7},{7,6},{8,9},{9,8},{10,11... | collective-permute-start | bytes 3538952 | tf_op jit(solution)/shard_map/ppermute | solution.py:342
  43.8 9.6 %collective-permute-start.7 = (bf16[3,22,384]{2,1,0:T(8,128)(2,1)S(1)}, bf16[3,22,384]{2,1,0:T(8,128)(2,1)S(1)}, u32[]{:S(2)}, u32[]{:S(2)}) collective-permute-start(bf16[3,22,384]{2,1,0:T(8,128)(2,1)S(1)} %get-tuple-element.173), channel_id=1, source_target_pairs={{4,8},{12,16},{20,24},{8,4},{16,12},{24,20},{5,9},{13,17},{21,25},... | collective-permute-start | bytes 152072 | tf_op jit(solution)/shard_map/ppermute | solution.py:330
  44.7 10.9 %collective-permute-start.6 = (bf16[3,22,384]{2,1,0:T(8,128)(2,1)S(1)}, bf16[3,22,384]{2,1,0:T(8,128)(2,1)S(1)}, u32[]{:S(2)}, u32[]{:S(2)}) collective-permute-start(bf16[3,22,384]{2,1,0:T(8,128)(2,1)S(1)} %get-tuple-element.174), channel_id=1, source_target_pairs={{0,4},{4,0},{8,12},{12,8},{16,20},{20,16},{24,28},{28,24},{1,5},{5... | collective-permute-start | bytes 152072 | tf_op jit(solution)/shard_map/ppermute | solution.py:325
  58.4 11.9 %collective-permute-start.10 = (bf16[1,4,2,48,384]{4,3,2,1,0:T(8,128)(2,1)S(1)}, bf16[1,4,2,48,384]{4,3,2,1,0:T(8,128)(2,1)S(1)}, u32[]{:S(2)}, u32[]{:S(2)}) collective-permute-start(bf16[1,4,2,48,384]{4,3,2,1,0:T(8,128)(2,1)S(1)} %get-tuple-element.153), channel_id=1, source_target_pairs={{0,4},{1,5},{2,6},{3,7},{4,0},{5,1},{6,2},{7,3},{8,12},{9,13},{10,... | collective-permute-start | bytes 884744 | tf_op jit(solution)/shard_map/ppermute | solution.py:342
  61.1 9.2 %collective-permute-start.9 = (bf16[1,8,1,48,384]{4,3,1,2,0:T(8,128)(2,1)S(1)}, bf16[1,8,1,48,384]{4,3,1,2,0:T(8,128)(2,1)S(1)}, u32[]{:S(2)}, u32[]{:S(2)}) collective-permute-start(bf16[1,8,1,48,384]{4,3,1,2,0:T(8,128)(2,1)S(1)} %get-tuple-element.155), channel_id=1, source_target_pairs={{0,2},{1,3},{2,0},{3,1},{4,6},{5,7},{6,4},{7,5},{8,10},{9,11},{10,... | collective-permute-start | bytes 884744 | tf_op jit(solution)/shard_map/ppermute | solution.py:342
  74.0 3.2 %collective-permute-start.11 = (bf16[1712,384]{1,0:T(8,128)(2,1)S(1)}, bf16[1712,384]{1,0:T(8,128)(2,1)}, u32[]{:S(2)}, u32[]{:S(2)}) collective-permute-start(bf16[1712,384]{1,0:T(8,128)(2,1)S(1)} %pad_maximum_fusion), channel_id=1, source_target_pairs={{0,1},{1,0},{2,3},{3,2},{4,5},{5,4},{6,7},{7,6},{8,9},{9,8},{10,11... | collective-permute-start | bytes 3944456 | tf_op jit(solution)/shard_map/ppermute | solution.py:342
  74.0 7.9 %collective-permute-start.12 = (bf16[16,3,384]{2,1,0:T(4,128)(2,1)S(1)}, bf16[16,3,384]{2,1,0:T(4,128)(2,1)S(1)}, u32[]{:S(2)}, u32[]{:S(2)}) collective-permute-start(bf16[16,3,384]{2,1,0:T(4,128)(2,1)S(1)} %get-tuple-element.179), channel_id=1, source_target_pairs={{1,2},{2,1},{5,6},{6,5},{9,10},{10,9},{13,14},{14,13},{17,18},{18,... | collective-permute-start | bytes 110600 | tf_op jit(solution)/shard_map/ppermute | solution.py:330
  75.5 24.7 %collective-permute-start.15 = (bf16[1,4,1,48,384]{4,3,1,2,0:T(8,128)(2,1)}, bf16[1,4,1,48,384]{4,3,1,2,0:T(8,128)(2,1)S(1)}, u32[]{:S(2)}, u32[]{:S(2)}) collective-permute-start(bf16[1,4,1,48,384]{4,3,1,2,0:T(8,128)(2,1)} %get-tuple-element.171), channel_id=1, source_target_pairs={{0,4},{1,5},{2,6},{3,7},{4,0},{5,1},{6,2},{7,3},{8,12},{9,13},{10,... | collective-permute-start | bytes 442376 | tf_op jit(solution)/shard_map/ppermute | solution.py:342
  83.9 6.4 %copy-start.7 = (bf16[1,4,2,48,384]{4,3,2,1,0:T(8,128)(2,1)S(1)}, bf16[1,4,2,48,384]{4,3,2,1,0:T(8,128)(2,1)}, u32[]{:S(2)}) copy-start(bf16[1,4,2,48,384]{4,3,2,1,0:T(8,128)(2,1)} %get-tuple-element.112) | copy-start | bytes 884740
  85.5 10.9 %collective-permute-start.14 = (bf16[450,384]{1,0:T(8,128)(2,1)}, bf16[450,384]{1,0:T(8,128)(2,1)S(1)}, u32[]{:S(2)}, u32[]{:S(2)}) collective-permute-start(bf16[450,384]{1,0:T(8,128)(2,1)} %pad_maximum_fusion.2), channel_id=1, source_target_pairs={{0,4},{1,5},{2,6},{3,7},{4,0},{5,1},{6,2},{7,3},{8,12},{9,13},{10,... | collective-permute-start | bytes 1036808 | tf_op jit(solution)/shard_map/ppermute | solution.py:342
  86.9 13.3 %collective-permute-start.13 = (bf16[512,384]{1,0:T(8,128)(2,1)S(1)}, bf16[512,384]{1,0:T(8,128)(2,1)S(1)}, u32[]{:S(2)}, u32[]{:S(2)}) collective-permute-start(bf16[512,384]{1,0:T(8,128)(2,1)S(1)} %pad_maximum_fusion.1), channel_id=1, source_target_pairs={{0,2},{1,3},{2,0},{3,1},{4,6},{5,7},{6,4},{7,5},{8,10},{9,11},{10,... | collective-permute-start | bytes 1179656 | tf_op jit(solution)/shard_map/ppermute | solution.py:342
  91.4 11.9 %collective-permute-start.16 = (bf16[1,4,1,48,384]{4,3,2,1,0:T(8,128)(2,1)S(1)}, bf16[1,4,1,48,384]{4,3,2,1,0:T(8,128)(2,1)S(1)}, u32[]{:S(2)}, u32[]{:S(2)}) collective-permute-start(bf16[1,4,1,48,384]{4,3,2,1,0:T(8,128)(2,1)S(1)} %get-tuple-element.169), channel_id=1, source_target_pairs={{0,2},{1,3},{2,0},{3,1},{4,6},{5,7},{6,4},{7,5},{8,10},{9,11},{10,... | collective-permute-start | bytes 442376 | tf_op jit(solution)/shard_map/ppermute | solution.py:342
  91.5 11.8 %collective-permute-start.17 = (bf16[3,22,384]{2,1,0:T(8,128)(2,1)}, bf16[3,22,384]{2,1,0:T(8,128)(2,1)S(1)}, u32[]{:S(2)}, u32[]{:S(2)}) collective-permute-start(bf16[3,22,384]{2,1,0:T(8,128)(2,1)} %get-tuple-element.167), channel_id=1, source_target_pairs={{4,8},{12,16},{20,24},{8,4},{16,12},{24,20},{5,9},{13,17},{21,25},... | collective-permute-start | bytes 152072 | tf_op jit(solution)/shard_map/ppermute | solution.py:330
  96.4 7.6 %copy-start.6 = (bf16[450,384]{1,0:T(8,128)(2,1)}, bf16[450,384]{1,0:T(8,128)(2,1)S(1)}, u32[]{:S(2)}) copy-start(bf16[450,384]{1,0:T(8,128)(2,1)S(1)} %collective-permute-done.14) | copy-start | bytes 1036804
  104.1 3.1 %slice-start = ((bf16[450,384]{1,0:T(8,128)(2,1)}), bf16[384,384]{1,0:T(8,128)(2,1)S(1)}, s32[]{:S(2)}) async-start(bf16[450,384]{1,0:T(8,128)(2,1)} %copy-done.6), calls=%async_computation | async-start | bytes 589824 | tf_op jit(solution)/shard_map/slice | solution.py:367
  105.1 9.5 %collective-permute-start.20 = (bf16[2,2,1,48,384]{4,3,1,0,2:T(8,128)(2,1)S(1)}, bf16[2,2,1,48,384]{4,3,1,0,2:T(8,128)(2,1)S(1)}, u32[]{:S(2)}, u32[]{:S(2)}) collective-permute-start(bf16[2,2,1,48,384]{4,3,1,0,2:T(8,128)(2,1)S(1)} %get-tuple-element.161), channel_id=1, source_target_pairs={{0,8},{1,9},{2,10},{3,11},{4,12},{5,13},{6,14},{7,15},{8,0},{9,1},... | collective-permute-start | bytes 442376 | tf_op jit(solution)/shard_map/ppermute | solution.py:342
  106.8 7.8 %collective-permute-start.18 = (bf16[320,384]{1,0:T(8,128)(2,1)S(1)}, bf16[320,384]{1,0:T(8,128)(2,1)S(1)}, u32[]{:S(2)}, u32[]{:S(2)}) collective-permute-start(bf16[320,384]{1,0:T(8,128)(2,1)S(1)} %pad_maximum_fusion.5), channel_id=1, source_target_pairs={{0,4},{1,5},{2,6},{3,7},{4,0},{5,1},{6,2},{7,3},{8,12},{9,13},{10,... | collective-permute-start | bytes 737288 | tf_op jit(solution)/shard_map/ppermute | solution.py:342
  107.2 7.4 %collective-permute-start.19 = (bf16[1,4,1,48,384]{4,3,2,1,0:T(8,128)(2,1)S(1)}, bf16[1,4,1,48,384]{4,3,2,1,0:T(8,128)(2,1)S(1)}, u32[]{:S(2)}, u32[]{:S(2)}) collective-permute-start(bf16[1,4,1,48,384]{4,3,2,1,0:T(8,128)(2,1)S(1)} %get-tuple-element.163), channel_id=1, source_target_pairs={{0,2},{1,3},{2,0},{3,1},{4,6},{5,7},{6,4},{7,5},{8,10},{9,11},{10,... | collective-permute-start | bytes 442376 | tf_op jit(solution)/shard_map/ppermute | solution.py:342
  114.7 6.0 %collective-permute-start.23 = (bf16[2,1,1,48,384]{4,3,1,0,2:T(8,128)(2,1)S(1)}, bf16[2,1,1,48,384]{4,3,1,0,2:T(8,128)(2,1)S(1)}, u32[]{:S(2)}, u32[]{:S(2)}) collective-permute-start(bf16[2,1,1,48,384]{4,3,1,0,2:T(8,128)(2,1)S(1)} %constant_dynamic-slice_fusion), channel_id=1, source_target_pairs={{0,16},{1,17},{2,18},{3,19},{4,20},{5,21},{6,22},{7,23},{8,24},{9,... | collective-permute-start | bytes 221192 | tf_op jit(solution)/shard_map/ppermute | solution.py:342
  116.3 8.4 %collective-permute-start.21 = (bf16[320,384]{1,0:T(8,128)(2,1)S(1)}, bf16[320,384]{1,0:T(8,128)(2,1)S(1)}, u32[]{:S(2)}, u32[]{:S(2)}) collective-permute-start(bf16[320,384]{1,0:T(8,128)(2,1)S(1)} %pad_maximum_fusion.6), channel_id=1, source_target_pairs={{0,8},{1,9},{2,10},{3,11},{4,12},{5,13},{6,14},{7,15},{8,0},{9,1},... | collective-permute-start | bytes 737288 | tf_op jit(solution)/shard_map/ppermute | solution.py:342
  124.9 9.6 %collective-permute-start.22 = (bf16[224,384]{1,0:T(8,128)(2,1)S(1)}, bf16[224,384]{1,0:T(8,128)(2,1)S(1)}, u32[]{:S(2)}, u32[]{:S(2)}) collective-permute-start(bf16[224,384]{1,0:T(8,128)(2,1)S(1)} %pad_maximum_fusion.7), channel_id=1, source_target_pairs={{0,16},{1,17},{2,18},{3,19},{4,20},{5,21},{6,22},{7,23},{8,24},{9,... | collective-permute-start | bytes 516104 | tf_op jit(solution)/shard_map/ppermute | solution.py:342
  (8 other events, 12.7 us)

commit v5 on v4

--- a/solution.py
+++ b/solution.py
@@ -308,7 +308,7 @@
         ],
         out_specs=tuple(vmem for _ in outs),
         scratch_shapes=[pltpu.VMEM(s.shape, s.dtype) for s in scratch] + semaphores,
-        compiler_params=pltpu.CompilerParams(vmem_limit_bytes=50 * 1024 * 1024),
+        compiler_params=pltpu.CompilerParams(vmem_limit_bytes=24 * 1024 * 1024),
         name=name,
     )(*args)
 
@@ -352,21 +352,12 @@
     return (own.astype(F32) + got.astype(F32)).astype(BF16)
 
 
-def step(chunks, order, bit, mine, *riders):
+def step(chunks, order, bit, mine):
     spot = order.index(bit)
     per = chunks.shape[-2:]
     pair = chunks.reshape((-1, 2 ** spot, 2, 2 ** (len(order) - spot - 1)) + per)
     send, keep = halves(pair, 2, mine[bit])
-    left = [b for b in order if b != bit]
-    if not riders:
-        return keep, flip_bit(send, bit), left, ()
-    parts = [part.reshape(-1, per[-1]) for part in (send,) + riders]
-    got = flip_bit(jnp.concatenate(parts, axis=0), bit)
-    came, first = [], 0
-    for part, like in zip(parts, (send,) + riders):
-        came.append(got[first : first + part.shape[0]].reshape(like.shape))
-        first += part.shape[0]
-    return keep, came[0], left, tuple(came[1:])
+    return keep, flip_bit(send, bit), [b for b in order if b != bit]
 
 
 def shards(activations, grad_out, kernels, norm_gains, norm_shifts, w_in, b_in, w_out):
@@ -457,32 +448,26 @@
     def settled(flight):
         return summed(flight[0], flight[1]), flight[2]
 
-    def start(dw, small, *riders):
+    def start(dw):
         chunks, order = dw.reshape(2, total, per, channels), list(range(bits - 1, -1, -1))
-        came = ()
-        for bit in range(col_bits - 1):
-            if bit:
-                chunks, order = settled(flight)
-                small = [summed(s, g) for s, g in zip(small, small_got)]
-            flight = step(chunks, order, bit, mine, *small, *(() if bit else riders))
-            small_got = flight[3][: len(small)]
-            came = came or flight[3][len(small) :]
-        return flight[:3], small, small_got, came
-
-    def fork(flight, first=(), second=()):
+        for bit in range(col_bits - 2):
+            chunks, order = settled(step(chunks, order, bit, mine))
+        return step(chunks, order, col_bits - 2, mine)
+
+    def fork(flight):
         chunks, order = settled(flight)
-        return [step(chunks[i], order, sides[i], mine, *r) for i, r in enumerate((first, second))]
-
-    def cross(flights, first=()):
+        return [step(chunks[i], order, sides[i], mine) for i in range(2)]
+
+    def cross(flights):
         done = [settled(f) for f in flights]
-        return [step(*done[i], sides[1 - i], mine, *r) for i, r in enumerate((first, ()))]
+        return [step(*done[i], sides[1 - i], mine) for i in range(2)]
 
     def merge(flights):
         done = [settled(f) for f in flights]
         return jnp.stack([d[0].reshape(-1, per, channels) for d in done]), done[0][1]
 
-    def onward(chunks, order, *riders):
-        return step(chunks, order, order[-1], mine, *riders)
+    def onward(chunks, order):
+        return step(chunks, order, order[-1], mine) if order else (chunks, jnp.zeros_like(chunks), order)
 
     def finish(flight):
         chunks, order = settled(flight)
@@ -502,7 +487,7 @@
     )
     tile1, twin, other, dw1, small1 = fenced(tile1, twin, other, dw1, small1)
     wide1 = rimmed(tile1, twin, other, 1, odd_col)
-    run1, _, _, _ = start(dw1, [])
+    run1 = start(dw1)
     twin, other = edges(wide1, 0, HALO, odd_row)
     twin, other = to_twin(twin, "rows"), to_other(other, "rows")
     wide1, twin, other, run1 = fenced(wide1, twin, other, run1)
@@ -518,6 +503,12 @@
         fetched=2,
         name="low",
     )
+    dz0, dw0, pair1, *small0 = fenced(dz0, dw0, pair1, *small0)
+    run0 = start(dw0)
+    pair1 = cross(pair1)
+    tile0 = dz0.reshape(rows, cols, channels)
+    twin, other = edges(tile0, 1, HALO, odd_col)
+    twin = to_twin(twin, "cols")
     (small0,) = run(
         low_taps_kernel,
         (shape(small_rows, channels, dtype=BF16),),
@@ -525,40 +516,49 @@
         (xpad, dz0, *small0),
         name="low_taps",
     )
-    dz0, dw0, pair1, small0 = fenced(dz0, dw0, pair1, small0)
-    tile0 = dz0.reshape(rows, cols, channels)
     small = jnp.concatenate([small0, small1], axis=0)
-    twin, other = edges(tile0, 1, HALO, odd_col)
-    run0, (small,), small_got, (twin,) = start(dw0, [small], twin)
+    small_got = flip_bit(small, 0)
+    run0, pair1, small, small_got, tile0, twin, other = fenced(
+        run0, pair1, small, small_got, tile0, twin, other
+    )
+    pair0 = fork(run0)
+    run1 = onward(*merge(pair1))
     other = to_other(other, "cols")
-    pair1 = cross(pair1)
-    run0, small, small_got, tile0, twin, other = fenced(run0, small, small_got, tile0, twin, other)
-    small = summed(small, small_got[0])
+    small = summed(small, small_got)
+    small_got = flip_bit(small, 1)
+    pair0, run1, tile0, twin, other, small, small_got = fenced(
+        pair0, run1, tile0, twin, other, small, small_got
+    )
+    pair0 = cross(pair0)
+    run1 = onward(*settled(run1))
     wide0 = rimmed(tile0, twin, other, 1, odd_col)
     twin, other = edges(wide0, 0, HALO, odd_row)
-    pair0 = fork(run0, (small,), (twin,))
+    twin = to_twin(twin, "rows")
+    small = summed(small, small_got)
+    small_got = flip_bit(small, 2)
+    pair0, run1, wide0, twin, other, small, small_got = fenced(
+        pair0, run1, wide0, twin, other, small, small_got
+    )
+    run0 = onward(*merge(pair0))
     other = to_other(other, "rows")
-    pair0, pair1, small, wide0, other = fenced(pair0, pair1, small, wide0, other)
-    small = summed(small, pair0[0][3][0])
-    twin = pair0[1][3][0]
-    pair0 = cross(pair0, (small,))
-    run1 = onward(*merge(pair1))
-    (grad_in,) = run(
-        last_kernel,
-        (tile_b,),
-        spread_scratch,
-        (filled(rimmed(wide0, twin, other, 0, odd_row)), grad_mid, taps_back),
-        name="last",
-    )
-    pair0, run1, small, grad_in = fenced(pair0, run1, small, grad_in)
-    small = summed(small, pair0[0][3][0])
-    run0 = onward(*merge(pair0), small)
     share1 = finish(run1)
-    while run0[2]:
-        run0, small = fenced(run0, small)
-        small = summed(small, run0[3][0])
-        run0 = onward(*settled(run0), small)
-    small = summed(small, run0[3][0])
+    wait = (wide0, twin, other)
+    for bit in range(3, bits):
+        small = summed(small, small_got)
+        small_got = flip_bit(small, bit)
+        if run0[2]:
+            run0, small, small_got, wait = fenced(run0, small, small_got, wait)
+            run0 = onward(*settled(run0))
+        if bit == 3:
+            (wait,) = run(
+                last_kernel,
+                (tile_b,),
+                spread_scratch,
+                (filled(rimmed(*wait, 0, odd_row)), grad_mid, taps_back),
+                name="last",
+            )
+    grad_in = wait
+    small = summed(small, small_got)
     shares = [finish(run0), share1]
     small = small.reshape(layers, small_rows, channels).astype(F32) * grad_scale
     count = hidden // channels

time: 138 us -> 139 us (level)
  waiting for transfers between devices: 36.3 us -> 25.1 us
  starting transfers between devices: 37.8 us -> 47.2 us
    ppermute x14 -> x19, starting transfers between devices: 13.5 us -> 28.2 us  [flip_bit(): return lax.ppermute(value, both, [(i, i ^ 1 << bit) for i in range(total)])]
    ppermute x14 -> x19, waiting for transfers between devices: 31.8 us -> 18.2 us  [flip_bit(): return lax.ppermute(value, both, [(i, i ^ 1 << bit) for i in range(total)])]
    unnamed x32 -> x68, local copies, waits for them, and re-layouts: 4.05 us -> 11.6 us
    ppermute x4 -> x6, starting transfers between devices: 19.6 us -> 13.2 us  [to_twin(): lax.ppermute(edge, axis, [(i, i ^ 1) for i in range(count) if i ^ 1 < cou...]
    slice x15 -> x2, local copies, waits for them, and re-layouts: 5.09 us -> 0.24 us  [fork(): return [step(chunks[i], order, sides[i], mine) for i in range(2)]]
    ppermute x4 -> x6, waiting for transfers between devices: 4.55 us -> 6.93 us  [to_twin(): lax.ppermute(edge, axis, [(i, i ^ 1) for i in range(count) if i ^ 1 < cou...]
    concatenate x6 -> x0, other arithmetic: 2.37 us -> none  [step(): got = flip_bit(jnp.concatenate(parts, axis=0), bit)]
    convert_element_type x16, other arithmetic: 6.98 us -> 5.05 us  [summed(): return (own.astype(F32) + got.astype(F32)).astype(BF16)]
  transfers between devices with their start and end apart: 24 -> 31, of which waited for: 11 -> 12; matrix products, arithmetic and copies ran while one was open for 10% -> 7% of each run, Pallas kernels for 11% -> 11%
where the time goes in v5:
time: 139 us; the launch traced here: 138 us
  starting transfers between devices  47.2 us (34%)
  Pallas kernels  29.4 us (21%)
  waiting for transfers between devices  25.1 us (18%)
  local copies, waits for them, and re-layouts  18.8 us (14%)
  other arithmetic  15.9 us (11%)
  between operations  1.4 us (1%)
    pallas_call x6, Pallas kernels, run(): pl.pallas_call(kernel, out_shape=outs, in_specs=[vmem if s is None else p...  29.4 us
    ppermute x19, starting transfers between devices, flip_bit(): return lax.ppermute(value, both, [(i, i ^ 1 << bit) for i in range(total)])  28.2 us
    ppermute x19, waiting for transfers between devices, flip_bit(): return lax.ppermute(value, both, [(i, i ^ 1 << bit) for i in range(total)])  18.2 us
    ppermute x6, starting transfers between devices, to_twin(): lax.ppermute(edge, axis, [(i, i ^ 1) for i in range(count) if i ^ 1 < cou...  13.2 us
    unnamed x68, local copies, waits for them, and re-layouts  11.6 us
    ppermute x6, waiting for transfers between devices, to_twin(): lax.ppermute(edge, axis, [(i, i ^ 1) for i in range(count) if i ^ 1 < cou...  6.93 us
    ppermute x6, starting transfers between devices, to_other(): return lax.ppermute(edge, axis, pairs + [(j, i) for i, j in pairs])  5.82 us
    convert_element_type x16, other arithmetic, summed(): return (own.astype(F32) + got.astype(F32)).astype(BF16)  5.05 us
  transfers between devices with their start and end apart: 31, of which 12 were waited for; matrix products, arithmetic and copies ran while one was open for 7% of the time, Pallas kernels for 11%

profile of v5, /device:TPU:0, one launch (start us, length us, event | category | flops | bytes accessed | tf_op | source)
XLA Modules:
  0.0 137.9 jit_solution(9323403668034778864)
XLA Ops:
  3.2 1.8 %broadcast_select_fusion.3 = (bf16[6,28,384]{2,1,0:T(8,128)(2,1)}, bf16[6,28,384]{2,1,0:T(8,128)(2,1)S(1)}) fusion(pred[]{:T(512)S(6)} %eq.9, bf16[16,6,384]{2,1,0:T(8,128)(2,1)S(1)} %get-tuple-element.202, bf16[16,16,384]{2,1,0:T(8,128)(2,1)} %param.8, bf16[16,6,384]{2,1,0:T(8,128)(2,1)S(1)} %get-tuple-element.201), kind=kLoop, calls=%fused_computation.87 | loop fusion | flops 903168 | bytes 602113 | tf_op jit(solution)/shard_map/jit(_where)/select_n | solution.py:320
  5.0 2.9 %collective-permute-start.2 = (bf16[6,28,384]{2,1,0:T(8,128)(2,1)}, bf16[6,28,384]{2,1,0:T(8,128)(2,1)S(1)}, u32[]{:S(2)}, u32[]{:S(2)}) collective-permute-start(bf16[6,28,384]{2,1,0:T(8,128)(2,1)} %get-tuple-element.175), channel_id=1, source_target_pairs={{0,4},{4,0},{8,12},{12,8},{16,20},{20,16},{24,28},{28,24},{1,5},{5... | collective-permute-start | bytes 387080 | tf_op jit(solution)/shard_map/ppermute | solution.py:325
  9.5 1.7 %collective-permute-done.2 = bf16[6,28,384]{2,1,0:T(8,128)(2,1)S(1)} collective-permute-done((bf16[6,28,384]{2,1,0:T(8,128)(2,1)}, bf16[6,28,384]{2,1,0:T(8,128)(2,1)S(1)}, u32[]{:S(2)}, u32[]{:S(2)}) %collective-permute-start.2) | collective-permute-done | bytes 129056 | tf_op jit(solution)/shard_map/ppermute | solution.py:325
  13.3 1.7 %copy-done.1 = bf16[2,384,1536]{2,1,0:T(8,128)(2,1)S(1)} copy-done((bf16[2,384,1536]{2,1,0:T(8,128)(2,1)S(1)}, bf16[2,384,1536]{2,1,0:T(8,128)(2,1)}, u32[]{:S(2)}) %copy-start.1) | copy-done | bytes 2359320
  14.9 9.5 %forward.1 = (f32[3,22,24,128]{3,2,1,0:T(8,128)S(1)}, f32[3,16,16,128]{3,2,1,0:T(8,128)S(1)}) custom-call(s32[4]{0:T(128)S(1)} %pad_add_fusion.place, bf16[28,32,384]{2,1,0:T(8,128)(2,1)S(1)} %fusion.12.xpad.source, f32[2,3,49,128]{3,2,1,0:T(8,128)S(1)} %bitcast.84, f32[2,384]{1,0:T(2,128)S(1)} %copy-done.21, f32[2,384]{1,0:T(2,128)S(1)} %copy-done.22, ...), custom_call_target="tpu_custom_call" | custom-call | tf_op jit(solution)/shard_map/forward/pallas_call | solution.py:303
  25.2 5.0 %top.1 = (bf16[256,384]{1,0:T(8,128)(2,1)S(1)}, bf16[256,384]{1,0:T(8,128)(2,1)S(1)}, bf16[256,1536]{1,0:T(8,128)(2,1)S(1)}, bf16[256,1536]{1,0:T(8,128)(2,1)S(1...) custom-call(f32[3,22,24,128]{3,2,1,0:T(8,128)S(1)} %get-tuple-element.83.mids.source, ...), custom_call_target="tpu_custom_call" | custom-call | tf_op jit(solution)/shard_map/top/pallas_call | solution.py:303
  33.3 4.3 %collective-permute-start.4 = (bf16[16,3,384]{2,1,0:T(4,128)(2,1)}, bf16[16,3,384]{2,1,0:T(4,128)(2,1)S(1)}, u32[]{:S(2)}, u32[]{:S(2)}) collective-permute-start(bf16[16,3,384]{2,1,0:T(4,128)(2,1)} %get-tuple-element.200), channel_id=1, source_target_pairs={{0,1},{1,0},{2,3},{3,2},{4,5},{5,4},{6,7},{7,6},{8,9},{9,8},{10,11... | collective-permute-start | bytes 110600 | tf_op jit(solution)/shard_map/ppermute | solution.py:325
  44.1 2.8 %top_taps.1 = (bf16[2,1536,384]{2,1,0:T(8,128)(2,1)S(1)}, bf16[64,384]{1,0:T(8,128)(2,1)S(1)}) custom-call(f32[3,22,24,128]{3,2,1,0:T(8,128)S(1)} %copy-done.4, bf16[256,384]{1,0:T(8,128)(2,1)S(1)} %copy-done.10, bf16[256,384]{1,0:T(8,128)(2,1)S(1)} %copy-done.20, bf16[256,1536]{1,0:T(8,128)(2,1)S(1)} %copy-done.12, bf16[256,1536]{1,0:T(8,128)(2,1)S(1)} %copy-done.14, ...), custom_call_target="tpu_custom_call" | custom-call | tf_op jit(solution)/shard_map/top_taps/pallas_call | solution.py:303
  46.9 1.6 %dynamic-slice_bitcast_fusion.2 = (bf16[2,16,1,48,384]{4,3,1,2,0:T(8,128)(2,1)}, bf16[2,16,1,48,384]{4,3,1,2,0:T(8,128)(2,1)}) fusion(bf16[2,16,2,1,48,384]{5,4,2,1,0,3:T(8,128)(2,1)S(1)} %bitcast.88, s32[]{:T(128)S(6)} %select_n.198, s32[]{:T(128)S(6)} %select_n.197), kind=kLoop, calls=%fused_computation.10 | loop fusion | bytes 4718600 | tf_op jit(solution)/shard_map/jit(dynamic_index_in_dim)/squeeze | solution.py:346
  48.6 3.1 %collective-permute-start.8 = (bf16[2,16,1,48,384]{4,3,1,2,0:T(8,128)(2,1)}, bf16[2,16,1,48,384]{4,3,1,2,0:T(8,128)(2,1)}, u32[]{:S(2)}, u32[]{:S(2)}) collective-permute-start(bf16[2,16,1,48,384]{4,3,1,2,0:T(8,128)(2,1)} %get-tuple-element.161), channel_id=1, source_target_pairs={{0,1},{1,0},{2,3},{3,2},{4,5},{5,4},{6,7},{7,6},{8,9},{9,8},{10,11... | collective-permute-start | bytes 3538952 | tf_op jit(solution)/shard_map/ppermute | solution.py:342
  54.1 4.7 %collective-permute-start.6 = (bf16[3,22,384]{2,1,0:T(8,128)(2,1)}, bf16[3,22,384]{2,1,0:T(8,128)(2,1)S(1)}, u32[]{:S(2)}, u32[]{:S(2)}) collective-permute-start(bf16[3,22,384]{2,1,0:T(8,128)(2,1)} %get-tuple-element.192), channel_id=1, source_target_pairs={{0,4},{4,0},{8,12},{12,8},{16,20},{20,16},{24,28},{28,24},{1,5},{5... | collective-permute-start | bytes 152072 | tf_op jit(solution)/shard_map/ppermute | solution.py:325
  61.1 1.9 %add_convert_fusion.1 = bf16[2,16,1,48,384]{4,3,1,2,0:T(8,128)(2,1)S(1)} fusion(bf16[2,16,1,48,384]{4,3,1,2,0:T(8,128)(2,1)} %collective-permute-done.8, bf16[2,16,1,48,384]{4,3,1,2,0:T(8,128)(2,1)} %get-tuple-element.103), kind=kLoop, calls=%fused_computation.1 | loop fusion | flops 2359296 | bytes 3538944 | tf_op jit(solution)/shard_map/convert_element_type | solution.py:352
  63.3 5.1 %collective-permute-start.10 = (bf16[1,4,2,48,384]{4,3,2,1,0:T(8,128)(2,1)S(1)}, bf16[1,4,2,48,384]{4,3,2,1,0:T(8,128)(2,1)S(1)}, u32[]{:S(2)}, u32[]{:S(2)}) collective-permute-start(bf16[1,4,2,48,384]{4,3,2,1,0:T(8,128)(2,1)S(1)} %get-tuple-element.171), channel_id=1, source_target_pairs={{0,4},{1,5},{2,6},{3,7},{4,0},{5,1},{6,2},{7,3},{8,12},{9,13},{10,... | collective-permute-start | bytes 884744 | tf_op jit(solution)/shard_map/ppermute | solution.py:342
  69.5 7.5 %low.1 = (bf16[256,384]{1,0:T(8,128)(2,1)S(1)}, bf16[256,384]{1,0:T(8,128)(2,1)S(1)}, bf16[2,1536,384]{2,1,0:T(8,128)(2,1)S(1)}, f32[1,1536]{1,0:T(1,128)S(1)}, ...) custom-call(bf16[22,32,384]{2,1,0:T(8,128)(2,1)S(1)} %fusion.18.dzpad, bf16[256,384]{1,0:T(8,128)(2,1)S(1)} %bitcast.91, ...), custom_call_target="tpu_custom_call" | custom-call | tf_op jit(solution)/shard_map/low/pallas_call | solution.py:303
  78.3 1.9 %low_taps.1 = bf16[64,384]{1,0:T(8,128)(2,1)S(1)} custom-call(bf16[28,32,384]{2,1,0:T(8,128)(2,1)S(1)} %fusion.12.xpad.source, bf16[256,384]{1,0:T(8,128)(2,1)S(1)} %get-tuple-element.113.dz, f32[1,1536]{1,0:T(1,128)S(1)} %get-tuple-element.114.db, f32[1,384]{1,0:T(1,128)S(1)} %get-tuple-element.115.dgain, f32[1,384]{1,0:T(1,128)S(1)} %get-tuple-element.116.dshift), custom_call_target="tpu_custom_call" | custom-call | tf_op jit(solution)/shard_map/low_taps/pallas_call | solution.py:303
  81.7 2.0 %collective-permute-start.13 = (bf16[1,4,1,48,384]{4,3,2,1,0:T(8,128)(2,1)}, bf16[1,4,1,48,384]{4,3,2,1,0:T(8,128)(2,1)S(1)}, u32[]{:S(2)}, u32[]{:S(2)}) collective-permute-start(bf16[1,4,1,48,384]{4,3,2,1,0:T(8,128)(2,1)} %get-tuple-element.187), channel_id=1, source_target_pairs={{0,2},{1,3},{2,0},{3,1},{4,6},{5,7},{6,4},{7,5},{8,10},{9,11},{10,... | collective-permute-start | bytes 442376 | tf_op jit(solution)/shard_map/ppermute | solution.py:342
  86.4 1.5 %collective-permute-done.13 = bf16[1,4,1,48,384]{4,3,2,1,0:T(8,128)(2,1)S(1)} collective-permute-done((bf16[1,4,1,48,384]{4,3,2,1,0:T(8,128)(2,1)}, bf16[1,4,1,48,384]{4,3,2,1,0:T(8,128)(2,1)S(1)}, u32[]{:S(2)}, u32[]{:S(2)}) %collective-permute-start.13) | collective-permute-done | bytes 147488 | tf_op jit(solution)/shard_map/ppermute | solution.py:342
  87.9 2.3 %collective-permute-done.12 = bf16[1,4,1,48,384]{4,3,1,2,0:T(8,128)(2,1)S(1)} collective-permute-done((bf16[1,4,1,48,384]{4,3,1,2,0:T(8,128)(2,1)}, bf16[1,4,1,48,384]{4,3,1,2,0:T(8,128)(2,1)S(1)}, u32[]{:S(2)}, u32[]{:S(2)}) %collective-permute-start.12) | collective-permute-done | bytes 147488 | tf_op jit(solution)/shard_map/ppermute | solution.py:342
  91.2 3.0 %collective-permute-start.18 = (bf16[2,2,1,48,384]{4,3,1,0,2:T(8,128)(2,1)}, bf16[2,2,1,48,384]{4,3,1,0,2:T(8,128)(2,1)}, u32[]{:S(2)}, u32[]{:S(2)}) collective-permute-start(bf16[2,2,1,48,384]{4,3,1,0,2:T(8,128)(2,1)} %get-tuple-element.185), channel_id=1, source_target_pairs={{0,8},{1,9},{2,10},{3,11},{4,12},{5,13},{6,14},{7,15},{8,0},{9,1},... | collective-permute-start | bytes 442376 | tf_op jit(solution)/shard_map/ppermute | solution.py:342
  94.2 1.6 %add_convert_fusion = bf16[2,16,1,48,384]{4,3,1,2,0:T(8,128)(2,1)S(1)} fusion(bf16[2,16,1,48,384]{4,3,1,2,0:T(8,128)(2,1)} %copy-done.26, bf16[2,16,1,48,384]{4,3,1,2,0:T(8,128)(2,1)S(1)} %get-tuple-element.118), kind=kLoop, calls=%fused_computation | loop fusion | flops 2359296 | bytes 3538944 | tf_op jit(solution)/shard_map/convert_element_type | solution.py:352
  97.0 1.8 %collective-permute-start.20 = (bf16[128,384]{1,0:T(8,128)(2,1)S(1)}, bf16[128,384]{1,0:T(8,128)(2,1)S(1)}, u32[]{:S(2)}, u32[]{:S(2)}) collective-permute-start(bf16[128,384]{1,0:T(8,128)(2,1)S(1)} %add_convert_fusion.16), channel_id=1, source_target_pairs={{0,2},{1,3},{2,0},{3,1},{4,6},{5,7},{6,4},{7,5},{8,10},{9,11},{10,... | collective-permute-start | bytes 294920 | tf_op jit(solution)/shard_map/ppermute | solution.py:342
  99.5 6.5 %collective-permute-done.20 = bf16[128,384]{1,0:T(8,128)(2,1)S(1)} collective-permute-done((bf16[128,384]{1,0:T(8,128)(2,1)S(1)}, bf16[128,384]{1,0:T(8,128)(2,1)S(1)}, u32[]{:S(2)}, u32[]{:S(2)}) %collective-permute-start.20) | collective-permute-done | bytes 98336 | tf_op jit(solution)/shard_map/ppermute | solution.py:342
  106.1 1.6 %collective-permute-start.25 = (bf16[128,384]{1,0:T(8,128)(2,1)S(1)}, bf16[128,384]{1,0:T(8,128)(2,1)S(1)}, u32[]{:S(2)}, u32[]{:S(2)}) collective-permute-start(bf16[128,384]{1,0:T(8,128)(2,1)S(1)} %add_convert_fusion.15), channel_id=1, source_target_pairs={{0,4},{1,5},{2,6},{3,7},{4,0},{5,1},{6,2},{7,3},{8,12},{9,13},{10,... | collective-permute-start | bytes 294920 | tf_op jit(solution)/shard_map/ppermute | solution.py:342
  108.7 1.4 collective-permute-start.23
  111.4 1.3 collective-permute-start.21
  113.8 3.4 %collective-permute-done.24 = bf16[3,22,384]{2,1,0:T(8,128)(2,1)S(1)} collective-permute-done((bf16[3,22,384]{2,1,0:T(8,128)(2,1)S(1)}, bf16[3,22,384]{2,1,0:T(8,128)(2,1)S(1)}, u32[]{:S(2)}, u32[]{:S(2)}) %collective-permute-start.24) | collective-permute-done | bytes 50720 | tf_op jit(solution)/shard_map/ppermute | solution.py:325
  117.3 1.8 %collective-permute-start.27 = (bf16[128,384]{1,0:T(8,128)(2,1)S(1)}, bf16[128,384]{1,0:T(8,128)(2,1)S(1)}, u32[]{:S(2)}, u32[]{:S(2)}) collective-permute-start(bf16[128,384]{1,0:T(8,128)(2,1)S(1)} %add_convert_fusion.14), channel_id=1, source_target_pairs={{0,8},{1,9},{2,10},{3,11},{4,12},{5,13},{6,14},{7,15},{8,0},{9,1},... | collective-permute-start | bytes 294920 | tf_op jit(solution)/shard_map/ppermute | solution.py:342
  120.4 1.8 %collective-permute-done.27 = bf16[128,384]{1,0:T(8,128)(2,1)S(1)} collective-permute-done((bf16[128,384]{1,0:T(8,128)(2,1)S(1)}, bf16[128,384]{1,0:T(8,128)(2,1)S(1)}, u32[]{:S(2)}, u32[]{:S(2)}) %collective-permute-start.27) | collective-permute-done | bytes 98336 | tf_op jit(solution)/shard_map/ppermute | solution.py:342
  122.1 2.4 %collective-permute-done.26 = bf16[2,2,1,48,384]{4,3,0,2,1:T(8,128)(2,1)S(1)} collective-permute-done((bf16[2,2,1,48,384]{4,3,0,2,1:T(8,128)(2,1)S(1)}, bf16[2,2,1,48,384]{4,3,0,2,1:T(8,128)(2,1)S(1)}, u32[]{:S(2)}, u32[]{:S(2)}) %collective-permute-start.26) | collective-permute-done | bytes 147488 | tf_op jit(solution)/shard_map/ppermute | solution.py:342
  124.6 3.8 %collective-permute-start.30 = (bf16[2,1,1,48,384]{4,3,0,2,1:T(8,128)(2,1)S(1)}, bf16[2,1,1,48,384]{4,3,0,2,1:T(8,128)(2,1)S(1)}, u32[]{:S(2)}, u32[]{:S(2)}) collective-permute-start(bf16[2,1,1,48,384]{4,3,0,2,1:T(8,128)(2,1)S(1)} %constant_dynamic-slice_fusion), channel_id=1, source_target_pairs={{0,16},{1,17},{2,18},{3,19},{4,20},{5,21},{6,22},{7,23},{8,24},{9,... | collective-permute-start | bytes 221192 | tf_op jit(solution)/shard_map/ppermute | solution.py:342
  128.6 2.7 %last.1 = bf16[256,384]{1,0:T(8,128)(2,1)} custom-call(bf16[22,32,384]{2,1,0:T(8,128)(2,1)S(1)} %fusion.16.dzpad, bf16[256,384]{1,0:T(8,128)(2,1)S(1)} %copy-done.18, f32[2,3,49,128]{3,2,1,0:T(8,128)S(1)} %copy-done.6), custom_call_target="tpu_custom_call" | custom-call | tf_op jit(solution)/shard_map/last/pallas_call | solution.py:303
  132.3 3.6 %collective-permute-done.29 = bf16[128,384]{1,0:T(8,128)(2,1)S(1)} collective-permute-done((bf16[128,384]{1,0:T(8,128)(2,1)S(1)}, bf16[128,384]{1,0:T(8,128)(2,1)S(1)}, u32[]{:S(2)}, u32[]{:S(2)}) %collective-permute-start.29) | collective-permute-done | bytes 98336 | tf_op jit(solution)/shard_map/ppermute | solution.py:342
  (170 shorter events, 38.7 us)
Async XLA Ops:
  1.7 1.5 %collective-permute-start = (bf16[16,6,384]{2,1,0:T(8,128)(2,1)S(1)}, bf16[16,6,384]{2,1,0:T(8,128)(2,1)S(1)}, u32[]{:S(2)}, u32[]{:S(2)}) collective-permute-start(bf16[16,6,384]{2,1,0:T(8,128)(2,1)S(1)} %get-tuple-element.203), channel_id=1, source_target_pairs={{0,1},{1,0},{2,3},{3,2},{4,5},{5,4},{6,7},{7,6},{8,9},{9,8},{10,11... | collective-permute-start | bytes 221192 | tf_op jit(solution)/shard_map/ppermute | solution.py:325
  2.2 0.9 collective-permute-start.1
  5.0 6.2 %collective-permute-start.2 = (bf16[6,28,384]{2,1,0:T(8,128)(2,1)}, bf16[6,28,384]{2,1,0:T(8,128)(2,1)S(1)}, u32[]{:S(2)}, u32[]{:S(2)}) collective-permute-start(bf16[6,28,384]{2,1,0:T(8,128)(2,1)} %get-tuple-element.175), channel_id=1, source_target_pairs={{0,4},{4,0},{8,12},{12,8},{16,20},{20,16},{24,28},{28,24},{1,5},{5... | collective-permute-start | bytes 387080 | tf_op jit(solution)/shard_map/ppermute | solution.py:325
  7.8 3.3 %collective-permute-start.3 = (bf16[6,28,384]{2,1,0:T(8,128)(2,1)S(1)}, bf16[6,28,384]{2,1,0:T(8,128)(2,1)}, u32[]{:S(2)}, u32[]{:S(2)}) collective-permute-start(bf16[6,28,384]{2,1,0:T(8,128)(2,1)S(1)} %get-tuple-element.176), channel_id=1, source_target_pairs={{4,8},{12,16},{20,24},{8,4},{16,12},{24,20},{5,9},{13,17},{21,25},... | collective-permute-start | bytes 387080 | tf_op jit(solution)/shard_map/ppermute | solution.py:330
  14.9 10.2 %copy-start.5 = (bf16[16,16,384]{2,1,0:T(8,128)(2,1)S(1)}, bf16[16,16,384]{2,1,0:T(8,128)(2,1)}, u32[]{:S(2)}) copy-start(bf16[16,16,384]{2,1,0:T(8,128)(2,1)} %param.9) | copy-start | bytes 589828
  33.3 13.6 %collective-permute-start.4 = (bf16[16,3,384]{2,1,0:T(4,128)(2,1)}, bf16[16,3,384]{2,1,0:T(4,128)(2,1)S(1)}, u32[]{:S(2)}, u32[]{:S(2)}) collective-permute-start(bf16[16,3,384]{2,1,0:T(4,128)(2,1)} %get-tuple-element.200), channel_id=1, source_target_pairs={{0,1},{1,0},{2,3},{3,2},{4,5},{5,4},{6,7},{7,6},{8,9},{9,8},{10,11... | collective-permute-start | bytes 110600 | tf_op jit(solution)/shard_map/ppermute | solution.py:325
  37.6 9.4 %collective-permute-start.5 = (bf16[16,3,384]{2,1,0:T(4,128)(2,1)}, bf16[16,3,384]{2,1,0:T(4,128)(2,1)}, u32[]{:S(2)}, u32[]{:S(2)}) collective-permute-start(bf16[16,3,384]{2,1,0:T(4,128)(2,1)} %get-tuple-element.199), channel_id=1, source_target_pairs={{1,2},{2,1},{5,6},{6,5},{9,10},{10,9},{13,14},{14,13},{17,18},{18,... | collective-permute-start | bytes 110600 | tf_op jit(solution)/shard_map/ppermute | solution.py:330
  48.6 12.6 %collective-permute-start.8 = (bf16[2,16,1,48,384]{4,3,1,2,0:T(8,128)(2,1)}, bf16[2,16,1,48,384]{4,3,1,2,0:T(8,128)(2,1)}, u32[]{:S(2)}, u32[]{:S(2)}) collective-permute-start(bf16[2,16,1,48,384]{4,3,1,2,0:T(8,128)(2,1)} %get-tuple-element.161), channel_id=1, source_target_pairs={{0,1},{1,0},{2,3},{3,2},{4,5},{5,4},{6,7},{7,6},{8,9},{9,8},{10,11... | collective-permute-start | bytes 3538952 | tf_op jit(solution)/shard_map/ppermute | solution.py:342
  54.1 7.0 %collective-permute-start.6 = (bf16[3,22,384]{2,1,0:T(8,128)(2,1)}, bf16[3,22,384]{2,1,0:T(8,128)(2,1)S(1)}, u32[]{:S(2)}, u32[]{:S(2)}) collective-permute-start(bf16[3,22,384]{2,1,0:T(8,128)(2,1)} %get-tuple-element.192), channel_id=1, source_target_pairs={{0,4},{4,0},{8,12},{12,8},{16,20},{20,16},{24,28},{28,24},{1,5},{5... | collective-permute-start | bytes 152072 | tf_op jit(solution)/shard_map/ppermute | solution.py:325
  58.8 2.3 %collective-permute-start.7 = (bf16[3,22,384]{2,1,0:T(8,128)(2,1)}, bf16[3,22,384]{2,1,0:T(8,128)(2,1)}, u32[]{:S(2)}, u32[]{:S(2)}) collective-permute-start(bf16[3,22,384]{2,1,0:T(8,128)(2,1)} %get-tuple-element.191), channel_id=1, source_target_pairs={{4,8},{12,16},{20,24},{8,4},{16,12},{24,20},{5,9},{13,17},{21,25},... | collective-permute-start | bytes 152072 | tf_op jit(solution)/shard_map/ppermute | solution.py:330
  63.3 13.7 %collective-permute-start.10 = (bf16[1,4,2,48,384]{4,3,2,1,0:T(8,128)(2,1)S(1)}, bf16[1,4,2,48,384]{4,3,2,1,0:T(8,128)(2,1)S(1)}, u32[]{:S(2)}, u32[]{:S(2)}) collective-permute-start(bf16[1,4,2,48,384]{4,3,2,1,0:T(8,128)(2,1)S(1)} %get-tuple-element.171), channel_id=1, source_target_pairs={{0,4},{1,5},{2,6},{3,7},{4,0},{5,1},{6,2},{7,3},{8,12},{9,13},{10,... | collective-permute-start | bytes 884744 | tf_op jit(solution)/shard_map/ppermute | solution.py:342
  68.5 8.6 %collective-permute-start.9 = (bf16[1,8,1,48,384]{4,3,1,2,0:T(8,128)(2,1)S(1)}, bf16[1,8,1,48,384]{4,3,1,2,0:T(8,128)(2,1)S(1)}, u32[]{:S(2)}, u32[]{:S(2)}) collective-permute-start(bf16[1,8,1,48,384]{4,3,1,2,0:T(8,128)(2,1)S(1)} %get-tuple-element.173), channel_id=1, source_target_pairs={{0,2},{1,3},{2,0},{3,1},{4,6},{5,7},{6,4},{7,5},{8,10},{9,11},{10,... | collective-permute-start | bytes 884744 | tf_op jit(solution)/shard_map/ppermute | solution.py:342
  78.3 11.8 %collective-permute-start.11 = (bf16[2,16,1,48,384]{4,3,1,2,0:T(8,128)(2,1)}, bf16[2,16,1,48,384]{4,3,1,2,0:T(8,128)(2,1)S(1)}, u32[]{:S(2)}, u32[]{:S(2)}) collective-permute-start(bf16[2,16,1,48,384]{4,3,1,2,0:T(8,128)(2,1)} %get-tuple-element.159), channel_id=1, source_target_pairs={{0,1},{1,0},{2,3},{3,2},{4,5},{5,4},{6,7},{7,6},{8,9},{9,8},{10,11... | collective-permute-start | bytes 3538952 | tf_op jit(solution)/shard_map/ppermute | solution.py:342
  80.3 6.1 %collective-permute-start.14 = (bf16[128,384]{1,0:T(8,128)(2,1)S(1)}, bf16[128,384]{1,0:T(8,128)(2,1)S(1)}, u32[]{:S(2)}, u32[]{:S(2)}) collective-permute-start(bf16[128,384]{1,0:T(8,128)(2,1)S(1)} %pad_maximum_fusion.7), channel_id=1, source_target_pairs={{0,1},{1,0},{2,3},{3,2},{4,5},{5,4},{6,7},{7,6},{8,9},{9,8},{10,11... | collective-permute-start | bytes 294920 | tf_op jit(solution)/shard_map/ppermute | solution.py:342
  81.7 6.2 %collective-permute-start.13 = (bf16[1,4,1,48,384]{4,3,2,1,0:T(8,128)(2,1)}, bf16[1,4,1,48,384]{4,3,2,1,0:T(8,128)(2,1)S(1)}, u32[]{:S(2)}, u32[]{:S(2)}) collective-permute-start(bf16[1,4,1,48,384]{4,3,2,1,0:T(8,128)(2,1)} %get-tuple-element.187), channel_id=1, source_target_pairs={{0,2},{1,3},{2,0},{3,1},{4,6},{5,7},{6,4},{7,5},{8,10},{9,11},{10,... | collective-permute-start | bytes 442376 | tf_op jit(solution)/shard_map/ppermute | solution.py:342
  84.5 5.7 %collective-permute-start.12 = (bf16[1,4,1,48,384]{4,3,1,2,0:T(8,128)(2,1)}, bf16[1,4,1,48,384]{4,3,1,2,0:T(8,128)(2,1)S(1)}, u32[]{:S(2)}, u32[]{:S(2)}) collective-permute-start(bf16[1,4,1,48,384]{4,3,1,2,0:T(8,128)(2,1)} %get-tuple-element.189), channel_id=1, source_target_pairs={{0,4},{1,5},{2,6},{3,7},{4,0},{5,1},{6,2},{7,3},{8,12},{9,13},{10,... | collective-permute-start | bytes 442376 | tf_op jit(solution)/shard_map/ppermute | solution.py:342
  85.2 1.2 collective-permute-start.15
  91.2 14.8 %collective-permute-start.18 = (bf16[2,2,1,48,384]{4,3,1,0,2:T(8,128)(2,1)}, bf16[2,2,1,48,384]{4,3,1,0,2:T(8,128)(2,1)}, u32[]{:S(2)}, u32[]{:S(2)}) collective-permute-start(bf16[2,2,1,48,384]{4,3,1,0,2:T(8,128)(2,1)} %get-tuple-element.185), channel_id=1, source_target_pairs={{0,8},{1,9},{2,10},{3,11},{4,12},{5,13},{6,14},{7,15},{8,0},{9,1},... | collective-permute-start | bytes 442376 | tf_op jit(solution)/shard_map/ppermute | solution.py:342
  96.0 10.0 %collective-permute-start.17 = (bf16[1,4,2,48,384]{4,3,2,1,0:T(8,128)(2,1)S(1)}, bf16[1,4,2,48,384]{4,3,2,1,0:T(8,128)(2,1)S(1)}, u32[]{:S(2)}, u32[]{:S(2)}) collective-permute-start(bf16[1,4,2,48,384]{4,3,2,1,0:T(8,128)(2,1)S(1)} %get-tuple-element.167), channel_id=1, source_target_pairs={{0,4},{1,5},{2,6},{3,7},{4,0},{5,1},{6,2},{7,3},{8,12},{9,13},{10,... | collective-permute-start | bytes 884744 | tf_op jit(solution)/shard_map/ppermute | solution.py:342
  96.6 9.4 %collective-permute-start.16 = (bf16[1,8,1,48,384]{4,3,1,2,0:T(8,128)(2,1)S(1)}, bf16[1,8,1,48,384]{4,3,1,2,0:T(8,128)(2,1)S(1)}, u32[]{:S(2)}, u32[]{:S(2)}) collective-permute-start(bf16[1,8,1,48,384]{4,3,1,2,0:T(8,128)(2,1)S(1)} %get-tuple-element.169), channel_id=1, source_target_pairs={{0,2},{1,3},{2,0},{3,1},{4,6},{5,7},{6,4},{7,5},{8,10},{9,11},{10,... | collective-permute-start | bytes 884744 | tf_op jit(solution)/shard_map/ppermute | solution.py:342
  97.0 9.0 %collective-permute-start.20 = (bf16[128,384]{1,0:T(8,128)(2,1)S(1)}, bf16[128,384]{1,0:T(8,128)(2,1)S(1)}, u32[]{:S(2)}, u32[]{:S(2)}) collective-permute-start(bf16[128,384]{1,0:T(8,128)(2,1)S(1)} %add_convert_fusion.16), channel_id=1, source_target_pairs={{0,2},{1,3},{2,0},{3,1},{4,6},{5,7},{6,4},{7,5},{8,10},{9,11},{10,... | collective-permute-start | bytes 294920 | tf_op jit(solution)/shard_map/ppermute | solution.py:342
  98.8 0.7 collective-permute-start.19
  106.1 11.2 %collective-permute-start.25 = (bf16[128,384]{1,0:T(8,128)(2,1)S(1)}, bf16[128,384]{1,0:T(8,128)(2,1)S(1)}, u32[]{:S(2)}, u32[]{:S(2)}) collective-permute-start(bf16[128,384]{1,0:T(8,128)(2,1)S(1)} %add_convert_fusion.15), channel_id=1, source_target_pairs={{0,4},{1,5},{2,6},{3,7},{4,0},{5,1},{6,2},{7,3},{8,12},{9,13},{10,... | collective-permute-start | bytes 294920 | tf_op jit(solution)/shard_map/ppermute | solution.py:342
  108.7 8.6 %collective-permute-start.23 = (bf16[2,1,1,48,384]{4,3,1,0,2:T(8,128)(2,1)S(1)}, bf16[2,1,1,48,384]{4,3,1,0,2:T(8,128)(2,1)S(1)}, u32[]{:S(2)}, u32[]{:S(2)}) collective-permute-start(bf16[2,1,1,48,384]{4,3,1,0,2:T(8,128)(2,1)S(1)} %get-tuple-element.209), channel_id=1, source_target_pairs={{0,16},{1,17},{2,18},{3,19},{4,20},{5,21},{6,22},{7,23},{8,24},{9,... | collective-permute-start | bytes 221192 | tf_op jit(solution)/shard_map/ppermute | solution.py:342
  110.2 7.1 %collective-permute-start.22 = (bf16[1,4,1,48,384]{4,3,2,1,0:T(8,128)(2,1)S(1)}, bf16[1,4,1,48,384]{4,3,2,1,0:T(8,128)(2,1)S(1)}, u32[]{:S(2)}, u32[]{:S(2)}) collective-permute-start(bf16[1,4,1,48,384]{4,3,2,1,0:T(8,128)(2,1)S(1)} %get-tuple-element.181), channel_id=1, source_target_pairs={{0,2},{1,3},{2,0},{3,1},{4,6},{5,7},{6,4},{7,5},{8,10},{9,11},{10,... | collective-permute-start | bytes 442376 | tf_op jit(solution)/shard_map/ppermute | solution.py:342
  111.4 5.8 %collective-permute-start.21 = (bf16[1,4,1,48,384]{4,3,1,2,0:T(8,128)(2,1)S(1)}, bf16[1,4,1,48,384]{4,3,1,2,0:T(8,128)(2,1)S(1)}, u32[]{:S(2)}, u32[]{:S(2)}) collective-permute-start(bf16[1,4,1,48,384]{4,3,1,2,0:T(8,128)(2,1)S(1)} %get-tuple-element.183), channel_id=1, source_target_pairs={{0,4},{1,5},{2,6},{3,7},{4,0},{5,1},{6,2},{7,3},{8,12},{9,13},{10,... | collective-permute-start | bytes 442376 | tf_op jit(solution)/shard_map/ppermute | solution.py:342
  113.0 4.2 %collective-permute-start.24 = (bf16[3,22,384]{2,1,0:T(8,128)(2,1)S(1)}, bf16[3,22,384]{2,1,0:T(8,128)(2,1)S(1)}, u32[]{:S(2)}, u32[]{:S(2)}) collective-permute-start(bf16[3,22,384]{2,1,0:T(8,128)(2,1)S(1)} %get-tuple-element.180), channel_id=1, source_target_pairs={{0,4},{4,0},{8,12},{12,8},{16,20},{20,16},{24,28},{28,24},{1,5},{5... | collective-permute-start | bytes 152072 | tf_op jit(solution)/shard_map/ppermute | solution.py:325
  117.3 4.8 %collective-permute-start.27 = (bf16[128,384]{1,0:T(8,128)(2,1)S(1)}, bf16[128,384]{1,0:T(8,128)(2,1)S(1)}, u32[]{:S(2)}, u32[]{:S(2)}) collective-permute-start(bf16[128,384]{1,0:T(8,128)(2,1)S(1)} %add_convert_fusion.14), channel_id=1, source_target_pairs={{0,8},{1,9},{2,10},{3,11},{4,12},{5,13},{6,14},{7,15},{8,0},{9,1},... | collective-permute-start | bytes 294920 | tf_op jit(solution)/shard_map/ppermute | solution.py:342
  119.3 5.2 %collective-permute-start.26 = (bf16[2,2,1,48,384]{4,3,0,2,1:T(8,128)(2,1)S(1)}, bf16[2,2,1,48,384]{4,3,0,2,1:T(8,128)(2,1)S(1)}, u32[]{:S(2)}, u32[]{:S(2)}) collective-permute-start(bf16[2,2,1,48,384]{4,3,0,2,1:T(8,128)(2,1)S(1)} %copy.30), channel_id=1, source_target_pairs={{0,8},{1,9},{2,10},{3,11},{4,12},{5,13},{6,14},{7,15},{8,0},{9,1},... | collective-permute-start | bytes 442376 | tf_op jit(solution)/shard_map/ppermute | solution.py:342
  119.6 0.7 collective-permute-start.28
  124.6 6.9 %collective-permute-start.30 = (bf16[2,1,1,48,384]{4,3,0,2,1:T(8,128)(2,1)S(1)}, bf16[2,1,1,48,384]{4,3,0,2,1:T(8,128)(2,1)S(1)}, u32[]{:S(2)}, u32[]{:S(2)}) collective-permute-start(bf16[2,1,1,48,384]{4,3,0,2,1:T(8,128)(2,1)S(1)} %constant_dynamic-slice_fusion), channel_id=1, source_target_pairs={{0,16},{1,17},{2,18},{3,19},{4,20},{5,21},{6,22},{7,23},{8,24},{9,... | collective-permute-start | bytes 221192 | tf_op jit(solution)/shard_map/ppermute | solution.py:342
  128.4 7.4 %collective-permute-start.29 = (bf16[128,384]{1,0:T(8,128)(2,1)S(1)}, bf16[128,384]{1,0:T(8,128)(2,1)S(1)}, u32[]{:S(2)}, u32[]{:S(2)}) collective-permute-start(bf16[128,384]{1,0:T(8,128)(2,1)S(1)} %add_convert_fusion.13), channel_id=1, source_target_pairs={{0,16},{1,17},{2,18},{3,19},{4,20},{5,21},{6,22},{7,23},{8,24},{9,... | collective-permute-start | bytes 294920 | tf_op jit(solution)/shard_map/ppermute | solution.py:342
  (32 other events, 114.1 us)

commit v6 on v5

--- a/solution.py
+++ b/solution.py
@@ -54,7 +54,7 @@
     return max(d for d in range(1, rows + 1) if rows % d == 0 and d <= most)
 
 
-def conv_pass(source, row0, col0, taps, target, rows, cols):
+def conv_pass(source, row0, col0, taps, target, rows, cols, back=False):
     strip = strip_rows(rows, cols)
     groups = source.shape[0]
 
@@ -63,7 +63,8 @@
         top = (step % (rows // strip)) * strip
         sums = [jnp.zeros((cols, LANES), F32) for _ in range(strip)]
         for b in range(7):
-            weights = [taps[g, pl.ds(7 * a + b, 1), :] for a in range(7)]
+            spots = [48 - 7 * a - b if back else 7 * a + b for a in range(7)]
+            weights = [taps[g, pl.ds(spot, 1), :] for spot in spots]
             for r in range(strip + 6):
                 line = source[g, row0 + top + r, pl.ds(col0 + b, cols), :]
                 for a in range(7):
@@ -239,12 +240,12 @@
 
 
 def low_kernel(
-    dzpad, grad, z0, taps_back, gains, shifts, w_in, w_out, b_in,
+    dzpad, grad, z0, taps, gains, shifts, w_in, w_out, b_in,
     gmid, dz_out, dw, db, dgain, dshift,
     dzs, spread, normed, act, gpre, w_in0, w_out0, arrived,
 ):
     waits = fetch_layers(((w_in, 0, w_in0), (w_out, 0, w_out0)), arrived)
-    spread_pass(dzpad, dzs, taps_back.at[1], spread)
+    spread_pass(dzpad, dzs, taps.at[1], spread)
     gmid[...] = (grad[...].astype(F32) + joined(spread, slice(None))).astype(BF16)
     block_back(
         z0, gmid, 0, gains, shifts, (w_in0, w_out0, waits), b_in,
@@ -252,14 +253,14 @@
     )
 
 
-def spread_pass(dzpad, dzs, taps_back, spread):
+def spread_pass(dzpad, dzs, taps, spread):
     for g in range(dzs.shape[0]):
         dzs[g] = dzpad[:, :, g * LANES : (g + 1) * LANES].astype(F32)
-    conv_pass(dzs, 0, 0, taps_back, spread, *spread.shape[1:3])
-
-
-def last_kernel(dzpad, gmid, taps_back, out, dzs, spread):
-    spread_pass(dzpad, dzs, taps_back.at[0], spread)
+    conv_pass(dzs, 0, 0, taps, spread, *spread.shape[1:3], back=True)
+
+
+def last_kernel(dzpad, gmid, taps, out, dzs, spread):
+    spread_pass(dzpad, dzs, taps.at[0], spread)
     out[...] = (gmid[...].astype(F32) + joined(spread, slice(None))).astype(BF16)
 
 
@@ -308,7 +309,7 @@
         ],
         out_specs=tuple(vmem for _ in outs),
         scratch_shapes=[pltpu.VMEM(s.shape, s.dtype) for s in scratch] + semaphores,
-        compiler_params=pltpu.CompilerParams(vmem_limit_bytes=24 * 1024 * 1024),
+        compiler_params=pltpu.CompilerParams(vmem_limit_bytes=50 * 1024 * 1024),
         name=name,
     )(*args)
 
@@ -343,9 +344,13 @@
 
 
 def halves(chunks, dim, mine):
-    other = lax.dynamic_index_in_dim(chunks, 1 - mine, dim, keepdims=False)
-    own = lax.dynamic_index_in_dim(chunks, mine, dim, keepdims=False)
-    return other, own
+    sizes = [1 if d == dim else n for d, n in enumerate(chunks.shape)]
+
+    def one(bit):
+        starts = [bit if d == dim else jnp.uint32(0) for d in range(chunks.ndim)]
+        return lax.squeeze(lax.dynamic_slice(chunks, starts, sizes), (dim,))
+
+    return one(mine[1]), one(mine[0])
 
 
 def summed(own, got):
@@ -368,13 +373,12 @@
     total = n_rows * n_cols
     bits = total.bit_length() - 1
     col_bits = n_cols.bit_length() - 1
-    me = lax.axis_index("rows") * n_cols + lax.axis_index("cols")
-    mine = [(me >> k) & 1 for k in range(bits)]
+    me = (lax.axis_index("rows") * n_cols + lax.axis_index("cols")).astype(jnp.uint32)
+    mine = [(((me >> k) & 1), 1 - ((me >> k) & 1)) for k in range(bits)]
     grad_scale = 1.0 / math.sqrt(rows * cols * total)
     pixels = rows * cols
 
     taps = kernels.reshape(layers, 49, groups, LANES).transpose(0, 2, 1, 3)
-    taps_back = taps[:, :, ::-1]
     biases = b_in[:, None, :]
     place = jnp.stack(
         [
@@ -386,8 +390,8 @@
     ).astype(jnp.int32)
     grad_flat = grad_out.reshape(pixels, channels)
 
-    odd_col = lax.axis_index("cols") % 2 == 1
-    odd_row = lax.axis_index("rows") % 2 == 1
+    odd_col = (lax.axis_index("cols") & 1) == 1
+    odd_row = (lax.axis_index("rows") & 1) == 1
 
     def rim_cols(tile, width):
         twin, other = edges(tile, 1, width, odd_col)
@@ -411,6 +415,7 @@
     small_rows = 64
 
     xpad = filled(rim_rows(rim_cols(activations, WIDE), WIDE))
+    xpad, place, mine, odd_col, odd_row = lax.optimization_barrier((xpad, place, mine, odd_col, odd_row))
     mids, z0 = run(
         forward_kernel,
         (shape(groups, mid_rows, mid_cols, LANES), tile_z),
@@ -498,7 +503,7 @@
         low_kernel,
         (tile_b, tile_b, grads_b) + small_outs,
         spread_scratch + [tile_b, tile_h, tile_h] + weights,
-        (dzpad1, grad_flat, z0, taps_back, norm_gains, norm_shifts, w_in, w_out, biases),
+        (dzpad1, grad_flat, z0, taps, norm_gains, norm_shifts, w_in, w_out, biases),
         [None] * 6 + [pl.ANY] * 2 + [None],
         fetched=2,
         name="low",
@@ -554,7 +559,7 @@
                 last_kernel,
                 (tile_b,),
                 spread_scratch,
-                (filled(rimmed(*wait, 0, odd_row)), grad_mid, taps_back),
+                (filled(rimmed(*wait, 0, odd_row)), grad_mid, taps),
                 name="last",
             )
     grad_in = wait

time: 139 us -> 114 us (0.82)
  local copies, waits for them, and re-layouts: 18.8 us -> 5.04 us
  other arithmetic: 15.9 us -> 5.33 us
  waiting for transfers between devices: 25.1 us -> 27.1 us
    unnamed x68 -> x14, local copies, waits for them, and re-layouts: 11.6 us -> 0.64 us
    convert_element_type x16, other arithmetic: 5.05 us -> 1.31 us  [summed(): return (own.astype(F32) + got.astype(F32)).astype(BF16)]
    select_n x6, other arithmetic: 4.84 us -> 2.24 us  [edges(): return (jnp.where(odd, low, high), jnp.where(odd, high, low))]
    select_n x6, other arithmetic: 2.72 us -> 0.18 us  [rimmed(): low = jnp.where(odd, from_twin, from_other)]
    squeeze x13, local copies, waits for them, and re-layouts: 4.7 us -> 2.58 us  [one(): return lax.squeeze(lax.dynamic_slice(chunks, starts, sizes), (dim,))]
    ppermute x6, starting transfers between devices: 5.82 us -> 4.1 us  [to_other(): return lax.ppermute(edge, axis, pairs + [(j, i) for i, j in pairs])]
    ppermute x6, waiting for transfers between devices: 6.93 us -> 8.44 us  [to_twin(): lax.ppermute(edge, axis, [(i, i ^ 1) for i in range(count) if i ^ 1 < cou...]
  transfers between devices with their start and end apart: 31 -> 31, of which waited for: 12 -> 13; matrix products, arithmetic and copies ran while one was open for 7% -> 3% of each run, Pallas kernels for 11% -> 14%
where the time goes in v6:
time: 114 us
  starting transfers between devices  45.9 us (40%)
  Pallas kernels  29.1 us (26%)
  waiting for transfers between devices  27.1 us (24%)
  other arithmetic  5.33 us (5%)
  local copies, waits for them, and re-layouts  5.04 us (4%)
  between operations  1.26 us (1%)
    pallas_call x6, Pallas kernels, run(): pl.pallas_call(kernel, out_shape=outs, in_specs=[vmem if s is None else p...  29.1 us
    ppermute x19, starting transfers between devices, flip_bit(): return lax.ppermute(value, both, [(i, i ^ 1 << bit) for i in range(total)])  28.1 us
    ppermute x19, waiting for transfers between devices, flip_bit(): return lax.ppermute(value, both, [(i, i ^ 1 << bit) for i in range(total)])  18.7 us
    ppermute x6, starting transfers between devices, to_twin(): lax.ppermute(edge, axis, [(i, i ^ 1) for i in range(count) if i ^ 1 < cou...  13.7 us
    ppermute x6, waiting for transfers between devices, to_twin(): lax.ppermute(edge, axis, [(i, i ^ 1) for i in range(count) if i ^ 1 < cou...  8.44 us
    ppermute x6, starting transfers between devices, to_other(): return lax.ppermute(edge, axis, pairs + [(j, i) for i, j in pairs])  4.1 us
    squeeze x13, local copies, waits for them, and re-layouts, one(): return lax.squeeze(lax.dynamic_slice(chunks, starts, sizes), (dim,))  2.58 us
  transfers between devices with their start and end apart: 31, of which 13 were waited for; matrix products, arithmetic and copies ran while one was open for 3% of the time, Pallas kernels for 14%

profile of v6, /device:TPU:0, one launch (start us, length us, event | category | flops | bytes accessed | tf_op | source)
XLA Modules:
  0.0 113.7 jit_solution(5024893822333946610)
XLA Ops:
  0.7 1.0 broadcast_select_fusion.7
  3.2 1.1 broadcast_select_fusion.3
  4.3 2.9 %collective-permute-start.2 = (bf16[6,28,384]{2,1,0:T(8,128)(2,1)S(1)}, bf16[6,28,384]{2,1,0:T(8,128)(2,1)S(1)}, u32[]{:S(2)}, u32[]{:S(2)}) collective-permute-start(bf16[6,28,384]{2,1,0:T(8,128)(2,1)S(1)} %get-tuple-element.203), channel_id=1, source_target_pairs={{0,4},{4,0},{8,12},{12,8},{16,20},{20,16},{24,28},{28,24},{1,5},{5... | collective-permute-start | bytes 387080 | tf_op jit(solution)/shard_map/ppermute | solution.py:326
  8.2 2.1 %collective-permute-done.2 = bf16[6,28,384]{2,1,0:T(8,128)(2,1)S(1)} collective-permute-done((bf16[6,28,384]{2,1,0:T(8,128)(2,1)S(1)}, bf16[6,28,384]{2,1,0:T(8,128)(2,1)S(1)}, u32[]{:S(2)}, u32[]{:S(2)}) %collective-permute-start.2) | collective-permute-done | bytes 129056 | tf_op jit(solution)/shard_map/ppermute | solution.py:326
  10.6 8.8 %forward.1 = (f32[3,22,24,128]{3,2,1,0:T(8,128)S(1)}, f32[3,16,16,128]{3,2,1,0:T(8,128)S(1)}) custom-call(s32[4]{0:T(128)S(1)} %pad_add_fusion.place, bf16[28,32,384]{2,1,0:T(8,128)(2,1)S(1)} %fusion.12.xpad.source, f32[2,3,49,128]{3,2,1,0:T(8,128)S(1)} %bitcast.84, f32[2,384]{1,0:T(2,128)S(1)} %copy-done.1, f32[2,384]{1,0:T(2,128)S(1)} %copy-done.2, ...), custom_call_target="tpu_custom_call" | custom-call | tf_op jit(solution)/shard_map/forward/pallas_call | solution.py:304
  19.4 4.8 %top.1 = (bf16[256,384]{1,0:T(8,128)(2,1)S(1)}, bf16[256,384]{1,0:T(8,128)(2,1)S(1)}, bf16[256,1536]{1,0:T(8,128)(2,1)S(1)}, bf16[256,1536]{1,0:T(8,128)(2,1)S(1...) custom-call(f32[3,22,24,128]{3,2,1,0:T(8,128)S(1)} %get-tuple-element.101.mids.source, ...), custom_call_target="tpu_custom_call" | custom-call | tf_op jit(solution)/shard_map/top/pallas_call | solution.py:304
  24.3 4.6 %collective-permute-start.4 = (bf16[16,3,384]{2,1,0:T(4,128)(2,1)S(1)}, bf16[16,3,384]{2,1,0:T(4,128)(2,1)S(1)}, u32[]{:S(2)}, u32[]{:S(2)}) collective-permute-start(bf16[16,3,384]{2,1,0:T(4,128)(2,1)S(1)} %get-tuple-element.228), channel_id=1, source_target_pairs={{0,1},{1,0},{2,3},{3,2},{4,5},{5,4},{6,7},{7,6},{8,9},{9,8},{10,11... | collective-permute-start | bytes 110600 | tf_op jit(solution)/shard_map/ppermute | solution.py:326
  29.6 4.2 %top_taps.1 = (bf16[2,1536,384]{2,1,0:T(8,128)(2,1)}, bf16[64,384]{1,0:T(8,128)(2,1)S(1)}) custom-call(f32[3,22,24,128]{3,2,1,0:T(8,128)S(1)} %get-tuple-element.101.mids.source, bf16[256,384]{1,0:T(8,128)(2,1)S(1)} %get-tuple-element.102.dz, bf16[256,384]{1,0:T(8,128)(2,1)S(1)} %get-tuple-element.103.normed, bf16[256,1536]{1,0:T(8,128)(2,1)S(1)} %get-tuple-element.104.act, ...), custom_call_target="tpu_custom_call" | custom-call | tf_op jit(solution)/shard_map/top_taps/pallas_call | solution.py:304
  33.8 1.9 %dynamic-slice_bitcast_fusion.2 = (bf16[2,16,1,48,384]{4,3,1,2,0:T(8,128)(2,1)S(1)}, bf16[2,16,1,48,384]{4,3,1,2,0:T(8,128)(2,1)S(1)}) fusion(bf16[2,16,2,1,48,384]{5,4,2,1,0,3:T(8,128)(2,1)} %bitcast.96, u32[]{:T(128)S(6)} %sub.15, u32[]{:T(128)S(6)} %and.30), kind=kLoop, calls=%fused_computation.10 | loop fusion | bytes 4718600 | tf_op jit(solution)/shard_map/squeeze | solution.py:351
  35.7 3.5 %collective-permute-start.8 = (bf16[2,16,1,48,384]{4,3,1,2,0:T(8,128)(2,1)S(1)}, bf16[2,16,1,48,384]{4,3,1,2,0:T(8,128)(2,1)S(1)}, u32[]{:S(2)}, u32[]{:S(2)}) collective-permute-start(bf16[2,16,1,48,384]{4,3,1,2,0:T(8,128)(2,1)S(1)} %get-tuple-element.189), channel_id=1, source_target_pairs={{0,1},{1,0},{2,3},{3,2},{4,5},{5,4},{6,7},{7,6},{8,9},{9,8},{10,11... | collective-permute-start | bytes 3538952 | tf_op jit(solution)/shard_map/ppermute | solution.py:343
  39.4 4.9 %collective-permute-start.6 = (bf16[3,22,384]{2,1,0:T(8,128)(2,1)S(1)}, bf16[3,22,384]{2,1,0:T(8,128)(2,1)S(1)}, u32[]{:S(2)}, u32[]{:S(2)}) collective-permute-start(bf16[3,22,384]{2,1,0:T(8,128)(2,1)S(1)} %get-tuple-element.220), channel_id=1, source_target_pairs={{0,4},{4,0},{8,12},{12,8},{16,20},{20,16},{24,28},{28,24},{1,5},{5... | collective-permute-start | bytes 152072 | tf_op jit(solution)/shard_map/ppermute | solution.py:326
  45.1 1.3 %collective-permute-done.6 = bf16[3,22,384]{2,1,0:T(8,128)(2,1)S(1)} collective-permute-done((bf16[3,22,384]{2,1,0:T(8,128)(2,1)S(1)}, bf16[3,22,384]{2,1,0:T(8,128)(2,1)S(1)}, u32[]{:S(2)}, u32[]{:S(2)}) %collective-permute-start.6) | collective-permute-done | bytes 50720 | tf_op jit(solution)/shard_map/ppermute | solution.py:326
  46.9 5.0 %collective-permute-start.10 = (bf16[1,4,2,48,384]{4,3,2,1,0:T(8,128)(2,1)S(1)}, bf16[1,4,2,48,384]{4,3,2,1,0:T(8,128)(2,1)S(1)}, u32[]{:S(2)}, u32[]{:S(2)}) collective-permute-start(bf16[1,4,2,48,384]{4,3,2,1,0:T(8,128)(2,1)S(1)} %get-tuple-element.199), channel_id=1, source_target_pairs={{0,4},{1,5},{2,6},{3,7},{4,0},{5,1},{6,2},{7,3},{8,12},{9,13},{10,... | collective-permute-start | bytes 884744 | tf_op jit(solution)/shard_map/ppermute | solution.py:343
  52.2 6.8 %low.1 = (bf16[256,384]{1,0:T(8,128)(2,1)S(1)}, bf16[256,384]{1,0:T(8,128)(2,1)S(1)}, bf16[2,1536,384]{2,1,0:T(8,128)(2,1)S(1)}, f32[1,1536]{1,0:T(1,128)S(1)}, ...) custom-call(bf16[22,32,384]{2,1,0:T(8,128)(2,1)S(1)} %fusion.18.dzpad, bf16[256,384]{1,0:T(8,128)(2,1)S(1)} %bitcast.91, ...), custom_call_target="tpu_custom_call" | custom-call | tf_op jit(solution)/shard_map/low/pallas_call | solution.py:304
  59.9 1.9 %low_taps.1 = bf16[64,384]{1,0:T(8,128)(2,1)S(1)} custom-call(bf16[28,32,384]{2,1,0:T(8,128)(2,1)S(1)} %fusion.12.xpad.source, bf16[256,384]{1,0:T(8,128)(2,1)S(1)} %get-tuple-element.137.dz, f32[1,1536]{1,0:T(1,128)S(1)} %get-tuple-element.138.db, f32[1,384]{1,0:T(1,128)S(1)} %get-tuple-element.139.dgain, f32[1,384]{1,0:T(1,128)S(1)} %get-tuple-element.140.dshift), custom_call_target="tpu_custom_call" | custom-call | tf_op jit(solution)/shard_map/low_taps/pallas_call | solution.py:304
  62.5 1.5 %collective-permute-start.13 = (bf16[1,4,1,48,384]{4,3,2,1,0:T(8,128)(2,1)S(1)}, bf16[1,4,1,48,384]{4,3,2,1,0:T(8,128)(2,1)S(1)}, u32[]{:S(2)}, u32[]{:S(2)}) collective-permute-start(bf16[1,4,1,48,384]{4,3,2,1,0:T(8,128)(2,1)S(1)} %get-tuple-element.215), channel_id=1, source_target_pairs={{0,2},{1,3},{2,0},{3,1},{4,6},{5,7},{6,4},{7,5},{8,10},{9,11},{10,... | collective-permute-start | bytes 442376 | tf_op jit(solution)/shard_map/ppermute | solution.py:343
  64.4 1.2 %collective-permute-done.15 = bf16[16,3,384]{2,1,0:T(4,128)(2,1)S(1)} collective-permute-done((bf16[16,3,384]{2,1,0:T(4,128)(2,1)S(1)}, bf16[16,3,384]{2,1,0:T(4,128)(2,1)S(1)}, u32[]{:S(2)}, u32[]{:S(2)}) %collective-permute-start.15) | collective-permute-done | bytes 36896 | tf_op jit(solution)/shard_map/ppermute | solution.py:326
  65.6 2.7 %collective-permute-done.13 = bf16[1,4,1,48,384]{4,3,2,1,0:T(8,128)(2,1)S(1)} collective-permute-done((bf16[1,4,1,48,384]{4,3,2,1,0:T(8,128)(2,1)S(1)}, bf16[1,4,1,48,384]{4,3,2,1,0:T(8,128)(2,1)S(1)}, u32[]{:S(2)}, u32[]{:S(2)}) %collective-permute-start.13) | collective-permute-done | bytes 147488 | tf_op jit(solution)/shard_map/ppermute | solution.py:343
  68.4 1.4 %collective-permute-done.12 = bf16[1,4,1,48,384]{4,3,1,2,0:T(8,128)(2,1)S(1)} collective-permute-done((bf16[1,4,1,48,384]{4,3,1,2,0:T(8,128)(2,1)S(1)}, bf16[1,4,1,48,384]{4,3,1,2,0:T(8,128)(2,1)S(1)}, u32[]{:S(2)}, u32[]{:S(2)}) %collective-permute-start.12) | collective-permute-done | bytes 147488 | tf_op jit(solution)/shard_map/ppermute | solution.py:343
  69.9 3.1 %collective-permute-start.18 = (bf16[2,2,1,48,384]{4,3,1,0,2:T(8,128)(2,1)S(1)}, bf16[2,2,1,48,384]{4,3,1,0,2:T(8,128)(2,1)S(1)}, u32[]{:S(2)}, u32[]{:S(2)}) collective-permute-start(bf16[2,2,1,48,384]{4,3,1,0,2:T(8,128)(2,1)S(1)} %get-tuple-element.213), channel_id=1, source_target_pairs={{0,8},{1,9},{2,10},{3,11},{4,12},{5,13},{6,14},{7,15},{8,0},{9,1},... | collective-permute-start | bytes 442376 | tf_op jit(solution)/shard_map/ppermute | solution.py:343
  74.5 1.8 %collective-permute-start.20 = (bf16[128,384]{1,0:T(8,128)(2,1)S(1)}, bf16[128,384]{1,0:T(8,128)(2,1)S(1)}, u32[]{:S(2)}, u32[]{:S(2)}) collective-permute-start(bf16[128,384]{1,0:T(8,128)(2,1)S(1)} %add_convert_fusion.16), channel_id=1, source_target_pairs={{0,2},{1,3},{2,0},{3,1},{4,6},{5,7},{6,4},{7,5},{8,10},{9,11},{10,... | collective-permute-start | bytes 294920 | tf_op jit(solution)/shard_map/ppermute | solution.py:343
  77.0 6.5 %collective-permute-done.20 = bf16[128,384]{1,0:T(8,128)(2,1)S(1)} collective-permute-done((bf16[128,384]{1,0:T(8,128)(2,1)S(1)}, bf16[128,384]{1,0:T(8,128)(2,1)S(1)}, u32[]{:S(2)}, u32[]{:S(2)}) %collective-permute-start.20) | collective-permute-done | bytes 98336 | tf_op jit(solution)/shard_map/ppermute | solution.py:343
  83.5 1.6 %collective-permute-start.25 = (bf16[128,384]{1,0:T(8,128)(2,1)S(1)}, bf16[128,384]{1,0:T(8,128)(2,1)S(1)}, u32[]{:S(2)}, u32[]{:S(2)}) collective-permute-start(bf16[128,384]{1,0:T(8,128)(2,1)S(1)} %add_convert_fusion.15), channel_id=1, source_target_pairs={{0,4},{1,5},{2,6},{3,7},{4,0},{5,1},{6,2},{7,3},{8,12},{9,13},{10,... | collective-permute-start | bytes 294920 | tf_op jit(solution)/shard_map/ppermute | solution.py:343
  85.2 1.4 %collective-permute-start.23 = (bf16[2,1,1,48,384]{4,3,1,0,2:T(8,128)(2,1)S(1)}, bf16[2,1,1,48,384]{4,3,1,0,2:T(8,128)(2,1)S(1)}, u32[]{:S(2)}, u32[]{:S(2)}) collective-permute-start(bf16[2,1,1,48,384]{4,3,1,0,2:T(8,128)(2,1)S(1)} %get-tuple-element.237), channel_id=1, source_target_pairs={{0,16},{1,17},{2,18},{3,19},{4,20},{5,21},{6,22},{7,23},{8,24},{9,... | collective-permute-start | bytes 221192 | tf_op jit(solution)/shard_map/ppermute | solution.py:343
  87.8 1.5 %collective-permute-start.21 = (bf16[1,4,1,48,384]{4,3,1,2,0:T(8,128)(2,1)S(1)}, bf16[1,4,1,48,384]{4,3,1,2,0:T(8,128)(2,1)S(1)}, u32[]{:S(2)}, u32[]{:S(2)}) collective-permute-start(bf16[1,4,1,48,384]{4,3,1,2,0:T(8,128)(2,1)S(1)} %get-tuple-element.211), channel_id=1, source_target_pairs={{0,4},{1,5},{2,6},{3,7},{4,0},{5,1},{6,2},{7,3},{8,12},{9,13},{10,... | collective-permute-start | bytes 442376 | tf_op jit(solution)/shard_map/ppermute | solution.py:343
  90.2 3.6 %collective-permute-done.24 = bf16[3,22,384]{2,1,0:T(8,128)(2,1)S(1)} collective-permute-done((bf16[3,22,384]{2,1,0:T(8,128)(2,1)S(1)}, bf16[3,22,384]{2,1,0:T(8,128)(2,1)S(1)}, u32[]{:S(2)}, u32[]{:S(2)}) %collective-permute-start.24) | collective-permute-done | bytes 50720 | tf_op jit(solution)/shard_map/ppermute | solution.py:326
  93.8 1.7 %collective-permute-start.27 = (bf16[128,384]{1,0:T(8,128)(2,1)S(1)}, bf16[128,384]{1,0:T(8,128)(2,1)S(1)}, u32[]{:S(2)}, u32[]{:S(2)}) collective-permute-start(bf16[128,384]{1,0:T(8,128)(2,1)S(1)} %add_convert_fusion.14), channel_id=1, source_target_pairs={{0,8},{1,9},{2,10},{3,11},{4,12},{5,13},{6,14},{7,15},{8,0},{9,1},... | collective-permute-start | bytes 294920 | tf_op jit(solution)/shard_map/ppermute | solution.py:343
  96.9 1.8 %collective-permute-done.27 = bf16[128,384]{1,0:T(8,128)(2,1)S(1)} collective-permute-done((bf16[128,384]{1,0:T(8,128)(2,1)S(1)}, bf16[128,384]{1,0:T(8,128)(2,1)S(1)}, u32[]{:S(2)}, u32[]{:S(2)}) %collective-permute-start.27) | collective-permute-done | bytes 98336 | tf_op jit(solution)/shard_map/ppermute | solution.py:343
  98.7 2.2 %collective-permute-done.26 = bf16[2,2,1,48,384]{4,3,0,2,1:T(8,128)(2,1)S(1)} collective-permute-done((bf16[2,2,1,48,384]{4,3,0,2,1:T(8,128)(2,1)S(1)}, bf16[2,2,1,48,384]{4,3,0,2,1:T(8,128)(2,1)S(1)}, u32[]{:S(2)}, u32[]{:S(2)}) %collective-permute-start.26) | collective-permute-done | bytes 147488 | tf_op jit(solution)/shard_map/ppermute | solution.py:343
  101.0 3.8 %collective-permute-start.30 = (bf16[2,1,1,48,384]{4,3,0,2,1:T(8,128)(2,1)S(1)}, bf16[2,1,1,48,384]{4,3,0,2,1:T(8,128)(2,1)S(1)}, u32[]{:S(2)}, u32[]{:S(2)}) collective-permute-start(bf16[2,1,1,48,384]{4,3,0,2,1:T(8,128)(2,1)S(1)} %constant_dynamic-slice_fusion), channel_id=1, source_target_pairs={{0,16},{1,17},{2,18},{3,19},{4,20},{5,21},{6,22},{7,23},{8,24},{9,... | collective-permute-start | bytes 221192 | tf_op jit(solution)/shard_map/ppermute | solution.py:343
  105.0 2.5 %last.1 = bf16[256,384]{1,0:T(8,128)(2,1)} custom-call(bf16[22,32,384]{2,1,0:T(8,128)(2,1)S(1)} %fusion.16.dzpad, bf16[256,384]{1,0:T(8,128)(2,1)S(1)} %get-tuple-element.180.gmid, f32[2,3,49,128]{3,2,1,0:T(8,128)S(1)} %bitcast.87), custom_call_target="tpu_custom_call" | custom-call | tf_op jit(solution)/shard_map/last/pallas_call | solution.py:304
  109.0 2.7 %collective-permute-done.29 = bf16[128,384]{1,0:T(8,128)(2,1)S(1)} collective-permute-done((bf16[128,384]{1,0:T(8,128)(2,1)S(1)}, bf16[128,384]{1,0:T(8,128)(2,1)S(1)}, u32[]{:S(2)}, u32[]{:S(2)}) %collective-permute-start.29) | collective-permute-done | bytes 98336 | tf_op jit(solution)/shard_map/ppermute | solution.py:343
  (115 shorter events, 16.5 us)
Async XLA Ops:
  1.7 1.5 %collective-permute-start = (bf16[16,6,384]{2,1,0:T(8,128)(2,1)S(1)}, bf16[16,6,384]{2,1,0:T(8,128)(2,1)S(1)}, u32[]{:S(2)}, u32[]{:S(2)}) collective-permute-start(bf16[16,6,384]{2,1,0:T(8,128)(2,1)S(1)} %get-tuple-element.231), channel_id=1, source_target_pairs={{0,1},{1,0},{2,3},{3,2},{4,5},{5,4},{6,7},{7,6},{8,9},{9,8},{10,11... | collective-permute-start | bytes 221192 | tf_op jit(solution)/shard_map/ppermute | solution.py:326
  2.2 0.9 collective-permute-start.1
  4.3 6.1 %collective-permute-start.2 = (bf16[6,28,384]{2,1,0:T(8,128)(2,1)S(1)}, bf16[6,28,384]{2,1,0:T(8,128)(2,1)S(1)}, u32[]{:S(2)}, u32[]{:S(2)}) collective-permute-start(bf16[6,28,384]{2,1,0:T(8,128)(2,1)S(1)} %get-tuple-element.203), channel_id=1, source_target_pairs={{0,4},{4,0},{8,12},{12,8},{16,20},{20,16},{24,28},{28,24},{1,5},{5... | collective-permute-start | bytes 387080 | tf_op jit(solution)/shard_map/ppermute | solution.py:326
  7.2 3.1 %collective-permute-start.3 = (bf16[6,28,384]{2,1,0:T(8,128)(2,1)S(1)}, bf16[6,28,384]{2,1,0:T(8,128)(2,1)S(1)}, u32[]{:S(2)}, u32[]{:S(2)}) collective-permute-start(bf16[6,28,384]{2,1,0:T(8,128)(2,1)S(1)} %get-tuple-element.204), channel_id=1, source_target_pairs={{4,8},{12,16},{20,24},{8,4},{16,12},{24,20},{5,9},{13,17},{21,25},... | collective-permute-start | bytes 387080 | tf_op jit(solution)/shard_map/ppermute | solution.py:331
  10.6 8.8 %copy-start = (bf16[16,16,384]{2,1,0:T(8,128)(2,1)S(1)}, bf16[16,16,384]{2,1,0:T(8,128)(2,1)}, u32[]{:S(2)}) copy-start(bf16[16,16,384]{2,1,0:T(8,128)(2,1)} %param.9) | copy-start | bytes 589828
  24.3 9.5 %collective-permute-start.4 = (bf16[16,3,384]{2,1,0:T(4,128)(2,1)S(1)}, bf16[16,3,384]{2,1,0:T(4,128)(2,1)S(1)}, u32[]{:S(2)}, u32[]{:S(2)}) collective-permute-start(bf16[16,3,384]{2,1,0:T(4,128)(2,1)S(1)} %get-tuple-element.228), channel_id=1, source_target_pairs={{0,1},{1,0},{2,3},{3,2},{4,5},{5,4},{6,7},{7,6},{8,9},{9,8},{10,11... | collective-permute-start | bytes 110600 | tf_op jit(solution)/shard_map/ppermute | solution.py:326
  28.9 4.9 %collective-permute-start.5 = (bf16[16,3,384]{2,1,0:T(4,128)(2,1)S(1)}, bf16[16,3,384]{2,1,0:T(4,128)(2,1)S(1)}, u32[]{:S(2)}, u32[]{:S(2)}) collective-permute-start(bf16[16,3,384]{2,1,0:T(4,128)(2,1)S(1)} %get-tuple-element.227), channel_id=1, source_target_pairs={{1,2},{2,1},{5,6},{6,5},{9,10},{10,9},{13,14},{14,13},{17,18},{18,... | collective-permute-start | bytes 110600 | tf_op jit(solution)/shard_map/ppermute | solution.py:331
  35.7 10.8 %collective-permute-start.8 = (bf16[2,16,1,48,384]{4,3,1,2,0:T(8,128)(2,1)S(1)}, bf16[2,16,1,48,384]{4,3,1,2,0:T(8,128)(2,1)S(1)}, u32[]{:S(2)}, u32[]{:S(2)}) collective-permute-start(bf16[2,16,1,48,384]{4,3,1,2,0:T(8,128)(2,1)S(1)} %get-tuple-element.189), channel_id=1, source_target_pairs={{0,1},{1,0},{2,3},{3,2},{4,5},{5,4},{6,7},{7,6},{8,9},{9,8},{10,11... | collective-permute-start | bytes 3538952 | tf_op jit(solution)/shard_map/ppermute | solution.py:343
  39.4 7.0 %collective-permute-start.6 = (bf16[3,22,384]{2,1,0:T(8,128)(2,1)S(1)}, bf16[3,22,384]{2,1,0:T(8,128)(2,1)S(1)}, u32[]{:S(2)}, u32[]{:S(2)}) collective-permute-start(bf16[3,22,384]{2,1,0:T(8,128)(2,1)S(1)} %get-tuple-element.220), channel_id=1, source_target_pairs={{0,4},{4,0},{8,12},{12,8},{16,20},{20,16},{24,28},{28,24},{1,5},{5... | collective-permute-start | bytes 152072 | tf_op jit(solution)/shard_map/ppermute | solution.py:326
  44.3 2.1 %collective-permute-start.7 = (bf16[3,22,384]{2,1,0:T(8,128)(2,1)S(1)}, bf16[3,22,384]{2,1,0:T(8,128)(2,1)S(1)}, u32[]{:S(2)}, u32[]{:S(2)}) collective-permute-start(bf16[3,22,384]{2,1,0:T(8,128)(2,1)S(1)} %get-tuple-element.219), channel_id=1, source_target_pairs={{4,8},{12,16},{20,24},{8,4},{16,12},{24,20},{5,9},{13,17},{21,25},... | collective-permute-start | bytes 152072 | tf_op jit(solution)/shard_map/ppermute | solution.py:331
  46.9 12.0 %collective-permute-start.10 = (bf16[1,4,2,48,384]{4,3,2,1,0:T(8,128)(2,1)S(1)}, bf16[1,4,2,48,384]{4,3,2,1,0:T(8,128)(2,1)S(1)}, u32[]{:S(2)}, u32[]{:S(2)}) collective-permute-start(bf16[1,4,2,48,384]{4,3,2,1,0:T(8,128)(2,1)S(1)} %get-tuple-element.199), channel_id=1, source_target_pairs={{0,4},{1,5},{2,6},{3,7},{4,0},{5,1},{6,2},{7,3},{8,12},{9,13},{10,... | collective-permute-start | bytes 884744 | tf_op jit(solution)/shard_map/ppermute | solution.py:343
  52.0 7.6 %collective-permute-start.9 = (bf16[1,8,1,48,384]{4,3,1,2,0:T(8,128)(2,1)S(1)}, bf16[1,8,1,48,384]{4,3,1,2,0:T(8,128)(2,1)S(1)}, u32[]{:S(2)}, u32[]{:S(2)}) collective-permute-start(bf16[1,8,1,48,384]{4,3,1,2,0:T(8,128)(2,1)S(1)} %get-tuple-element.201), channel_id=1, source_target_pairs={{0,2},{1,3},{2,0},{3,1},{4,6},{5,7},{6,4},{7,5},{8,10},{9,11},{10,... | collective-permute-start | bytes 884744 | tf_op jit(solution)/shard_map/ppermute | solution.py:343
  59.8 10.0 %collective-permute-start.11 = (bf16[2,16,1,48,384]{4,3,1,2,0:T(8,128)(2,1)S(1)}, bf16[2,16,1,48,384]{4,3,1,2,0:T(8,128)(2,1)S(1)}, u32[]{:S(2)}, u32[]{:S(2)}) collective-permute-start(bf16[2,16,1,48,384]{4,3,1,2,0:T(8,128)(2,1)S(1)} %get-tuple-element.187), channel_id=1, source_target_pairs={{0,1},{1,0},{2,3},{3,2},{4,5},{5,4},{6,7},{7,6},{8,9},{9,8},{10,11... | collective-permute-start | bytes 3538952 | tf_op jit(solution)/shard_map/ppermute | solution.py:343
  61.8 3.8 %collective-permute-start.14 = (bf16[128,384]{1,0:T(8,128)(2,1)S(1)}, bf16[128,384]{1,0:T(8,128)(2,1)S(1)}, u32[]{:S(2)}, u32[]{:S(2)}) collective-permute-start(bf16[128,384]{1,0:T(8,128)(2,1)S(1)} %pad_maximum_fusion.7), channel_id=1, source_target_pairs={{0,1},{1,0},{2,3},{3,2},{4,5},{5,4},{6,7},{7,6},{8,9},{9,8},{10,11... | collective-permute-start | bytes 294920 | tf_op jit(solution)/shard_map/ppermute | solution.py:343
  62.5 5.8 %collective-permute-start.13 = (bf16[1,4,1,48,384]{4,3,2,1,0:T(8,128)(2,1)S(1)}, bf16[1,4,1,48,384]{4,3,2,1,0:T(8,128)(2,1)S(1)}, u32[]{:S(2)}, u32[]{:S(2)}) collective-permute-start(bf16[1,4,1,48,384]{4,3,2,1,0:T(8,128)(2,1)S(1)} %get-tuple-element.215), channel_id=1, source_target_pairs={{0,2},{1,3},{2,0},{3,1},{4,6},{5,7},{6,4},{7,5},{8,10},{9,11},{10,... | collective-permute-start | bytes 442376 | tf_op jit(solution)/shard_map/ppermute | solution.py:343
  64.2 5.6 %collective-permute-start.12 = (bf16[1,4,1,48,384]{4,3,1,2,0:T(8,128)(2,1)S(1)}, bf16[1,4,1,48,384]{4,3,1,2,0:T(8,128)(2,1)S(1)}, u32[]{:S(2)}, u32[]{:S(2)}) collective-permute-start(bf16[1,4,1,48,384]{4,3,1,2,0:T(8,128)(2,1)S(1)} %get-tuple-element.217), channel_id=1, source_target_pairs={{0,4},{1,5},{2,6},{3,7},{4,0},{5,1},{6,2},{7,3},{8,12},{9,13},{10,... | collective-permute-start | bytes 442376 | tf_op jit(solution)/shard_map/ppermute | solution.py:343
  64.3 1.3 %collective-permute-start.15 = (bf16[16,3,384]{2,1,0:T(4,128)(2,1)S(1)}, bf16[16,3,384]{2,1,0:T(4,128)(2,1)S(1)}, u32[]{:S(2)}, u32[]{:S(2)}) collective-permute-start(bf16[16,3,384]{2,1,0:T(4,128)(2,1)S(1)} %get-tuple-element.226), channel_id=1, source_target_pairs={{0,1},{1,0},{2,3},{3,2},{4,5},{5,4},{6,7},{7,6},{8,9},{9,8},{10,11... | collective-permute-start | bytes 110600 | tf_op jit(solution)/shard_map/ppermute | solution.py:326
  69.9 13.6 %collective-permute-start.18 = (bf16[2,2,1,48,384]{4,3,1,0,2:T(8,128)(2,1)S(1)}, bf16[2,2,1,48,384]{4,3,1,0,2:T(8,128)(2,1)S(1)}, u32[]{:S(2)}, u32[]{:S(2)}) collective-permute-start(bf16[2,2,1,48,384]{4,3,1,0,2:T(8,128)(2,1)S(1)} %get-tuple-element.213), channel_id=1, source_target_pairs={{0,8},{1,9},{2,10},{3,11},{4,12},{5,13},{6,14},{7,15},{8,0},{9,1},... | collective-permute-start | bytes 442376 | tf_op jit(solution)/shard_map/ppermute | solution.py:343
  73.5 10.0 %collective-permute-start.17 = (bf16[1,4,2,48,384]{4,3,2,1,0:T(8,128)(2,1)S(1)}, bf16[1,4,2,48,384]{4,3,2,1,0:T(8,128)(2,1)S(1)}, u32[]{:S(2)}, u32[]{:S(2)}) collective-permute-start(bf16[1,4,2,48,384]{4,3,2,1,0:T(8,128)(2,1)S(1)} %get-tuple-element.195), channel_id=1, source_target_pairs={{0,4},{1,5},{2,6},{3,7},{4,0},{5,1},{6,2},{7,3},{8,12},{9,13},{10,... | collective-permute-start | bytes 884744 | tf_op jit(solution)/shard_map/ppermute | solution.py:343
  74.1 9.4 %collective-permute-start.16 = (bf16[1,8,1,48,384]{4,3,1,2,0:T(8,128)(2,1)S(1)}, bf16[1,8,1,48,384]{4,3,1,2,0:T(8,128)(2,1)S(1)}, u32[]{:S(2)}, u32[]{:S(2)}) collective-permute-start(bf16[1,8,1,48,384]{4,3,1,2,0:T(8,128)(2,1)S(1)} %get-tuple-element.197), channel_id=1, source_target_pairs={{0,2},{1,3},{2,0},{3,1},{4,6},{5,7},{6,4},{7,5},{8,10},{9,11},{10,... | collective-permute-start | bytes 884744 | tf_op jit(solution)/shard_map/ppermute | solution.py:343
  74.5 9.0 %collective-permute-start.20 = (bf16[128,384]{1,0:T(8,128)(2,1)S(1)}, bf16[128,384]{1,0:T(8,128)(2,1)S(1)}, u32[]{:S(2)}, u32[]{:S(2)}) collective-permute-start(bf16[128,384]{1,0:T(8,128)(2,1)S(1)} %add_convert_fusion.16), channel_id=1, source_target_pairs={{0,2},{1,3},{2,0},{3,1},{4,6},{5,7},{6,4},{7,5},{8,10},{9,11},{10,... | collective-permute-start | bytes 294920 | tf_op jit(solution)/shard_map/ppermute | solution.py:343
  76.3 0.7 collective-permute-start.19
  83.5 10.2 %collective-permute-start.25 = (bf16[128,384]{1,0:T(8,128)(2,1)S(1)}, bf16[128,384]{1,0:T(8,128)(2,1)S(1)}, u32[]{:S(2)}, u32[]{:S(2)}) collective-permute-start(bf16[128,384]{1,0:T(8,128)(2,1)S(1)} %add_convert_fusion.15), channel_id=1, source_target_pairs={{0,4},{1,5},{2,6},{3,7},{4,0},{5,1},{6,2},{7,3},{8,12},{9,13},{10,... | collective-permute-start | bytes 294920 | tf_op jit(solution)/shard_map/ppermute | solution.py:343
  85.2 8.5 %collective-permute-start.23 = (bf16[2,1,1,48,384]{4,3,1,0,2:T(8,128)(2,1)S(1)}, bf16[2,1,1,48,384]{4,3,1,0,2:T(8,128)(2,1)S(1)}, u32[]{:S(2)}, u32[]{:S(2)}) collective-permute-start(bf16[2,1,1,48,384]{4,3,1,0,2:T(8,128)(2,1)S(1)} %get-tuple-element.237), channel_id=1, source_target_pairs={{0,16},{1,17},{2,18},{3,19},{4,20},{5,21},{6,22},{7,23},{8,24},{9,... | collective-permute-start | bytes 221192 | tf_op jit(solution)/shard_map/ppermute | solution.py:343
  86.7 7.1 %collective-permute-start.22 = (bf16[1,4,1,48,384]{4,3,2,1,0:T(8,128)(2,1)S(1)}, bf16[1,4,1,48,384]{4,3,2,1,0:T(8,128)(2,1)S(1)}, u32[]{:S(2)}, u32[]{:S(2)}) collective-permute-start(bf16[1,4,1,48,384]{4,3,2,1,0:T(8,128)(2,1)S(1)} %get-tuple-element.209), channel_id=1, source_target_pairs={{0,2},{1,3},{2,0},{3,1},{4,6},{5,7},{6,4},{7,5},{8,10},{9,11},{10,... | collective-permute-start | bytes 442376 | tf_op jit(solution)/shard_map/ppermute | solution.py:343
  87.8 6.0 %collective-permute-start.21 = (bf16[1,4,1,48,384]{4,3,1,2,0:T(8,128)(2,1)S(1)}, bf16[1,4,1,48,384]{4,3,1,2,0:T(8,128)(2,1)S(1)}, u32[]{:S(2)}, u32[]{:S(2)}) collective-permute-start(bf16[1,4,1,48,384]{4,3,1,2,0:T(8,128)(2,1)S(1)} %get-tuple-element.211), channel_id=1, source_target_pairs={{0,4},{1,5},{2,6},{3,7},{4,0},{5,1},{6,2},{7,3},{8,12},{9,13},{10,... | collective-permute-start | bytes 442376 | tf_op jit(solution)/shard_map/ppermute | solution.py:343
  89.5 4.2 %collective-permute-start.24 = (bf16[3,22,384]{2,1,0:T(8,128)(2,1)S(1)}, bf16[3,22,384]{2,1,0:T(8,128)(2,1)S(1)}, u32[]{:S(2)}, u32[]{:S(2)}) collective-permute-start(bf16[3,22,384]{2,1,0:T(8,128)(2,1)S(1)} %get-tuple-element.208), channel_id=1, source_target_pairs={{0,4},{4,0},{8,12},{12,8},{16,20},{20,16},{24,28},{28,24},{1,5},{5... | collective-permute-start | bytes 152072 | tf_op jit(solution)/shard_map/ppermute | solution.py:326
  93.8 4.9 %collective-permute-start.27 = (bf16[128,384]{1,0:T(8,128)(2,1)S(1)}, bf16[128,384]{1,0:T(8,128)(2,1)S(1)}, u32[]{:S(2)}, u32[]{:S(2)}) collective-permute-start(bf16[128,384]{1,0:T(8,128)(2,1)S(1)} %add_convert_fusion.14), channel_id=1, source_target_pairs={{0,8},{1,9},{2,10},{3,11},{4,12},{5,13},{6,14},{7,15},{8,0},{9,1},... | collective-permute-start | bytes 294920 | tf_op jit(solution)/shard_map/ppermute | solution.py:343
  95.7 5.2 %collective-permute-start.26 = (bf16[2,2,1,48,384]{4,3,0,2,1:T(8,128)(2,1)S(1)}, bf16[2,2,1,48,384]{4,3,0,2,1:T(8,128)(2,1)S(1)}, u32[]{:S(2)}, u32[]{:S(2)}) collective-permute-start(bf16[2,2,1,48,384]{4,3,0,2,1:T(8,128)(2,1)S(1)} %copy.30), channel_id=1, source_target_pairs={{0,8},{1,9},{2,10},{3,11},{4,12},{5,13},{6,14},{7,15},{8,0},{9,1},... | collective-permute-start | bytes 442376 | tf_op jit(solution)/shard_map/ppermute | solution.py:343
  96.2 0.7 collective-permute-start.28
  101.0 7.2 %collective-permute-start.30 = (bf16[2,1,1,48,384]{4,3,0,2,1:T(8,128)(2,1)S(1)}, bf16[2,1,1,48,384]{4,3,0,2,1:T(8,128)(2,1)S(1)}, u32[]{:S(2)}, u32[]{:S(2)}) collective-permute-start(bf16[2,1,1,48,384]{4,3,0,2,1:T(8,128)(2,1)S(1)} %constant_dynamic-slice_fusion), channel_id=1, source_target_pairs={{0,16},{1,17},{2,18},{3,19},{4,20},{5,21},{6,22},{7,23},{8,24},{9,... | collective-permute-start | bytes 221192 | tf_op jit(solution)/shard_map/ppermute | solution.py:343
  104.8 6.9 %collective-permute-start.29 = (bf16[128,384]{1,0:T(8,128)(2,1)S(1)}, bf16[128,384]{1,0:T(8,128)(2,1)S(1)}, u32[]{:S(2)}, u32[]{:S(2)}) collective-permute-start(bf16[128,384]{1,0:T(8,128)(2,1)S(1)} %add_convert_fusion.13), channel_id=1, source_target_pairs={{0,16},{1,17},{2,18},{3,19},{4,20},{5,21},{6,22},{7,23},{8,24},{9,... | collective-permute-start | bytes 294920 | tf_op jit(solution)/shard_map/ppermute | solution.py:343
  (5 other events, 27.2 us)

commit v7 on v6

--- a/solution.py
+++ b/solution.py
@@ -143,7 +143,7 @@
     return [slice(start, start + size) for start in range(0, hidden, size)]
 
 
-def mlp_grads(normed, grad, w_in, b_in, w_out, act, gpre, dw, db):
+def mlp_grads(normed, grad, w_in, b_in, w_out, act, gpre, db):
     pixels = grad.shape[0]
     for cut in hidden_chunks(w_in.shape[2]):
         bias = b_in[:, cut]
@@ -157,13 +157,23 @@
             part = jnp.sum(gradient, axis=0, keepdims=True)
             bias_sum = part if bias_sum is None else bias_sum + part
         db[:, cut] = bias_sum
-        if dw is not None:
-            weight_grads(normed, grad, act, gpre, dw, cut)
-
-
-def weight_grads(normed, grad, act, gpre, dw, cut):
-    dw[1, cut, :] = dot_tn(act[:, cut], grad[...]).astype(BF16)
-    dw[0, cut, :] = dot_tn(gpre[:, cut], normed[...]).astype(BF16)
+
+
+def weight_grads(place, normed, grad, act, gpre, dw, per):
+    hidden, channels = act.shape[1], grad.shape[1]
+    size = min(n for n in range(128, hidden + 1, 128) if hidden % n == 0 and n % (2 * per) == 0 and n >= 256)
+    for first in range(0, hidden, size):
+        cut = slice(first, first + size)
+        for i, (left, right) in enumerate(((gpre, normed), (act, grad))):
+            value = dot_tn(left[:, cut], right[...]).astype(BF16)
+            if len(dw) == 1:
+                dw[0][i, cut, :] = value
+                continue
+            value = value.reshape(size // (2 * per), 2, per, channels)
+            upper = place[4] == 1
+            half = slice(first // 2, (first + size) // 2)
+            dw[0][i, half, :] = jnp.where(upper, value[:, 0], value[:, 1]).reshape(-1, channels)
+            dw[1][i, half, :] = jnp.where(upper, value[:, 1], value[:, 0]).reshape(-1, channels)
 
 
 def fetch_layers(triples, arrived):
@@ -177,7 +187,7 @@
 
 
 def block_back(z, grad, layer, gains, shifts, weights, b_in, outs, scratch):
-    dz_out, dw, db, dgain, dshift = outs
+    dz_out, db, dgain, dshift = outs
     normed, act, gpre = scratch
     gain = gains[layer : layer + 1]
     hat, inv = norm_parts(joined(z, slice(None)))
@@ -185,7 +195,7 @@
     w_in, w_out, waits = weights
     for wait in waits:
         wait.wait()
-    mlp_grads(normed, grad, w_in, b_in.at[layer], w_out, act, gpre, dw, db)
+    mlp_grads(normed, grad, w_in, b_in.at[layer], w_out, act, gpre, db)
     dn = dot_nt(gpre[...], w_in[0])
     dgain[...] = jnp.sum(dn * hat, axis=0, keepdims=True)
     dshift[...] = jnp.sum(dn, axis=0, keepdims=True)
@@ -235,22 +245,23 @@
     conv_pass(mids, 0, 0, taps.at[1], z, *z.shape[1:3])
     block_back(
         z, grad, 1, gains, shifts, (w_in1, w_out1, waits), b_in,
-        (dz_out, None, db, dgain, dshift), (normed, act, gpre),
+        (dz_out, db, dgain, dshift), (normed, act, gpre),
     )
 
 
 def low_kernel(
-    dzpad, grad, z0, taps, gains, shifts, w_in, w_out, b_in,
-    gmid, dz_out, dw, db, dgain, dshift,
-    dzs, spread, normed, act, gpre, w_in0, w_out0, arrived,
+    per, place, dzpad, grad, z0, taps, gains, shifts, w_in, w_out, b_in,
+    gmid, dz_out, db, dgain, dshift, *rest,
 ):
+    *dw, dzs, spread, normed, act, gpre, w_in0, w_out0, arrived = rest
     waits = fetch_layers(((w_in, 0, w_in0), (w_out, 0, w_out0)), arrived)
     spread_pass(dzpad, dzs, taps.at[1], spread)
     gmid[...] = (grad[...].astype(F32) + joined(spread, slice(None))).astype(BF16)
     block_back(
         z0, gmid, 0, gains, shifts, (w_in0, w_out0, waits), b_in,
-        (dz_out, dw, db, dgain, dshift), (normed, act, gpre),
-    )
+        (dz_out, db, dgain, dshift), (normed, act, gpre),
+    )
+    weight_grads(place, normed, gmid, act, gpre, dw, per)
 
 
 def spread_pass(dzpad, dzs, taps, spread):
@@ -284,9 +295,9 @@
     out[...] = sums[...].astype(BF16)
 
 
-def top_taps_kernel(source, dz, normed, act, gpre, grad, db, dgain, dshift, dw, out, dzs, sums):
-    for cut in hidden_chunks(act.shape[1]):
-        weight_grads(normed, grad, act, gpre, dw, cut)
+def top_taps_kernel(per, place, source, dz, normed, act, gpre, grad, db, dgain, dshift, out, *rest):
+    *dw, dzs, sums = rest
+    weight_grads(place, normed, grad, act, gpre, dw, per)
     taps_kernel(source, 0, 0, dz, db, dgain, dshift, out, None, dzs, sums)
 
 
@@ -327,11 +338,23 @@
 
 
 def to_other(edge, axis):
-    pairs = [(i, i + 1) for i in range(1, lax.axis_size(axis) - 1, 2)]
-    return lax.ppermute(edge, axis, pairs + [(j, i) for i, j in pairs])
-
-
-def rimmed(tile, from_twin, from_other, axis, odd):
+    n_rows, n_cols = lax.axis_size("rows"), lax.axis_size("cols")
+    count = lax.axis_size(axis)
+    pairs = []
+    for r in range(n_rows):
+        for c in range(n_cols):
+            at = r if axis == "rows" else c
+            partner = at + 1 if at % 2 else at - 1
+            if 0 <= partner < count:
+                there = (partner, c) if axis == "rows" else (r, partner)
+            else:
+                there = (r, c ^ 1) if axis == "rows" else (r ^ 1, c)
+            pairs.append((r * n_cols + c, there[0] * n_cols + there[1]))
+    return lax.ppermute(edge, ("rows", "cols"), pairs)
+
+
+def rimmed(tile, from_twin, from_other, axis, odd, outer):
+    from_other = jnp.where(outer, jnp.zeros_like(from_other), from_other)
     low = jnp.where(odd, from_twin, from_other)
     high = jnp.where(odd, from_other, from_twin)
     return jnp.concatenate([low, tile, high], axis=axis)
@@ -386,20 +409,23 @@
             lax.axis_index("cols") * cols,
             jnp.int32(rows * n_rows),
             jnp.int32(cols * n_cols),
+            lax.axis_index("cols") & 1,
         ]
     ).astype(jnp.int32)
     grad_flat = grad_out.reshape(pixels, channels)
 
-    odd_col = (lax.axis_index("cols") & 1) == 1
-    odd_row = (lax.axis_index("rows") & 1) == 1
+    at_row, at_col = lax.axis_index("rows"), lax.axis_index("cols")
+    odd_col, odd_row = (at_col & 1) == 1, (at_row & 1) == 1
+    outer_col = (at_col == 0) | (at_col == n_cols - 1)
+    outer_row = (at_row == 0) | (at_row == n_rows - 1)
 
     def rim_cols(tile, width):
         twin, other = edges(tile, 1, width, odd_col)
-        return rimmed(tile, to_twin(twin, "cols"), to_other(other, "cols"), 1, odd_col)
+        return rimmed(tile, to_twin(twin, "cols"), to_other(other, "cols"), 1, odd_col, outer_col)
 
     def rim_rows(tile, width):
         twin, other = edges(tile, 0, width, odd_row)
-        return rimmed(tile, to_twin(twin, "rows"), to_other(other, "rows"), 0, odd_row)
+        return rimmed(tile, to_twin(twin, "rows"), to_other(other, "rows"), 0, odd_row, outer_row)
 
     def filled(wide):
         return jnp.pad(wide, ((0, 0), (0, cols + 16 - wide.shape[1]), (0, 0)))
@@ -410,12 +436,16 @@
     tile_z = shape(groups, rows, cols, LANES)
     tile_b = shape(pixels, channels, dtype=BF16)
     tile_h = shape(pixels, hidden, dtype=BF16)
-    grads_b = shape(2, hidden, channels, dtype=BF16)
+    per = hidden // total
+    split = 2 if per % 16 == 0 and col_bits == 2 else 1
+    grads_b = (shape(2, hidden // split, channels, dtype=BF16),) * split
     small_outs = (shape(1, hidden), shape(1, channels), shape(1, channels))
     small_rows = 64
 
     xpad = filled(rim_rows(rim_cols(activations, WIDE), WIDE))
-    xpad, place, mine, odd_col, odd_row = lax.optimization_barrier((xpad, place, mine, odd_col, odd_row))
+    xpad, place, mine, odd_col, odd_row, outer_col, outer_row = lax.optimization_barrier(
+        (xpad, place, mine, odd_col, odd_row, outer_col, outer_row)
+    )
     mids, z0 = run(
         forward_kernel,
         (shape(groups, mid_rows, mid_cols, LANES), tile_z),
@@ -440,7 +470,6 @@
         name="top",
     )
 
-    per = hidden // total
     sides = (col_bits - 1, col_bits)
 
     def fenced(*values):
@@ -454,7 +483,11 @@
         return summed(flight[0], flight[1]), flight[2]
 
     def start(dw):
-        chunks, order = dw.reshape(2, total, per, channels), list(range(bits - 1, -1, -1))
+        order = list(range(bits - 1, -1, -1))
+        if split == 2:
+            send, keep = (d.reshape(2, total // 2, per, channels) for d in dw)
+            return keep, flip_bit(send, 0), order[:-1]
+        chunks = dw[0].reshape(2, total, per, channels)
         for bit in range(col_bits - 2):
             chunks, order = settled(step(chunks, order, bit, mine))
         return step(chunks, order, col_bits - 2, mine)
@@ -483,37 +516,36 @@
     tile1 = dz1.reshape(rows, cols, channels)
     twin, other = edges(tile1, 1, HALO, odd_col)
     twin, other = to_twin(twin, "cols"), to_other(other, "cols")
-    dw1, small1 = run(
-        top_taps_kernel,
-        (grads_b, shape(small_rows, channels, dtype=BF16)),
+    small1, *dw1 = run(
+        functools.partial(top_taps_kernel, per),
+        (shape(small_rows, channels, dtype=BF16),) + grads_b,
         [tile_z, shape(small_rows, channels)],
-        (mids, dz1, normed1, act1, gpre1, grad_flat, *small1),
+        (place, mids, dz1, normed1, act1, gpre1, grad_flat, *small1),
+        [pltpu.SMEM] + [None] * 9,
         name="top_taps",
     )
     tile1, twin, other, dw1, small1 = fenced(tile1, twin, other, dw1, small1)
-    wide1 = rimmed(tile1, twin, other, 1, odd_col)
+    wide1 = rimmed(tile1, twin, other, 1, odd_col, outer_col)
     run1 = start(dw1)
     twin, other = edges(wide1, 0, HALO, odd_row)
     twin, other = to_twin(twin, "rows"), to_other(other, "rows")
     wide1, twin, other, run1 = fenced(wide1, twin, other, run1)
     pair1 = fork(run1)
-    dzpad1 = filled(rimmed(wide1, twin, other, 0, odd_row))
+    dzpad1 = filled(rimmed(wide1, twin, other, 0, odd_row, outer_row))
     spread_scratch = [shape(groups, *dzpad1.shape[:2], LANES), tile_z]
-    grad_mid, dz0, dw0, *small0 = run(
-        low_kernel,
-        (tile_b, tile_b, grads_b) + small_outs,
+    grad_mid, dz0, *rest = run(
+        functools.partial(low_kernel, per),
+        (tile_b, tile_b) + small_outs + grads_b,
         spread_scratch + [tile_b, tile_h, tile_h] + weights,
-        (dzpad1, grad_flat, z0, taps, norm_gains, norm_shifts, w_in, w_out, biases),
-        [None] * 6 + [pl.ANY] * 2 + [None],
+        (place, dzpad1, grad_flat, z0, taps, norm_gains, norm_shifts, w_in, w_out, biases),
+        [pltpu.SMEM] + [None] * 6 + [pl.ANY] * 2 + [None],
         fetched=2,
         name="low",
     )
+    small0, dw0 = rest[:3], rest[3:]
     dz0, dw0, pair1, *small0 = fenced(dz0, dw0, pair1, *small0)
     run0 = start(dw0)
     pair1 = cross(pair1)
-    tile0 = dz0.reshape(rows, cols, channels)
-    twin, other = edges(tile0, 1, HALO, odd_col)
-    twin = to_twin(twin, "cols")
     (small0,) = run(
         low_taps_kernel,
         (shape(small_rows, channels, dtype=BF16),),
@@ -523,20 +555,19 @@
     )
     small = jnp.concatenate([small0, small1], axis=0)
     small_got = flip_bit(small, 0)
-    run0, pair1, small, small_got, tile0, twin, other = fenced(
-        run0, pair1, small, small_got, tile0, twin, other
-    )
+    run0, small, small_got, dz0 = fenced(run0, small, small_got, dz0)
     pair0 = fork(run0)
-    run1 = onward(*merge(pair1))
-    other = to_other(other, "cols")
+    tile0 = dz0.reshape(rows, cols, channels)
+    twin, other = edges(tile0, 1, HALO, odd_col)
+    twin, other = to_twin(twin, "cols"), to_other(other, "cols")
     small = summed(small, small_got)
     small_got = flip_bit(small, 1)
-    pair0, run1, tile0, twin, other, small, small_got = fenced(
-        pair0, run1, tile0, twin, other, small, small_got
+    pair0, pair1, tile0, twin, other, small, small_got = fenced(
+        pair0, pair1, tile0, twin, other, small, small_got
     )
     pair0 = cross(pair0)
-    run1 = onward(*settled(run1))
-    wide0 = rimmed(tile0, twin, other, 1, odd_col)
+    run1 = onward(*merge(pair1))
+    wide0 = rimmed(tile0, twin, other, 1, odd_col, outer_col)
     twin, other = edges(wide0, 0, HALO, odd_row)
     twin = to_twin(twin, "rows")
     small = summed(small, small_got)
@@ -545,24 +576,24 @@
         pair0, run1, wide0, twin, other, small, small_got
     )
     run0 = onward(*merge(pair0))
+    run1 = onward(*settled(run1))
     other = to_other(other, "rows")
-    share1 = finish(run1)
     wait = (wide0, twin, other)
     for bit in range(3, bits):
         small = summed(small, small_got)
         small_got = flip_bit(small, bit)
         if run0[2]:
-            run0, small, small_got, wait = fenced(run0, small, small_got, wait)
+            run0, run1, small, small_got, wait = fenced(run0, run1, small, small_got, wait)
             run0 = onward(*settled(run0))
         if bit == 3:
             (wait,) = run(
                 last_kernel,
                 (tile_b,),
                 spread_scratch,
-                (filled(rimmed(*wait, 0, odd_row)), grad_mid, taps),
+                (filled(rimmed(*wait, 0, odd_row, outer_row)), grad_mid, taps),
                 name="last",
             )
-    grad_in = wait
+    grad_in, share1 = wait, finish(run1)
     small = summed(small, small_got)
     shares = [finish(run0), share1]
     small = small.reshape(layers, small_rows, channels).astype(F32) * grad_scale

time: 114 us -> 108 us (0.947)
  starting transfers between devices: 45.9 us -> 38.3 us
  waiting for transfers between devices: 27.1 us -> 29 us
  other arithmetic: 5.33 us -> 7.03 us
  local copies, waits for them, and re-layouts: 5.04 us -> 3.72 us
    ppermute x6, waiting for transfers between devices: 0.02 us -> 7.96 us  [to_other(): return lax.ppermute(edge, ('rows', 'cols'), pairs)]
    ppermute x19, waiting for transfers between devices: 18.7 us -> 10.8 us  [flip_bit(): return lax.ppermute(value, both, [(i, i ^ 1 << bit) for i in range(total)])]
    ppermute x19, starting transfers between devices: 28.1 us -> 23 us  [flip_bit(): return lax.ppermute(value, both, [(i, i ^ 1 << bit) for i in range(total)])]
    ppermute x6, starting transfers between devices: 13.7 us -> 9.12 us  [to_twin(): lax.ppermute(edge, axis, [(i, i ^ 1) for i in range(count) if i ^ 1 < cou...]
    squeeze x13 -> x9, local copies, waits for them, and re-layouts: 2.58 us -> 0.34 us  [one(): return lax.squeeze(lax.dynamic_slice(chunks, starts, sizes), (dim,))]
    ppermute x6, starting transfers between devices: 4.1 us -> 6.12 us  [to_other(): return lax.ppermute(edge, ('rows', 'cols'), pairs)]
    ppermute x6, waiting for transfers between devices: 8.44 us -> 10.2 us  [to_twin(): lax.ppermute(edge, axis, [(i, i ^ 1) for i in range(count) if i ^ 1 < cou...]
    unnamed x14 -> x20, local copies, waits for them, and re-layouts: 0.64 us -> 1.93 us
  transfers between devices with their start and end apart: 31 -> 31, of which waited for: 13 -> 12; matrix products, arithmetic and copies ran while one was open for 3% -> 3% of each run, Pallas kernels for 14% -> 14%
where the time goes in v7:
time: 108 us
  starting transfers between devices  38.3 us (35%)
  waiting for transfers between devices  29 us (27%)
  Pallas kernels  28.6 us (26%)
  other arithmetic  7.03 us (7%)
  local copies, waits for them, and re-layouts  3.72 us (3%)
  between operations  1.18 us (1%)
    pallas_call x6, Pallas kernels, run(): pl.pallas_call(kernel, out_shape=outs, in_specs=[vmem if s is None else p...  28.6 us
    ppermute x19, starting transfers between devices, flip_bit(): return lax.ppermute(value, both, [(i, i ^ 1 << bit) for i in range(total)])  23 us
    ppermute x19, waiting for transfers between devices, flip_bit(): return lax.ppermute(value, both, [(i, i ^ 1 << bit) for i in range(total)])  10.8 us
    ppermute x6, waiting for transfers between devices, to_twin(): lax.ppermute(edge, axis, [(i, i ^ 1) for i in range(count) if i ^ 1 < cou...  10.2 us
    ppermute x6, starting transfers between devices, to_twin(): lax.ppermute(edge, axis, [(i, i ^ 1) for i in range(count) if i ^ 1 < cou...  9.12 us
    ppermute x6, waiting for transfers between devices, to_other(): return lax.ppermute(edge, ('rows', 'cols'), pairs)  7.96 us
    ppermute x6, starting transfers between devices, to_other(): return lax.ppermute(edge, ('rows', 'cols'), pairs)  6.12 us
    convert_element_type x15, other arithmetic, summed(): return (own.astype(F32) + got.astype(F32)).astype(BF16)  2.48 us
  transfers between devices with their start and end apart: 31, of which 12 were waited for; matrix products, arithmetic and copies ran while one was open for 3% of the time, Pallas kernels for 14%

profile of v7, /device:TPU:0, one launch (start us, length us, event | category | flops | bytes accessed | tf_op | source)
XLA Modules:
  0.0 107.8 jit_solution(13555895373352142639)
XLA Ops:
  1.7 3.0 %collective-permute-start.1 = (bf16[16,6,384]{2,1,0:T(8,128)(2,1)S(1)}, bf16[16,6,384]{2,1,0:T(8,128)(2,1)S(1)}, u32[]{:S(2)}, u32[]{:S(2)}) collective-permute-start(bf16[16,6,384]{2,1,0:T(8,128)(2,1)S(1)} %get-tuple-element.231), channel_id=1, source_target_pairs={{0,4},{1,2},{2,1},{3,7},{4,0},{5,6},{6,5},{7,3},{8,12},{9,10},{10,... | collective-permute-start | bytes 221192 | tf_op jit(solution)/shard_map/ppermute | solution.py:353
  4.8 2.5 %collective-permute-done.1 = bf16[16,6,384]{2,1,0:T(8,128)(2,1)S(1)} collective-permute-done((bf16[16,6,384]{2,1,0:T(8,128)(2,1)S(1)}, bf16[16,6,384]{2,1,0:T(8,128)(2,1)S(1)}, u32[]{:S(2)}, u32[]{:S(2)}) %collective-permute-start.1) | collective-permute-done | bytes 73760 | tf_op jit(solution)/shard_map/ppermute | solution.py:353
  8.6 3.5 %collective-permute-start.2 = (bf16[6,28,384]{2,1,0:T(8,128)(2,1)S(1)}, bf16[6,28,384]{2,1,0:T(8,128)(2,1)S(1)}, u32[]{:S(2)}, u32[]{:S(2)}) collective-permute-start(bf16[6,28,384]{2,1,0:T(8,128)(2,1)S(1)} %get-tuple-element.204), channel_id=1, source_target_pairs={{0,4},{4,0},{8,12},{12,8},{16,20},{20,16},{24,28},{28,24},{1,5},{5... | collective-permute-start | bytes 387080 | tf_op jit(solution)/shard_map/ppermute | solution.py:337
  12.4 5.0 %collective-permute-done.2 = bf16[6,28,384]{2,1,0:T(8,128)(2,1)S(1)} collective-permute-done((bf16[6,28,384]{2,1,0:T(8,128)(2,1)S(1)}, bf16[6,28,384]{2,1,0:T(8,128)(2,1)S(1)}, u32[]{:S(2)}, u32[]{:S(2)}) %collective-permute-start.2) | collective-permute-done | bytes 129056 | tf_op jit(solution)/shard_map/ppermute | solution.py:337
  17.7 8.6 %forward.1 = (f32[3,22,24,128]{3,2,1,0:T(8,128)S(1)}, f32[3,16,16,128]{3,2,1,0:T(8,128)S(1)}) custom-call(s32[5]{0:T(128)S(1)} %stack.35.place, bf16[28,32,384]{2,1,0:T(8,128)(2,1)S(1)} %fusion.12.xpad.source, f32[2,3,49,128]{3,2,1,0:T(8,128)S(1)} %bitcast.93, f32[2,384]{1,0:T(2,128)S(1)} %copy-done.1, f32[2,384]{1,0:T(2,128)S(1)} %copy-done.2, ...), custom_call_target="tpu_custom_call" | custom-call | tf_op jit(solution)/shard_map/forward/pallas_call | solution.py:315
  26.4 4.7 %top.1 = (bf16[256,384]{1,0:T(8,128)(2,1)S(1)}, bf16[256,384]{1,0:T(8,128)(2,1)S(1)}, bf16[256,1536]{1,0:T(8,128)(2,1)S(1)}, bf16[256,1536]{1,0:T(8,128)(2,1)S(1...) custom-call(f32[3,22,24,128]{3,2,1,0:T(8,128)S(1)} %get-tuple-element.103.mids.source, ...), custom_call_target="tpu_custom_call" | custom-call | tf_op jit(solution)/shard_map/top/pallas_call | solution.py:315
  31.2 2.6 %collective-permute-start.5 = (bf16[16,3,384]{2,1,0:T(4,128)(2,1)S(1)}, bf16[16,3,384]{2,1,0:T(4,128)(2,1)S(1)}, u32[]{:S(2)}, u32[]{:S(2)}) collective-permute-start(bf16[16,3,384]{2,1,0:T(4,128)(2,1)S(1)} %get-tuple-element.227), channel_id=1, source_target_pairs={{0,4},{1,2},{2,1},{3,7},{4,0},{5,6},{6,5},{7,3},{8,12},{9,10},{10,... | collective-permute-start | bytes 110600 | tf_op jit(solution)/shard_map/ppermute | solution.py:353
  33.7 4.7 %top_taps.1 = (bf16[64,384]{1,0:T(8,128)(2,1)S(1)}, bf16[2,768,384]{2,1,0:T(8,128)(2,1)}, bf16[2,768,384]{2,1,0:T(8,128)(2,1)}) custom-call(s32[5]{0:T(128)S(1)} %stack.35.place, f32[3,22,24,128]{3,2,1,0:T(8,128)S(1)} %get-tuple-element.103.mids.source, bf16[256,384]{1,0:T(8,128)(2,1)S(1)} %get-tuple-element.104.dz, ...), custom_call_target="tpu_custom_call" | custom-call | tf_op jit(solution)/shard_map/top_taps/pallas_call | solution.py:315
  39.3 3.0 %collective-permute-start.6 = (bf16[3,22,384]{2,1,0:T(8,128)(2,1)S(1)}, bf16[3,22,384]{2,1,0:T(8,128)(2,1)S(1)}, u32[]{:S(2)}, u32[]{:S(2)}) collective-permute-start(bf16[3,22,384]{2,1,0:T(8,128)(2,1)S(1)} %get-tuple-element.220), channel_id=1, source_target_pairs={{0,4},{4,0},{8,12},{12,8},{16,20},{20,16},{24,28},{28,24},{1,5},{5... | collective-permute-start | bytes 152072 | tf_op jit(solution)/shard_map/ppermute | solution.py:337
  42.3 2.1 %collective-permute-done.6 = bf16[3,22,384]{2,1,0:T(8,128)(2,1)S(1)} collective-permute-done((bf16[3,22,384]{2,1,0:T(8,128)(2,1)S(1)}, bf16[3,22,384]{2,1,0:T(8,128)(2,1)S(1)}, u32[]{:S(2)}, u32[]{:S(2)}) %collective-permute-start.6) | collective-permute-done | bytes 50720 | tf_op jit(solution)/shard_map/ppermute | solution.py:337
  44.4 1.6 %add_convert_fusion.1 = bf16[2,16,48,384]{3,2,1,0:T(8,128)(2,1)S(1)} fusion(bf16[2,16,48,384]{3,2,1,0:T(8,128)(2,1)S(1)} %collective-permute-done.8, bf16[2,16,48,384]{3,2,1,0:T(8,128)(2,1)} %bitcast.110), kind=kLoop, calls=%fused_computation.1 | loop fusion | flops 2359296 | bytes 3538944 | tf_op jit(solution)/shard_map/convert_element_type | solution.py:380
  46.3 2.1 %collective-permute-start.10 = (bf16[1,4,2,48,384]{4,3,1,2,0:T(8,128)(2,1)S(1)}, bf16[1,4,2,48,384]{4,3,1,2,0:T(8,128)(2,1)S(1)}, u32[]{:S(2)}, u32[]{:S(2)}) collective-permute-start(bf16[1,4,2,48,384]{4,3,1,2,0:T(8,128)(2,1)S(1)} %bitcast.123), channel_id=1, source_target_pairs={{0,4},{1,5},{2,6},{3,7},{4,0},{5,1},{6,2},{7,3},{8,12},{9,13},{10,... | collective-permute-start | bytes 884744 | tf_op jit(solution)/shard_map/ppermute | solution.py:366
  49.2 6.1 %low.1 = (bf16[256,384]{1,0:T(8,128)(2,1)S(1)}, bf16[256,384]{1,0:T(8,128)(2,1)S(1)}, f32[1,1536]{1,0:T(1,128)S(1)}, f32[1,384]{1,0:T(1,128)S(1)}, f32[1,384]{1,...) custom-call(s32[5]{0:T(128)S(1)} %stack.35.place, ...), custom_call_target="tpu_custom_call" | custom-call | tf_op jit(solution)/shard_map/low/pallas_call | solution.py:315
  56.0 1.9 %low_taps.1 = bf16[64,384]{1,0:T(8,128)(2,1)S(1)} custom-call(bf16[28,32,384]{2,1,0:T(8,128)(2,1)S(1)} %fusion.12.xpad.source, bf16[256,384]{1,0:T(8,128)(2,1)S(1)} %get-tuple-element.150.dz, f32[1,1536]{1,0:T(1,128)S(1)} %get-tuple-element.140.db, f32[1,384]{1,0:T(1,128)S(1)} %get-tuple-element.141.dgain, f32[1,384]{1,0:T(1,128)S(1)} %get-tuple-element.142.dshift), custom_call_target="tpu_custom_call" | custom-call | tf_op jit(solution)/shard_map/low_taps/pallas_call | solution.py:315
  59.2 1.6 %collective-permute-start.16 = (bf16[1,4,1,48,384]{4,3,1,2,0:T(8,128)(2,1)S(1)}, bf16[1,4,1,48,384]{4,3,1,2,0:T(8,128)(2,1)S(1)}, u32[]{:S(2)}, u32[]{:S(2)}) collective-permute-start(bf16[1,4,1,48,384]{4,3,1,2,0:T(8,128)(2,1)S(1)} %get-tuple-element.215), channel_id=1, source_target_pairs={{0,2},{1,3},{2,0},{3,1},{4,6},{5,7},{6,4},{7,5},{8,10},{9,11},{10,... | collective-permute-start | bytes 442376 | tf_op jit(solution)/shard_map/ppermute | solution.py:366
  61.4 1.8 %collective-permute-start.14 = (bf16[1,4,2,48,384]{4,3,1,2,0:T(8,128)(2,1)S(1)}, bf16[1,4,2,48,384]{4,3,1,2,0:T(8,128)(2,1)S(1)}, u32[]{:S(2)}, u32[]{:S(2)}) collective-permute-start(bf16[1,4,2,48,384]{4,3,1,2,0:T(8,128)(2,1)S(1)} %bitcast.122), channel_id=1, source_target_pairs={{0,4},{1,5},{2,6},{3,7},{4,0},{5,1},{6,2},{7,3},{8,12},{9,13},{10,... | collective-permute-start | bytes 884744 | tf_op jit(solution)/shard_map/ppermute | solution.py:366
  63.7 1.6 %collective-permute-start.19 = (bf16[128,384]{1,0:T(8,128)(2,1)S(1)}, bf16[128,384]{1,0:T(8,128)(2,1)S(1)}, u32[]{:S(2)}, u32[]{:S(2)}) collective-permute-start(bf16[128,384]{1,0:T(8,128)(2,1)S(1)} %add_convert_fusion.16), channel_id=1, source_target_pairs={{0,2},{1,3},{2,0},{3,1},{4,6},{5,7},{6,4},{7,5},{8,10},{9,11},{10,... | collective-permute-start | bytes 294920 | tf_op jit(solution)/shard_map/ppermute | solution.py:366
  65.8 1.4 %collective-permute-start.17 = (bf16[16,3,384]{2,1,0:T(4,128)(2,1)S(1)}, bf16[16,3,384]{2,1,0:T(4,128)(2,1)S(1)}, u32[]{:S(2)}, u32[]{:S(2)}) collective-permute-start(bf16[16,3,384]{2,1,0:T(4,128)(2,1)S(1)} %get-tuple-element.226), channel_id=1, source_target_pairs={{0,1},{1,0},{2,3},{3,2},{4,5},{5,4},{6,7},{7,6},{8,9},{9,8},{10,11... | collective-permute-start | bytes 110600 | tf_op jit(solution)/shard_map/ppermute | solution.py:337
  67.2 4.2 %collective-permute-done.18 = bf16[16,3,384]{2,1,0:T(4,128)(2,1)S(1)} collective-permute-done((bf16[16,3,384]{2,1,0:T(4,128)(2,1)S(1)}, bf16[16,3,384]{2,1,0:T(4,128)(2,1)S(1)}, u32[]{:S(2)}, u32[]{:S(2)}) %collective-permute-start.18) | collective-permute-done | bytes 36896 | tf_op jit(solution)/shard_map/ppermute | solution.py:353
  71.4 2.0 %collective-permute-done.19 = bf16[128,384]{1,0:T(8,128)(2,1)S(1)} collective-permute-done((bf16[128,384]{1,0:T(8,128)(2,1)S(1)}, bf16[128,384]{1,0:T(8,128)(2,1)S(1)}, u32[]{:S(2)}, u32[]{:S(2)}) %collective-permute-start.19) | collective-permute-done | bytes 98336 | tf_op jit(solution)/shard_map/ppermute | solution.py:366
  73.6 1.6 %collective-permute-start.24 = (bf16[128,384]{1,0:T(8,128)(2,1)S(1)}, bf16[128,384]{1,0:T(8,128)(2,1)S(1)}, u32[]{:S(2)}, u32[]{:S(2)}) collective-permute-start(bf16[128,384]{1,0:T(8,128)(2,1)S(1)} %add_convert_fusion.15), channel_id=1, source_target_pairs={{0,4},{1,5},{2,6},{3,7},{4,0},{5,1},{6,2},{7,3},{8,12},{9,13},{10,... | collective-permute-start | bytes 294920 | tf_op jit(solution)/shard_map/ppermute | solution.py:366
  75.8 1.9 %collective-permute-start.21 = (bf16[1,4,1,48,384]{4,3,1,2,0:T(8,128)(2,1)S(1)}, bf16[1,4,1,48,384]{4,3,1,2,0:T(8,128)(2,1)S(1)}, u32[]{:S(2)}, u32[]{:S(2)}) collective-permute-start(bf16[1,4,1,48,384]{4,3,1,2,0:T(8,128)(2,1)S(1)} %get-tuple-element.211), channel_id=1, source_target_pairs={{0,2},{1,3},{2,0},{3,1},{4,6},{5,7},{6,4},{7,5},{8,10},{9,11},{10,... | collective-permute-start | bytes 442376 | tf_op jit(solution)/shard_map/ppermute | solution.py:366
  77.8 2.3 %collective-permute-start.22 = (bf16[2,2,1,48,384]{4,3,1,0,2:T(8,128)(2,1)S(1)}, bf16[2,2,1,48,384]{4,3,1,0,2:T(8,128)(2,1)S(1)}, u32[]{:S(2)}, u32[]{:S(2)}) collective-permute-start(bf16[2,2,1,48,384]{4,3,1,0,2:T(8,128)(2,1)S(1)} %get-tuple-element.209), channel_id=1, source_target_pairs={{0,8},{1,9},{2,10},{3,11},{4,12},{5,13},{6,14},{7,15},{8,0},{9,1},... | collective-permute-start | bytes 442376 | tf_op jit(solution)/shard_map/ppermute | solution.py:366
  81.5 3.0 %collective-permute-done.23 = bf16[3,22,384]{2,1,0:T(8,128)(2,1)S(1)} collective-permute-done((bf16[3,22,384]{2,1,0:T(8,128)(2,1)S(1)}, bf16[3,22,384]{2,1,0:T(8,128)(2,1)S(1)}, u32[]{:S(2)}, u32[]{:S(2)}) %collective-permute-start.23) | collective-permute-done | bytes 50720 | tf_op jit(solution)/shard_map/ppermute | solution.py:337
  87.0 1.9 %collective-permute-start.26 = (bf16[2,1,1,48,384]{4,3,1,0,2:T(8,128)(2,1)S(1)}, bf16[2,1,1,48,384]{4,3,1,0,2:T(8,128)(2,1)S(1)}, u32[]{:S(2)}, u32[]{:S(2)}) collective-permute-start(bf16[2,1,1,48,384]{4,3,1,0,2:T(8,128)(2,1)S(1)} %get-tuple-element.237), channel_id=1, source_target_pairs={{0,16},{1,17},{2,18},{3,19},{4,20},{5,21},{6,22},{7,23},{8,24},{9,... | collective-permute-start | bytes 221192 | tf_op jit(solution)/shard_map/ppermute | solution.py:366
  88.9 1.2 %collective-permute-done.28 = bf16[3,22,384]{2,1,0:T(8,128)(2,1)S(1)} collective-permute-done((bf16[3,22,384]{2,1,0:T(8,128)(2,1)S(1)}, bf16[3,22,384]{2,1,0:T(8,128)(2,1)S(1)}, u32[]{:S(2)}, u32[]{:S(2)}) %collective-permute-start.28) | collective-permute-done | bytes 50720 | tf_op jit(solution)/shard_map/ppermute | solution.py:353
  90.1 2.3 %collective-permute-done.26 = bf16[2,1,1,48,384]{4,3,1,0,2:T(8,128)(2,1)S(1)} collective-permute-done((bf16[2,1,1,48,384]{4,3,1,0,2:T(8,128)(2,1)S(1)}, bf16[2,1,1,48,384]{4,3,1,0,2:T(8,128)(2,1)S(1)}, u32[]{:S(2)}, u32[]{:S(2)}) %collective-permute-start.26) | collective-permute-done | bytes 73760 | tf_op jit(solution)/shard_map/ppermute | solution.py:366
  92.4 1.9 %collective-permute-done.25 = bf16[2,2,1,48,384]{4,3,0,2,1:T(8,128)(2,1)S(1)} collective-permute-done((bf16[2,2,1,48,384]{4,3,0,2,1:T(8,128)(2,1)S(1)}, bf16[2,2,1,48,384]{4,3,0,2,1:T(8,128)(2,1)S(1)}, u32[]{:S(2)}, u32[]{:S(2)}) %collective-permute-start.25) | collective-permute-done | bytes 147488 | tf_op jit(solution)/shard_map/ppermute | solution.py:366
  94.3 1.5 %collective-permute-start.29 = (bf16[128,384]{1,0:T(8,128)(2,1)S(1)}, bf16[128,384]{1,0:T(8,128)(2,1)S(1)}, u32[]{:S(2)}, u32[]{:S(2)}) collective-permute-start(bf16[128,384]{1,0:T(8,128)(2,1)S(1)} %add_convert_fusion.13), channel_id=1, source_target_pairs={{0,16},{1,17},{2,18},{3,19},{4,20},{5,21},{6,22},{7,23},{8,24},{9,... | collective-permute-start | bytes 294920 | tf_op jit(solution)/shard_map/ppermute | solution.py:366
  95.8 1.6 %collective-permute-start.30 = (bf16[2,1,1,48,384]{4,3,0,2,1:T(8,128)(2,1)S(1)}, bf16[2,1,1,48,384]{4,3,0,2,1:T(8,128)(2,1)S(1)}, u32[]{:S(2)}, u32[]{:S(2)}) collective-permute-start(bf16[2,1,1,48,384]{4,3,0,2,1:T(8,128)(2,1)S(1)} %constant_dynamic-slice_fusion), channel_id=1, source_target_pairs={{0,16},{1,17},{2,18},{3,19},{4,20},{5,21},{6,22},{7,23},{8,24},{9,... | collective-permute-start | bytes 221192 | tf_op jit(solution)/shard_map/ppermute | solution.py:366
  97.6 2.4 %last.1 = bf16[256,384]{1,0:T(8,128)(2,1)} custom-call(bf16[22,32,384]{2,1,0:T(8,128)(2,1)S(1)} %fusion.16.dzpad, bf16[256,384]{1,0:T(8,128)(2,1)S(1)} %get-tuple-element.184.gmid, f32[2,3,49,128]{3,2,1,0:T(8,128)S(1)} %bitcast.96), custom_call_target="tpu_custom_call" | custom-call | tf_op jit(solution)/shard_map/last/pallas_call | solution.py:315
  100.0 3.8 %collective-permute-done.30 = bf16[2,1,1,48,384]{4,3,0,2,1:T(8,128)(2,1)S(1)} collective-permute-done((bf16[2,1,1,48,384]{4,3,0,2,1:T(8,128)(2,1)S(1)}, bf16[2,1,1,48,384]{4,3,0,2,1:T(8,128)(2,1)S(1)}, u32[]{:S(2)}, u32[]{:S(2)}) %collective-permute-start.30) | collective-permute-done | bytes 73760 | tf_op jit(solution)/shard_map/ppermute | solution.py:366
  (118 shorter events, 17.1 us)
Async XLA Ops:
  1.7 5.6 %collective-permute-start.1 = (bf16[16,6,384]{2,1,0:T(8,128)(2,1)S(1)}, bf16[16,6,384]{2,1,0:T(8,128)(2,1)S(1)}, u32[]{:S(2)}, u32[]{:S(2)}) collective-permute-start(bf16[16,6,384]{2,1,0:T(8,128)(2,1)S(1)} %get-tuple-element.231), channel_id=1, source_target_pairs={{0,4},{1,2},{2,1},{3,7},{4,0},{5,6},{6,5},{7,3},{8,12},{9,10},{10,... | collective-permute-start | bytes 221192 | tf_op jit(solution)/shard_map/ppermute | solution.py:353
  4.7 2.6 %collective-permute-start = (bf16[16,6,384]{2,1,0:T(8,128)(2,1)S(1)}, bf16[16,6,384]{2,1,0:T(8,128)(2,1)S(1)}, u32[]{:S(2)}, u32[]{:S(2)}) collective-permute-start(bf16[16,6,384]{2,1,0:T(8,128)(2,1)S(1)} %get-tuple-element.232), channel_id=1, source_target_pairs={{0,1},{1,0},{2,3},{3,2},{4,5},{5,4},{6,7},{7,6},{8,9},{9,8},{10,11... | collective-permute-start | bytes 221192 | tf_op jit(solution)/shard_map/ppermute | solution.py:337
  4.8 12.7 %copy-start.3 = (bf16[16,16,384]{2,1,0:T(8,128)(2,1)S(1)}, bf16[16,16,384]{2,1,0:T(8,128)(2,1)}, u32[]{:S(2)}) copy-start(bf16[16,16,384]{2,1,0:T(8,128)(2,1)} %param.8) | copy-start | bytes 589828
  8.4 4.0 %collective-permute-start.3 = (bf16[6,28,384]{2,1,0:T(8,128)(2,1)S(1)}, bf16[6,28,384]{2,1,0:T(8,128)(2,1)S(1)}, u32[]{:S(2)}, u32[]{:S(2)}) collective-permute-start(bf16[6,28,384]{2,1,0:T(8,128)(2,1)S(1)} %get-tuple-element.203), channel_id=1, source_target_pairs={{0,1},{1,0},{2,3},{3,2},{4,8},{5,9},{6,10},{7,11},{8,4},{9,5},{10,... | collective-permute-start | bytes 387080 | tf_op jit(solution)/shard_map/ppermute | solution.py:353
  8.6 8.8 %collective-permute-start.2 = (bf16[6,28,384]{2,1,0:T(8,128)(2,1)S(1)}, bf16[6,28,384]{2,1,0:T(8,128)(2,1)S(1)}, u32[]{:S(2)}, u32[]{:S(2)}) collective-permute-start(bf16[6,28,384]{2,1,0:T(8,128)(2,1)S(1)} %get-tuple-element.204), channel_id=1, source_target_pairs={{0,4},{4,0},{8,12},{12,8},{16,20},{20,16},{24,28},{28,24},{1,5},{5... | collective-permute-start | bytes 387080 | tf_op jit(solution)/shard_map/ppermute | solution.py:337
  31.2 7.3 %collective-permute-start.5 = (bf16[16,3,384]{2,1,0:T(4,128)(2,1)S(1)}, bf16[16,3,384]{2,1,0:T(4,128)(2,1)S(1)}, u32[]{:S(2)}, u32[]{:S(2)}) collective-permute-start(bf16[16,3,384]{2,1,0:T(4,128)(2,1)S(1)} %get-tuple-element.227), channel_id=1, source_target_pairs={{0,4},{1,2},{2,1},{3,7},{4,0},{5,6},{6,5},{7,3},{8,12},{9,10},{10,... | collective-permute-start | bytes 110600 | tf_op jit(solution)/shard_map/ppermute | solution.py:353
  33.7 4.7 %collective-permute-start.4 = (bf16[16,3,384]{2,1,0:T(4,128)(2,1)S(1)}, bf16[16,3,384]{2,1,0:T(4,128)(2,1)S(1)}, u32[]{:S(2)}, u32[]{:S(2)}) collective-permute-start(bf16[16,3,384]{2,1,0:T(4,128)(2,1)S(1)} %get-tuple-element.228), channel_id=1, source_target_pairs={{0,1},{1,0},{2,3},{3,2},{4,5},{5,4},{6,7},{7,6},{8,9},{9,8},{10,11... | collective-permute-start | bytes 110600 | tf_op jit(solution)/shard_map/ppermute | solution.py:337
  38.5 6.0 %collective-permute-start.8 = (bf16[2,16,48,384]{3,2,1,0:T(8,128)(2,1)}, bf16[2,16,48,384]{3,2,1,0:T(8,128)(2,1)S(1)}, u32[]{:S(2)}, u32[]{:S(2)}) collective-permute-start(bf16[2,16,48,384]{3,2,1,0:T(8,128)(2,1)} %bitcast.129), channel_id=1, source_target_pairs={{0,1},{1,0},{2,3},{3,2},{4,5},{5,4},{6,7},{7,6},{8,9},{9,8},{10,11... | collective-permute-start | bytes 3538952 | tf_op jit(solution)/shard_map/ppermute | solution.py:366
  39.2 3.1 %collective-permute-start.7 = (bf16[3,22,384]{2,1,0:T(8,128)(2,1)S(1)}, bf16[3,22,384]{2,1,0:T(8,128)(2,1)S(1)}, u32[]{:S(2)}, u32[]{:S(2)}) collective-permute-start(bf16[3,22,384]{2,1,0:T(8,128)(2,1)S(1)} %get-tuple-element.219), channel_id=1, source_target_pairs={{0,1},{1,0},{2,3},{3,2},{4,8},{5,9},{6,10},{7,11},{8,4},{9,5},{10,... | collective-permute-start | bytes 152072 | tf_op jit(solution)/shard_map/ppermute | solution.py:353
  39.3 5.2 %collective-permute-start.6 = (bf16[3,22,384]{2,1,0:T(8,128)(2,1)S(1)}, bf16[3,22,384]{2,1,0:T(8,128)(2,1)S(1)}, u32[]{:S(2)}, u32[]{:S(2)}) collective-permute-start(bf16[3,22,384]{2,1,0:T(8,128)(2,1)S(1)} %get-tuple-element.220), channel_id=1, source_target_pairs={{0,4},{4,0},{8,12},{12,8},{16,20},{20,16},{24,28},{28,24},{1,5},{5... | collective-permute-start | bytes 152072 | tf_op jit(solution)/shard_map/ppermute | solution.py:337
  46.3 9.0 %collective-permute-start.10 = (bf16[1,4,2,48,384]{4,3,1,2,0:T(8,128)(2,1)S(1)}, bf16[1,4,2,48,384]{4,3,1,2,0:T(8,128)(2,1)S(1)}, u32[]{:S(2)}, u32[]{:S(2)}) collective-permute-start(bf16[1,4,2,48,384]{4,3,1,2,0:T(8,128)(2,1)S(1)} %bitcast.123), channel_id=1, source_target_pairs={{0,4},{1,5},{2,6},{3,7},{4,0},{5,1},{6,2},{7,3},{8,12},{9,13},{10,... | collective-permute-start | bytes 884744 | tf_op jit(solution)/shard_map/ppermute | solution.py:366
  48.4 7.6 %collective-permute-start.9 = (bf16[1,8,1,48,384]{4,3,1,2,0:T(8,128)(2,1)S(1)}, bf16[1,8,1,48,384]{4,3,1,2,0:T(8,128)(2,1)S(1)}, u32[]{:S(2)}, u32[]{:S(2)}) collective-permute-start(bf16[1,8,1,48,384]{4,3,1,2,0:T(8,128)(2,1)S(1)} %get-tuple-element.201), channel_id=1, source_target_pairs={{0,2},{1,3},{2,0},{3,1},{4,6},{5,7},{6,4},{7,5},{8,10},{9,11},{10,... | collective-permute-start | bytes 884744 | tf_op jit(solution)/shard_map/ppermute | solution.py:366
  56.0 4.8 %collective-permute-start.11 = (bf16[2,16,48,384]{3,2,1,0:T(8,128)(2,1)S(1)}, bf16[2,16,48,384]{3,2,1,0:T(8,128)(2,1)S(1)}, u32[]{:S(2)}, u32[]{:S(2)}) collective-permute-start(bf16[2,16,48,384]{3,2,1,0:T(8,128)(2,1)S(1)} %bitcast.105), channel_id=1, source_target_pairs={{0,1},{1,0},{2,3},{3,2},{4,5},{5,4},{6,7},{7,6},{8,9},{9,8},{10,11... | collective-permute-start | bytes 3538952 | tf_op jit(solution)/shard_map/ppermute | solution.py:366
  58.0 2.8 %collective-permute-start.12 = (bf16[128,384]{1,0:T(8,128)(2,1)S(1)}, bf16[128,384]{1,0:T(8,128)(2,1)S(1)}, u32[]{:S(2)}, u32[]{:S(2)}) collective-permute-start(bf16[128,384]{1,0:T(8,128)(2,1)S(1)} %pad_maximum_fusion.7), channel_id=1, source_target_pairs={{0,1},{1,0},{2,3},{3,2},{4,5},{5,4},{6,7},{7,6},{8,9},{9,8},{10,11... | collective-permute-start | bytes 294920 | tf_op jit(solution)/shard_map/ppermute | solution.py:366
  58.7 6.8 %collective-permute-start.15 = (bf16[1,4,1,48,384]{4,3,1,2,0:T(8,128)(2,1)S(1)}, bf16[1,4,1,48,384]{4,3,1,2,0:T(8,128)(2,1)S(1)}, u32[]{:S(2)}, u32[]{:S(2)}) collective-permute-start(bf16[1,4,1,48,384]{4,3,1,2,0:T(8,128)(2,1)S(1)} %get-tuple-element.217), channel_id=1, source_target_pairs={{0,4},{1,5},{2,6},{3,7},{4,0},{5,1},{6,2},{7,3},{8,12},{9,13},{10,... | collective-permute-start | bytes 442376 | tf_op jit(solution)/shard_map/ppermute | solution.py:366
  59.2 6.6 %collective-permute-start.16 = (bf16[1,4,1,48,384]{4,3,1,2,0:T(8,128)(2,1)S(1)}, bf16[1,4,1,48,384]{4,3,1,2,0:T(8,128)(2,1)S(1)}, u32[]{:S(2)}, u32[]{:S(2)}) collective-permute-start(bf16[1,4,1,48,384]{4,3,1,2,0:T(8,128)(2,1)S(1)} %get-tuple-element.215), channel_id=1, source_target_pairs={{0,2},{1,3},{2,0},{3,1},{4,6},{5,7},{6,4},{7,5},{8,10},{9,11},{10,... | collective-permute-start | bytes 442376 | tf_op jit(solution)/shard_map/ppermute | solution.py:366
  61.4 12.0 %collective-permute-start.14 = (bf16[1,4,2,48,384]{4,3,1,2,0:T(8,128)(2,1)S(1)}, bf16[1,4,2,48,384]{4,3,1,2,0:T(8,128)(2,1)S(1)}, u32[]{:S(2)}, u32[]{:S(2)}) collective-permute-start(bf16[1,4,2,48,384]{4,3,1,2,0:T(8,128)(2,1)S(1)} %bitcast.122), channel_id=1, source_target_pairs={{0,4},{1,5},{2,6},{3,7},{4,0},{5,1},{6,2},{7,3},{8,12},{9,13},{10,... | collective-permute-start | bytes 884744 | tf_op jit(solution)/shard_map/ppermute | solution.py:366
  63.2 10.2 %collective-permute-start.13 = (bf16[1,8,1,48,384]{4,3,1,2,0:T(8,128)(2,1)S(1)}, bf16[1,8,1,48,384]{4,3,1,2,0:T(8,128)(2,1)S(1)}, u32[]{:S(2)}, u32[]{:S(2)}) collective-permute-start(bf16[1,8,1,48,384]{4,3,1,2,0:T(8,128)(2,1)S(1)} %get-tuple-element.197), channel_id=1, source_target_pairs={{0,2},{1,3},{2,0},{3,1},{4,6},{5,7},{6,4},{7,5},{8,10},{9,11},{10,... | collective-permute-start | bytes 884744 | tf_op jit(solution)/shard_map/ppermute | solution.py:366
  63.7 9.7 %collective-permute-start.19 = (bf16[128,384]{1,0:T(8,128)(2,1)S(1)}, bf16[128,384]{1,0:T(8,128)(2,1)S(1)}, u32[]{:S(2)}, u32[]{:S(2)}) collective-permute-start(bf16[128,384]{1,0:T(8,128)(2,1)S(1)} %add_convert_fusion.16), channel_id=1, source_target_pairs={{0,2},{1,3},{2,0},{3,1},{4,6},{5,7},{6,4},{7,5},{8,10},{9,11},{10,... | collective-permute-start | bytes 294920 | tf_op jit(solution)/shard_map/ppermute | solution.py:366
  65.5 5.9 %collective-permute-start.18 = (bf16[16,3,384]{2,1,0:T(4,128)(2,1)S(1)}, bf16[16,3,384]{2,1,0:T(4,128)(2,1)S(1)}, u32[]{:S(2)}, u32[]{:S(2)}) collective-permute-start(bf16[16,3,384]{2,1,0:T(4,128)(2,1)S(1)} %get-tuple-element.225), channel_id=1, source_target_pairs={{0,4},{1,2},{2,1},{3,7},{4,0},{5,6},{6,5},{7,3},{8,12},{9,10},{10,... | collective-permute-start | bytes 110600 | tf_op jit(solution)/shard_map/ppermute | solution.py:353
  65.8 5.6 %collective-permute-start.17 = (bf16[16,3,384]{2,1,0:T(4,128)(2,1)S(1)}, bf16[16,3,384]{2,1,0:T(4,128)(2,1)S(1)}, u32[]{:S(2)}, u32[]{:S(2)}) collective-permute-start(bf16[16,3,384]{2,1,0:T(4,128)(2,1)S(1)} %get-tuple-element.226), channel_id=1, source_target_pairs={{0,1},{1,0},{2,3},{3,2},{4,5},{5,4},{6,7},{7,6},{8,9},{9,8},{10,11... | collective-permute-start | bytes 110600 | tf_op jit(solution)/shard_map/ppermute | solution.py:337
  73.6 10.9 %collective-permute-start.24 = (bf16[128,384]{1,0:T(8,128)(2,1)S(1)}, bf16[128,384]{1,0:T(8,128)(2,1)S(1)}, u32[]{:S(2)}, u32[]{:S(2)}) collective-permute-start(bf16[128,384]{1,0:T(8,128)(2,1)S(1)} %add_convert_fusion.15), channel_id=1, source_target_pairs={{0,4},{1,5},{2,6},{3,7},{4,0},{5,1},{6,2},{7,3},{8,12},{9,13},{10,... | collective-permute-start | bytes 294920 | tf_op jit(solution)/shard_map/ppermute | solution.py:366
  75.1 9.4 %collective-permute-start.20 = (bf16[1,4,1,48,384]{4,3,1,2,0:T(8,128)(2,1)S(1)}, bf16[1,4,1,48,384]{4,3,1,2,0:T(8,128)(2,1)S(1)}, u32[]{:S(2)}, u32[]{:S(2)}) collective-permute-start(bf16[1,4,1,48,384]{4,3,1,2,0:T(8,128)(2,1)S(1)} %get-tuple-element.213), channel_id=1, source_target_pairs={{0,4},{1,5},{2,6},{3,7},{4,0},{5,1},{6,2},{7,3},{8,12},{9,13},{10,... | collective-permute-start | bytes 442376 | tf_op jit(solution)/shard_map/ppermute | solution.py:366
  75.8 8.7 %collective-permute-start.21 = (bf16[1,4,1,48,384]{4,3,1,2,0:T(8,128)(2,1)S(1)}, bf16[1,4,1,48,384]{4,3,1,2,0:T(8,128)(2,1)S(1)}, u32[]{:S(2)}, u32[]{:S(2)}) collective-permute-start(bf16[1,4,1,48,384]{4,3,1,2,0:T(8,128)(2,1)S(1)} %get-tuple-element.211), channel_id=1, source_target_pairs={{0,2},{1,3},{2,0},{3,1},{4,6},{5,7},{6,4},{7,5},{8,10},{9,11},{10,... | collective-permute-start | bytes 442376 | tf_op jit(solution)/shard_map/ppermute | solution.py:366
  77.8 6.7 %collective-permute-start.22 = (bf16[2,2,1,48,384]{4,3,1,0,2:T(8,128)(2,1)S(1)}, bf16[2,2,1,48,384]{4,3,1,0,2:T(8,128)(2,1)S(1)}, u32[]{:S(2)}, u32[]{:S(2)}) collective-permute-start(bf16[2,2,1,48,384]{4,3,1,0,2:T(8,128)(2,1)S(1)} %get-tuple-element.209), channel_id=1, source_target_pairs={{0,8},{1,9},{2,10},{3,11},{4,12},{5,13},{6,14},{7,15},{8,0},{9,1},... | collective-permute-start | bytes 442376 | tf_op jit(solution)/shard_map/ppermute | solution.py:366
  80.3 4.2 %collective-permute-start.23 = (bf16[3,22,384]{2,1,0:T(8,128)(2,1)S(1)}, bf16[3,22,384]{2,1,0:T(8,128)(2,1)S(1)}, u32[]{:S(2)}, u32[]{:S(2)}) collective-permute-start(bf16[3,22,384]{2,1,0:T(8,128)(2,1)S(1)} %get-tuple-element.208), channel_id=1, source_target_pairs={{0,4},{4,0},{8,12},{12,8},{16,20},{20,16},{24,28},{28,24},{1,5},{5... | collective-permute-start | bytes 152072 | tf_op jit(solution)/shard_map/ppermute | solution.py:337
  84.6 7.8 %collective-permute-start.27 = (bf16[128,384]{1,0:T(8,128)(2,1)S(1)}, bf16[128,384]{1,0:T(8,128)(2,1)S(1)}, u32[]{:S(2)}, u32[]{:S(2)}) collective-permute-start(bf16[128,384]{1,0:T(8,128)(2,1)S(1)} %add_convert_fusion.14), channel_id=1, source_target_pairs={{0,8},{1,9},{2,10},{3,11},{4,12},{5,13},{6,14},{7,15},{8,0},{9,1},... | collective-permute-start | bytes 294920 | tf_op jit(solution)/shard_map/ppermute | solution.py:366
  85.9 8.3 %collective-permute-start.25 = (bf16[2,2,1,48,384]{4,3,0,2,1:T(8,128)(2,1)S(1)}, bf16[2,2,1,48,384]{4,3,0,2,1:T(8,128)(2,1)S(1)}, u32[]{:S(2)}, u32[]{:S(2)}) collective-permute-start(bf16[2,2,1,48,384]{4,3,0,2,1:T(8,128)(2,1)S(1)} %copy.35), channel_id=1, source_target_pairs={{0,8},{1,9},{2,10},{3,11},{4,12},{5,13},{6,14},{7,15},{8,0},{9,1},... | collective-permute-start | bytes 442376 | tf_op jit(solution)/shard_map/ppermute | solution.py:366
  87.0 5.4 %collective-permute-start.26 = (bf16[2,1,1,48,384]{4,3,1,0,2:T(8,128)(2,1)S(1)}, bf16[2,1,1,48,384]{4,3,1,0,2:T(8,128)(2,1)S(1)}, u32[]{:S(2)}, u32[]{:S(2)}) collective-permute-start(bf16[2,1,1,48,384]{4,3,1,0,2:T(8,128)(2,1)S(1)} %get-tuple-element.237), channel_id=1, source_target_pairs={{0,16},{1,17},{2,18},{3,19},{4,20},{5,21},{6,22},{7,23},{8,24},{9,... | collective-permute-start | bytes 221192 | tf_op jit(solution)/shard_map/ppermute | solution.py:366
  88.9 1.2 %collective-permute-start.28 = (bf16[3,22,384]{2,1,0:T(8,128)(2,1)S(1)}, bf16[3,22,384]{2,1,0:T(8,128)(2,1)S(1)}, u32[]{:S(2)}, u32[]{:S(2)}) collective-permute-start(bf16[3,22,384]{2,1,0:T(8,128)(2,1)S(1)} %get-tuple-element.180), channel_id=1, source_target_pairs={{0,1},{1,0},{2,3},{3,2},{4,8},{5,9},{6,10},{7,11},{8,4},{9,5},{10,... | collective-permute-start | bytes 152072 | tf_op jit(solution)/shard_map/ppermute | solution.py:353
  94.3 10.9 %collective-permute-start.29 = (bf16[128,384]{1,0:T(8,128)(2,1)S(1)}, bf16[128,384]{1,0:T(8,128)(2,1)S(1)}, u32[]{:S(2)}, u32[]{:S(2)}) collective-permute-start(bf16[128,384]{1,0:T(8,128)(2,1)S(1)} %add_convert_fusion.13), channel_id=1, source_target_pairs={{0,16},{1,17},{2,18},{3,19},{4,20},{5,21},{6,22},{7,23},{8,24},{9,... | collective-permute-start | bytes 294920 | tf_op jit(solution)/shard_map/ppermute | solution.py:366
  95.8 7.9 %collective-permute-start.30 = (bf16[2,1,1,48,384]{4,3,0,2,1:T(8,128)(2,1)S(1)}, bf16[2,1,1,48,384]{4,3,0,2,1:T(8,128)(2,1)S(1)}, u32[]{:S(2)}, u32[]{:S(2)}) collective-permute-start(bf16[2,1,1,48,384]{4,3,0,2,1:T(8,128)(2,1)S(1)} %constant_dynamic-slice_fusion), channel_id=1, source_target_pairs={{0,16},{1,17},{2,18},{3,19},{4,20},{5,21},{6,22},{7,23},{8,24},{9,... | collective-permute-start | bytes 221192 | tf_op jit(solution)/shard_map/ppermute | solution.py:366
  (5 other events, 42.4 us)

commit v8 on v7

--- a/solution.py
+++ b/solution.py
@@ -264,6 +264,10 @@
     weight_grads(place, normed, gmid, act, gpre, dw, per)
 
 
+def weights_top_kernel(per, place, normed, act, gpre, grad, *dw):
+    weight_grads(place, normed, grad, act, gpre, dw, per)
+
+
 def spread_pass(dzpad, dzs, taps, spread):
     for g in range(dzs.shape[0]):
         dzs[g] = dzpad[:, :, g * LANES : (g + 1) * LANES].astype(F32)
@@ -275,34 +279,52 @@
     out[...] = (gmid[...].astype(F32) + joined(spread, slice(None))).astype(BF16)
 
 
-def taps_kernel(source, row0, col0, dz, db, dgain, dshift, out, xs, dzs, sums):
+def small_rows_of(values, row0, col0, dz, dzs, db, dgain, dshift, sums):
     rows, cols = dzs.shape[1:3]
-    channels = out.shape[1]
+    channels = sums.shape[1]
     split_to(dzs, slice(None), dz[...].astype(F32), (rows, cols))
-    if xs is None:
-        values = source
-    else:
-        for g in range(dzs.shape[0]):
-            xs[g] = source[:, :, g * LANES : (g + 1) * LANES].astype(F32)
-        values = xs
-    sums[...] = jnp.zeros(sums.shape, F32)
     count = db.shape[1] // channels
     for k in range(count):
         sums[k : k + 1, :] = db[:, k * channels : (k + 1) * channels]
     sums[count : count + 1, :] = dgain[...]
     sums[count + 1 : count + 2, :] = dshift[...]
     tap_pass(values, row0, col0, dzs, 0, 0, sums, count + 2, rows, cols)
-    out[...] = sums[...].astype(BF16)
-
-
-def top_taps_kernel(per, place, source, dz, normed, act, gpre, grad, db, dgain, dshift, out, *rest):
-    *dw, dzs, sums = rest
-    weight_grads(place, normed, grad, act, gpre, dw, per)
-    taps_kernel(source, 0, 0, dz, db, dgain, dshift, out, None, dzs, sums)
-
-
-def low_taps_kernel(source, dz, db, dgain, dshift, out, xs, dzs, sums):
-    taps_kernel(source, HALO, HALO, dz, db, dgain, dshift, out, xs, dzs, sums)
+
+
+def taps_kernel(
+    place, mids, xpad, dz0, dz1, db0, dgain0, dshift0, db1, dgain1, dshift1, send, keep,
+    xs, dzs, sums0, sums1,
+):
+    for g in range(dzs.shape[0]):
+        xs[g] = xpad[:, :, g * LANES : (g + 1) * LANES].astype(F32)
+    sums0[...] = jnp.zeros(sums0.shape, F32)
+    sums1[...] = jnp.zeros(sums1.shape, F32)
+    small_rows_of(mids, 0, 0, dz1, dzs, db1, dgain1, dshift1, sums1)
+    small_rows_of(xs, HALO, HALO, dz0, dzs, db0, dgain0, dshift0, sums0)
+    upper = place[4] == 1
+    send[...] = jnp.where(upper, sums0[...], sums1[...]).astype(BF16)
+    keep[...] = jnp.where(upper, sums1[...], sums0[...]).astype(BF16)
+
+
+def small_kernel(scale, place, mine, got, taps_out, gains, shifts, biases):
+    upper = place[4] == 1
+    own, came = mine[...].astype(F32) * scale, got[...].astype(F32) * scale
+    channels = own.shape[1]
+    count = biases.shape[1] // channels
+    for layer, part in enumerate((jnp.where(upper, came, own), jnp.where(upper, own, came))):
+        at = slice(layer, layer + 1)
+        for k in range(count):
+            biases[at, k * channels : (k + 1) * channels] = part[k : k + 1, :]
+        gains[at, :] = part[count : count + 1, :]
+        shifts[at, :] = part[count + 1 : count + 2, :]
+        for tap in range(49):
+            taps_out[tap, at, :] = part[count + 2 + tap : count + 3 + tap, :]
+
+
+def weights_kernel(scale, keep0, got0, keep1, got1, out_in, out_out):
+    for layer, (keep, got) in enumerate(((keep0, got0), (keep1, got1))):
+        for i, out in enumerate((out_in, out_out)):
+            out[layer] = (keep[i].astype(F32) + got[i].astype(F32)) * scale
 
 
 def shape(*dims, dtype=F32):
@@ -380,12 +402,17 @@
     return (own.astype(F32) + got.astype(F32)).astype(BF16)
 
 
-def step(chunks, order, bit, mine):
+def cut(chunks, order, bit, mine):
     spot = order.index(bit)
     per = chunks.shape[-2:]
     pair = chunks.reshape((-1, 2 ** spot, 2, 2 ** (len(order) - spot - 1)) + per)
     send, keep = halves(pair, 2, mine[bit])
-    return keep, flip_bit(send, bit), [b for b in order if b != bit]
+    return send, keep, [b for b in order if b != bit]
+
+
+def step(chunks, order, bit, mine):
+    send, keep, left = cut(chunks, order, bit, mine)
+    return keep, flip_bit(send, bit), left
 
 
 def shards(activations, grad_out, kernels, norm_gains, norm_shifts, w_in, b_in, w_out):
@@ -442,7 +469,7 @@
     small_outs = (shape(1, hidden), shape(1, channels), shape(1, channels))
     small_rows = 64
 
-    xpad = filled(rim_rows(rim_cols(activations, WIDE), WIDE))
+    xpad = filled(rim_cols(rim_rows(activations, WIDE), WIDE))
     xpad, place, mine, odd_col, odd_row, outer_col, outer_row = lax.optimization_barrier(
         (xpad, place, mine, odd_col, odd_row, outer_col, outer_row)
     )
@@ -496,42 +523,44 @@
         chunks, order = settled(flight)
         return [step(chunks[i], order, sides[i], mine) for i in range(2)]
 
-    def cross(flights):
-        done = [settled(f) for f in flights]
-        return [step(*done[i], sides[1 - i], mine) for i in range(2)]
-
-    def merge(flights):
+    def onward(parts, bit):
+        kept, sent, lefts = [], [], []
+        for chunks, order in parts:
+            send, keep, left = cut(chunks, order, bit, mine)
+            kept.append(keep)
+            sent.append(send.reshape(-1, per, channels))
+            lefts.append(left)
+        got = flip_bit(jnp.concatenate(sent, axis=0), bit)
+        flights, first = [], 0
+        for keep, send, left in zip(kept, sent, lefts):
+            came = got[first : first + send.shape[0]].reshape(keep.shape)
+            flights.append((keep, came, left))
+            first += send.shape[0]
+        return flights
+
+    def merged(flights):
         done = [settled(f) for f in flights]
         return jnp.stack([d[0].reshape(-1, per, channels) for d in done]), done[0][1]
 
-    def onward(chunks, order):
-        return step(chunks, order, order[-1], mine) if order else (chunks, jnp.zeros_like(chunks), order)
-
-    def finish(flight):
-        chunks, order = settled(flight)
-        while order:
-            chunks, order = settled(onward(chunks, order))
-        return jnp.swapaxes(chunks.reshape(2, per, channels).astype(F32) * grad_scale, 1, 2)
-
     tile1 = dz1.reshape(rows, cols, channels)
-    twin, other = edges(tile1, 1, HALO, odd_col)
+    twin, other = edges(tile1, 0, HALO, odd_row)
+    twin, other = to_twin(twin, "rows"), to_other(other, "rows")
+    dw1 = run(
+        functools.partial(weights_top_kernel, per),
+        grads_b,
+        [],
+        (place, normed1, act1, gpre1, grad_flat),
+        [pltpu.SMEM] + [None] * 4,
+        name="weights_top",
+    )
+    tile1, twin, other, dw1 = fenced(tile1, twin, other, dw1)
+    wide1 = rimmed(tile1, twin, other, 0, odd_row, outer_row)
+    run1 = start(dw1)
+    twin, other = edges(wide1, 1, HALO, odd_col)
     twin, other = to_twin(twin, "cols"), to_other(other, "cols")
-    small1, *dw1 = run(
-        functools.partial(top_taps_kernel, per),
-        (shape(small_rows, channels, dtype=BF16),) + grads_b,
-        [tile_z, shape(small_rows, channels)],
-        (place, mids, dz1, normed1, act1, gpre1, grad_flat, *small1),
-        [pltpu.SMEM] + [None] * 9,
-        name="top_taps",
-    )
-    tile1, twin, other, dw1, small1 = fenced(tile1, twin, other, dw1, small1)
-    wide1 = rimmed(tile1, twin, other, 1, odd_col, outer_col)
-    run1 = start(dw1)
-    twin, other = edges(wide1, 0, HALO, odd_row)
-    twin, other = to_twin(twin, "rows"), to_other(other, "rows")
     wide1, twin, other, run1 = fenced(wide1, twin, other, run1)
     pair1 = fork(run1)
-    dzpad1 = filled(rimmed(wide1, twin, other, 0, odd_row, outer_row))
+    dzpad1 = filled(rimmed(wide1, twin, other, 1, odd_col, outer_col))
     spread_scratch = [shape(groups, *dzpad1.shape[:2], LANES), tile_z]
     grad_mid, dz0, *rest = run(
         functools.partial(low_kernel, per),
@@ -543,69 +572,92 @@
         name="low",
     )
     small0, dw0 = rest[:3], rest[3:]
-    dz0, dw0, pair1, *small0 = fenced(dz0, dw0, pair1, *small0)
+    dz0, dw0, pair1, small0 = fenced(dz0, dw0, pair1, small0)
     run0 = start(dw0)
-    pair1 = cross(pair1)
-    (small0,) = run(
-        low_taps_kernel,
-        (shape(small_rows, channels, dtype=BF16),),
-        [shape(groups, *xpad.shape[:2], LANES), tile_z, shape(small_rows, channels)],
-        (xpad, dz0, *small0),
-        name="low_taps",
-    )
-    small = jnp.concatenate([small0, small1], axis=0)
-    small_got = flip_bit(small, 0)
+    low_bit = col_bits + 1
+    pair1 = onward([settled(f) for f in pair1], low_bit)
+    small_b = shape(small_rows, channels, dtype=BF16)
+    small_f = shape(small_rows, channels)
+    send, small = run(
+        taps_kernel,
+        (small_b, small_b),
+        [shape(groups, *xpad.shape[:2], LANES), tile_z, small_f, small_f],
+        (place, mids, xpad, dz0, dz1, *small0, *small1),
+        [pltpu.SMEM] + [None] * 10,
+        name="taps",
+    )
+    small_got = flip_bit(send, 0)
     run0, small, small_got, dz0 = fenced(run0, small, small_got, dz0)
     pair0 = fork(run0)
     tile0 = dz0.reshape(rows, cols, channels)
-    twin, other = edges(tile0, 1, HALO, odd_col)
-    twin, other = to_twin(twin, "cols"), to_other(other, "cols")
+    twin, other = edges(tile0, 0, HALO, odd_row)
+    twin, other = to_twin(twin, "rows"), to_other(other, "rows")
     small = summed(small, small_got)
     small_got = flip_bit(small, 1)
     pair0, pair1, tile0, twin, other, small, small_got = fenced(
         pair0, pair1, tile0, twin, other, small, small_got
     )
-    pair0 = cross(pair0)
-    run1 = onward(*merge(pair1))
-    wide0 = rimmed(tile0, twin, other, 1, odd_col, outer_col)
-    twin, other = edges(wide0, 0, HALO, odd_row)
-    twin = to_twin(twin, "rows")
+    both = [onward([settled(pair0[i]), settled(pair1[i])], sides[1 - i]) for i in range(2)]
+    wide0 = rimmed(tile0, twin, other, 0, odd_row, outer_row)
+    twin, other = edges(wide0, 1, HALO, odd_col)
+    twin, other = to_twin(twin, "cols"), to_other(other, "cols")
     small = summed(small, small_got)
     small_got = flip_bit(small, 2)
-    pair0, run1, wide0, twin, other, small, small_got = fenced(
-        pair0, run1, wide0, twin, other, small, small_got
-    )
-    run0 = onward(*merge(pair0))
-    run1 = onward(*settled(run1))
-    other = to_other(other, "rows")
-    wait = (wide0, twin, other)
-    for bit in range(3, bits):
+    both, wide0, twin, other, small, small_got = fenced(both, wide0, twin, other, small, small_got)
+    (run0,) = onward([merged([both[0][0], both[1][0]])], low_bit)
+    part1, order1 = merged([both[0][1], both[1][1]])
+    flight1 = (part1, jnp.zeros_like(part1), order1)
+    if order1:
+        (flight1,) = onward([(part1, order1)], order1[-1])
+    small = summed(small, small_got)
+    small_got = flip_bit(small, 3)
+    (grad_in,) = run(
+        last_kernel,
+        (tile_b,),
+        spread_scratch,
+        (filled(rimmed(wide0, twin, other, 1, odd_col, outer_col)), grad_mid, taps),
+        name="last",
+    )
+    for bit in range(4, bits):
+        run0, flight1, small, small_got, grad_in = fenced(run0, flight1, small, small_got, grad_in)
+        if run0[2]:
+            (run0,) = onward([settled(run0)], run0[2][-1])
+        if flight1[2]:
+            (flight1,) = onward([settled(flight1)], flight1[2][-1])
         small = summed(small, small_got)
         small_got = flip_bit(small, bit)
-        if run0[2]:
-            run0, run1, small, small_got, wait = fenced(run0, run1, small, small_got, wait)
-            run0 = onward(*settled(run0))
-        if bit == 3:
-            (wait,) = run(
-                last_kernel,
-                (tile_b,),
-                spread_scratch,
-                (filled(rimmed(*wait, 0, odd_row, outer_row)), grad_mid, taps),
-                name="last",
-            )
-    grad_in, share1 = wait, finish(run1)
+    run0, flight1, small, small_got = fenced(run0, flight1, small, small_got)
     small = summed(small, small_got)
-    shares = [finish(run0), share1]
-    small = small.reshape(layers, small_rows, channels).astype(F32) * grad_scale
-    count = hidden // channels
+    small_got = flip_bit(small, 0)
+    share = shape(layers, per, channels)
+    grad_w_in, grad_w_out = run(
+        functools.partial(weights_kernel, grad_scale),
+        (share, share),
+        [],
+        [part.reshape(2, per, channels) for part in run0[:2] + flight1[:2]],
+        name="weights",
+    )
+    grad_taps, grad_gains, grad_shifts, grad_b_in = run(
+        functools.partial(small_kernel, grad_scale),
+        (
+            shape(49, layers, channels),
+            shape(layers, channels),
+            shape(layers, channels),
+            shape(layers, hidden),
+        ),
+        [],
+        (place, small, small_got),
+        [pltpu.SMEM, None, None],
+        name="small",
+    )
     return (
         grad_in.reshape(rows, cols, channels),
-        small[:, count + 2 : count + 51].reshape(layers, 7, 7, channels),
-        small[:, count],
-        small[:, count + 1],
-        small[:, :count].reshape(layers, hidden),
-        jnp.stack([share[0] for share in shares]),
-        jnp.stack([share[1] for share in shares]),
+        grad_taps.reshape(7, 7, layers, channels).transpose(2, 0, 1, 3),
+        grad_gains,
+        grad_shifts,
+        grad_b_in,
+        jnp.swapaxes(grad_w_in, 1, 2),
+        jnp.swapaxes(grad_w_out, 1, 2),
     )
 
 

time: 108 us -> 103 us (0.954)
  starting transfers between devices: 38.3 us -> 34 us
  local copies, waits for them, and re-layouts: 3.72 us -> 1.21 us
  Pallas kernels: 28.6 us -> 30.6 us
    ppermute x19 -> x18, waiting for transfers between devices: 10.8 us -> 19.3 us  [flip_bit(): return lax.ppermute(value, both, [(i, i ^ 1 << bit) for i in range(total)])]
    ppermute x6, waiting for transfers between devices: 10.2 us -> 5.25 us  [to_twin(): lax.ppermute(edge, axis, [(i, i ^ 1) for i in range(count) if i ^ 1 < cou...]
    ppermute x6, waiting for transfers between devices: 7.96 us -> 5.31 us  [to_other(): return lax.ppermute(edge, ('rows', 'cols'), pairs)]
    ppermute x19 -> x18, starting transfers between devices: 23 us -> 20.5 us  [flip_bit(): return lax.ppermute(value, both, [(i, i ^ 1 << bit) for i in range(total)])]
    pallas_call x6 -> x8, Pallas kernels: 28.6 us -> 30.6 us  [run(): pl.pallas_call(kernel, out_shape=outs, in_specs=[vmem if s is None else p...]
    unnamed x20 -> x14, local copies, waits for them, and re-layouts: 1.93 us -> 0.1 us
    ppermute x6, starting transfers between devices: 9.12 us -> 7.71 us  [to_twin(): lax.ppermute(edge, axis, [(i, i ^ 1) for i in range(count) if i ^ 1 < cou...]
    concatenate x5 -> x6, other arithmetic: 0.6 us -> 1.89 us  [rimmed(): return jnp.concatenate([low, tile, high], axis=axis)]
  transfers between devices with their start and end apart: 31 -> 30, of which waited for: 12 -> 13; matrix products, arithmetic and copies ran while one was open for 3% -> 3% of each run, Pallas kernels for 14% -> 16%
where the time goes in v8:
time: 103 us
  starting transfers between devices  34 us (33%)
  Pallas kernels  30.6 us (30%)
  waiting for transfers between devices  29.9 us (29%)
  other arithmetic  6.07 us (6%)
  local copies, waits for them, and re-layouts  1.21 us (1%)
  between operations  1.19 us (1%)
    pallas_call x8, Pallas kernels, run(): pl.pallas_call(kernel, out_shape=outs, in_specs=[vmem if s is None else p...  30.6 us
    ppermute x18, starting transfers between devices, flip_bit(): return lax.ppermute(value, both, [(i, i ^ 1 << bit) for i in range(total)])  20.5 us
    ppermute x18, waiting for transfers between devices, flip_bit(): return lax.ppermute(value, both, [(i, i ^ 1 << bit) for i in range(total)])  19.3 us
    ppermute x6, starting transfers between devices, to_twin(): lax.ppermute(edge, axis, [(i, i ^ 1) for i in range(count) if i ^ 1 < cou...  7.71 us
    ppermute x6, starting transfers between devices, to_other(): return lax.ppermute(edge, ('rows', 'cols'), pairs)  5.76 us
    ppermute x6, waiting for transfers between devices, to_other(): return lax.ppermute(edge, ('rows', 'cols'), pairs)  5.31 us
    ppermute x6, waiting for transfers between devices, to_twin(): lax.ppermute(edge, axis, [(i, i ^ 1) for i in range(count) if i ^ 1 < cou...  5.25 us
    convert_element_type x16, other arithmetic, summed(): return (own.astype(F32) + got.astype(F32)).astype(BF16)  2.5 us
  transfers between devices with their start and end apart: 30, of which 13 were waited for; matrix products, arithmetic and copies ran while one was open for 3% of the time, Pallas kernels for 16%

profile of v8, /device:TPU:0, one launch (start us, length us, event | category | flops | bytes accessed | tf_op | source)
XLA Modules:
  0.0 103.0 jit_solution(13746497918269927920)
XLA Ops:
  2.2 4.0 %collective-permute-start = (bf16[6,16,384]{2,1,0:T(8,128)(2,1)S(1)}, bf16[6,16,384]{2,1,0:T(8,128)(2,1)S(1)}, u32[]{:S(2)}, u32[]{:S(2)}) collective-permute-start(bf16[6,16,384]{2,1,0:T(8,128)(2,1)S(1)} %get-tuple-element.252), channel_id=1, source_target_pairs={{0,4},{4,0},{8,12},{12,8},{16,20},{20,16},{24,28},{28,24},{1,5},{5... | collective-permute-start | bytes 221192 | tf_op jit(solution)/shard_map/ppermute | solution.py:359
  6.2 2.5 %collective-permute-done = bf16[6,16,384]{2,1,0:T(8,128)(2,1)S(1)} collective-permute-done((bf16[6,16,384]{2,1,0:T(8,128)(2,1)S(1)}, bf16[6,16,384]{2,1,0:T(8,128)(2,1)S(1)}, u32[]{:S(2)}, u32[]{:S(2)}) %collective-permute-start) | collective-permute-done | bytes 73760 | tf_op jit(solution)/shard_map/ppermute | solution.py:359
  9.8 2.5 %collective-permute-start.3 = (bf16[28,6,384]{2,1,0:T(8,128)(2,1)S(1)}, bf16[28,6,384]{2,1,0:T(8,128)(2,1)S(1)}, u32[]{:S(2)}, u32[]{:S(2)}) collective-permute-start(bf16[28,6,384]{2,1,0:T(8,128)(2,1)S(1)} %get-tuple-element.229), channel_id=1, source_target_pairs={{0,4},{1,2},{2,1},{3,7},{4,0},{5,6},{6,5},{7,3},{8,12},{9,10},{10,... | collective-permute-start | bytes 387080 | tf_op jit(solution)/shard_map/ppermute | solution.py:375
  12.7 3.0 %collective-permute-done.3 = bf16[28,6,384]{2,1,0:T(8,128)(2,1)S(1)} collective-permute-done((bf16[28,6,384]{2,1,0:T(8,128)(2,1)S(1)}, bf16[28,6,384]{2,1,0:T(8,128)(2,1)S(1)}, u32[]{:S(2)}, u32[]{:S(2)}) %collective-permute-start.3) | collective-permute-done | bytes 129056 | tf_op jit(solution)/shard_map/ppermute | solution.py:375
  16.1 8.6 %forward.1 = (f32[3,22,24,128]{3,2,1,0:T(8,128)S(1)}, f32[3,16,16,128]{3,2,1,0:T(8,128)S(1)}) custom-call(s32[5]{0:T(128)S(1)} %stack.25.place, bf16[28,32,384]{2,1,0:T(8,128)(2,1)S(1)} %fusion.12.xpad, f32[2,3,49,128]{3,2,1,0:T(8,128)S(1)} %bitcast.115, f32[2,384]{1,0:T(2,128)S(1)} %copy-done.1, f32[2,384]{1,0:T(2,128)S(1)} %copy-done.2, ...), custom_call_target="tpu_custom_call" | custom-call | tf_op jit(solution)/shard_map/forward/pallas_call | solution.py:337
  24.8 4.6 %top.1 = (bf16[256,384]{1,0:T(8,128)(2,1)S(1)}, bf16[256,384]{1,0:T(8,128)(2,1)S(1)}, bf16[256,1536]{1,0:T(8,128)(2,1)S(1)}, bf16[256,1536]{1,0:T(8,128)(2,1)S(1...) custom-call(f32[3,22,24,128]{3,2,1,0:T(8,128)S(1)} %get-tuple-element.115.mids, ...), custom_call_target="tpu_custom_call" | custom-call | tf_op jit(solution)/shard_map/top/pallas_call | solution.py:337
  29.4 2.1 %collective-permute-start.4 = (bf16[3,16,384]{2,1,0:T(8,128)(2,1)S(1)}, bf16[3,16,384]{2,1,0:T(8,128)(2,1)S(1)}, u32[]{:S(2)}, u32[]{:S(2)}) collective-permute-start(bf16[3,16,384]{2,1,0:T(8,128)(2,1)S(1)} %bitcast.152), channel_id=1, source_target_pairs={{0,4},{4,0},{8,12},{12,8},{16,20},{20,16},{24,28},{28,24},{1,5},{5... | collective-permute-start | bytes 110600 | tf_op jit(solution)/shard_map/ppermute | solution.py:359
  31.5 2.6 %weights_top.1 = (bf16[2,768,384]{2,1,0:T(8,128)(2,1)S(1)}, bf16[2,768,384]{2,1,0:T(8,128)(2,1)}) custom-call(s32[5]{0:T(128)S(1)} %stack.25.place, bf16[256,384]{1,0:T(8,128)(2,1)S(1)} %get-tuple-element.117.normed, bf16[256,1536]{1,0:T(8,128)(2,1)S(1)} %get-tuple-element.118.act, bf16[256,1536]{1,0:T(8,128)(2,1)S(1)} %get-tuple-element.119.gpre, ...), custom_call_target="tpu_custom_call" | custom-call | tf_op jit(solution)/shard_map/weights_top/pallas_call | solution.py:337
  34.8 2.6 %collective-permute-start.7 = (bf16[22,3,384]{2,1,0:T(4,128)(2,1)S(1)}, bf16[22,3,384]{2,1,0:T(4,128)(2,1)S(1)}, u32[]{:S(2)}, u32[]{:S(2)}) collective-permute-start(bf16[22,3,384]{2,1,0:T(4,128)(2,1)S(1)} %get-tuple-element.245), channel_id=1, source_target_pairs={{0,4},{1,2},{2,1},{3,7},{4,0},{5,6},{6,5},{7,3},{8,12},{9,10},{10,... | collective-permute-start | bytes 152072 | tf_op jit(solution)/shard_map/ppermute | solution.py:375
  37.4 2.3 %collective-permute-done.7 = bf16[22,3,384]{2,1,0:T(4,128)(2,1)S(1)} collective-permute-done((bf16[22,3,384]{2,1,0:T(4,128)(2,1)S(1)}, bf16[22,3,384]{2,1,0:T(4,128)(2,1)S(1)}, u32[]{:S(2)}, u32[]{:S(2)}) %collective-permute-start.7) | collective-permute-done | bytes 50720 | tf_op jit(solution)/shard_map/ppermute | solution.py:375
  39.6 1.6 %add_convert_fusion.1 = bf16[2,16,48,384]{3,2,1,0:T(8,128)(2,1)S(1)} fusion(bf16[2,16,48,384]{3,2,1,0:T(8,128)(2,1)S(1)} %collective-permute-done.8, bf16[2,16,48,384]{3,2,1,0:T(8,128)(2,1)} %bitcast.133), kind=kLoop, calls=%fused_computation.1 | loop fusion | flops 2359296 | bytes 3538944 | tf_op jit(solution)/shard_map/convert_element_type | solution.py:402
  41.4 2.1 %collective-permute-start.10 = (bf16[1,4,2,48,384]{4,3,2,1,0:T(8,128)(2,1)S(1)}, bf16[1,4,2,48,384]{4,3,2,1,0:T(8,128)(2,1)S(1)}, u32[]{:S(2)}, u32[]{:S(2)}) collective-permute-start(bf16[1,4,2,48,384]{4,3,2,1,0:T(8,128)(2,1)S(1)} %get-tuple-element.223), channel_id=1, source_target_pairs={{0,4},{1,5},{2,6},{3,7},{4,0},{5,1},{6,2},{7,3},{8,12},{9,13},{10,... | collective-permute-start | bytes 884744 | tf_op jit(solution)/shard_map/ppermute | solution.py:388
  44.3 6.1 %low.1 = (bf16[256,384]{1,0:T(8,128)(2,1)S(1)}, bf16[256,384]{1,0:T(8,128)(2,1)S(1)}, f32[1,1536]{1,0:T(1,128)S(1)}, f32[1,384]{1,0:T(1,128)S(1)}, f32[1,384]{1,...) custom-call(s32[5]{0:T(128)S(1)} %stack.25.place, ...), custom_call_target="tpu_custom_call" | custom-call | tf_op jit(solution)/shard_map/low/pallas_call | solution.py:337
  50.8 1.6 %collective-permute-done.9 = bf16[1,8,1,48,384]{4,3,1,2,0:T(8,128)(2,1)S(1)} collective-permute-done((bf16[1,8,1,48,384]{4,3,1,2,0:T(8,128)(2,1)S(1)}, bf16[1,8,1,48,384]{4,3,1,2,0:T(8,128)(2,1)S(1)}, u32[]{:S(2)}, u32[]{:S(2)}) %collective-permute-start.9) | collective-permute-done | bytes 294944 | tf_op jit(solution)/shard_map/ppermute | solution.py:388
  52.4 4.3 %taps.1 = (bf16[64,384]{1,0:T(8,128)(2,1)S(1)}, bf16[64,384]{1,0:T(8,128)(2,1)S(1)}) custom-call(s32[5]{0:T(128)S(1)} %stack.25.place, f32[3,22,24,128]{3,2,1,0:T(8,128)S(1)} %get-tuple-element.115.mids, bf16[28,32,384]{2,1,0:T(8,128)(2,1)S(1)} %fusion.12.xpad, bf16[256,384]{1,0:T(8,128)(2,1)S(1)} %get-tuple-element.164.dz0, ...), custom_call_target="tpu_custom_call" | custom-call | tf_op jit(solution)/shard_map/taps/pallas_call | solution.py:337
  57.6 1.6 %collective-permute-start.15 = (bf16[8,48,384]{2,1,0:T(8,128)(2,1)S(1)}, bf16[8,48,384]{2,1,0:T(8,128)(2,1)S(1)}, u32[]{:S(2)}, u32[]{:S(2)}) collective-permute-start(bf16[8,48,384]{2,1,0:T(8,128)(2,1)S(1)} %pad_maximum_fusion.1), channel_id=1, source_target_pairs={{0,8},{1,9},{2,10},{3,11},{4,12},{5,13},{6,14},{7,15},{8,0},{9,1},... | collective-permute-start | bytes 884744 | tf_op jit(solution)/shard_map/ppermute | solution.py:388
  60.2 1.2 %collective-permute-start.14 = (bf16[1,4,2,48,384]{4,3,1,2,0:T(8,128)(2,1)S(1)}, bf16[1,4,2,48,384]{4,3,1,2,0:T(8,128)(2,1)S(1)}, u32[]{:S(2)}, u32[]{:S(2)}) collective-permute-start(bf16[1,4,2,48,384]{4,3,1,2,0:T(8,128)(2,1)S(1)} %bitcast.145), channel_id=1, source_target_pairs={{0,4},{1,5},{2,6},{3,7},{4,0},{5,1},{6,2},{7,3},{8,12},{9,13},{10,... | collective-permute-start | bytes 884744 | tf_op jit(solution)/shard_map/ppermute | solution.py:388
  61.5 1.7 %collective-permute-start.13 = (bf16[1,8,1,48,384]{4,3,1,2,0:T(8,128)(2,1)S(1)}, bf16[1,8,1,48,384]{4,3,1,2,0:T(8,128)(2,1)S(1)}, u32[]{:S(2)}, u32[]{:S(2)}) collective-permute-start(bf16[1,8,1,48,384]{4,3,1,2,0:T(8,128)(2,1)S(1)} %get-tuple-element.221), channel_id=1, source_target_pairs={{0,2},{1,3},{2,0},{3,1},{4,6},{5,7},{6,4},{7,5},{8,10},{9,11},{10,... | collective-permute-start | bytes 884744 | tf_op jit(solution)/shard_map/ppermute | solution.py:388
  64.2 2.4 %collective-permute-done.15 = bf16[8,48,384]{2,1,0:T(8,128)(2,1)S(1)} collective-permute-done((bf16[8,48,384]{2,1,0:T(8,128)(2,1)S(1)}, bf16[8,48,384]{2,1,0:T(8,128)(2,1)S(1)}, u32[]{:S(2)}, u32[]{:S(2)}) %collective-permute-start.15) | collective-permute-done | bytes 294944 | tf_op jit(solution)/shard_map/ppermute | solution.py:388
  66.7 2.8 %collective-permute-done.16 = bf16[3,16,384]{2,1,0:T(8,128)(2,1)S(1)} collective-permute-done((bf16[3,16,384]{2,1,0:T(8,128)(2,1)S(1)}, bf16[3,16,384]{2,1,0:T(8,128)(2,1)S(1)}, u32[]{:S(2)}, u32[]{:S(2)}) %collective-permute-start.16) | collective-permute-done | bytes 36896 | tf_op jit(solution)/shard_map/ppermute | solution.py:359
  70.4 2.4 %collective-permute-start.23 = (bf16[64,384]{1,0:T(8,128)(2,1)S(1)}, bf16[64,384]{1,0:T(8,128)(2,1)S(1)}, u32[]{:S(2)}, u32[]{:S(2)}) collective-permute-start(bf16[64,384]{1,0:T(8,128)(2,1)S(1)} %add_convert_fusion.16), channel_id=1, source_target_pairs={{0,4},{1,5},{2,6},{3,7},{4,0},{5,1},{6,2},{7,3},{8,12},{9,13},{10,... | collective-permute-start | bytes 147464 | tf_op jit(solution)/shard_map/ppermute | solution.py:388
  73.8 1.4 %collective-permute-start.19 = (bf16[6,48,384]{2,1,0:T(8,128)(2,1)S(1)}, bf16[6,48,384]{2,1,0:T(8,128)(2,1)S(1)}, u32[]{:S(2)}, u32[]{:S(2)}) collective-permute-start(bf16[6,48,384]{2,1,0:T(8,128)(2,1)S(1)} %pad_maximum_fusion.4), channel_id=1, source_target_pairs={{0,4},{1,5},{2,6},{3,7},{4,0},{5,1},{6,2},{7,3},{8,12},{9,13},{10,... | collective-permute-start | bytes 663560 | tf_op jit(solution)/shard_map/ppermute | solution.py:388
  75.5 6.5 %collective-permute-done.19 = bf16[6,48,384]{2,1,0:T(8,128)(2,1)S(1)} collective-permute-done((bf16[6,48,384]{2,1,0:T(8,128)(2,1)S(1)}, bf16[6,48,384]{2,1,0:T(8,128)(2,1)S(1)}, u32[]{:S(2)}, u32[]{:S(2)}) %collective-permute-start.19) | collective-permute-done | bytes 221216 | tf_op jit(solution)/shard_map/ppermute | solution.py:388
  83.1 1.8 %collective-permute-start.26 = (bf16[64,384]{1,0:T(8,128)(2,1)S(1)}, bf16[64,384]{1,0:T(8,128)(2,1)S(1)}, u32[]{:S(2)}, u32[]{:S(2)}) collective-permute-start(bf16[64,384]{1,0:T(8,128)(2,1)S(1)} %add_convert_fusion.15), channel_id=1, source_target_pairs={{0,8},{1,9},{2,10},{3,11},{4,12},{5,13},{6,14},{7,15},{8,0},{9,1},... | collective-permute-start | bytes 147464 | tf_op jit(solution)/shard_map/ppermute | solution.py:388
  85.0 1.1 %collective-permute-start.25 = (bf16[2,48,384]{2,1,0:T(8,128)(2,1)S(1)}, bf16[2,48,384]{2,1,0:T(8,128)(2,1)S(1)}, u32[]{:S(2)}, u32[]{:S(2)}) collective-permute-start(bf16[2,48,384]{2,1,0:T(8,128)(2,1)S(1)} %get-tuple-element.255), channel_id=1, source_target_pairs={{0,16},{1,17},{2,18},{3,19},{4,20},{5,21},{6,22},{7,23},{8,24},{9,... | collective-permute-start | bytes 221192 | tf_op jit(solution)/shard_map/ppermute | solution.py:388
  86.2 2.1 %collective-permute-start.24 = (bf16[4,48,384]{2,1,0:T(8,128)(2,1)S(1)}, bf16[4,48,384]{2,1,0:T(8,128)(2,1)S(1)}, u32[]{:S(2)}, u32[]{:S(2)}) collective-permute-start(bf16[4,48,384]{2,1,0:T(8,128)(2,1)S(1)} %bitcast.148), channel_id=1, source_target_pairs={{0,8},{1,9},{2,10},{3,11},{4,12},{5,13},{6,14},{7,15},{8,0},{9,1},... | collective-permute-start | bytes 442376 | tf_op jit(solution)/shard_map/ppermute | solution.py:388
  88.7 2.4 %last.1 = bf16[256,384]{1,0:T(8,128)(2,1)} custom-call(bf16[22,32,384]{2,1,0:T(8,128)(2,1)S(1)} %fusion.18.dzpad, bf16[256,384]{1,0:T(8,128)(2,1)S(1)} %get-tuple-element.195.gmid, f32[2,3,49,128]{3,2,1,0:T(8,128)S(1)} %bitcast.118), custom_call_target="tpu_custom_call" | custom-call | tf_op jit(solution)/shard_map/last/pallas_call | solution.py:337
  91.1 1.4 %collective-permute-done.24 = bf16[4,48,384]{2,1,0:T(8,128)(2,1)S(1)} collective-permute-done((bf16[4,48,384]{2,1,0:T(8,128)(2,1)S(1)}, bf16[4,48,384]{2,1,0:T(8,128)(2,1)S(1)}, u32[]{:S(2)}, u32[]{:S(2)}) %collective-permute-start.24) | collective-permute-done | bytes 147488 | tf_op jit(solution)/shard_map/ppermute | solution.py:388
  92.6 1.6 %collective-permute-start.27 = (bf16[2,48,384]{2,1,0:T(8,128)(2,1)S(1)}, bf16[2,48,384]{2,1,0:T(8,128)(2,1)S(1)}, u32[]{:S(2)}, u32[]{:S(2)}) collective-permute-start(bf16[2,48,384]{2,1,0:T(8,128)(2,1)S(1)} %get-tuple-element.253), channel_id=1, source_target_pairs={{0,16},{1,17},{2,18},{3,19},{4,20},{5,21},{6,22},{7,23},{8,24},{9,... | collective-permute-start | bytes 221192 | tf_op jit(solution)/shard_map/ppermute | solution.py:388
  94.1 1.5 %collective-permute-start.28 = (bf16[64,384]{1,0:T(8,128)(2,1)S(1)}, bf16[64,384]{1,0:T(8,128)(2,1)S(1)}, u32[]{:S(2)}, u32[]{:S(2)}) collective-permute-start(bf16[64,384]{1,0:T(8,128)(2,1)S(1)} %add_convert_fusion.14), channel_id=1, source_target_pairs={{0,16},{1,17},{2,18},{3,19},{4,20},{5,21},{6,22},{7,23},{8,24},{9,... | collective-permute-start | bytes 147464 | tf_op jit(solution)/shard_map/ppermute | solution.py:388
  95.6 4.8 %collective-permute-done.28 = bf16[64,384]{1,0:T(8,128)(2,1)S(1)} collective-permute-done((bf16[64,384]{1,0:T(8,128)(2,1)S(1)}, bf16[64,384]{1,0:T(8,128)(2,1)S(1)}, u32[]{:S(2)}, u32[]{:S(2)}) %collective-permute-start.28) | collective-permute-done | bytes 49184 | tf_op jit(solution)/shard_map/ppermute | solution.py:388
  101.7 1.3 %small.1 = (f32[49,2,384]{2,1,0:T(2,128)}, f32[2,384]{1,0:T(2,128)}, f32[2,384]{1,0:T(2,128)}, f32[2,1536]{1,0:T(2,128)}) custom-call(s32[5]{0:T(128)S(1)} %stack.25.place, bf16[64,384]{1,0:T(8,128)(2,1)S(1)} %add_convert_fusion.13.mine, bf16[64,384]{1,0:T(8,128)(2,1)S(1)} %collective-permute-done.29.got), custom_call_target="tpu_custom_call" | custom-call | tf_op jit(solution)/shard_map/small/pallas_call | solution.py:337
  (113 shorter events, 13.4 us)
Async XLA Ops:
  0.6 11.7 %copy-start.5 = (f32[2,1536]{1,0:T(2,128)S(1)}, f32[2,1536]{1,0:T(2,128)}, u32[]{:S(2)}) copy-start(f32[2,1536]{1,0:T(2,128)} %param.14) | copy-start | bytes 36868
  0.6 11.7 %copy-start.4 = (f32[2,7,7,384]{3,0,2,1:T(2,128)S(1)}, f32[2,7,7,384]{3,0,2,1:T(2,128)}, u32[]{:S(2)}) copy-start(f32[2,7,7,384]{3,0,2,1:T(2,128)} %param.10) | copy-start | bytes 451588
  1.6 4.6 %collective-permute-start.1 = (bf16[6,16,384]{2,1,0:T(8,128)(2,1)S(1)}, bf16[6,16,384]{2,1,0:T(8,128)(2,1)S(1)}, u32[]{:S(2)}, u32[]{:S(2)}) collective-permute-start(bf16[6,16,384]{2,1,0:T(8,128)(2,1)S(1)} %get-tuple-element.251), channel_id=1, source_target_pairs={{0,1},{1,0},{2,3},{3,2},{4,8},{5,9},{6,10},{7,11},{8,4},{9,5},{10,... | collective-permute-start | bytes 221192 | tf_op jit(solution)/shard_map/ppermute | solution.py:375
  2.2 6.5 %collective-permute-start = (bf16[6,16,384]{2,1,0:T(8,128)(2,1)S(1)}, bf16[6,16,384]{2,1,0:T(8,128)(2,1)S(1)}, u32[]{:S(2)}, u32[]{:S(2)}) collective-permute-start(bf16[6,16,384]{2,1,0:T(8,128)(2,1)S(1)} %get-tuple-element.252), channel_id=1, source_target_pairs={{0,4},{4,0},{8,12},{12,8},{16,20},{20,16},{24,28},{28,24},{1,5},{5... | collective-permute-start | bytes 221192 | tf_op jit(solution)/shard_map/ppermute | solution.py:359
  9.8 5.9 %collective-permute-start.3 = (bf16[28,6,384]{2,1,0:T(8,128)(2,1)S(1)}, bf16[28,6,384]{2,1,0:T(8,128)(2,1)S(1)}, u32[]{:S(2)}, u32[]{:S(2)}) collective-permute-start(bf16[28,6,384]{2,1,0:T(8,128)(2,1)S(1)} %get-tuple-element.229), channel_id=1, source_target_pairs={{0,4},{1,2},{2,1},{3,7},{4,0},{5,6},{6,5},{7,3},{8,12},{9,10},{10,... | collective-permute-start | bytes 387080 | tf_op jit(solution)/shard_map/ppermute | solution.py:375
  12.3 3.4 %collective-permute-start.2 = (bf16[28,6,384]{2,1,0:T(8,128)(2,1)S(1)}, bf16[28,6,384]{2,1,0:T(8,128)(2,1)S(1)}, u32[]{:S(2)}, u32[]{:S(2)}) collective-permute-start(bf16[28,6,384]{2,1,0:T(8,128)(2,1)S(1)} %get-tuple-element.230), channel_id=1, source_target_pairs={{0,1},{1,0},{2,3},{3,2},{4,5},{5,4},{6,7},{7,6},{8,9},{9,8},{10,11... | collective-permute-start | bytes 387080 | tf_op jit(solution)/shard_map/ppermute | solution.py:359
  29.4 4.7 %collective-permute-start.4 = (bf16[3,16,384]{2,1,0:T(8,128)(2,1)S(1)}, bf16[3,16,384]{2,1,0:T(8,128)(2,1)S(1)}, u32[]{:S(2)}, u32[]{:S(2)}) collective-permute-start(bf16[3,16,384]{2,1,0:T(8,128)(2,1)S(1)} %bitcast.152), channel_id=1, source_target_pairs={{0,4},{4,0},{8,12},{12,8},{16,20},{20,16},{24,28},{28,24},{1,5},{5... | collective-permute-start | bytes 110600 | tf_op jit(solution)/shard_map/ppermute | solution.py:359
  31.5 2.6 %collective-permute-start.5 = (bf16[3,16,384]{2,1,0:T(8,128)(2,1)S(1)}, bf16[3,16,384]{2,1,0:T(8,128)(2,1)S(1)}, u32[]{:S(2)}, u32[]{:S(2)}) collective-permute-start(bf16[3,16,384]{2,1,0:T(8,128)(2,1)S(1)} %bitcast.151), channel_id=1, source_target_pairs={{0,1},{1,0},{2,3},{3,2},{4,8},{5,9},{6,10},{7,11},{8,4},{9,5},{10,... | collective-permute-start | bytes 110600 | tf_op jit(solution)/shard_map/ppermute | solution.py:375
  34.1 5.5 %collective-permute-start.8 = (bf16[2,16,48,384]{3,2,1,0:T(8,128)(2,1)S(1)}, bf16[2,16,48,384]{3,2,1,0:T(8,128)(2,1)S(1)}, u32[]{:S(2)}, u32[]{:S(2)}) collective-permute-start(bf16[2,16,48,384]{3,2,1,0:T(8,128)(2,1)S(1)} %bitcast.128), channel_id=1, source_target_pairs={{0,1},{1,0},{2,3},{3,2},{4,5},{5,4},{6,7},{7,6},{8,9},{9,8},{10,11... | collective-permute-start | bytes 3538952 | tf_op jit(solution)/shard_map/ppermute | solution.py:388
  34.8 4.9 %collective-permute-start.7 = (bf16[22,3,384]{2,1,0:T(4,128)(2,1)S(1)}, bf16[22,3,384]{2,1,0:T(4,128)(2,1)S(1)}, u32[]{:S(2)}, u32[]{:S(2)}) collective-permute-start(bf16[22,3,384]{2,1,0:T(4,128)(2,1)S(1)} %get-tuple-element.245), channel_id=1, source_target_pairs={{0,4},{1,2},{2,1},{3,7},{4,0},{5,6},{6,5},{7,3},{8,12},{9,10},{10,... | collective-permute-start | bytes 152072 | tf_op jit(solution)/shard_map/ppermute | solution.py:375
  37.4 2.3 %collective-permute-start.6 = (bf16[22,3,384]{2,1,0:T(4,128)(2,1)S(1)}, bf16[22,3,384]{2,1,0:T(4,128)(2,1)S(1)}, u32[]{:S(2)}, u32[]{:S(2)}) collective-permute-start(bf16[22,3,384]{2,1,0:T(4,128)(2,1)S(1)} %get-tuple-element.246), channel_id=1, source_target_pairs={{0,1},{1,0},{2,3},{3,2},{4,5},{5,4},{6,7},{7,6},{8,9},{9,8},{10,11... | collective-permute-start | bytes 152072 | tf_op jit(solution)/shard_map/ppermute | solution.py:359
  41.4 9.4 %collective-permute-start.10 = (bf16[1,4,2,48,384]{4,3,2,1,0:T(8,128)(2,1)S(1)}, bf16[1,4,2,48,384]{4,3,2,1,0:T(8,128)(2,1)S(1)}, u32[]{:S(2)}, u32[]{:S(2)}) collective-permute-start(bf16[1,4,2,48,384]{4,3,2,1,0:T(8,128)(2,1)S(1)} %get-tuple-element.223), channel_id=1, source_target_pairs={{0,4},{1,5},{2,6},{3,7},{4,0},{5,1},{6,2},{7,3},{8,12},{9,13},{10,... | collective-permute-start | bytes 884744 | tf_op jit(solution)/shard_map/ppermute | solution.py:388
  43.6 8.8 %collective-permute-start.9 = (bf16[1,8,1,48,384]{4,3,1,2,0:T(8,128)(2,1)S(1)}, bf16[1,8,1,48,384]{4,3,1,2,0:T(8,128)(2,1)S(1)}, u32[]{:S(2)}, u32[]{:S(2)}) collective-permute-start(bf16[1,8,1,48,384]{4,3,1,2,0:T(8,128)(2,1)S(1)} %get-tuple-element.225), channel_id=1, source_target_pairs={{0,2},{1,3},{2,0},{3,1},{4,6},{5,7},{6,4},{7,5},{8,10},{9,11},{10,... | collective-permute-start | bytes 884744 | tf_op jit(solution)/shard_map/ppermute | solution.py:388
  52.4 6.8 %collective-permute-start.11 = (bf16[2,16,48,384]{3,2,1,0:T(8,128)(2,1)S(1)}, bf16[2,16,48,384]{3,2,1,0:T(8,128)(2,1)S(1)}, u32[]{:S(2)}, u32[]{:S(2)}) collective-permute-start(bf16[2,16,48,384]{3,2,1,0:T(8,128)(2,1)S(1)} %bitcast.127), channel_id=1, source_target_pairs={{0,1},{1,0},{2,3},{3,2},{4,5},{5,4},{6,7},{7,6},{8,9},{9,8},{10,11... | collective-permute-start | bytes 3538952 | tf_op jit(solution)/shard_map/ppermute | solution.py:388
  56.7 2.5 %collective-permute-start.12 = (bf16[64,384]{1,0:T(8,128)(2,1)S(1)}, bf16[64,384]{1,0:T(8,128)(2,1)S(1)}, u32[]{:S(2)}, u32[]{:S(2)}) collective-permute-start(bf16[64,384]{1,0:T(8,128)(2,1)S(1)} %get-tuple-element.155), channel_id=1, source_target_pairs={{0,1},{1,0},{2,3},{3,2},{4,5},{5,4},{6,7},{7,6},{8,9},{9,8},{10,11... | collective-permute-start | bytes 147464 | tf_op jit(solution)/shard_map/ppermute | solution.py:388
  57.6 9.0 %collective-permute-start.15 = (bf16[8,48,384]{2,1,0:T(8,128)(2,1)S(1)}, bf16[8,48,384]{2,1,0:T(8,128)(2,1)S(1)}, u32[]{:S(2)}, u32[]{:S(2)}) collective-permute-start(bf16[8,48,384]{2,1,0:T(8,128)(2,1)S(1)} %pad_maximum_fusion.1), channel_id=1, source_target_pairs={{0,8},{1,9},{2,10},{3,11},{4,12},{5,13},{6,14},{7,15},{8,0},{9,1},... | collective-permute-start | bytes 884744 | tf_op jit(solution)/shard_map/ppermute | solution.py:388
  59.8 9.6 %collective-permute-start.18 = (bf16[64,384]{1,0:T(8,128)(2,1)S(1)}, bf16[64,384]{1,0:T(8,128)(2,1)S(1)}, u32[]{:S(2)}, u32[]{:S(2)}) collective-permute-start(bf16[64,384]{1,0:T(8,128)(2,1)S(1)} %add_convert_fusion.17), channel_id=1, source_target_pairs={{0,2},{1,3},{2,0},{3,1},{4,6},{5,7},{6,4},{7,5},{8,10},{9,11},{10,... | collective-permute-start | bytes 147464 | tf_op jit(solution)/shard_map/ppermute | solution.py:388
  60.2 9.2 %collective-permute-start.14 = (bf16[1,4,2,48,384]{4,3,1,2,0:T(8,128)(2,1)S(1)}, bf16[1,4,2,48,384]{4,3,1,2,0:T(8,128)(2,1)S(1)}, u32[]{:S(2)}, u32[]{:S(2)}) collective-permute-start(bf16[1,4,2,48,384]{4,3,1,2,0:T(8,128)(2,1)S(1)} %bitcast.145), channel_id=1, source_target_pairs={{0,4},{1,5},{2,6},{3,7},{4,0},{5,1},{6,2},{7,3},{8,12},{9,13},{10,... | collective-permute-start | bytes 884744 | tf_op jit(solution)/shard_map/ppermute | solution.py:388
  61.5 8.7 %collective-permute-start.13 = (bf16[1,8,1,48,384]{4,3,1,2,0:T(8,128)(2,1)S(1)}, bf16[1,8,1,48,384]{4,3,1,2,0:T(8,128)(2,1)S(1)}, u32[]{:S(2)}, u32[]{:S(2)}) collective-permute-start(bf16[1,8,1,48,384]{4,3,1,2,0:T(8,128)(2,1)S(1)} %get-tuple-element.221), channel_id=1, source_target_pairs={{0,2},{1,3},{2,0},{3,1},{4,6},{5,7},{6,4},{7,5},{8,10},{9,11},{10,... | collective-permute-start | bytes 884744 | tf_op jit(solution)/shard_map/ppermute | solution.py:388
  63.3 6.1 %collective-permute-start.16 = (bf16[3,16,384]{2,1,0:T(8,128)(2,1)S(1)}, bf16[3,16,384]{2,1,0:T(8,128)(2,1)S(1)}, u32[]{:S(2)}, u32[]{:S(2)}) collective-permute-start(bf16[3,16,384]{2,1,0:T(8,128)(2,1)S(1)} %bitcast.150), channel_id=1, source_target_pairs={{0,4},{4,0},{8,12},{12,8},{16,20},{20,16},{24,28},{28,24},{1,5},{5... | collective-permute-start | bytes 110600 | tf_op jit(solution)/shard_map/ppermute | solution.py:359
  66.6 2.8 %collective-permute-start.17 = (bf16[3,16,384]{2,1,0:T(8,128)(2,1)S(1)}, bf16[3,16,384]{2,1,0:T(8,128)(2,1)S(1)}, u32[]{:S(2)}, u32[]{:S(2)}) collective-permute-start(bf16[3,16,384]{2,1,0:T(8,128)(2,1)S(1)} %bitcast.149), channel_id=1, source_target_pairs={{0,1},{1,0},{2,3},{3,2},{4,8},{5,9},{6,10},{7,11},{8,4},{9,5},{10,... | collective-permute-start | bytes 110600 | tf_op jit(solution)/shard_map/ppermute | solution.py:375
  70.4 12.7 %collective-permute-start.23 = (bf16[64,384]{1,0:T(8,128)(2,1)S(1)}, bf16[64,384]{1,0:T(8,128)(2,1)S(1)}, u32[]{:S(2)}, u32[]{:S(2)}) collective-permute-start(bf16[64,384]{1,0:T(8,128)(2,1)S(1)} %add_convert_fusion.16), channel_id=1, source_target_pairs={{0,4},{1,5},{2,6},{3,7},{4,0},{5,1},{6,2},{7,3},{8,12},{9,13},{10,... | collective-permute-start | bytes 147464 | tf_op jit(solution)/shard_map/ppermute | solution.py:388
  72.9 10.2 %collective-permute-start.22 = (bf16[22,3,384]{2,1,0:T(4,128)(2,1)S(1)}, bf16[22,3,384]{2,1,0:T(4,128)(2,1)S(1)}, u32[]{:S(2)}, u32[]{:S(2)}) collective-permute-start(bf16[22,3,384]{2,1,0:T(4,128)(2,1)S(1)} %get-tuple-element.243), channel_id=1, source_target_pairs={{0,4},{1,2},{2,1},{3,7},{4,0},{5,6},{6,5},{7,3},{8,12},{9,10},{10,... | collective-permute-start | bytes 152072 | tf_op jit(solution)/shard_map/ppermute | solution.py:375
  73.0 10.1 %collective-permute-start.21 = (bf16[22,3,384]{2,1,0:T(4,128)(2,1)S(1)}, bf16[22,3,384]{2,1,0:T(4,128)(2,1)S(1)}, u32[]{:S(2)}, u32[]{:S(2)}) collective-permute-start(bf16[22,3,384]{2,1,0:T(4,128)(2,1)S(1)} %get-tuple-element.244), channel_id=1, source_target_pairs={{0,1},{1,0},{2,3},{3,2},{4,5},{5,4},{6,7},{7,6},{8,9},{9,8},{10,11... | collective-permute-start | bytes 152072 | tf_op jit(solution)/shard_map/ppermute | solution.py:359
  73.8 8.2 %collective-permute-start.19 = (bf16[6,48,384]{2,1,0:T(8,128)(2,1)S(1)}, bf16[6,48,384]{2,1,0:T(8,128)(2,1)S(1)}, u32[]{:S(2)}, u32[]{:S(2)}) collective-permute-start(bf16[6,48,384]{2,1,0:T(8,128)(2,1)S(1)} %pad_maximum_fusion.4), channel_id=1, source_target_pairs={{0,4},{1,5},{2,6},{3,7},{4,0},{5,1},{6,2},{7,3},{8,12},{9,13},{10,... | collective-permute-start | bytes 663560 | tf_op jit(solution)/shard_map/ppermute | solution.py:388
  75.4 7.6 %collective-permute-start.20 = (bf16[6,48,384]{2,1,0:T(8,128)(2,1)S(1)}, bf16[6,48,384]{2,1,0:T(8,128)(2,1)S(1)}, u32[]{:S(2)}, u32[]{:S(2)}) collective-permute-start(bf16[6,48,384]{2,1,0:T(8,128)(2,1)S(1)} %pad_maximum_fusion.5), channel_id=1, source_target_pairs={{0,2},{1,3},{2,0},{3,1},{4,6},{5,7},{6,4},{7,5},{8,10},{9,11},{10,... | collective-permute-start | bytes 663560 | tf_op jit(solution)/shard_map/ppermute | solution.py:388
  83.1 8.0 %collective-permute-start.26 = (bf16[64,384]{1,0:T(8,128)(2,1)S(1)}, bf16[64,384]{1,0:T(8,128)(2,1)S(1)}, u32[]{:S(2)}, u32[]{:S(2)}) collective-permute-start(bf16[64,384]{1,0:T(8,128)(2,1)S(1)} %add_convert_fusion.15), channel_id=1, source_target_pairs={{0,8},{1,9},{2,10},{3,11},{4,12},{5,13},{6,14},{7,15},{8,0},{9,1},... | collective-permute-start | bytes 147464 | tf_op jit(solution)/shard_map/ppermute | solution.py:388
  85.0 6.1 %collective-permute-start.25 = (bf16[2,48,384]{2,1,0:T(8,128)(2,1)S(1)}, bf16[2,48,384]{2,1,0:T(8,128)(2,1)S(1)}, u32[]{:S(2)}, u32[]{:S(2)}) collective-permute-start(bf16[2,48,384]{2,1,0:T(8,128)(2,1)S(1)} %get-tuple-element.255), channel_id=1, source_target_pairs={{0,16},{1,17},{2,18},{3,19},{4,20},{5,21},{6,22},{7,23},{8,24},{9,... | collective-permute-start | bytes 221192 | tf_op jit(solution)/shard_map/ppermute | solution.py:388
  86.2 6.2 %collective-permute-start.24 = (bf16[4,48,384]{2,1,0:T(8,128)(2,1)S(1)}, bf16[4,48,384]{2,1,0:T(8,128)(2,1)S(1)}, u32[]{:S(2)}, u32[]{:S(2)}) collective-permute-start(bf16[4,48,384]{2,1,0:T(8,128)(2,1)S(1)} %bitcast.148), channel_id=1, source_target_pairs={{0,8},{1,9},{2,10},{3,11},{4,12},{5,13},{6,14},{7,15},{8,0},{9,1},... | collective-permute-start | bytes 442376 | tf_op jit(solution)/shard_map/ppermute | solution.py:388
  92.6 7.8 %collective-permute-start.27 = (bf16[2,48,384]{2,1,0:T(8,128)(2,1)S(1)}, bf16[2,48,384]{2,1,0:T(8,128)(2,1)S(1)}, u32[]{:S(2)}, u32[]{:S(2)}) collective-permute-start(bf16[2,48,384]{2,1,0:T(8,128)(2,1)S(1)} %get-tuple-element.253), channel_id=1, source_target_pairs={{0,16},{1,17},{2,18},{3,19},{4,20},{5,21},{6,22},{7,23},{8,24},{9,... | collective-permute-start | bytes 221192 | tf_op jit(solution)/shard_map/ppermute | solution.py:388
  94.1 6.3 %collective-permute-start.28 = (bf16[64,384]{1,0:T(8,128)(2,1)S(1)}, bf16[64,384]{1,0:T(8,128)(2,1)S(1)}, u32[]{:S(2)}, u32[]{:S(2)}) collective-permute-start(bf16[64,384]{1,0:T(8,128)(2,1)S(1)} %add_convert_fusion.14), channel_id=1, source_target_pairs={{0,16},{1,17},{2,18},{3,19},{4,20},{5,21},{6,22},{7,23},{8,24},{9,... | collective-permute-start | bytes 147464 | tf_op jit(solution)/shard_map/ppermute | solution.py:388
  100.4 1.3 %collective-permute-start.29 = (bf16[64,384]{1,0:T(8,128)(2,1)S(1)}, bf16[64,384]{1,0:T(8,128)(2,1)S(1)}, u32[]{:S(2)}, u32[]{:S(2)}) collective-permute-start(bf16[64,384]{1,0:T(8,128)(2,1)S(1)} %add_convert_fusion.13.mine), channel_id=1, source_target_pairs={{0,1},{1,0},{2,3},{3,2},{4,5},{5,4},{6,7},{7,6},{8,9},{9,8},{10,11... | collective-permute-start | bytes 147464 | tf_op jit(solution)/shard_map/ppermute | solution.py:388
  (4 other events, 21.9 us)

commit v9 on v8

--- a/solution.py
+++ b/solution.py
@@ -77,23 +77,23 @@
     lax.fori_loop(0, groups * (rows // strip), one_strip, 0)
 
 
-def tap_pass(source, row0, col0, grad, grow0, gcol0, target, first, rows, cols):
-    for g in range(source.shape[0]):
-        lanes = slice(g * LANES, (g + 1) * LANES)
+def tap_pass(source, row0, col0, grad, target, rows, cols):
+    def one_group(g, carry):
+        lines = [grad[g, i] for i in range(rows)]
         for b in range(7):
-            def one_row(i, sums):
-                line = grad[g, grow0 + i, pl.ds(gcol0, cols), :]
-                out = []
+            sums = [None] * 7
+            for r in range(rows + 6):
+                line = source[g, row0 + r, pl.ds(col0 + b, cols), :]
                 for a in range(7):
-                    part = line * source[g, row0 + i + a, pl.ds(col0 + b, cols), :]
-                    out.append(sums[a] + part.reshape(cols // 8, 8, LANES).sum(0))
-                return tuple(out)
-
-            sums = lax.fori_loop(
-                0, rows, one_row, tuple(jnp.zeros((8, LANES), F32) for _ in range(7)), unroll=4
-            )
+                    if 0 <= r - a < rows:
+                        part = lines[r - a] * line
+                        sums[a] = part if sums[a] is None else sums[a] + part
             for a in range(7):
-                target[pl.ds(first + 7 * a + b, 1), lanes] = jnp.sum(sums[a], axis=0, keepdims=True)
+                total = jnp.sum(sums[a], axis=0, keepdims=True)
+                target[g, pl.ds(7 * a + b, 1), :] = total
+        return carry
+
+    lax.fori_loop(0, source.shape[0], one_group, 0)
 
 
 def joined(ref, rows, cols=slice(None)):
@@ -141,6 +141,32 @@
 def hidden_chunks(hidden):
     size = 256 if hidden % 256 == 0 else hidden
     return [slice(start, start + size) for start in range(0, hidden, size)]
+
+
+def hidden_forward(normed, w_in, bias, act, slope):
+    for cut in hidden_chunks(w_in.shape[2]):
+        for block in pixel_blocks(normed.shape[0]):
+            value, factor = gelu_parts(dot_nn(normed[block, :], w_in[0, :, cut]) + bias[:, cut])
+            act[block, cut] = value.astype(BF16)
+            slope[block, cut] = factor
+
+
+def hidden_back(grad, w_out, slope, gpre, db):
+    for cut in hidden_chunks(w_out.shape[2]):
+        bias_sum = None
+        for block in pixel_blocks(grad.shape[0]):
+            gradient = dot_nn(grad[block, :], w_out[0, :, cut]) * slope[block, cut]
+            gpre[block, cut] = gradient.astype(BF16)
+            part = jnp.sum(gradient, axis=0, keepdims=True)
+            bias_sum = part if bias_sum is None else bias_sum + part
+        db[:, cut] = bias_sum
+
+
+def dz_of(gpre, w_in, hat, inv, gain, dz_out, dgain, dshift):
+    dn = dot_nt(gpre[...], w_in[0])
+    dgain[...] = jnp.sum(dn * hat, axis=0, keepdims=True)
+    dshift[...] = jnp.sum(dn, axis=0, keepdims=True)
+    dz_out[...] = norm_back(dn, hat, inv, gain).astype(BF16)
 
 
 def mlp_grads(normed, grad, w_in, b_in, w_out, act, gpre, db):
@@ -184,22 +210,6 @@
     for copy in copies:
         copy.start()
     return copies
-
-
-def block_back(z, grad, layer, gains, shifts, weights, b_in, outs, scratch):
-    dz_out, db, dgain, dshift = outs
-    normed, act, gpre = scratch
-    gain = gains[layer : layer + 1]
-    hat, inv = norm_parts(joined(z, slice(None)))
-    normed[...] = (hat * gain + shifts[layer : layer + 1]).astype(BF16)
-    w_in, w_out, waits = weights
-    for wait in waits:
-        wait.wait()
-    mlp_grads(normed, grad, w_in, b_in.at[layer], w_out, act, gpre, db)
-    dn = dot_nt(gpre[...], w_in[0])
-    dgain[...] = jnp.sum(dn * hat, axis=0, keepdims=True)
-    dshift[...] = jnp.sum(dn, axis=0, keepdims=True)
-    dz_out[...] = norm_back(dn, hat, inv, gain).astype(BF16)
 
 
 def forward_kernel(
@@ -243,24 +253,36 @@
 ):
     waits = fetch_layers(((w_in, 1, w_in1), (w_out, 1, w_out1)), arrived)
     conv_pass(mids, 0, 0, taps.at[1], z, *z.shape[1:3])
-    block_back(
-        z, grad, 1, gains, shifts, (w_in1, w_out1, waits), b_in,
-        (dz_out, db, dgain, dshift), (normed, act, gpre),
-    )
+    hat, inv = norm_parts(joined(z, slice(None)))
+    normed[...] = (hat * gains[1:2] + shifts[1:2]).astype(BF16)
+    for wait in waits:
+        wait.wait()
+    mlp_grads(normed, grad, w_in1, b_in.at[1], w_out1, act, gpre, db)
+    dz_of(gpre, w_in1, hat, inv, gains[1:2], dz_out, dgain, dshift)
+
+
+def again_kernel(z0, gains, shifts, w_in, b_in, hat_out, inv_out, normed, act, slope, w_in0, arrived):
+    (wait,) = fetch_layers(((w_in, 0, w_in0),), arrived)
+    hat, inv = norm_parts(joined(z0, slice(None)))
+    hat_out[...] = hat
+    inv_out[...] = jnp.broadcast_to(inv, inv_out.shape)
+    normed[...] = (hat * gains[0:1] + shifts[0:1]).astype(BF16)
+    wait.wait()
+    hidden_forward(normed, w_in0, b_in.at[0], act, slope)
 
 
 def low_kernel(
-    per, place, dzpad, grad, z0, taps, gains, shifts, w_in, w_out, b_in,
+    per, place, dzpad, grad, hat, inv, normed, act, slope, taps, gains, w_in, w_out,
     gmid, dz_out, db, dgain, dshift, *rest,
 ):
-    *dw, dzs, spread, normed, act, gpre, w_in0, w_out0, arrived = rest
-    waits = fetch_layers(((w_in, 0, w_in0), (w_out, 0, w_out0)), arrived)
+    *dw, dzs, spread, gpre, w_in0, w_out0, arrived = rest
+    waits = fetch_layers(((w_out, 0, w_out0), (w_in, 0, w_in0)), arrived)
     spread_pass(dzpad, dzs, taps.at[1], spread)
     gmid[...] = (grad[...].astype(F32) + joined(spread, slice(None))).astype(BF16)
-    block_back(
-        z0, gmid, 0, gains, shifts, (w_in0, w_out0, waits), b_in,
-        (dz_out, db, dgain, dshift), (normed, act, gpre),
-    )
+    for wait in waits:
+        wait.wait()
+    hidden_back(gmid, w_out0, slope, gpre, db)
+    dz_of(gpre, w_in0, hat[...], inv[:, :1], gains[0:1], dz_out, dgain, dshift)
     weight_grads(place, normed, gmid, act, gpre, dw, per)
 
 
@@ -279,7 +301,7 @@
     out[...] = (gmid[...].astype(F32) + joined(spread, slice(None))).astype(BF16)
 
 
-def small_rows_of(values, row0, col0, dz, dzs, db, dgain, dshift, sums):
+def small_rows_of(values, row0, col0, dz, dzs, taps, db, dgain, dshift, sums):
     rows, cols = dzs.shape[1:3]
     channels = sums.shape[1]
     split_to(dzs, slice(None), dz[...].astype(F32), (rows, cols))
@@ -288,19 +310,21 @@
         sums[k : k + 1, :] = db[:, k * channels : (k + 1) * channels]
     sums[count : count + 1, :] = dgain[...]
     sums[count + 1 : count + 2, :] = dshift[...]
-    tap_pass(values, row0, col0, dzs, 0, 0, sums, count + 2, rows, cols)
+    tap_pass(values, row0, col0, dzs, taps, rows, cols)
+    for g in range(taps.shape[0]):
+        sums[count + 2 : count + 51, g * LANES : (g + 1) * LANES] = taps[g]
 
 
 def taps_kernel(
     place, mids, xpad, dz0, dz1, db0, dgain0, dshift0, db1, dgain1, dshift1, send, keep,
-    xs, dzs, sums0, sums1,
+    xs, dzs, taps, sums0, sums1,
 ):
     for g in range(dzs.shape[0]):
         xs[g] = xpad[:, :, g * LANES : (g + 1) * LANES].astype(F32)
     sums0[...] = jnp.zeros(sums0.shape, F32)
     sums1[...] = jnp.zeros(sums1.shape, F32)
-    small_rows_of(mids, 0, 0, dz1, dzs, db1, dgain1, dshift1, sums1)
-    small_rows_of(xs, HALO, HALO, dz0, dzs, db0, dgain0, dshift0, sums0)
+    small_rows_of(mids, 0, 0, dz1, dzs, taps, db1, dgain1, dshift1, sums1)
+    small_rows_of(xs, HALO, HALO, dz0, dzs, taps, db0, dgain0, dshift0, sums0)
     upper = place[4] == 1
     send[...] = jnp.where(upper, sums0[...], sums1[...]).astype(BF16)
     keep[...] = jnp.where(upper, sums1[...], sums0[...]).astype(BF16)
@@ -342,7 +366,7 @@
         ],
         out_specs=tuple(vmem for _ in outs),
         scratch_shapes=[pltpu.VMEM(s.shape, s.dtype) for s in scratch] + semaphores,
-        compiler_params=pltpu.CompilerParams(vmem_limit_bytes=50 * 1024 * 1024),
+        compiler_params=pltpu.CompilerParams(vmem_limit_bytes=46 * 1024 * 1024),
         name=name,
     )(*args)
 
@@ -382,10 +406,11 @@
     return jnp.concatenate([low, tile, high], axis=axis)
 
 
-def flip_bit(value, bit):
+def flip_bit(value, *bits):
+    flip = sum(1 << bit for bit in bits)
     both = ("rows", "cols")
     total = lax.axis_size("rows") * lax.axis_size("cols")
-    return lax.ppermute(value, both, [(i, i ^ (1 << bit)) for i in range(total)])
+    return lax.ppermute(value, both, [(i, i ^ flip) for i in range(total)])
 
 
 def halves(chunks, dim, mine):
@@ -398,8 +423,11 @@
     return one(mine[1]), one(mine[0])
 
 
-def summed(own, got):
-    return (own.astype(F32) + got.astype(F32)).astype(BF16)
+def summed(own, *got):
+    parts = [part.astype(F32) for part in (own,) + got]
+    while len(parts) > 1:
+        parts = [a + b for a, b in zip(parts[::2], parts[1::2])]
+    return parts[0].astype(BF16)
 
 
 def cut(chunks, order, bit, mine):
@@ -523,20 +551,20 @@
         chunks, order = settled(flight)
         return [step(chunks[i], order, sides[i], mine) for i in range(2)]
 
-    def onward(parts, bit):
+    def onward(parts, bit, *riders):
         kept, sent, lefts = [], [], []
         for chunks, order in parts:
             send, keep, left = cut(chunks, order, bit, mine)
             kept.append(keep)
-            sent.append(send.reshape(-1, per, channels))
+            sent.append(send.reshape(-1, channels))
             lefts.append(left)
-        got = flip_bit(jnp.concatenate(sent, axis=0), bit)
+        got = flip_bit(jnp.concatenate(sent + list(riders), axis=0), bit)
         flights, first = [], 0
         for keep, send, left in zip(kept, sent, lefts):
             came = got[first : first + send.shape[0]].reshape(keep.shape)
             flights.append((keep, came, left))
             first += send.shape[0]
-        return flights
+        return flights, [got[first:]] if riders else []
 
     def merged(flights):
         done = [settled(f) for f in flights]
@@ -553,21 +581,31 @@
         [pltpu.SMEM] + [None] * 4,
         name="weights_top",
     )
-    tile1, twin, other, dw1 = fenced(tile1, twin, other, dw1)
+    tile1, twin, other, dw1, z0 = fenced(tile1, twin, other, dw1, z0)
     wide1 = rimmed(tile1, twin, other, 0, odd_row, outer_row)
     run1 = start(dw1)
     twin, other = edges(wide1, 1, HALO, odd_col)
     twin, other = to_twin(twin, "cols"), to_other(other, "cols")
-    wide1, twin, other, run1 = fenced(wide1, twin, other, run1)
+    tile_f = shape(pixels, channels)
+    again = run(
+        again_kernel,
+        (tile_f, shape(pixels, LANES), tile_b, tile_h, shape(pixels, hidden)),
+        weights[:1],
+        (z0, norm_gains, norm_shifts, w_in, biases),
+        [None] * 3 + [pl.ANY, None],
+        fetched=1,
+        name="again",
+    )
+    wide1, twin, other, run1, again = fenced(wide1, twin, other, run1, again)
     pair1 = fork(run1)
     dzpad1 = filled(rimmed(wide1, twin, other, 1, odd_col, outer_col))
     spread_scratch = [shape(groups, *dzpad1.shape[:2], LANES), tile_z]
     grad_mid, dz0, *rest = run(
         functools.partial(low_kernel, per),
         (tile_b, tile_b) + small_outs + grads_b,
-        spread_scratch + [tile_b, tile_h, tile_h] + weights,
-        (place, dzpad1, grad_flat, z0, taps, norm_gains, norm_shifts, w_in, w_out, biases),
-        [pltpu.SMEM] + [None] * 6 + [pl.ANY] * 2 + [None],
+        spread_scratch + [tile_h] + weights,
+        (place, dzpad1, grad_flat, *again, taps, norm_gains, w_in, w_out),
+        [pltpu.SMEM] + [None] * 9 + [pl.ANY] * 2,
         fetched=2,
         name="low",
     )
@@ -575,42 +613,48 @@
     dz0, dw0, pair1, small0 = fenced(dz0, dw0, pair1, small0)
     run0 = start(dw0)
     low_bit = col_bits + 1
-    pair1 = onward([settled(f) for f in pair1], low_bit)
+    pair1, _ = onward([settled(f) for f in pair1], low_bit)
+    run0, dz0, small0 = fenced(run0, dz0, small0)
+    pair0 = fork(run0)
+    tile0 = dz0.reshape(rows, cols, channels)
+    twin, other = edges(tile0, 0, HALO, odd_row)
+    twin, other = to_twin(twin, "rows"), to_other(other, "rows")
     small_b = shape(small_rows, channels, dtype=BF16)
     small_f = shape(small_rows, channels)
     send, small = run(
         taps_kernel,
         (small_b, small_b),
-        [shape(groups, *xpad.shape[:2], LANES), tile_z, small_f, small_f],
+        [
+            shape(groups, *xpad.shape[:2], LANES), tile_z, shape(groups, 49, LANES),
+            small_f, small_f,
+        ],
         (place, mids, xpad, dz0, dz1, *small0, *small1),
         [pltpu.SMEM] + [None] * 10,
         name="taps",
     )
     small_got = flip_bit(send, 0)
-    run0, small, small_got, dz0 = fenced(run0, small, small_got, dz0)
-    pair0 = fork(run0)
-    tile0 = dz0.reshape(rows, cols, channels)
-    twin, other = edges(tile0, 0, HALO, odd_row)
-    twin, other = to_twin(twin, "rows"), to_other(other, "rows")
-    small = summed(small, small_got)
-    small_got = flip_bit(small, 1)
     pair0, pair1, tile0, twin, other, small, small_got = fenced(
         pair0, pair1, tile0, twin, other, small, small_got
     )
-    both = [onward([settled(pair0[i]), settled(pair1[i])], sides[1 - i]) for i in range(2)]
+    small = summed(small, small_got)
+    for bit in range(1, col_bits - 1):
+        small = summed(small, flip_bit(small, bit))
+    both, small_by = [], []
+    for i in range(2):
+        flights, (came,) = onward([settled(pair0[i]), settled(pair1[i])], sides[1 - i], small)
+        both.append(flights)
+        small_by.append(came)
+    small_by.append(flip_bit(small, *sides))
     wide0 = rimmed(tile0, twin, other, 0, odd_row, outer_row)
     twin, other = edges(wide0, 1, HALO, odd_col)
     twin, other = to_twin(twin, "cols"), to_other(other, "cols")
-    small = summed(small, small_got)
-    small_got = flip_bit(small, 2)
-    both, wide0, twin, other, small, small_got = fenced(both, wide0, twin, other, small, small_got)
-    (run0,) = onward([merged([both[0][0], both[1][0]])], low_bit)
+    both, wide0, twin, other, small, small_by = fenced(both, wide0, twin, other, small, small_by)
+    small = summed(small, small_by[0], small_by[1], small_by[2])
+    (run0,), (small_got,) = onward([merged([both[0][0], both[1][0]])], low_bit, small)
     part1, order1 = merged([both[0][1], both[1][1]])
     flight1 = (part1, jnp.zeros_like(part1), order1)
     if order1:
-        (flight1,) = onward([(part1, order1)], order1[-1])
-    small = summed(small, small_got)
-    small_got = flip_bit(small, 3)
+        (flight1,), _ = onward([(part1, order1)], order1[-1])
     (grad_in,) = run(
         last_kernel,
         (tile_b,),
@@ -618,14 +662,12 @@
         (filled(rimmed(wide0, twin, other, 1, odd_col, outer_col)), grad_mid, taps),
         name="last",
     )
-    for bit in range(4, bits):
+    while run0[2]:
         run0, flight1, small, small_got, grad_in = fenced(run0, flight1, small, small_got, grad_in)
-        if run0[2]:
-            (run0,) = onward([settled(run0)], run0[2][-1])
+        small = summed(small, small_got)
+        (run0,), (small_got,) = onward([settled(run0)], run0[2][-1], small)
         if flight1[2]:
-            (flight1,) = onward([settled(flight1)], flight1[2][-1])
-        small = summed(small, small_got)
-        small_got = flip_bit(small, bit)
+            (flight1,), _ = onward([settled(flight1)], flight1[2][-1])
     run0, flight1, small, small_got = fenced(run0, flight1, small, small_got)
     small = summed(small, small_got)
     small_got = flip_bit(small, 0)

time: 103 us -> 100 us (0.971)
  waiting for transfers between devices: 29.9 us -> 27.6 us
  starting transfers between devices: 34 us -> 32.1 us
  local copies, waits for them, and re-layouts: 1.21 us -> 2.92 us
    ppermute x6, waiting for transfers between devices: 5.31 us -> 3.14 us  [to_other(): return lax.ppermute(edge, ('rows', 'cols'), pairs)]
    ppermute x18 -> x15, starting transfers between devices: 20.5 us -> 18.5 us  [flip_bit(): return lax.ppermute(value, both, [(i, i ^ flip) for i in range(total)])]
    unnamed x14 -> x18, local copies, waits for them, and re-layouts: 0.1 us -> 1.76 us
    convert_element_type x16 -> x15, other arithmetic: 2.5 us -> 1.19 us  [summed(): return parts[0].astype(BF16)]
    ppermute x18 -> x15, waiting for transfers between devices: 19.3 us -> 18.5 us  [flip_bit(): return lax.ppermute(value, both, [(i, i ^ flip) for i in range(total)])]
    pallas_call x8 -> x9, Pallas kernels: 30.6 us -> 30.8 us  [run(): pl.pallas_call(kernel, out_shape=outs, in_specs=[vmem if s is None else p...]
  transfers between devices with their start and end apart: 30 -> 27, of which waited for: 13 -> 11; matrix products, arithmetic and copies ran while one was open for 3% -> 2% of each run, Pallas kernels for 16% -> 15%
where the time goes in v9:
time: 100 us
  starting transfers between devices  32.1 us (32%)
  Pallas kernels  30.8 us (31%)
  waiting for transfers between devices  27.6 us (28%)
  other arithmetic  5.46 us (5%)
  local copies, waits for them, and re-layouts  2.92 us (3%)
  between operations  1.31 us (1%)
    pallas_call x9, Pallas kernels, run(): pl.pallas_call(kernel, out_shape=outs, in_specs=[vmem if s is None else p...  30.8 us
    ppermute x15, waiting for transfers between devices, flip_bit(): return lax.ppermute(value, both, [(i, i ^ flip) for i in range(total)])  18.5 us
    ppermute x15, starting transfers between devices, flip_bit(): return lax.ppermute(value, both, [(i, i ^ flip) for i in range(total)])  18.5 us
    ppermute x6, starting transfers between devices, to_twin(): lax.ppermute(edge, axis, [(i, i ^ 1) for i in range(count) if i ^ 1 < cou...  7.12 us
    ppermute x6, starting transfers between devices, to_other(): return lax.ppermute(edge, ('rows', 'cols'), pairs)  6.5 us
    ppermute x6, waiting for transfers between devices, to_twin(): lax.ppermute(edge, axis, [(i, i ^ 1) for i in range(count) if i ^ 1 < cou...  6.01 us
    ppermute x6, waiting for transfers between devices, to_other(): return lax.ppermute(edge, ('rows', 'cols'), pairs)  3.14 us
  transfers between devices with their start and end apart: 27, of which 11 were waited for; matrix products, arithmetic and copies ran while one was open for 2% of the time, Pallas kernels for 15%

profile of v9, /device:TPU:0, one launch (start us, length us, event | category | flops | bytes accessed | tf_op | source)
XLA Modules:
  0.0 100.2 jit_solution(8196889347333408182)
XLA Ops:
  1.6 3.0 %collective-permute-start = (bf16[6,16,384]{2,1,0:T(8,128)(2,1)S(1)}, bf16[6,16,384]{2,1,0:T(8,128)(2,1)S(1)}, u32[]{:S(2)}, u32[]{:S(2)}) collective-permute-start(bf16[6,16,384]{2,1,0:T(8,128)(2,1)S(1)} %get-tuple-element.280), channel_id=1, source_target_pairs={{0,4},{4,0},{8,12},{12,8},{16,20},{20,16},{24,28},{28,24},{1,5},{5... | collective-permute-start | bytes 221192 | tf_op jit(solution)/shard_map/ppermute | solution.py:383
  4.7 3.4 %collective-permute-done = bf16[6,16,384]{2,1,0:T(8,128)(2,1)S(1)} collective-permute-done((bf16[6,16,384]{2,1,0:T(8,128)(2,1)S(1)}, bf16[6,16,384]{2,1,0:T(8,128)(2,1)S(1)}, u32[]{:S(2)}, u32[]{:S(2)}) %collective-permute-start) | collective-permute-done | bytes 73760 | tf_op jit(solution)/shard_map/ppermute | solution.py:383
  8.1 1.0 pad_maximum_fusion.2
  9.8 2.4 %collective-permute-start.3 = (bf16[28,6,384]{2,1,0:T(8,128)(2,1)S(1)}, bf16[28,6,384]{2,1,0:T(8,128)(2,1)}, u32[]{:S(2)}, u32[]{:S(2)}) collective-permute-start(bf16[28,6,384]{2,1,0:T(8,128)(2,1)S(1)} %get-tuple-element.257), channel_id=1, source_target_pairs={{0,4},{1,2},{2,1},{3,7},{4,0},{5,6},{6,5},{7,3},{8,12},{9,10},{10,... | collective-permute-start | bytes 387080 | tf_op jit(solution)/shard_map/ppermute | solution.py:399
  12.6 3.1 %collective-permute-done.3 = bf16[28,6,384]{2,1,0:T(8,128)(2,1)} collective-permute-done((bf16[28,6,384]{2,1,0:T(8,128)(2,1)S(1)}, bf16[28,6,384]{2,1,0:T(8,128)(2,1)}, u32[]{:S(2)}, u32[]{:S(2)}) %collective-permute-start.3) | collective-permute-done | bytes 129056 | tf_op jit(solution)/shard_map/ppermute | solution.py:399
  16.2 1.7 %copy-done.1 = bf16[2,384,1536]{2,1,0:T(8,128)(2,1)S(1)} copy-done((bf16[2,384,1536]{2,1,0:T(8,128)(2,1)S(1)}, bf16[2,384,1536]{2,1,0:T(8,128)(2,1)}, u32[]{:S(2)}) %copy-start.1) | copy-done | bytes 2359320
  17.8 9.1 %forward.1 = (f32[3,22,24,128]{3,2,1,0:T(8,128)S(1)}, f32[3,16,16,128]{3,2,1,0:T(8,128)S(1)}) custom-call(s32[5]{0:T(128)S(1)} %stack.25.place, bf16[28,32,384]{2,1,0:T(8,128)(2,1)S(1)} %fusion.12.xpad, f32[2,3,49,128]{3,2,1,0:T(8,128)S(1)} %bitcast.103, f32[2,384]{1,0:T(2,128)S(1)} %copy-done.3, f32[2,384]{1,0:T(2,128)S(1)} %copy-done.4, ...), custom_call_target="tpu_custom_call" | custom-call | tf_op jit(solution)/shard_map/forward/pallas_call | solution.py:361
  27.0 5.2 %top.1 = (bf16[256,384]{1,0:T(8,128)(2,1)S(1)}, bf16[256,384]{1,0:T(8,128)(2,1)S(1)}, bf16[256,1536]{1,0:T(8,128)(2,1)S(1)}, bf16[256,1536]{1,0:T(8,128)(2,1)S(1...) custom-call(f32[3,22,24,128]{3,2,1,0:T(8,128)S(1)} %get-tuple-element.129.mids, ...), custom_call_target="tpu_custom_call" | custom-call | tf_op jit(solution)/shard_map/top/pallas_call | solution.py:361
  32.2 2.1 %collective-permute-start.4 = (bf16[3,16,384]{2,1,0:T(8,128)(2,1)S(1)}, bf16[3,16,384]{2,1,0:T(8,128)(2,1)S(1)}, u32[]{:S(2)}, u32[]{:S(2)}) collective-permute-start(bf16[3,16,384]{2,1,0:T(8,128)(2,1)S(1)} %bitcast.152), channel_id=1, source_target_pairs={{0,4},{4,0},{8,12},{12,8},{16,20},{20,16},{24,28},{28,24},{1,5},{5... | collective-permute-start | bytes 110600 | tf_op jit(solution)/shard_map/ppermute | solution.py:383
  35.0 1.6 %weights_top.1 = (bf16[2,768,384]{2,1,0:T(8,128)(2,1)S(1)}, bf16[2,768,384]{2,1,0:T(8,128)(2,1)S(1)}) custom-call(s32[5]{0:T(128)S(1)} %stack.25.place, bf16[256,384]{1,0:T(8,128)(2,1)S(1)} %get-tuple-element.131.normed, bf16[256,1536]{1,0:T(8,128)(2,1)S(1)} %get-tuple-element.132.act, bf16[256,1536]{1,0:T(8,128)(2,1)S(1)} %get-tuple-element.133.gpre, ...), custom_call_target="tpu_custom_call" | custom-call | tf_op jit(solution)/shard_map/weights_top/pallas_call | solution.py:361
  37.4 3.0 %collective-permute-start.7 = (bf16[22,3,384]{2,1,0:T(4,128)(2,1)S(1)}, bf16[22,3,384]{2,1,0:T(4,128)(2,1)S(1)}, u32[]{:S(2)}, u32[]{:S(2)}) collective-permute-start(bf16[22,3,384]{2,1,0:T(4,128)(2,1)S(1)} %get-tuple-element.273), channel_id=1, source_target_pairs={{0,4},{1,2},{2,1},{3,7},{4,0},{5,6},{6,5},{7,3},{8,12},{9,10},{10,... | collective-permute-start | bytes 152072 | tf_op jit(solution)/shard_map/ppermute | solution.py:399
  40.4 2.4 %again.1 = (f32[256,384]{1,0:T(8,128)S(1)}, f32[256,128]{1,0:T(8,128)S(1)}, bf16[256,384]{1,0:T(8,128)(2,1)S(1)}, bf16[256,1536]{1,0:T(8,128)(2,1)S(1)}, f32[256,1536]{1,0:T(8,128)S(1)}) custom-call(f32[3,16,16,128]{3,2,1,0:T(8,128)S(1)} %get-tuple-element.143.z0, f32[2,384]{1,0:T(2,128)S(1)} %copy-done.3, f32[2,384]{1,0:T(2,128)S(1)} %copy-done.4, ...), custom_call_target="tpu_custom_call" | custom-call | tf_op jit(solution)/shard_map/again/pallas_call | solution.py:361
  43.4 1.9 %collective-permute-start.10 = (bf16[1,4,2,48,384]{4,3,2,1,0:T(8,128)(2,1)S(1)}, bf16[1,4,2,48,384]{4,3,2,1,0:T(8,128)(2,1)S(1)}, u32[]{:S(2)}, u32[]{:S(2)}) collective-permute-start(bf16[1,4,2,48,384]{4,3,2,1,0:T(8,128)(2,1)S(1)} %get-tuple-element.251), channel_id=1, source_target_pairs={{0,4},{1,5},{2,6},{3,7},{4,0},{5,1},{6,2},{7,3},{8,12},{9,13},{10,... | collective-permute-start | bytes 884744 | tf_op jit(solution)/shard_map/ppermute | solution.py:413
  45.4 1.0 collective-permute-start.9
  46.7 4.4 %low.1 = (bf16[256,384]{1,0:T(8,128)(2,1)S(1)}, bf16[256,384]{1,0:T(8,128)(2,1)S(1)}, f32[1,1536]{1,0:T(1,128)S(1)}, f32[1,384]{1,0:T(1,128)S(1)}, f32[1,384]{1,...) custom-call(s32[5]{0:T(128)S(1)} %stack.25.place, ...), custom_call_target="tpu_custom_call" | custom-call | tf_op jit(solution)/shard_map/low/pallas_call | solution.py:361
  51.1 1.2 %collective-permute-done.10 = bf16[1,4,2,48,384]{4,3,2,1,0:T(8,128)(2,1)S(1)} collective-permute-done((bf16[1,4,2,48,384]{4,3,2,1,0:T(8,128)(2,1)S(1)}, bf16[1,4,2,48,384]{4,3,2,1,0:T(8,128)(2,1)S(1)}, u32[]{:S(2)}, u32[]{:S(2)}) %collective-permute-start.10) | collective-permute-done | bytes 294944 | tf_op jit(solution)/shard_map/ppermute | solution.py:413
  52.3 1.6 %collective-permute-done.9 = bf16[1,8,1,48,384]{4,3,1,2,0:T(8,128)(2,1)S(1)} collective-permute-done((bf16[1,8,1,48,384]{4,3,1,2,0:T(8,128)(2,1)S(1)}, bf16[1,8,1,48,384]{4,3,1,2,0:T(8,128)(2,1)S(1)}, u32[]{:S(2)}, u32[]{:S(2)}) %collective-permute-start.9) | collective-permute-done | bytes 294944 | tf_op jit(solution)/shard_map/ppermute | solution.py:413
  54.2 2.8 %collective-permute-start.14 = (bf16[384,384]{1,0:T(8,128)(2,1)S(1)}, bf16[384,384]{1,0:T(8,128)(2,1)S(1)}, u32[]{:S(2)}, u32[]{:S(2)}) collective-permute-start(bf16[384,384]{1,0:T(8,128)(2,1)S(1)} %pad_maximum_fusion.3), channel_id=1, source_target_pairs={{0,8},{1,9},{2,10},{3,11},{4,12},{5,13},{6,14},{7,15},{8,0},{9,1},... | collective-permute-start | bytes 884744 | tf_op jit(solution)/shard_map/ppermute | solution.py:413
  58.3 1.1 %collective-permute-start.12 = (bf16[1,8,1,48,384]{4,3,1,2,0:T(8,128)(2,1)S(1)}, bf16[1,8,1,48,384]{4,3,1,2,0:T(8,128)(2,1)S(1)}, u32[]{:S(2)}, u32[]{:S(2)}) collective-permute-start(bf16[1,8,1,48,384]{4,3,1,2,0:T(8,128)(2,1)S(1)} %get-tuple-element.249), channel_id=1, source_target_pairs={{0,2},{1,3},{2,0},{3,1},{4,6},{5,7},{6,4},{7,5},{8,10},{9,11},{10,... | collective-permute-start | bytes 884744 | tf_op jit(solution)/shard_map/ppermute | solution.py:413
  59.4 3.7 %taps.1 = (bf16[64,384]{1,0:T(8,128)(2,1)S(1)}, bf16[64,384]{1,0:T(8,128)(2,1)S(1)}) custom-call(s32[5]{0:T(128)S(1)} %stack.25.place, f32[3,22,24,128]{3,2,1,0:T(8,128)S(1)} %get-tuple-element.129.mids, bf16[28,32,384]{2,1,0:T(8,128)(2,1)S(1)} %fusion.12.xpad, bf16[256,384]{1,0:T(8,128)(2,1)S(1)} %get-tuple-element.184.dz0, ...), custom_call_target="tpu_custom_call" | custom-call | tf_op jit(solution)/shard_map/taps/pallas_call | solution.py:361
  63.3 1.4 %collective-permute-start.15 = (bf16[3,16,384]{2,1,0:T(8,128)(2,1)S(1)}, bf16[3,16,384]{2,1,0:T(8,128)(2,1)S(1)}, u32[]{:S(2)}, u32[]{:S(2)}) collective-permute-start(bf16[3,16,384]{2,1,0:T(8,128)(2,1)S(1)} %bitcast.150), channel_id=1, source_target_pairs={{0,4},{4,0},{8,12},{12,8},{16,20},{20,16},{24,28},{28,24},{1,5},{5... | collective-permute-start | bytes 110600 | tf_op jit(solution)/shard_map/ppermute | solution.py:383
  64.9 2.6 %collective-permute-done.15 = bf16[3,16,384]{2,1,0:T(8,128)(2,1)S(1)} collective-permute-done((bf16[3,16,384]{2,1,0:T(8,128)(2,1)S(1)}, bf16[3,16,384]{2,1,0:T(8,128)(2,1)S(1)}, u32[]{:S(2)}, u32[]{:S(2)}) %collective-permute-start.15) | collective-permute-done | bytes 36896 | tf_op jit(solution)/shard_map/ppermute | solution.py:383
  68.1 3.1 %collective-permute-start.18 = (bf16[352,384]{1,0:T(8,128)(2,1)S(1)}, bf16[352,384]{1,0:T(8,128)(2,1)S(1)}, u32[]{:S(2)}, u32[]{:S(2)}) collective-permute-start(bf16[352,384]{1,0:T(8,128)(2,1)S(1)} %get-tuple-element.300), channel_id=1, source_target_pairs={{0,4},{1,5},{2,6},{3,7},{4,0},{5,1},{6,2},{7,3},{8,12},{9,13},{10,... | collective-permute-start | bytes 811016 | tf_op jit(solution)/shard_map/ppermute | solution.py:413
  71.1 1.0 %collective-permute-start.19 = (bf16[352,384]{1,0:T(8,128)(2,1)S(1)}, bf16[352,384]{1,0:T(8,128)(2,1)S(1)}, u32[]{:S(2)}, u32[]{:S(2)}) collective-permute-start(bf16[352,384]{1,0:T(8,128)(2,1)S(1)} %get-tuple-element.299), channel_id=1, source_target_pairs={{0,2},{1,3},{2,0},{3,1},{4,6},{5,7},{6,4},{7,5},{8,10},{9,11},{10,... | collective-permute-start | bytes 811016 | tf_op jit(solution)/shard_map/ppermute | solution.py:413
  72.5 1.5 %collective-permute-start.22 = (bf16[64,384]{1,0:T(8,128)(2,1)S(1)}, bf16[64,384]{1,0:T(8,128)(2,1)S(1)}, u32[]{:S(2)}, u32[]{:S(2)}) collective-permute-start(bf16[64,384]{1,0:T(8,128)(2,1)S(1)} %add_convert_fusion.16), channel_id=1, source_target_pairs={{0,6},{1,7},{2,4},{3,5},{4,2},{5,3},{6,0},{7,1},{8,14},{9,15},{10,... | collective-permute-start | bytes 147464 | tf_op jit(solution)/shard_map/ppermute | solution.py:413
  74.0 3.0 %collective-permute-done.18 = bf16[352,384]{1,0:T(8,128)(2,1)S(1)} collective-permute-done((bf16[352,384]{1,0:T(8,128)(2,1)S(1)}, bf16[352,384]{1,0:T(8,128)(2,1)S(1)}, u32[]{:S(2)}, u32[]{:S(2)}) %collective-permute-start.18) | collective-permute-done | bytes 270368 | tf_op jit(solution)/shard_map/ppermute | solution.py:413
  77.1 1.9 %collective-permute-done.19 = bf16[352,384]{1,0:T(8,128)(2,1)S(1)} collective-permute-done((bf16[352,384]{1,0:T(8,128)(2,1)S(1)}, bf16[352,384]{1,0:T(8,128)(2,1)S(1)}, u32[]{:S(2)}, u32[]{:S(2)}) %collective-permute-start.19) | collective-permute-done | bytes 270368 | tf_op jit(solution)/shard_map/ppermute | solution.py:413
  80.2 3.9 %collective-permute-start.24 = (bf16[96,384]{1,0:T(8,128)(2,1)S(1)}, bf16[96,384]{1,0:T(8,128)(2,1)S(1)}, u32[]{:S(2)}, u32[]{:S(2)}) collective-permute-start(bf16[96,384]{1,0:T(8,128)(2,1)S(1)} %bitcast.148), channel_id=1, source_target_pairs={{0,16},{1,17},{2,18},{3,19},{4,20},{5,21},{6,22},{7,23},{8,24},{9,... | collective-permute-start | bytes 221192 | tf_op jit(solution)/shard_map/ppermute | solution.py:413
  85.1 2.4 %last.1 = bf16[256,384]{1,0:T(8,128)(2,1)} custom-call(bf16[22,32,384]{2,1,0:T(8,128)(2,1)S(1)} %fusion.18.dzpad, bf16[256,384]{1,0:T(8,128)(2,1)S(1)} %get-tuple-element.223.gmid, f32[2,3,49,128]{3,2,1,0:T(8,128)S(1)} %bitcast.106), custom_call_target="tpu_custom_call" | custom-call | tf_op jit(solution)/shard_map/last/pallas_call | solution.py:361
  87.5 2.8 %collective-permute-done.23 = bf16[256,384]{1,0:T(8,128)(2,1)S(1)} collective-permute-done((bf16[256,384]{1,0:T(8,128)(2,1)S(1)}, bf16[256,384]{1,0:T(8,128)(2,1)S(1)}, u32[]{:S(2)}, u32[]{:S(2)}) %collective-permute-start.23) | collective-permute-done | bytes 196640 | tf_op jit(solution)/shard_map/ppermute | solution.py:413
  91.2 6.4 %collective-permute-done.25 = bf16[160,384]{1,0:T(8,128)(2,1)S(1)} collective-permute-done((bf16[160,384]{1,0:T(8,128)(2,1)S(1)}, bf16[160,384]{1,0:T(8,128)(2,1)S(1)}, u32[]{:S(2)}, u32[]{:S(2)}) %collective-permute-start.25) | collective-permute-done | bytes 122912 | tf_op jit(solution)/shard_map/ppermute | solution.py:413
  98.9 1.3 %small.1 = (f32[49,2,384]{2,1,0:T(2,128)}, f32[2,384]{1,0:T(2,128)}, f32[2,384]{1,0:T(2,128)}, f32[2,1536]{1,0:T(2,128)}) custom-call(s32[5]{0:T(128)S(1)} %stack.25.place, bf16[64,384]{1,0:T(8,128)(2,1)S(1)} %add_convert_fusion.13.mine, bf16[64,384]{1,0:T(8,128)(2,1)S(1)} %collective-permute-done.26.got), custom_call_target="tpu_custom_call" | custom-call | tf_op jit(solution)/shard_map/small/pallas_call | solution.py:361
  (118 shorter events, 11.8 us)
Async XLA Ops:
  0.6 11.6 %copy-start.6 = (f32[2,7,7,384]{3,0,2,1:T(2,128)S(1)}, f32[2,7,7,384]{3,0,2,1:T(2,128)}, u32[]{:S(2)}) copy-start(f32[2,7,7,384]{3,0,2,1:T(2,128)} %param.10) | copy-start | bytes 451588
  1.6 6.4 %collective-permute-start = (bf16[6,16,384]{2,1,0:T(8,128)(2,1)S(1)}, bf16[6,16,384]{2,1,0:T(8,128)(2,1)S(1)}, u32[]{:S(2)}, u32[]{:S(2)}) collective-permute-start(bf16[6,16,384]{2,1,0:T(8,128)(2,1)S(1)} %get-tuple-element.280), channel_id=1, source_target_pairs={{0,4},{4,0},{8,12},{12,8},{16,20},{20,16},{24,28},{28,24},{1,5},{5... | collective-permute-start | bytes 221192 | tf_op jit(solution)/shard_map/ppermute | solution.py:383
  4.7 3.4 %collective-permute-start.1 = (bf16[6,16,384]{2,1,0:T(8,128)(2,1)S(1)}, bf16[6,16,384]{2,1,0:T(8,128)(2,1)S(1)}, u32[]{:S(2)}, u32[]{:S(2)}) collective-permute-start(bf16[6,16,384]{2,1,0:T(8,128)(2,1)S(1)} %get-tuple-element.279), channel_id=1, source_target_pairs={{0,1},{1,0},{2,3},{3,2},{4,8},{5,9},{6,10},{7,11},{8,4},{9,5},{10,... | collective-permute-start | bytes 221192 | tf_op jit(solution)/shard_map/ppermute | solution.py:399
  4.7 7.8 %copy-start.7 = (f32[2,1536]{1,0:T(2,128)S(1)}, f32[2,1536]{1,0:T(2,128)}, u32[]{:S(2)}) copy-start(f32[2,1536]{1,0:T(2,128)} %param.14) | copy-start | bytes 36868
  9.0 6.8 %copy-start.5 = (bf16[16,16,384]{2,1,0:T(8,128)(2,1)S(1)}, bf16[16,16,384]{2,1,0:T(8,128)(2,1)}, u32[]{:S(2)}) copy-start(bf16[16,16,384]{2,1,0:T(8,128)(2,1)} %param.8) | copy-start | bytes 589828
  9.8 2.8 %collective-permute-start.2 = (bf16[28,6,384]{2,1,0:T(8,128)(2,1)}, bf16[28,6,384]{2,1,0:T(8,128)(2,1)S(1)}, u32[]{:S(2)}, u32[]{:S(2)}) collective-permute-start(bf16[28,6,384]{2,1,0:T(8,128)(2,1)} %get-tuple-element.258), channel_id=1, source_target_pairs={{0,1},{1,0},{2,3},{3,2},{4,5},{5,4},{6,7},{7,6},{8,9},{9,8},{10,11... | collective-permute-start | bytes 387080 | tf_op jit(solution)/shard_map/ppermute | solution.py:383
  9.8 5.9 %collective-permute-start.3 = (bf16[28,6,384]{2,1,0:T(8,128)(2,1)S(1)}, bf16[28,6,384]{2,1,0:T(8,128)(2,1)}, u32[]{:S(2)}, u32[]{:S(2)}) collective-permute-start(bf16[28,6,384]{2,1,0:T(8,128)(2,1)S(1)} %get-tuple-element.257), channel_id=1, source_target_pairs={{0,4},{1,2},{2,1},{3,7},{4,0},{5,6},{6,5},{7,3},{8,12},{9,10},{10,... | collective-permute-start | bytes 387080 | tf_op jit(solution)/shard_map/ppermute | solution.py:399
  12.4 3.7 %copy-start = (bf16[2,384,1536]{2,1,0:T(8,128)(2,1)S(1)}, bf16[2,384,1536]{2,1,0:T(8,128)(2,1)}, u32[]{:S(2)}) copy-start(bf16[2,384,1536]{2,1,0:T(8,128)(2,1)} %w_in.7) | copy-start | bytes 7077892
  17.8 9.1 %copy-start.2 = (bf16[16,16,384]{2,1,0:T(8,128)(2,1)S(1)}, bf16[16,16,384]{2,1,0:T(8,128)(2,1)}, u32[]{:S(2)}) copy-start(bf16[16,16,384]{2,1,0:T(8,128)(2,1)} %param.9) | copy-start | bytes 589828
  32.2 4.4 %collective-permute-start.4 = (bf16[3,16,384]{2,1,0:T(8,128)(2,1)S(1)}, bf16[3,16,384]{2,1,0:T(8,128)(2,1)S(1)}, u32[]{:S(2)}, u32[]{:S(2)}) collective-permute-start(bf16[3,16,384]{2,1,0:T(8,128)(2,1)S(1)} %bitcast.152), channel_id=1, source_target_pairs={{0,4},{4,0},{8,12},{12,8},{16,20},{20,16},{24,28},{28,24},{1,5},{5... | collective-permute-start | bytes 110600 | tf_op jit(solution)/shard_map/ppermute | solution.py:383
  34.3 2.3 %collective-permute-start.5 = (bf16[3,16,384]{2,1,0:T(8,128)(2,1)S(1)}, bf16[3,16,384]{2,1,0:T(8,128)(2,1)S(1)}, u32[]{:S(2)}, u32[]{:S(2)}) collective-permute-start(bf16[3,16,384]{2,1,0:T(8,128)(2,1)S(1)} %bitcast.151), channel_id=1, source_target_pairs={{0,1},{1,0},{2,3},{3,2},{4,8},{5,9},{6,10},{7,11},{8,4},{9,5},{10,... | collective-permute-start | bytes 110600 | tf_op jit(solution)/shard_map/ppermute | solution.py:399
  36.6 6.2 %collective-permute-start.8 = (bf16[2,16,48,384]{3,2,1,0:T(8,128)(2,1)S(1)}, bf16[2,16,48,384]{3,2,1,0:T(8,128)(2,1)S(1)}, u32[]{:S(2)}, u32[]{:S(2)}) collective-permute-start(bf16[2,16,48,384]{3,2,1,0:T(8,128)(2,1)S(1)} %bitcast.118), channel_id=1, source_target_pairs={{0,1},{1,0},{2,3},{3,2},{4,5},{5,4},{6,7},{7,6},{8,9},{9,8},{10,11... | collective-permute-start | bytes 3538952 | tf_op jit(solution)/shard_map/ppermute | solution.py:413
  36.9 6.0 %collective-permute-start.6 = (bf16[22,3,384]{2,1,0:T(4,128)(2,1)S(1)}, bf16[22,3,384]{2,1,0:T(4,128)(2,1)S(1)}, u32[]{:S(2)}, u32[]{:S(2)}) collective-permute-start(bf16[22,3,384]{2,1,0:T(4,128)(2,1)S(1)} %get-tuple-element.274), channel_id=1, source_target_pairs={{0,1},{1,0},{2,3},{3,2},{4,5},{5,4},{6,7},{7,6},{8,9},{9,8},{10,11... | collective-permute-start | bytes 152072 | tf_op jit(solution)/shard_map/ppermute | solution.py:383
  37.4 5.4 %collective-permute-start.7 = (bf16[22,3,384]{2,1,0:T(4,128)(2,1)S(1)}, bf16[22,3,384]{2,1,0:T(4,128)(2,1)S(1)}, u32[]{:S(2)}, u32[]{:S(2)}) collective-permute-start(bf16[22,3,384]{2,1,0:T(4,128)(2,1)S(1)} %get-tuple-element.273), channel_id=1, source_target_pairs={{0,4},{1,2},{2,1},{3,7},{4,0},{5,6},{6,5},{7,3},{8,12},{9,10},{10,... | collective-permute-start | bytes 152072 | tf_op jit(solution)/shard_map/ppermute | solution.py:399
  43.4 8.9 %collective-permute-start.10 = (bf16[1,4,2,48,384]{4,3,2,1,0:T(8,128)(2,1)S(1)}, bf16[1,4,2,48,384]{4,3,2,1,0:T(8,128)(2,1)S(1)}, u32[]{:S(2)}, u32[]{:S(2)}) collective-permute-start(bf16[1,4,2,48,384]{4,3,2,1,0:T(8,128)(2,1)S(1)} %get-tuple-element.251), channel_id=1, source_target_pairs={{0,4},{1,5},{2,6},{3,7},{4,0},{5,1},{6,2},{7,3},{8,12},{9,13},{10,... | collective-permute-start | bytes 884744 | tf_op jit(solution)/shard_map/ppermute | solution.py:413
  45.4 8.5 %collective-permute-start.9 = (bf16[1,8,1,48,384]{4,3,1,2,0:T(8,128)(2,1)S(1)}, bf16[1,8,1,48,384]{4,3,1,2,0:T(8,128)(2,1)S(1)}, u32[]{:S(2)}, u32[]{:S(2)}) collective-permute-start(bf16[1,8,1,48,384]{4,3,1,2,0:T(8,128)(2,1)S(1)} %get-tuple-element.253), channel_id=1, source_target_pairs={{0,2},{1,3},{2,0},{3,1},{4,6},{5,7},{6,4},{7,5},{8,10},{9,11},{10,... | collective-permute-start | bytes 884744 | tf_op jit(solution)/shard_map/ppermute | solution.py:413
  53.9 3.1 %collective-permute-start.11 = (bf16[2,16,48,384]{3,2,1,0:T(8,128)(2,1)S(1)}, bf16[2,16,48,384]{3,2,1,0:T(8,128)(2,1)S(1)}, u32[]{:S(2)}, u32[]{:S(2)}) collective-permute-start(bf16[2,16,48,384]{3,2,1,0:T(8,128)(2,1)S(1)} %bitcast.119), channel_id=1, source_target_pairs={{0,1},{1,0},{2,3},{3,2},{4,5},{5,4},{6,7},{7,6},{8,9},{9,8},{10,11... | collective-permute-start | bytes 3538952 | tf_op jit(solution)/shard_map/ppermute | solution.py:413
  54.2 10.5 %collective-permute-start.14 = (bf16[384,384]{1,0:T(8,128)(2,1)S(1)}, bf16[384,384]{1,0:T(8,128)(2,1)S(1)}, u32[]{:S(2)}, u32[]{:S(2)}) collective-permute-start(bf16[384,384]{1,0:T(8,128)(2,1)S(1)} %pad_maximum_fusion.3), channel_id=1, source_target_pairs={{0,8},{1,9},{2,10},{3,11},{4,12},{5,13},{6,14},{7,15},{8,0},{9,1},... | collective-permute-start | bytes 884744 | tf_op jit(solution)/shard_map/ppermute | solution.py:413
  57.5 10.0 %collective-permute-start.13 = (bf16[1,4,2,48,384]{4,3,1,2,0:T(8,128)(2,1)S(1)}, bf16[1,4,2,48,384]{4,3,1,2,0:T(8,128)(2,1)S(1)}, u32[]{:S(2)}, u32[]{:S(2)}) collective-permute-start(bf16[1,4,2,48,384]{4,3,1,2,0:T(8,128)(2,1)S(1)} %bitcast.145), channel_id=1, source_target_pairs={{0,4},{1,5},{2,6},{3,7},{4,0},{5,1},{6,2},{7,3},{8,12},{9,13},{10,... | collective-permute-start | bytes 884744 | tf_op jit(solution)/shard_map/ppermute | solution.py:413
  58.3 9.2 %collective-permute-start.12 = (bf16[1,8,1,48,384]{4,3,1,2,0:T(8,128)(2,1)S(1)}, bf16[1,8,1,48,384]{4,3,1,2,0:T(8,128)(2,1)S(1)}, u32[]{:S(2)}, u32[]{:S(2)}) collective-permute-start(bf16[1,8,1,48,384]{4,3,1,2,0:T(8,128)(2,1)S(1)} %get-tuple-element.249), channel_id=1, source_target_pairs={{0,2},{1,3},{2,0},{3,1},{4,6},{5,7},{6,4},{7,5},{8,10},{9,11},{10,... | collective-permute-start | bytes 884744 | tf_op jit(solution)/shard_map/ppermute | solution.py:413
  63.2 4.3 %collective-permute-start.17 = (bf16[64,384]{1,0:T(8,128)(2,1)S(1)}, bf16[64,384]{1,0:T(8,128)(2,1)S(1)}, u32[]{:S(2)}, u32[]{:S(2)}) collective-permute-start(bf16[64,384]{1,0:T(8,128)(2,1)S(1)} %get-tuple-element.192), channel_id=1, source_target_pairs={{0,1},{1,0},{2,3},{3,2},{4,5},{5,4},{6,7},{7,6},{8,9},{9,8},{10,11... | collective-permute-start | bytes 147464 | tf_op jit(solution)/shard_map/ppermute | solution.py:413
  63.3 4.3 %collective-permute-start.15 = (bf16[3,16,384]{2,1,0:T(8,128)(2,1)S(1)}, bf16[3,16,384]{2,1,0:T(8,128)(2,1)S(1)}, u32[]{:S(2)}, u32[]{:S(2)}) collective-permute-start(bf16[3,16,384]{2,1,0:T(8,128)(2,1)S(1)} %bitcast.150), channel_id=1, source_target_pairs={{0,4},{4,0},{8,12},{12,8},{16,20},{20,16},{24,28},{28,24},{1,5},{5... | collective-permute-start | bytes 110600 | tf_op jit(solution)/shard_map/ppermute | solution.py:383
  64.7 2.9 %collective-permute-start.16 = (bf16[3,16,384]{2,1,0:T(8,128)(2,1)S(1)}, bf16[3,16,384]{2,1,0:T(8,128)(2,1)S(1)}, u32[]{:S(2)}, u32[]{:S(2)}) collective-permute-start(bf16[3,16,384]{2,1,0:T(8,128)(2,1)S(1)} %bitcast.149), channel_id=1, source_target_pairs={{0,1},{1,0},{2,3},{3,2},{4,8},{5,9},{6,10},{7,11},{8,4},{9,5},{10,... | collective-permute-start | bytes 110600 | tf_op jit(solution)/shard_map/ppermute | solution.py:399
  68.1 9.0 %collective-permute-start.18 = (bf16[352,384]{1,0:T(8,128)(2,1)S(1)}, bf16[352,384]{1,0:T(8,128)(2,1)S(1)}, u32[]{:S(2)}, u32[]{:S(2)}) collective-permute-start(bf16[352,384]{1,0:T(8,128)(2,1)S(1)} %get-tuple-element.300), channel_id=1, source_target_pairs={{0,4},{1,5},{2,6},{3,7},{4,0},{5,1},{6,2},{7,3},{8,12},{9,13},{10,... | collective-permute-start | bytes 811016 | tf_op jit(solution)/shard_map/ppermute | solution.py:413
  71.1 7.9 %collective-permute-start.19 = (bf16[352,384]{1,0:T(8,128)(2,1)S(1)}, bf16[352,384]{1,0:T(8,128)(2,1)S(1)}, u32[]{:S(2)}, u32[]{:S(2)}) collective-permute-start(bf16[352,384]{1,0:T(8,128)(2,1)S(1)} %get-tuple-element.299), channel_id=1, source_target_pairs={{0,2},{1,3},{2,0},{3,1},{4,6},{5,7},{6,4},{7,5},{8,10},{9,11},{10,... | collective-permute-start | bytes 811016 | tf_op jit(solution)/shard_map/ppermute | solution.py:413
  72.3 7.8 %collective-permute-start.20 = (bf16[22,3,384]{2,1,0:T(4,128)(2,1)S(1)}, bf16[22,3,384]{2,1,0:T(4,128)(2,1)S(1)}, u32[]{:S(2)}, u32[]{:S(2)}) collective-permute-start(bf16[22,3,384]{2,1,0:T(4,128)(2,1)S(1)} %get-tuple-element.272), channel_id=1, source_target_pairs={{0,1},{1,0},{2,3},{3,2},{4,5},{5,4},{6,7},{7,6},{8,9},{9,8},{10,11... | collective-permute-start | bytes 152072 | tf_op jit(solution)/shard_map/ppermute | solution.py:383
  72.4 7.7 %collective-permute-start.21 = (bf16[22,3,384]{2,1,0:T(4,128)(2,1)S(1)}, bf16[22,3,384]{2,1,0:T(4,128)(2,1)S(1)}, u32[]{:S(2)}, u32[]{:S(2)}) collective-permute-start(bf16[22,3,384]{2,1,0:T(4,128)(2,1)S(1)} %get-tuple-element.271), channel_id=1, source_target_pairs={{0,4},{1,2},{2,1},{3,7},{4,0},{5,6},{6,5},{7,3},{8,12},{9,10},{10,... | collective-permute-start | bytes 152072 | tf_op jit(solution)/shard_map/ppermute | solution.py:399
  72.5 7.6 %collective-permute-start.22 = (bf16[64,384]{1,0:T(8,128)(2,1)S(1)}, bf16[64,384]{1,0:T(8,128)(2,1)S(1)}, u32[]{:S(2)}, u32[]{:S(2)}) collective-permute-start(bf16[64,384]{1,0:T(8,128)(2,1)S(1)} %add_convert_fusion.16), channel_id=1, source_target_pairs={{0,6},{1,7},{2,4},{3,5},{4,2},{5,3},{6,0},{7,1},{8,14},{9,15},{10,... | collective-permute-start | bytes 147464 | tf_op jit(solution)/shard_map/ppermute | solution.py:413
  80.2 10.1 %collective-permute-start.24 = (bf16[96,384]{1,0:T(8,128)(2,1)S(1)}, bf16[96,384]{1,0:T(8,128)(2,1)S(1)}, u32[]{:S(2)}, u32[]{:S(2)}) collective-permute-start(bf16[96,384]{1,0:T(8,128)(2,1)S(1)} %bitcast.148), channel_id=1, source_target_pairs={{0,16},{1,17},{2,18},{3,19},{4,20},{5,21},{6,22},{7,23},{8,24},{9,... | collective-permute-start | bytes 221192 | tf_op jit(solution)/shard_map/ppermute | solution.py:413
  84.3 5.9 %collective-permute-start.23 = (bf16[256,384]{1,0:T(8,128)(2,1)S(1)}, bf16[256,384]{1,0:T(8,128)(2,1)S(1)}, u32[]{:S(2)}, u32[]{:S(2)}) collective-permute-start(bf16[256,384]{1,0:T(8,128)(2,1)S(1)} %pad_maximum_fusion.6), channel_id=1, source_target_pairs={{0,8},{1,9},{2,10},{3,11},{4,12},{5,13},{6,14},{7,15},{8,0},{9,1},... | collective-permute-start | bytes 589832 | tf_op jit(solution)/shard_map/ppermute | solution.py:413
  90.4 7.2 %collective-permute-start.25 = (bf16[160,384]{1,0:T(8,128)(2,1)S(1)}, bf16[160,384]{1,0:T(8,128)(2,1)S(1)}, u32[]{:S(2)}, u32[]{:S(2)}) collective-permute-start(bf16[160,384]{1,0:T(8,128)(2,1)S(1)} %pad_maximum_fusion.7), channel_id=1, source_target_pairs={{0,16},{1,17},{2,18},{3,19},{4,20},{5,21},{6,22},{7,23},{8,24},{9,... | collective-permute-start | bytes 368648 | tf_op jit(solution)/shard_map/ppermute | solution.py:413
  97.7 1.3 %collective-permute-start.26 = (bf16[64,384]{1,0:T(8,128)(2,1)S(1)}, bf16[64,384]{1,0:T(8,128)(2,1)S(1)}, u32[]{:S(2)}, u32[]{:S(2)}) collective-permute-start(bf16[64,384]{1,0:T(8,128)(2,1)S(1)} %add_convert_fusion.13.mine), channel_id=1, source_target_pairs={{0,1},{1,0},{2,3},{3,2},{4,5},{5,4},{6,7},{7,6},{8,9},{9,8},{10,11... | collective-permute-start | bytes 147464 | tf_op jit(solution)/shard_map/ppermute | solution.py:413
  (3 other events, 9.1 us)

commit v10 on v9

--- a/solution.py
+++ b/solution.py
@@ -54,17 +54,18 @@
     return max(d for d in range(1, rows + 1) if rows % d == 0 and d <= most)
 
 
-def conv_pass(source, row0, col0, taps, target, rows, cols, back=False):
+def conv_pass(source, row0, col0, taps, layer, target, rows, cols, back=False):
     strip = strip_rows(rows, cols)
     groups = source.shape[0]
 
     def one_strip(step, carry):
         g = step // (rows // strip)
         top = (step % (rows // strip)) * strip
+        lanes = pl.ds(pl.multiple_of(g * LANES, LANES), LANES)
         sums = [jnp.zeros((cols, LANES), F32) for _ in range(strip)]
         for b in range(7):
             spots = [48 - 7 * a - b if back else 7 * a + b for a in range(7)]
-            weights = [taps[g, pl.ds(spot, 1), :] for spot in spots]
+            weights = [taps[spot, pl.ds(layer, 1), lanes] for spot in spots]
             for r in range(strip + 6):
                 line = source[g, row0 + top + r, pl.ds(col0 + b, cols), :]
                 for a in range(7):
@@ -146,7 +147,7 @@
 def hidden_forward(normed, w_in, bias, act, slope):
     for cut in hidden_chunks(w_in.shape[2]):
         for block in pixel_blocks(normed.shape[0]):
-            value, factor = gelu_parts(dot_nn(normed[block, :], w_in[0, :, cut]) + bias[:, cut])
+            value, factor = gelu_parts(dot_nn(normed[block, :], w_in[0, :, cut]) + bias[0:1, cut])
             act[block, cut] = value.astype(BF16)
             slope[block, cut] = factor
 
@@ -163,22 +164,22 @@
 
 
 def dz_of(gpre, w_in, hat, inv, gain, dz_out, dgain, dshift):
-    dn = dot_nt(gpre[...], w_in[0])
+    dn = dot_nt(gpre[...], w_in)
     dgain[...] = jnp.sum(dn * hat, axis=0, keepdims=True)
     dshift[...] = jnp.sum(dn, axis=0, keepdims=True)
     dz_out[...] = norm_back(dn, hat, inv, gain).astype(BF16)
 
 
-def mlp_grads(normed, grad, w_in, b_in, w_out, act, gpre, db):
+def mlp_grads(normed, grad, w_in, b_in, w_out, layer, act, gpre, db):
     pixels = grad.shape[0]
     for cut in hidden_chunks(w_in.shape[2]):
-        bias = b_in[:, cut]
+        bias = b_in[layer : layer + 1, cut]
         bias_sum = None
         for block in pixel_blocks(pixels):
-            pre = dot_nn(normed[block, :], w_in[0, :, cut]) + bias
+            pre = dot_nn(normed[block, :], w_in[layer, :, cut]) + bias
             value, slope = gelu_parts(pre)
             act[block, cut] = value.astype(BF16)
-            gradient = dot_nn(grad[block, :], w_out[0, :, cut]) * slope
+            gradient = dot_nn(grad[block, :], w_out[layer, :, cut]) * slope
             gpre[block, cut] = gradient.astype(BF16)
             part = jnp.sum(gradient, axis=0, keepdims=True)
             bias_sum = part if bias_sum is None else bias_sum + part
@@ -202,39 +203,26 @@
             dw[1][i, half, :] = jnp.where(upper, value[:, 1], value[:, 0]).reshape(-1, channels)
 
 
-def fetch_layers(triples, arrived):
-    copies = [
-        pltpu.make_async_copy(source.at[pl.ds(layer, 1)], target, arrived.at[i])
-        for i, (source, layer, target) in enumerate(triples)
-    ]
-    for copy in copies:
-        copy.start()
-    return copies
-
-
 def forward_kernel(
     place, xpad, taps, gains, shifts, w_in, w_out, b_in, mids, z_out,
-    xs, zs, act, w_in0, w_out0, arrived,
+    xs, zs, act,
 ):
-    waits = fetch_layers(((w_in, 0, w_in0), (w_out, 0, w_out0)), arrived)
     groups, mid_rows, mid_cols = zs.shape[:3]
     rows, cols = z_out.shape[1:3]
     for g in range(groups):
         xs[g] = xpad[:, :, g * LANES : (g + 1) * LANES].astype(F32)
-    conv_pass(xs, 0, 0, taps.at[0], zs, mid_rows, mid_cols)
+    conv_pass(xs, 0, 0, taps, 0, zs, mid_rows, mid_cols)
     z_out[...] = zs[:, HALO : HALO + rows, HALO : HALO + cols, :]
     strip = act.shape[0] // mid_cols
-    for wait in waits:
-        wait.wait()
 
     def one_strip(step, carry):
         top = step * strip
         hat, _ = norm_parts(joined(zs, pl.ds(top, strip)))
         normed = (hat * gains[0:1] + shifts[0:1]).astype(BF16)
-        for cut in hidden_chunks(w_in0.shape[2]):
-            pre = dot_nn(normed, w_in0[0, :, cut]) + b_in[0, :, cut]
+        for cut in hidden_chunks(w_in.shape[2]):
+            pre = dot_nn(normed, w_in[0, :, cut]) + b_in[0:1, cut]
             act[:, cut] = gelu_only(pre).astype(BF16)
-        mixed = dot_nt(act[...], w_out0[0])
+        mixed = dot_nt(act[...], w_out[0])
         row = lax.broadcasted_iota(jnp.int32, (strip, mid_cols, 1), 0) + (top - HALO) + place[0]
         col = lax.broadcasted_iota(jnp.int32, (strip, mid_cols, 1), 1) - HALO + place[1]
         real = (row >= 0) & (row < place[2]) & (col >= 0) & (col < place[3])
@@ -249,40 +237,32 @@
 
 def top_kernel(
     mids, grad, taps, gains, shifts, w_in, w_out, b_in,
-    dz_out, normed, act, gpre, db, dgain, dshift, z, w_in1, w_out1, arrived,
+    dz_out, normed, act, gpre, db, dgain, dshift, z,
 ):
-    waits = fetch_layers(((w_in, 1, w_in1), (w_out, 1, w_out1)), arrived)
-    conv_pass(mids, 0, 0, taps.at[1], z, *z.shape[1:3])
+    conv_pass(mids, 0, 0, taps, 1, z, *z.shape[1:3])
     hat, inv = norm_parts(joined(z, slice(None)))
     normed[...] = (hat * gains[1:2] + shifts[1:2]).astype(BF16)
-    for wait in waits:
-        wait.wait()
-    mlp_grads(normed, grad, w_in1, b_in.at[1], w_out1, act, gpre, db)
-    dz_of(gpre, w_in1, hat, inv, gains[1:2], dz_out, dgain, dshift)
-
-
-def again_kernel(z0, gains, shifts, w_in, b_in, hat_out, inv_out, normed, act, slope, w_in0, arrived):
-    (wait,) = fetch_layers(((w_in, 0, w_in0),), arrived)
+    mlp_grads(normed, grad, w_in, b_in, w_out, 1, act, gpre, db)
+    dz_of(gpre, w_in[1], hat, inv, gains[1:2], dz_out, dgain, dshift)
+
+
+def again_kernel(z0, gains, shifts, w_in, b_in, hat_out, inv_out, normed, act, slope):
     hat, inv = norm_parts(joined(z0, slice(None)))
     hat_out[...] = hat
     inv_out[...] = jnp.broadcast_to(inv, inv_out.shape)
     normed[...] = (hat * gains[0:1] + shifts[0:1]).astype(BF16)
-    wait.wait()
-    hidden_forward(normed, w_in0, b_in.at[0], act, slope)
+    hidden_forward(normed, w_in, b_in, act, slope)
 
 
 def low_kernel(
     per, place, dzpad, grad, hat, inv, normed, act, slope, taps, gains, w_in, w_out,
     gmid, dz_out, db, dgain, dshift, *rest,
 ):
-    *dw, dzs, spread, gpre, w_in0, w_out0, arrived = rest
-    waits = fetch_layers(((w_out, 0, w_out0), (w_in, 0, w_in0)), arrived)
-    spread_pass(dzpad, dzs, taps.at[1], spread)
+    *dw, dzs, spread, gpre = rest
+    spread_pass(dzpad, dzs, taps, 1, spread)
     gmid[...] = (grad[...].astype(F32) + joined(spread, slice(None))).astype(BF16)
-    for wait in waits:
-        wait.wait()
-    hidden_back(gmid, w_out0, slope, gpre, db)
-    dz_of(gpre, w_in0, hat[...], inv[:, :1], gains[0:1], dz_out, dgain, dshift)
+    hidden_back(gmid, w_out, slope, gpre, db)
+    dz_of(gpre, w_in[0], hat[...], inv[:, :1], gains[0:1], dz_out, dgain, dshift)
     weight_grads(place, normed, gmid, act, gpre, dw, per)
 
 
@@ -290,14 +270,14 @@
     weight_grads(place, normed, grad, act, gpre, dw, per)
 
 
-def spread_pass(dzpad, dzs, taps, spread):
+def spread_pass(dzpad, dzs, taps, layer, spread):
     for g in range(dzs.shape[0]):
         dzs[g] = dzpad[:, :, g * LANES : (g + 1) * LANES].astype(F32)
-    conv_pass(dzs, 0, 0, taps, spread, *spread.shape[1:3], back=True)
+    conv_pass(dzs, 0, 0, taps, layer, spread, *spread.shape[1:3], back=True)
 
 
 def last_kernel(dzpad, gmid, taps, out, dzs, spread):
-    spread_pass(dzpad, dzs, taps.at[0], spread)
+    spread_pass(dzpad, dzs, taps, 0, spread)
     out[...] = (gmid[...].astype(F32) + joined(spread, slice(None))).astype(BF16)
 
 
@@ -355,9 +335,8 @@
     return jax.ShapeDtypeStruct(dims, dtype)
 
 
-def run(kernel, outs, scratch, args, specs=None, fetched=0, name=None):
+def run(kernel, outs, scratch, args, specs=None, name=None):
     vmem = pl.BlockSpec(memory_space=pltpu.VMEM)
-    semaphores = [pltpu.SemaphoreType.DMA((fetched,))] if fetched else []
     return pl.pallas_call(
         kernel,
         out_shape=outs,
@@ -365,7 +344,7 @@
             vmem if s is None else pl.BlockSpec(memory_space=s) for s in (specs or [None] * len(args))
         ],
         out_specs=tuple(vmem for _ in outs),
-        scratch_shapes=[pltpu.VMEM(s.shape, s.dtype) for s in scratch] + semaphores,
+        scratch_shapes=[pltpu.VMEM(s.shape, s.dtype) for s in scratch],
         compiler_params=pltpu.CompilerParams(vmem_limit_bytes=46 * 1024 * 1024),
         name=name,
     )(*args)
@@ -456,8 +435,7 @@
     grad_scale = 1.0 / math.sqrt(rows * cols * total)
     pixels = rows * cols
 
-    taps = kernels.reshape(layers, 49, groups, LANES).transpose(0, 2, 1, 3)
-    biases = b_in[:, None, :]
+    taps = kernels.transpose(1, 2, 0, 3).reshape(49, layers, channels)
     place = jnp.stack(
         [
             lax.axis_index("rows") * rows,
@@ -473,6 +451,9 @@
     odd_col, odd_row = (at_col & 1) == 1, (at_row & 1) == 1
     outer_col = (at_col == 0) | (at_col == n_cols - 1)
     outer_row = (at_row == 0) | (at_row == n_rows - 1)
+    activations, place, mine, odd_col, odd_row, outer_col, outer_row = lax.optimization_barrier(
+        (activations, place, mine, odd_col, odd_row, outer_col, outer_row)
+    )
 
     def rim_cols(tile, width):
         twin, other = edges(tile, 1, width, odd_col)
@@ -487,7 +468,6 @@
 
     mid_rows, mid_cols = rows + 2 * HALO, cols + 8
     strip = max(d for d in range(1, mid_rows + 1) if mid_rows % d == 0 and d * mid_cols <= 264)
-    weights = [shape(1, channels, hidden, dtype=BF16)] * 2
     tile_z = shape(groups, rows, cols, LANES)
     tile_b = shape(pixels, channels, dtype=BF16)
     tile_h = shape(pixels, hidden, dtype=BF16)
@@ -498,9 +478,6 @@
     small_rows = 64
 
     xpad = filled(rim_cols(rim_rows(activations, WIDE), WIDE))
-    xpad, place, mine, odd_col, odd_row, outer_col, outer_row = lax.optimization_barrier(
-        (xpad, place, mine, odd_col, odd_row, outer_col, outer_row)
-    )
     mids, z0 = run(
         forward_kernel,
         (shape(groups, mid_rows, mid_cols, LANES), tile_z),
@@ -508,20 +485,16 @@
             shape(groups, *xpad.shape[:2], LANES),
             shape(groups, mid_rows, mid_cols, LANES),
             shape(strip * mid_cols, hidden, dtype=BF16),
-        ]
-        + weights,
-        (place, xpad, taps, norm_gains, norm_shifts, w_in, w_out, biases),
-        [pltpu.SMEM] + [None] * 4 + [pl.ANY] * 2 + [None],
-        fetched=2,
+        ],
+        (place, xpad, taps, norm_gains, norm_shifts, w_in, w_out, b_in),
+        [pltpu.SMEM] + [None] * 7,
         name="forward",
     )
     dz1, normed1, act1, gpre1, *small1 = run(
         top_kernel,
         (tile_b, tile_b, tile_h, tile_h) + small_outs,
-        [tile_z] + weights,
-        (mids, grad_flat, taps, norm_gains, norm_shifts, w_in, w_out, biases),
-        [None] * 5 + [pl.ANY] * 2 + [None],
-        fetched=2,
+        [tile_z],
+        (mids, grad_flat, taps, norm_gains, norm_shifts, w_in, w_out, b_in),
         name="top",
     )
 
@@ -590,10 +563,8 @@
     again = run(
         again_kernel,
         (tile_f, shape(pixels, LANES), tile_b, tile_h, shape(pixels, hidden)),
-        weights[:1],
-        (z0, norm_gains, norm_shifts, w_in, biases),
-        [None] * 3 + [pl.ANY, None],
-        fetched=1,
+        [],
+        (z0, norm_gains, norm_shifts, w_in, b_in),
         name="again",
     )
     wide1, twin, other, run1, again = fenced(wide1, twin, other, run1, again)
@@ -603,14 +574,13 @@
     grad_mid, dz0, *rest = run(
         functools.partial(low_kernel, per),
         (tile_b, tile_b) + small_outs + grads_b,
-        spread_scratch + [tile_h] + weights,
+        spread_scratch + [tile_h],
         (place, dzpad1, grad_flat, *again, taps, norm_gains, w_in, w_out),
-        [pltpu.SMEM] + [None] * 9 + [pl.ANY] * 2,
-        fetched=2,
+        [pltpu.SMEM] + [None] * 11,
         name="low",
     )
     small0, dw0 = rest[:3], rest[3:]
-    dz0, dw0, pair1, small0 = fenced(dz0, dw0, pair1, small0)
+    dz0, dw0, small0 = fenced(dz0, dw0, small0)
     run0 = start(dw0)
     low_bit = col_bits + 1
     pair1, _ = onward([settled(f) for f in pair1], low_bit)

time: 100 us -> 102 us (1.020)
  waiting for transfers between devices: 27.6 us -> 32.6 us
  starting transfers between devices: 32.1 us -> 29.7 us
    ppermute x15, waiting for transfers between devices: 18.5 us -> 23 us  [flip_bit(): return lax.ppermute(value, both, [(i, i ^ flip) for i in range(total)])]
    ppermute x15, starting transfers between devices: 18.5 us -> 16.2 us  [flip_bit(): return lax.ppermute(value, both, [(i, i ^ flip) for i in range(total)])]
  transfers between devices with their start and end apart: 27 -> 27, of which waited for: 11 -> 14; matrix products, arithmetic and copies ran while one was open for 2% -> 2% of each run, Pallas kernels for 15% -> 10%
where the time goes in v10:
time: 102 us
  waiting for transfers between devices  32.6 us (32%)
  Pallas kernels  31.2 us (31%)
  starting transfers between devices  29.7 us (29%)
  other arithmetic  4.77 us (5%)
  local copies, waits for them, and re-layouts  2.66 us (3%)
  between operations  1.23 us (1%)
    pallas_call x9, Pallas kernels, run(): pl.pallas_call(kernel, out_shape=outs, in_specs=[vmem if s is None else p...  31.2 us
    ppermute x15, waiting for transfers between devices, flip_bit(): return lax.ppermute(value, both, [(i, i ^ flip) for i in range(total)])  23 us
    ppermute x15, starting transfers between devices, flip_bit(): return lax.ppermute(value, both, [(i, i ^ flip) for i in range(total)])  16.2 us
    ppermute x6, starting transfers between devices, to_twin(): lax.ppermute(edge, axis, [(i, i ^ 1) for i in range(count) if i ^ 1 < cou...  7.3 us
    ppermute x6, starting transfers between devices, to_other(): return lax.ppermute(edge, ('rows', 'cols'), pairs)  6.17 us
    ppermute x6, waiting for transfers between devices, to_twin(): lax.ppermute(edge, axis, [(i, i ^ 1) for i in range(count) if i ^ 1 < cou...  5.89 us
    ppermute x6, waiting for transfers between devices, to_other(): return lax.ppermute(edge, ('rows', 'cols'), pairs)  3.7 us
  transfers between devices with their start and end apart: 27, of which 14 were waited for; matrix products, arithmetic and copies ran while one was open for 2% of the time, Pallas kernels for 10%

profile of v10, /device:TPU:0, one launch (start us, length us, event | category | flops | bytes accessed | tf_op | source)
XLA Modules:
  0.0 102.1 jit_solution(2612411708811256866)
XLA Ops:
  2.2 4.0 %collective-permute-start = (bf16[6,16,384]{2,1,0:T(8,128)(2,1)S(1)}, bf16[6,16,384]{2,1,0:T(8,128)(2,1)S(1)}, u32[]{:S(2)}, u32[]{:S(2)}) collective-permute-start(bf16[6,16,384]{2,1,0:T(8,128)(2,1)S(1)} %get-tuple-element.268), channel_id=1, source_target_pairs={{0,4},{4,0},{8,12},{12,8},{16,20},{20,16},{24,28},{28,24},{1,5},{5... | collective-permute-start | bytes 221192 | tf_op jit(solution)/shard_map/ppermute | solution.py:362
  6.2 2.5 %collective-permute-done = bf16[6,16,384]{2,1,0:T(8,128)(2,1)S(1)} collective-permute-done((bf16[6,16,384]{2,1,0:T(8,128)(2,1)S(1)}, bf16[6,16,384]{2,1,0:T(8,128)(2,1)S(1)}, u32[]{:S(2)}, u32[]{:S(2)}) %collective-permute-start) | collective-permute-done | bytes 73760 | tf_op jit(solution)/shard_map/ppermute | solution.py:362
  8.8 1.0 pad_maximum_fusion.2
  9.9 2.5 %collective-permute-start.3 = (bf16[28,6,384]{2,1,0:T(8,128)(2,1)S(1)}, bf16[28,6,384]{2,1,0:T(8,128)(2,1)S(1)}, u32[]{:S(2)}, u32[]{:S(2)}) collective-permute-start(bf16[28,6,384]{2,1,0:T(8,128)(2,1)S(1)} %get-tuple-element.245), channel_id=1, source_target_pairs={{0,4},{1,2},{2,1},{3,7},{4,0},{5,6},{6,5},{7,3},{8,12},{9,10},{10,... | collective-permute-start | bytes 387080 | tf_op jit(solution)/shard_map/ppermute | solution.py:378
  12.4 3.4 %collective-permute-done.3 = bf16[28,6,384]{2,1,0:T(8,128)(2,1)S(1)} collective-permute-done((bf16[28,6,384]{2,1,0:T(8,128)(2,1)S(1)}, bf16[28,6,384]{2,1,0:T(8,128)(2,1)S(1)}, u32[]{:S(2)}, u32[]{:S(2)}) %collective-permute-start.3) | collective-permute-done | bytes 129056 | tf_op jit(solution)/shard_map/ppermute | solution.py:378
  16.3 1.7 %copy-done.1 = bf16[2,384,1536]{2,1,0:T(8,128)(2,1)S(1)} copy-done((bf16[2,384,1536]{2,1,0:T(8,128)(2,1)S(1)}, bf16[2,384,1536]{2,1,0:T(8,128)(2,1)}, u32[]{:S(2)}) %copy-start.1) | copy-done | bytes 2359320
  17.9 8.6 %forward.1 = (f32[3,22,24,128]{3,2,1,0:T(8,128)S(1)}, f32[3,16,16,128]{3,2,1,0:T(8,128)S(1)}) custom-call(s32[5]{0:T(128)S(1)} %stack.25.place, bf16[28,32,384]{2,1,0:T(8,128)(2,1)S(1)} %fusion.12.xpad, f32[49,2,384]{2,1,0:T(2,128)S(1)} %bitcast.95, f32[2,384]{1,0:T(2,128)S(1)} %copy-done.5, f32[2,384]{1,0:T(2,128)S(1)} %copy-done.6, ...), custom_call_target="tpu_custom_call" | custom-call | tf_op jit(solution)/shard_map/forward/pallas_call | solution.py:340
  26.6 4.5 %top.1 = (bf16[256,384]{1,0:T(8,128)(2,1)S(1)}, bf16[256,384]{1,0:T(8,128)(2,1)S(1)}, bf16[256,1536]{1,0:T(8,128)(2,1)S(1)}, bf16[256,1536]{1,0:T(8,128)(2,1)S(1...) custom-call(f32[3,22,24,128]{3,2,1,0:T(8,128)S(1)} %get-tuple-element.127.mids, ...), custom_call_target="tpu_custom_call" | custom-call | tf_op jit(solution)/shard_map/top/pallas_call | solution.py:340
  31.1 2.1 %collective-permute-start.4 = (bf16[3,16,384]{2,1,0:T(8,128)(2,1)S(1)}, bf16[3,16,384]{2,1,0:T(8,128)(2,1)S(1)}, u32[]{:S(2)}, u32[]{:S(2)}) collective-permute-start(bf16[3,16,384]{2,1,0:T(8,128)(2,1)S(1)} %bitcast.146), channel_id=1, source_target_pairs={{0,4},{4,0},{8,12},{12,8},{16,20},{20,16},{24,28},{28,24},{1,5},{5... | collective-permute-start | bytes 110600 | tf_op jit(solution)/shard_map/ppermute | solution.py:362
  33.2 1.6 %weights_top.1 = (bf16[2,768,384]{2,1,0:T(8,128)(2,1)S(1)}, bf16[2,768,384]{2,1,0:T(8,128)(2,1)S(1)}) custom-call(s32[5]{0:T(128)S(1)} %stack.25.place, bf16[256,384]{1,0:T(8,128)(2,1)S(1)} %get-tuple-element.129.normed, bf16[256,1536]{1,0:T(8,128)(2,1)S(1)} %get-tuple-element.130.act, bf16[256,1536]{1,0:T(8,128)(2,1)S(1)} %get-tuple-element.131.gpre, ...), custom_call_target="tpu_custom_call" | custom-call | tf_op jit(solution)/shard_map/weights_top/pallas_call | solution.py:340
  35.5 2.9 %collective-permute-start.7 = (bf16[22,3,384]{2,1,0:T(4,128)(2,1)S(1)}, bf16[22,3,384]{2,1,0:T(4,128)(2,1)S(1)}, u32[]{:S(2)}, u32[]{:S(2)}) collective-permute-start(bf16[22,3,384]{2,1,0:T(4,128)(2,1)S(1)} %get-tuple-element.261), channel_id=1, source_target_pairs={{0,4},{1,2},{2,1},{3,7},{4,0},{5,6},{6,5},{7,3},{8,12},{9,10},{10,... | collective-permute-start | bytes 152072 | tf_op jit(solution)/shard_map/ppermute | solution.py:378
  38.4 2.1 %again.1 = (f32[256,384]{1,0:T(8,128)S(1)}, f32[256,128]{1,0:T(8,128)S(1)}, bf16[256,384]{1,0:T(8,128)(2,1)S(1)}, bf16[256,1536]{1,0:T(8,128)(2,1)S(1)}, f32[256,1536]{1,0:T(8,128)S(1)}) custom-call(f32[3,16,16,128]{3,2,1,0:T(8,128)S(1)} %get-tuple-element.140.z0, f32[2,384]{1,0:T(2,128)S(1)} %copy-done.5, f32[2,384]{1,0:T(2,128)S(1)} %copy-done.6, ...), custom_call_target="tpu_custom_call" | custom-call | tf_op jit(solution)/shard_map/again/pallas_call | solution.py:340
  41.0 6.2 %low.1 = (bf16[256,384]{1,0:T(8,128)(2,1)S(1)}, bf16[256,384]{1,0:T(8,128)(2,1)S(1)}, f32[1,1536]{1,0:T(1,128)S(1)}, f32[1,384]{1,0:T(1,128)S(1)}, f32[1,384]{1,...) custom-call(s32[5]{0:T(128)S(1)} %stack.25.place, ...), custom_call_target="tpu_custom_call" | custom-call | tf_op jit(solution)/shard_map/low/pallas_call | solution.py:340
  48.2 1.9 %collective-permute-start.13 = (bf16[1,4,2,48,384]{4,3,2,1,0:T(8,128)(2,1)S(1)}, bf16[1,4,2,48,384]{4,3,2,1,0:T(8,128)(2,1)S(1)}, u32[]{:S(2)}, u32[]{:S(2)}) collective-permute-start(bf16[1,4,2,48,384]{4,3,2,1,0:T(8,128)(2,1)S(1)} %dynamic-slice_bitcast_fusion), channel_id=1, source_target_pairs={{0,4},{1,5},{2,6},{3,7},{4,0},{5,1},{6,2},{7,3},{8,12},{9,13},{10,... | collective-permute-start | bytes 884744 | tf_op jit(solution)/shard_map/ppermute | solution.py:392
  50.5 7.1 %collective-permute-done.13 = bf16[1,4,2,48,384]{4,3,2,1,0:T(8,128)(2,1)S(1)} collective-permute-done((bf16[1,4,2,48,384]{4,3,2,1,0:T(8,128)(2,1)S(1)}, bf16[1,4,2,48,384]{4,3,2,1,0:T(8,128)(2,1)S(1)}, u32[]{:S(2)}, u32[]{:S(2)}) %collective-permute-start.13) | collective-permute-done | bytes 294944 | tf_op jit(solution)/shard_map/ppermute | solution.py:392
  57.7 1.4 %collective-permute-done.12 = bf16[1,8,1,48,384]{4,3,1,2,0:T(8,128)(2,1)S(1)} collective-permute-done((bf16[1,8,1,48,384]{4,3,1,2,0:T(8,128)(2,1)S(1)}, bf16[1,8,1,48,384]{4,3,1,2,0:T(8,128)(2,1)S(1)}, u32[]{:S(2)}, u32[]{:S(2)}) %collective-permute-start.12) | collective-permute-done | bytes 294944 | tf_op jit(solution)/shard_map/ppermute | solution.py:392
  59.3 2.1 %collective-permute-start.14 = (bf16[384,384]{1,0:T(8,128)(2,1)S(1)}, bf16[384,384]{1,0:T(8,128)(2,1)S(1)}, u32[]{:S(2)}, u32[]{:S(2)}) collective-permute-start(bf16[384,384]{1,0:T(8,128)(2,1)S(1)} %pad_maximum_fusion.3), channel_id=1, source_target_pairs={{0,8},{1,9},{2,10},{3,11},{4,12},{5,13},{6,14},{7,15},{8,0},{9,1},... | collective-permute-start | bytes 884744 | tf_op jit(solution)/shard_map/ppermute | solution.py:392
  61.9 1.6 %collective-permute-start.11 = (bf16[1,4,2,48,384]{4,3,1,2,0:T(8,128)(2,1)S(1)}, bf16[1,4,2,48,384]{4,3,1,2,0:T(8,128)(2,1)S(1)}, u32[]{:S(2)}, u32[]{:S(2)}) collective-permute-start(bf16[1,4,2,48,384]{4,3,1,2,0:T(8,128)(2,1)S(1)} %bitcast.139), channel_id=1, source_target_pairs={{0,4},{1,5},{2,6},{3,7},{4,0},{5,1},{6,2},{7,3},{8,12},{9,13},{10,... | collective-permute-start | bytes 884744 | tf_op jit(solution)/shard_map/ppermute | solution.py:392
  63.9 3.7 %taps.1 = (bf16[64,384]{1,0:T(8,128)(2,1)S(1)}, bf16[64,384]{1,0:T(8,128)(2,1)S(1)}) custom-call(s32[5]{0:T(128)S(1)} %stack.25.place, f32[3,22,24,128]{3,2,1,0:T(8,128)S(1)} %get-tuple-element.127.mids, bf16[28,32,384]{2,1,0:T(8,128)(2,1)S(1)} %fusion.12.xpad, bf16[256,384]{1,0:T(8,128)(2,1)S(1)} %get-tuple-element.176.dz0, ...), custom_call_target="tpu_custom_call" | custom-call | tf_op jit(solution)/shard_map/taps/pallas_call | solution.py:340
  68.7 3.0 %collective-permute-done.15 = bf16[3,16,384]{2,1,0:T(8,128)(2,1)S(1)} collective-permute-done((bf16[3,16,384]{2,1,0:T(8,128)(2,1)S(1)}, bf16[3,16,384]{2,1,0:T(8,128)(2,1)S(1)}, u32[]{:S(2)}, u32[]{:S(2)}) %collective-permute-start.15) | collective-permute-done | bytes 36896 | tf_op jit(solution)/shard_map/ppermute | solution.py:362
  72.3 1.8 %collective-permute-start.19 = (bf16[352,384]{1,0:T(8,128)(2,1)S(1)}, bf16[352,384]{1,0:T(8,128)(2,1)S(1)}, u32[]{:S(2)}, u32[]{:S(2)}) collective-permute-start(bf16[352,384]{1,0:T(8,128)(2,1)S(1)} %get-tuple-element.287), channel_id=1, source_target_pairs={{0,2},{1,3},{2,0},{3,1},{4,6},{5,7},{6,4},{7,5},{8,10},{9,11},{10,... | collective-permute-start | bytes 811016 | tf_op jit(solution)/shard_map/ppermute | solution.py:392
  74.0 2.9 %collective-permute-start.18 = (bf16[352,384]{1,0:T(8,128)(2,1)S(1)}, bf16[352,384]{1,0:T(8,128)(2,1)S(1)}, u32[]{:S(2)}, u32[]{:S(2)}) collective-permute-start(bf16[352,384]{1,0:T(8,128)(2,1)S(1)} %get-tuple-element.288), channel_id=1, source_target_pairs={{0,4},{1,5},{2,6},{3,7},{4,0},{5,1},{6,2},{7,3},{8,12},{9,13},{10,... | collective-permute-start | bytes 811016 | tf_op jit(solution)/shard_map/ppermute | solution.py:392
  77.6 2.8 %collective-permute-done.19 = bf16[352,384]{1,0:T(8,128)(2,1)S(1)} collective-permute-done((bf16[352,384]{1,0:T(8,128)(2,1)S(1)}, bf16[352,384]{1,0:T(8,128)(2,1)S(1)}, u32[]{:S(2)}, u32[]{:S(2)}) %collective-permute-start.19) | collective-permute-done | bytes 270368 | tf_op jit(solution)/shard_map/ppermute | solution.py:392
  80.4 2.4 %collective-permute-done.18 = bf16[352,384]{1,0:T(8,128)(2,1)S(1)} collective-permute-done((bf16[352,384]{1,0:T(8,128)(2,1)S(1)}, bf16[352,384]{1,0:T(8,128)(2,1)S(1)}, u32[]{:S(2)}, u32[]{:S(2)}) %collective-permute-start.18) | collective-permute-done | bytes 270368 | tf_op jit(solution)/shard_map/ppermute | solution.py:392
  82.9 1.1 %collective-permute-done.22 = bf16[64,384]{1,0:T(8,128)(2,1)S(1)} collective-permute-done((bf16[64,384]{1,0:T(8,128)(2,1)S(1)}, bf16[64,384]{1,0:T(8,128)(2,1)S(1)}, u32[]{:S(2)}, u32[]{:S(2)}) %collective-permute-start.22) | collective-permute-done | bytes 49184 | tf_op jit(solution)/shard_map/ppermute | solution.py:392
  84.2 1.3 %collective-permute-start.24 = (bf16[96,384]{1,0:T(8,128)(2,1)S(1)}, bf16[96,384]{1,0:T(8,128)(2,1)S(1)}, u32[]{:S(2)}, u32[]{:S(2)}) collective-permute-start(bf16[96,384]{1,0:T(8,128)(2,1)S(1)} %bitcast.142), channel_id=1, source_target_pairs={{0,16},{1,17},{2,18},{3,19},{4,20},{5,21},{6,22},{7,23},{8,24},{9,... | collective-permute-start | bytes 221192 | tf_op jit(solution)/shard_map/ppermute | solution.py:392
  85.7 2.1 %collective-permute-start.23 = (bf16[256,384]{1,0:T(8,128)(2,1)S(1)}, bf16[256,384]{1,0:T(8,128)(2,1)S(1)}, u32[]{:S(2)}, u32[]{:S(2)}) collective-permute-start(bf16[256,384]{1,0:T(8,128)(2,1)S(1)} %pad_maximum_fusion.6), channel_id=1, source_target_pairs={{0,8},{1,9},{2,10},{3,11},{4,12},{5,13},{6,14},{7,15},{8,0},{9,1},... | collective-permute-start | bytes 589832 | tf_op jit(solution)/shard_map/ppermute | solution.py:392
  88.1 2.5 %last.1 = bf16[256,384]{1,0:T(8,128)(2,1)} custom-call(bf16[22,32,384]{2,1,0:T(8,128)(2,1)S(1)} %fusion.20.dzpad, bf16[256,384]{1,0:T(8,128)(2,1)S(1)} %get-tuple-element.215.gmid, f32[49,2,384]{2,1,0:T(2,128)S(1)} %bitcast.98), custom_call_target="tpu_custom_call" | custom-call | tf_op jit(solution)/shard_map/last/pallas_call | solution.py:340
  90.6 1.6 %collective-permute-done.23 = bf16[256,384]{1,0:T(8,128)(2,1)S(1)} collective-permute-done((bf16[256,384]{1,0:T(8,128)(2,1)S(1)}, bf16[256,384]{1,0:T(8,128)(2,1)S(1)}, u32[]{:S(2)}, u32[]{:S(2)}) %collective-permute-start.23) | collective-permute-done | bytes 196640 | tf_op jit(solution)/shard_map/ppermute | solution.py:392
  92.4 1.0 collective-permute-start.25
  93.4 6.2 %collective-permute-done.25 = bf16[160,384]{1,0:T(8,128)(2,1)S(1)} collective-permute-done((bf16[160,384]{1,0:T(8,128)(2,1)S(1)}, bf16[160,384]{1,0:T(8,128)(2,1)S(1)}, u32[]{:S(2)}, u32[]{:S(2)}) %collective-permute-start.25) | collective-permute-done | bytes 122912 | tf_op jit(solution)/shard_map/ppermute | solution.py:392
  100.9 1.3 %small.1 = (f32[49,2,384]{2,1,0:T(2,128)}, f32[2,384]{1,0:T(2,128)}, f32[2,384]{1,0:T(2,128)}, f32[2,1536]{1,0:T(2,128)}) custom-call(s32[5]{0:T(128)S(1)} %stack.25.place, bf16[64,384]{1,0:T(8,128)(2,1)S(1)} %add_convert_fusion.11.mine, bf16[64,384]{1,0:T(8,128)(2,1)S(1)} %collective-permute-done.26.got), custom_call_target="tpu_custom_call" | custom-call | tf_op jit(solution)/shard_map/small/pallas_call | solution.py:340
  (115 shorter events, 10.3 us)
Async XLA Ops:
  1.7 4.6 %collective-permute-start.1 = (bf16[6,16,384]{2,1,0:T(8,128)(2,1)S(1)}, bf16[6,16,384]{2,1,0:T(8,128)(2,1)S(1)}, u32[]{:S(2)}, u32[]{:S(2)}) collective-permute-start(bf16[6,16,384]{2,1,0:T(8,128)(2,1)S(1)} %get-tuple-element.267), channel_id=1, source_target_pairs={{0,1},{1,0},{2,3},{3,2},{4,8},{5,9},{6,10},{7,11},{8,4},{9,5},{10,... | collective-permute-start | bytes 221192 | tf_op jit(solution)/shard_map/ppermute | solution.py:378
  2.2 13.7 %copy-start.7 = (bf16[16,16,384]{2,1,0:T(8,128)(2,1)S(1)}, bf16[16,16,384]{2,1,0:T(8,128)(2,1)}, u32[]{:S(2)}) copy-start(bf16[16,16,384]{2,1,0:T(8,128)(2,1)} %param.8) | copy-start | bytes 589828
  2.2 6.5 %collective-permute-start = (bf16[6,16,384]{2,1,0:T(8,128)(2,1)S(1)}, bf16[6,16,384]{2,1,0:T(8,128)(2,1)S(1)}, u32[]{:S(2)}, u32[]{:S(2)}) collective-permute-start(bf16[6,16,384]{2,1,0:T(8,128)(2,1)S(1)} %get-tuple-element.268), channel_id=1, source_target_pairs={{0,4},{4,0},{8,12},{12,8},{16,20},{20,16},{24,28},{28,24},{1,5},{5... | collective-permute-start | bytes 221192 | tf_op jit(solution)/shard_map/ppermute | solution.py:362
  9.7 6.5 %copy-start = (bf16[2,384,1536]{2,1,0:T(8,128)(2,1)S(1)}, bf16[2,384,1536]{2,1,0:T(8,128)(2,1)}, u32[]{:S(2)}) copy-start(bf16[2,384,1536]{2,1,0:T(8,128)(2,1)} %w_in.7) | copy-start | bytes 7077892
  9.8 6.4 %copy-start.2 = (f32[2,7,7,384]{3,0,2,1:T(2,128)S(1)}, f32[2,7,7,384]{3,0,2,1:T(2,128)}, u32[]{:S(2)}) copy-start(f32[2,7,7,384]{3,0,2,1:T(2,128)} %param.10) | copy-start | bytes 451588
  9.8 6.4 %copy-start.4 = (f32[2,1536]{1,0:T(2,128)S(1)}, f32[2,1536]{1,0:T(2,128)}, u32[]{:S(2)}) copy-start(f32[2,1536]{1,0:T(2,128)} %b_in.5) | copy-start | bytes 36868
  9.9 5.9 %collective-permute-start.3 = (bf16[28,6,384]{2,1,0:T(8,128)(2,1)S(1)}, bf16[28,6,384]{2,1,0:T(8,128)(2,1)S(1)}, u32[]{:S(2)}, u32[]{:S(2)}) collective-permute-start(bf16[28,6,384]{2,1,0:T(8,128)(2,1)S(1)} %get-tuple-element.245), channel_id=1, source_target_pairs={{0,4},{1,2},{2,1},{3,7},{4,0},{5,6},{6,5},{7,3},{8,12},{9,10},{10,... | collective-permute-start | bytes 387080 | tf_op jit(solution)/shard_map/ppermute | solution.py:378
  12.4 3.4 %collective-permute-start.2 = (bf16[28,6,384]{2,1,0:T(8,128)(2,1)S(1)}, bf16[28,6,384]{2,1,0:T(8,128)(2,1)S(1)}, u32[]{:S(2)}, u32[]{:S(2)}) collective-permute-start(bf16[28,6,384]{2,1,0:T(8,128)(2,1)S(1)} %get-tuple-element.246), channel_id=1, source_target_pairs={{0,1},{1,0},{2,3},{3,2},{4,5},{5,4},{6,7},{7,6},{8,9},{9,8},{10,11... | collective-permute-start | bytes 387080 | tf_op jit(solution)/shard_map/ppermute | solution.py:362
  17.9 8.7 %copy-start.3 = (bf16[16,16,384]{2,1,0:T(8,128)(2,1)S(1)}, bf16[16,16,384]{2,1,0:T(8,128)(2,1)}, u32[]{:S(2)}) copy-start(bf16[16,16,384]{2,1,0:T(8,128)(2,1)} %param.9) | copy-start | bytes 589828
  31.1 4.0 %collective-permute-start.4 = (bf16[3,16,384]{2,1,0:T(8,128)(2,1)S(1)}, bf16[3,16,384]{2,1,0:T(8,128)(2,1)S(1)}, u32[]{:S(2)}, u32[]{:S(2)}) collective-permute-start(bf16[3,16,384]{2,1,0:T(8,128)(2,1)S(1)} %bitcast.146), channel_id=1, source_target_pairs={{0,4},{4,0},{8,12},{12,8},{16,20},{20,16},{24,28},{28,24},{1,5},{5... | collective-permute-start | bytes 110600 | tf_op jit(solution)/shard_map/ppermute | solution.py:362
  33.2 1.9 %collective-permute-start.5 = (bf16[3,16,384]{2,1,0:T(8,128)(2,1)S(1)}, bf16[3,16,384]{2,1,0:T(8,128)(2,1)S(1)}, u32[]{:S(2)}, u32[]{:S(2)}) collective-permute-start(bf16[3,16,384]{2,1,0:T(8,128)(2,1)S(1)} %bitcast.145), channel_id=1, source_target_pairs={{0,1},{1,0},{2,3},{3,2},{4,8},{5,9},{6,10},{7,11},{8,4},{9,5},{10,... | collective-permute-start | bytes 110600 | tf_op jit(solution)/shard_map/ppermute | solution.py:378
  35.1 5.5 %collective-permute-start.8 = (bf16[2,16,48,384]{3,2,1,0:T(8,128)(2,1)S(1)}, bf16[2,16,48,384]{3,2,1,0:T(8,128)(2,1)S(1)}, u32[]{:S(2)}, u32[]{:S(2)}) collective-permute-start(bf16[2,16,48,384]{3,2,1,0:T(8,128)(2,1)S(1)} %bitcast.111), channel_id=1, source_target_pairs={{0,1},{1,0},{2,3},{3,2},{4,5},{5,4},{6,7},{7,6},{8,9},{9,8},{10,11... | collective-permute-start | bytes 3538952 | tf_op jit(solution)/shard_map/ppermute | solution.py:392
  35.5 5.1 %collective-permute-start.7 = (bf16[22,3,384]{2,1,0:T(4,128)(2,1)S(1)}, bf16[22,3,384]{2,1,0:T(4,128)(2,1)S(1)}, u32[]{:S(2)}, u32[]{:S(2)}) collective-permute-start(bf16[22,3,384]{2,1,0:T(4,128)(2,1)S(1)} %get-tuple-element.261), channel_id=1, source_target_pairs={{0,4},{1,2},{2,1},{3,7},{4,0},{5,6},{6,5},{7,3},{8,12},{9,10},{10,... | collective-permute-start | bytes 152072 | tf_op jit(solution)/shard_map/ppermute | solution.py:378
  38.4 2.3 %collective-permute-start.6 = (bf16[22,3,384]{2,1,0:T(4,128)(2,1)S(1)}, bf16[22,3,384]{2,1,0:T(4,128)(2,1)S(1)}, u32[]{:S(2)}, u32[]{:S(2)}) collective-permute-start(bf16[22,3,384]{2,1,0:T(4,128)(2,1)S(1)} %get-tuple-element.262), channel_id=1, source_target_pairs={{0,1},{1,0},{2,3},{3,2},{4,5},{5,4},{6,7},{7,6},{8,9},{9,8},{10,11... | collective-permute-start | bytes 152072 | tf_op jit(solution)/shard_map/ppermute | solution.py:362
  47.7 13.7 %collective-permute-start.9 = (bf16[2,16,48,384]{3,2,1,0:T(8,128)(2,1)S(1)}, bf16[2,16,48,384]{3,2,1,0:T(8,128)(2,1)S(1)}, u32[]{:S(2)}, u32[]{:S(2)}) collective-permute-start(bf16[2,16,48,384]{3,2,1,0:T(8,128)(2,1)S(1)} %bitcast.110), channel_id=1, source_target_pairs={{0,1},{1,0},{2,3},{3,2},{4,5},{5,4},{6,7},{7,6},{8,9},{9,8},{10,11... | collective-permute-start | bytes 3538952 | tf_op jit(solution)/shard_map/ppermute | solution.py:392
  48.2 9.4 %collective-permute-start.13 = (bf16[1,4,2,48,384]{4,3,2,1,0:T(8,128)(2,1)S(1)}, bf16[1,4,2,48,384]{4,3,2,1,0:T(8,128)(2,1)S(1)}, u32[]{:S(2)}, u32[]{:S(2)}) collective-permute-start(bf16[1,4,2,48,384]{4,3,2,1,0:T(8,128)(2,1)S(1)} %dynamic-slice_bitcast_fusion), channel_id=1, source_target_pairs={{0,4},{1,5},{2,6},{3,7},{4,0},{5,1},{6,2},{7,3},{8,12},{9,13},{10,... | collective-permute-start | bytes 884744 | tf_op jit(solution)/shard_map/ppermute | solution.py:392
  50.1 9.1 %collective-permute-start.12 = (bf16[1,8,1,48,384]{4,3,1,2,0:T(8,128)(2,1)S(1)}, bf16[1,8,1,48,384]{4,3,1,2,0:T(8,128)(2,1)S(1)}, u32[]{:S(2)}, u32[]{:S(2)}) collective-permute-start(bf16[1,8,1,48,384]{4,3,1,2,0:T(8,128)(2,1)S(1)} %dynamic-slice_bitcast_fusion.1), channel_id=1, source_target_pairs={{0,2},{1,3},{2,0},{3,1},{4,6},{5,7},{6,4},{7,5},{8,10},{9,11},{10,... | collective-permute-start | bytes 884744 | tf_op jit(solution)/shard_map/ppermute | solution.py:392
  59.3 9.2 %collective-permute-start.14 = (bf16[384,384]{1,0:T(8,128)(2,1)S(1)}, bf16[384,384]{1,0:T(8,128)(2,1)S(1)}, u32[]{:S(2)}, u32[]{:S(2)}) collective-permute-start(bf16[384,384]{1,0:T(8,128)(2,1)S(1)} %pad_maximum_fusion.3), channel_id=1, source_target_pairs={{0,8},{1,9},{2,10},{3,11},{4,12},{5,13},{6,14},{7,15},{8,0},{9,1},... | collective-permute-start | bytes 884744 | tf_op jit(solution)/shard_map/ppermute | solution.py:392
  61.9 9.8 %collective-permute-start.11 = (bf16[1,4,2,48,384]{4,3,1,2,0:T(8,128)(2,1)S(1)}, bf16[1,4,2,48,384]{4,3,1,2,0:T(8,128)(2,1)S(1)}, u32[]{:S(2)}, u32[]{:S(2)}) collective-permute-start(bf16[1,4,2,48,384]{4,3,1,2,0:T(8,128)(2,1)S(1)} %bitcast.139), channel_id=1, source_target_pairs={{0,4},{1,5},{2,6},{3,7},{4,0},{5,1},{6,2},{7,3},{8,12},{9,13},{10,... | collective-permute-start | bytes 884744 | tf_op jit(solution)/shard_map/ppermute | solution.py:392
  63.5 8.2 %collective-permute-start.10 = (bf16[1,8,1,48,384]{4,3,1,2,0:T(8,128)(2,1)S(1)}, bf16[1,8,1,48,384]{4,3,1,2,0:T(8,128)(2,1)S(1)}, u32[]{:S(2)}, u32[]{:S(2)}) collective-permute-start(bf16[1,8,1,48,384]{4,3,1,2,0:T(8,128)(2,1)S(1)} %get-tuple-element.241), channel_id=1, source_target_pairs={{0,2},{1,3},{2,0},{3,1},{4,6},{5,7},{6,4},{7,5},{8,10},{9,11},{10,... | collective-permute-start | bytes 884744 | tf_op jit(solution)/shard_map/ppermute | solution.py:392
  67.6 4.1 %collective-permute-start.17 = (bf16[64,384]{1,0:T(8,128)(2,1)S(1)}, bf16[64,384]{1,0:T(8,128)(2,1)S(1)}, u32[]{:S(2)}, u32[]{:S(2)}) collective-permute-start(bf16[64,384]{1,0:T(8,128)(2,1)S(1)} %get-tuple-element.184), channel_id=1, source_target_pairs={{0,1},{1,0},{2,3},{3,2},{4,5},{5,4},{6,7},{7,6},{8,9},{9,8},{10,11... | collective-permute-start | bytes 147464 | tf_op jit(solution)/shard_map/ppermute | solution.py:392
  67.7 4.0 %collective-permute-start.15 = (bf16[3,16,384]{2,1,0:T(8,128)(2,1)S(1)}, bf16[3,16,384]{2,1,0:T(8,128)(2,1)S(1)}, u32[]{:S(2)}, u32[]{:S(2)}) collective-permute-start(bf16[3,16,384]{2,1,0:T(8,128)(2,1)S(1)} %bitcast.144), channel_id=1, source_target_pairs={{0,4},{4,0},{8,12},{12,8},{16,20},{20,16},{24,28},{28,24},{1,5},{5... | collective-permute-start | bytes 110600 | tf_op jit(solution)/shard_map/ppermute | solution.py:362
  68.5 3.3 %collective-permute-start.16 = (bf16[3,16,384]{2,1,0:T(8,128)(2,1)S(1)}, bf16[3,16,384]{2,1,0:T(8,128)(2,1)S(1)}, u32[]{:S(2)}, u32[]{:S(2)}) collective-permute-start(bf16[3,16,384]{2,1,0:T(8,128)(2,1)S(1)} %bitcast.143), channel_id=1, source_target_pairs={{0,1},{1,0},{2,3},{3,2},{4,8},{5,9},{6,10},{7,11},{8,4},{9,5},{10,... | collective-permute-start | bytes 110600 | tf_op jit(solution)/shard_map/ppermute | solution.py:378
  72.3 8.1 %collective-permute-start.19 = (bf16[352,384]{1,0:T(8,128)(2,1)S(1)}, bf16[352,384]{1,0:T(8,128)(2,1)S(1)}, u32[]{:S(2)}, u32[]{:S(2)}) collective-permute-start(bf16[352,384]{1,0:T(8,128)(2,1)S(1)} %get-tuple-element.287), channel_id=1, source_target_pairs={{0,2},{1,3},{2,0},{3,1},{4,6},{5,7},{6,4},{7,5},{8,10},{9,11},{10,... | collective-permute-start | bytes 811016 | tf_op jit(solution)/shard_map/ppermute | solution.py:392
  74.0 8.8 %collective-permute-start.18 = (bf16[352,384]{1,0:T(8,128)(2,1)S(1)}, bf16[352,384]{1,0:T(8,128)(2,1)S(1)}, u32[]{:S(2)}, u32[]{:S(2)}) collective-permute-start(bf16[352,384]{1,0:T(8,128)(2,1)S(1)} %get-tuple-element.288), channel_id=1, source_target_pairs={{0,4},{1,5},{2,6},{3,7},{4,0},{5,1},{6,2},{7,3},{8,12},{9,13},{10,... | collective-permute-start | bytes 811016 | tf_op jit(solution)/shard_map/ppermute | solution.py:392
  77.1 7.0 %collective-permute-start.21 = (bf16[22,3,384]{2,1,0:T(4,128)(2,1)S(1)}, bf16[22,3,384]{2,1,0:T(4,128)(2,1)S(1)}, u32[]{:S(2)}, u32[]{:S(2)}) collective-permute-start(bf16[22,3,384]{2,1,0:T(4,128)(2,1)S(1)} %get-tuple-element.259), channel_id=1, source_target_pairs={{0,4},{1,2},{2,1},{3,7},{4,0},{5,6},{6,5},{7,3},{8,12},{9,10},{10,... | collective-permute-start | bytes 152072 | tf_op jit(solution)/shard_map/ppermute | solution.py:378
  77.2 6.9 %collective-permute-start.20 = (bf16[22,3,384]{2,1,0:T(4,128)(2,1)S(1)}, bf16[22,3,384]{2,1,0:T(4,128)(2,1)S(1)}, u32[]{:S(2)}, u32[]{:S(2)}) collective-permute-start(bf16[22,3,384]{2,1,0:T(4,128)(2,1)S(1)} %get-tuple-element.260), channel_id=1, source_target_pairs={{0,1},{1,0},{2,3},{3,2},{4,5},{5,4},{6,7},{7,6},{8,9},{9,8},{10,11... | collective-permute-start | bytes 152072 | tf_op jit(solution)/shard_map/ppermute | solution.py:362
  77.6 6.4 %collective-permute-start.22 = (bf16[64,384]{1,0:T(8,128)(2,1)S(1)}, bf16[64,384]{1,0:T(8,128)(2,1)S(1)}, u32[]{:S(2)}, u32[]{:S(2)}) collective-permute-start(bf16[64,384]{1,0:T(8,128)(2,1)S(1)} %add_convert_fusion.14), channel_id=1, source_target_pairs={{0,6},{1,7},{2,4},{3,5},{4,2},{5,3},{6,0},{7,1},{8,14},{9,15},{10,... | collective-permute-start | bytes 147464 | tf_op jit(solution)/shard_map/ppermute | solution.py:392
  84.2 8.0 %collective-permute-start.24 = (bf16[96,384]{1,0:T(8,128)(2,1)S(1)}, bf16[96,384]{1,0:T(8,128)(2,1)S(1)}, u32[]{:S(2)}, u32[]{:S(2)}) collective-permute-start(bf16[96,384]{1,0:T(8,128)(2,1)S(1)} %bitcast.142), channel_id=1, source_target_pairs={{0,16},{1,17},{2,18},{3,19},{4,20},{5,21},{6,22},{7,23},{8,24},{9,... | collective-permute-start | bytes 221192 | tf_op jit(solution)/shard_map/ppermute | solution.py:392
  85.7 6.5 %collective-permute-start.23 = (bf16[256,384]{1,0:T(8,128)(2,1)S(1)}, bf16[256,384]{1,0:T(8,128)(2,1)S(1)}, u32[]{:S(2)}, u32[]{:S(2)}) collective-permute-start(bf16[256,384]{1,0:T(8,128)(2,1)S(1)} %pad_maximum_fusion.6), channel_id=1, source_target_pairs={{0,8},{1,9},{2,10},{3,11},{4,12},{5,13},{6,14},{7,15},{8,0},{9,1},... | collective-permute-start | bytes 589832 | tf_op jit(solution)/shard_map/ppermute | solution.py:392
  92.4 7.2 %collective-permute-start.25 = (bf16[160,384]{1,0:T(8,128)(2,1)S(1)}, bf16[160,384]{1,0:T(8,128)(2,1)S(1)}, u32[]{:S(2)}, u32[]{:S(2)}) collective-permute-start(bf16[160,384]{1,0:T(8,128)(2,1)S(1)} %pad_maximum_fusion.7), channel_id=1, source_target_pairs={{0,16},{1,17},{2,18},{3,19},{4,20},{5,21},{6,22},{7,23},{8,24},{9,... | collective-permute-start | bytes 368648 | tf_op jit(solution)/shard_map/ppermute | solution.py:392
  99.6 1.3 %collective-permute-start.26 = (bf16[64,384]{1,0:T(8,128)(2,1)S(1)}, bf16[64,384]{1,0:T(8,128)(2,1)S(1)}, u32[]{:S(2)}, u32[]{:S(2)}) collective-permute-start(bf16[64,384]{1,0:T(8,128)(2,1)S(1)} %add_convert_fusion.11.mine), channel_id=1, source_target_pairs={{0,1},{1,0},{2,3},{3,2},{4,5},{5,4},{6,7},{7,6},{8,9},{9,8},{10,11... | collective-permute-start | bytes 147464 | tf_op jit(solution)/shard_map/ppermute | solution.py:392
  (3 other events, 14.4 us)

commit v11 on v9

--- a/solution.py
+++ b/solution.py
@@ -54,17 +54,18 @@
     return max(d for d in range(1, rows + 1) if rows % d == 0 and d <= most)
 
 
-def conv_pass(source, row0, col0, taps, target, rows, cols, back=False):
+def conv_pass(source, row0, col0, taps, layer, target, rows, cols, back=False):
     strip = strip_rows(rows, cols)
     groups = source.shape[0]
 
     def one_strip(step, carry):
         g = step // (rows // strip)
         top = (step % (rows // strip)) * strip
+        lanes = pl.ds(pl.multiple_of(g * LANES, LANES), LANES)
         sums = [jnp.zeros((cols, LANES), F32) for _ in range(strip)]
         for b in range(7):
             spots = [48 - 7 * a - b if back else 7 * a + b for a in range(7)]
-            weights = [taps[g, pl.ds(spot, 1), :] for spot in spots]
+            weights = [taps[spot, pl.ds(layer, 1), lanes] for spot in spots]
             for r in range(strip + 6):
                 line = source[g, row0 + top + r, pl.ds(col0 + b, cols), :]
                 for a in range(7):
@@ -221,7 +222,7 @@
     rows, cols = z_out.shape[1:3]
     for g in range(groups):
         xs[g] = xpad[:, :, g * LANES : (g + 1) * LANES].astype(F32)
-    conv_pass(xs, 0, 0, taps.at[0], zs, mid_rows, mid_cols)
+    conv_pass(xs, 0, 0, taps, 0, zs, mid_rows, mid_cols)
     z_out[...] = zs[:, HALO : HALO + rows, HALO : HALO + cols, :]
     strip = act.shape[0] // mid_cols
     for wait in waits:
@@ -232,7 +233,7 @@
         hat, _ = norm_parts(joined(zs, pl.ds(top, strip)))
         normed = (hat * gains[0:1] + shifts[0:1]).astype(BF16)
         for cut in hidden_chunks(w_in0.shape[2]):
-            pre = dot_nn(normed, w_in0[0, :, cut]) + b_in[0, :, cut]
+            pre = dot_nn(normed, w_in0[0, :, cut]) + b_in[0:1, cut]
             act[:, cut] = gelu_only(pre).astype(BF16)
         mixed = dot_nt(act[...], w_out0[0])
         row = lax.broadcasted_iota(jnp.int32, (strip, mid_cols, 1), 0) + (top - HALO) + place[0]
@@ -252,12 +253,12 @@
     dz_out, normed, act, gpre, db, dgain, dshift, z, w_in1, w_out1, arrived,
 ):
     waits = fetch_layers(((w_in, 1, w_in1), (w_out, 1, w_out1)), arrived)
-    conv_pass(mids, 0, 0, taps.at[1], z, *z.shape[1:3])
+    conv_pass(mids, 0, 0, taps, 1, z, *z.shape[1:3])
     hat, inv = norm_parts(joined(z, slice(None)))
     normed[...] = (hat * gains[1:2] + shifts[1:2]).astype(BF16)
     for wait in waits:
         wait.wait()
-    mlp_grads(normed, grad, w_in1, b_in.at[1], w_out1, act, gpre, db)
+    mlp_grads(normed, grad, w_in1, b_in.at[pl.ds(1, 1)], w_out1, act, gpre, db)
     dz_of(gpre, w_in1, hat, inv, gains[1:2], dz_out, dgain, dshift)
 
 
@@ -268,7 +269,7 @@
     inv_out[...] = jnp.broadcast_to(inv, inv_out.shape)
     normed[...] = (hat * gains[0:1] + shifts[0:1]).astype(BF16)
     wait.wait()
-    hidden_forward(normed, w_in0, b_in.at[0], act, slope)
+    hidden_forward(normed, w_in0, b_in.at[pl.ds(0, 1)], act, slope)
 
 
 def low_kernel(
@@ -277,7 +278,7 @@
 ):
     *dw, dzs, spread, gpre, w_in0, w_out0, arrived = rest
     waits = fetch_layers(((w_out, 0, w_out0), (w_in, 0, w_in0)), arrived)
-    spread_pass(dzpad, dzs, taps.at[1], spread)
+    spread_pass(dzpad, dzs, taps, 1, spread)
     gmid[...] = (grad[...].astype(F32) + joined(spread, slice(None))).astype(BF16)
     for wait in waits:
         wait.wait()
@@ -290,14 +291,14 @@
     weight_grads(place, normed, grad, act, gpre, dw, per)
 
 
-def spread_pass(dzpad, dzs, taps, spread):
+def spread_pass(dzpad, dzs, taps, layer, spread):
     for g in range(dzs.shape[0]):
         dzs[g] = dzpad[:, :, g * LANES : (g + 1) * LANES].astype(F32)
-    conv_pass(dzs, 0, 0, taps, spread, *spread.shape[1:3], back=True)
+    conv_pass(dzs, 0, 0, taps, layer, spread, *spread.shape[1:3], back=True)
 
 
 def last_kernel(dzpad, gmid, taps, out, dzs, spread):
-    spread_pass(dzpad, dzs, taps.at[0], spread)
+    spread_pass(dzpad, dzs, taps, 0, spread)
     out[...] = (gmid[...].astype(F32) + joined(spread, slice(None))).astype(BF16)
 
 
@@ -355,7 +356,7 @@
     return jax.ShapeDtypeStruct(dims, dtype)
 
 
-def run(kernel, outs, scratch, args, specs=None, fetched=0, name=None):
+def run(kernel, outs, scratch, args, specs=None, fetched=0, name=None, room=46):
     vmem = pl.BlockSpec(memory_space=pltpu.VMEM)
     semaphores = [pltpu.SemaphoreType.DMA((fetched,))] if fetched else []
     return pl.pallas_call(
@@ -366,7 +367,7 @@
         ],
         out_specs=tuple(vmem for _ in outs),
         scratch_shapes=[pltpu.VMEM(s.shape, s.dtype) for s in scratch] + semaphores,
-        compiler_params=pltpu.CompilerParams(vmem_limit_bytes=46 * 1024 * 1024),
+        compiler_params=pltpu.CompilerParams(vmem_limit_bytes=room * 1024 * 1024),
         name=name,
     )(*args)
 
@@ -456,8 +457,7 @@
     grad_scale = 1.0 / math.sqrt(rows * cols * total)
     pixels = rows * cols
 
-    taps = kernels.reshape(layers, 49, groups, LANES).transpose(0, 2, 1, 3)
-    biases = b_in[:, None, :]
+    taps = kernels.transpose(1, 2, 0, 3).reshape(49, layers, channels)
     place = jnp.stack(
         [
             lax.axis_index("rows") * rows,
@@ -473,6 +473,9 @@
     odd_col, odd_row = (at_col & 1) == 1, (at_row & 1) == 1
     outer_col = (at_col == 0) | (at_col == n_cols - 1)
     outer_row = (at_row == 0) | (at_row == n_rows - 1)
+    activations, place, mine, odd_col, odd_row, outer_col, outer_row = lax.optimization_barrier(
+        (activations, place, mine, odd_col, odd_row, outer_col, outer_row)
+    )
 
     def rim_cols(tile, width):
         twin, other = edges(tile, 1, width, odd_col)
@@ -498,9 +501,6 @@
     small_rows = 64
 
     xpad = filled(rim_cols(rim_rows(activations, WIDE), WIDE))
-    xpad, place, mine, odd_col, odd_row, outer_col, outer_row = lax.optimization_barrier(
-        (xpad, place, mine, odd_col, odd_row, outer_col, outer_row)
-    )
     mids, z0 = run(
         forward_kernel,
         (shape(groups, mid_rows, mid_cols, LANES), tile_z),
@@ -510,19 +510,21 @@
             shape(strip * mid_cols, hidden, dtype=BF16),
         ]
         + weights,
-        (place, xpad, taps, norm_gains, norm_shifts, w_in, w_out, biases),
+        (place, xpad, taps, norm_gains, norm_shifts, w_in, w_out, b_in),
         [pltpu.SMEM] + [None] * 4 + [pl.ANY] * 2 + [None],
         fetched=2,
         name="forward",
+        room=50,
     )
     dz1, normed1, act1, gpre1, *small1 = run(
         top_kernel,
         (tile_b, tile_b, tile_h, tile_h) + small_outs,
         [tile_z] + weights,
-        (mids, grad_flat, taps, norm_gains, norm_shifts, w_in, w_out, biases),
+        (mids, grad_flat, taps, norm_gains, norm_shifts, w_in, w_out, b_in),
         [None] * 5 + [pl.ANY] * 2 + [None],
         fetched=2,
         name="top",
+        room=50,
     )
 
     sides = (col_bits - 1, col_bits)
@@ -591,7 +593,7 @@
         again_kernel,
         (tile_f, shape(pixels, LANES), tile_b, tile_h, shape(pixels, hidden)),
         weights[:1],
-        (z0, norm_gains, norm_shifts, w_in, biases),
+        (z0, norm_gains, norm_shifts, w_in, b_in),
         [None] * 3 + [pl.ANY, None],
         fetched=1,
         name="again",

time: 100 us -> 96.6 us (0.966)
  local copies, waits for them, and re-layouts: 2.92 us -> 1.07 us
  starting transfers between devices: 32.1 us -> 30.3 us
  waiting for transfers between devices: 27.6 us -> 28.7 us
    unnamed x18 -> x16, local copies, waits for them, and re-layouts: 1.76 us -> 0.1 us
  transfers between devices with their start and end apart: 27 -> 27, of which waited for: 11 -> 13; matrix products, arithmetic and copies ran while one was open for 2% -> 2% of each run, Pallas kernels for 15% -> 16%
where the time goes in v11:
time: 96.6 us; the launch traced here: 96.4 us
  starting transfers between devices  30.3 us (31%)
  Pallas kernels  30.2 us (31%)
  waiting for transfers between devices  28.7 us (30%)
  other arithmetic  4.8 us (5%)
  between operations  1.27 us (1%)
  local copies, waits for them, and re-layouts  1.07 us (1%)
    pallas_call x9, Pallas kernels, run(): pl.pallas_call(kernel, out_shape=outs, in_specs=[vmem if s is None else p...  30.2 us
    ppermute x15, waiting for transfers between devices, flip_bit(): return lax.ppermute(value, both, [(i, i ^ flip) for i in range(total)])  18.8 us
    ppermute x15, starting transfers between devices, flip_bit(): return lax.ppermute(value, both, [(i, i ^ flip) for i in range(total)])  17.5 us
    ppermute x6, starting transfers between devices, to_twin(): lax.ppermute(edge, axis, [(i, i ^ 1) for i in range(count) if i ^ 1 < cou...  6.96 us
    ppermute x6, waiting for transfers between devices, to_twin(): lax.ppermute(edge, axis, [(i, i ^ 1) for i in range(count) if i ^ 1 < cou...  6.55 us
    ppermute x6, starting transfers between devices, to_other(): return lax.ppermute(edge, ('rows', 'cols'), pairs)  5.8 us
    ppermute x6, waiting for transfers between devices, to_other(): return lax.ppermute(edge, ('rows', 'cols'), pairs)  3.4 us
  transfers between devices with their start and end apart: 27, of which 13 were waited for; matrix products, arithmetic and copies ran while one was open for 2% of the time, Pallas kernels for 16%

profile of v11, /device:TPU:0, one launch (start us, length us, event | category | flops | bytes accessed | tf_op | source)
XLA Modules:
  0.0 96.4 jit_solution(9212410357270970489)
XLA Ops:
  0.7 0.9 broadcast_select_fusion.8
  1.7 3.0 %collective-permute-start = (bf16[6,16,384]{2,1,0:T(8,128)(2,1)S(1)}, bf16[6,16,384]{2,1,0:T(8,128)(2,1)S(1)}, u32[]{:S(2)}, u32[]{:S(2)}) collective-permute-start(bf16[6,16,384]{2,1,0:T(8,128)(2,1)S(1)} %get-tuple-element.280), channel_id=1, source_target_pairs={{0,4},{4,0},{8,12},{12,8},{16,20},{20,16},{24,28},{28,24},{1,5},{5... | collective-permute-start | bytes 221192 | tf_op jit(solution)/shard_map/ppermute | solution.py:384
  4.7 3.4 %collective-permute-done = bf16[6,16,384]{2,1,0:T(8,128)(2,1)S(1)} collective-permute-done((bf16[6,16,384]{2,1,0:T(8,128)(2,1)S(1)}, bf16[6,16,384]{2,1,0:T(8,128)(2,1)S(1)}, u32[]{:S(2)}, u32[]{:S(2)}) %collective-permute-start) | collective-permute-done | bytes 73760 | tf_op jit(solution)/shard_map/ppermute | solution.py:384
  8.1 1.0 %pad_maximum_fusion.2 = bf16[28,16,384]{2,1,0:T(8,128)(2,1)S(1)} fusion(bf16[6,16,384]{2,1,0:T(8,128)(2,1)S(1)} %get-tuple-element.290, bf16[16,16,384]{2,1,0:T(8,128)(2,1)} %param.8, bf16[6,16,384]{2,1,0:T(8,128)(2,1)S(1)} %get-tuple-element.289), kind=kLoop, calls=%fused_computation.29 | loop fusion | flops 344064 | bytes 688128 | tf_op jit(solution)/shard_map/concatenate | solution.py:407
  9.3 2.5 %collective-permute-start.3 = (bf16[28,6,384]{2,1,0:T(8,128)(2,1)S(1)}, bf16[28,6,384]{2,1,0:T(8,128)(2,1)S(1)}, u32[]{:S(2)}, u32[]{:S(2)}) collective-permute-start(bf16[28,6,384]{2,1,0:T(8,128)(2,1)S(1)} %get-tuple-element.257), channel_id=1, source_target_pairs={{0,4},{1,2},{2,1},{3,7},{4,0},{5,6},{6,5},{7,3},{8,12},{9,10},{10,... | collective-permute-start | bytes 387080 | tf_op jit(solution)/shard_map/ppermute | solution.py:400
  11.8 3.4 %collective-permute-done.3 = bf16[28,6,384]{2,1,0:T(8,128)(2,1)S(1)} collective-permute-done((bf16[28,6,384]{2,1,0:T(8,128)(2,1)S(1)}, bf16[28,6,384]{2,1,0:T(8,128)(2,1)S(1)}, u32[]{:S(2)}, u32[]{:S(2)}) %collective-permute-start.3) | collective-permute-done | bytes 129056 | tf_op jit(solution)/shard_map/ppermute | solution.py:400
  15.7 8.8 %forward.1 = (f32[3,22,24,128]{3,2,1,0:T(8,128)S(1)}, f32[3,16,16,128]{3,2,1,0:T(8,128)S(1)}) custom-call(s32[5]{0:T(128)S(1)} %stack.25.place, bf16[28,32,384]{2,1,0:T(8,128)(2,1)S(1)} %fusion.12.xpad, f32[49,2,384]{2,1,0:T(2,128)S(1)} %bitcast.101, f32[2,384]{1,0:T(2,128)S(1)} %copy-done.4, f32[2,384]{1,0:T(2,128)S(1)} %copy-done.5, ...), custom_call_target="tpu_custom_call" | custom-call | tf_op jit(solution)/shard_map/forward/pallas_call | solution.py:362
  24.5 4.7 %top.1 = (bf16[256,384]{1,0:T(8,128)(2,1)S(1)}, bf16[256,384]{1,0:T(8,128)(2,1)S(1)}, bf16[256,1536]{1,0:T(8,128)(2,1)S(1)}, bf16[256,1536]{1,0:T(8,128)(2,1)S(1...) custom-call(f32[3,22,24,128]{3,2,1,0:T(8,128)S(1)} %get-tuple-element.131.mids, ...), custom_call_target="tpu_custom_call" | custom-call | tf_op jit(solution)/shard_map/top/pallas_call | solution.py:362
  29.3 2.1 %collective-permute-start.4 = (bf16[3,16,384]{2,1,0:T(8,128)(2,1)S(1)}, bf16[3,16,384]{2,1,0:T(8,128)(2,1)S(1)}, u32[]{:S(2)}, u32[]{:S(2)}) collective-permute-start(bf16[3,16,384]{2,1,0:T(8,128)(2,1)S(1)} %bitcast.150), channel_id=1, source_target_pairs={{0,4},{4,0},{8,12},{12,8},{16,20},{20,16},{24,28},{28,24},{1,5},{5... | collective-permute-start | bytes 110600 | tf_op jit(solution)/shard_map/ppermute | solution.py:384
  31.3 1.6 %weights_top.1 = (bf16[2,768,384]{2,1,0:T(8,128)(2,1)S(1)}, bf16[2,768,384]{2,1,0:T(8,128)(2,1)S(1)}) custom-call(s32[5]{0:T(128)S(1)} %stack.25.place, bf16[256,384]{1,0:T(8,128)(2,1)S(1)} %get-tuple-element.133.normed, bf16[256,1536]{1,0:T(8,128)(2,1)S(1)} %get-tuple-element.134.act, bf16[256,1536]{1,0:T(8,128)(2,1)S(1)} %get-tuple-element.135.gpre, ...), custom_call_target="tpu_custom_call" | custom-call | tf_op jit(solution)/shard_map/weights_top/pallas_call | solution.py:362
  34.0 3.1 %collective-permute-start.7 = (bf16[22,3,384]{2,1,0:T(4,128)(2,1)S(1)}, bf16[22,3,384]{2,1,0:T(4,128)(2,1)S(1)}, u32[]{:S(2)}, u32[]{:S(2)}) collective-permute-start(bf16[22,3,384]{2,1,0:T(4,128)(2,1)S(1)} %get-tuple-element.273), channel_id=1, source_target_pairs={{0,4},{1,2},{2,1},{3,7},{4,0},{5,6},{6,5},{7,3},{8,12},{9,10},{10,... | collective-permute-start | bytes 152072 | tf_op jit(solution)/shard_map/ppermute | solution.py:400
  37.2 2.4 %again.1 = (f32[256,384]{1,0:T(8,128)S(1)}, f32[256,128]{1,0:T(8,128)S(1)}, bf16[256,384]{1,0:T(8,128)(2,1)S(1)}, bf16[256,1536]{1,0:T(8,128)(2,1)S(1)}, f32[256,1536]{1,0:T(8,128)S(1)}) custom-call(f32[3,16,16,128]{3,2,1,0:T(8,128)S(1)} %get-tuple-element.144.z0, f32[2,384]{1,0:T(2,128)S(1)} %copy-done.4, f32[2,384]{1,0:T(2,128)S(1)} %copy-done.5, ...), custom_call_target="tpu_custom_call" | custom-call | tf_op jit(solution)/shard_map/again/pallas_call | solution.py:362
  40.1 1.9 %collective-permute-start.10 = (bf16[1,4,2,48,384]{4,3,2,1,0:T(8,128)(2,1)S(1)}, bf16[1,4,2,48,384]{4,3,2,1,0:T(8,128)(2,1)S(1)}, u32[]{:S(2)}, u32[]{:S(2)}) collective-permute-start(bf16[1,4,2,48,384]{4,3,2,1,0:T(8,128)(2,1)S(1)} %get-tuple-element.251), channel_id=1, source_target_pairs={{0,4},{1,5},{2,6},{3,7},{4,0},{5,1},{6,2},{7,3},{8,12},{9,13},{10,... | collective-permute-start | bytes 884744 | tf_op jit(solution)/shard_map/ppermute | solution.py:414
  42.8 4.5 %low.1 = (bf16[256,384]{1,0:T(8,128)(2,1)S(1)}, bf16[256,384]{1,0:T(8,128)(2,1)S(1)}, f32[1,1536]{1,0:T(1,128)S(1)}, f32[1,384]{1,0:T(1,128)S(1)}, f32[1,384]{1,...) custom-call(s32[5]{0:T(128)S(1)} %stack.25.place, ...), custom_call_target="tpu_custom_call" | custom-call | tf_op jit(solution)/shard_map/low/pallas_call | solution.py:362
  47.3 1.7 %collective-permute-done.10 = bf16[1,4,2,48,384]{4,3,2,1,0:T(8,128)(2,1)S(1)} collective-permute-done((bf16[1,4,2,48,384]{4,3,2,1,0:T(8,128)(2,1)S(1)}, bf16[1,4,2,48,384]{4,3,2,1,0:T(8,128)(2,1)S(1)}, u32[]{:S(2)}, u32[]{:S(2)}) %collective-permute-start.10) | collective-permute-done | bytes 294944 | tf_op jit(solution)/shard_map/ppermute | solution.py:414
  49.0 1.6 %collective-permute-done.9 = bf16[1,8,1,48,384]{4,3,1,2,0:T(8,128)(2,1)S(1)} collective-permute-done((bf16[1,8,1,48,384]{4,3,1,2,0:T(8,128)(2,1)S(1)}, bf16[1,8,1,48,384]{4,3,1,2,0:T(8,128)(2,1)S(1)}, u32[]{:S(2)}, u32[]{:S(2)}) %collective-permute-start.9) | collective-permute-done | bytes 294944 | tf_op jit(solution)/shard_map/ppermute | solution.py:414
  50.9 2.9 %collective-permute-start.14 = (bf16[384,384]{1,0:T(8,128)(2,1)S(1)}, bf16[384,384]{1,0:T(8,128)(2,1)S(1)}, u32[]{:S(2)}, u32[]{:S(2)}) collective-permute-start(bf16[384,384]{1,0:T(8,128)(2,1)S(1)} %pad_maximum_fusion.3), channel_id=1, source_target_pairs={{0,8},{1,9},{2,10},{3,11},{4,12},{5,13},{6,14},{7,15},{8,0},{9,1},... | collective-permute-start | bytes 884744 | tf_op jit(solution)/shard_map/ppermute | solution.py:414
  55.6 3.7 %taps.1 = (bf16[64,384]{1,0:T(8,128)(2,1)S(1)}, bf16[64,384]{1,0:T(8,128)(2,1)S(1)}) custom-call(s32[5]{0:T(128)S(1)} %stack.25.place, f32[3,22,24,128]{3,2,1,0:T(8,128)S(1)} %get-tuple-element.131.mids, bf16[28,32,384]{2,1,0:T(8,128)(2,1)S(1)} %fusion.12.xpad, bf16[256,384]{1,0:T(8,128)(2,1)S(1)} %get-tuple-element.184.dz0, ...), custom_call_target="tpu_custom_call" | custom-call | tf_op jit(solution)/shard_map/taps/pallas_call | solution.py:362
  59.5 1.4 %collective-permute-start.15 = (bf16[3,16,384]{2,1,0:T(8,128)(2,1)S(1)}, bf16[3,16,384]{2,1,0:T(8,128)(2,1)S(1)}, u32[]{:S(2)}, u32[]{:S(2)}) collective-permute-start(bf16[3,16,384]{2,1,0:T(8,128)(2,1)S(1)} %bitcast.148), channel_id=1, source_target_pairs={{0,4},{4,0},{8,12},{12,8},{16,20},{20,16},{24,28},{28,24},{1,5},{5... | collective-permute-start | bytes 110600 | tf_op jit(solution)/shard_map/ppermute | solution.py:384
  61.5 2.8 %collective-permute-done.15 = bf16[3,16,384]{2,1,0:T(8,128)(2,1)S(1)} collective-permute-done((bf16[3,16,384]{2,1,0:T(8,128)(2,1)S(1)}, bf16[3,16,384]{2,1,0:T(8,128)(2,1)S(1)}, u32[]{:S(2)}, u32[]{:S(2)}) %collective-permute-start.15) | collective-permute-done | bytes 36896 | tf_op jit(solution)/shard_map/ppermute | solution.py:384
  64.9 2.7 %collective-permute-start.18 = (bf16[352,384]{1,0:T(8,128)(2,1)S(1)}, bf16[352,384]{1,0:T(8,128)(2,1)S(1)}, u32[]{:S(2)}, u32[]{:S(2)}) collective-permute-start(bf16[352,384]{1,0:T(8,128)(2,1)S(1)} %get-tuple-element.300), channel_id=1, source_target_pairs={{0,4},{1,5},{2,6},{3,7},{4,0},{5,1},{6,2},{7,3},{8,12},{9,13},{10,... | collective-permute-start | bytes 811016 | tf_op jit(solution)/shard_map/ppermute | solution.py:414
  67.6 1.4 %collective-permute-start.19 = (bf16[352,384]{1,0:T(8,128)(2,1)S(1)}, bf16[352,384]{1,0:T(8,128)(2,1)S(1)}, u32[]{:S(2)}, u32[]{:S(2)}) collective-permute-start(bf16[352,384]{1,0:T(8,128)(2,1)S(1)} %get-tuple-element.299), channel_id=1, source_target_pairs={{0,2},{1,3},{2,0},{3,1},{4,6},{5,7},{6,4},{7,5},{8,10},{9,11},{10,... | collective-permute-start | bytes 811016 | tf_op jit(solution)/shard_map/ppermute | solution.py:414
  69.4 1.5 %collective-permute-start.22 = (bf16[64,384]{1,0:T(8,128)(2,1)S(1)}, bf16[64,384]{1,0:T(8,128)(2,1)S(1)}, u32[]{:S(2)}, u32[]{:S(2)}) collective-permute-start(bf16[64,384]{1,0:T(8,128)(2,1)S(1)} %add_convert_fusion.16), channel_id=1, source_target_pairs={{0,6},{1,7},{2,4},{3,5},{4,2},{5,3},{6,0},{7,1},{8,14},{9,15},{10,... | collective-permute-start | bytes 147464 | tf_op jit(solution)/shard_map/ppermute | solution.py:414
  70.9 2.4 %collective-permute-done.18 = bf16[352,384]{1,0:T(8,128)(2,1)S(1)} collective-permute-done((bf16[352,384]{1,0:T(8,128)(2,1)S(1)}, bf16[352,384]{1,0:T(8,128)(2,1)S(1)}, u32[]{:S(2)}, u32[]{:S(2)}) %collective-permute-start.18) | collective-permute-done | bytes 270368 | tf_op jit(solution)/shard_map/ppermute | solution.py:414
  73.3 1.9 %collective-permute-done.19 = bf16[352,384]{1,0:T(8,128)(2,1)S(1)} collective-permute-done((bf16[352,384]{1,0:T(8,128)(2,1)S(1)}, bf16[352,384]{1,0:T(8,128)(2,1)S(1)}, u32[]{:S(2)}, u32[]{:S(2)}) %collective-permute-start.19) | collective-permute-done | bytes 270368 | tf_op jit(solution)/shard_map/ppermute | solution.py:414
  75.3 1.0 %collective-permute-done.22 = bf16[64,384]{1,0:T(8,128)(2,1)S(1)} collective-permute-done((bf16[64,384]{1,0:T(8,128)(2,1)S(1)}, bf16[64,384]{1,0:T(8,128)(2,1)S(1)}, u32[]{:S(2)}, u32[]{:S(2)}) %collective-permute-start.22) | collective-permute-done | bytes 49184 | tf_op jit(solution)/shard_map/ppermute | solution.py:414
  76.4 3.9 %collective-permute-start.24 = (bf16[96,384]{1,0:T(8,128)(2,1)S(1)}, bf16[96,384]{1,0:T(8,128)(2,1)S(1)}, u32[]{:S(2)}, u32[]{:S(2)}) collective-permute-start(bf16[96,384]{1,0:T(8,128)(2,1)S(1)} %bitcast.146), channel_id=1, source_target_pairs={{0,16},{1,17},{2,18},{3,19},{4,20},{5,21},{6,22},{7,23},{8,24},{9,... | collective-permute-start | bytes 221192 | tf_op jit(solution)/shard_map/ppermute | solution.py:414
  81.3 2.5 %last.1 = bf16[256,384]{1,0:T(8,128)(2,1)} custom-call(bf16[22,32,384]{2,1,0:T(8,128)(2,1)S(1)} %fusion.18.dzpad, bf16[256,384]{1,0:T(8,128)(2,1)S(1)} %get-tuple-element.223.gmid, f32[49,2,384]{2,1,0:T(2,128)S(1)} %bitcast.104), custom_call_target="tpu_custom_call" | custom-call | tf_op jit(solution)/shard_map/last/pallas_call | solution.py:362
  83.8 2.6 %collective-permute-done.23 = bf16[256,384]{1,0:T(8,128)(2,1)S(1)} collective-permute-done((bf16[256,384]{1,0:T(8,128)(2,1)S(1)}, bf16[256,384]{1,0:T(8,128)(2,1)S(1)}, u32[]{:S(2)}, u32[]{:S(2)}) %collective-permute-start.23) | collective-permute-done | bytes 196640 | tf_op jit(solution)/shard_map/ppermute | solution.py:414
  87.4 6.4 %collective-permute-done.25 = bf16[160,384]{1,0:T(8,128)(2,1)S(1)} collective-permute-done((bf16[160,384]{1,0:T(8,128)(2,1)S(1)}, bf16[160,384]{1,0:T(8,128)(2,1)S(1)}, u32[]{:S(2)}, u32[]{:S(2)}) %collective-permute-start.25) | collective-permute-done | bytes 122912 | tf_op jit(solution)/shard_map/ppermute | solution.py:414
  93.9 0.7 weights.1
  95.1 1.3 %small.1 = (f32[49,2,384]{2,1,0:T(2,128)}, f32[2,384]{1,0:T(2,128)}, f32[2,384]{1,0:T(2,128)}, f32[2,1536]{1,0:T(2,128)}) custom-call(s32[5]{0:T(128)S(1)} %stack.25.place, bf16[64,384]{1,0:T(8,128)(2,1)S(1)} %add_convert_fusion.13.mine, bf16[64,384]{1,0:T(8,128)(2,1)S(1)} %collective-permute-done.26.got), custom_call_target="tpu_custom_call" | custom-call | tf_op jit(solution)/shard_map/small/pallas_call | solution.py:362
  (113 shorter events, 9.2 us)
Async XLA Ops:
  1.7 6.4 %collective-permute-start = (bf16[6,16,384]{2,1,0:T(8,128)(2,1)S(1)}, bf16[6,16,384]{2,1,0:T(8,128)(2,1)S(1)}, u32[]{:S(2)}, u32[]{:S(2)}) collective-permute-start(bf16[6,16,384]{2,1,0:T(8,128)(2,1)S(1)} %get-tuple-element.280), channel_id=1, source_target_pairs={{0,4},{4,0},{8,12},{12,8},{16,20},{20,16},{24,28},{28,24},{1,5},{5... | collective-permute-start | bytes 221192 | tf_op jit(solution)/shard_map/ppermute | solution.py:384
  4.7 10.5 %copy-start.6 = (bf16[16,16,384]{2,1,0:T(8,128)(2,1)S(1)}, bf16[16,16,384]{2,1,0:T(8,128)(2,1)}, u32[]{:S(2)}) copy-start(bf16[16,16,384]{2,1,0:T(8,128)(2,1)} %param.8) | copy-start | bytes 589828
  4.7 3.4 %collective-permute-start.1 = (bf16[6,16,384]{2,1,0:T(8,128)(2,1)S(1)}, bf16[6,16,384]{2,1,0:T(8,128)(2,1)S(1)}, u32[]{:S(2)}, u32[]{:S(2)}) collective-permute-start(bf16[6,16,384]{2,1,0:T(8,128)(2,1)S(1)} %get-tuple-element.279), channel_id=1, source_target_pairs={{0,1},{1,0},{2,3},{3,2},{4,8},{5,9},{6,10},{7,11},{8,4},{9,5},{10,... | collective-permute-start | bytes 221192 | tf_op jit(solution)/shard_map/ppermute | solution.py:400
  9.2 6.4 %copy-start.1 = (f32[2,7,7,384]{3,0,2,1:T(2,128)S(1)}, f32[2,7,7,384]{3,0,2,1:T(2,128)}, u32[]{:S(2)}) copy-start(f32[2,7,7,384]{3,0,2,1:T(2,128)} %param.10) | copy-start | bytes 451588
  9.2 6.4 %copy-start.3 = (f32[2,1536]{1,0:T(2,128)S(1)}, f32[2,1536]{1,0:T(2,128)}, u32[]{:S(2)}) copy-start(f32[2,1536]{1,0:T(2,128)} %b_in.5) | copy-start | bytes 36868
  9.2 6.4 %copy-start.4 = (f32[2,384]{1,0:T(2,128)S(1)}, f32[2,384]{1,0:T(2,128)}, u32[]{:S(2)}) copy-start(f32[2,384]{1,0:T(2,128)} %gains.7) | copy-start | bytes 9220
  9.2 2.6 %collective-permute-start.2 = (bf16[28,6,384]{2,1,0:T(8,128)(2,1)S(1)}, bf16[28,6,384]{2,1,0:T(8,128)(2,1)S(1)}, u32[]{:S(2)}, u32[]{:S(2)}) collective-permute-start(bf16[28,6,384]{2,1,0:T(8,128)(2,1)S(1)} %get-tuple-element.258), channel_id=1, source_target_pairs={{0,1},{1,0},{2,3},{3,2},{4,5},{5,4},{6,7},{7,6},{8,9},{9,8},{10,11... | collective-permute-start | bytes 387080 | tf_op jit(solution)/shard_map/ppermute | solution.py:384
  9.3 5.9 %collective-permute-start.3 = (bf16[28,6,384]{2,1,0:T(8,128)(2,1)S(1)}, bf16[28,6,384]{2,1,0:T(8,128)(2,1)S(1)}, u32[]{:S(2)}, u32[]{:S(2)}) collective-permute-start(bf16[28,6,384]{2,1,0:T(8,128)(2,1)S(1)} %get-tuple-element.257), channel_id=1, source_target_pairs={{0,4},{1,2},{2,1},{3,7},{4,0},{5,6},{6,5},{7,3},{8,12},{9,10},{10,... | collective-permute-start | bytes 387080 | tf_op jit(solution)/shard_map/ppermute | solution.py:400
  15.6 8.8 %copy-start.2 = (bf16[16,16,384]{2,1,0:T(8,128)(2,1)S(1)}, bf16[16,16,384]{2,1,0:T(8,128)(2,1)}, u32[]{:S(2)}) copy-start(bf16[16,16,384]{2,1,0:T(8,128)(2,1)} %param.9) | copy-start | bytes 589828
  29.3 4.0 %collective-permute-start.4 = (bf16[3,16,384]{2,1,0:T(8,128)(2,1)S(1)}, bf16[3,16,384]{2,1,0:T(8,128)(2,1)S(1)}, u32[]{:S(2)}, u32[]{:S(2)}) collective-permute-start(bf16[3,16,384]{2,1,0:T(8,128)(2,1)S(1)} %bitcast.150), channel_id=1, source_target_pairs={{0,4},{4,0},{8,12},{12,8},{16,20},{20,16},{24,28},{28,24},{1,5},{5... | collective-permute-start | bytes 110600 | tf_op jit(solution)/shard_map/ppermute | solution.py:384
  31.3 1.9 %collective-permute-start.5 = (bf16[3,16,384]{2,1,0:T(8,128)(2,1)S(1)}, bf16[3,16,384]{2,1,0:T(8,128)(2,1)S(1)}, u32[]{:S(2)}, u32[]{:S(2)}) collective-permute-start(bf16[3,16,384]{2,1,0:T(8,128)(2,1)S(1)} %bitcast.149), channel_id=1, source_target_pairs={{0,1},{1,0},{2,3},{3,2},{4,8},{5,9},{6,10},{7,11},{8,4},{9,5},{10,... | collective-permute-start | bytes 110600 | tf_op jit(solution)/shard_map/ppermute | solution.py:400
  33.3 6.3 %collective-permute-start.8 = (bf16[2,16,48,384]{3,2,1,0:T(8,128)(2,1)S(1)}, bf16[2,16,48,384]{3,2,1,0:T(8,128)(2,1)S(1)}, u32[]{:S(2)}, u32[]{:S(2)}) collective-permute-start(bf16[2,16,48,384]{3,2,1,0:T(8,128)(2,1)S(1)} %bitcast.116), channel_id=1, source_target_pairs={{0,1},{1,0},{2,3},{3,2},{4,5},{5,4},{6,7},{7,6},{8,9},{9,8},{10,11... | collective-permute-start | bytes 3538952 | tf_op jit(solution)/shard_map/ppermute | solution.py:414
  33.7 5.9 %collective-permute-start.6 = (bf16[22,3,384]{2,1,0:T(4,128)(2,1)S(1)}, bf16[22,3,384]{2,1,0:T(4,128)(2,1)S(1)}, u32[]{:S(2)}, u32[]{:S(2)}) collective-permute-start(bf16[22,3,384]{2,1,0:T(4,128)(2,1)S(1)} %get-tuple-element.274), channel_id=1, source_target_pairs={{0,1},{1,0},{2,3},{3,2},{4,5},{5,4},{6,7},{7,6},{8,9},{9,8},{10,11... | collective-permute-start | bytes 152072 | tf_op jit(solution)/shard_map/ppermute | solution.py:384
  34.0 5.5 %collective-permute-start.7 = (bf16[22,3,384]{2,1,0:T(4,128)(2,1)S(1)}, bf16[22,3,384]{2,1,0:T(4,128)(2,1)S(1)}, u32[]{:S(2)}, u32[]{:S(2)}) collective-permute-start(bf16[22,3,384]{2,1,0:T(4,128)(2,1)S(1)} %get-tuple-element.273), channel_id=1, source_target_pairs={{0,4},{1,2},{2,1},{3,7},{4,0},{5,6},{6,5},{7,3},{8,12},{9,10},{10,... | collective-permute-start | bytes 152072 | tf_op jit(solution)/shard_map/ppermute | solution.py:400
  40.1 8.9 %collective-permute-start.10 = (bf16[1,4,2,48,384]{4,3,2,1,0:T(8,128)(2,1)S(1)}, bf16[1,4,2,48,384]{4,3,2,1,0:T(8,128)(2,1)S(1)}, u32[]{:S(2)}, u32[]{:S(2)}) collective-permute-start(bf16[1,4,2,48,384]{4,3,2,1,0:T(8,128)(2,1)S(1)} %get-tuple-element.251), channel_id=1, source_target_pairs={{0,4},{1,5},{2,6},{3,7},{4,0},{5,1},{6,2},{7,3},{8,12},{9,13},{10,... | collective-permute-start | bytes 884744 | tf_op jit(solution)/shard_map/ppermute | solution.py:414
  42.1 8.5 %collective-permute-start.9 = (bf16[1,8,1,48,384]{4,3,1,2,0:T(8,128)(2,1)S(1)}, bf16[1,8,1,48,384]{4,3,1,2,0:T(8,128)(2,1)S(1)}, u32[]{:S(2)}, u32[]{:S(2)}) collective-permute-start(bf16[1,8,1,48,384]{4,3,1,2,0:T(8,128)(2,1)S(1)} %get-tuple-element.253), channel_id=1, source_target_pairs={{0,2},{1,3},{2,0},{3,1},{4,6},{5,7},{6,4},{7,5},{8,10},{9,11},{10,... | collective-permute-start | bytes 884744 | tf_op jit(solution)/shard_map/ppermute | solution.py:414
  50.6 3.2 %collective-permute-start.11 = (bf16[2,16,48,384]{3,2,1,0:T(8,128)(2,1)S(1)}, bf16[2,16,48,384]{3,2,1,0:T(8,128)(2,1)S(1)}, u32[]{:S(2)}, u32[]{:S(2)}) collective-permute-start(bf16[2,16,48,384]{3,2,1,0:T(8,128)(2,1)S(1)} %bitcast.117), channel_id=1, source_target_pairs={{0,1},{1,0},{2,3},{3,2},{4,5},{5,4},{6,7},{7,6},{8,9},{9,8},{10,11... | collective-permute-start | bytes 3538952 | tf_op jit(solution)/shard_map/ppermute | solution.py:414
  50.9 10.6 %collective-permute-start.14 = (bf16[384,384]{1,0:T(8,128)(2,1)S(1)}, bf16[384,384]{1,0:T(8,128)(2,1)S(1)}, u32[]{:S(2)}, u32[]{:S(2)}) collective-permute-start(bf16[384,384]{1,0:T(8,128)(2,1)S(1)} %pad_maximum_fusion.3), channel_id=1, source_target_pairs={{0,8},{1,9},{2,10},{3,11},{4,12},{5,13},{6,14},{7,15},{8,0},{9,1},... | collective-permute-start | bytes 884744 | tf_op jit(solution)/shard_map/ppermute | solution.py:414
  54.3 10.0 %collective-permute-start.13 = (bf16[1,4,2,48,384]{4,3,1,2,0:T(8,128)(2,1)S(1)}, bf16[1,4,2,48,384]{4,3,1,2,0:T(8,128)(2,1)S(1)}, u32[]{:S(2)}, u32[]{:S(2)}) collective-permute-start(bf16[1,4,2,48,384]{4,3,1,2,0:T(8,128)(2,1)S(1)} %bitcast.143), channel_id=1, source_target_pairs={{0,4},{1,5},{2,6},{3,7},{4,0},{5,1},{6,2},{7,3},{8,12},{9,13},{10,... | collective-permute-start | bytes 884744 | tf_op jit(solution)/shard_map/ppermute | solution.py:414
  55.1 9.2 %collective-permute-start.12 = (bf16[1,8,1,48,384]{4,3,1,2,0:T(8,128)(2,1)S(1)}, bf16[1,8,1,48,384]{4,3,1,2,0:T(8,128)(2,1)S(1)}, u32[]{:S(2)}, u32[]{:S(2)}) collective-permute-start(bf16[1,8,1,48,384]{4,3,1,2,0:T(8,128)(2,1)S(1)} %get-tuple-element.249), channel_id=1, source_target_pairs={{0,2},{1,3},{2,0},{3,1},{4,6},{5,7},{6,4},{7,5},{8,10},{9,11},{10,... | collective-permute-start | bytes 884744 | tf_op jit(solution)/shard_map/ppermute | solution.py:414
  59.4 5.0 %collective-permute-start.17 = (bf16[64,384]{1,0:T(8,128)(2,1)S(1)}, bf16[64,384]{1,0:T(8,128)(2,1)S(1)}, u32[]{:S(2)}, u32[]{:S(2)}) collective-permute-start(bf16[64,384]{1,0:T(8,128)(2,1)S(1)} %get-tuple-element.192), channel_id=1, source_target_pairs={{0,1},{1,0},{2,3},{3,2},{4,5},{5,4},{6,7},{7,6},{8,9},{9,8},{10,11... | collective-permute-start | bytes 147464 | tf_op jit(solution)/shard_map/ppermute | solution.py:414
  59.5 4.9 %collective-permute-start.15 = (bf16[3,16,384]{2,1,0:T(8,128)(2,1)S(1)}, bf16[3,16,384]{2,1,0:T(8,128)(2,1)S(1)}, u32[]{:S(2)}, u32[]{:S(2)}) collective-permute-start(bf16[3,16,384]{2,1,0:T(8,128)(2,1)S(1)} %bitcast.148), channel_id=1, source_target_pairs={{0,4},{4,0},{8,12},{12,8},{16,20},{20,16},{24,28},{28,24},{1,5},{5... | collective-permute-start | bytes 110600 | tf_op jit(solution)/shard_map/ppermute | solution.py:384
  61.4 2.9 %collective-permute-start.16 = (bf16[3,16,384]{2,1,0:T(8,128)(2,1)S(1)}, bf16[3,16,384]{2,1,0:T(8,128)(2,1)S(1)}, u32[]{:S(2)}, u32[]{:S(2)}) collective-permute-start(bf16[3,16,384]{2,1,0:T(8,128)(2,1)S(1)} %bitcast.147), channel_id=1, source_target_pairs={{0,1},{1,0},{2,3},{3,2},{4,8},{5,9},{6,10},{7,11},{8,4},{9,5},{10,... | collective-permute-start | bytes 110600 | tf_op jit(solution)/shard_map/ppermute | solution.py:400
  64.9 8.4 %collective-permute-start.18 = (bf16[352,384]{1,0:T(8,128)(2,1)S(1)}, bf16[352,384]{1,0:T(8,128)(2,1)S(1)}, u32[]{:S(2)}, u32[]{:S(2)}) collective-permute-start(bf16[352,384]{1,0:T(8,128)(2,1)S(1)} %get-tuple-element.300), channel_id=1, source_target_pairs={{0,4},{1,5},{2,6},{3,7},{4,0},{5,1},{6,2},{7,3},{8,12},{9,13},{10,... | collective-permute-start | bytes 811016 | tf_op jit(solution)/shard_map/ppermute | solution.py:414
  67.6 7.7 %collective-permute-start.19 = (bf16[352,384]{1,0:T(8,128)(2,1)S(1)}, bf16[352,384]{1,0:T(8,128)(2,1)S(1)}, u32[]{:S(2)}, u32[]{:S(2)}) collective-permute-start(bf16[352,384]{1,0:T(8,128)(2,1)S(1)} %get-tuple-element.299), channel_id=1, source_target_pairs={{0,2},{1,3},{2,0},{3,1},{4,6},{5,7},{6,4},{7,5},{8,10},{9,11},{10,... | collective-permute-start | bytes 811016 | tf_op jit(solution)/shard_map/ppermute | solution.py:414
  69.1 7.1 %collective-permute-start.20 = (bf16[22,3,384]{2,1,0:T(4,128)(2,1)S(1)}, bf16[22,3,384]{2,1,0:T(4,128)(2,1)S(1)}, u32[]{:S(2)}, u32[]{:S(2)}) collective-permute-start(bf16[22,3,384]{2,1,0:T(4,128)(2,1)S(1)} %get-tuple-element.272), channel_id=1, source_target_pairs={{0,1},{1,0},{2,3},{3,2},{4,5},{5,4},{6,7},{7,6},{8,9},{9,8},{10,11... | collective-permute-start | bytes 152072 | tf_op jit(solution)/shard_map/ppermute | solution.py:384
  69.2 7.1 %collective-permute-start.21 = (bf16[22,3,384]{2,1,0:T(4,128)(2,1)S(1)}, bf16[22,3,384]{2,1,0:T(4,128)(2,1)S(1)}, u32[]{:S(2)}, u32[]{:S(2)}) collective-permute-start(bf16[22,3,384]{2,1,0:T(4,128)(2,1)S(1)} %get-tuple-element.271), channel_id=1, source_target_pairs={{0,4},{1,2},{2,1},{3,7},{4,0},{5,6},{6,5},{7,3},{8,12},{9,10},{10,... | collective-permute-start | bytes 152072 | tf_op jit(solution)/shard_map/ppermute | solution.py:400
  69.4 6.9 %collective-permute-start.22 = (bf16[64,384]{1,0:T(8,128)(2,1)S(1)}, bf16[64,384]{1,0:T(8,128)(2,1)S(1)}, u32[]{:S(2)}, u32[]{:S(2)}) collective-permute-start(bf16[64,384]{1,0:T(8,128)(2,1)S(1)} %add_convert_fusion.16), channel_id=1, source_target_pairs={{0,6},{1,7},{2,4},{3,5},{4,2},{5,3},{6,0},{7,1},{8,14},{9,15},{10,... | collective-permute-start | bytes 147464 | tf_op jit(solution)/shard_map/ppermute | solution.py:414
  76.4 10.1 %collective-permute-start.24 = (bf16[96,384]{1,0:T(8,128)(2,1)S(1)}, bf16[96,384]{1,0:T(8,128)(2,1)S(1)}, u32[]{:S(2)}, u32[]{:S(2)}) collective-permute-start(bf16[96,384]{1,0:T(8,128)(2,1)S(1)} %bitcast.146), channel_id=1, source_target_pairs={{0,16},{1,17},{2,18},{3,19},{4,20},{5,21},{6,22},{7,23},{8,24},{9,... | collective-permute-start | bytes 221192 | tf_op jit(solution)/shard_map/ppermute | solution.py:414
  80.5 5.9 %collective-permute-start.23 = (bf16[256,384]{1,0:T(8,128)(2,1)S(1)}, bf16[256,384]{1,0:T(8,128)(2,1)S(1)}, u32[]{:S(2)}, u32[]{:S(2)}) collective-permute-start(bf16[256,384]{1,0:T(8,128)(2,1)S(1)} %pad_maximum_fusion.6), channel_id=1, source_target_pairs={{0,8},{1,9},{2,10},{3,11},{4,12},{5,13},{6,14},{7,15},{8,0},{9,1},... | collective-permute-start | bytes 589832 | tf_op jit(solution)/shard_map/ppermute | solution.py:414
  86.6 7.2 %collective-permute-start.25 = (bf16[160,384]{1,0:T(8,128)(2,1)S(1)}, bf16[160,384]{1,0:T(8,128)(2,1)S(1)}, u32[]{:S(2)}, u32[]{:S(2)}) collective-permute-start(bf16[160,384]{1,0:T(8,128)(2,1)S(1)} %pad_maximum_fusion.7), channel_id=1, source_target_pairs={{0,16},{1,17},{2,18},{3,19},{4,20},{5,21},{6,22},{7,23},{8,24},{9,... | collective-permute-start | bytes 368648 | tf_op jit(solution)/shard_map/ppermute | solution.py:414
  93.8 1.3 %collective-permute-start.26 = (bf16[64,384]{1,0:T(8,128)(2,1)S(1)}, bf16[64,384]{1,0:T(8,128)(2,1)S(1)}, u32[]{:S(2)}, u32[]{:S(2)}) collective-permute-start(bf16[64,384]{1,0:T(8,128)(2,1)S(1)} %add_convert_fusion.13.mine), channel_id=1, source_target_pairs={{0,1},{1,0},{2,3},{3,2},{4,5},{5,4},{6,7},{7,6},{8,9},{9,8},{10,11... | collective-permute-start | bytes 147464 | tf_op jit(solution)/shard_map/ppermute | solution.py:414
  (2 other events, 12.2 us)

commit v12 on v11

--- a/solution.py
+++ b/solution.py
@@ -13,14 +13,12 @@
 HALF_LOG2E = 0.7213475204444817
 ERFC_SLOPE = 0.4 * 0.7071067811865476
 ERFC_TERMS = (
-    0.22479419400284972,
-    0.2383621945582281,
-    0.12991301634379934,
-    0.4353236101490443,
-    -0.41611664430523265,
-    0.7235898182708315,
-    -0.41436965913692125,
-    0.07850346878444278,
+    0.23195388609975262,
+    0.16163296978938874,
+    0.4687286953098433,
+    -0.3714470456115026,
+    0.7094654203066808,
+    -0.2003339536843631,
 )
 LANES = 128
 HALO = 3
@@ -30,23 +28,24 @@
 
 
 def normal_parts(x):
+    size = jnp.abs(x)
     bell = jnp.exp2(x * x * (-HALF_LOG2E))
-    t = 1.0 / (1.0 + ERFC_SLOPE * jnp.abs(x))
-    series = 0.5 * ERFC_TERMS[7]
-    for term in ERFC_TERMS[6::-1]:
+    t = pl.reciprocal(1.0 + ERFC_SLOPE * size, approx=True)
+    series = 0.5 * ERFC_TERMS[-1]
+    for term in ERFC_TERMS[-2::-1]:
         series = series * t + 0.5 * term
-    tail = series * t * bell
-    return jnp.where(x >= 0, 1.0 - tail, tail), bell
+    return size, series * t * bell, bell
 
 
 def gelu_only(x):
-    cdf, _ = normal_parts(x)
-    return x * cdf
+    size, tail, _ = normal_parts(x)
+    return jnp.maximum(x, 0.0) - size * tail
 
 
 def gelu_parts(x):
-    cdf, bell = normal_parts(x)
-    return x * cdf, cdf + x * bell * INV_ROOT_TAU
+    size, tail, bell = normal_parts(x)
+    cdf = jnp.where(x >= 0, 1.0 - tail, tail)
+    return jnp.maximum(x, 0.0) - size * tail, cdf + x * bell * INV_ROOT_TAU
 
 
 def strip_rows(rows, cols):

time: 96.6 us -> 96 us (level)
  no operation moved by 1% of the time
where the time goes in v12:
time: 96 us; the launch traced here: 95.8 us
  starting transfers between devices  30.3 us (32%)
  Pallas kernels  29.7 us (31%)
  waiting for transfers between devices  28.8 us (30%)
  other arithmetic  4.8 us (5%)
  between operations  1.27 us (1%)
  local copies, waits for them, and re-layouts  1.07 us (1%)
    pallas_call x9, Pallas kernels, run(): pl.pallas_call(kernel, out_shape=outs, in_specs=[vmem if s is None else p...  29.7 us
    ppermute x15, waiting for transfers between devices, flip_bit(): return lax.ppermute(value, both, [(i, i ^ flip) for i in range(total)])  18.8 us
    ppermute x15, starting transfers between devices, flip_bit(): return lax.ppermute(value, both, [(i, i ^ flip) for i in range(total)])  17.5 us
    ppermute x6, starting transfers between devices, to_twin(): lax.ppermute(edge, axis, [(i, i ^ 1) for i in range(count) if i ^ 1 < cou...  7.01 us
    ppermute x6, waiting for transfers between devices, to_twin(): lax.ppermute(edge, axis, [(i, i ^ 1) for i in range(count) if i ^ 1 < cou...  6.54 us
    ppermute x6, starting transfers between devices, to_other(): return lax.ppermute(edge, ('rows', 'cols'), pairs)  5.81 us
    ppermute x6, waiting for transfers between devices, to_other(): return lax.ppermute(edge, ('rows', 'cols'), pairs)  3.4 us
  transfers between devices with their start and end apart: 27, of which 13 were waited for; matrix products, arithmetic and copies ran while one was open for 2% of the time, Pallas kernels for 16%

profile of v12, /device:TPU:0, one launch (start us, length us, event | category | flops | bytes accessed | tf_op | source)
XLA Modules:
  0.0 95.8 jit_solution(16553099371251505461)
XLA Ops:
  0.7 0.9 broadcast_select_fusion.8
  1.7 3.0 %collective-permute-start = (bf16[6,16,384]{2,1,0:T(8,128)(2,1)S(1)}, bf16[6,16,384]{2,1,0:T(8,128)(2,1)S(1)}, u32[]{:S(2)}, u32[]{:S(2)}) collective-permute-start(bf16[6,16,384]{2,1,0:T(8,128)(2,1)S(1)} %get-tuple-element.280), channel_id=1, source_target_pairs={{0,4},{4,0},{8,12},{12,8},{16,20},{20,16},{24,28},{28,24},{1,5},{5... | collective-permute-start | bytes 221192 | tf_op jit(solution)/shard_map/ppermute | solution.py:383
  4.7 3.4 %collective-permute-done = bf16[6,16,384]{2,1,0:T(8,128)(2,1)S(1)} collective-permute-done((bf16[6,16,384]{2,1,0:T(8,128)(2,1)S(1)}, bf16[6,16,384]{2,1,0:T(8,128)(2,1)S(1)}, u32[]{:S(2)}, u32[]{:S(2)}) %collective-permute-start) | collective-permute-done | bytes 73760 | tf_op jit(solution)/shard_map/ppermute | solution.py:383
  8.1 1.0 %pad_maximum_fusion.2 = bf16[28,16,384]{2,1,0:T(8,128)(2,1)S(1)} fusion(bf16[6,16,384]{2,1,0:T(8,128)(2,1)S(1)} %get-tuple-element.290, bf16[16,16,384]{2,1,0:T(8,128)(2,1)} %param.8, bf16[6,16,384]{2,1,0:T(8,128)(2,1)S(1)} %get-tuple-element.289), kind=kLoop, calls=%fused_computation.29 | loop fusion | flops 344064 | bytes 688128 | tf_op jit(solution)/shard_map/concatenate | solution.py:406
  9.3 2.5 %collective-permute-start.3 = (bf16[28,6,384]{2,1,0:T(8,128)(2,1)S(1)}, bf16[28,6,384]{2,1,0:T(8,128)(2,1)S(1)}, u32[]{:S(2)}, u32[]{:S(2)}) collective-permute-start(bf16[28,6,384]{2,1,0:T(8,128)(2,1)S(1)} %get-tuple-element.257), channel_id=1, source_target_pairs={{0,4},{1,2},{2,1},{3,7},{4,0},{5,6},{6,5},{7,3},{8,12},{9,10},{10,... | collective-permute-start | bytes 387080 | tf_op jit(solution)/shard_map/ppermute | solution.py:399
  11.8 3.4 %collective-permute-done.3 = bf16[28,6,384]{2,1,0:T(8,128)(2,1)S(1)} collective-permute-done((bf16[28,6,384]{2,1,0:T(8,128)(2,1)S(1)}, bf16[28,6,384]{2,1,0:T(8,128)(2,1)S(1)}, u32[]{:S(2)}, u32[]{:S(2)}) %collective-permute-start.3) | collective-permute-done | bytes 129056 | tf_op jit(solution)/shard_map/ppermute | solution.py:399
  15.7 8.3 %forward.1 = (f32[3,22,24,128]{3,2,1,0:T(8,128)S(1)}, f32[3,16,16,128]{3,2,1,0:T(8,128)S(1)}) custom-call(s32[5]{0:T(128)S(1)} %stack.25.place, bf16[28,32,384]{2,1,0:T(8,128)(2,1)S(1)} %fusion.12.xpad, f32[49,2,384]{2,1,0:T(2,128)S(1)} %bitcast.101, f32[2,384]{1,0:T(2,128)S(1)} %copy-done.4, f32[2,384]{1,0:T(2,128)S(1)} %copy-done.5, ...), custom_call_target="tpu_custom_call" | custom-call | tf_op jit(solution)/shard_map/forward/pallas_call | solution.py:361
  24.0 4.7 %top.1 = (bf16[256,384]{1,0:T(8,128)(2,1)S(1)}, bf16[256,384]{1,0:T(8,128)(2,1)S(1)}, bf16[256,1536]{1,0:T(8,128)(2,1)S(1)}, bf16[256,1536]{1,0:T(8,128)(2,1)S(1...) custom-call(f32[3,22,24,128]{3,2,1,0:T(8,128)S(1)} %get-tuple-element.131.mids, ...), custom_call_target="tpu_custom_call" | custom-call | tf_op jit(solution)/shard_map/top/pallas_call | solution.py:361
  28.8 2.1 %collective-permute-start.4 = (bf16[3,16,384]{2,1,0:T(8,128)(2,1)S(1)}, bf16[3,16,384]{2,1,0:T(8,128)(2,1)S(1)}, u32[]{:S(2)}, u32[]{:S(2)}) collective-permute-start(bf16[3,16,384]{2,1,0:T(8,128)(2,1)S(1)} %bitcast.150), channel_id=1, source_target_pairs={{0,4},{4,0},{8,12},{12,8},{16,20},{20,16},{24,28},{28,24},{1,5},{5... | collective-permute-start | bytes 110600 | tf_op jit(solution)/shard_map/ppermute | solution.py:383
  30.9 1.6 %weights_top.1 = (bf16[2,768,384]{2,1,0:T(8,128)(2,1)S(1)}, bf16[2,768,384]{2,1,0:T(8,128)(2,1)S(1)}) custom-call(s32[5]{0:T(128)S(1)} %stack.25.place, bf16[256,384]{1,0:T(8,128)(2,1)S(1)} %get-tuple-element.133.normed, bf16[256,1536]{1,0:T(8,128)(2,1)S(1)} %get-tuple-element.134.act, bf16[256,1536]{1,0:T(8,128)(2,1)S(1)} %get-tuple-element.135.gpre, ...), custom_call_target="tpu_custom_call" | custom-call | tf_op jit(solution)/shard_map/weights_top/pallas_call | solution.py:361
  33.5 3.1 %collective-permute-start.7 = (bf16[22,3,384]{2,1,0:T(4,128)(2,1)S(1)}, bf16[22,3,384]{2,1,0:T(4,128)(2,1)S(1)}, u32[]{:S(2)}, u32[]{:S(2)}) collective-permute-start(bf16[22,3,384]{2,1,0:T(4,128)(2,1)S(1)} %get-tuple-element.273), channel_id=1, source_target_pairs={{0,4},{1,2},{2,1},{3,7},{4,0},{5,6},{6,5},{7,3},{8,12},{9,10},{10,... | collective-permute-start | bytes 152072 | tf_op jit(solution)/shard_map/ppermute | solution.py:399
  36.7 2.3 %again.1 = (f32[256,384]{1,0:T(8,128)S(1)}, f32[256,128]{1,0:T(8,128)S(1)}, bf16[256,384]{1,0:T(8,128)(2,1)S(1)}, bf16[256,1536]{1,0:T(8,128)(2,1)S(1)}, f32[256,1536]{1,0:T(8,128)S(1)}) custom-call(f32[3,16,16,128]{3,2,1,0:T(8,128)S(1)} %get-tuple-element.144.z0, f32[2,384]{1,0:T(2,128)S(1)} %copy-done.4, f32[2,384]{1,0:T(2,128)S(1)} %copy-done.5, ...), custom_call_target="tpu_custom_call" | custom-call | tf_op jit(solution)/shard_map/again/pallas_call | solution.py:361
  39.5 2.0 %collective-permute-start.10 = (bf16[1,4,2,48,384]{4,3,2,1,0:T(8,128)(2,1)S(1)}, bf16[1,4,2,48,384]{4,3,2,1,0:T(8,128)(2,1)S(1)}, u32[]{:S(2)}, u32[]{:S(2)}) collective-permute-start(bf16[1,4,2,48,384]{4,3,2,1,0:T(8,128)(2,1)S(1)} %get-tuple-element.251), channel_id=1, source_target_pairs={{0,4},{1,5},{2,6},{3,7},{4,0},{5,1},{6,2},{7,3},{8,12},{9,13},{10,... | collective-permute-start | bytes 884744 | tf_op jit(solution)/shard_map/ppermute | solution.py:413
  42.3 4.5 %low.1 = (bf16[256,384]{1,0:T(8,128)(2,1)S(1)}, bf16[256,384]{1,0:T(8,128)(2,1)S(1)}, f32[1,1536]{1,0:T(1,128)S(1)}, f32[1,384]{1,0:T(1,128)S(1)}, f32[1,384]{1,...) custom-call(s32[5]{0:T(128)S(1)} %stack.25.place, ...), custom_call_target="tpu_custom_call" | custom-call | tf_op jit(solution)/shard_map/low/pallas_call | solution.py:361
  46.8 1.7 %collective-permute-done.10 = bf16[1,4,2,48,384]{4,3,2,1,0:T(8,128)(2,1)S(1)} collective-permute-done((bf16[1,4,2,48,384]{4,3,2,1,0:T(8,128)(2,1)S(1)}, bf16[1,4,2,48,384]{4,3,2,1,0:T(8,128)(2,1)S(1)}, u32[]{:S(2)}, u32[]{:S(2)}) %collective-permute-start.10) | collective-permute-done | bytes 294944 | tf_op jit(solution)/shard_map/ppermute | solution.py:413
  48.5 1.6 %collective-permute-done.9 = bf16[1,8,1,48,384]{4,3,1,2,0:T(8,128)(2,1)S(1)} collective-permute-done((bf16[1,8,1,48,384]{4,3,1,2,0:T(8,128)(2,1)S(1)}, bf16[1,8,1,48,384]{4,3,1,2,0:T(8,128)(2,1)S(1)}, u32[]{:S(2)}, u32[]{:S(2)}) %collective-permute-start.9) | collective-permute-done | bytes 294944 | tf_op jit(solution)/shard_map/ppermute | solution.py:413
  50.4 2.9 %collective-permute-start.14 = (bf16[384,384]{1,0:T(8,128)(2,1)S(1)}, bf16[384,384]{1,0:T(8,128)(2,1)S(1)}, u32[]{:S(2)}, u32[]{:S(2)}) collective-permute-start(bf16[384,384]{1,0:T(8,128)(2,1)S(1)} %pad_maximum_fusion.3), channel_id=1, source_target_pairs={{0,8},{1,9},{2,10},{3,11},{4,12},{5,13},{6,14},{7,15},{8,0},{9,1},... | collective-permute-start | bytes 884744 | tf_op jit(solution)/shard_map/ppermute | solution.py:413
  55.1 3.7 %taps.1 = (bf16[64,384]{1,0:T(8,128)(2,1)S(1)}, bf16[64,384]{1,0:T(8,128)(2,1)S(1)}) custom-call(s32[5]{0:T(128)S(1)} %stack.25.place, f32[3,22,24,128]{3,2,1,0:T(8,128)S(1)} %get-tuple-element.131.mids, bf16[28,32,384]{2,1,0:T(8,128)(2,1)S(1)} %fusion.12.xpad, bf16[256,384]{1,0:T(8,128)(2,1)S(1)} %get-tuple-element.184.dz0, ...), custom_call_target="tpu_custom_call" | custom-call | tf_op jit(solution)/shard_map/taps/pallas_call | solution.py:361
  58.9 1.4 %collective-permute-start.15 = (bf16[3,16,384]{2,1,0:T(8,128)(2,1)S(1)}, bf16[3,16,384]{2,1,0:T(8,128)(2,1)S(1)}, u32[]{:S(2)}, u32[]{:S(2)}) collective-permute-start(bf16[3,16,384]{2,1,0:T(8,128)(2,1)S(1)} %bitcast.148), channel_id=1, source_target_pairs={{0,4},{4,0},{8,12},{12,8},{16,20},{20,16},{24,28},{28,24},{1,5},{5... | collective-permute-start | bytes 110600 | tf_op jit(solution)/shard_map/ppermute | solution.py:383
  61.0 2.8 %collective-permute-done.15 = bf16[3,16,384]{2,1,0:T(8,128)(2,1)S(1)} collective-permute-done((bf16[3,16,384]{2,1,0:T(8,128)(2,1)S(1)}, bf16[3,16,384]{2,1,0:T(8,128)(2,1)S(1)}, u32[]{:S(2)}, u32[]{:S(2)}) %collective-permute-start.15) | collective-permute-done | bytes 36896 | tf_op jit(solution)/shard_map/ppermute | solution.py:383
  64.4 2.7 %collective-permute-start.18 = (bf16[352,384]{1,0:T(8,128)(2,1)S(1)}, bf16[352,384]{1,0:T(8,128)(2,1)S(1)}, u32[]{:S(2)}, u32[]{:S(2)}) collective-permute-start(bf16[352,384]{1,0:T(8,128)(2,1)S(1)} %get-tuple-element.300), channel_id=1, source_target_pairs={{0,4},{1,5},{2,6},{3,7},{4,0},{5,1},{6,2},{7,3},{8,12},{9,13},{10,... | collective-permute-start | bytes 811016 | tf_op jit(solution)/shard_map/ppermute | solution.py:413
  67.1 1.4 %collective-permute-start.19 = (bf16[352,384]{1,0:T(8,128)(2,1)S(1)}, bf16[352,384]{1,0:T(8,128)(2,1)S(1)}, u32[]{:S(2)}, u32[]{:S(2)}) collective-permute-start(bf16[352,384]{1,0:T(8,128)(2,1)S(1)} %get-tuple-element.299), channel_id=1, source_target_pairs={{0,2},{1,3},{2,0},{3,1},{4,6},{5,7},{6,4},{7,5},{8,10},{9,11},{10,... | collective-permute-start | bytes 811016 | tf_op jit(solution)/shard_map/ppermute | solution.py:413
  68.9 1.5 %collective-permute-start.22 = (bf16[64,384]{1,0:T(8,128)(2,1)S(1)}, bf16[64,384]{1,0:T(8,128)(2,1)S(1)}, u32[]{:S(2)}, u32[]{:S(2)}) collective-permute-start(bf16[64,384]{1,0:T(8,128)(2,1)S(1)} %add_convert_fusion.16), channel_id=1, source_target_pairs={{0,6},{1,7},{2,4},{3,5},{4,2},{5,3},{6,0},{7,1},{8,14},{9,15},{10,... | collective-permute-start | bytes 147464 | tf_op jit(solution)/shard_map/ppermute | solution.py:413
  70.4 2.4 %collective-permute-done.18 = bf16[352,384]{1,0:T(8,128)(2,1)S(1)} collective-permute-done((bf16[352,384]{1,0:T(8,128)(2,1)S(1)}, bf16[352,384]{1,0:T(8,128)(2,1)S(1)}, u32[]{:S(2)}, u32[]{:S(2)}) %collective-permute-start.18) | collective-permute-done | bytes 270368 | tf_op jit(solution)/shard_map/ppermute | solution.py:413
  72.8 1.9 %collective-permute-done.19 = bf16[352,384]{1,0:T(8,128)(2,1)S(1)} collective-permute-done((bf16[352,384]{1,0:T(8,128)(2,1)S(1)}, bf16[352,384]{1,0:T(8,128)(2,1)S(1)}, u32[]{:S(2)}, u32[]{:S(2)}) %collective-permute-start.19) | collective-permute-done | bytes 270368 | tf_op jit(solution)/shard_map/ppermute | solution.py:413
  74.8 1.0 %collective-permute-done.22 = bf16[64,384]{1,0:T(8,128)(2,1)S(1)} collective-permute-done((bf16[64,384]{1,0:T(8,128)(2,1)S(1)}, bf16[64,384]{1,0:T(8,128)(2,1)S(1)}, u32[]{:S(2)}, u32[]{:S(2)}) %collective-permute-start.22) | collective-permute-done | bytes 49184 | tf_op jit(solution)/shard_map/ppermute | solution.py:413
  75.9 3.9 %collective-permute-start.24 = (bf16[96,384]{1,0:T(8,128)(2,1)S(1)}, bf16[96,384]{1,0:T(8,128)(2,1)S(1)}, u32[]{:S(2)}, u32[]{:S(2)}) collective-permute-start(bf16[96,384]{1,0:T(8,128)(2,1)S(1)} %bitcast.146), channel_id=1, source_target_pairs={{0,16},{1,17},{2,18},{3,19},{4,20},{5,21},{6,22},{7,23},{8,24},{9,... | collective-permute-start | bytes 221192 | tf_op jit(solution)/shard_map/ppermute | solution.py:413
  80.7 2.5 %last.1 = bf16[256,384]{1,0:T(8,128)(2,1)} custom-call(bf16[22,32,384]{2,1,0:T(8,128)(2,1)S(1)} %fusion.18.dzpad, bf16[256,384]{1,0:T(8,128)(2,1)S(1)} %get-tuple-element.223.gmid, f32[49,2,384]{2,1,0:T(2,128)S(1)} %bitcast.104), custom_call_target="tpu_custom_call" | custom-call | tf_op jit(solution)/shard_map/last/pallas_call | solution.py:361
  83.2 2.7 %collective-permute-done.23 = bf16[256,384]{1,0:T(8,128)(2,1)S(1)} collective-permute-done((bf16[256,384]{1,0:T(8,128)(2,1)S(1)}, bf16[256,384]{1,0:T(8,128)(2,1)S(1)}, u32[]{:S(2)}, u32[]{:S(2)}) %collective-permute-start.23) | collective-permute-done | bytes 196640 | tf_op jit(solution)/shard_map/ppermute | solution.py:413
  86.1 0.8 collective-permute-start.25
  86.8 6.4 %collective-permute-done.25 = bf16[160,384]{1,0:T(8,128)(2,1)S(1)} collective-permute-done((bf16[160,384]{1,0:T(8,128)(2,1)S(1)}, bf16[160,384]{1,0:T(8,128)(2,1)S(1)}, u32[]{:S(2)}, u32[]{:S(2)}) %collective-permute-start.25) | collective-permute-done | bytes 122912 | tf_op jit(solution)/shard_map/ppermute | solution.py:413
  94.6 1.3 %small.1 = (f32[49,2,384]{2,1,0:T(2,128)}, f32[2,384]{1,0:T(2,128)}, f32[2,384]{1,0:T(2,128)}, f32[2,1536]{1,0:T(2,128)}) custom-call(s32[5]{0:T(128)S(1)} %stack.25.place, bf16[64,384]{1,0:T(8,128)(2,1)S(1)} %add_convert_fusion.13.mine, bf16[64,384]{1,0:T(8,128)(2,1)S(1)} %collective-permute-done.26.got), custom_call_target="tpu_custom_call" | custom-call | tf_op jit(solution)/shard_map/small/pallas_call | solution.py:361
  (113 shorter events, 9.1 us)
Async XLA Ops:
  1.7 6.4 %collective-permute-start = (bf16[6,16,384]{2,1,0:T(8,128)(2,1)S(1)}, bf16[6,16,384]{2,1,0:T(8,128)(2,1)S(1)}, u32[]{:S(2)}, u32[]{:S(2)}) collective-permute-start(bf16[6,16,384]{2,1,0:T(8,128)(2,1)S(1)} %get-tuple-element.280), channel_id=1, source_target_pairs={{0,4},{4,0},{8,12},{12,8},{16,20},{20,16},{24,28},{28,24},{1,5},{5... | collective-permute-start | bytes 221192 | tf_op jit(solution)/shard_map/ppermute | solution.py:383
  4.7 10.5 %copy-start.6 = (bf16[16,16,384]{2,1,0:T(8,128)(2,1)S(1)}, bf16[16,16,384]{2,1,0:T(8,128)(2,1)}, u32[]{:S(2)}) copy-start(bf16[16,16,384]{2,1,0:T(8,128)(2,1)} %param.8) | copy-start | bytes 589828
  4.7 3.4 %collective-permute-start.1 = (bf16[6,16,384]{2,1,0:T(8,128)(2,1)S(1)}, bf16[6,16,384]{2,1,0:T(8,128)(2,1)S(1)}, u32[]{:S(2)}, u32[]{:S(2)}) collective-permute-start(bf16[6,16,384]{2,1,0:T(8,128)(2,1)S(1)} %get-tuple-element.279), channel_id=1, source_target_pairs={{0,1},{1,0},{2,3},{3,2},{4,8},{5,9},{6,10},{7,11},{8,4},{9,5},{10,... | collective-permute-start | bytes 221192 | tf_op jit(solution)/shard_map/ppermute | solution.py:399
  9.2 6.4 %copy-start.1 = (f32[2,7,7,384]{3,0,2,1:T(2,128)S(1)}, f32[2,7,7,384]{3,0,2,1:T(2,128)}, u32[]{:S(2)}) copy-start(f32[2,7,7,384]{3,0,2,1:T(2,128)} %param.10) | copy-start | bytes 451588
  9.2 6.4 %copy-start.3 = (f32[2,1536]{1,0:T(2,128)S(1)}, f32[2,1536]{1,0:T(2,128)}, u32[]{:S(2)}) copy-start(f32[2,1536]{1,0:T(2,128)} %b_in.5) | copy-start | bytes 36868
  9.2 6.4 %copy-start.4 = (f32[2,384]{1,0:T(2,128)S(1)}, f32[2,384]{1,0:T(2,128)}, u32[]{:S(2)}) copy-start(f32[2,384]{1,0:T(2,128)} %gains.7) | copy-start | bytes 9220
  9.2 2.6 %collective-permute-start.2 = (bf16[28,6,384]{2,1,0:T(8,128)(2,1)S(1)}, bf16[28,6,384]{2,1,0:T(8,128)(2,1)S(1)}, u32[]{:S(2)}, u32[]{:S(2)}) collective-permute-start(bf16[28,6,384]{2,1,0:T(8,128)(2,1)S(1)} %get-tuple-element.258), channel_id=1, source_target_pairs={{0,1},{1,0},{2,3},{3,2},{4,5},{5,4},{6,7},{7,6},{8,9},{9,8},{10,11... | collective-permute-start | bytes 387080 | tf_op jit(solution)/shard_map/ppermute | solution.py:383
  9.3 5.9 %collective-permute-start.3 = (bf16[28,6,384]{2,1,0:T(8,128)(2,1)S(1)}, bf16[28,6,384]{2,1,0:T(8,128)(2,1)S(1)}, u32[]{:S(2)}, u32[]{:S(2)}) collective-permute-start(bf16[28,6,384]{2,1,0:T(8,128)(2,1)S(1)} %get-tuple-element.257), channel_id=1, source_target_pairs={{0,4},{1,2},{2,1},{3,7},{4,0},{5,6},{6,5},{7,3},{8,12},{9,10},{10,... | collective-permute-start | bytes 387080 | tf_op jit(solution)/shard_map/ppermute | solution.py:399
  15.6 8.4 %copy-start.2 = (bf16[16,16,384]{2,1,0:T(8,128)(2,1)S(1)}, bf16[16,16,384]{2,1,0:T(8,128)(2,1)}, u32[]{:S(2)}) copy-start(bf16[16,16,384]{2,1,0:T(8,128)(2,1)} %param.9) | copy-start | bytes 589828
  28.8 4.0 %collective-permute-start.4 = (bf16[3,16,384]{2,1,0:T(8,128)(2,1)S(1)}, bf16[3,16,384]{2,1,0:T(8,128)(2,1)S(1)}, u32[]{:S(2)}, u32[]{:S(2)}) collective-permute-start(bf16[3,16,384]{2,1,0:T(8,128)(2,1)S(1)} %bitcast.150), channel_id=1, source_target_pairs={{0,4},{4,0},{8,12},{12,8},{16,20},{20,16},{24,28},{28,24},{1,5},{5... | collective-permute-start | bytes 110600 | tf_op jit(solution)/shard_map/ppermute | solution.py:383
  30.9 1.9 %collective-permute-start.5 = (bf16[3,16,384]{2,1,0:T(8,128)(2,1)S(1)}, bf16[3,16,384]{2,1,0:T(8,128)(2,1)S(1)}, u32[]{:S(2)}, u32[]{:S(2)}) collective-permute-start(bf16[3,16,384]{2,1,0:T(8,128)(2,1)S(1)} %bitcast.149), channel_id=1, source_target_pairs={{0,1},{1,0},{2,3},{3,2},{4,8},{5,9},{6,10},{7,11},{8,4},{9,5},{10,... | collective-permute-start | bytes 110600 | tf_op jit(solution)/shard_map/ppermute | solution.py:399
  32.8 6.2 %collective-permute-start.8 = (bf16[2,16,48,384]{3,2,1,0:T(8,128)(2,1)S(1)}, bf16[2,16,48,384]{3,2,1,0:T(8,128)(2,1)S(1)}, u32[]{:S(2)}, u32[]{:S(2)}) collective-permute-start(bf16[2,16,48,384]{3,2,1,0:T(8,128)(2,1)S(1)} %bitcast.116), channel_id=1, source_target_pairs={{0,1},{1,0},{2,3},{3,2},{4,5},{5,4},{6,7},{7,6},{8,9},{9,8},{10,11... | collective-permute-start | bytes 3538952 | tf_op jit(solution)/shard_map/ppermute | solution.py:413
  33.2 5.8 %collective-permute-start.6 = (bf16[22,3,384]{2,1,0:T(4,128)(2,1)S(1)}, bf16[22,3,384]{2,1,0:T(4,128)(2,1)S(1)}, u32[]{:S(2)}, u32[]{:S(2)}) collective-permute-start(bf16[22,3,384]{2,1,0:T(4,128)(2,1)S(1)} %get-tuple-element.274), channel_id=1, source_target_pairs={{0,1},{1,0},{2,3},{3,2},{4,5},{5,4},{6,7},{7,6},{8,9},{9,8},{10,11... | collective-permute-start | bytes 152072 | tf_op jit(solution)/shard_map/ppermute | solution.py:383
  33.5 5.5 %collective-permute-start.7 = (bf16[22,3,384]{2,1,0:T(4,128)(2,1)S(1)}, bf16[22,3,384]{2,1,0:T(4,128)(2,1)S(1)}, u32[]{:S(2)}, u32[]{:S(2)}) collective-permute-start(bf16[22,3,384]{2,1,0:T(4,128)(2,1)S(1)} %get-tuple-element.273), channel_id=1, source_target_pairs={{0,4},{1,2},{2,1},{3,7},{4,0},{5,6},{6,5},{7,3},{8,12},{9,10},{10,... | collective-permute-start | bytes 152072 | tf_op jit(solution)/shard_map/ppermute | solution.py:399
  39.5 9.0 %collective-permute-start.10 = (bf16[1,4,2,48,384]{4,3,2,1,0:T(8,128)(2,1)S(1)}, bf16[1,4,2,48,384]{4,3,2,1,0:T(8,128)(2,1)S(1)}, u32[]{:S(2)}, u32[]{:S(2)}) collective-permute-start(bf16[1,4,2,48,384]{4,3,2,1,0:T(8,128)(2,1)S(1)} %get-tuple-element.251), channel_id=1, source_target_pairs={{0,4},{1,5},{2,6},{3,7},{4,0},{5,1},{6,2},{7,3},{8,12},{9,13},{10,... | collective-permute-start | bytes 884744 | tf_op jit(solution)/shard_map/ppermute | solution.py:413
  41.6 8.5 %collective-permute-start.9 = (bf16[1,8,1,48,384]{4,3,1,2,0:T(8,128)(2,1)S(1)}, bf16[1,8,1,48,384]{4,3,1,2,0:T(8,128)(2,1)S(1)}, u32[]{:S(2)}, u32[]{:S(2)}) collective-permute-start(bf16[1,8,1,48,384]{4,3,1,2,0:T(8,128)(2,1)S(1)} %get-tuple-element.253), channel_id=1, source_target_pairs={{0,2},{1,3},{2,0},{3,1},{4,6},{5,7},{6,4},{7,5},{8,10},{9,11},{10,... | collective-permute-start | bytes 884744 | tf_op jit(solution)/shard_map/ppermute | solution.py:413
  50.1 3.2 %collective-permute-start.11 = (bf16[2,16,48,384]{3,2,1,0:T(8,128)(2,1)S(1)}, bf16[2,16,48,384]{3,2,1,0:T(8,128)(2,1)S(1)}, u32[]{:S(2)}, u32[]{:S(2)}) collective-permute-start(bf16[2,16,48,384]{3,2,1,0:T(8,128)(2,1)S(1)} %bitcast.117), channel_id=1, source_target_pairs={{0,1},{1,0},{2,3},{3,2},{4,5},{5,4},{6,7},{7,6},{8,9},{9,8},{10,11... | collective-permute-start | bytes 3538952 | tf_op jit(solution)/shard_map/ppermute | solution.py:413
  50.4 10.5 %collective-permute-start.14 = (bf16[384,384]{1,0:T(8,128)(2,1)S(1)}, bf16[384,384]{1,0:T(8,128)(2,1)S(1)}, u32[]{:S(2)}, u32[]{:S(2)}) collective-permute-start(bf16[384,384]{1,0:T(8,128)(2,1)S(1)} %pad_maximum_fusion.3), channel_id=1, source_target_pairs={{0,8},{1,9},{2,10},{3,11},{4,12},{5,13},{6,14},{7,15},{8,0},{9,1},... | collective-permute-start | bytes 884744 | tf_op jit(solution)/shard_map/ppermute | solution.py:413
  53.8 10.0 %collective-permute-start.13 = (bf16[1,4,2,48,384]{4,3,1,2,0:T(8,128)(2,1)S(1)}, bf16[1,4,2,48,384]{4,3,1,2,0:T(8,128)(2,1)S(1)}, u32[]{:S(2)}, u32[]{:S(2)}) collective-permute-start(bf16[1,4,2,48,384]{4,3,1,2,0:T(8,128)(2,1)S(1)} %bitcast.143), channel_id=1, source_target_pairs={{0,4},{1,5},{2,6},{3,7},{4,0},{5,1},{6,2},{7,3},{8,12},{9,13},{10,... | collective-permute-start | bytes 884744 | tf_op jit(solution)/shard_map/ppermute | solution.py:413
  54.7 9.2 %collective-permute-start.12 = (bf16[1,8,1,48,384]{4,3,1,2,0:T(8,128)(2,1)S(1)}, bf16[1,8,1,48,384]{4,3,1,2,0:T(8,128)(2,1)S(1)}, u32[]{:S(2)}, u32[]{:S(2)}) collective-permute-start(bf16[1,8,1,48,384]{4,3,1,2,0:T(8,128)(2,1)S(1)} %get-tuple-element.249), channel_id=1, source_target_pairs={{0,2},{1,3},{2,0},{3,1},{4,6},{5,7},{6,4},{7,5},{8,10},{9,11},{10,... | collective-permute-start | bytes 884744 | tf_op jit(solution)/shard_map/ppermute | solution.py:413
  58.8 5.0 %collective-permute-start.17 = (bf16[64,384]{1,0:T(8,128)(2,1)S(1)}, bf16[64,384]{1,0:T(8,128)(2,1)S(1)}, u32[]{:S(2)}, u32[]{:S(2)}) collective-permute-start(bf16[64,384]{1,0:T(8,128)(2,1)S(1)} %get-tuple-element.192), channel_id=1, source_target_pairs={{0,1},{1,0},{2,3},{3,2},{4,5},{5,4},{6,7},{7,6},{8,9},{9,8},{10,11... | collective-permute-start | bytes 147464 | tf_op jit(solution)/shard_map/ppermute | solution.py:413
  58.9 4.9 %collective-permute-start.15 = (bf16[3,16,384]{2,1,0:T(8,128)(2,1)S(1)}, bf16[3,16,384]{2,1,0:T(8,128)(2,1)S(1)}, u32[]{:S(2)}, u32[]{:S(2)}) collective-permute-start(bf16[3,16,384]{2,1,0:T(8,128)(2,1)S(1)} %bitcast.148), channel_id=1, source_target_pairs={{0,4},{4,0},{8,12},{12,8},{16,20},{20,16},{24,28},{28,24},{1,5},{5... | collective-permute-start | bytes 110600 | tf_op jit(solution)/shard_map/ppermute | solution.py:383
  60.9 2.9 %collective-permute-start.16 = (bf16[3,16,384]{2,1,0:T(8,128)(2,1)S(1)}, bf16[3,16,384]{2,1,0:T(8,128)(2,1)S(1)}, u32[]{:S(2)}, u32[]{:S(2)}) collective-permute-start(bf16[3,16,384]{2,1,0:T(8,128)(2,1)S(1)} %bitcast.147), channel_id=1, source_target_pairs={{0,1},{1,0},{2,3},{3,2},{4,8},{5,9},{6,10},{7,11},{8,4},{9,5},{10,... | collective-permute-start | bytes 110600 | tf_op jit(solution)/shard_map/ppermute | solution.py:399
  64.4 8.4 %collective-permute-start.18 = (bf16[352,384]{1,0:T(8,128)(2,1)S(1)}, bf16[352,384]{1,0:T(8,128)(2,1)S(1)}, u32[]{:S(2)}, u32[]{:S(2)}) collective-permute-start(bf16[352,384]{1,0:T(8,128)(2,1)S(1)} %get-tuple-element.300), channel_id=1, source_target_pairs={{0,4},{1,5},{2,6},{3,7},{4,0},{5,1},{6,2},{7,3},{8,12},{9,13},{10,... | collective-permute-start | bytes 811016 | tf_op jit(solution)/shard_map/ppermute | solution.py:413
  67.1 7.7 %collective-permute-start.19 = (bf16[352,384]{1,0:T(8,128)(2,1)S(1)}, bf16[352,384]{1,0:T(8,128)(2,1)S(1)}, u32[]{:S(2)}, u32[]{:S(2)}) collective-permute-start(bf16[352,384]{1,0:T(8,128)(2,1)S(1)} %get-tuple-element.299), channel_id=1, source_target_pairs={{0,2},{1,3},{2,0},{3,1},{4,6},{5,7},{6,4},{7,5},{8,10},{9,11},{10,... | collective-permute-start | bytes 811016 | tf_op jit(solution)/shard_map/ppermute | solution.py:413
  68.6 7.1 %collective-permute-start.20 = (bf16[22,3,384]{2,1,0:T(4,128)(2,1)S(1)}, bf16[22,3,384]{2,1,0:T(4,128)(2,1)S(1)}, u32[]{:S(2)}, u32[]{:S(2)}) collective-permute-start(bf16[22,3,384]{2,1,0:T(4,128)(2,1)S(1)} %get-tuple-element.272), channel_id=1, source_target_pairs={{0,1},{1,0},{2,3},{3,2},{4,5},{5,4},{6,7},{7,6},{8,9},{9,8},{10,11... | collective-permute-start | bytes 152072 | tf_op jit(solution)/shard_map/ppermute | solution.py:383
  68.7 7.1 %collective-permute-start.21 = (bf16[22,3,384]{2,1,0:T(4,128)(2,1)S(1)}, bf16[22,3,384]{2,1,0:T(4,128)(2,1)S(1)}, u32[]{:S(2)}, u32[]{:S(2)}) collective-permute-start(bf16[22,3,384]{2,1,0:T(4,128)(2,1)S(1)} %get-tuple-element.271), channel_id=1, source_target_pairs={{0,4},{1,2},{2,1},{3,7},{4,0},{5,6},{6,5},{7,3},{8,12},{9,10},{10,... | collective-permute-start | bytes 152072 | tf_op jit(solution)/shard_map/ppermute | solution.py:399
  68.9 6.9 %collective-permute-start.22 = (bf16[64,384]{1,0:T(8,128)(2,1)S(1)}, bf16[64,384]{1,0:T(8,128)(2,1)S(1)}, u32[]{:S(2)}, u32[]{:S(2)}) collective-permute-start(bf16[64,384]{1,0:T(8,128)(2,1)S(1)} %add_convert_fusion.16), channel_id=1, source_target_pairs={{0,6},{1,7},{2,4},{3,5},{4,2},{5,3},{6,0},{7,1},{8,14},{9,15},{10,... | collective-permute-start | bytes 147464 | tf_op jit(solution)/shard_map/ppermute | solution.py:413
  75.9 10.1 %collective-permute-start.24 = (bf16[96,384]{1,0:T(8,128)(2,1)S(1)}, bf16[96,384]{1,0:T(8,128)(2,1)S(1)}, u32[]{:S(2)}, u32[]{:S(2)}) collective-permute-start(bf16[96,384]{1,0:T(8,128)(2,1)S(1)} %bitcast.146), channel_id=1, source_target_pairs={{0,16},{1,17},{2,18},{3,19},{4,20},{5,21},{6,22},{7,23},{8,24},{9,... | collective-permute-start | bytes 221192 | tf_op jit(solution)/shard_map/ppermute | solution.py:413
  80.0 5.9 %collective-permute-start.23 = (bf16[256,384]{1,0:T(8,128)(2,1)S(1)}, bf16[256,384]{1,0:T(8,128)(2,1)S(1)}, u32[]{:S(2)}, u32[]{:S(2)}) collective-permute-start(bf16[256,384]{1,0:T(8,128)(2,1)S(1)} %pad_maximum_fusion.6), channel_id=1, source_target_pairs={{0,8},{1,9},{2,10},{3,11},{4,12},{5,13},{6,14},{7,15},{8,0},{9,1},... | collective-permute-start | bytes 589832 | tf_op jit(solution)/shard_map/ppermute | solution.py:413
  86.1 7.2 %collective-permute-start.25 = (bf16[160,384]{1,0:T(8,128)(2,1)S(1)}, bf16[160,384]{1,0:T(8,128)(2,1)S(1)}, u32[]{:S(2)}, u32[]{:S(2)}) collective-permute-start(bf16[160,384]{1,0:T(8,128)(2,1)S(1)} %pad_maximum_fusion.7), channel_id=1, source_target_pairs={{0,16},{1,17},{2,18},{3,19},{4,20},{5,21},{6,22},{7,23},{8,24},{9,... | collective-permute-start | bytes 368648 | tf_op jit(solution)/shard_map/ppermute | solution.py:413
  93.3 1.3 %collective-permute-start.26 = (bf16[64,384]{1,0:T(8,128)(2,1)S(1)}, bf16[64,384]{1,0:T(8,128)(2,1)S(1)}, u32[]{:S(2)}, u32[]{:S(2)}) collective-permute-start(bf16[64,384]{1,0:T(8,128)(2,1)S(1)} %add_convert_fusion.13.mine), channel_id=1, source_target_pairs={{0,1},{1,0},{2,3},{3,2},{4,5},{5,4},{6,7},{7,6},{8,9},{9,8},{10,11... | collective-permute-start | bytes 147464 | tf_op jit(solution)/shard_map/ppermute | solution.py:413
  (2 other events, 12.2 us)

commit v13 on v12

--- a/solution.py
+++ b/solution.py
@@ -244,7 +244,7 @@
         split_to(mids, pl.ds(top, strip), mid, (strip, mid_cols))
         return carry
 
-    lax.fori_loop(0, mid_rows // strip, one_strip, 0)
+    lax.fori_loop(0, mid_rows // strip, one_strip, 0, unroll=True)
 
 
 def top_kernel(
@@ -582,11 +582,13 @@
         [pltpu.SMEM] + [None] * 4,
         name="weights_top",
     )
-    tile1, twin, other, dw1, z0 = fenced(tile1, twin, other, dw1, z0)
+    run1 = start(dw1)
+    tile1, twin, other = fenced(tile1, twin, other)
     wide1 = rimmed(tile1, twin, other, 0, odd_row, outer_row)
-    run1 = start(dw1)
     twin, other = edges(wide1, 1, HALO, odd_col)
     twin, other = to_twin(twin, "cols"), to_other(other, "cols")
+    run1, z0 = fenced(run1, z0)
+    pair1 = fork(run1)
     tile_f = shape(pixels, channels)
     again = run(
         again_kernel,
@@ -597,8 +599,7 @@
         fetched=1,
         name="again",
     )
-    wide1, twin, other, run1, again = fenced(wide1, twin, other, run1, again)
-    pair1 = fork(run1)
+    wide1, twin, other, again = fenced(wide1, twin, other, again)
     dzpad1 = filled(rimmed(wide1, twin, other, 1, odd_col, outer_col))
     spread_scratch = [shape(groups, *dzpad1.shape[:2], LANES), tile_z]
     grad_mid, dz0, *rest = run(

time: 96 us -> 94.9 us (0.989)
  starting transfers between devices: 30.3 us -> 28.9 us
    ppermute x15, starting transfers between devices: 17.5 us -> 14.9 us  [flip_bit(): return lax.ppermute(value, both, [(i, i ^ flip) for i in range(total)])]
  transfers between devices with their start and end apart: 27 -> 27, of which waited for: 13 -> 14; matrix products, arithmetic and copies ran while one was open for 2% -> 3% of each run, Pallas kernels for 16% -> 15%
where the time goes in v13:
time: 94.9 us; the launch traced here: 94.7 us
  Pallas kernels  29.4 us (31%)
  starting transfers between devices  28.9 us (30%)
  waiting for transfers between devices  28.8 us (30%)
  other arithmetic  4.83 us (5%)
  local copies, waits for them, and re-layouts  1.41 us (1%)
  between operations  1.26 us (1%)
    pallas_call x9, Pallas kernels, run(): pl.pallas_call(kernel, out_shape=outs, in_specs=[vmem if s is None else p...  29.4 us
    ppermute x15, waiting for transfers between devices, flip_bit(): return lax.ppermute(value, both, [(i, i ^ flip) for i in range(total)])  18 us
    ppermute x15, starting transfers between devices, flip_bit(): return lax.ppermute(value, both, [(i, i ^ flip) for i in range(total)])  14.9 us
    ppermute x6, starting transfers between devices, to_twin(): lax.ppermute(edge, axis, [(i, i ^ 1) for i in range(count) if i ^ 1 < cou...  7.74 us
    ppermute x6, waiting for transfers between devices, to_twin(): lax.ppermute(edge, axis, [(i, i ^ 1) for i in range(count) if i ^ 1 < cou...  7.23 us
    ppermute x6, starting transfers between devices, to_other(): return lax.ppermute(edge, ('rows', 'cols'), pairs)  6.25 us
    ppermute x6, waiting for transfers between devices, to_other(): return lax.ppermute(edge, ('rows', 'cols'), pairs)  3.56 us
  transfers between devices with their start and end apart: 27, of which 14 were waited for; matrix products, arithmetic and copies ran while one was open for 3% of the time, Pallas kernels for 15%

profile of v13, /device:TPU:0, one launch (start us, length us, event | category | flops | bytes accessed | tf_op | source)
XLA Modules:
  0.0 94.7 jit_solution(11184447622651688808)
XLA Ops:
  0.7 0.9 broadcast_select_fusion.8
  2.2 4.0 %collective-permute-start = (bf16[6,16,384]{2,1,0:T(8,128)(2,1)S(1)}, bf16[6,16,384]{2,1,0:T(8,128)(2,1)S(1)}, u32[]{:S(2)}, u32[]{:S(2)}) collective-permute-start(bf16[6,16,384]{2,1,0:T(8,128)(2,1)S(1)} %get-tuple-element.276), channel_id=1, source_target_pairs={{0,4},{4,0},{8,12},{12,8},{16,20},{20,16},{24,28},{28,24},{1,5},{5... | collective-permute-start | bytes 221192 | tf_op jit(solution)/shard_map/ppermute | solution.py:383
  6.2 2.5 %collective-permute-done = bf16[6,16,384]{2,1,0:T(8,128)(2,1)S(1)} collective-permute-done((bf16[6,16,384]{2,1,0:T(8,128)(2,1)S(1)}, bf16[6,16,384]{2,1,0:T(8,128)(2,1)S(1)}, u32[]{:S(2)}, u32[]{:S(2)}) %collective-permute-start) | collective-permute-done | bytes 73760 | tf_op jit(solution)/shard_map/ppermute | solution.py:383
  8.8 1.0 %pad_maximum_fusion.2 = bf16[28,16,384]{2,1,0:T(8,128)(2,1)S(1)} fusion(bf16[6,16,384]{2,1,0:T(8,128)(2,1)S(1)} %get-tuple-element.286, bf16[16,16,384]{2,1,0:T(8,128)(2,1)} %param.8, bf16[6,16,384]{2,1,0:T(8,128)(2,1)S(1)} %get-tuple-element.285), kind=kLoop, calls=%fused_computation.29 | loop fusion | flops 344064 | bytes 688128 | tf_op jit(solution)/shard_map/concatenate | solution.py:406
  9.9 2.5 %collective-permute-start.3 = (bf16[28,6,384]{2,1,0:T(8,128)(2,1)S(1)}, bf16[28,6,384]{2,1,0:T(8,128)(2,1)S(1)}, u32[]{:S(2)}, u32[]{:S(2)}) collective-permute-start(bf16[28,6,384]{2,1,0:T(8,128)(2,1)S(1)} %get-tuple-element.253), channel_id=1, source_target_pairs={{0,4},{1,2},{2,1},{3,7},{4,0},{5,6},{6,5},{7,3},{8,12},{9,10},{10,... | collective-permute-start | bytes 387080 | tf_op jit(solution)/shard_map/ppermute | solution.py:399
  12.4 3.4 %collective-permute-done.3 = bf16[28,6,384]{2,1,0:T(8,128)(2,1)S(1)} collective-permute-done((bf16[28,6,384]{2,1,0:T(8,128)(2,1)S(1)}, bf16[28,6,384]{2,1,0:T(8,128)(2,1)S(1)}, u32[]{:S(2)}, u32[]{:S(2)}) %collective-permute-start.3) | collective-permute-done | bytes 129056 | tf_op jit(solution)/shard_map/ppermute | solution.py:399
  16.2 8.1 %forward.1 = (f32[3,22,24,128]{3,2,1,0:T(8,128)S(1)}, f32[3,16,16,128]{3,2,1,0:T(8,128)S(1)}) custom-call(s32[5]{0:T(128)S(1)} %stack.25.place, bf16[28,32,384]{2,1,0:T(8,128)(2,1)S(1)} %fusion.12.xpad, f32[49,2,384]{2,1,0:T(2,128)S(1)} %bitcast.101, f32[2,384]{1,0:T(2,128)S(1)} %copy-done.4, f32[2,384]{1,0:T(2,128)S(1)} %copy-done.5, ...), custom_call_target="tpu_custom_call" | custom-call | tf_op jit(solution)/shard_map/forward/pallas_call | solution.py:361
  24.4 4.7 %top.1 = (bf16[256,384]{1,0:T(8,128)(2,1)S(1)}, bf16[256,384]{1,0:T(8,128)(2,1)S(1)}, bf16[256,1536]{1,0:T(8,128)(2,1)S(1)}, bf16[256,1536]{1,0:T(8,128)(2,1)S(1...) custom-call(f32[3,22,24,128]{3,2,1,0:T(8,128)S(1)} %get-tuple-element.129.mids, ...), custom_call_target="tpu_custom_call" | custom-call | tf_op jit(solution)/shard_map/top/pallas_call | solution.py:361
  29.1 1.6 %weights_top.1 = (bf16[2,768,384]{2,1,0:T(8,128)(2,1)S(1)}, bf16[2,768,384]{2,1,0:T(8,128)(2,1)S(1)}) custom-call(s32[5]{0:T(128)S(1)} %stack.25.place, bf16[256,384]{1,0:T(8,128)(2,1)S(1)} %get-tuple-element.134.normed, bf16[256,1536]{1,0:T(8,128)(2,1)S(1)} %get-tuple-element.135.act, bf16[256,1536]{1,0:T(8,128)(2,1)S(1)} %get-tuple-element.136.gpre, ...), custom_call_target="tpu_custom_call" | custom-call | tf_op jit(solution)/shard_map/weights_top/pallas_call | solution.py:361
  30.8 2.1 %collective-permute-start.4 = (bf16[3,16,384]{2,1,0:T(8,128)(2,1)S(1)}, bf16[3,16,384]{2,1,0:T(8,128)(2,1)S(1)}, u32[]{:S(2)}, u32[]{:S(2)}) collective-permute-start(bf16[3,16,384]{2,1,0:T(8,128)(2,1)S(1)} %bitcast.150), channel_id=1, source_target_pairs={{0,4},{4,0},{8,12},{12,8},{16,20},{20,16},{24,28},{28,24},{1,5},{5... | collective-permute-start | bytes 110600 | tf_op jit(solution)/shard_map/ppermute | solution.py:383
  33.1 1.9 %collective-permute-done.4 = bf16[3,16,384]{2,1,0:T(8,128)(2,1)S(1)} collective-permute-done((bf16[3,16,384]{2,1,0:T(8,128)(2,1)S(1)}, bf16[3,16,384]{2,1,0:T(8,128)(2,1)S(1)}, u32[]{:S(2)}, u32[]{:S(2)}) %collective-permute-start.4) | collective-permute-done | bytes 36896 | tf_op jit(solution)/shard_map/ppermute | solution.py:383
  35.2 2.9 %collective-permute-start.7 = (bf16[22,3,384]{2,1,0:T(4,128)(2,1)S(1)}, bf16[22,3,384]{2,1,0:T(4,128)(2,1)S(1)}, u32[]{:S(2)}, u32[]{:S(2)}) collective-permute-start(bf16[22,3,384]{2,1,0:T(4,128)(2,1)S(1)} %get-tuple-element.269), channel_id=1, source_target_pairs={{0,4},{1,2},{2,1},{3,7},{4,0},{5,6},{6,5},{7,3},{8,12},{9,10},{10,... | collective-permute-start | bytes 152072 | tf_op jit(solution)/shard_map/ppermute | solution.py:399
  38.6 1.1 %collective-permute-start.10 = (bf16[1,4,2,48,384]{4,3,2,1,0:T(8,128)(2,1)S(1)}, bf16[1,4,2,48,384]{4,3,2,1,0:T(8,128)(2,1)S(1)}, u32[]{:S(2)}, u32[]{:S(2)}) collective-permute-start(bf16[1,4,2,48,384]{4,3,2,1,0:T(8,128)(2,1)S(1)} %get-tuple-element.247), channel_id=1, source_target_pairs={{0,4},{1,5},{2,6},{3,7},{4,0},{5,1},{6,2},{7,3},{8,12},{9,13},{10,... | collective-permute-start | bytes 884744 | tf_op jit(solution)/shard_map/ppermute | solution.py:413
  40.2 2.3 %again.1 = (f32[256,384]{1,0:T(8,128)S(1)}, f32[256,128]{1,0:T(8,128)S(1)}, bf16[256,384]{1,0:T(8,128)(2,1)S(1)}, bf16[256,1536]{1,0:T(8,128)(2,1)S(1)}, f32[256,1536]{1,0:T(8,128)S(1)}) custom-call(f32[3,16,16,128]{3,2,1,0:T(8,128)S(1)} %get-tuple-element.140.z0, f32[2,384]{1,0:T(2,128)S(1)} %copy-done.4, f32[2,384]{1,0:T(2,128)S(1)} %copy-done.5, ...), custom_call_target="tpu_custom_call" | custom-call | tf_op jit(solution)/shard_map/again/pallas_call | solution.py:361
  42.9 4.5 %low.1 = (bf16[256,384]{1,0:T(8,128)(2,1)S(1)}, bf16[256,384]{1,0:T(8,128)(2,1)S(1)}, f32[1,1536]{1,0:T(1,128)S(1)}, f32[1,384]{1,0:T(1,128)S(1)}, f32[1,384]{1,...) custom-call(s32[5]{0:T(128)S(1)} %stack.25.place, ...), custom_call_target="tpu_custom_call" | custom-call | tf_op jit(solution)/shard_map/low/pallas_call | solution.py:361
  47.3 0.8 collective-permute-done.10
  48.8 3.0 %collective-permute-start.14 = (bf16[384,384]{1,0:T(8,128)(2,1)S(1)}, bf16[384,384]{1,0:T(8,128)(2,1)S(1)}, u32[]{:S(2)}, u32[]{:S(2)}) collective-permute-start(bf16[384,384]{1,0:T(8,128)(2,1)S(1)} %pad_maximum_fusion.3), channel_id=1, source_target_pairs={{0,8},{1,9},{2,10},{3,11},{4,12},{5,13},{6,14},{7,15},{8,0},{9,1},... | collective-permute-start | bytes 884744 | tf_op jit(solution)/shard_map/ppermute | solution.py:413
  52.4 1.1 %collective-permute-start.13 = (bf16[1,4,2,48,384]{4,3,1,2,0:T(8,128)(2,1)S(1)}, bf16[1,4,2,48,384]{4,3,1,2,0:T(8,128)(2,1)S(1)}, u32[]{:S(2)}, u32[]{:S(2)}) collective-permute-start(bf16[1,4,2,48,384]{4,3,1,2,0:T(8,128)(2,1)S(1)} %bitcast.143), channel_id=1, source_target_pairs={{0,4},{1,5},{2,6},{3,7},{4,0},{5,1},{6,2},{7,3},{8,12},{9,13},{10,... | collective-permute-start | bytes 884744 | tf_op jit(solution)/shard_map/ppermute | solution.py:413
  53.9 3.7 %taps.1 = (bf16[64,384]{1,0:T(8,128)(2,1)S(1)}, bf16[64,384]{1,0:T(8,128)(2,1)S(1)}) custom-call(s32[5]{0:T(128)S(1)} %stack.25.place, f32[3,22,24,128]{3,2,1,0:T(8,128)S(1)} %get-tuple-element.129.mids, bf16[28,32,384]{2,1,0:T(8,128)(2,1)S(1)} %fusion.12.xpad, bf16[256,384]{1,0:T(8,128)(2,1)S(1)} %get-tuple-element.180.dz0, ...), custom_call_target="tpu_custom_call" | custom-call | tf_op jit(solution)/shard_map/taps/pallas_call | solution.py:361
  57.8 1.1 %collective-permute-start.15 = (bf16[3,16,384]{2,1,0:T(8,128)(2,1)S(1)}, bf16[3,16,384]{2,1,0:T(8,128)(2,1)S(1)}, u32[]{:S(2)}, u32[]{:S(2)}) collective-permute-start(bf16[3,16,384]{2,1,0:T(8,128)(2,1)S(1)} %bitcast.148), channel_id=1, source_target_pairs={{0,4},{4,0},{8,12},{12,8},{16,20},{20,16},{24,28},{28,24},{1,5},{5... | collective-permute-start | bytes 110600 | tf_op jit(solution)/shard_map/ppermute | solution.py:383
  59.6 2.8 %collective-permute-done.15 = bf16[3,16,384]{2,1,0:T(8,128)(2,1)S(1)} collective-permute-done((bf16[3,16,384]{2,1,0:T(8,128)(2,1)S(1)}, bf16[3,16,384]{2,1,0:T(8,128)(2,1)S(1)}, u32[]{:S(2)}, u32[]{:S(2)}) %collective-permute-start.15) | collective-permute-done | bytes 36896 | tf_op jit(solution)/shard_map/ppermute | solution.py:383
  62.9 1.2 %collective-permute-start.19 = (bf16[352,384]{1,0:T(8,128)(2,1)S(1)}, bf16[352,384]{1,0:T(8,128)(2,1)S(1)}, u32[]{:S(2)}, u32[]{:S(2)}) collective-permute-start(bf16[352,384]{1,0:T(8,128)(2,1)S(1)} %get-tuple-element.295), channel_id=1, source_target_pairs={{0,2},{1,3},{2,0},{3,1},{4,6},{5,7},{6,4},{7,5},{8,10},{9,11},{10,... | collective-permute-start | bytes 811016 | tf_op jit(solution)/shard_map/ppermute | solution.py:413
  64.1 2.9 %collective-permute-start.18 = (bf16[352,384]{1,0:T(8,128)(2,1)S(1)}, bf16[352,384]{1,0:T(8,128)(2,1)S(1)}, u32[]{:S(2)}, u32[]{:S(2)}) collective-permute-start(bf16[352,384]{1,0:T(8,128)(2,1)S(1)} %get-tuple-element.296), channel_id=1, source_target_pairs={{0,4},{1,5},{2,6},{3,7},{4,0},{5,1},{6,2},{7,3},{8,12},{9,13},{10,... | collective-permute-start | bytes 811016 | tf_op jit(solution)/shard_map/ppermute | solution.py:413
  67.8 2.9 %collective-permute-done.19 = bf16[352,384]{1,0:T(8,128)(2,1)S(1)} collective-permute-done((bf16[352,384]{1,0:T(8,128)(2,1)S(1)}, bf16[352,384]{1,0:T(8,128)(2,1)S(1)}, u32[]{:S(2)}, u32[]{:S(2)}) %collective-permute-start.19) | collective-permute-done | bytes 270368 | tf_op jit(solution)/shard_map/ppermute | solution.py:413
  70.8 2.4 %collective-permute-done.18 = bf16[352,384]{1,0:T(8,128)(2,1)S(1)} collective-permute-done((bf16[352,384]{1,0:T(8,128)(2,1)S(1)}, bf16[352,384]{1,0:T(8,128)(2,1)S(1)}, u32[]{:S(2)}, u32[]{:S(2)}) %collective-permute-start.18) | collective-permute-done | bytes 270368 | tf_op jit(solution)/shard_map/ppermute | solution.py:413
  73.3 1.0 %collective-permute-done.22 = bf16[64,384]{1,0:T(8,128)(2,1)S(1)} collective-permute-done((bf16[64,384]{1,0:T(8,128)(2,1)S(1)}, bf16[64,384]{1,0:T(8,128)(2,1)S(1)}, u32[]{:S(2)}, u32[]{:S(2)}) %collective-permute-start.22) | collective-permute-done | bytes 49184 | tf_op jit(solution)/shard_map/ppermute | solution.py:413
  74.6 4.0 %collective-permute-start.24 = (bf16[96,384]{1,0:T(8,128)(2,1)S(1)}, bf16[96,384]{1,0:T(8,128)(2,1)S(1)}, u32[]{:S(2)}, u32[]{:S(2)}) collective-permute-start(bf16[96,384]{1,0:T(8,128)(2,1)S(1)} %bitcast.146), channel_id=1, source_target_pairs={{0,16},{1,17},{2,18},{3,19},{4,20},{5,21},{6,22},{7,23},{8,24},{9,... | collective-permute-start | bytes 221192 | tf_op jit(solution)/shard_map/ppermute | solution.py:413
  79.3 2.5 %last.1 = bf16[256,384]{1,0:T(8,128)(2,1)} custom-call(bf16[22,32,384]{2,1,0:T(8,128)(2,1)S(1)} %fusion.18.dzpad, bf16[256,384]{1,0:T(8,128)(2,1)S(1)} %get-tuple-element.219.gmid, f32[49,2,384]{2,1,0:T(2,128)S(1)} %bitcast.104), custom_call_target="tpu_custom_call" | custom-call | tf_op jit(solution)/shard_map/last/pallas_call | solution.py:361
  81.8 2.9 %collective-permute-done.23 = bf16[256,384]{1,0:T(8,128)(2,1)S(1)} collective-permute-done((bf16[256,384]{1,0:T(8,128)(2,1)S(1)}, bf16[256,384]{1,0:T(8,128)(2,1)S(1)}, u32[]{:S(2)}, u32[]{:S(2)}) %collective-permute-start.23) | collective-permute-done | bytes 196640 | tf_op jit(solution)/shard_map/ppermute | solution.py:413
  85.7 6.4 %collective-permute-done.25 = bf16[160,384]{1,0:T(8,128)(2,1)S(1)} collective-permute-done((bf16[160,384]{1,0:T(8,128)(2,1)S(1)}, bf16[160,384]{1,0:T(8,128)(2,1)S(1)}, u32[]{:S(2)}, u32[]{:S(2)}) %collective-permute-start.25) | collective-permute-done | bytes 122912 | tf_op jit(solution)/shard_map/ppermute | solution.py:413
  92.2 0.7 weights.1
  93.4 1.3 %small.1 = (f32[49,2,384]{2,1,0:T(2,128)}, f32[2,384]{1,0:T(2,128)}, f32[2,384]{1,0:T(2,128)}, f32[2,1536]{1,0:T(2,128)}) custom-call(s32[5]{0:T(128)S(1)} %stack.25.place, bf16[64,384]{1,0:T(8,128)(2,1)S(1)} %add_convert_fusion.13.mine, bf16[64,384]{1,0:T(8,128)(2,1)S(1)} %collective-permute-done.26.got), custom_call_target="tpu_custom_call" | custom-call | tf_op jit(solution)/shard_map/small/pallas_call | solution.py:361
  (113 shorter events, 9.0 us)
Async XLA Ops:
  1.7 4.6 %collective-permute-start.1 = (bf16[6,16,384]{2,1,0:T(8,128)(2,1)S(1)}, bf16[6,16,384]{2,1,0:T(8,128)(2,1)S(1)}, u32[]{:S(2)}, u32[]{:S(2)}) collective-permute-start(bf16[6,16,384]{2,1,0:T(8,128)(2,1)S(1)} %get-tuple-element.275), channel_id=1, source_target_pairs={{0,1},{1,0},{2,3},{3,2},{4,8},{5,9},{6,10},{7,11},{8,4},{9,5},{10,... | collective-permute-start | bytes 221192 | tf_op jit(solution)/shard_map/ppermute | solution.py:399
  2.2 13.6 %copy-start.6 = (bf16[16,16,384]{2,1,0:T(8,128)(2,1)S(1)}, bf16[16,16,384]{2,1,0:T(8,128)(2,1)}, u32[]{:S(2)}) copy-start(bf16[16,16,384]{2,1,0:T(8,128)(2,1)} %param.8) | copy-start | bytes 589828
  2.2 6.5 %collective-permute-start = (bf16[6,16,384]{2,1,0:T(8,128)(2,1)S(1)}, bf16[6,16,384]{2,1,0:T(8,128)(2,1)S(1)}, u32[]{:S(2)}, u32[]{:S(2)}) collective-permute-start(bf16[6,16,384]{2,1,0:T(8,128)(2,1)S(1)} %get-tuple-element.276), channel_id=1, source_target_pairs={{0,4},{4,0},{8,12},{12,8},{16,20},{20,16},{24,28},{28,24},{1,5},{5... | collective-permute-start | bytes 221192 | tf_op jit(solution)/shard_map/ppermute | solution.py:383
  9.8 6.4 %copy-start.1 = (f32[2,7,7,384]{3,0,2,1:T(2,128)S(1)}, f32[2,7,7,384]{3,0,2,1:T(2,128)}, u32[]{:S(2)}) copy-start(f32[2,7,7,384]{3,0,2,1:T(2,128)} %param.10) | copy-start | bytes 451588
  9.8 6.4 %copy-start.3 = (f32[2,1536]{1,0:T(2,128)S(1)}, f32[2,1536]{1,0:T(2,128)}, u32[]{:S(2)}) copy-start(f32[2,1536]{1,0:T(2,128)} %b_in.5) | copy-start | bytes 36868
  9.8 6.4 %copy-start.4 = (f32[2,384]{1,0:T(2,128)S(1)}, f32[2,384]{1,0:T(2,128)}, u32[]{:S(2)}) copy-start(f32[2,384]{1,0:T(2,128)} %gains.7) | copy-start | bytes 9220
  9.9 5.9 %collective-permute-start.3 = (bf16[28,6,384]{2,1,0:T(8,128)(2,1)S(1)}, bf16[28,6,384]{2,1,0:T(8,128)(2,1)S(1)}, u32[]{:S(2)}, u32[]{:S(2)}) collective-permute-start(bf16[28,6,384]{2,1,0:T(8,128)(2,1)S(1)} %get-tuple-element.253), channel_id=1, source_target_pairs={{0,4},{1,2},{2,1},{3,7},{4,0},{5,6},{6,5},{7,3},{8,12},{9,10},{10,... | collective-permute-start | bytes 387080 | tf_op jit(solution)/shard_map/ppermute | solution.py:399
  12.4 3.4 %collective-permute-start.2 = (bf16[28,6,384]{2,1,0:T(8,128)(2,1)S(1)}, bf16[28,6,384]{2,1,0:T(8,128)(2,1)S(1)}, u32[]{:S(2)}, u32[]{:S(2)}) collective-permute-start(bf16[28,6,384]{2,1,0:T(8,128)(2,1)S(1)} %get-tuple-element.254), channel_id=1, source_target_pairs={{0,1},{1,0},{2,3},{3,2},{4,5},{5,4},{6,7},{7,6},{8,9},{9,8},{10,11... | collective-permute-start | bytes 387080 | tf_op jit(solution)/shard_map/ppermute | solution.py:383
  16.2 8.2 %copy-start.2 = (bf16[16,16,384]{2,1,0:T(8,128)(2,1)S(1)}, bf16[16,16,384]{2,1,0:T(8,128)(2,1)}, u32[]{:S(2)}) copy-start(bf16[16,16,384]{2,1,0:T(8,128)(2,1)} %param.9) | copy-start | bytes 589828
  30.7 7.4 %collective-permute-start.8 = (bf16[2,16,48,384]{3,2,1,0:T(8,128)(2,1)S(1)}, bf16[2,16,48,384]{3,2,1,0:T(8,128)(2,1)S(1)}, u32[]{:S(2)}, u32[]{:S(2)}) collective-permute-start(bf16[2,16,48,384]{3,2,1,0:T(8,128)(2,1)S(1)} %bitcast.116), channel_id=1, source_target_pairs={{0,1},{1,0},{2,3},{3,2},{4,5},{5,4},{6,7},{7,6},{8,9},{9,8},{10,11... | collective-permute-start | bytes 3538952 | tf_op jit(solution)/shard_map/ppermute | solution.py:413
  30.8 4.2 %collective-permute-start.4 = (bf16[3,16,384]{2,1,0:T(8,128)(2,1)S(1)}, bf16[3,16,384]{2,1,0:T(8,128)(2,1)S(1)}, u32[]{:S(2)}, u32[]{:S(2)}) collective-permute-start(bf16[3,16,384]{2,1,0:T(8,128)(2,1)S(1)} %bitcast.150), channel_id=1, source_target_pairs={{0,4},{4,0},{8,12},{12,8},{16,20},{20,16},{24,28},{28,24},{1,5},{5... | collective-permute-start | bytes 110600 | tf_op jit(solution)/shard_map/ppermute | solution.py:383
  32.9 2.1 %collective-permute-start.5 = (bf16[3,16,384]{2,1,0:T(8,128)(2,1)S(1)}, bf16[3,16,384]{2,1,0:T(8,128)(2,1)S(1)}, u32[]{:S(2)}, u32[]{:S(2)}) collective-permute-start(bf16[3,16,384]{2,1,0:T(8,128)(2,1)S(1)} %bitcast.149), channel_id=1, source_target_pairs={{0,1},{1,0},{2,3},{3,2},{4,8},{5,9},{6,10},{7,11},{8,4},{9,5},{10,... | collective-permute-start | bytes 110600 | tf_op jit(solution)/shard_map/ppermute | solution.py:399
  35.2 7.3 %collective-permute-start.7 = (bf16[22,3,384]{2,1,0:T(4,128)(2,1)S(1)}, bf16[22,3,384]{2,1,0:T(4,128)(2,1)S(1)}, u32[]{:S(2)}, u32[]{:S(2)}) collective-permute-start(bf16[22,3,384]{2,1,0:T(4,128)(2,1)S(1)} %get-tuple-element.269), channel_id=1, source_target_pairs={{0,4},{1,2},{2,1},{3,7},{4,0},{5,6},{6,5},{7,3},{8,12},{9,10},{10,... | collective-permute-start | bytes 152072 | tf_op jit(solution)/shard_map/ppermute | solution.py:399
  38.1 4.5 %collective-permute-start.6 = (bf16[22,3,384]{2,1,0:T(4,128)(2,1)S(1)}, bf16[22,3,384]{2,1,0:T(4,128)(2,1)S(1)}, u32[]{:S(2)}, u32[]{:S(2)}) collective-permute-start(bf16[22,3,384]{2,1,0:T(4,128)(2,1)S(1)} %get-tuple-element.270), channel_id=1, source_target_pairs={{0,1},{1,0},{2,3},{3,2},{4,5},{5,4},{6,7},{7,6},{8,9},{9,8},{10,11... | collective-permute-start | bytes 152072 | tf_op jit(solution)/shard_map/ppermute | solution.py:383
  38.6 9.5 %collective-permute-start.10 = (bf16[1,4,2,48,384]{4,3,2,1,0:T(8,128)(2,1)S(1)}, bf16[1,4,2,48,384]{4,3,2,1,0:T(8,128)(2,1)S(1)}, u32[]{:S(2)}, u32[]{:S(2)}) collective-permute-start(bf16[1,4,2,48,384]{4,3,2,1,0:T(8,128)(2,1)S(1)} %get-tuple-element.247), channel_id=1, source_target_pairs={{0,4},{1,5},{2,6},{3,7},{4,0},{5,1},{6,2},{7,3},{8,12},{9,13},{10,... | collective-permute-start | bytes 884744 | tf_op jit(solution)/shard_map/ppermute | solution.py:413
  39.8 8.7 %collective-permute-start.9 = (bf16[1,8,1,48,384]{4,3,1,2,0:T(8,128)(2,1)S(1)}, bf16[1,8,1,48,384]{4,3,1,2,0:T(8,128)(2,1)S(1)}, u32[]{:S(2)}, u32[]{:S(2)}) collective-permute-start(bf16[1,8,1,48,384]{4,3,1,2,0:T(8,128)(2,1)S(1)} %get-tuple-element.249), channel_id=1, source_target_pairs={{0,2},{1,3},{2,0},{3,1},{4,6},{5,7},{6,4},{7,5},{8,10},{9,11},{10,... | collective-permute-start | bytes 884744 | tf_op jit(solution)/shard_map/ppermute | solution.py:413
  48.5 3.3 %collective-permute-start.11 = (bf16[2,16,48,384]{3,2,1,0:T(8,128)(2,1)S(1)}, bf16[2,16,48,384]{3,2,1,0:T(8,128)(2,1)S(1)}, u32[]{:S(2)}, u32[]{:S(2)}) collective-permute-start(bf16[2,16,48,384]{3,2,1,0:T(8,128)(2,1)S(1)} %bitcast.117), channel_id=1, source_target_pairs={{0,1},{1,0},{2,3},{3,2},{4,5},{5,4},{6,7},{7,6},{8,9},{9,8},{10,11... | collective-permute-start | bytes 3538952 | tf_op jit(solution)/shard_map/ppermute | solution.py:413
  48.8 10.7 %collective-permute-start.14 = (bf16[384,384]{1,0:T(8,128)(2,1)S(1)}, bf16[384,384]{1,0:T(8,128)(2,1)S(1)}, u32[]{:S(2)}, u32[]{:S(2)}) collective-permute-start(bf16[384,384]{1,0:T(8,128)(2,1)S(1)} %pad_maximum_fusion.3), channel_id=1, source_target_pairs={{0,8},{1,9},{2,10},{3,11},{4,12},{5,13},{6,14},{7,15},{8,0},{9,1},... | collective-permute-start | bytes 884744 | tf_op jit(solution)/shard_map/ppermute | solution.py:413
  52.4 10.0 %collective-permute-start.13 = (bf16[1,4,2,48,384]{4,3,1,2,0:T(8,128)(2,1)S(1)}, bf16[1,4,2,48,384]{4,3,1,2,0:T(8,128)(2,1)S(1)}, u32[]{:S(2)}, u32[]{:S(2)}) collective-permute-start(bf16[1,4,2,48,384]{4,3,1,2,0:T(8,128)(2,1)S(1)} %bitcast.143), channel_id=1, source_target_pairs={{0,4},{1,5},{2,6},{3,7},{4,0},{5,1},{6,2},{7,3},{8,12},{9,13},{10,... | collective-permute-start | bytes 884744 | tf_op jit(solution)/shard_map/ppermute | solution.py:413
  53.6 8.8 %collective-permute-start.12 = (bf16[1,8,1,48,384]{4,3,1,2,0:T(8,128)(2,1)S(1)}, bf16[1,8,1,48,384]{4,3,1,2,0:T(8,128)(2,1)S(1)}, u32[]{:S(2)}, u32[]{:S(2)}) collective-permute-start(bf16[1,8,1,48,384]{4,3,1,2,0:T(8,128)(2,1)S(1)} %get-tuple-element.245), channel_id=1, source_target_pairs={{0,2},{1,3},{2,0},{3,1},{4,6},{5,7},{6,4},{7,5},{8,10},{9,11},{10,... | collective-permute-start | bytes 884744 | tf_op jit(solution)/shard_map/ppermute | solution.py:413
  57.7 4.7 %collective-permute-start.17 = (bf16[64,384]{1,0:T(8,128)(2,1)S(1)}, bf16[64,384]{1,0:T(8,128)(2,1)S(1)}, u32[]{:S(2)}, u32[]{:S(2)}) collective-permute-start(bf16[64,384]{1,0:T(8,128)(2,1)S(1)} %get-tuple-element.188), channel_id=1, source_target_pairs={{0,1},{1,0},{2,3},{3,2},{4,5},{5,4},{6,7},{7,6},{8,9},{9,8},{10,11... | collective-permute-start | bytes 147464 | tf_op jit(solution)/shard_map/ppermute | solution.py:413
  57.8 4.6 %collective-permute-start.15 = (bf16[3,16,384]{2,1,0:T(8,128)(2,1)S(1)}, bf16[3,16,384]{2,1,0:T(8,128)(2,1)S(1)}, u32[]{:S(2)}, u32[]{:S(2)}) collective-permute-start(bf16[3,16,384]{2,1,0:T(8,128)(2,1)S(1)} %bitcast.148), channel_id=1, source_target_pairs={{0,4},{4,0},{8,12},{12,8},{16,20},{20,16},{24,28},{28,24},{1,5},{5... | collective-permute-start | bytes 110600 | tf_op jit(solution)/shard_map/ppermute | solution.py:383
  59.5 2.9 %collective-permute-start.16 = (bf16[3,16,384]{2,1,0:T(8,128)(2,1)S(1)}, bf16[3,16,384]{2,1,0:T(8,128)(2,1)S(1)}, u32[]{:S(2)}, u32[]{:S(2)}) collective-permute-start(bf16[3,16,384]{2,1,0:T(8,128)(2,1)S(1)} %bitcast.147), channel_id=1, source_target_pairs={{0,1},{1,0},{2,3},{3,2},{4,8},{5,9},{6,10},{7,11},{8,4},{9,5},{10,... | collective-permute-start | bytes 110600 | tf_op jit(solution)/shard_map/ppermute | solution.py:399
  62.9 7.9 %collective-permute-start.19 = (bf16[352,384]{1,0:T(8,128)(2,1)S(1)}, bf16[352,384]{1,0:T(8,128)(2,1)S(1)}, u32[]{:S(2)}, u32[]{:S(2)}) collective-permute-start(bf16[352,384]{1,0:T(8,128)(2,1)S(1)} %get-tuple-element.295), channel_id=1, source_target_pairs={{0,2},{1,3},{2,0},{3,1},{4,6},{5,7},{6,4},{7,5},{8,10},{9,11},{10,... | collective-permute-start | bytes 811016 | tf_op jit(solution)/shard_map/ppermute | solution.py:413
  64.1 9.1 %collective-permute-start.18 = (bf16[352,384]{1,0:T(8,128)(2,1)S(1)}, bf16[352,384]{1,0:T(8,128)(2,1)S(1)}, u32[]{:S(2)}, u32[]{:S(2)}) collective-permute-start(bf16[352,384]{1,0:T(8,128)(2,1)S(1)} %get-tuple-element.296), channel_id=1, source_target_pairs={{0,4},{1,5},{2,6},{3,7},{4,0},{5,1},{6,2},{7,3},{8,12},{9,13},{10,... | collective-permute-start | bytes 811016 | tf_op jit(solution)/shard_map/ppermute | solution.py:413
  67.2 7.3 %collective-permute-start.21 = (bf16[22,3,384]{2,1,0:T(4,128)(2,1)S(1)}, bf16[22,3,384]{2,1,0:T(4,128)(2,1)S(1)}, u32[]{:S(2)}, u32[]{:S(2)}) collective-permute-start(bf16[22,3,384]{2,1,0:T(4,128)(2,1)S(1)} %get-tuple-element.267), channel_id=1, source_target_pairs={{0,4},{1,2},{2,1},{3,7},{4,0},{5,6},{6,5},{7,3},{8,12},{9,10},{10,... | collective-permute-start | bytes 152072 | tf_op jit(solution)/shard_map/ppermute | solution.py:399
  67.3 7.2 %collective-permute-start.20 = (bf16[22,3,384]{2,1,0:T(4,128)(2,1)S(1)}, bf16[22,3,384]{2,1,0:T(4,128)(2,1)S(1)}, u32[]{:S(2)}, u32[]{:S(2)}) collective-permute-start(bf16[22,3,384]{2,1,0:T(4,128)(2,1)S(1)} %get-tuple-element.268), channel_id=1, source_target_pairs={{0,1},{1,0},{2,3},{3,2},{4,5},{5,4},{6,7},{7,6},{8,9},{9,8},{10,11... | collective-permute-start | bytes 152072 | tf_op jit(solution)/shard_map/ppermute | solution.py:383
  67.8 6.5 %collective-permute-start.22 = (bf16[64,384]{1,0:T(8,128)(2,1)S(1)}, bf16[64,384]{1,0:T(8,128)(2,1)S(1)}, u32[]{:S(2)}, u32[]{:S(2)}) collective-permute-start(bf16[64,384]{1,0:T(8,128)(2,1)S(1)} %add_convert_fusion.16), channel_id=1, source_target_pairs={{0,6},{1,7},{2,4},{3,5},{4,2},{5,3},{6,0},{7,1},{8,14},{9,15},{10,... | collective-permute-start | bytes 147464 | tf_op jit(solution)/shard_map/ppermute | solution.py:413
  74.6 10.2 %collective-permute-start.24 = (bf16[96,384]{1,0:T(8,128)(2,1)S(1)}, bf16[96,384]{1,0:T(8,128)(2,1)S(1)}, u32[]{:S(2)}, u32[]{:S(2)}) collective-permute-start(bf16[96,384]{1,0:T(8,128)(2,1)S(1)} %bitcast.146), channel_id=1, source_target_pairs={{0,16},{1,17},{2,18},{3,19},{4,20},{5,21},{6,22},{7,23},{8,24},{9,... | collective-permute-start | bytes 221192 | tf_op jit(solution)/shard_map/ppermute | solution.py:413
  78.8 6.0 %collective-permute-start.23 = (bf16[256,384]{1,0:T(8,128)(2,1)S(1)}, bf16[256,384]{1,0:T(8,128)(2,1)S(1)}, u32[]{:S(2)}, u32[]{:S(2)}) collective-permute-start(bf16[256,384]{1,0:T(8,128)(2,1)S(1)} %pad_maximum_fusion.6), channel_id=1, source_target_pairs={{0,8},{1,9},{2,10},{3,11},{4,12},{5,13},{6,14},{7,15},{8,0},{9,1},... | collective-permute-start | bytes 589832 | tf_op jit(solution)/shard_map/ppermute | solution.py:413
  84.9 7.2 %collective-permute-start.25 = (bf16[160,384]{1,0:T(8,128)(2,1)S(1)}, bf16[160,384]{1,0:T(8,128)(2,1)S(1)}, u32[]{:S(2)}, u32[]{:S(2)}) collective-permute-start(bf16[160,384]{1,0:T(8,128)(2,1)S(1)} %pad_maximum_fusion.7), channel_id=1, source_target_pairs={{0,16},{1,17},{2,18},{3,19},{4,20},{5,21},{6,22},{7,23},{8,24},{9,... | collective-permute-start | bytes 368648 | tf_op jit(solution)/shard_map/ppermute | solution.py:413
  92.1 1.3 %collective-permute-start.26 = (bf16[64,384]{1,0:T(8,128)(2,1)S(1)}, bf16[64,384]{1,0:T(8,128)(2,1)S(1)}, u32[]{:S(2)}, u32[]{:S(2)}) collective-permute-start(bf16[64,384]{1,0:T(8,128)(2,1)S(1)} %add_convert_fusion.13.mine), channel_id=1, source_target_pairs={{0,1},{1,0},{2,3},{3,2},{4,5},{5,4},{6,7},{7,6},{8,9},{9,8},{10,11... | collective-permute-start | bytes 147464 | tf_op jit(solution)/shard_map/ppermute | solution.py:413
  (2 other events, 8.0 us)

commit v14 on v13

--- a/solution.py
+++ b/solution.py
@@ -212,6 +212,15 @@
     return copies
 
 
+def edges_kernel(place, tile, copy, twin, other):
+    width = twin.shape[0]
+    odd = place[5] == 1
+    copy[...] = tile[...]
+    low, high = tile[:width].astype(F32), tile[tile.shape[0] - width :].astype(F32)
+    twin[...] = jnp.where(odd, low, high).astype(BF16)
+    other[...] = jnp.where(odd, high, low).astype(BF16)
+
+
 def forward_kernel(
     place, xpad, taps, gains, shifts, w_in, w_out, b_in, mids, z_out,
     xs, zs, act, w_in0, w_out0, arrived,
@@ -315,16 +324,16 @@
         sums[count + 2 : count + 51, g * LANES : (g + 1) * LANES] = taps[g]
 
 
-def taps_kernel(
-    place, mids, xpad, dz0, dz1, db0, dgain0, dshift0, db1, dgain1, dshift1, send, keep,
-    xs, dzs, taps, sums0, sums1,
-):
+def top_taps_kernel(mids, dz, db, dgain, dshift, sums, dzs, taps):
+    sums[...] = jnp.zeros(sums.shape, F32)
+    small_rows_of(mids, 0, 0, dz, dzs, taps, db, dgain, dshift, sums)
+
+
+def taps_kernel(place, xpad, dz, db, dgain, dshift, sums1, send, keep, xs, dzs, taps, sums0):
     for g in range(dzs.shape[0]):
         xs[g] = xpad[:, :, g * LANES : (g + 1) * LANES].astype(F32)
     sums0[...] = jnp.zeros(sums0.shape, F32)
-    sums1[...] = jnp.zeros(sums1.shape, F32)
-    small_rows_of(mids, 0, 0, dz1, dzs, taps, db1, dgain1, dshift1, sums1)
-    small_rows_of(xs, HALO, HALO, dz0, dzs, taps, db0, dgain0, dshift0, sums0)
+    small_rows_of(xs, HALO, HALO, dz, dzs, taps, db, dgain, dshift, sums0)
     upper = place[4] == 1
     send[...] = jnp.where(upper, sums0[...], sums1[...]).astype(BF16)
     keep[...] = jnp.where(upper, sums1[...], sums0[...]).astype(BF16)
@@ -464,6 +473,7 @@
             jnp.int32(rows * n_rows),
             jnp.int32(cols * n_cols),
             lax.axis_index("cols") & 1,
+            lax.axis_index("rows") & 1,
         ]
     ).astype(jnp.int32)
     grad_flat = grad_out.reshape(pixels, channels)
@@ -479,10 +489,6 @@
     def rim_cols(tile, width):
         twin, other = edges(tile, 1, width, odd_col)
         return rimmed(tile, to_twin(twin, "cols"), to_other(other, "cols"), 1, odd_col, outer_col)
-
-    def rim_rows(tile, width):
-        twin, other = edges(tile, 0, width, odd_row)
-        return rimmed(tile, to_twin(twin, "rows"), to_other(other, "rows"), 0, odd_row, outer_row)
 
     def filled(wide):
         return jnp.pad(wide, ((0, 0), (0, cols + 16 - wide.shape[1]), (0, 0)))
@@ -497,9 +503,19 @@
     split = 2 if per % 16 == 0 and col_bits == 2 else 1
     grads_b = (shape(2, hidden // split, channels, dtype=BF16),) * split
     small_outs = (shape(1, hidden), shape(1, channels), shape(1, channels))
-    small_rows = 64
-
-    xpad = filled(rim_cols(rim_rows(activations, WIDE), WIDE))
+    small_rows = -(-(hidden // channels + 51) // 8) * 8
+
+    edge = shape(WIDE, cols, channels, dtype=BF16)
+    tile, twin, other = run(
+        edges_kernel,
+        (shape(rows, cols, channels, dtype=BF16), edge, edge),
+        [],
+        (place, activations),
+        [pltpu.SMEM, None],
+        name="edges",
+    )
+    wide = rimmed(tile, to_twin(twin, "rows"), to_other(other, "rows"), 0, odd_row, outer_row)
+    xpad = filled(rim_cols(wide, WIDE))
     mids, z0 = run(
         forward_kernel,
         (shape(groups, mid_rows, mid_cols, LANES), tile_z),
@@ -583,7 +599,15 @@
         name="weights_top",
     )
     run1 = start(dw1)
-    tile1, twin, other = fenced(tile1, twin, other)
+    small_f = shape(small_rows, channels)
+    (small1,) = run(
+        top_taps_kernel,
+        (small_f,),
+        [tile_z, shape(groups, 49, LANES)],
+        (mids, dz1, *small1),
+        name="top_taps",
+    )
+    tile1, twin, other, small1 = fenced(tile1, twin, other, small1)
     wide1 = rimmed(tile1, twin, other, 0, odd_row, outer_row)
     twin, other = edges(wide1, 1, HALO, odd_col)
     twin, other = to_twin(twin, "cols"), to_other(other, "cols")
@@ -616,42 +640,37 @@
     run0 = start(dw0)
     low_bit = col_bits + 1
     pair1, _ = onward([settled(f) for f in pair1], low_bit)
-    run0, dz0, small0 = fenced(run0, dz0, small0)
+    small_b = shape(small_rows, channels, dtype=BF16)
+    send, small = run(
+        taps_kernel,
+        (small_b, small_b),
+        [shape(groups, *xpad.shape[:2], LANES), tile_z, shape(groups, 49, LANES), small_f],
+        (place, xpad, dz0, *small0, small1),
+        [pltpu.SMEM] + [None] * 6,
+        name="taps",
+    )
+    small_got = flip_bit(send, 0)
+    run0, dz0, small, small_got = fenced(run0, dz0, small, small_got)
     pair0 = fork(run0)
     tile0 = dz0.reshape(rows, cols, channels)
     twin, other = edges(tile0, 0, HALO, odd_row)
     twin, other = to_twin(twin, "rows"), to_other(other, "rows")
-    small_b = shape(small_rows, channels, dtype=BF16)
-    small_f = shape(small_rows, channels)
-    send, small = run(
-        taps_kernel,
-        (small_b, small_b),
-        [
-            shape(groups, *xpad.shape[:2], LANES), tile_z, shape(groups, 49, LANES),
-            small_f, small_f,
-        ],
-        (place, mids, xpad, dz0, dz1, *small0, *small1),
-        [pltpu.SMEM] + [None] * 10,
-        name="taps",
-    )
-    small_got = flip_bit(send, 0)
-    pair0, pair1, tile0, twin, other, small, small_got = fenced(
-        pair0, pair1, tile0, twin, other, small, small_got
-    )
     small = summed(small, small_got)
     for bit in range(1, col_bits - 1):
         small = summed(small, flip_bit(small, bit))
-    both, small_by = [], []
-    for i in range(2):
-        flights, (came,) = onward([settled(pair0[i]), settled(pair1[i])], sides[1 - i], small)
-        both.append(flights)
-        small_by.append(came)
-    small_by.append(flip_bit(small, *sides))
+    small_got = flip_bit(small, sides[0])
+    pair0, pair1, tile0, twin, other, small, small_got = fenced(
+        pair0, pair1, tile0, twin, other, small, small_got
+    )
+    small = summed(small, small_got)
+    moved_in, (small_got,) = onward([settled(pair0[0]), settled(pair1[0])], sides[1], small)
+    moved_out, _ = onward([settled(pair0[1]), settled(pair1[1])], sides[0])
+    both = [moved_in, moved_out]
     wide0 = rimmed(tile0, twin, other, 0, odd_row, outer_row)
     twin, other = edges(wide0, 1, HALO, odd_col)
     twin, other = to_twin(twin, "cols"), to_other(other, "cols")
-    both, wide0, twin, other, small, small_by = fenced(both, wide0, twin, other, small, small_by)
-    small = summed(small, small_by[0], small_by[1], small_by[2])
+    both, wide0, twin, other, small, small_got = fenced(both, wide0, twin, other, small, small_got)
+    small = summed(small, small_got)
     (run0,), (small_got,) = onward([merged([both[0][0], both[1][0]])], low_bit, small)
     part1, order1 = merged([both[0][1], both[1][1]])
     flight1 = (part1, jnp.zeros_like(part1), order1)

time: 94.9 us -> 94.9 us (level)
  other arithmetic: 4.83 us -> 2.91 us
    ppermute x15, starting transfers between devices: 14.9 us -> 16.3 us  [flip_bit(): return lax.ppermute(value, both, [(i, i ^ flip) for i in range(total)])]
    ppermute x15, waiting for transfers between devices: 18 us -> 19.1 us  [flip_bit(): return lax.ppermute(value, both, [(i, i ^ flip) for i in range(total)])]
    pallas_call x9 -> x11, Pallas kernels: 29.4 us -> 29.7 us  [run(): pl.pallas_call(kernel, out_shape=outs, in_specs=[vmem if s is None else p...]
  transfers between devices with their start and end apart: 27 -> 27, of which waited for: 14 -> 12; matrix products, arithmetic and copies ran while one was open for 3% -> 3% of each run, Pallas kernels for 15% -> 14%
where the time goes in v14:
time: 94.9 us; the launch traced here: 94.7 us
  Pallas kernels  29.7 us (31%)
  starting transfers between devices  29.5 us (31%)
  waiting for transfers between devices  29.2 us (31%)
  other arithmetic  2.91 us (3%)
  local copies, waits for them, and re-layouts  2.12 us (2%)
  between operations  1.27 us (1%)
    pallas_call x11, Pallas kernels, run(): pl.pallas_call(kernel, out_shape=outs, in_specs=[vmem if s is None else p...  29.7 us
    ppermute x15, waiting for transfers between devices, flip_bit(): return lax.ppermute(value, both, [(i, i ^ flip) for i in range(total)])  19.1 us
    ppermute x15, starting transfers between devices, flip_bit(): return lax.ppermute(value, both, [(i, i ^ flip) for i in range(total)])  16.3 us
    ppermute x6, starting transfers between devices, to_twin(): lax.ppermute(edge, axis, [(i, i ^ 1) for i in range(count) if i ^ 1 < cou...  7.18 us
    ppermute x6, waiting for transfers between devices, to_twin(): lax.ppermute(edge, axis, [(i, i ^ 1) for i in range(count) if i ^ 1 < cou...  6.68 us
    ppermute x6, starting transfers between devices, to_other(): return lax.ppermute(edge, ('rows', 'cols'), pairs)  6.08 us
    ppermute x6, waiting for transfers between devices, to_other(): return lax.ppermute(edge, ('rows', 'cols'), pairs)  3.4 us
  transfers between devices with their start and end apart: 27, of which 12 were waited for; matrix products, arithmetic and copies ran while one was open for 3% of the time, Pallas kernels for 14%

profile of v14, /device:TPU:0, one launch (start us, length us, event | category | flops | bytes accessed | tf_op | source)
XLA Modules:
  0.0 94.7 jit_solution(3966563435178467321)
XLA Ops:
  0.7 0.9 copy-done.3
  2.3 3.0 %collective-permute-start = (bf16[6,16,384]{2,1,0:T(8,128)(2,1)S(1)}, bf16[6,16,384]{2,1,0:T(8,128)(2,1)S(1)}, u32[]{:S(2)}, u32[]{:S(2)}) collective-permute-start(bf16[6,16,384]{2,1,0:T(8,128)(2,1)S(1)} %get-tuple-element.128), channel_id=1, source_target_pairs={{0,4},{4,0},{8,12},{12,8},{16,20},{20,16},{24,28},{28,24},{1,5},{5... | collective-permute-start | bytes 221192 | tf_op jit(solution)/shard_map/ppermute | solution.py:392
  5.3 3.4 %collective-permute-done = bf16[6,16,384]{2,1,0:T(8,128)(2,1)S(1)} collective-permute-done((bf16[6,16,384]{2,1,0:T(8,128)(2,1)S(1)}, bf16[6,16,384]{2,1,0:T(8,128)(2,1)S(1)}, u32[]{:S(2)}, u32[]{:S(2)}) %collective-permute-start) | collective-permute-done | bytes 73760 | tf_op jit(solution)/shard_map/ppermute | solution.py:392
  8.9 2.5 %collective-permute-start.3 = (bf16[28,6,384]{2,1,0:T(8,128)(2,1)S(1)}, bf16[28,6,384]{2,1,0:T(8,128)(2,1)S(1)}, u32[]{:S(2)}, u32[]{:S(2)}) collective-permute-start(bf16[28,6,384]{2,1,0:T(8,128)(2,1)S(1)} %get-tuple-element.255), channel_id=1, source_target_pairs={{0,4},{1,2},{2,1},{3,7},{4,0},{5,6},{6,5},{7,3},{8,12},{9,10},{10,... | collective-permute-start | bytes 387080 | tf_op jit(solution)/shard_map/ppermute | solution.py:408
  11.4 3.4 %collective-permute-done.3 = bf16[28,6,384]{2,1,0:T(8,128)(2,1)S(1)} collective-permute-done((bf16[28,6,384]{2,1,0:T(8,128)(2,1)S(1)}, bf16[28,6,384]{2,1,0:T(8,128)(2,1)S(1)}, u32[]{:S(2)}, u32[]{:S(2)}) %collective-permute-start.3) | collective-permute-done | bytes 129056 | tf_op jit(solution)/shard_map/ppermute | solution.py:408
  15.2 8.1 %forward.1 = (f32[3,22,24,128]{3,2,1,0:T(8,128)S(1)}, f32[3,16,16,128]{3,2,1,0:T(8,128)S(1)}) custom-call(s32[6]{0:T(128)S(1)} %stack.29.place, bf16[28,32,384]{2,1,0:T(8,128)(2,1)S(1)} %fusion.12.xpad, f32[49,2,384]{2,1,0:T(2,128)S(1)} %bitcast.96, f32[2,384]{1,0:T(2,128)S(1)} %copy-done.5, f32[2,384]{1,0:T(2,128)S(1)} %copy-done.6, ...), custom_call_target="tpu_custom_call" | custom-call | tf_op jit(solution)/shard_map/forward/pallas_call | solution.py:370
  23.4 4.5 %top.1 = (bf16[256,384]{1,0:T(8,128)(2,1)S(1)}, bf16[256,384]{1,0:T(8,128)(2,1)S(1)}, bf16[256,1536]{1,0:T(8,128)(2,1)S(1)}, bf16[256,1536]{1,0:T(8,128)(2,1)S(1...) custom-call(f32[3,22,24,128]{3,2,1,0:T(8,128)S(1)} %get-tuple-element.133.mids, ...), custom_call_target="tpu_custom_call" | custom-call | tf_op jit(solution)/shard_map/top/pallas_call | solution.py:370
  27.9 1.6 %weights_top.1 = (bf16[2,768,384]{2,1,0:T(8,128)(2,1)S(1)}, bf16[2,768,384]{2,1,0:T(8,128)(2,1)S(1)}) custom-call(s32[6]{0:T(128)S(1)} %stack.29.place, bf16[256,384]{1,0:T(8,128)(2,1)S(1)} %get-tuple-element.141.normed, bf16[256,1536]{1,0:T(8,128)(2,1)S(1)} %get-tuple-element.142.act, bf16[256,1536]{1,0:T(8,128)(2,1)S(1)} %get-tuple-element.143.gpre, ...), custom_call_target="tpu_custom_call" | custom-call | tf_op jit(solution)/shard_map/weights_top/pallas_call | solution.py:370
  29.6 2.1 %collective-permute-start.4 = (bf16[3,16,384]{2,1,0:T(8,128)(2,1)S(1)}, bf16[3,16,384]{2,1,0:T(8,128)(2,1)S(1)}, u32[]{:S(2)}, u32[]{:S(2)}) collective-permute-start(bf16[3,16,384]{2,1,0:T(8,128)(2,1)S(1)} %bitcast.143), channel_id=1, source_target_pairs={{0,4},{4,0},{8,12},{12,8},{16,20},{20,16},{24,28},{28,24},{1,5},{5... | collective-permute-start | bytes 110600 | tf_op jit(solution)/shard_map/ppermute | solution.py:392
  31.9 1.5 %top_taps.1.sums1 = f32[56,384]{1,0:T(8,128)S(1)} custom-call(f32[3,22,24,128]{3,2,1,0:T(8,128)S(1)} %get-tuple-element.133.mids, bf16[256,384]{1,0:T(8,128)(2,1)S(1)} %get-tuple-element.134.dz, f32[1,1536]{1,0:T(1,128)S(1)} %get-tuple-element.135.db, f32[1,384]{1,0:T(1,128)S(1)} %get-tuple-element.136.dgain, f32[1,384]{1,0:T(1,128)S(1)} %get-tuple-element.137.dshift), custom_call_target="tpu_custom_call" | custom-call | tf_op jit(solution)/shard_map/top_taps/pallas_call | solution.py:370
  34.0 3.0 %collective-permute-start.7 = (bf16[22,3,384]{2,1,0:T(4,128)(2,1)S(1)}, bf16[22,3,384]{2,1,0:T(4,128)(2,1)S(1)}, u32[]{:S(2)}, u32[]{:S(2)}) collective-permute-start(bf16[22,3,384]{2,1,0:T(4,128)(2,1)S(1)} %get-tuple-element.271), channel_id=1, source_target_pairs={{0,4},{1,2},{2,1},{3,7},{4,0},{5,6},{6,5},{7,3},{8,12},{9,10},{10,... | collective-permute-start | bytes 152072 | tf_op jit(solution)/shard_map/ppermute | solution.py:408
  37.6 1.1 %collective-permute-start.10 = (bf16[1,4,2,48,384]{4,3,2,1,0:T(8,128)(2,1)S(1)}, bf16[1,4,2,48,384]{4,3,2,1,0:T(8,128)(2,1)S(1)}, u32[]{:S(2)}, u32[]{:S(2)}) collective-permute-start(bf16[1,4,2,48,384]{4,3,2,1,0:T(8,128)(2,1)S(1)} %get-tuple-element.249), channel_id=1, source_target_pairs={{0,4},{1,5},{2,6},{3,7},{4,0},{5,1},{6,2},{7,3},{8,12},{9,13},{10,... | collective-permute-start | bytes 884744 | tf_op jit(solution)/shard_map/ppermute | solution.py:422
  39.1 2.5 %again.1 = (f32[256,384]{1,0:T(8,128)S(1)}, f32[256,128]{1,0:T(8,128)S(1)}, bf16[256,384]{1,0:T(8,128)(2,1)S(1)}, bf16[256,1536]{1,0:T(8,128)(2,1)S(1)}, f32[256,1536]{1,0:T(8,128)S(1)}) custom-call(f32[3,16,16,128]{3,2,1,0:T(8,128)S(1)} %get-tuple-element.147.z0, f32[2,384]{1,0:T(2,128)S(1)} %copy-done.5, f32[2,384]{1,0:T(2,128)S(1)} %copy-done.6, ...), custom_call_target="tpu_custom_call" | custom-call | tf_op jit(solution)/shard_map/again/pallas_call | solution.py:370
  42.0 4.2 %low.1 = (bf16[256,384]{1,0:T(8,128)(2,1)S(1)}, bf16[256,384]{1,0:T(8,128)(2,1)S(1)}, f32[1,1536]{1,0:T(1,128)S(1)}, f32[1,384]{1,0:T(1,128)S(1)}, f32[1,384]{1,...) custom-call(s32[6]{0:T(128)S(1)} %stack.29.place, ...), custom_call_target="tpu_custom_call" | custom-call | tf_op jit(solution)/shard_map/low/pallas_call | solution.py:370
  46.2 0.8 collective-permute-done.10
  47.4 2.1 %taps.1 = (bf16[56,384]{1,0:T(8,128)(2,1)S(1)}, bf16[56,384]{1,0:T(8,128)(2,1)S(1)}) custom-call(s32[6]{0:T(128)S(1)} %stack.29.place, bf16[28,32,384]{2,1,0:T(8,128)(2,1)S(1)} %fusion.12.xpad, bf16[256,384]{1,0:T(8,128)(2,1)S(1)} %get-tuple-element.190.dz, f32[1,1536]{1,0:T(1,128)S(1)} %get-tuple-element.176.db, f32[1,384]{1,0:T(1,128)S(1)} %get-tuple-element.177.dgain, ...), custom_call_target="tpu_custom_call" | custom-call | tf_op jit(solution)/shard_map/taps/pallas_call | solution.py:370
  50.4 3.0 %collective-permute-start.15 = (bf16[384,384]{1,0:T(8,128)(2,1)S(1)}, bf16[384,384]{1,0:T(8,128)(2,1)S(1)}, u32[]{:S(2)}, u32[]{:S(2)}) collective-permute-start(bf16[384,384]{1,0:T(8,128)(2,1)S(1)} %pad_maximum_fusion.1), channel_id=1, source_target_pairs={{0,8},{1,9},{2,10},{3,11},{4,12},{5,13},{6,14},{7,15},{8,0},{9,1},... | collective-permute-start | bytes 884744 | tf_op jit(solution)/shard_map/ppermute | solution.py:422
  54.4 1.3 %collective-permute-start.14 = (bf16[1,4,2,48,384]{4,3,2,1,0:T(8,128)(2,1)S(1)}, bf16[1,4,2,48,384]{4,3,2,1,0:T(8,128)(2,1)S(1)}, u32[]{:S(2)}, u32[]{:S(2)}) collective-permute-start(bf16[1,4,2,48,384]{4,3,2,1,0:T(8,128)(2,1)S(1)} %get-tuple-element.245), channel_id=1, source_target_pairs={{0,4},{1,5},{2,6},{3,7},{4,0},{5,1},{6,2},{7,3},{8,12},{9,13},{10,... | collective-permute-start | bytes 884744 | tf_op jit(solution)/shard_map/ppermute | solution.py:422
  55.7 1.8 %collective-permute-start.13 = (bf16[1,8,1,48,384]{4,3,1,2,0:T(8,128)(2,1)S(1)}, bf16[1,8,1,48,384]{4,3,1,2,0:T(8,128)(2,1)S(1)}, u32[]{:S(2)}, u32[]{:S(2)}) collective-permute-start(bf16[1,8,1,48,384]{4,3,1,2,0:T(8,128)(2,1)S(1)} %get-tuple-element.247), channel_id=1, source_target_pairs={{0,2},{1,3},{2,0},{3,1},{4,6},{5,7},{6,4},{7,5},{8,10},{9,11},{10,... | collective-permute-start | bytes 884744 | tf_op jit(solution)/shard_map/ppermute | solution.py:422
  58.3 2.3 %collective-permute-done.15 = bf16[384,384]{1,0:T(8,128)(2,1)S(1)} collective-permute-done((bf16[384,384]{1,0:T(8,128)(2,1)S(1)}, bf16[384,384]{1,0:T(8,128)(2,1)S(1)}, u32[]{:S(2)}, u32[]{:S(2)}) %collective-permute-start.15) | collective-permute-done | bytes 294944 | tf_op jit(solution)/shard_map/ppermute | solution.py:422
  60.7 2.9 %collective-permute-done.16 = bf16[3,16,384]{2,1,0:T(8,128)(2,1)S(1)} collective-permute-done((bf16[3,16,384]{2,1,0:T(8,128)(2,1)S(1)}, bf16[3,16,384]{2,1,0:T(8,128)(2,1)S(1)}, u32[]{:S(2)}, u32[]{:S(2)}) %collective-permute-start.16) | collective-permute-done | bytes 36896 | tf_op jit(solution)/shard_map/ppermute | solution.py:392
  63.6 0.8 collective-permute-done.13
  64.7 2.5 %collective-permute-start.19 = (bf16[344,384]{1,0:T(8,128)(2,1)S(1)}, bf16[344,384]{1,0:T(8,128)(2,1)S(1)}, u32[]{:S(2)}, u32[]{:S(2)}) collective-permute-start(bf16[344,384]{1,0:T(8,128)(2,1)S(1)} %pad_maximum_fusion.4), channel_id=1, source_target_pairs={{0,4},{1,5},{2,6},{3,7},{4,0},{5,1},{6,2},{7,3},{8,12},{9,13},{10,... | collective-permute-start | bytes 792584 | tf_op jit(solution)/shard_map/ppermute | solution.py:422
  68.5 1.3 %collective-permute-start.21 = (bf16[22,3,384]{2,1,0:T(4,128)(2,1)S(1)}, bf16[22,3,384]{2,1,0:T(4,128)(2,1)S(1)}, u32[]{:S(2)}, u32[]{:S(2)}) collective-permute-start(bf16[22,3,384]{2,1,0:T(4,128)(2,1)S(1)} %get-tuple-element.270), channel_id=1, source_target_pairs={{0,1},{1,0},{2,3},{3,2},{4,5},{5,4},{6,7},{7,6},{8,9},{9,8},{10,11... | collective-permute-start | bytes 152072 | tf_op jit(solution)/shard_map/ppermute | solution.py:392
  69.8 3.6 %collective-permute-done.20 = bf16[288,384]{1,0:T(8,128)(2,1)S(1)} collective-permute-done((bf16[288,384]{1,0:T(8,128)(2,1)S(1)}, bf16[288,384]{1,0:T(8,128)(2,1)S(1)}, u32[]{:S(2)}, u32[]{:S(2)}) %collective-permute-start.20) | collective-permute-done | bytes 221216 | tf_op jit(solution)/shard_map/ppermute | solution.py:422
  73.6 2.8 %collective-permute-start.24 = (bf16[96,384]{1,0:T(8,128)(2,1)S(1)}, bf16[96,384]{1,0:T(8,128)(2,1)S(1)}, u32[]{:S(2)}, u32[]{:S(2)}) collective-permute-start(bf16[96,384]{1,0:T(8,128)(2,1)S(1)} %bitcast.139), channel_id=1, source_target_pairs={{0,16},{1,17},{2,18},{3,19},{4,20},{5,21},{6,22},{7,23},{8,24},{9,... | collective-permute-start | bytes 221192 | tf_op jit(solution)/shard_map/ppermute | solution.py:422
  77.5 2.5 %last.1 = bf16[256,384]{1,0:T(8,128)(2,1)} custom-call(bf16[22,32,384]{2,1,0:T(8,128)(2,1)S(1)} %fusion.18.dzpad, bf16[256,384]{1,0:T(8,128)(2,1)S(1)} %get-tuple-element.221.gmid, f32[49,2,384]{2,1,0:T(2,128)S(1)} %bitcast.99), custom_call_target="tpu_custom_call" | custom-call | tf_op jit(solution)/shard_map/last/pallas_call | solution.py:370
  80.0 3.9 %collective-permute-done.23 = bf16[248,384]{1,0:T(8,128)(2,1)S(1)} collective-permute-done((bf16[248,384]{1,0:T(8,128)(2,1)S(1)}, bf16[248,384]{1,0:T(8,128)(2,1)S(1)}, u32[]{:S(2)}, u32[]{:S(2)}) %collective-permute-start.23) | collective-permute-done | bytes 190496 | tf_op jit(solution)/shard_map/ppermute | solution.py:422
  84.1 1.2 %collective-permute-start.25 = (bf16[152,384]{1,0:T(8,128)(2,1)S(1)}, bf16[152,384]{1,0:T(8,128)(2,1)S(1)}, u32[]{:S(2)}, u32[]{:S(2)}) collective-permute-start(bf16[152,384]{1,0:T(8,128)(2,1)S(1)} %pad_maximum_fusion.7), channel_id=1, source_target_pairs={{0,16},{1,17},{2,18},{3,19},{4,20},{5,21},{6,22},{7,23},{8,24},{9,... | collective-permute-start | bytes 350216 | tf_op jit(solution)/shard_map/ppermute | solution.py:422
  85.3 6.8 %collective-permute-done.25 = bf16[152,384]{1,0:T(8,128)(2,1)S(1)} collective-permute-done((bf16[152,384]{1,0:T(8,128)(2,1)S(1)}, bf16[152,384]{1,0:T(8,128)(2,1)S(1)}, u32[]{:S(2)}, u32[]{:S(2)}) %collective-permute-start.25) | collective-permute-done | bytes 116768 | tf_op jit(solution)/shard_map/ppermute | solution.py:422
  92.2 0.7 weights.1
  93.4 1.3 %small.1 = (f32[49,2,384]{2,1,0:T(2,128)}, f32[2,384]{1,0:T(2,128)}, f32[2,384]{1,0:T(2,128)}, f32[2,1536]{1,0:T(2,128)}) custom-call(s32[6]{0:T(128)S(1)} %stack.29.place, bf16[56,384]{1,0:T(8,128)(2,1)S(1)} %add_convert_fusion.13.mine, bf16[56,384]{1,0:T(8,128)(2,1)S(1)} %collective-permute-done.26.got), custom_call_target="tpu_custom_call" | custom-call | tf_op jit(solution)/shard_map/small/pallas_call | solution.py:370
  (113 shorter events, 9.8 us)
Async XLA Ops:
  2.3 6.4 %collective-permute-start = (bf16[6,16,384]{2,1,0:T(8,128)(2,1)S(1)}, bf16[6,16,384]{2,1,0:T(8,128)(2,1)S(1)}, u32[]{:S(2)}, u32[]{:S(2)}) collective-permute-start(bf16[6,16,384]{2,1,0:T(8,128)(2,1)S(1)} %get-tuple-element.128), channel_id=1, source_target_pairs={{0,4},{4,0},{8,12},{12,8},{16,20},{20,16},{24,28},{28,24},{1,5},{5... | collective-permute-start | bytes 221192 | tf_op jit(solution)/shard_map/ppermute | solution.py:392
  5.3 3.4 %collective-permute-start.1 = (bf16[6,16,384]{2,1,0:T(8,128)(2,1)S(1)}, bf16[6,16,384]{2,1,0:T(8,128)(2,1)S(1)}, u32[]{:S(2)}, u32[]{:S(2)}) collective-permute-start(bf16[6,16,384]{2,1,0:T(8,128)(2,1)S(1)} %get-tuple-element.130), channel_id=1, source_target_pairs={{0,1},{1,0},{2,3},{3,2},{4,8},{5,9},{6,10},{7,11},{8,4},{9,5},{10,... | collective-permute-start | bytes 221192 | tf_op jit(solution)/shard_map/ppermute | solution.py:408
  8.8 6.3 %copy-start.1 = (f32[2,7,7,384]{3,0,2,1:T(2,128)S(1)}, f32[2,7,7,384]{3,0,2,1:T(2,128)}, u32[]{:S(2)}) copy-start(f32[2,7,7,384]{3,0,2,1:T(2,128)} %param.10) | copy-start | bytes 451588
  8.9 6.3 %copy-start.4 = (f32[2,1536]{1,0:T(2,128)S(1)}, f32[2,1536]{1,0:T(2,128)}, u32[]{:S(2)}) copy-start(f32[2,1536]{1,0:T(2,128)} %b_in.5) | copy-start | bytes 36868
  8.9 6.3 %copy-start.5 = (f32[2,384]{1,0:T(2,128)S(1)}, f32[2,384]{1,0:T(2,128)}, u32[]{:S(2)}) copy-start(f32[2,384]{1,0:T(2,128)} %gains.7) | copy-start | bytes 9220
  8.9 6.3 %copy-start.6 = (f32[2,384]{1,0:T(2,128)S(1)}, f32[2,384]{1,0:T(2,128)}, u32[]{:S(2)}) copy-start(f32[2,384]{1,0:T(2,128)} %shifts.5) | copy-start | bytes 9220
  8.9 5.9 %collective-permute-start.3 = (bf16[28,6,384]{2,1,0:T(8,128)(2,1)S(1)}, bf16[28,6,384]{2,1,0:T(8,128)(2,1)S(1)}, u32[]{:S(2)}, u32[]{:S(2)}) collective-permute-start(bf16[28,6,384]{2,1,0:T(8,128)(2,1)S(1)} %get-tuple-element.255), channel_id=1, source_target_pairs={{0,4},{1,2},{2,1},{3,7},{4,0},{5,6},{6,5},{7,3},{8,12},{9,10},{10,... | collective-permute-start | bytes 387080 | tf_op jit(solution)/shard_map/ppermute | solution.py:408
  11.4 3.4 %collective-permute-start.2 = (bf16[28,6,384]{2,1,0:T(8,128)(2,1)S(1)}, bf16[28,6,384]{2,1,0:T(8,128)(2,1)S(1)}, u32[]{:S(2)}, u32[]{:S(2)}) collective-permute-start(bf16[28,6,384]{2,1,0:T(8,128)(2,1)S(1)} %get-tuple-element.256), channel_id=1, source_target_pairs={{0,1},{1,0},{2,3},{3,2},{4,5},{5,4},{6,7},{7,6},{8,9},{9,8},{10,11... | collective-permute-start | bytes 387080 | tf_op jit(solution)/shard_map/ppermute | solution.py:392
  15.2 8.1 %copy-start.2 = (bf16[16,16,384]{2,1,0:T(8,128)(2,1)S(1)}, bf16[16,16,384]{2,1,0:T(8,128)(2,1)}, u32[]{:S(2)}) copy-start(bf16[16,16,384]{2,1,0:T(8,128)(2,1)} %param.9) | copy-start | bytes 589828
  29.5 7.5 %collective-permute-start.8 = (bf16[2,16,48,384]{3,2,1,0:T(8,128)(2,1)S(1)}, bf16[2,16,48,384]{3,2,1,0:T(8,128)(2,1)S(1)}, u32[]{:S(2)}, u32[]{:S(2)}) collective-permute-start(bf16[2,16,48,384]{3,2,1,0:T(8,128)(2,1)S(1)} %bitcast.112), channel_id=1, source_target_pairs={{0,1},{1,0},{2,3},{3,2},{4,5},{5,4},{6,7},{7,6},{8,9},{9,8},{10,11... | collective-permute-start | bytes 3538952 | tf_op jit(solution)/shard_map/ppermute | solution.py:422
  29.6 4.2 %collective-permute-start.4 = (bf16[3,16,384]{2,1,0:T(8,128)(2,1)S(1)}, bf16[3,16,384]{2,1,0:T(8,128)(2,1)S(1)}, u32[]{:S(2)}, u32[]{:S(2)}) collective-permute-start(bf16[3,16,384]{2,1,0:T(8,128)(2,1)S(1)} %bitcast.143), channel_id=1, source_target_pairs={{0,4},{4,0},{8,12},{12,8},{16,20},{20,16},{24,28},{28,24},{1,5},{5... | collective-permute-start | bytes 110600 | tf_op jit(solution)/shard_map/ppermute | solution.py:392
  31.7 2.1 %collective-permute-start.5 = (bf16[3,16,384]{2,1,0:T(8,128)(2,1)S(1)}, bf16[3,16,384]{2,1,0:T(8,128)(2,1)S(1)}, u32[]{:S(2)}, u32[]{:S(2)}) collective-permute-start(bf16[3,16,384]{2,1,0:T(8,128)(2,1)S(1)} %bitcast.141), channel_id=1, source_target_pairs={{0,1},{1,0},{2,3},{3,2},{4,8},{5,9},{6,10},{7,11},{8,4},{9,5},{10,... | collective-permute-start | bytes 110600 | tf_op jit(solution)/shard_map/ppermute | solution.py:408
  34.0 7.6 %collective-permute-start.7 = (bf16[22,3,384]{2,1,0:T(4,128)(2,1)S(1)}, bf16[22,3,384]{2,1,0:T(4,128)(2,1)S(1)}, u32[]{:S(2)}, u32[]{:S(2)}) collective-permute-start(bf16[22,3,384]{2,1,0:T(4,128)(2,1)S(1)} %get-tuple-element.271), channel_id=1, source_target_pairs={{0,4},{1,2},{2,1},{3,7},{4,0},{5,6},{6,5},{7,3},{8,12},{9,10},{10,... | collective-permute-start | bytes 152072 | tf_op jit(solution)/shard_map/ppermute | solution.py:408
  37.0 4.6 %collective-permute-start.6 = (bf16[22,3,384]{2,1,0:T(4,128)(2,1)S(1)}, bf16[22,3,384]{2,1,0:T(4,128)(2,1)S(1)}, u32[]{:S(2)}, u32[]{:S(2)}) collective-permute-start(bf16[22,3,384]{2,1,0:T(4,128)(2,1)S(1)} %get-tuple-element.272), channel_id=1, source_target_pairs={{0,1},{1,0},{2,3},{3,2},{4,5},{5,4},{6,7},{7,6},{8,9},{9,8},{10,11... | collective-permute-start | bytes 152072 | tf_op jit(solution)/shard_map/ppermute | solution.py:392
  37.6 9.5 %collective-permute-start.10 = (bf16[1,4,2,48,384]{4,3,2,1,0:T(8,128)(2,1)S(1)}, bf16[1,4,2,48,384]{4,3,2,1,0:T(8,128)(2,1)S(1)}, u32[]{:S(2)}, u32[]{:S(2)}) collective-permute-start(bf16[1,4,2,48,384]{4,3,2,1,0:T(8,128)(2,1)S(1)} %get-tuple-element.249), channel_id=1, source_target_pairs={{0,4},{1,5},{2,6},{3,7},{4,0},{5,1},{6,2},{7,3},{8,12},{9,13},{10,... | collective-permute-start | bytes 884744 | tf_op jit(solution)/shard_map/ppermute | solution.py:422
  38.7 8.7 %collective-permute-start.9 = (bf16[1,8,1,48,384]{4,3,1,2,0:T(8,128)(2,1)S(1)}, bf16[1,8,1,48,384]{4,3,1,2,0:T(8,128)(2,1)S(1)}, u32[]{:S(2)}, u32[]{:S(2)}) collective-permute-start(bf16[1,8,1,48,384]{4,3,1,2,0:T(8,128)(2,1)S(1)} %get-tuple-element.251), channel_id=1, source_target_pairs={{0,2},{1,3},{2,0},{3,1},{4,6},{5,7},{6,4},{7,5},{8,10},{9,11},{10,... | collective-permute-start | bytes 884744 | tf_op jit(solution)/shard_map/ppermute | solution.py:422
  47.4 6.0 %collective-permute-start.11 = (bf16[2,16,48,384]{3,2,1,0:T(8,128)(2,1)S(1)}, bf16[2,16,48,384]{3,2,1,0:T(8,128)(2,1)S(1)}, u32[]{:S(2)}, u32[]{:S(2)}) collective-permute-start(bf16[2,16,48,384]{3,2,1,0:T(8,128)(2,1)S(1)} %bitcast.111), channel_id=1, source_target_pairs={{0,1},{1,0},{2,3},{3,2},{4,5},{5,4},{6,7},{7,6},{8,9},{9,8},{10,11... | collective-permute-start | bytes 3538952 | tf_op jit(solution)/shard_map/ppermute | solution.py:422
  49.6 3.9 %collective-permute-start.12 = (bf16[56,384]{1,0:T(8,128)(2,1)S(1)}, bf16[56,384]{1,0:T(8,128)(2,1)S(1)}, u32[]{:S(2)}, u32[]{:S(2)}) collective-permute-start(bf16[56,384]{1,0:T(8,128)(2,1)S(1)} %get-tuple-element.181), channel_id=1, source_target_pairs={{0,1},{1,0},{2,3},{3,2},{4,5},{5,4},{6,7},{7,6},{8,9},{9,8},{10,11... | collective-permute-start | bytes 129032 | tf_op jit(solution)/shard_map/ppermute | solution.py:422
  50.4 10.2 %collective-permute-start.15 = (bf16[384,384]{1,0:T(8,128)(2,1)S(1)}, bf16[384,384]{1,0:T(8,128)(2,1)S(1)}, u32[]{:S(2)}, u32[]{:S(2)}) collective-permute-start(bf16[384,384]{1,0:T(8,128)(2,1)S(1)} %pad_maximum_fusion.1), channel_id=1, source_target_pairs={{0,8},{1,9},{2,10},{3,11},{4,12},{5,13},{6,14},{7,15},{8,0},{9,1},... | collective-permute-start | bytes 884744 | tf_op jit(solution)/shard_map/ppermute | solution.py:422
  54.0 9.6 %collective-permute-start.18 = (bf16[56,384]{1,0:T(8,128)(2,1)S(1)}, bf16[56,384]{1,0:T(8,128)(2,1)S(1)}, u32[]{:S(2)}, u32[]{:S(2)}) collective-permute-start(bf16[56,384]{1,0:T(8,128)(2,1)S(1)} %add_convert_fusion.17), channel_id=1, source_target_pairs={{0,2},{1,3},{2,0},{3,1},{4,6},{5,7},{6,4},{7,5},{8,10},{9,11},{10,... | collective-permute-start | bytes 129032 | tf_op jit(solution)/shard_map/ppermute | solution.py:422
  54.4 9.2 %collective-permute-start.14 = (bf16[1,4,2,48,384]{4,3,2,1,0:T(8,128)(2,1)S(1)}, bf16[1,4,2,48,384]{4,3,2,1,0:T(8,128)(2,1)S(1)}, u32[]{:S(2)}, u32[]{:S(2)}) collective-permute-start(bf16[1,4,2,48,384]{4,3,2,1,0:T(8,128)(2,1)S(1)} %get-tuple-element.245), channel_id=1, source_target_pairs={{0,4},{1,5},{2,6},{3,7},{4,0},{5,1},{6,2},{7,3},{8,12},{9,13},{10,... | collective-permute-start | bytes 884744 | tf_op jit(solution)/shard_map/ppermute | solution.py:422
  55.7 8.6 %collective-permute-start.13 = (bf16[1,8,1,48,384]{4,3,1,2,0:T(8,128)(2,1)S(1)}, bf16[1,8,1,48,384]{4,3,1,2,0:T(8,128)(2,1)S(1)}, u32[]{:S(2)}, u32[]{:S(2)}) collective-permute-start(bf16[1,8,1,48,384]{4,3,1,2,0:T(8,128)(2,1)S(1)} %get-tuple-element.247), channel_id=1, source_target_pairs={{0,2},{1,3},{2,0},{3,1},{4,6},{5,7},{6,4},{7,5},{8,10},{9,11},{10,... | collective-permute-start | bytes 884744 | tf_op jit(solution)/shard_map/ppermute | solution.py:422
  57.6 6.0 %collective-permute-start.16 = (bf16[3,16,384]{2,1,0:T(8,128)(2,1)S(1)}, bf16[3,16,384]{2,1,0:T(8,128)(2,1)S(1)}, u32[]{:S(2)}, u32[]{:S(2)}) collective-permute-start(bf16[3,16,384]{2,1,0:T(8,128)(2,1)S(1)} %bitcast.142), channel_id=1, source_target_pairs={{0,4},{4,0},{8,12},{12,8},{16,20},{20,16},{24,28},{28,24},{1,5},{5... | collective-permute-start | bytes 110600 | tf_op jit(solution)/shard_map/ppermute | solution.py:392
  60.6 3.0 %collective-permute-start.17 = (bf16[3,16,384]{2,1,0:T(8,128)(2,1)S(1)}, bf16[3,16,384]{2,1,0:T(8,128)(2,1)S(1)}, u32[]{:S(2)}, u32[]{:S(2)}) collective-permute-start(bf16[3,16,384]{2,1,0:T(8,128)(2,1)S(1)} %bitcast.140), channel_id=1, source_target_pairs={{0,1},{1,0},{2,3},{3,2},{4,8},{5,9},{6,10},{7,11},{8,4},{9,5},{10,... | collective-permute-start | bytes 110600 | tf_op jit(solution)/shard_map/ppermute | solution.py:408
  64.7 8.7 %collective-permute-start.19 = (bf16[344,384]{1,0:T(8,128)(2,1)S(1)}, bf16[344,384]{1,0:T(8,128)(2,1)S(1)}, u32[]{:S(2)}, u32[]{:S(2)}) collective-permute-start(bf16[344,384]{1,0:T(8,128)(2,1)S(1)} %pad_maximum_fusion.4), channel_id=1, source_target_pairs={{0,4},{1,5},{2,6},{3,7},{4,0},{5,1},{6,2},{7,3},{8,12},{9,13},{10,... | collective-permute-start | bytes 792584 | tf_op jit(solution)/shard_map/ppermute | solution.py:422
  67.4 6.0 %collective-permute-start.20 = (bf16[288,384]{1,0:T(8,128)(2,1)S(1)}, bf16[288,384]{1,0:T(8,128)(2,1)S(1)}, u32[]{:S(2)}, u32[]{:S(2)}) collective-permute-start(bf16[288,384]{1,0:T(8,128)(2,1)S(1)} %pad_maximum_fusion.5), channel_id=1, source_target_pairs={{0,2},{1,3},{2,0},{3,1},{4,6},{5,7},{6,4},{7,5},{8,10},{9,11},{10,... | collective-permute-start | bytes 663560 | tf_op jit(solution)/shard_map/ppermute | solution.py:422
  68.2 5.3 %collective-permute-start.22 = (bf16[22,3,384]{2,1,0:T(4,128)(2,1)S(1)}, bf16[22,3,384]{2,1,0:T(4,128)(2,1)S(1)}, u32[]{:S(2)}, u32[]{:S(2)}) collective-permute-start(bf16[22,3,384]{2,1,0:T(4,128)(2,1)S(1)} %get-tuple-element.269), channel_id=1, source_target_pairs={{0,4},{1,2},{2,1},{3,7},{4,0},{5,6},{6,5},{7,3},{8,12},{9,10},{10,... | collective-permute-start | bytes 152072 | tf_op jit(solution)/shard_map/ppermute | solution.py:408
  68.5 5.0 %collective-permute-start.21 = (bf16[22,3,384]{2,1,0:T(4,128)(2,1)S(1)}, bf16[22,3,384]{2,1,0:T(4,128)(2,1)S(1)}, u32[]{:S(2)}, u32[]{:S(2)}) collective-permute-start(bf16[22,3,384]{2,1,0:T(4,128)(2,1)S(1)} %get-tuple-element.270), channel_id=1, source_target_pairs={{0,1},{1,0},{2,3},{3,2},{4,5},{5,4},{6,7},{7,6},{8,9},{9,8},{10,11... | collective-permute-start | bytes 152072 | tf_op jit(solution)/shard_map/ppermute | solution.py:392
  73.6 10.3 %collective-permute-start.24 = (bf16[96,384]{1,0:T(8,128)(2,1)S(1)}, bf16[96,384]{1,0:T(8,128)(2,1)S(1)}, u32[]{:S(2)}, u32[]{:S(2)}) collective-permute-start(bf16[96,384]{1,0:T(8,128)(2,1)S(1)} %bitcast.139), channel_id=1, source_target_pairs={{0,16},{1,17},{2,18},{3,19},{4,20},{5,21},{6,22},{7,23},{8,24},{9,... | collective-permute-start | bytes 221192 | tf_op jit(solution)/shard_map/ppermute | solution.py:422
  76.6 7.3 %collective-permute-start.23 = (bf16[248,384]{1,0:T(8,128)(2,1)S(1)}, bf16[248,384]{1,0:T(8,128)(2,1)S(1)}, u32[]{:S(2)}, u32[]{:S(2)}) collective-permute-start(bf16[248,384]{1,0:T(8,128)(2,1)S(1)} %pad_maximum_fusion.6), channel_id=1, source_target_pairs={{0,8},{1,9},{2,10},{3,11},{4,12},{5,13},{6,14},{7,15},{8,0},{9,1},... | collective-permute-start | bytes 571400 | tf_op jit(solution)/shard_map/ppermute | solution.py:422
  84.1 8.0 %collective-permute-start.25 = (bf16[152,384]{1,0:T(8,128)(2,1)S(1)}, bf16[152,384]{1,0:T(8,128)(2,1)S(1)}, u32[]{:S(2)}, u32[]{:S(2)}) collective-permute-start(bf16[152,384]{1,0:T(8,128)(2,1)S(1)} %pad_maximum_fusion.7), channel_id=1, source_target_pairs={{0,16},{1,17},{2,18},{3,19},{4,20},{5,21},{6,22},{7,23},{8,24},{9,... | collective-permute-start | bytes 350216 | tf_op jit(solution)/shard_map/ppermute | solution.py:422
  92.1 1.3 %collective-permute-start.26 = (bf16[56,384]{1,0:T(8,128)(2,1)S(1)}, bf16[56,384]{1,0:T(8,128)(2,1)S(1)}, u32[]{:S(2)}, u32[]{:S(2)}) collective-permute-start(bf16[56,384]{1,0:T(8,128)(2,1)S(1)} %add_convert_fusion.13.mine), channel_id=1, source_target_pairs={{0,1},{1,0},{2,3},{3,2},{4,5},{5,4},{6,7},{7,6},{8,9},{9,8},{10,11... | collective-permute-start | bytes 129032 | tf_op jit(solution)/shard_map/ppermute | solution.py:422
  (2 other events, 2.6 us)

commit v15 on v14

--- a/solution.py
+++ b/solution.py
@@ -599,20 +599,6 @@
         name="weights_top",
     )
     run1 = start(dw1)
-    small_f = shape(small_rows, channels)
-    (small1,) = run(
-        top_taps_kernel,
-        (small_f,),
-        [tile_z, shape(groups, 49, LANES)],
-        (mids, dz1, *small1),
-        name="top_taps",
-    )
-    tile1, twin, other, small1 = fenced(tile1, twin, other, small1)
-    wide1 = rimmed(tile1, twin, other, 0, odd_row, outer_row)
-    twin, other = edges(wide1, 1, HALO, odd_col)
-    twin, other = to_twin(twin, "cols"), to_other(other, "cols")
-    run1, z0 = fenced(run1, z0)
-    pair1 = fork(run1)
     tile_f = shape(pixels, channels)
     again = run(
         again_kernel,
@@ -623,7 +609,21 @@
         fetched=1,
         name="again",
     )
-    wide1, twin, other, again = fenced(wide1, twin, other, again)
+    tile1, twin, other, again = fenced(tile1, twin, other, again)
+    wide1 = rimmed(tile1, twin, other, 0, odd_row, outer_row)
+    twin, other = edges(wide1, 1, HALO, odd_col)
+    twin, other = to_twin(twin, "cols"), to_other(other, "cols")
+    run1, mids = fenced(run1, mids)
+    pair1 = fork(run1)
+    small_f = shape(small_rows, channels)
+    (small1,) = run(
+        top_taps_kernel,
+        (small_f,),
+        [tile_z, shape(groups, 49, LANES)],
+        (mids, dz1, *small1),
+        name="top_taps",
+    )
+    wide1, twin, other, small1 = fenced(wide1, twin, other, small1)
     dzpad1 = filled(rimmed(wide1, twin, other, 1, odd_col, outer_col))
     spread_scratch = [shape(groups, *dzpad1.shape[:2], LANES), tile_z]
     grad_mid, dz0, *rest = run(

time: 94.9 us -> 94.7 us (level)
  transfers between devices with their start and end apart: 27 -> 27, of which waited for: 12 -> 11; matrix products, arithmetic and copies ran while one was open for 3% -> 3% of each run, Pallas kernels for 14% -> 14%
where the time goes in v15:
time: 94.7 us; the launch traced here: 94.6 us
  Pallas kernels  29.7 us (31%)
  starting transfers between devices  29.5 us (31%)
  waiting for transfers between devices  29.2 us (31%)
  other arithmetic  2.93 us (3%)
  local copies, waits for them, and re-layouts  1.92 us (2%)
  between operations  1.3 us (1%)
    pallas_call x11, Pallas kernels, run(): pl.pallas_call(kernel, out_shape=outs, in_specs=[vmem if s is None else p...  29.7 us
    ppermute x15, waiting for transfers between devices, flip_bit(): return lax.ppermute(value, both, [(i, i ^ flip) for i in range(total)])  19.6 us
    ppermute x15, starting transfers between devices, flip_bit(): return lax.ppermute(value, both, [(i, i ^ flip) for i in range(total)])  16.3 us
    ppermute x6, starting transfers between devices, to_twin(): lax.ppermute(edge, axis, [(i, i ^ 1) for i in range(count) if i ^ 1 < cou...  7.16 us
    ppermute x6, waiting for transfers between devices, to_twin(): lax.ppermute(edge, axis, [(i, i ^ 1) for i in range(count) if i ^ 1 < cou...  6.28 us
    ppermute x6, starting transfers between devices, to_other(): return lax.ppermute(edge, ('rows', 'cols'), pairs)  6.07 us
    ppermute x6, waiting for transfers between devices, to_other(): return lax.ppermute(edge, ('rows', 'cols'), pairs)  3.4 us
  transfers between devices with their start and end apart: 27, of which 11 were waited for; matrix products, arithmetic and copies ran while one was open for 3% of the time, Pallas kernels for 14%

profile of v15, /device:TPU:0, one launch (start us, length us, event | category | flops | bytes accessed | tf_op | source)
XLA Modules:
  0.0 94.6 jit_solution(5408926761228470939)
XLA Ops:
  0.7 0.9 copy-done.3
  2.3 3.0 %collective-permute-start = (bf16[6,16,384]{2,1,0:T(8,128)(2,1)S(1)}, bf16[6,16,384]{2,1,0:T(8,128)(2,1)S(1)}, u32[]{:S(2)}, u32[]{:S(2)}) collective-permute-start(bf16[6,16,384]{2,1,0:T(8,128)(2,1)S(1)} %get-tuple-element.128), channel_id=1, source_target_pairs={{0,4},{4,0},{8,12},{12,8},{16,20},{20,16},{24,28},{28,24},{1,5},{5... | collective-permute-start | bytes 221192 | tf_op jit(solution)/shard_map/ppermute | solution.py:392
  5.3 3.4 %collective-permute-done = bf16[6,16,384]{2,1,0:T(8,128)(2,1)S(1)} collective-permute-done((bf16[6,16,384]{2,1,0:T(8,128)(2,1)S(1)}, bf16[6,16,384]{2,1,0:T(8,128)(2,1)S(1)}, u32[]{:S(2)}, u32[]{:S(2)}) %collective-permute-start) | collective-permute-done | bytes 73760 | tf_op jit(solution)/shard_map/ppermute | solution.py:392
  8.9 2.5 %collective-permute-start.3 = (bf16[28,6,384]{2,1,0:T(8,128)(2,1)S(1)}, bf16[28,6,384]{2,1,0:T(8,128)(2,1)S(1)}, u32[]{:S(2)}, u32[]{:S(2)}) collective-permute-start(bf16[28,6,384]{2,1,0:T(8,128)(2,1)S(1)} %get-tuple-element.255), channel_id=1, source_target_pairs={{0,4},{1,2},{2,1},{3,7},{4,0},{5,6},{6,5},{7,3},{8,12},{9,10},{10,... | collective-permute-start | bytes 387080 | tf_op jit(solution)/shard_map/ppermute | solution.py:408
  11.4 3.4 %collective-permute-done.3 = bf16[28,6,384]{2,1,0:T(8,128)(2,1)S(1)} collective-permute-done((bf16[28,6,384]{2,1,0:T(8,128)(2,1)S(1)}, bf16[28,6,384]{2,1,0:T(8,128)(2,1)S(1)}, u32[]{:S(2)}, u32[]{:S(2)}) %collective-permute-start.3) | collective-permute-done | bytes 129056 | tf_op jit(solution)/shard_map/ppermute | solution.py:408
  15.2 8.0 %forward.1 = (f32[3,22,24,128]{3,2,1,0:T(8,128)S(1)}, f32[3,16,16,128]{3,2,1,0:T(8,128)S(1)}) custom-call(s32[6]{0:T(128)S(1)} %stack.29.place, bf16[28,32,384]{2,1,0:T(8,128)(2,1)S(1)} %fusion.12.xpad, f32[49,2,384]{2,1,0:T(2,128)S(1)} %bitcast.96, f32[2,384]{1,0:T(2,128)S(1)} %copy-done.5, f32[2,384]{1,0:T(2,128)S(1)} %copy-done.6, ...), custom_call_target="tpu_custom_call" | custom-call | tf_op jit(solution)/shard_map/forward/pallas_call | solution.py:370
  23.3 4.6 %top.1 = (bf16[256,384]{1,0:T(8,128)(2,1)S(1)}, bf16[256,384]{1,0:T(8,128)(2,1)S(1)}, bf16[256,1536]{1,0:T(8,128)(2,1)S(1)}, bf16[256,1536]{1,0:T(8,128)(2,1)S(1...) custom-call(f32[3,22,24,128]{3,2,1,0:T(8,128)S(1)} %get-tuple-element.149.mids, ...), custom_call_target="tpu_custom_call" | custom-call | tf_op jit(solution)/shard_map/top/pallas_call | solution.py:370
  27.9 1.6 %weights_top.1 = (bf16[2,768,384]{2,1,0:T(8,128)(2,1)S(1)}, bf16[2,768,384]{2,1,0:T(8,128)(2,1)S(1)}) custom-call(s32[6]{0:T(128)S(1)} %stack.29.place, bf16[256,384]{1,0:T(8,128)(2,1)S(1)} %get-tuple-element.144.normed, bf16[256,1536]{1,0:T(8,128)(2,1)S(1)} %get-tuple-element.145.act, bf16[256,1536]{1,0:T(8,128)(2,1)S(1)} %get-tuple-element.146.gpre, ...), custom_call_target="tpu_custom_call" | custom-call | tf_op jit(solution)/shard_map/weights_top/pallas_call | solution.py:370
  29.6 2.1 %collective-permute-start.4 = (bf16[3,16,384]{2,1,0:T(8,128)(2,1)S(1)}, bf16[3,16,384]{2,1,0:T(8,128)(2,1)S(1)}, u32[]{:S(2)}, u32[]{:S(2)}) collective-permute-start(bf16[3,16,384]{2,1,0:T(8,128)(2,1)S(1)} %bitcast.142), channel_id=1, source_target_pairs={{0,4},{4,0},{8,12},{12,8},{16,20},{20,16},{24,28},{28,24},{1,5},{5... | collective-permute-start | bytes 110600 | tf_op jit(solution)/shard_map/ppermute | solution.py:392
  31.8 2.3 %again.1 = (f32[256,384]{1,0:T(8,128)S(1)}, f32[256,128]{1,0:T(8,128)S(1)}, bf16[256,384]{1,0:T(8,128)(2,1)S(1)}, bf16[256,1536]{1,0:T(8,128)(2,1)S(1)}, f32[256,1536]{1,0:T(8,128)S(1)}) custom-call(f32[3,16,16,128]{3,2,1,0:T(8,128)S(1)} %get-tuple-element.135.z0, f32[2,384]{1,0:T(2,128)S(1)} %copy-done.5, f32[2,384]{1,0:T(2,128)S(1)} %copy-done.6, ...), custom_call_target="tpu_custom_call" | custom-call | tf_op jit(solution)/shard_map/again/pallas_call | solution.py:370
  34.3 3.0 %collective-permute-start.7 = (bf16[22,3,384]{2,1,0:T(4,128)(2,1)S(1)}, bf16[22,3,384]{2,1,0:T(4,128)(2,1)S(1)}, u32[]{:S(2)}, u32[]{:S(2)}) collective-permute-start(bf16[22,3,384]{2,1,0:T(4,128)(2,1)S(1)} %get-tuple-element.271), channel_id=1, source_target_pairs={{0,4},{1,2},{2,1},{3,7},{4,0},{5,6},{6,5},{7,3},{8,12},{9,10},{10,... | collective-permute-start | bytes 152072 | tf_op jit(solution)/shard_map/ppermute | solution.py:408
  37.9 1.1 %collective-permute-start.10 = (bf16[1,4,2,48,384]{4,3,2,1,0:T(8,128)(2,1)S(1)}, bf16[1,4,2,48,384]{4,3,2,1,0:T(8,128)(2,1)S(1)}, u32[]{:S(2)}, u32[]{:S(2)}) collective-permute-start(bf16[1,4,2,48,384]{4,3,2,1,0:T(8,128)(2,1)S(1)} %get-tuple-element.249), channel_id=1, source_target_pairs={{0,4},{1,5},{2,6},{3,7},{4,0},{5,1},{6,2},{7,3},{8,12},{9,13},{10,... | collective-permute-start | bytes 884744 | tf_op jit(solution)/shard_map/ppermute | solution.py:422
  39.6 1.7 %top_taps.1.sums1 = f32[56,384]{1,0:T(8,128)S(1)} custom-call(f32[3,22,24,128]{3,2,1,0:T(8,128)S(1)} %get-tuple-element.149.mids, bf16[256,384]{1,0:T(8,128)(2,1)S(1)} %get-tuple-element.134.dz, f32[1,1536]{1,0:T(1,128)S(1)} %get-tuple-element.150.db, f32[1,384]{1,0:T(1,128)S(1)} %get-tuple-element.151.dgain, f32[1,384]{1,0:T(1,128)S(1)} %get-tuple-element.152.dshift), custom_call_target="tpu_custom_call" | custom-call | tf_op jit(solution)/shard_map/top_taps/pallas_call | solution.py:370
  41.7 4.3 %low.1 = (bf16[256,384]{1,0:T(8,128)(2,1)S(1)}, bf16[256,384]{1,0:T(8,128)(2,1)S(1)}, f32[1,1536]{1,0:T(1,128)S(1)}, f32[1,384]{1,0:T(1,128)S(1)}, f32[1,384]{1,...) custom-call(s32[6]{0:T(128)S(1)} %stack.29.place, ...), custom_call_target="tpu_custom_call" | custom-call | tf_op jit(solution)/shard_map/low/pallas_call | solution.py:370
  46.0 1.4 %collective-permute-done.10 = bf16[1,4,2,48,384]{4,3,2,1,0:T(8,128)(2,1)S(1)} collective-permute-done((bf16[1,4,2,48,384]{4,3,2,1,0:T(8,128)(2,1)S(1)}, bf16[1,4,2,48,384]{4,3,2,1,0:T(8,128)(2,1)S(1)}, u32[]{:S(2)}, u32[]{:S(2)}) %collective-permute-start.10) | collective-permute-done | bytes 294944 | tf_op jit(solution)/shard_map/ppermute | solution.py:422
  47.7 2.1 %taps.1 = (bf16[56,384]{1,0:T(8,128)(2,1)S(1)}, bf16[56,384]{1,0:T(8,128)(2,1)S(1)}) custom-call(s32[6]{0:T(128)S(1)} %stack.29.place, bf16[28,32,384]{2,1,0:T(8,128)(2,1)S(1)} %fusion.12.xpad, bf16[256,384]{1,0:T(8,128)(2,1)S(1)} %get-tuple-element.190.dz, f32[1,1536]{1,0:T(1,128)S(1)} %get-tuple-element.176.db, f32[1,384]{1,0:T(1,128)S(1)} %get-tuple-element.177.dgain, ...), custom_call_target="tpu_custom_call" | custom-call | tf_op jit(solution)/shard_map/taps/pallas_call | solution.py:370
  50.7 2.6 %collective-permute-start.15 = (bf16[384,384]{1,0:T(8,128)(2,1)S(1)}, bf16[384,384]{1,0:T(8,128)(2,1)S(1)}, u32[]{:S(2)}, u32[]{:S(2)}) collective-permute-start(bf16[384,384]{1,0:T(8,128)(2,1)S(1)} %pad_maximum_fusion.1), channel_id=1, source_target_pairs={{0,8},{1,9},{2,10},{3,11},{4,12},{5,13},{6,14},{7,15},{8,0},{9,1},... | collective-permute-start | bytes 884744 | tf_op jit(solution)/shard_map/ppermute | solution.py:422
  54.3 1.3 %collective-permute-start.14 = (bf16[1,4,2,48,384]{4,3,2,1,0:T(8,128)(2,1)S(1)}, bf16[1,4,2,48,384]{4,3,2,1,0:T(8,128)(2,1)S(1)}, u32[]{:S(2)}, u32[]{:S(2)}) collective-permute-start(bf16[1,4,2,48,384]{4,3,2,1,0:T(8,128)(2,1)S(1)} %get-tuple-element.245), channel_id=1, source_target_pairs={{0,4},{1,5},{2,6},{3,7},{4,0},{5,1},{6,2},{7,3},{8,12},{9,13},{10,... | collective-permute-start | bytes 884744 | tf_op jit(solution)/shard_map/ppermute | solution.py:422
  55.7 1.8 %collective-permute-start.13 = (bf16[1,8,1,48,384]{4,3,1,2,0:T(8,128)(2,1)S(1)}, bf16[1,8,1,48,384]{4,3,1,2,0:T(8,128)(2,1)S(1)}, u32[]{:S(2)}, u32[]{:S(2)}) collective-permute-start(bf16[1,8,1,48,384]{4,3,1,2,0:T(8,128)(2,1)S(1)} %get-tuple-element.247), channel_id=1, source_target_pairs={{0,2},{1,3},{2,0},{3,1},{4,6},{5,7},{6,4},{7,5},{8,10},{9,11},{10,... | collective-permute-start | bytes 884744 | tf_op jit(solution)/shard_map/ppermute | solution.py:422
  58.3 2.3 %collective-permute-done.15 = bf16[384,384]{1,0:T(8,128)(2,1)S(1)} collective-permute-done((bf16[384,384]{1,0:T(8,128)(2,1)S(1)}, bf16[384,384]{1,0:T(8,128)(2,1)S(1)}, u32[]{:S(2)}, u32[]{:S(2)}) %collective-permute-start.15) | collective-permute-done | bytes 294944 | tf_op jit(solution)/shard_map/ppermute | solution.py:422
  60.6 2.9 %collective-permute-done.16 = bf16[3,16,384]{2,1,0:T(8,128)(2,1)S(1)} collective-permute-done((bf16[3,16,384]{2,1,0:T(8,128)(2,1)S(1)}, bf16[3,16,384]{2,1,0:T(8,128)(2,1)S(1)}, u32[]{:S(2)}, u32[]{:S(2)}) %collective-permute-start.16) | collective-permute-done | bytes 36896 | tf_op jit(solution)/shard_map/ppermute | solution.py:392
  63.5 0.8 collective-permute-done.13
  64.7 2.5 %collective-permute-start.19 = (bf16[344,384]{1,0:T(8,128)(2,1)S(1)}, bf16[344,384]{1,0:T(8,128)(2,1)S(1)}, u32[]{:S(2)}, u32[]{:S(2)}) collective-permute-start(bf16[344,384]{1,0:T(8,128)(2,1)S(1)} %pad_maximum_fusion.4), channel_id=1, source_target_pairs={{0,4},{1,5},{2,6},{3,7},{4,0},{5,1},{6,2},{7,3},{8,12},{9,13},{10,... | collective-permute-start | bytes 792584 | tf_op jit(solution)/shard_map/ppermute | solution.py:422
  68.5 1.3 %collective-permute-start.21 = (bf16[22,3,384]{2,1,0:T(4,128)(2,1)S(1)}, bf16[22,3,384]{2,1,0:T(4,128)(2,1)S(1)}, u32[]{:S(2)}, u32[]{:S(2)}) collective-permute-start(bf16[22,3,384]{2,1,0:T(4,128)(2,1)S(1)} %get-tuple-element.270), channel_id=1, source_target_pairs={{0,1},{1,0},{2,3},{3,2},{4,5},{5,4},{6,7},{7,6},{8,9},{9,8},{10,11... | collective-permute-start | bytes 152072 | tf_op jit(solution)/shard_map/ppermute | solution.py:392
  69.8 3.6 %collective-permute-done.20 = bf16[288,384]{1,0:T(8,128)(2,1)S(1)} collective-permute-done((bf16[288,384]{1,0:T(8,128)(2,1)S(1)}, bf16[288,384]{1,0:T(8,128)(2,1)S(1)}, u32[]{:S(2)}, u32[]{:S(2)}) %collective-permute-start.20) | collective-permute-done | bytes 221216 | tf_op jit(solution)/shard_map/ppermute | solution.py:422
  73.6 2.8 %collective-permute-start.24 = (bf16[96,384]{1,0:T(8,128)(2,1)S(1)}, bf16[96,384]{1,0:T(8,128)(2,1)S(1)}, u32[]{:S(2)}, u32[]{:S(2)}) collective-permute-start(bf16[96,384]{1,0:T(8,128)(2,1)S(1)} %bitcast.139), channel_id=1, source_target_pairs={{0,16},{1,17},{2,18},{3,19},{4,20},{5,21},{6,22},{7,23},{8,24},{9,... | collective-permute-start | bytes 221192 | tf_op jit(solution)/shard_map/ppermute | solution.py:422
  77.5 2.5 %last.1 = bf16[256,384]{1,0:T(8,128)(2,1)} custom-call(bf16[22,32,384]{2,1,0:T(8,128)(2,1)S(1)} %fusion.18.dzpad, bf16[256,384]{1,0:T(8,128)(2,1)S(1)} %get-tuple-element.221.gmid, f32[49,2,384]{2,1,0:T(2,128)S(1)} %bitcast.99), custom_call_target="tpu_custom_call" | custom-call | tf_op jit(solution)/shard_map/last/pallas_call | solution.py:370
  79.9 3.9 %collective-permute-done.23 = bf16[248,384]{1,0:T(8,128)(2,1)S(1)} collective-permute-done((bf16[248,384]{1,0:T(8,128)(2,1)S(1)}, bf16[248,384]{1,0:T(8,128)(2,1)S(1)}, u32[]{:S(2)}, u32[]{:S(2)}) %collective-permute-start.23) | collective-permute-done | bytes 190496 | tf_op jit(solution)/shard_map/ppermute | solution.py:422
  84.0 1.2 %collective-permute-start.25 = (bf16[152,384]{1,0:T(8,128)(2,1)S(1)}, bf16[152,384]{1,0:T(8,128)(2,1)S(1)}, u32[]{:S(2)}, u32[]{:S(2)}) collective-permute-start(bf16[152,384]{1,0:T(8,128)(2,1)S(1)} %pad_maximum_fusion.7), channel_id=1, source_target_pairs={{0,16},{1,17},{2,18},{3,19},{4,20},{5,21},{6,22},{7,23},{8,24},{9,... | collective-permute-start | bytes 350216 | tf_op jit(solution)/shard_map/ppermute | solution.py:422
  85.2 6.8 %collective-permute-done.25 = bf16[152,384]{1,0:T(8,128)(2,1)S(1)} collective-permute-done((bf16[152,384]{1,0:T(8,128)(2,1)S(1)}, bf16[152,384]{1,0:T(8,128)(2,1)S(1)}, u32[]{:S(2)}, u32[]{:S(2)}) %collective-permute-start.25) | collective-permute-done | bytes 116768 | tf_op jit(solution)/shard_map/ppermute | solution.py:422
  92.1 0.7 weights.1
  93.3 1.3 %small.1 = (f32[49,2,384]{2,1,0:T(2,128)}, f32[2,384]{1,0:T(2,128)}, f32[2,384]{1,0:T(2,128)}, f32[2,1536]{1,0:T(2,128)}) custom-call(s32[6]{0:T(128)S(1)} %stack.29.place, bf16[56,384]{1,0:T(8,128)(2,1)S(1)} %add_convert_fusion.13.mine, bf16[56,384]{1,0:T(8,128)(2,1)S(1)} %collective-permute-done.26.got), custom_call_target="tpu_custom_call" | custom-call | tf_op jit(solution)/shard_map/small/pallas_call | solution.py:370
  (113 shorter events, 9.5 us)
Async XLA Ops:
  2.3 6.4 %collective-permute-start = (bf16[6,16,384]{2,1,0:T(8,128)(2,1)S(1)}, bf16[6,16,384]{2,1,0:T(8,128)(2,1)S(1)}, u32[]{:S(2)}, u32[]{:S(2)}) collective-permute-start(bf16[6,16,384]{2,1,0:T(8,128)(2,1)S(1)} %get-tuple-element.128), channel_id=1, source_target_pairs={{0,4},{4,0},{8,12},{12,8},{16,20},{20,16},{24,28},{28,24},{1,5},{5... | collective-permute-start | bytes 221192 | tf_op jit(solution)/shard_map/ppermute | solution.py:392
  5.3 3.4 %collective-permute-start.1 = (bf16[6,16,384]{2,1,0:T(8,128)(2,1)S(1)}, bf16[6,16,384]{2,1,0:T(8,128)(2,1)S(1)}, u32[]{:S(2)}, u32[]{:S(2)}) collective-permute-start(bf16[6,16,384]{2,1,0:T(8,128)(2,1)S(1)} %get-tuple-element.130), channel_id=1, source_target_pairs={{0,1},{1,0},{2,3},{3,2},{4,8},{5,9},{6,10},{7,11},{8,4},{9,5},{10,... | collective-permute-start | bytes 221192 | tf_op jit(solution)/shard_map/ppermute | solution.py:408
  8.8 6.3 %copy-start.1 = (f32[2,7,7,384]{3,0,2,1:T(2,128)S(1)}, f32[2,7,7,384]{3,0,2,1:T(2,128)}, u32[]{:S(2)}) copy-start(f32[2,7,7,384]{3,0,2,1:T(2,128)} %param.10) | copy-start | bytes 451588
  8.9 6.3 %copy-start.4 = (f32[2,1536]{1,0:T(2,128)S(1)}, f32[2,1536]{1,0:T(2,128)}, u32[]{:S(2)}) copy-start(f32[2,1536]{1,0:T(2,128)} %b_in.5) | copy-start | bytes 36868
  8.9 6.3 %copy-start.5 = (f32[2,384]{1,0:T(2,128)S(1)}, f32[2,384]{1,0:T(2,128)}, u32[]{:S(2)}) copy-start(f32[2,384]{1,0:T(2,128)} %gains.7) | copy-start | bytes 9220
  8.9 5.9 %collective-permute-start.3 = (bf16[28,6,384]{2,1,0:T(8,128)(2,1)S(1)}, bf16[28,6,384]{2,1,0:T(8,128)(2,1)S(1)}, u32[]{:S(2)}, u32[]{:S(2)}) collective-permute-start(bf16[28,6,384]{2,1,0:T(8,128)(2,1)S(1)} %get-tuple-element.255), channel_id=1, source_target_pairs={{0,4},{1,2},{2,1},{3,7},{4,0},{5,6},{6,5},{7,3},{8,12},{9,10},{10,... | collective-permute-start | bytes 387080 | tf_op jit(solution)/shard_map/ppermute | solution.py:408
  11.4 3.4 %collective-permute-start.2 = (bf16[28,6,384]{2,1,0:T(8,128)(2,1)S(1)}, bf16[28,6,384]{2,1,0:T(8,128)(2,1)S(1)}, u32[]{:S(2)}, u32[]{:S(2)}) collective-permute-start(bf16[28,6,384]{2,1,0:T(8,128)(2,1)S(1)} %get-tuple-element.256), channel_id=1, source_target_pairs={{0,1},{1,0},{2,3},{3,2},{4,5},{5,4},{6,7},{7,6},{8,9},{9,8},{10,11... | collective-permute-start | bytes 387080 | tf_op jit(solution)/shard_map/ppermute | solution.py:392
  15.2 8.1 %copy-start.2 = (bf16[16,16,384]{2,1,0:T(8,128)(2,1)S(1)}, bf16[16,16,384]{2,1,0:T(8,128)(2,1)}, u32[]{:S(2)}) copy-start(bf16[16,16,384]{2,1,0:T(8,128)(2,1)} %param.9) | copy-start | bytes 589828
  23.3 8.6 %copy-start = (bf16[2,384,1536]{2,1,0:T(8,128)(2,1)S(1)}, bf16[2,384,1536]{2,1,0:T(8,128)(2,1)}, u32[]{:S(2)}) copy-start(bf16[2,384,1536]{2,1,0:T(8,128)(2,1)} %w_in.7) | copy-start | bytes 7077892
  29.5 7.9 %collective-permute-start.8 = (bf16[2,16,48,384]{3,2,1,0:T(8,128)(2,1)S(1)}, bf16[2,16,48,384]{3,2,1,0:T(8,128)(2,1)S(1)}, u32[]{:S(2)}, u32[]{:S(2)}) collective-permute-start(bf16[2,16,48,384]{3,2,1,0:T(8,128)(2,1)S(1)} %bitcast.112), channel_id=1, source_target_pairs={{0,1},{1,0},{2,3},{3,2},{4,5},{5,4},{6,7},{7,6},{8,9},{9,8},{10,11... | collective-permute-start | bytes 3538952 | tf_op jit(solution)/shard_map/ppermute | solution.py:422
  29.6 4.6 %collective-permute-start.4 = (bf16[3,16,384]{2,1,0:T(8,128)(2,1)S(1)}, bf16[3,16,384]{2,1,0:T(8,128)(2,1)S(1)}, u32[]{:S(2)}, u32[]{:S(2)}) collective-permute-start(bf16[3,16,384]{2,1,0:T(8,128)(2,1)S(1)} %bitcast.142), channel_id=1, source_target_pairs={{0,4},{4,0},{8,12},{12,8},{16,20},{20,16},{24,28},{28,24},{1,5},{5... | collective-permute-start | bytes 110600 | tf_op jit(solution)/shard_map/ppermute | solution.py:392
  31.6 2.5 %collective-permute-start.5 = (bf16[3,16,384]{2,1,0:T(8,128)(2,1)S(1)}, bf16[3,16,384]{2,1,0:T(8,128)(2,1)S(1)}, u32[]{:S(2)}, u32[]{:S(2)}) collective-permute-start(bf16[3,16,384]{2,1,0:T(8,128)(2,1)S(1)} %bitcast.140), channel_id=1, source_target_pairs={{0,1},{1,0},{2,3},{3,2},{4,8},{5,9},{6,10},{7,11},{8,4},{9,5},{10,... | collective-permute-start | bytes 110600 | tf_op jit(solution)/shard_map/ppermute | solution.py:408
  34.3 7.0 %collective-permute-start.7 = (bf16[22,3,384]{2,1,0:T(4,128)(2,1)S(1)}, bf16[22,3,384]{2,1,0:T(4,128)(2,1)S(1)}, u32[]{:S(2)}, u32[]{:S(2)}) collective-permute-start(bf16[22,3,384]{2,1,0:T(4,128)(2,1)S(1)} %get-tuple-element.271), channel_id=1, source_target_pairs={{0,4},{1,2},{2,1},{3,7},{4,0},{5,6},{6,5},{7,3},{8,12},{9,10},{10,... | collective-permute-start | bytes 152072 | tf_op jit(solution)/shard_map/ppermute | solution.py:408
  37.3 4.0 %collective-permute-start.6 = (bf16[22,3,384]{2,1,0:T(4,128)(2,1)S(1)}, bf16[22,3,384]{2,1,0:T(4,128)(2,1)S(1)}, u32[]{:S(2)}, u32[]{:S(2)}) collective-permute-start(bf16[22,3,384]{2,1,0:T(4,128)(2,1)S(1)} %get-tuple-element.272), channel_id=1, source_target_pairs={{0,1},{1,0},{2,3},{3,2},{4,5},{5,4},{6,7},{7,6},{8,9},{9,8},{10,11... | collective-permute-start | bytes 152072 | tf_op jit(solution)/shard_map/ppermute | solution.py:392
  37.9 9.5 %collective-permute-start.10 = (bf16[1,4,2,48,384]{4,3,2,1,0:T(8,128)(2,1)S(1)}, bf16[1,4,2,48,384]{4,3,2,1,0:T(8,128)(2,1)S(1)}, u32[]{:S(2)}, u32[]{:S(2)}) collective-permute-start(bf16[1,4,2,48,384]{4,3,2,1,0:T(8,128)(2,1)S(1)} %get-tuple-element.249), channel_id=1, source_target_pairs={{0,4},{1,5},{2,6},{3,7},{4,0},{5,1},{6,2},{7,3},{8,12},{9,13},{10,... | collective-permute-start | bytes 884744 | tf_op jit(solution)/shard_map/ppermute | solution.py:422
  39.0 8.7 %collective-permute-start.9 = (bf16[1,8,1,48,384]{4,3,1,2,0:T(8,128)(2,1)S(1)}, bf16[1,8,1,48,384]{4,3,1,2,0:T(8,128)(2,1)S(1)}, u32[]{:S(2)}, u32[]{:S(2)}) collective-permute-start(bf16[1,8,1,48,384]{4,3,1,2,0:T(8,128)(2,1)S(1)} %get-tuple-element.251), channel_id=1, source_target_pairs={{0,2},{1,3},{2,0},{3,1},{4,6},{5,7},{6,4},{7,5},{8,10},{9,11},{10,... | collective-permute-start | bytes 884744 | tf_op jit(solution)/shard_map/ppermute | solution.py:422
  47.7 5.6 %collective-permute-start.11 = (bf16[2,16,48,384]{3,2,1,0:T(8,128)(2,1)S(1)}, bf16[2,16,48,384]{3,2,1,0:T(8,128)(2,1)S(1)}, u32[]{:S(2)}, u32[]{:S(2)}) collective-permute-start(bf16[2,16,48,384]{3,2,1,0:T(8,128)(2,1)S(1)} %bitcast.111), channel_id=1, source_target_pairs={{0,1},{1,0},{2,3},{3,2},{4,5},{5,4},{6,7},{7,6},{8,9},{9,8},{10,11... | collective-permute-start | bytes 3538952 | tf_op jit(solution)/shard_map/ppermute | solution.py:422
  49.9 3.5 %collective-permute-start.12 = (bf16[56,384]{1,0:T(8,128)(2,1)S(1)}, bf16[56,384]{1,0:T(8,128)(2,1)S(1)}, u32[]{:S(2)}, u32[]{:S(2)}) collective-permute-start(bf16[56,384]{1,0:T(8,128)(2,1)S(1)} %get-tuple-element.181), channel_id=1, source_target_pairs={{0,1},{1,0},{2,3},{3,2},{4,5},{5,4},{6,7},{7,6},{8,9},{9,8},{10,11... | collective-permute-start | bytes 129032 | tf_op jit(solution)/shard_map/ppermute | solution.py:422
  50.7 9.8 %collective-permute-start.15 = (bf16[384,384]{1,0:T(8,128)(2,1)S(1)}, bf16[384,384]{1,0:T(8,128)(2,1)S(1)}, u32[]{:S(2)}, u32[]{:S(2)}) collective-permute-start(bf16[384,384]{1,0:T(8,128)(2,1)S(1)} %pad_maximum_fusion.1), channel_id=1, source_target_pairs={{0,8},{1,9},{2,10},{3,11},{4,12},{5,13},{6,14},{7,15},{8,0},{9,1},... | collective-permute-start | bytes 884744 | tf_op jit(solution)/shard_map/ppermute | solution.py:422
  53.9 9.6 %collective-permute-start.18 = (bf16[56,384]{1,0:T(8,128)(2,1)S(1)}, bf16[56,384]{1,0:T(8,128)(2,1)S(1)}, u32[]{:S(2)}, u32[]{:S(2)}) collective-permute-start(bf16[56,384]{1,0:T(8,128)(2,1)S(1)} %add_convert_fusion.17), channel_id=1, source_target_pairs={{0,2},{1,3},{2,0},{3,1},{4,6},{5,7},{6,4},{7,5},{8,10},{9,11},{10,... | collective-permute-start | bytes 129032 | tf_op jit(solution)/shard_map/ppermute | solution.py:422
  54.3 9.2 %collective-permute-start.14 = (bf16[1,4,2,48,384]{4,3,2,1,0:T(8,128)(2,1)S(1)}, bf16[1,4,2,48,384]{4,3,2,1,0:T(8,128)(2,1)S(1)}, u32[]{:S(2)}, u32[]{:S(2)}) collective-permute-start(bf16[1,4,2,48,384]{4,3,2,1,0:T(8,128)(2,1)S(1)} %get-tuple-element.245), channel_id=1, source_target_pairs={{0,4},{1,5},{2,6},{3,7},{4,0},{5,1},{6,2},{7,3},{8,12},{9,13},{10,... | collective-permute-start | bytes 884744 | tf_op jit(solution)/shard_map/ppermute | solution.py:422
  55.7 8.6 %collective-permute-start.13 = (bf16[1,8,1,48,384]{4,3,1,2,0:T(8,128)(2,1)S(1)}, bf16[1,8,1,48,384]{4,3,1,2,0:T(8,128)(2,1)S(1)}, u32[]{:S(2)}, u32[]{:S(2)}) collective-permute-start(bf16[1,8,1,48,384]{4,3,1,2,0:T(8,128)(2,1)S(1)} %get-tuple-element.247), channel_id=1, source_target_pairs={{0,2},{1,3},{2,0},{3,1},{4,6},{5,7},{6,4},{7,5},{8,10},{9,11},{10,... | collective-permute-start | bytes 884744 | tf_op jit(solution)/shard_map/ppermute | solution.py:422
  57.5 6.0 %collective-permute-start.16 = (bf16[3,16,384]{2,1,0:T(8,128)(2,1)S(1)}, bf16[3,16,384]{2,1,0:T(8,128)(2,1)S(1)}, u32[]{:S(2)}, u32[]{:S(2)}) collective-permute-start(bf16[3,16,384]{2,1,0:T(8,128)(2,1)S(1)} %bitcast.143), channel_id=1, source_target_pairs={{0,4},{4,0},{8,12},{12,8},{16,20},{20,16},{24,28},{28,24},{1,5},{5... | collective-permute-start | bytes 110600 | tf_op jit(solution)/shard_map/ppermute | solution.py:392
  60.6 2.9 %collective-permute-start.17 = (bf16[3,16,384]{2,1,0:T(8,128)(2,1)S(1)}, bf16[3,16,384]{2,1,0:T(8,128)(2,1)S(1)}, u32[]{:S(2)}, u32[]{:S(2)}) collective-permute-start(bf16[3,16,384]{2,1,0:T(8,128)(2,1)S(1)} %bitcast.141), channel_id=1, source_target_pairs={{0,1},{1,0},{2,3},{3,2},{4,8},{5,9},{6,10},{7,11},{8,4},{9,5},{10,... | collective-permute-start | bytes 110600 | tf_op jit(solution)/shard_map/ppermute | solution.py:408
  64.7 8.7 %collective-permute-start.19 = (bf16[344,384]{1,0:T(8,128)(2,1)S(1)}, bf16[344,384]{1,0:T(8,128)(2,1)S(1)}, u32[]{:S(2)}, u32[]{:S(2)}) collective-permute-start(bf16[344,384]{1,0:T(8,128)(2,1)S(1)} %pad_maximum_fusion.4), channel_id=1, source_target_pairs={{0,4},{1,5},{2,6},{3,7},{4,0},{5,1},{6,2},{7,3},{8,12},{9,13},{10,... | collective-permute-start | bytes 792584 | tf_op jit(solution)/shard_map/ppermute | solution.py:422
  67.4 6.0 %collective-permute-start.20 = (bf16[288,384]{1,0:T(8,128)(2,1)S(1)}, bf16[288,384]{1,0:T(8,128)(2,1)S(1)}, u32[]{:S(2)}, u32[]{:S(2)}) collective-permute-start(bf16[288,384]{1,0:T(8,128)(2,1)S(1)} %pad_maximum_fusion.5), channel_id=1, source_target_pairs={{0,2},{1,3},{2,0},{3,1},{4,6},{5,7},{6,4},{7,5},{8,10},{9,11},{10,... | collective-permute-start | bytes 663560 | tf_op jit(solution)/shard_map/ppermute | solution.py:422
  68.1 5.3 %collective-permute-start.22 = (bf16[22,3,384]{2,1,0:T(4,128)(2,1)S(1)}, bf16[22,3,384]{2,1,0:T(4,128)(2,1)S(1)}, u32[]{:S(2)}, u32[]{:S(2)}) collective-permute-start(bf16[22,3,384]{2,1,0:T(4,128)(2,1)S(1)} %get-tuple-element.269), channel_id=1, source_target_pairs={{0,4},{1,2},{2,1},{3,7},{4,0},{5,6},{6,5},{7,3},{8,12},{9,10},{10,... | collective-permute-start | bytes 152072 | tf_op jit(solution)/shard_map/ppermute | solution.py:408
  68.5 5.0 %collective-permute-start.21 = (bf16[22,3,384]{2,1,0:T(4,128)(2,1)S(1)}, bf16[22,3,384]{2,1,0:T(4,128)(2,1)S(1)}, u32[]{:S(2)}, u32[]{:S(2)}) collective-permute-start(bf16[22,3,384]{2,1,0:T(4,128)(2,1)S(1)} %get-tuple-element.270), channel_id=1, source_target_pairs={{0,1},{1,0},{2,3},{3,2},{4,5},{5,4},{6,7},{7,6},{8,9},{9,8},{10,11... | collective-permute-start | bytes 152072 | tf_op jit(solution)/shard_map/ppermute | solution.py:392
  73.6 10.3 %collective-permute-start.24 = (bf16[96,384]{1,0:T(8,128)(2,1)S(1)}, bf16[96,384]{1,0:T(8,128)(2,1)S(1)}, u32[]{:S(2)}, u32[]{:S(2)}) collective-permute-start(bf16[96,384]{1,0:T(8,128)(2,1)S(1)} %bitcast.139), channel_id=1, source_target_pairs={{0,16},{1,17},{2,18},{3,19},{4,20},{5,21},{6,22},{7,23},{8,24},{9,... | collective-permute-start | bytes 221192 | tf_op jit(solution)/shard_map/ppermute | solution.py:422
  76.6 7.3 %collective-permute-start.23 = (bf16[248,384]{1,0:T(8,128)(2,1)S(1)}, bf16[248,384]{1,0:T(8,128)(2,1)S(1)}, u32[]{:S(2)}, u32[]{:S(2)}) collective-permute-start(bf16[248,384]{1,0:T(8,128)(2,1)S(1)} %pad_maximum_fusion.6), channel_id=1, source_target_pairs={{0,8},{1,9},{2,10},{3,11},{4,12},{5,13},{6,14},{7,15},{8,0},{9,1},... | collective-permute-start | bytes 571400 | tf_op jit(solution)/shard_map/ppermute | solution.py:422
  84.0 8.0 %collective-permute-start.25 = (bf16[152,384]{1,0:T(8,128)(2,1)S(1)}, bf16[152,384]{1,0:T(8,128)(2,1)S(1)}, u32[]{:S(2)}, u32[]{:S(2)}) collective-permute-start(bf16[152,384]{1,0:T(8,128)(2,1)S(1)} %pad_maximum_fusion.7), channel_id=1, source_target_pairs={{0,16},{1,17},{2,18},{3,19},{4,20},{5,21},{6,22},{7,23},{8,24},{9,... | collective-permute-start | bytes 350216 | tf_op jit(solution)/shard_map/ppermute | solution.py:422
  92.0 1.3 %collective-permute-start.26 = (bf16[56,384]{1,0:T(8,128)(2,1)S(1)}, bf16[56,384]{1,0:T(8,128)(2,1)S(1)}, u32[]{:S(2)}, u32[]{:S(2)}) collective-permute-start(bf16[56,384]{1,0:T(8,128)(2,1)S(1)} %add_convert_fusion.13.mine), channel_id=1, source_target_pairs={{0,1},{1,0},{2,3},{3,2},{4,5},{5,4},{6,7},{7,6},{8,9},{9,8},{10,11... | collective-permute-start | bytes 129032 | tf_op jit(solution)/shard_map/ppermute | solution.py:422
  (2 other events, 7.3 us)

commit v16 on v15

--- a/solution.py
+++ b/solution.py
@@ -652,46 +652,58 @@
     small_got = flip_bit(send, 0)
     run0, dz0, small, small_got = fenced(run0, dz0, small, small_got)
     pair0 = fork(run0)
+    small = summed(small, small_got)
+    for bit in range(1, col_bits - 1):
+        small = summed(small, flip_bit(small, bit))
+    small_by = [flip_bit(small, sides[1]), flip_bit(small, sides[0]), flip_bit(small, *sides)]
+    pair0, pair1, dz0, small, small_by = fenced(pair0, pair1, dz0, small, small_by)
+    both = [onward([settled(pair0[i]), settled(pair1[i])], sides[1 - i])[0] for i in range(2)]
+    small = summed(small, *small_by)
+    small_got = flip_bit(small, low_bit)
     tile0 = dz0.reshape(rows, cols, channels)
     twin, other = edges(tile0, 0, HALO, odd_row)
     twin, other = to_twin(twin, "rows"), to_other(other, "rows")
+    both, tile0, twin, other, small, small_got = fenced(both, tile0, twin, other, small, small_got)
+    (run0,), _ = onward([merged([both[0][0], both[1][0]])], low_bit)
     small = summed(small, small_got)
-    for bit in range(1, col_bits - 1):
-        small = summed(small, flip_bit(small, bit))
-    small_got = flip_bit(small, sides[0])
-    pair0, pair1, tile0, twin, other, small, small_got = fenced(
-        pair0, pair1, tile0, twin, other, small, small_got
-    )
-    small = summed(small, small_got)
-    moved_in, (small_got,) = onward([settled(pair0[0]), settled(pair1[0])], sides[1], small)
-    moved_out, _ = onward([settled(pair0[1]), settled(pair1[1])], sides[0])
-    both = [moved_in, moved_out]
+    (flight1,), (small_got,) = onward([merged([both[0][1], both[1][1]])], low_bit + 1, small)
     wide0 = rimmed(tile0, twin, other, 0, odd_row, outer_row)
     twin, other = edges(wide0, 1, HALO, odd_col)
     twin, other = to_twin(twin, "cols"), to_other(other, "cols")
-    both, wide0, twin, other, small, small_got = fenced(both, wide0, twin, other, small, small_got)
-    small = summed(small, small_got)
-    (run0,), (small_got,) = onward([merged([both[0][0], both[1][0]])], low_bit, small)
-    part1, order1 = merged([both[0][1], both[1][1]])
-    flight1 = (part1, jnp.zeros_like(part1), order1)
-    if order1:
-        (flight1,), _ = onward([(part1, order1)], order1[-1])
-    (grad_in,) = run(
-        last_kernel,
-        (tile_b,),
-        spread_scratch,
-        (filled(rimmed(wide0, twin, other, 1, odd_col, outer_col)), grad_mid, taps),
-        name="last",
-    )
+    outs = None
     while run0[2]:
-        run0, flight1, small, small_got, grad_in = fenced(run0, flight1, small, small_got, grad_in)
-        small = summed(small, small_got)
-        (run0,), (small_got,) = onward([settled(run0)], run0[2][-1], small)
+        run0, flight1, small, small_got, wide0, twin, other = fenced(
+            run0, flight1, small, small_got, wide0, twin, other
+        )
+        (run0,), _ = onward([settled(run0)], run0[2][-1])
+        if small_got is not None:
+            small = summed(small, small_got)
+            small_got = None
         if flight1[2]:
-            (flight1,), _ = onward([settled(flight1)], flight1[2][-1])
-    run0, flight1, small, small_got = fenced(run0, flight1, small, small_got)
-    small = summed(small, small_got)
-    small_got = flip_bit(small, 0)
+            (flight1,), (small_got,) = onward([settled(flight1)], flight1[2][-1], small)
+        elif outs is None:
+            (grad_in,) = run(
+                last_kernel,
+                (tile_b,),
+                spread_scratch,
+                (filled(rimmed(wide0, twin, other, 1, odd_col, outer_col)), grad_mid, taps),
+                name="last",
+            )
+            outs = run(
+                functools.partial(small_kernel, grad_scale),
+                (
+                    shape(49, layers, channels),
+                    shape(layers, channels),
+                    shape(layers, channels),
+                    shape(layers, hidden),
+                ),
+                [],
+                (place, small, flip_bit(small, 0)),
+                [pltpu.SMEM, None, None],
+                name="small",
+            )
+    run0, flight1, grad_in, outs = fenced(run0, flight1, grad_in, outs)
+    grad_taps, grad_gains, grad_shifts, grad_b_in = outs
     share = shape(layers, per, channels)
     grad_w_in, grad_w_out = run(
         functools.partial(weights_kernel, grad_scale),
@@ -699,19 +711,6 @@
         [],
         [part.reshape(2, per, channels) for part in run0[:2] + flight1[:2]],
         name="weights",
-    )
-    grad_taps, grad_gains, grad_shifts, grad_b_in = run(
-        functools.partial(small_kernel, grad_scale),
-        (
-            shape(49, layers, channels),
-            shape(layers, channels),
-            shape(layers, channels),
-            shape(layers, hidden),
-        ),
-        [],
-        (place, small, small_got),
-        [pltpu.SMEM, None, None],
-        name="small",
     )
     return (
         grad_in.reshape(rows, cols, channels),

time: 94.7 us -> 91.4 us (0.965)
  waiting for transfers between devices: 29.2 us -> 25.2 us
    ppermute x6, waiting for transfers between devices: 6.28 us -> 3.38 us  [to_twin(): lax.ppermute(edge, axis, [(i, i ^ 1) for i in range(count) if i ^ 1 < cou...]
    ppermute x15 -> x18, waiting for transfers between devices: 19.6 us -> 17.4 us  [flip_bit(): return lax.ppermute(value, both, [(i, i ^ flip) for i in range(total)])]
    ppermute x6, waiting for transfers between devices: 3.4 us -> 4.37 us  [to_other(): return lax.ppermute(edge, ('rows', 'cols'), pairs)]
    ppermute x15 -> x18, starting transfers between devices: 16.3 us -> 17.2 us  [flip_bit(): return lax.ppermute(value, both, [(i, i ^ flip) for i in range(total)])]
  transfers between devices with their start and end apart: 27 -> 30, of which waited for: 11 -> 13; matrix products, arithmetic and copies ran while one was open for 3% -> 3% of each run, Pallas kernels for 14% -> 16%
where the time goes in v16:
time: 91.4 us; the launch traced here: 91.3 us
  starting transfers between devices  30.4 us (33%)
  Pallas kernels  29.7 us (32%)
  waiting for transfers between devices  25.2 us (28%)
  other arithmetic  2.91 us (3%)
  local copies, waits for them, and re-layouts  1.89 us (2%)
  between operations  1.25 us (1%)
    pallas_call x11, Pallas kernels, run(): pl.pallas_call(kernel, out_shape=outs, in_specs=[vmem if s is None else p...  29.7 us
    ppermute x18, waiting for transfers between devices, flip_bit(): return lax.ppermute(value, both, [(i, i ^ flip) for i in range(total)])  17.4 us
    ppermute x18, starting transfers between devices, flip_bit(): return lax.ppermute(value, both, [(i, i ^ flip) for i in range(total)])  17.2 us
    ppermute x6, starting transfers between devices, to_twin(): lax.ppermute(edge, axis, [(i, i ^ 1) for i in range(count) if i ^ 1 < cou...  6.91 us
    ppermute x6, starting transfers between devices, to_other(): return lax.ppermute(edge, ('rows', 'cols'), pairs)  6.25 us
    ppermute x6, waiting for transfers between devices, to_other(): return lax.ppermute(edge, ('rows', 'cols'), pairs)  4.37 us
    ppermute x6, waiting for transfers between devices, to_twin(): lax.ppermute(edge, axis, [(i, i ^ 1) for i in range(count) if i ^ 1 < cou...  3.38 us
  transfers between devices with their start and end apart: 30, of which 13 were waited for; matrix products, arithmetic and copies ran while one was open for 3% of the time, Pallas kernels for 16%

profile of v16, /device:TPU:0, one launch (start us, length us, event | category | flops | bytes accessed | tf_op | source)
XLA Modules:
  0.0 91.3 jit_solution(17381801407247640563)
XLA Ops:
  2.3 3.0 %collective-permute-start = (bf16[6,16,384]{2,1,0:T(8,128)(2,1)S(1)}, bf16[6,16,384]{2,1,0:T(8,128)(2,1)S(1)}, u32[]{:S(2)}, u32[]{:S(2)}) collective-permute-start(bf16[6,16,384]{2,1,0:T(8,128)(2,1)S(1)} %get-tuple-element.133), channel_id=1, source_target_pairs={{0,4},{4,0},{8,12},{12,8},{16,20},{20,16},{24,28},{28,24},{1,5},{5... | collective-permute-start | bytes 221192 | tf_op jit(solution)/shard_map/ppermute | solution.py:392
  5.3 3.4 %collective-permute-done = bf16[6,16,384]{2,1,0:T(8,128)(2,1)S(1)} collective-permute-done((bf16[6,16,384]{2,1,0:T(8,128)(2,1)S(1)}, bf16[6,16,384]{2,1,0:T(8,128)(2,1)S(1)}, u32[]{:S(2)}, u32[]{:S(2)}) %collective-permute-start) | collective-permute-done | bytes 73760 | tf_op jit(solution)/shard_map/ppermute | solution.py:392
  8.9 2.5 %collective-permute-start.3 = (bf16[28,6,384]{2,1,0:T(8,128)(2,1)S(1)}, bf16[28,6,384]{2,1,0:T(8,128)(2,1)S(1)}, u32[]{:S(2)}, u32[]{:S(2)}) collective-permute-start(bf16[28,6,384]{2,1,0:T(8,128)(2,1)S(1)} %get-tuple-element.265), channel_id=1, source_target_pairs={{0,4},{1,2},{2,1},{3,7},{4,0},{5,6},{6,5},{7,3},{8,12},{9,10},{10,... | collective-permute-start | bytes 387080 | tf_op jit(solution)/shard_map/ppermute | solution.py:408
  11.4 3.4 %collective-permute-done.3 = bf16[28,6,384]{2,1,0:T(8,128)(2,1)S(1)} collective-permute-done((bf16[28,6,384]{2,1,0:T(8,128)(2,1)S(1)}, bf16[28,6,384]{2,1,0:T(8,128)(2,1)S(1)}, u32[]{:S(2)}, u32[]{:S(2)}) %collective-permute-start.3) | collective-permute-done | bytes 129056 | tf_op jit(solution)/shard_map/ppermute | solution.py:408
  15.2 8.0 %forward.1 = (f32[3,22,24,128]{3,2,1,0:T(8,128)S(1)}, f32[3,16,16,128]{3,2,1,0:T(8,128)S(1)}) custom-call(s32[6]{0:T(128)S(1)} %stack.29.place, bf16[28,32,384]{2,1,0:T(8,128)(2,1)S(1)} %fusion.12.xpad, f32[49,2,384]{2,1,0:T(2,128)S(1)} %bitcast.94, f32[2,384]{1,0:T(2,128)S(1)} %copy-done.5, f32[2,384]{1,0:T(2,128)S(1)} %copy-done.6, ...), custom_call_target="tpu_custom_call" | custom-call | tf_op jit(solution)/shard_map/forward/pallas_call | solution.py:370
  23.3 4.6 %top.1 = (bf16[256,384]{1,0:T(8,128)(2,1)S(1)}, bf16[256,384]{1,0:T(8,128)(2,1)S(1)}, bf16[256,1536]{1,0:T(8,128)(2,1)S(1)}, bf16[256,1536]{1,0:T(8,128)(2,1)S(1...) custom-call(f32[3,22,24,128]{3,2,1,0:T(8,128)S(1)} %get-tuple-element.154.mids, ...), custom_call_target="tpu_custom_call" | custom-call | tf_op jit(solution)/shard_map/top/pallas_call | solution.py:370
  27.9 1.6 %weights_top.1 = (bf16[2,768,384]{2,1,0:T(8,128)(2,1)S(1)}, bf16[2,768,384]{2,1,0:T(8,128)(2,1)S(1)}) custom-call(s32[6]{0:T(128)S(1)} %stack.29.place, bf16[256,384]{1,0:T(8,128)(2,1)S(1)} %get-tuple-element.149.normed, bf16[256,1536]{1,0:T(8,128)(2,1)S(1)} %get-tuple-element.150.act, bf16[256,1536]{1,0:T(8,128)(2,1)S(1)} %get-tuple-element.151.gpre, ...), custom_call_target="tpu_custom_call" | custom-call | tf_op jit(solution)/shard_map/weights_top/pallas_call | solution.py:370
  29.6 2.1 %collective-permute-start.4 = (bf16[3,16,384]{2,1,0:T(8,128)(2,1)S(1)}, bf16[3,16,384]{2,1,0:T(8,128)(2,1)S(1)}, u32[]{:S(2)}, u32[]{:S(2)}) collective-permute-start(bf16[3,16,384]{2,1,0:T(8,128)(2,1)S(1)} %bitcast.141), channel_id=1, source_target_pairs={{0,4},{4,0},{8,12},{12,8},{16,20},{20,16},{24,28},{28,24},{1,5},{5... | collective-permute-start | bytes 110600 | tf_op jit(solution)/shard_map/ppermute | solution.py:392
  31.8 2.3 %again.1 = (f32[256,384]{1,0:T(8,128)S(1)}, f32[256,128]{1,0:T(8,128)S(1)}, bf16[256,384]{1,0:T(8,128)(2,1)S(1)}, bf16[256,1536]{1,0:T(8,128)(2,1)S(1)}, f32[256,1536]{1,0:T(8,128)S(1)}) custom-call(f32[3,16,16,128]{3,2,1,0:T(8,128)S(1)} %get-tuple-element.140.z0, f32[2,384]{1,0:T(2,128)S(1)} %copy-done.5, f32[2,384]{1,0:T(2,128)S(1)} %copy-done.6, ...), custom_call_target="tpu_custom_call" | custom-call | tf_op jit(solution)/shard_map/again/pallas_call | solution.py:370
  34.3 3.0 %collective-permute-start.7 = (bf16[22,3,384]{2,1,0:T(4,128)(2,1)S(1)}, bf16[22,3,384]{2,1,0:T(4,128)(2,1)S(1)}, u32[]{:S(2)}, u32[]{:S(2)}) collective-permute-start(bf16[22,3,384]{2,1,0:T(4,128)(2,1)S(1)} %get-tuple-element.281), channel_id=1, source_target_pairs={{0,4},{1,2},{2,1},{3,7},{4,0},{5,6},{6,5},{7,3},{8,12},{9,10},{10,... | collective-permute-start | bytes 152072 | tf_op jit(solution)/shard_map/ppermute | solution.py:408
  37.9 1.1 %collective-permute-start.10 = (bf16[1,4,2,48,384]{4,3,2,1,0:T(8,128)(2,1)S(1)}, bf16[1,4,2,48,384]{4,3,2,1,0:T(8,128)(2,1)S(1)}, u32[]{:S(2)}, u32[]{:S(2)}) collective-permute-start(bf16[1,4,2,48,384]{4,3,2,1,0:T(8,128)(2,1)S(1)} %get-tuple-element.259), channel_id=1, source_target_pairs={{0,4},{1,5},{2,6},{3,7},{4,0},{5,1},{6,2},{7,3},{8,12},{9,13},{10,... | collective-permute-start | bytes 884744 | tf_op jit(solution)/shard_map/ppermute | solution.py:422
  39.6 1.7 %top_taps.1.sums1 = f32[56,384]{1,0:T(8,128)S(1)} custom-call(f32[3,22,24,128]{3,2,1,0:T(8,128)S(1)} %get-tuple-element.154.mids, bf16[256,384]{1,0:T(8,128)(2,1)S(1)} %get-tuple-element.139.dz, f32[1,1536]{1,0:T(1,128)S(1)} %get-tuple-element.155.db, f32[1,384]{1,0:T(1,128)S(1)} %get-tuple-element.156.dgain, f32[1,384]{1,0:T(1,128)S(1)} %get-tuple-element.157.dshift), custom_call_target="tpu_custom_call" | custom-call | tf_op jit(solution)/shard_map/top_taps/pallas_call | solution.py:370
  41.7 4.3 %low.1 = (bf16[256,384]{1,0:T(8,128)(2,1)S(1)}, bf16[256,384]{1,0:T(8,128)(2,1)S(1)}, f32[1,1536]{1,0:T(1,128)S(1)}, f32[1,384]{1,0:T(1,128)S(1)}, f32[1,384]{1,...) custom-call(s32[6]{0:T(128)S(1)} %stack.29.place, ...), custom_call_target="tpu_custom_call" | custom-call | tf_op jit(solution)/shard_map/low/pallas_call | solution.py:370
  46.0 1.4 %collective-permute-done.10 = bf16[1,4,2,48,384]{4,3,2,1,0:T(8,128)(2,1)S(1)} collective-permute-done((bf16[1,4,2,48,384]{4,3,2,1,0:T(8,128)(2,1)S(1)}, bf16[1,4,2,48,384]{4,3,2,1,0:T(8,128)(2,1)S(1)}, u32[]{:S(2)}, u32[]{:S(2)}) %collective-permute-start.10) | collective-permute-done | bytes 294944 | tf_op jit(solution)/shard_map/ppermute | solution.py:422
  47.7 2.1 %taps.1 = (bf16[56,384]{1,0:T(8,128)(2,1)S(1)}, bf16[56,384]{1,0:T(8,128)(2,1)S(1)}) custom-call(s32[6]{0:T(128)S(1)} %stack.29.place, bf16[28,32,384]{2,1,0:T(8,128)(2,1)S(1)} %fusion.12.xpad, bf16[256,384]{1,0:T(8,128)(2,1)S(1)} %get-tuple-element.206.dz, f32[1,1536]{1,0:T(1,128)S(1)} %get-tuple-element.181.db, f32[1,384]{1,0:T(1,128)S(1)} %get-tuple-element.182.dgain, ...), custom_call_target="tpu_custom_call" | custom-call | tf_op jit(solution)/shard_map/taps/pallas_call | solution.py:370
  50.7 2.6 %collective-permute-start.15 = (bf16[384,384]{1,0:T(8,128)(2,1)S(1)}, bf16[384,384]{1,0:T(8,128)(2,1)S(1)}, u32[]{:S(2)}, u32[]{:S(2)}) collective-permute-start(bf16[384,384]{1,0:T(8,128)(2,1)S(1)} %pad_maximum_fusion.1), channel_id=1, source_target_pairs={{0,8},{1,9},{2,10},{3,11},{4,12},{5,13},{6,14},{7,15},{8,0},{9,1},... | collective-permute-start | bytes 884744 | tf_op jit(solution)/shard_map/ppermute | solution.py:422
  53.9 1.4 %collective-permute-start.14 = (bf16[1,4,2,48,384]{4,3,2,1,0:T(8,128)(2,1)S(1)}, bf16[1,4,2,48,384]{4,3,2,1,0:T(8,128)(2,1)S(1)}, u32[]{:S(2)}, u32[]{:S(2)}) collective-permute-start(bf16[1,4,2,48,384]{4,3,2,1,0:T(8,128)(2,1)S(1)} %get-tuple-element.255), channel_id=1, source_target_pairs={{0,4},{1,5},{2,6},{3,7},{4,0},{5,1},{6,2},{7,3},{8,12},{9,13},{10,... | collective-permute-start | bytes 884744 | tf_op jit(solution)/shard_map/ppermute | solution.py:422
  55.7 1.9 %collective-permute-start.18 = (bf16[56,384]{1,0:T(8,128)(2,1)S(1)}, bf16[56,384]{1,0:T(8,128)(2,1)S(1)}, u32[]{:S(2)}, u32[]{:S(2)}) collective-permute-start(bf16[56,384]{1,0:T(8,128)(2,1)S(1)} %add_convert_fusion.16), channel_id=1, source_target_pairs={{0,6},{1,7},{2,4},{3,5},{4,2},{5,3},{6,0},{7,1},{8,14},{9,15},{10,... | collective-permute-start | bytes 129032 | tf_op jit(solution)/shard_map/ppermute | solution.py:422
  58.0 2.6 %collective-permute-done.15 = bf16[384,384]{1,0:T(8,128)(2,1)S(1)} collective-permute-done((bf16[384,384]{1,0:T(8,128)(2,1)S(1)}, bf16[384,384]{1,0:T(8,128)(2,1)S(1)}, u32[]{:S(2)}, u32[]{:S(2)}) %collective-permute-start.15) | collective-permute-done | bytes 294944 | tf_op jit(solution)/shard_map/ppermute | solution.py:422
  60.6 1.3 %collective-permute-start.16 = (bf16[56,384]{1,0:T(8,128)(2,1)S(1)}, bf16[56,384]{1,0:T(8,128)(2,1)S(1)}, u32[]{:S(2)}, u32[]{:S(2)}) collective-permute-start(bf16[56,384]{1,0:T(8,128)(2,1)S(1)} %add_convert_fusion.16), channel_id=1, source_target_pairs={{0,4},{1,5},{2,6},{3,7},{4,0},{5,1},{6,2},{7,3},{8,12},{9,13},{10,... | collective-permute-start | bytes 129032 | tf_op jit(solution)/shard_map/ppermute | solution.py:422
  61.9 3.4 %collective-permute-done.18 = bf16[56,384]{1,0:T(8,128)(2,1)S(1)} collective-permute-done((bf16[56,384]{1,0:T(8,128)(2,1)S(1)}, bf16[56,384]{1,0:T(8,128)(2,1)S(1)}, u32[]{:S(2)}, u32[]{:S(2)}) %collective-permute-start.18) | collective-permute-done | bytes 43040 | tf_op jit(solution)/shard_map/ppermute | solution.py:422
  65.8 1.2 %collective-permute-start.23 = (bf16[56,384]{1,0:T(8,128)(2,1)S(1)}, bf16[56,384]{1,0:T(8,128)(2,1)S(1)}, u32[]{:S(2)}, u32[]{:S(2)}) collective-permute-start(bf16[56,384]{1,0:T(8,128)(2,1)S(1)} %add_convert_fusion.15), channel_id=1, source_target_pairs={{0,8},{1,9},{2,10},{3,11},{4,12},{5,13},{6,14},{7,15},{8,0},{9,1},... | collective-permute-start | bytes 129032 | tf_op jit(solution)/shard_map/ppermute | solution.py:422
  67.2 1.4 %collective-permute-start.19 = (bf16[288,384]{1,0:T(8,128)(2,1)S(1)}, bf16[288,384]{1,0:T(8,128)(2,1)S(1)}, u32[]{:S(2)}, u32[]{:S(2)}) collective-permute-start(bf16[288,384]{1,0:T(8,128)(2,1)S(1)} %pad_maximum_fusion.4), channel_id=1, source_target_pairs={{0,4},{1,5},{2,6},{3,7},{4,0},{5,1},{6,2},{7,3},{8,12},{9,13},{10,... | collective-permute-start | bytes 663560 | tf_op jit(solution)/shard_map/ppermute | solution.py:422
  69.9 4.0 %collective-permute-done.19 = bf16[288,384]{1,0:T(8,128)(2,1)S(1)} collective-permute-done((bf16[288,384]{1,0:T(8,128)(2,1)S(1)}, bf16[288,384]{1,0:T(8,128)(2,1)S(1)}, u32[]{:S(2)}, u32[]{:S(2)}) %collective-permute-start.19) | collective-permute-done | bytes 221216 | tf_op jit(solution)/shard_map/ppermute | solution.py:422
  75.0 2.0 %collective-permute-start.25 = (bf16[152,384]{1,0:T(8,128)(2,1)S(1)}, bf16[152,384]{1,0:T(8,128)(2,1)S(1)}, u32[]{:S(2)}, u32[]{:S(2)}) collective-permute-start(bf16[152,384]{1,0:T(8,128)(2,1)S(1)} %pad_maximum_fusion.6), channel_id=1, source_target_pairs={{0,16},{1,17},{2,18},{3,19},{4,20},{5,21},{6,22},{7,23},{8,24},{9,... | collective-permute-start | bytes 350216 | tf_op jit(solution)/shard_map/ppermute | solution.py:422
  77.1 1.5 %collective-permute-start.24 = (bf16[192,384]{1,0:T(8,128)(2,1)S(1)}, bf16[192,384]{1,0:T(8,128)(2,1)S(1)}, u32[]{:S(2)}, u32[]{:S(2)}) collective-permute-start(bf16[192,384]{1,0:T(8,128)(2,1)S(1)} %bitcast.136), channel_id=1, source_target_pairs={{0,8},{1,9},{2,10},{3,11},{4,12},{5,13},{6,14},{7,15},{8,0},{9,1},... | collective-permute-start | bytes 442376 | tf_op jit(solution)/shard_map/ppermute | solution.py:422
  79.3 1.0 %collective-permute-start.26 = (bf16[22,3,384]{2,1,0:T(4,128)(2,1)S(1)}, bf16[22,3,384]{2,1,0:T(4,128)(2,1)S(1)}, u32[]{:S(2)}, u32[]{:S(2)}) collective-permute-start(bf16[22,3,384]{2,1,0:T(4,128)(2,1)S(1)} %get-tuple-element.280), channel_id=1, source_target_pairs={{0,1},{1,0},{2,3},{3,2},{4,5},{5,4},{6,7},{7,6},{8,9},{9,8},{10,11... | collective-permute-start | bytes 152072 | tf_op jit(solution)/shard_map/ppermute | solution.py:392
  80.3 1.8 %collective-permute-done.25 = bf16[152,384]{1,0:T(8,128)(2,1)S(1)} collective-permute-done((bf16[152,384]{1,0:T(8,128)(2,1)S(1)}, bf16[152,384]{1,0:T(8,128)(2,1)S(1)}, u32[]{:S(2)}, u32[]{:S(2)}) %collective-permute-start.25) | collective-permute-done | bytes 116768 | tf_op jit(solution)/shard_map/ppermute | solution.py:422
  82.1 1.0 %collective-permute-done.27 = bf16[22,3,384]{2,1,0:T(4,128)(2,1)S(1)} collective-permute-done((bf16[22,3,384]{2,1,0:T(4,128)(2,1)S(1)}, bf16[22,3,384]{2,1,0:T(4,128)(2,1)S(1)}, u32[]{:S(2)}, u32[]{:S(2)}) %collective-permute-start.27) | collective-permute-done | bytes 50720 | tf_op jit(solution)/shard_map/ppermute | solution.py:408
  84.1 2.5 %last.1 = bf16[256,384]{1,0:T(8,128)(2,1)} custom-call(bf16[22,32,384]{2,1,0:T(8,128)(2,1)S(1)} %fusion.18.dzpad, bf16[256,384]{1,0:T(8,128)(2,1)S(1)} %get-tuple-element.233.gmid, f32[49,2,384]{2,1,0:T(2,128)S(1)} %bitcast.97), custom_call_target="tpu_custom_call" | custom-call | tf_op jit(solution)/shard_map/last/pallas_call | solution.py:370
  86.6 1.3 %small.1 = (f32[49,2,384]{2,1,0:T(2,128)}, f32[2,384]{1,0:T(2,128)}, f32[2,384]{1,0:T(2,128)}, f32[2,1536]{1,0:T(2,128)}) custom-call(s32[6]{0:T(128)S(1)} %stack.29.place, bf16[56,384]{1,0:T(8,128)(2,1)S(1)} %add_convert_fusion.13.mine, bf16[56,384]{1,0:T(8,128)(2,1)S(1)} %collective-permute-done.29.got), custom_call_target="tpu_custom_call" | custom-call | tf_op jit(solution)/shard_map/small/pallas_call | solution.py:370
  87.8 2.7 %collective-permute-done.28 = bf16[96,384]{1,0:T(8,128)(2,1)S(1)} collective-permute-done((bf16[96,384]{1,0:T(8,128)(2,1)S(1)}, bf16[96,384]{1,0:T(8,128)(2,1)S(1)}, u32[]{:S(2)}, u32[]{:S(2)}) %collective-permute-start.28) | collective-permute-done | bytes 73760 | tf_op jit(solution)/shard_map/ppermute | solution.py:422
  (114 shorter events, 12.0 us)
Async XLA Ops:
  2.3 6.4 %collective-permute-start = (bf16[6,16,384]{2,1,0:T(8,128)(2,1)S(1)}, bf16[6,16,384]{2,1,0:T(8,128)(2,1)S(1)}, u32[]{:S(2)}, u32[]{:S(2)}) collective-permute-start(bf16[6,16,384]{2,1,0:T(8,128)(2,1)S(1)} %get-tuple-element.133), channel_id=1, source_target_pairs={{0,4},{4,0},{8,12},{12,8},{16,20},{20,16},{24,28},{28,24},{1,5},{5... | collective-permute-start | bytes 221192 | tf_op jit(solution)/shard_map/ppermute | solution.py:392
  5.3 3.4 %collective-permute-start.1 = (bf16[6,16,384]{2,1,0:T(8,128)(2,1)S(1)}, bf16[6,16,384]{2,1,0:T(8,128)(2,1)S(1)}, u32[]{:S(2)}, u32[]{:S(2)}) collective-permute-start(bf16[6,16,384]{2,1,0:T(8,128)(2,1)S(1)} %get-tuple-element.135), channel_id=1, source_target_pairs={{0,1},{1,0},{2,3},{3,2},{4,8},{5,9},{6,10},{7,11},{8,4},{9,5},{10,... | collective-permute-start | bytes 221192 | tf_op jit(solution)/shard_map/ppermute | solution.py:408
  8.9 5.9 %collective-permute-start.3 = (bf16[28,6,384]{2,1,0:T(8,128)(2,1)S(1)}, bf16[28,6,384]{2,1,0:T(8,128)(2,1)S(1)}, u32[]{:S(2)}, u32[]{:S(2)}) collective-permute-start(bf16[28,6,384]{2,1,0:T(8,128)(2,1)S(1)} %get-tuple-element.265), channel_id=1, source_target_pairs={{0,4},{1,2},{2,1},{3,7},{4,0},{5,6},{6,5},{7,3},{8,12},{9,10},{10,... | collective-permute-start | bytes 387080 | tf_op jit(solution)/shard_map/ppermute | solution.py:408
  11.4 3.4 %collective-permute-start.2 = (bf16[28,6,384]{2,1,0:T(8,128)(2,1)S(1)}, bf16[28,6,384]{2,1,0:T(8,128)(2,1)S(1)}, u32[]{:S(2)}, u32[]{:S(2)}) collective-permute-start(bf16[28,6,384]{2,1,0:T(8,128)(2,1)S(1)} %get-tuple-element.266), channel_id=1, source_target_pairs={{0,1},{1,0},{2,3},{3,2},{4,5},{5,4},{6,7},{7,6},{8,9},{9,8},{10,11... | collective-permute-start | bytes 387080 | tf_op jit(solution)/shard_map/ppermute | solution.py:392
  15.2 8.0 %copy-start.2 = (bf16[16,16,384]{2,1,0:T(8,128)(2,1)S(1)}, bf16[16,16,384]{2,1,0:T(8,128)(2,1)}, u32[]{:S(2)}) copy-start(bf16[16,16,384]{2,1,0:T(8,128)(2,1)} %param.9) | copy-start | bytes 589828
  23.3 8.6 %copy-start = (bf16[2,384,1536]{2,1,0:T(8,128)(2,1)S(1)}, bf16[2,384,1536]{2,1,0:T(8,128)(2,1)}, u32[]{:S(2)}) copy-start(bf16[2,384,1536]{2,1,0:T(8,128)(2,1)} %w_in.7) | copy-start | bytes 7077892
  29.5 7.9 %collective-permute-start.8 = (bf16[2,16,48,384]{3,2,1,0:T(8,128)(2,1)S(1)}, bf16[2,16,48,384]{3,2,1,0:T(8,128)(2,1)S(1)}, u32[]{:S(2)}, u32[]{:S(2)}) collective-permute-start(bf16[2,16,48,384]{3,2,1,0:T(8,128)(2,1)S(1)} %bitcast.110), channel_id=1, source_target_pairs={{0,1},{1,0},{2,3},{3,2},{4,5},{5,4},{6,7},{7,6},{8,9},{9,8},{10,11... | collective-permute-start | bytes 3538952 | tf_op jit(solution)/shard_map/ppermute | solution.py:422
  29.6 4.6 %collective-permute-start.4 = (bf16[3,16,384]{2,1,0:T(8,128)(2,1)S(1)}, bf16[3,16,384]{2,1,0:T(8,128)(2,1)S(1)}, u32[]{:S(2)}, u32[]{:S(2)}) collective-permute-start(bf16[3,16,384]{2,1,0:T(8,128)(2,1)S(1)} %bitcast.141), channel_id=1, source_target_pairs={{0,4},{4,0},{8,12},{12,8},{16,20},{20,16},{24,28},{28,24},{1,5},{5... | collective-permute-start | bytes 110600 | tf_op jit(solution)/shard_map/ppermute | solution.py:392
  31.6 2.5 %collective-permute-start.5 = (bf16[3,16,384]{2,1,0:T(8,128)(2,1)S(1)}, bf16[3,16,384]{2,1,0:T(8,128)(2,1)S(1)}, u32[]{:S(2)}, u32[]{:S(2)}) collective-permute-start(bf16[3,16,384]{2,1,0:T(8,128)(2,1)S(1)} %bitcast.140), channel_id=1, source_target_pairs={{0,1},{1,0},{2,3},{3,2},{4,8},{5,9},{6,10},{7,11},{8,4},{9,5},{10,... | collective-permute-start | bytes 110600 | tf_op jit(solution)/shard_map/ppermute | solution.py:408
  34.3 7.0 %collective-permute-start.7 = (bf16[22,3,384]{2,1,0:T(4,128)(2,1)S(1)}, bf16[22,3,384]{2,1,0:T(4,128)(2,1)S(1)}, u32[]{:S(2)}, u32[]{:S(2)}) collective-permute-start(bf16[22,3,384]{2,1,0:T(4,128)(2,1)S(1)} %get-tuple-element.281), channel_id=1, source_target_pairs={{0,4},{1,2},{2,1},{3,7},{4,0},{5,6},{6,5},{7,3},{8,12},{9,10},{10,... | collective-permute-start | bytes 152072 | tf_op jit(solution)/shard_map/ppermute | solution.py:408
  37.3 4.0 %collective-permute-start.6 = (bf16[22,3,384]{2,1,0:T(4,128)(2,1)S(1)}, bf16[22,3,384]{2,1,0:T(4,128)(2,1)S(1)}, u32[]{:S(2)}, u32[]{:S(2)}) collective-permute-start(bf16[22,3,384]{2,1,0:T(4,128)(2,1)S(1)} %get-tuple-element.282), channel_id=1, source_target_pairs={{0,1},{1,0},{2,3},{3,2},{4,5},{5,4},{6,7},{7,6},{8,9},{9,8},{10,11... | collective-permute-start | bytes 152072 | tf_op jit(solution)/shard_map/ppermute | solution.py:392
  37.9 9.5 %collective-permute-start.10 = (bf16[1,4,2,48,384]{4,3,2,1,0:T(8,128)(2,1)S(1)}, bf16[1,4,2,48,384]{4,3,2,1,0:T(8,128)(2,1)S(1)}, u32[]{:S(2)}, u32[]{:S(2)}) collective-permute-start(bf16[1,4,2,48,384]{4,3,2,1,0:T(8,128)(2,1)S(1)} %get-tuple-element.259), channel_id=1, source_target_pairs={{0,4},{1,5},{2,6},{3,7},{4,0},{5,1},{6,2},{7,3},{8,12},{9,13},{10,... | collective-permute-start | bytes 884744 | tf_op jit(solution)/shard_map/ppermute | solution.py:422
  39.0 8.7 %collective-permute-start.9 = (bf16[1,8,1,48,384]{4,3,1,2,0:T(8,128)(2,1)S(1)}, bf16[1,8,1,48,384]{4,3,1,2,0:T(8,128)(2,1)S(1)}, u32[]{:S(2)}, u32[]{:S(2)}) collective-permute-start(bf16[1,8,1,48,384]{4,3,1,2,0:T(8,128)(2,1)S(1)} %get-tuple-element.261), channel_id=1, source_target_pairs={{0,2},{1,3},{2,0},{3,1},{4,6},{5,7},{6,4},{7,5},{8,10},{9,11},{10,... | collective-permute-start | bytes 884744 | tf_op jit(solution)/shard_map/ppermute | solution.py:422
  47.7 5.6 %collective-permute-start.11 = (bf16[2,16,48,384]{3,2,1,0:T(8,128)(2,1)S(1)}, bf16[2,16,48,384]{3,2,1,0:T(8,128)(2,1)S(1)}, u32[]{:S(2)}, u32[]{:S(2)}) collective-permute-start(bf16[2,16,48,384]{3,2,1,0:T(8,128)(2,1)S(1)} %bitcast.109), channel_id=1, source_target_pairs={{0,1},{1,0},{2,3},{3,2},{4,5},{5,4},{6,7},{7,6},{8,9},{9,8},{10,11... | collective-permute-start | bytes 3538952 | tf_op jit(solution)/shard_map/ppermute | solution.py:422
  49.9 3.5 %collective-permute-start.12 = (bf16[56,384]{1,0:T(8,128)(2,1)S(1)}, bf16[56,384]{1,0:T(8,128)(2,1)S(1)}, u32[]{:S(2)}, u32[]{:S(2)}) collective-permute-start(bf16[56,384]{1,0:T(8,128)(2,1)S(1)} %get-tuple-element.186), channel_id=1, source_target_pairs={{0,1},{1,0},{2,3},{3,2},{4,5},{5,4},{6,7},{7,6},{8,9},{9,8},{10,11... | collective-permute-start | bytes 129032 | tf_op jit(solution)/shard_map/ppermute | solution.py:422
  50.7 9.8 %collective-permute-start.15 = (bf16[384,384]{1,0:T(8,128)(2,1)S(1)}, bf16[384,384]{1,0:T(8,128)(2,1)S(1)}, u32[]{:S(2)}, u32[]{:S(2)}) collective-permute-start(bf16[384,384]{1,0:T(8,128)(2,1)S(1)} %pad_maximum_fusion.1), channel_id=1, source_target_pairs={{0,8},{1,9},{2,10},{3,11},{4,12},{5,13},{6,14},{7,15},{8,0},{9,1},... | collective-permute-start | bytes 884744 | tf_op jit(solution)/shard_map/ppermute | solution.py:422
  53.9 11.8 %collective-permute-start.14 = (bf16[1,4,2,48,384]{4,3,2,1,0:T(8,128)(2,1)S(1)}, bf16[1,4,2,48,384]{4,3,2,1,0:T(8,128)(2,1)S(1)}, u32[]{:S(2)}, u32[]{:S(2)}) collective-permute-start(bf16[1,4,2,48,384]{4,3,2,1,0:T(8,128)(2,1)S(1)} %get-tuple-element.255), channel_id=1, source_target_pairs={{0,4},{1,5},{2,6},{3,7},{4,0},{5,1},{6,2},{7,3},{8,12},{9,13},{10,... | collective-permute-start | bytes 884744 | tf_op jit(solution)/shard_map/ppermute | solution.py:422
  55.4 10.3 %collective-permute-start.13 = (bf16[1,8,1,48,384]{4,3,1,2,0:T(8,128)(2,1)S(1)}, bf16[1,8,1,48,384]{4,3,1,2,0:T(8,128)(2,1)S(1)}, u32[]{:S(2)}, u32[]{:S(2)}) collective-permute-start(bf16[1,8,1,48,384]{4,3,1,2,0:T(8,128)(2,1)S(1)} %get-tuple-element.257), channel_id=1, source_target_pairs={{0,2},{1,3},{2,0},{3,1},{4,6},{5,7},{6,4},{7,5},{8,10},{9,11},{10,... | collective-permute-start | bytes 884744 | tf_op jit(solution)/shard_map/ppermute | solution.py:422
  55.7 9.6 %collective-permute-start.18 = (bf16[56,384]{1,0:T(8,128)(2,1)S(1)}, bf16[56,384]{1,0:T(8,128)(2,1)S(1)}, u32[]{:S(2)}, u32[]{:S(2)}) collective-permute-start(bf16[56,384]{1,0:T(8,128)(2,1)S(1)} %add_convert_fusion.16), channel_id=1, source_target_pairs={{0,6},{1,7},{2,4},{3,5},{4,2},{5,3},{6,0},{7,1},{8,14},{9,15},{10,... | collective-permute-start | bytes 129032 | tf_op jit(solution)/shard_map/ppermute | solution.py:422
  57.7 8.0 %collective-permute-start.17 = (bf16[56,384]{1,0:T(8,128)(2,1)S(1)}, bf16[56,384]{1,0:T(8,128)(2,1)S(1)}, u32[]{:S(2)}, u32[]{:S(2)}) collective-permute-start(bf16[56,384]{1,0:T(8,128)(2,1)S(1)} %add_convert_fusion.16), channel_id=1, source_target_pairs={{0,2},{1,3},{2,0},{3,1},{4,6},{5,7},{6,4},{7,5},{8,10},{9,11},{10,... | collective-permute-start | bytes 129032 | tf_op jit(solution)/shard_map/ppermute | solution.py:422
  60.6 5.1 %collective-permute-start.16 = (bf16[56,384]{1,0:T(8,128)(2,1)S(1)}, bf16[56,384]{1,0:T(8,128)(2,1)S(1)}, u32[]{:S(2)}, u32[]{:S(2)}) collective-permute-start(bf16[56,384]{1,0:T(8,128)(2,1)S(1)} %add_convert_fusion.16), channel_id=1, source_target_pairs={{0,4},{1,5},{2,6},{3,7},{4,0},{5,1},{6,2},{7,3},{8,12},{9,13},{10,... | collective-permute-start | bytes 129032 | tf_op jit(solution)/shard_map/ppermute | solution.py:422
  65.8 9.0 %collective-permute-start.23 = (bf16[56,384]{1,0:T(8,128)(2,1)S(1)}, bf16[56,384]{1,0:T(8,128)(2,1)S(1)}, u32[]{:S(2)}, u32[]{:S(2)}) collective-permute-start(bf16[56,384]{1,0:T(8,128)(2,1)S(1)} %add_convert_fusion.15), channel_id=1, source_target_pairs={{0,8},{1,9},{2,10},{3,11},{4,12},{5,13},{6,14},{7,15},{8,0},{9,1},... | collective-permute-start | bytes 129032 | tf_op jit(solution)/shard_map/ppermute | solution.py:422
  67.2 6.7 %collective-permute-start.19 = (bf16[288,384]{1,0:T(8,128)(2,1)S(1)}, bf16[288,384]{1,0:T(8,128)(2,1)S(1)}, u32[]{:S(2)}, u32[]{:S(2)}) collective-permute-start(bf16[288,384]{1,0:T(8,128)(2,1)S(1)} %pad_maximum_fusion.4), channel_id=1, source_target_pairs={{0,4},{1,5},{2,6},{3,7},{4,0},{5,1},{6,2},{7,3},{8,12},{9,13},{10,... | collective-permute-start | bytes 663560 | tf_op jit(solution)/shard_map/ppermute | solution.py:422
  68.8 6.0 %collective-permute-start.20 = (bf16[288,384]{1,0:T(8,128)(2,1)S(1)}, bf16[288,384]{1,0:T(8,128)(2,1)S(1)}, u32[]{:S(2)}, u32[]{:S(2)}) collective-permute-start(bf16[288,384]{1,0:T(8,128)(2,1)S(1)} %pad_maximum_fusion.5), channel_id=1, source_target_pairs={{0,2},{1,3},{2,0},{3,1},{4,6},{5,7},{6,4},{7,5},{8,10},{9,11},{10,... | collective-permute-start | bytes 663560 | tf_op jit(solution)/shard_map/ppermute | solution.py:422
  69.1 5.7 %collective-permute-start.21 = (bf16[3,16,384]{2,1,0:T(8,128)(2,1)S(1)}, bf16[3,16,384]{2,1,0:T(8,128)(2,1)S(1)}, u32[]{:S(2)}, u32[]{:S(2)}) collective-permute-start(bf16[3,16,384]{2,1,0:T(8,128)(2,1)S(1)} %bitcast.139), channel_id=1, source_target_pairs={{0,4},{4,0},{8,12},{12,8},{16,20},{20,16},{24,28},{28,24},{1,5},{5... | collective-permute-start | bytes 110600 | tf_op jit(solution)/shard_map/ppermute | solution.py:392
  69.9 4.9 %collective-permute-start.22 = (bf16[3,16,384]{2,1,0:T(8,128)(2,1)S(1)}, bf16[3,16,384]{2,1,0:T(8,128)(2,1)S(1)}, u32[]{:S(2)}, u32[]{:S(2)}) collective-permute-start(bf16[3,16,384]{2,1,0:T(8,128)(2,1)S(1)} %bitcast.138), channel_id=1, source_target_pairs={{0,1},{1,0},{2,3},{3,2},{4,8},{5,9},{6,10},{7,11},{8,4},{9,5},{10,... | collective-permute-start | bytes 110600 | tf_op jit(solution)/shard_map/ppermute | solution.py:408
  75.0 7.1 %collective-permute-start.25 = (bf16[152,384]{1,0:T(8,128)(2,1)S(1)}, bf16[152,384]{1,0:T(8,128)(2,1)S(1)}, u32[]{:S(2)}, u32[]{:S(2)}) collective-permute-start(bf16[152,384]{1,0:T(8,128)(2,1)S(1)} %pad_maximum_fusion.6), channel_id=1, source_target_pairs={{0,16},{1,17},{2,18},{3,19},{4,20},{5,21},{6,22},{7,23},{8,24},{9,... | collective-permute-start | bytes 350216 | tf_op jit(solution)/shard_map/ppermute | solution.py:422
  77.1 6.1 %collective-permute-start.24 = (bf16[192,384]{1,0:T(8,128)(2,1)S(1)}, bf16[192,384]{1,0:T(8,128)(2,1)S(1)}, u32[]{:S(2)}, u32[]{:S(2)}) collective-permute-start(bf16[192,384]{1,0:T(8,128)(2,1)S(1)} %bitcast.136), channel_id=1, source_target_pairs={{0,8},{1,9},{2,10},{3,11},{4,12},{5,13},{6,14},{7,15},{8,0},{9,1},... | collective-permute-start | bytes 442376 | tf_op jit(solution)/shard_map/ppermute | solution.py:422
  78.8 4.4 %collective-permute-start.27 = (bf16[22,3,384]{2,1,0:T(4,128)(2,1)S(1)}, bf16[22,3,384]{2,1,0:T(4,128)(2,1)S(1)}, u32[]{:S(2)}, u32[]{:S(2)}) collective-permute-start(bf16[22,3,384]{2,1,0:T(4,128)(2,1)S(1)} %get-tuple-element.279), channel_id=1, source_target_pairs={{0,4},{1,2},{2,1},{3,7},{4,0},{5,6},{6,5},{7,3},{8,12},{9,10},{10,... | collective-permute-start | bytes 152072 | tf_op jit(solution)/shard_map/ppermute | solution.py:408
  79.3 3.8 %collective-permute-start.26 = (bf16[22,3,384]{2,1,0:T(4,128)(2,1)S(1)}, bf16[22,3,384]{2,1,0:T(4,128)(2,1)S(1)}, u32[]{:S(2)}, u32[]{:S(2)}) collective-permute-start(bf16[22,3,384]{2,1,0:T(4,128)(2,1)S(1)} %get-tuple-element.280), channel_id=1, source_target_pairs={{0,1},{1,0},{2,3},{3,2},{4,5},{5,4},{6,7},{7,6},{8,9},{9,8},{10,11... | collective-permute-start | bytes 152072 | tf_op jit(solution)/shard_map/ppermute | solution.py:392
  83.3 3.2 %collective-permute-start.29 = (bf16[56,384]{1,0:T(8,128)(2,1)S(1)}, bf16[56,384]{1,0:T(8,128)(2,1)S(1)}, u32[]{:S(2)}, u32[]{:S(2)}) collective-permute-start(bf16[56,384]{1,0:T(8,128)(2,1)S(1)} %add_convert_fusion.13.mine), channel_id=1, source_target_pairs={{0,1},{1,0},{2,3},{3,2},{4,5},{5,4},{6,7},{7,6},{8,9},{9,8},{10,11... | collective-permute-start | bytes 129032 | tf_op jit(solution)/shard_map/ppermute | solution.py:422
  83.4 7.1 %collective-permute-start.28 = (bf16[96,384]{1,0:T(8,128)(2,1)S(1)}, bf16[96,384]{1,0:T(8,128)(2,1)S(1)}, u32[]{:S(2)}, u32[]{:S(2)}) collective-permute-start(bf16[96,384]{1,0:T(8,128)(2,1)S(1)} %bitcast.137), channel_id=1, source_target_pairs={{0,16},{1,17},{2,18},{3,19},{4,20},{5,21},{6,22},{7,23},{8,24},{9,... | collective-permute-start | bytes 221192 | tf_op jit(solution)/shard_map/ppermute | solution.py:422
  (5 other events, 26.3 us)

commit v17 on v16

--- a/solution.py
+++ b/solution.py
@@ -134,7 +134,7 @@
 
 
 def pixel_blocks(pixels):
-    best = max(d for d in range(16, 257, 16) if pixels % d == 0)
+    best = max(d for d in range(16, 129, 16) if pixels % d == 0)
     return [slice(start, start + best) for start in range(0, pixels, best)]
 
 

time: 91.4 us -> 91.6 us (level)
  no operation moved by 1% of the time
where the time goes in v17:
time: 91.6 us; the launch traced here: 91.4 us
  starting transfers between devices  30.4 us (33%)
  Pallas kernels  30 us (33%)
  waiting for transfers between devices  25.1 us (27%)
  other arithmetic  2.91 us (3%)
  local copies, waits for them, and re-layouts  1.89 us (2%)
  between operations  1.25 us (1%)
    pallas_call x11, Pallas kernels, run(): pl.pallas_call(kernel, out_shape=outs, in_specs=[vmem if s is None else p...  30 us
    ppermute x18, waiting for transfers between devices, flip_bit(): return lax.ppermute(value, both, [(i, i ^ flip) for i in range(total)])  17.3 us
    ppermute x18, starting transfers between devices, flip_bit(): return lax.ppermute(value, both, [(i, i ^ flip) for i in range(total)])  17.2 us
    ppermute x6, starting transfers between devices, to_twin(): lax.ppermute(edge, axis, [(i, i ^ 1) for i in range(count) if i ^ 1 < cou...  6.9 us
    ppermute x6, starting transfers between devices, to_other(): return lax.ppermute(edge, ('rows', 'cols'), pairs)  6.25 us
    ppermute x6, waiting for transfers between devices, to_other(): return lax.ppermute(edge, ('rows', 'cols'), pairs)  4.35 us
    ppermute x6, waiting for transfers between devices, to_twin(): lax.ppermute(edge, axis, [(i, i ^ 1) for i in range(count) if i ^ 1 < cou...  3.38 us
  transfers between devices with their start and end apart: 30, of which 13 were waited for; matrix products, arithmetic and copies ran while one was open for 3% of the time, Pallas kernels for 16%

profile of v17, /device:TPU:0, one launch (start us, length us, event | category | flops | bytes accessed | tf_op | source)
XLA Modules:
  0.0 91.4 jit_solution(13735706151927373285)
XLA Ops:
  2.3 3.0 %collective-permute-start = (bf16[6,16,384]{2,1,0:T(8,128)(2,1)S(1)}, bf16[6,16,384]{2,1,0:T(8,128)(2,1)S(1)}, u32[]{:S(2)}, u32[]{:S(2)}) collective-permute-start(bf16[6,16,384]{2,1,0:T(8,128)(2,1)S(1)} %get-tuple-element.133), channel_id=1, source_target_pairs={{0,4},{4,0},{8,12},{12,8},{16,20},{20,16},{24,28},{28,24},{1,5},{5... | collective-permute-start | bytes 221192 | tf_op jit(solution)/shard_map/ppermute | solution.py:392
  5.3 3.4 %collective-permute-done = bf16[6,16,384]{2,1,0:T(8,128)(2,1)S(1)} collective-permute-done((bf16[6,16,384]{2,1,0:T(8,128)(2,1)S(1)}, bf16[6,16,384]{2,1,0:T(8,128)(2,1)S(1)}, u32[]{:S(2)}, u32[]{:S(2)}) %collective-permute-start) | collective-permute-done | bytes 73760 | tf_op jit(solution)/shard_map/ppermute | solution.py:392
  8.9 2.5 %collective-permute-start.3 = (bf16[28,6,384]{2,1,0:T(8,128)(2,1)S(1)}, bf16[28,6,384]{2,1,0:T(8,128)(2,1)S(1)}, u32[]{:S(2)}, u32[]{:S(2)}) collective-permute-start(bf16[28,6,384]{2,1,0:T(8,128)(2,1)S(1)} %get-tuple-element.265), channel_id=1, source_target_pairs={{0,4},{1,2},{2,1},{3,7},{4,0},{5,6},{6,5},{7,3},{8,12},{9,10},{10,... | collective-permute-start | bytes 387080 | tf_op jit(solution)/shard_map/ppermute | solution.py:408
  11.4 3.4 %collective-permute-done.3 = bf16[28,6,384]{2,1,0:T(8,128)(2,1)S(1)} collective-permute-done((bf16[28,6,384]{2,1,0:T(8,128)(2,1)S(1)}, bf16[28,6,384]{2,1,0:T(8,128)(2,1)S(1)}, u32[]{:S(2)}, u32[]{:S(2)}) %collective-permute-start.3) | collective-permute-done | bytes 129056 | tf_op jit(solution)/shard_map/ppermute | solution.py:408
  15.2 8.0 %forward.1 = (f32[3,22,24,128]{3,2,1,0:T(8,128)S(1)}, f32[3,16,16,128]{3,2,1,0:T(8,128)S(1)}) custom-call(s32[6]{0:T(128)S(1)} %stack.29.place, bf16[28,32,384]{2,1,0:T(8,128)(2,1)S(1)} %fusion.12.xpad, f32[49,2,384]{2,1,0:T(2,128)S(1)} %bitcast.94, f32[2,384]{1,0:T(2,128)S(1)} %copy-done.5, f32[2,384]{1,0:T(2,128)S(1)} %copy-done.6, ...), custom_call_target="tpu_custom_call" | custom-call | tf_op jit(solution)/shard_map/forward/pallas_call | solution.py:370
  23.3 4.7 %top.1 = (bf16[256,384]{1,0:T(8,128)(2,1)S(1)}, bf16[256,384]{1,0:T(8,128)(2,1)S(1)}, bf16[256,1536]{1,0:T(8,128)(2,1)S(1)}, bf16[256,1536]{1,0:T(8,128)(2,1)S(1...) custom-call(f32[3,22,24,128]{3,2,1,0:T(8,128)S(1)} %get-tuple-element.154.mids, ...), custom_call_target="tpu_custom_call" | custom-call | tf_op jit(solution)/shard_map/top/pallas_call | solution.py:370
  28.0 1.6 %weights_top.1 = (bf16[2,768,384]{2,1,0:T(8,128)(2,1)S(1)}, bf16[2,768,384]{2,1,0:T(8,128)(2,1)S(1)}) custom-call(s32[6]{0:T(128)S(1)} %stack.29.place, bf16[256,384]{1,0:T(8,128)(2,1)S(1)} %get-tuple-element.149.normed, bf16[256,1536]{1,0:T(8,128)(2,1)S(1)} %get-tuple-element.150.act, bf16[256,1536]{1,0:T(8,128)(2,1)S(1)} %get-tuple-element.151.gpre, ...), custom_call_target="tpu_custom_call" | custom-call | tf_op jit(solution)/shard_map/weights_top/pallas_call | solution.py:370
  29.7 2.1 %collective-permute-start.4 = (bf16[3,16,384]{2,1,0:T(8,128)(2,1)S(1)}, bf16[3,16,384]{2,1,0:T(8,128)(2,1)S(1)}, u32[]{:S(2)}, u32[]{:S(2)}) collective-permute-start(bf16[3,16,384]{2,1,0:T(8,128)(2,1)S(1)} %bitcast.141), channel_id=1, source_target_pairs={{0,4},{4,0},{8,12},{12,8},{16,20},{20,16},{24,28},{28,24},{1,5},{5... | collective-permute-start | bytes 110600 | tf_op jit(solution)/shard_map/ppermute | solution.py:392
  32.0 2.3 %again.1 = (f32[256,384]{1,0:T(8,128)S(1)}, f32[256,128]{1,0:T(8,128)S(1)}, bf16[256,384]{1,0:T(8,128)(2,1)S(1)}, bf16[256,1536]{1,0:T(8,128)(2,1)S(1)}, f32[256,1536]{1,0:T(8,128)S(1)}) custom-call(f32[3,16,16,128]{3,2,1,0:T(8,128)S(1)} %get-tuple-element.140.z0, f32[2,384]{1,0:T(2,128)S(1)} %copy-done.5, f32[2,384]{1,0:T(2,128)S(1)} %copy-done.6, ...), custom_call_target="tpu_custom_call" | custom-call | tf_op jit(solution)/shard_map/again/pallas_call | solution.py:370
  34.5 3.0 %collective-permute-start.7 = (bf16[22,3,384]{2,1,0:T(4,128)(2,1)S(1)}, bf16[22,3,384]{2,1,0:T(4,128)(2,1)S(1)}, u32[]{:S(2)}, u32[]{:S(2)}) collective-permute-start(bf16[22,3,384]{2,1,0:T(4,128)(2,1)S(1)} %get-tuple-element.281), channel_id=1, source_target_pairs={{0,4},{1,2},{2,1},{3,7},{4,0},{5,6},{6,5},{7,3},{8,12},{9,10},{10,... | collective-permute-start | bytes 152072 | tf_op jit(solution)/shard_map/ppermute | solution.py:408
  38.0 1.1 %collective-permute-start.10 = (bf16[1,4,2,48,384]{4,3,2,1,0:T(8,128)(2,1)S(1)}, bf16[1,4,2,48,384]{4,3,2,1,0:T(8,128)(2,1)S(1)}, u32[]{:S(2)}, u32[]{:S(2)}) collective-permute-start(bf16[1,4,2,48,384]{4,3,2,1,0:T(8,128)(2,1)S(1)} %get-tuple-element.259), channel_id=1, source_target_pairs={{0,4},{1,5},{2,6},{3,7},{4,0},{5,1},{6,2},{7,3},{8,12},{9,13},{10,... | collective-permute-start | bytes 884744 | tf_op jit(solution)/shard_map/ppermute | solution.py:422
  39.8 1.7 %top_taps.1.sums1 = f32[56,384]{1,0:T(8,128)S(1)} custom-call(f32[3,22,24,128]{3,2,1,0:T(8,128)S(1)} %get-tuple-element.154.mids, bf16[256,384]{1,0:T(8,128)(2,1)S(1)} %get-tuple-element.139.dz, f32[1,1536]{1,0:T(1,128)S(1)} %get-tuple-element.155.db, f32[1,384]{1,0:T(1,128)S(1)} %get-tuple-element.156.dgain, f32[1,384]{1,0:T(1,128)S(1)} %get-tuple-element.157.dshift), custom_call_target="tpu_custom_call" | custom-call | tf_op jit(solution)/shard_map/top_taps/pallas_call | solution.py:370
  41.9 4.4 %low.1 = (bf16[256,384]{1,0:T(8,128)(2,1)S(1)}, bf16[256,384]{1,0:T(8,128)(2,1)S(1)}, f32[1,1536]{1,0:T(1,128)S(1)}, f32[1,384]{1,0:T(1,128)S(1)}, f32[1,384]{1,...) custom-call(s32[6]{0:T(128)S(1)} %stack.29.place, ...), custom_call_target="tpu_custom_call" | custom-call | tf_op jit(solution)/shard_map/low/pallas_call | solution.py:370
  46.3 1.2 %collective-permute-done.10 = bf16[1,4,2,48,384]{4,3,2,1,0:T(8,128)(2,1)S(1)} collective-permute-done((bf16[1,4,2,48,384]{4,3,2,1,0:T(8,128)(2,1)S(1)}, bf16[1,4,2,48,384]{4,3,2,1,0:T(8,128)(2,1)S(1)}, u32[]{:S(2)}, u32[]{:S(2)}) %collective-permute-start.10) | collective-permute-done | bytes 294944 | tf_op jit(solution)/shard_map/ppermute | solution.py:422
  47.9 2.1 %taps.1 = (bf16[56,384]{1,0:T(8,128)(2,1)S(1)}, bf16[56,384]{1,0:T(8,128)(2,1)S(1)}) custom-call(s32[6]{0:T(128)S(1)} %stack.29.place, bf16[28,32,384]{2,1,0:T(8,128)(2,1)S(1)} %fusion.12.xpad, bf16[256,384]{1,0:T(8,128)(2,1)S(1)} %get-tuple-element.206.dz, f32[1,1536]{1,0:T(1,128)S(1)} %get-tuple-element.181.db, f32[1,384]{1,0:T(1,128)S(1)} %get-tuple-element.182.dgain, ...), custom_call_target="tpu_custom_call" | custom-call | tf_op jit(solution)/shard_map/taps/pallas_call | solution.py:370
  50.9 2.6 %collective-permute-start.15 = (bf16[384,384]{1,0:T(8,128)(2,1)S(1)}, bf16[384,384]{1,0:T(8,128)(2,1)S(1)}, u32[]{:S(2)}, u32[]{:S(2)}) collective-permute-start(bf16[384,384]{1,0:T(8,128)(2,1)S(1)} %pad_maximum_fusion.1), channel_id=1, source_target_pairs={{0,8},{1,9},{2,10},{3,11},{4,12},{5,13},{6,14},{7,15},{8,0},{9,1},... | collective-permute-start | bytes 884744 | tf_op jit(solution)/shard_map/ppermute | solution.py:422
  54.1 1.4 %collective-permute-start.14 = (bf16[1,4,2,48,384]{4,3,2,1,0:T(8,128)(2,1)S(1)}, bf16[1,4,2,48,384]{4,3,2,1,0:T(8,128)(2,1)S(1)}, u32[]{:S(2)}, u32[]{:S(2)}) collective-permute-start(bf16[1,4,2,48,384]{4,3,2,1,0:T(8,128)(2,1)S(1)} %get-tuple-element.255), channel_id=1, source_target_pairs={{0,4},{1,5},{2,6},{3,7},{4,0},{5,1},{6,2},{7,3},{8,12},{9,13},{10,... | collective-permute-start | bytes 884744 | tf_op jit(solution)/shard_map/ppermute | solution.py:422
  55.9 1.9 %collective-permute-start.18 = (bf16[56,384]{1,0:T(8,128)(2,1)S(1)}, bf16[56,384]{1,0:T(8,128)(2,1)S(1)}, u32[]{:S(2)}, u32[]{:S(2)}) collective-permute-start(bf16[56,384]{1,0:T(8,128)(2,1)S(1)} %add_convert_fusion.16), channel_id=1, source_target_pairs={{0,6},{1,7},{2,4},{3,5},{4,2},{5,3},{6,0},{7,1},{8,14},{9,15},{10,... | collective-permute-start | bytes 129032 | tf_op jit(solution)/shard_map/ppermute | solution.py:422
  58.2 2.6 %collective-permute-done.15 = bf16[384,384]{1,0:T(8,128)(2,1)S(1)} collective-permute-done((bf16[384,384]{1,0:T(8,128)(2,1)S(1)}, bf16[384,384]{1,0:T(8,128)(2,1)S(1)}, u32[]{:S(2)}, u32[]{:S(2)}) %collective-permute-start.15) | collective-permute-done | bytes 294944 | tf_op jit(solution)/shard_map/ppermute | solution.py:422
  60.7 1.4 %collective-permute-start.16 = (bf16[56,384]{1,0:T(8,128)(2,1)S(1)}, bf16[56,384]{1,0:T(8,128)(2,1)S(1)}, u32[]{:S(2)}, u32[]{:S(2)}) collective-permute-start(bf16[56,384]{1,0:T(8,128)(2,1)S(1)} %add_convert_fusion.16), channel_id=1, source_target_pairs={{0,4},{1,5},{2,6},{3,7},{4,0},{5,1},{6,2},{7,3},{8,12},{9,13},{10,... | collective-permute-start | bytes 129032 | tf_op jit(solution)/shard_map/ppermute | solution.py:422
  62.1 3.4 %collective-permute-done.18 = bf16[56,384]{1,0:T(8,128)(2,1)S(1)} collective-permute-done((bf16[56,384]{1,0:T(8,128)(2,1)S(1)}, bf16[56,384]{1,0:T(8,128)(2,1)S(1)}, u32[]{:S(2)}, u32[]{:S(2)}) %collective-permute-start.18) | collective-permute-done | bytes 43040 | tf_op jit(solution)/shard_map/ppermute | solution.py:422
  66.0 1.2 %collective-permute-start.23 = (bf16[56,384]{1,0:T(8,128)(2,1)S(1)}, bf16[56,384]{1,0:T(8,128)(2,1)S(1)}, u32[]{:S(2)}, u32[]{:S(2)}) collective-permute-start(bf16[56,384]{1,0:T(8,128)(2,1)S(1)} %add_convert_fusion.15), channel_id=1, source_target_pairs={{0,8},{1,9},{2,10},{3,11},{4,12},{5,13},{6,14},{7,15},{8,0},{9,1},... | collective-permute-start | bytes 129032 | tf_op jit(solution)/shard_map/ppermute | solution.py:422
  67.4 1.4 %collective-permute-start.19 = (bf16[288,384]{1,0:T(8,128)(2,1)S(1)}, bf16[288,384]{1,0:T(8,128)(2,1)S(1)}, u32[]{:S(2)}, u32[]{:S(2)}) collective-permute-start(bf16[288,384]{1,0:T(8,128)(2,1)S(1)} %pad_maximum_fusion.4), channel_id=1, source_target_pairs={{0,4},{1,5},{2,6},{3,7},{4,0},{5,1},{6,2},{7,3},{8,12},{9,13},{10,... | collective-permute-start | bytes 663560 | tf_op jit(solution)/shard_map/ppermute | solution.py:422
  70.1 4.0 %collective-permute-done.19 = bf16[288,384]{1,0:T(8,128)(2,1)S(1)} collective-permute-done((bf16[288,384]{1,0:T(8,128)(2,1)S(1)}, bf16[288,384]{1,0:T(8,128)(2,1)S(1)}, u32[]{:S(2)}, u32[]{:S(2)}) %collective-permute-start.19) | collective-permute-done | bytes 221216 | tf_op jit(solution)/shard_map/ppermute | solution.py:422
  75.2 1.9 %collective-permute-start.25 = (bf16[152,384]{1,0:T(8,128)(2,1)S(1)}, bf16[152,384]{1,0:T(8,128)(2,1)S(1)}, u32[]{:S(2)}, u32[]{:S(2)}) collective-permute-start(bf16[152,384]{1,0:T(8,128)(2,1)S(1)} %pad_maximum_fusion.6), channel_id=1, source_target_pairs={{0,16},{1,17},{2,18},{3,19},{4,20},{5,21},{6,22},{7,23},{8,24},{9,... | collective-permute-start | bytes 350216 | tf_op jit(solution)/shard_map/ppermute | solution.py:422
  77.2 1.5 %collective-permute-start.24 = (bf16[192,384]{1,0:T(8,128)(2,1)S(1)}, bf16[192,384]{1,0:T(8,128)(2,1)S(1)}, u32[]{:S(2)}, u32[]{:S(2)}) collective-permute-start(bf16[192,384]{1,0:T(8,128)(2,1)S(1)} %bitcast.136), channel_id=1, source_target_pairs={{0,8},{1,9},{2,10},{3,11},{4,12},{5,13},{6,14},{7,15},{8,0},{9,1},... | collective-permute-start | bytes 442376 | tf_op jit(solution)/shard_map/ppermute | solution.py:422
  79.4 1.0 %collective-permute-start.26 = (bf16[22,3,384]{2,1,0:T(4,128)(2,1)S(1)}, bf16[22,3,384]{2,1,0:T(4,128)(2,1)S(1)}, u32[]{:S(2)}, u32[]{:S(2)}) collective-permute-start(bf16[22,3,384]{2,1,0:T(4,128)(2,1)S(1)} %get-tuple-element.280), channel_id=1, source_target_pairs={{0,1},{1,0},{2,3},{3,2},{4,5},{5,4},{6,7},{7,6},{8,9},{9,8},{10,11... | collective-permute-start | bytes 152072 | tf_op jit(solution)/shard_map/ppermute | solution.py:392
  80.5 1.8 %collective-permute-done.25 = bf16[152,384]{1,0:T(8,128)(2,1)S(1)} collective-permute-done((bf16[152,384]{1,0:T(8,128)(2,1)S(1)}, bf16[152,384]{1,0:T(8,128)(2,1)S(1)}, u32[]{:S(2)}, u32[]{:S(2)}) %collective-permute-start.25) | collective-permute-done | bytes 116768 | tf_op jit(solution)/shard_map/ppermute | solution.py:422
  82.3 1.0 %collective-permute-done.27 = bf16[22,3,384]{2,1,0:T(4,128)(2,1)S(1)} collective-permute-done((bf16[22,3,384]{2,1,0:T(4,128)(2,1)S(1)}, bf16[22,3,384]{2,1,0:T(4,128)(2,1)S(1)}, u32[]{:S(2)}, u32[]{:S(2)}) %collective-permute-start.27) | collective-permute-done | bytes 50720 | tf_op jit(solution)/shard_map/ppermute | solution.py:408
  84.2 2.5 %last.1 = bf16[256,384]{1,0:T(8,128)(2,1)} custom-call(bf16[22,32,384]{2,1,0:T(8,128)(2,1)S(1)} %fusion.18.dzpad, bf16[256,384]{1,0:T(8,128)(2,1)S(1)} %get-tuple-element.233.gmid, f32[49,2,384]{2,1,0:T(2,128)S(1)} %bitcast.97), custom_call_target="tpu_custom_call" | custom-call | tf_op jit(solution)/shard_map/last/pallas_call | solution.py:370
  86.7 1.3 %small.1 = (f32[49,2,384]{2,1,0:T(2,128)}, f32[2,384]{1,0:T(2,128)}, f32[2,384]{1,0:T(2,128)}, f32[2,1536]{1,0:T(2,128)}) custom-call(s32[6]{0:T(128)S(1)} %stack.29.place, bf16[56,384]{1,0:T(8,128)(2,1)S(1)} %add_convert_fusion.13.mine, bf16[56,384]{1,0:T(8,128)(2,1)S(1)} %collective-permute-done.29.got), custom_call_target="tpu_custom_call" | custom-call | tf_op jit(solution)/shard_map/small/pallas_call | solution.py:370
  88.0 2.7 %collective-permute-done.28 = bf16[96,384]{1,0:T(8,128)(2,1)S(1)} collective-permute-done((bf16[96,384]{1,0:T(8,128)(2,1)S(1)}, bf16[96,384]{1,0:T(8,128)(2,1)S(1)}, u32[]{:S(2)}, u32[]{:S(2)}) %collective-permute-start.28) | collective-permute-done | bytes 73760 | tf_op jit(solution)/shard_map/ppermute | solution.py:422
  (114 shorter events, 12.1 us)
Async XLA Ops:
  2.3 6.4 %collective-permute-start = (bf16[6,16,384]{2,1,0:T(8,128)(2,1)S(1)}, bf16[6,16,384]{2,1,0:T(8,128)(2,1)S(1)}, u32[]{:S(2)}, u32[]{:S(2)}) collective-permute-start(bf16[6,16,384]{2,1,0:T(8,128)(2,1)S(1)} %get-tuple-element.133), channel_id=1, source_target_pairs={{0,4},{4,0},{8,12},{12,8},{16,20},{20,16},{24,28},{28,24},{1,5},{5... | collective-permute-start | bytes 221192 | tf_op jit(solution)/shard_map/ppermute | solution.py:392
  5.3 3.4 %collective-permute-start.1 = (bf16[6,16,384]{2,1,0:T(8,128)(2,1)S(1)}, bf16[6,16,384]{2,1,0:T(8,128)(2,1)S(1)}, u32[]{:S(2)}, u32[]{:S(2)}) collective-permute-start(bf16[6,16,384]{2,1,0:T(8,128)(2,1)S(1)} %get-tuple-element.135), channel_id=1, source_target_pairs={{0,1},{1,0},{2,3},{3,2},{4,8},{5,9},{6,10},{7,11},{8,4},{9,5},{10,... | collective-permute-start | bytes 221192 | tf_op jit(solution)/shard_map/ppermute | solution.py:408
  8.9 5.9 %collective-permute-start.3 = (bf16[28,6,384]{2,1,0:T(8,128)(2,1)S(1)}, bf16[28,6,384]{2,1,0:T(8,128)(2,1)S(1)}, u32[]{:S(2)}, u32[]{:S(2)}) collective-permute-start(bf16[28,6,384]{2,1,0:T(8,128)(2,1)S(1)} %get-tuple-element.265), channel_id=1, source_target_pairs={{0,4},{1,2},{2,1},{3,7},{4,0},{5,6},{6,5},{7,3},{8,12},{9,10},{10,... | collective-permute-start | bytes 387080 | tf_op jit(solution)/shard_map/ppermute | solution.py:408
  11.4 3.4 %collective-permute-start.2 = (bf16[28,6,384]{2,1,0:T(8,128)(2,1)S(1)}, bf16[28,6,384]{2,1,0:T(8,128)(2,1)S(1)}, u32[]{:S(2)}, u32[]{:S(2)}) collective-permute-start(bf16[28,6,384]{2,1,0:T(8,128)(2,1)S(1)} %get-tuple-element.266), channel_id=1, source_target_pairs={{0,1},{1,0},{2,3},{3,2},{4,5},{5,4},{6,7},{7,6},{8,9},{9,8},{10,11... | collective-permute-start | bytes 387080 | tf_op jit(solution)/shard_map/ppermute | solution.py:392
  15.2 8.1 %copy-start.2 = (bf16[16,16,384]{2,1,0:T(8,128)(2,1)S(1)}, bf16[16,16,384]{2,1,0:T(8,128)(2,1)}, u32[]{:S(2)}) copy-start(bf16[16,16,384]{2,1,0:T(8,128)(2,1)} %param.9) | copy-start | bytes 589828
  23.3 8.7 %copy-start = (bf16[2,384,1536]{2,1,0:T(8,128)(2,1)S(1)}, bf16[2,384,1536]{2,1,0:T(8,128)(2,1)}, u32[]{:S(2)}) copy-start(bf16[2,384,1536]{2,1,0:T(8,128)(2,1)} %w_in.7) | copy-start | bytes 7077892
  29.6 7.9 %collective-permute-start.8 = (bf16[2,16,48,384]{3,2,1,0:T(8,128)(2,1)S(1)}, bf16[2,16,48,384]{3,2,1,0:T(8,128)(2,1)S(1)}, u32[]{:S(2)}, u32[]{:S(2)}) collective-permute-start(bf16[2,16,48,384]{3,2,1,0:T(8,128)(2,1)S(1)} %bitcast.110), channel_id=1, source_target_pairs={{0,1},{1,0},{2,3},{3,2},{4,5},{5,4},{6,7},{7,6},{8,9},{9,8},{10,11... | collective-permute-start | bytes 3538952 | tf_op jit(solution)/shard_map/ppermute | solution.py:422
  29.7 4.6 %collective-permute-start.4 = (bf16[3,16,384]{2,1,0:T(8,128)(2,1)S(1)}, bf16[3,16,384]{2,1,0:T(8,128)(2,1)S(1)}, u32[]{:S(2)}, u32[]{:S(2)}) collective-permute-start(bf16[3,16,384]{2,1,0:T(8,128)(2,1)S(1)} %bitcast.141), channel_id=1, source_target_pairs={{0,4},{4,0},{8,12},{12,8},{16,20},{20,16},{24,28},{28,24},{1,5},{5... | collective-permute-start | bytes 110600 | tf_op jit(solution)/shard_map/ppermute | solution.py:392
  31.8 2.5 %collective-permute-start.5 = (bf16[3,16,384]{2,1,0:T(8,128)(2,1)S(1)}, bf16[3,16,384]{2,1,0:T(8,128)(2,1)S(1)}, u32[]{:S(2)}, u32[]{:S(2)}) collective-permute-start(bf16[3,16,384]{2,1,0:T(8,128)(2,1)S(1)} %bitcast.140), channel_id=1, source_target_pairs={{0,1},{1,0},{2,3},{3,2},{4,8},{5,9},{6,10},{7,11},{8,4},{9,5},{10,... | collective-permute-start | bytes 110600 | tf_op jit(solution)/shard_map/ppermute | solution.py:408
  34.5 7.0 %collective-permute-start.7 = (bf16[22,3,384]{2,1,0:T(4,128)(2,1)S(1)}, bf16[22,3,384]{2,1,0:T(4,128)(2,1)S(1)}, u32[]{:S(2)}, u32[]{:S(2)}) collective-permute-start(bf16[22,3,384]{2,1,0:T(4,128)(2,1)S(1)} %get-tuple-element.281), channel_id=1, source_target_pairs={{0,4},{1,2},{2,1},{3,7},{4,0},{5,6},{6,5},{7,3},{8,12},{9,10},{10,... | collective-permute-start | bytes 152072 | tf_op jit(solution)/shard_map/ppermute | solution.py:408
  37.5 4.0 %collective-permute-start.6 = (bf16[22,3,384]{2,1,0:T(4,128)(2,1)S(1)}, bf16[22,3,384]{2,1,0:T(4,128)(2,1)S(1)}, u32[]{:S(2)}, u32[]{:S(2)}) collective-permute-start(bf16[22,3,384]{2,1,0:T(4,128)(2,1)S(1)} %get-tuple-element.282), channel_id=1, source_target_pairs={{0,1},{1,0},{2,3},{3,2},{4,5},{5,4},{6,7},{7,6},{8,9},{9,8},{10,11... | collective-permute-start | bytes 152072 | tf_op jit(solution)/shard_map/ppermute | solution.py:392
  38.0 9.5 %collective-permute-start.10 = (bf16[1,4,2,48,384]{4,3,2,1,0:T(8,128)(2,1)S(1)}, bf16[1,4,2,48,384]{4,3,2,1,0:T(8,128)(2,1)S(1)}, u32[]{:S(2)}, u32[]{:S(2)}) collective-permute-start(bf16[1,4,2,48,384]{4,3,2,1,0:T(8,128)(2,1)S(1)} %get-tuple-element.259), channel_id=1, source_target_pairs={{0,4},{1,5},{2,6},{3,7},{4,0},{5,1},{6,2},{7,3},{8,12},{9,13},{10,... | collective-permute-start | bytes 884744 | tf_op jit(solution)/shard_map/ppermute | solution.py:422
  39.2 8.7 %collective-permute-start.9 = (bf16[1,8,1,48,384]{4,3,1,2,0:T(8,128)(2,1)S(1)}, bf16[1,8,1,48,384]{4,3,1,2,0:T(8,128)(2,1)S(1)}, u32[]{:S(2)}, u32[]{:S(2)}) collective-permute-start(bf16[1,8,1,48,384]{4,3,1,2,0:T(8,128)(2,1)S(1)} %get-tuple-element.261), channel_id=1, source_target_pairs={{0,2},{1,3},{2,0},{3,1},{4,6},{5,7},{6,4},{7,5},{8,10},{9,11},{10,... | collective-permute-start | bytes 884744 | tf_op jit(solution)/shard_map/ppermute | solution.py:422
  47.9 5.6 %collective-permute-start.11 = (bf16[2,16,48,384]{3,2,1,0:T(8,128)(2,1)S(1)}, bf16[2,16,48,384]{3,2,1,0:T(8,128)(2,1)S(1)}, u32[]{:S(2)}, u32[]{:S(2)}) collective-permute-start(bf16[2,16,48,384]{3,2,1,0:T(8,128)(2,1)S(1)} %bitcast.109), channel_id=1, source_target_pairs={{0,1},{1,0},{2,3},{3,2},{4,5},{5,4},{6,7},{7,6},{8,9},{9,8},{10,11... | collective-permute-start | bytes 3538952 | tf_op jit(solution)/shard_map/ppermute | solution.py:422
  50.0 3.5 %collective-permute-start.12 = (bf16[56,384]{1,0:T(8,128)(2,1)S(1)}, bf16[56,384]{1,0:T(8,128)(2,1)S(1)}, u32[]{:S(2)}, u32[]{:S(2)}) collective-permute-start(bf16[56,384]{1,0:T(8,128)(2,1)S(1)} %get-tuple-element.186), channel_id=1, source_target_pairs={{0,1},{1,0},{2,3},{3,2},{4,5},{5,4},{6,7},{7,6},{8,9},{9,8},{10,11... | collective-permute-start | bytes 129032 | tf_op jit(solution)/shard_map/ppermute | solution.py:422
  50.9 9.8 %collective-permute-start.15 = (bf16[384,384]{1,0:T(8,128)(2,1)S(1)}, bf16[384,384]{1,0:T(8,128)(2,1)S(1)}, u32[]{:S(2)}, u32[]{:S(2)}) collective-permute-start(bf16[384,384]{1,0:T(8,128)(2,1)S(1)} %pad_maximum_fusion.1), channel_id=1, source_target_pairs={{0,8},{1,9},{2,10},{3,11},{4,12},{5,13},{6,14},{7,15},{8,0},{9,1},... | collective-permute-start | bytes 884744 | tf_op jit(solution)/shard_map/ppermute | solution.py:422
  54.1 11.8 %collective-permute-start.14 = (bf16[1,4,2,48,384]{4,3,2,1,0:T(8,128)(2,1)S(1)}, bf16[1,4,2,48,384]{4,3,2,1,0:T(8,128)(2,1)S(1)}, u32[]{:S(2)}, u32[]{:S(2)}) collective-permute-start(bf16[1,4,2,48,384]{4,3,2,1,0:T(8,128)(2,1)S(1)} %get-tuple-element.255), channel_id=1, source_target_pairs={{0,4},{1,5},{2,6},{3,7},{4,0},{5,1},{6,2},{7,3},{8,12},{9,13},{10,... | collective-permute-start | bytes 884744 | tf_op jit(solution)/shard_map/ppermute | solution.py:422
  55.5 10.3 %collective-permute-start.13 = (bf16[1,8,1,48,384]{4,3,1,2,0:T(8,128)(2,1)S(1)}, bf16[1,8,1,48,384]{4,3,1,2,0:T(8,128)(2,1)S(1)}, u32[]{:S(2)}, u32[]{:S(2)}) collective-permute-start(bf16[1,8,1,48,384]{4,3,1,2,0:T(8,128)(2,1)S(1)} %get-tuple-element.257), channel_id=1, source_target_pairs={{0,2},{1,3},{2,0},{3,1},{4,6},{5,7},{6,4},{7,5},{8,10},{9,11},{10,... | collective-permute-start | bytes 884744 | tf_op jit(solution)/shard_map/ppermute | solution.py:422
  55.9 9.5 %collective-permute-start.18 = (bf16[56,384]{1,0:T(8,128)(2,1)S(1)}, bf16[56,384]{1,0:T(8,128)(2,1)S(1)}, u32[]{:S(2)}, u32[]{:S(2)}) collective-permute-start(bf16[56,384]{1,0:T(8,128)(2,1)S(1)} %add_convert_fusion.16), channel_id=1, source_target_pairs={{0,6},{1,7},{2,4},{3,5},{4,2},{5,3},{6,0},{7,1},{8,14},{9,15},{10,... | collective-permute-start | bytes 129032 | tf_op jit(solution)/shard_map/ppermute | solution.py:422
  57.8 8.0 %collective-permute-start.17 = (bf16[56,384]{1,0:T(8,128)(2,1)S(1)}, bf16[56,384]{1,0:T(8,128)(2,1)S(1)}, u32[]{:S(2)}, u32[]{:S(2)}) collective-permute-start(bf16[56,384]{1,0:T(8,128)(2,1)S(1)} %add_convert_fusion.16), channel_id=1, source_target_pairs={{0,2},{1,3},{2,0},{3,1},{4,6},{5,7},{6,4},{7,5},{8,10},{9,11},{10,... | collective-permute-start | bytes 129032 | tf_op jit(solution)/shard_map/ppermute | solution.py:422
  60.7 5.1 %collective-permute-start.16 = (bf16[56,384]{1,0:T(8,128)(2,1)S(1)}, bf16[56,384]{1,0:T(8,128)(2,1)S(1)}, u32[]{:S(2)}, u32[]{:S(2)}) collective-permute-start(bf16[56,384]{1,0:T(8,128)(2,1)S(1)} %add_convert_fusion.16), channel_id=1, source_target_pairs={{0,4},{1,5},{2,6},{3,7},{4,0},{5,1},{6,2},{7,3},{8,12},{9,13},{10,... | collective-permute-start | bytes 129032 | tf_op jit(solution)/shard_map/ppermute | solution.py:422
  66.0 9.0 %collective-permute-start.23 = (bf16[56,384]{1,0:T(8,128)(2,1)S(1)}, bf16[56,384]{1,0:T(8,128)(2,1)S(1)}, u32[]{:S(2)}, u32[]{:S(2)}) collective-permute-start(bf16[56,384]{1,0:T(8,128)(2,1)S(1)} %add_convert_fusion.15), channel_id=1, source_target_pairs={{0,8},{1,9},{2,10},{3,11},{4,12},{5,13},{6,14},{7,15},{8,0},{9,1},... | collective-permute-start | bytes 129032 | tf_op jit(solution)/shard_map/ppermute | solution.py:422
  67.4 6.7 %collective-permute-start.19 = (bf16[288,384]{1,0:T(8,128)(2,1)S(1)}, bf16[288,384]{1,0:T(8,128)(2,1)S(1)}, u32[]{:S(2)}, u32[]{:S(2)}) collective-permute-start(bf16[288,384]{1,0:T(8,128)(2,1)S(1)} %pad_maximum_fusion.4), channel_id=1, source_target_pairs={{0,4},{1,5},{2,6},{3,7},{4,0},{5,1},{6,2},{7,3},{8,12},{9,13},{10,... | collective-permute-start | bytes 663560 | tf_op jit(solution)/shard_map/ppermute | solution.py:422
  68.9 6.0 %collective-permute-start.20 = (bf16[288,384]{1,0:T(8,128)(2,1)S(1)}, bf16[288,384]{1,0:T(8,128)(2,1)S(1)}, u32[]{:S(2)}, u32[]{:S(2)}) collective-permute-start(bf16[288,384]{1,0:T(8,128)(2,1)S(1)} %pad_maximum_fusion.5), channel_id=1, source_target_pairs={{0,2},{1,3},{2,0},{3,1},{4,6},{5,7},{6,4},{7,5},{8,10},{9,11},{10,... | collective-permute-start | bytes 663560 | tf_op jit(solution)/shard_map/ppermute | solution.py:422
  69.3 5.7 %collective-permute-start.21 = (bf16[3,16,384]{2,1,0:T(8,128)(2,1)S(1)}, bf16[3,16,384]{2,1,0:T(8,128)(2,1)S(1)}, u32[]{:S(2)}, u32[]{:S(2)}) collective-permute-start(bf16[3,16,384]{2,1,0:T(8,128)(2,1)S(1)} %bitcast.139), channel_id=1, source_target_pairs={{0,4},{4,0},{8,12},{12,8},{16,20},{20,16},{24,28},{28,24},{1,5},{5... | collective-permute-start | bytes 110600 | tf_op jit(solution)/shard_map/ppermute | solution.py:392
  70.1 4.9 %collective-permute-start.22 = (bf16[3,16,384]{2,1,0:T(8,128)(2,1)S(1)}, bf16[3,16,384]{2,1,0:T(8,128)(2,1)S(1)}, u32[]{:S(2)}, u32[]{:S(2)}) collective-permute-start(bf16[3,16,384]{2,1,0:T(8,128)(2,1)S(1)} %bitcast.138), channel_id=1, source_target_pairs={{0,1},{1,0},{2,3},{3,2},{4,8},{5,9},{6,10},{7,11},{8,4},{9,5},{10,... | collective-permute-start | bytes 110600 | tf_op jit(solution)/shard_map/ppermute | solution.py:408
  75.2 7.1 %collective-permute-start.25 = (bf16[152,384]{1,0:T(8,128)(2,1)S(1)}, bf16[152,384]{1,0:T(8,128)(2,1)S(1)}, u32[]{:S(2)}, u32[]{:S(2)}) collective-permute-start(bf16[152,384]{1,0:T(8,128)(2,1)S(1)} %pad_maximum_fusion.6), channel_id=1, source_target_pairs={{0,16},{1,17},{2,18},{3,19},{4,20},{5,21},{6,22},{7,23},{8,24},{9,... | collective-permute-start | bytes 350216 | tf_op jit(solution)/shard_map/ppermute | solution.py:422
  77.2 6.1 %collective-permute-start.24 = (bf16[192,384]{1,0:T(8,128)(2,1)S(1)}, bf16[192,384]{1,0:T(8,128)(2,1)S(1)}, u32[]{:S(2)}, u32[]{:S(2)}) collective-permute-start(bf16[192,384]{1,0:T(8,128)(2,1)S(1)} %bitcast.136), channel_id=1, source_target_pairs={{0,8},{1,9},{2,10},{3,11},{4,12},{5,13},{6,14},{7,15},{8,0},{9,1},... | collective-permute-start | bytes 442376 | tf_op jit(solution)/shard_map/ppermute | solution.py:422
  78.9 4.4 %collective-permute-start.27 = (bf16[22,3,384]{2,1,0:T(4,128)(2,1)S(1)}, bf16[22,3,384]{2,1,0:T(4,128)(2,1)S(1)}, u32[]{:S(2)}, u32[]{:S(2)}) collective-permute-start(bf16[22,3,384]{2,1,0:T(4,128)(2,1)S(1)} %get-tuple-element.279), channel_id=1, source_target_pairs={{0,4},{1,2},{2,1},{3,7},{4,0},{5,6},{6,5},{7,3},{8,12},{9,10},{10,... | collective-permute-start | bytes 152072 | tf_op jit(solution)/shard_map/ppermute | solution.py:408
  79.4 3.8 %collective-permute-start.26 = (bf16[22,3,384]{2,1,0:T(4,128)(2,1)S(1)}, bf16[22,3,384]{2,1,0:T(4,128)(2,1)S(1)}, u32[]{:S(2)}, u32[]{:S(2)}) collective-permute-start(bf16[22,3,384]{2,1,0:T(4,128)(2,1)S(1)} %get-tuple-element.280), channel_id=1, source_target_pairs={{0,1},{1,0},{2,3},{3,2},{4,5},{5,4},{6,7},{7,6},{8,9},{9,8},{10,11... | collective-permute-start | bytes 152072 | tf_op jit(solution)/shard_map/ppermute | solution.py:392
  83.5 3.3 %collective-permute-start.29 = (bf16[56,384]{1,0:T(8,128)(2,1)S(1)}, bf16[56,384]{1,0:T(8,128)(2,1)S(1)}, u32[]{:S(2)}, u32[]{:S(2)}) collective-permute-start(bf16[56,384]{1,0:T(8,128)(2,1)S(1)} %add_convert_fusion.13.mine), channel_id=1, source_target_pairs={{0,1},{1,0},{2,3},{3,2},{4,5},{5,4},{6,7},{7,6},{8,9},{9,8},{10,11... | collective-permute-start | bytes 129032 | tf_op jit(solution)/shard_map/ppermute | solution.py:422
  83.5 7.1 %collective-permute-start.28 = (bf16[96,384]{1,0:T(8,128)(2,1)S(1)}, bf16[96,384]{1,0:T(8,128)(2,1)S(1)}, u32[]{:S(2)}, u32[]{:S(2)}) collective-permute-start(bf16[96,384]{1,0:T(8,128)(2,1)S(1)} %bitcast.137), channel_id=1, source_target_pairs={{0,16},{1,17},{2,18},{3,19},{4,20},{5,21},{6,22},{7,23},{8,24},{9,... | collective-permute-start | bytes 221192 | tf_op jit(solution)/shard_map/ppermute | solution.py:422
  (5 other events, 26.3 us)
